TPU v7x, 32 devices: a whole 2x2x4 slice. The times are simulated.
32 devices in a mesh: groups: 2 (over y), expert: 4 (over z), mp: 4 (over x, core).
Axes of the slice: x: 2, y: 2, z: 4, core: 2. Of those that a mesh axis runs over, the one named last changes fastest.
Arguments:
- tokens: bfloat16 [2048, 1024], P(('groups', 'expert')), parts along dimension 0, may hold values from -6 to 6
- encoder_states: bfloat16 [8, 2, 512, 1024], P(('groups', 'expert'), None, None, 'mp'), parts along dimension 0, may hold values from -64 to 64
- source_owner: int32 [8], P(('groups', 'expert')), parts along dimension 0, may hold values from 0 to 3
- query_weight: bfloat16 [1024, 1024], P(None, 'mp'), may hold values from -0.1875 to 0.1875
- output_weight: bfloat16 [1024, 1024], P('mp'), may hold values from -0.1875 to 0.1875
- router_weight: bfloat16 [1024, 4], replicated, may hold values from -0.1875 to 0.1875
- expert_choice: int32 [2048, 2], P(('groups', 'expert')), parts along dimension 0, may hold values from 0 to 3, all different within a row; in each aligned block of 256 rows (0 to 255, 256 to 511, ...) at most 192 rows name the same one
- expand_weight: bfloat16 [4, 1024, 4096], P('expert', None, 'mp'), may hold values from -0.1875 to 0.1875
- shrink_weight: bfloat16 [4, 4096, 1024], P('expert', 'mp'), may hold values from -0.09375 to 0.09375
Outputs:
- layer_out: bfloat16 [2048, 1024], P(('groups', 'expert'), 'mp'), parts along dimension 0
There are 2 independent parts, one for each index of `groups`. A program takes and returns all parts, laid end to end along the dimension named above; an argument that names none is the same for every part. Nothing has to cross between parts.
Inputs may be any that keep to these rules, and one draw needn't show every extreme that they name: `expert_choice`: in each aligned block of 256 rows (the rows of one device) no expert is named more than 192 times, a bound that some block reaches; the two experts of a row differ.
All inputs are finite; a program needn't handle non-finite values.
Results may differ from a plain program's by a relative error of at most 0.0072.
Values may be sent and summed in bfloat16 or wider, within the bound.
No kernel may reach another device: no remote copies, remote signals or barrier semaphores. Data moves between devices by JAX's collectives and lax.ppermute only.
A program may use at most 64 MiB of HBM per device.

v0:
```python
import jax
import jax.numpy as jnp
from jax import lax
from jax.sharding import PartitionSpec as P

HEAD_DIM = 128


def local(
    tokens,
    encoder_states,
    source_owner,
    query_weight,
    output_weight,
    router_weight,
    expert_choice,
    expand_weight,
    shrink_weight,
):
    token_count = tokens.shape[0]
    features = tokens.shape[1]
    groups = lax.axis_size("expert")
    slices = lax.axis_size("mp")
    column_index = lax.axis_index("mp")
    part_width = features // slices
    experts = expand_weight.shape[0] * groups
    capacity = max(2, 3 * token_count // experts)
    head_count = part_width // HEAD_DIM
    owner = source_owner[0]
    empty_source = jnp.zeros(encoder_states.shape[1:], jnp.bfloat16)
    piece = lax.all_gather(encoder_states, "expert", axis=0, tiled=True)
    count = piece.shape[0]
    inside = (owner >= 0) & (owner < count)
    taken = lax.dynamic_index_in_dim(piece, jnp.clip(owner, 0, count - 1), 0, keepdims=False)
    source = jnp.where(inside, taken, empty_source)
    queries = jnp.dot(tokens, query_weight, preferred_element_type=jnp.float32).astype(jnp.bfloat16)
    query_heads = queries.reshape(token_count, head_count, HEAD_DIM)
    key_heads = source[0].reshape(-1, head_count, HEAD_DIM)
    value_heads = source[1].reshape(-1, head_count, HEAD_DIM)
    scores = jnp.einsum(
        "thd,shd->hts", query_heads, key_heads, preferred_element_type=jnp.float32
    ) * HEAD_DIM ** (-0.5)
    weights = jnp.exp(scores - jnp.max(scores, axis=2, keepdims=True))
    weights = (weights / jnp.sum(weights, axis=2, keepdims=True)).astype(jnp.bfloat16)
    context = jnp.einsum("hts,shd->thd", weights, value_heads, preferred_element_type=jnp.float32)
    context = context.astype(jnp.bfloat16).reshape(token_count, part_width)
    projected = jnp.dot(context, output_weight, preferred_element_type=jnp.float32)
    attention = lax.psum_scatter(projected, "mp", scatter_dimension=1, tiled=True)
    own_tokens = lax.dynamic_slice_in_dim(tokens, column_index * part_width, part_width, 1)
    state = (own_tokens.astype(jnp.float32) + attention).astype(jnp.bfloat16)
    whole_state = lax.all_gather(state, "mp", axis=1, tiled=True)
    logits = jnp.dot(whole_state, router_weight, preferred_element_type=jnp.float32)
    flat_choice = expert_choice.reshape(-1)
    one_hot = (flat_choice[:, None] == jnp.arange(experts, dtype=jnp.int32)[None, :]).astype(
        jnp.int32
    )
    earlier = jnp.cumsum(one_hot, axis=0) - one_hot
    slot_of = jnp.sum(earlier * one_hot, axis=1)
    place = flat_choice * capacity + slot_of
    picked = jnp.sum(
        one_hot.reshape(token_count, 2, experts).astype(jnp.float32) * logits[:, None, :], axis=2
    )
    gate_first = jax.nn.sigmoid(picked[:, 0] - picked[:, 1])
    gate_second = jax.nn.sigmoid(picked[:, 1] - picked[:, 0])
    repeated = jnp.repeat(whole_state, 2, axis=0)
    outgoing = jnp.zeros((experts * capacity, features), jnp.bfloat16).at[place].set(repeated)
    arrived = lax.all_to_all(
        outgoing.reshape(experts, capacity, features),
        "expert",
        split_axis=0,
        concat_axis=0,
        tiled=True,
    )
    arrived = arrived.reshape(-1, features)
    hidden = jnp.maximum(
        jnp.dot(arrived, expand_weight[0], preferred_element_type=jnp.float32), 0.0
    ).astype(jnp.bfloat16)
    partial_out = jnp.dot(hidden, shrink_weight[0], preferred_element_type=jnp.float32)
    summed = lax.psum(partial_out, "mp").astype(jnp.bfloat16)
    returned = lax.all_to_all(
        summed.reshape(groups, capacity, features),
        "expert",
        split_axis=0,
        concat_axis=0,
        tiled=True,
    )
    returned = lax.dynamic_slice_in_dim(returned, column_index * part_width, part_width, 2)
    results = returned.reshape(experts * capacity, part_width)[place]
    results = results.reshape(token_count, 2, part_width).astype(jnp.float32)
    combined = (
        state.astype(jnp.float32)
        + gate_first[:, None] * results[:, 0]
        + gate_second[:, None] * results[:, 1]
    )
    return combined.astype(jnp.bfloat16)


def solution(mesh):
    return jax.shard_map(
        local,
        mesh=mesh,
        in_specs=(
            P(("groups", "expert"), None),
            P(("groups", "expert"), None, None, "mp"),
            P(("groups", "expert")),
            P(None, "mp"),
            P("mp", None),
            P(),
            P(("groups", "expert"), None),
            P("expert", None, "mp"),
            P("expert", "mp", None),
        ),
        out_specs=P(("groups", "expert"), "mp"),
        check_vma=False,
    )
```

profile of v0, /device:TPU:0, one launch (start us, length us, event | category | flops | bytes accessed | tf_op | source)
XLA Modules:
  0.0 266.7 jit_solution(11671307366697370485)
XLA Ops:
  6.5 0.0 copy-start
  6.5 0.0 all-gather.2.cloned.1.call-start
  6.5 0.7 all-gather.2.cloned.1.call-update
  7.3 0.0 reduce-scatter.2.cloned.1.call-start
  8.0 1.5 convolution_convert_fusion.1
  9.5 48.1 %all-gather.2.cloned.1.call-done = bf16[4,2,512,256]{3,2,1,0:T(8,128)(2,1)} async-done(((bf16[1,2,512,256]{3,2,1,0:T(8,128)(2,1)}), bf16[4,2,512,256]{3,2,1,0:T(8,128)(2,1)}) %all-gather.2.cloned.1.call-update) | async-done | bytes 2097168 | tf_op jit(solution)/shard_map/all_gather | solution.py:31
  57.6 1.1 constant_dynamic-slice_fusion.1
  58.7 0.2 copy.44
  58.9 0.7 fusion.26
  59.7 0.6 fusion.27
  60.2 0.3 convolution_multiply_fusion
  60.6 2.0 convolution_convert_fusion
  62.6 0.0 copy-start.1
  62.6 2.4 fusion.28
  64.9 0.0 reduce-scatter.2.cloned.1.call-update
  65.0 0.0 copy-done.1
  65.0 0.1 copy.38
  65.1 0.1 eq.39
  65.3 0.1 eq.35
  65.4 0.1 copy.37
  65.6 0.1 mul.66
  65.7 1.2 reduce-window.6
  67.0 0.2 slice_reduce_fusion
  67.2 0.2 reduce-window.9
  67.4 0.1 add_bitcast_fusion
  67.5 21.3 %reduce-scatter.2.cloned.1.call-done = f32[256,256]{1,0:T(8,128)} async-done(((f32[256,1024]{1,0:T(8,128)}), f32[256,256]{1,0:T(8,128)}) %reduce-scatter.2.cloned.1.call-update) | async-done | bytes 262160 | tf_op jit(solution)/shard_map/reduce_scatter | solution.py:48
  88.7 1.0 add_convert_fusion
  89.7 6.8 %all_gather.7 = bf16[256,1024]{1,0:T(8,128)(2,1)S(1)} all-gather(bf16[256,256]{1,0:T(8,128)(2,1)S(1)} %add_convert_fusion), channel_id=1, replica_groups=mesh['groups'=2,'expert'=4,'mp'=4] {'mp'}, dimensions={1}, use_global_device_ids=true | all-gather | bytes 655360 | tf_op jit(solution)/shard_map/all_gather | solution.py:51
  96.5 1.5 broadcast_in_dim.8
  98.1 2.3 reshape.119
  100.3 4.5 %scatter_custom_fusion = bf16[768,1024]{1,0:T(8,128)(2,1)} fusion(s32[512]{0:T(512)S(1)} %bitcast.85, bf16[512,1024]{1,0:T(8,128)(2,1)} %reshape.119, bf16[]{:T(256)} %constant.21.clone.1), kind=kCustom, calls=%fused_computation.14 | custom fusion | bytes 1573376 | tf_op jit(solution)/shard_map/scatter | solution.py:66
  104.8 42.2 %all_to_all.10 = bf16[4,192,1024]{2,1,0:T(8,128)(2,1)} all-to-all(bf16[4,192,1024]{2,1,0:T(8,128)(2,1)} %bitcast.76), channel_id=1, replica_groups=mesh['groups'=2,'expert'=4,'mp'=4] {'expert'}, dimensions={0} | all-to-all | bytes 3145728 | tf_op jit(solution)/shard_map/all_to_all | solution.py:67
  147.0 0.0 copy-done
  147.0 7.2 %fusion.1 = f32[768,1024]{1,0:T(8,128)} fusion(bf16[1,1024,1024]{2,1,0:T(8,128)(2,1)S(1)} %copy-done, bf16[768,1024]{1,0:T(8,128)(2,1)} %bitcast.78, bf16[1,1024,1024]{2,1,0:T(8,128)(2,1)} %param.16), kind=kOutput, calls=%fused_computation.4 | convolution fusion | flops 3222798336 | bytes 8912896 | tf_op jit(solution)/shard_map/dot_general | solution.py:78
  154.1 58.5 %all-reduce.1 = bf16[768,1024]{1,0:T(8,128)(2,1)} all-reduce(f32[768,1024]{1,0:T(8,128)} %fusion.1), channel_id=1, replica_groups=mesh['groups'=2,'expert'=4,'mp'=4] {'mp'}, use_global_device_ids=true, to_apply=%region_8.9 | all-reduce | flops 786432 | bytes 4718592 | tf_op jit(solution)/shard_map/psum | solution.py:79
  212.7 0.0 copy-start.2
  212.7 4.5 %all-to-all-start.1 = ((bf16[4,192,1024]{2,1,0:T(8,128)(2,1)}), bf16[4,192,1024]{2,1,0:T(8,128)(2,1)}, u32[]{:S(2)}, u32[]{:S(2)}) async-start(bf16[4,192,1024]{2,1,0:T(8,128)(2,1)} %bitcast.77), calls=%async_computation.2 | async-start | bytes 3145728 | tf_op jit(solution)/shard_map/all_to_all | solution.py:80
  217.2 0.0 copy-done.2
  217.2 0.2 fusion.29
  217.5 37.9 %all-to-all-done.1 = bf16[4,192,1024]{2,1,0:T(8,128)(2,1)} async-done(((bf16[4,192,1024]{2,1,0:T(8,128)(2,1)}), bf16[4,192,1024]{2,1,0:T(8,128)(2,1)}, u32[]{:S(2)}, u32[]{:S(2)}) %all-to-all-start.1) | async-done | bytes 1572896 | tf_op jit(solution)/shard_map/all_to_all | solution.py:80
  255.4 1.0 constant_dynamic-slice_fusion
  256.4 2.0 gather_fusion
  258.3 0.3 reshape.106
  258.6 0.4 fusion.25
  259.0 0.8 fusion.15
  (8 shorter events, 0.1 us)
Async XLA Ops:
  6.5 140.4 %copy-start = (bf16[1,1024,1024]{2,1,0:T(8,128)(2,1)S(1)}, bf16[1,1024,1024]{2,1,0:T(8,128)(2,1)}, u32[]{:S(2)}) copy-start(bf16[1,1024,1024]{2,1,0:T(8,128)(2,1)} %param.17) | copy-start | bytes 6291460
  6.5 51.1 %all-gather.2.cloned.1.call-start = ((), (), s32[]{:S(2)}) async-start(), calls=%async_computation.3 | async-start | bytes 2621440 | tf_op jit(solution)/shard_map/all_gather | solution.py:31
  7.3 81.5 %reduce-scatter.2.cloned.1.call-start = ((), (), s32[]{:S(2)}) async-start(), calls=%async_computation.4 | async-start | bytes 1310720 | tf_op jit(solution)/shard_map/reduce_scatter | solution.py:48
  62.6 2.4 copy-start.1
  212.7 4.5 %copy-start.2 = (bf16[1024,4]{0,1:T(4,128)(2,1)S(1)}, bf16[1024,4]{0,1:T(4,128)(2,1)}, u32[]{:S(2)}) copy-start(bf16[1024,4]{0,1:T(4,128)(2,1)} %param.14) | copy-start | bytes 24580
  212.7 42.7 %all-to-all-start.1 = ((bf16[4,192,1024]{2,1,0:T(8,128)(2,1)}), bf16[4,192,1024]{2,1,0:T(8,128)(2,1)}, u32[]{:S(2)}, u32[]{:S(2)}) async-start(bf16[4,192,1024]{2,1,0:T(8,128)(2,1)} %bitcast.77), calls=%async_computation.2 | async-start | bytes 3145728 | tf_op jit(solution)/shard_map/all_to_all | solution.py:80
Sparse Core Ops, SparseCore 0:
  8.9 48.6 all-gather.1
  65.1 23.5 reduce-scatter.1
where the time goes:
time: 267 us
  waiting for transfers between devices  108 us (40%)
  blocking collectives  107 us (40%)
  local copies, waits for them, and re-layouts  14.9 us (6%)
  matrix products  14.2 us (5%)
  between operations  14.2 us (5%)
  starting transfers between devices  4.51 us (2%)
  other arithmetic  3.43 us (1%)
    psum x1, blocking collectives, local(): summed = lax.psum(partial_out, 'mp').astype(jnp.bfloat16)  58.5 us
    all_gather x1, waiting for transfers between devices, local(): piece = lax.all_gather(encoder_states, 'expert', axis=0, tiled=True)  48.1 us
    all_to_all x1, blocking collectives, local(): lax.all_to_all(outgoing.reshape(experts, capacity, features), 'expert', s...  42.2 us
    all_to_all x1, waiting for transfers between devices, local(): lax.all_to_all(summed.reshape(groups, capacity, features), 'expert', spli...  37.9 us
    reduce_scatter x1, waiting for transfers between devices, local(): lax.psum_scatter(projected, 'mp', scatter_dimension=1, tiled=True)  21.3 us
    dot_general x1, matrix products, local(): jnp.dot(hidden, shrink_weight[0], preferred_element_type=jnp.float32)  7.15 us
    all_gather x1, blocking collectives, local(): whole_state = lax.all_gather(state, 'mp', axis=1, tiled=True)  6.78 us
  transfers between devices with their start and end apart: 3, of which 3 were waited for; matrix products, arithmetic and copies ran while one was open for 2% of the time, Pallas kernels for 0%

commit v1 on v0

v1 whole, which is shorter than its diff:
```python
import functools

import jax
import jax.numpy as jnp
from jax import lax
from jax.experimental import pallas as pl
from jax.experimental.pallas import tpu as pltpu
from jax.sharding import PartitionSpec as P

HEAD_DIM = 128
DIRECT = 8
F32, BF16 = jnp.float32, jnp.bfloat16
PARAMS = pltpu.CompilerParams(vmem_limit_bytes=40 * 2**20)
SCALARS = pl.BlockSpec(memory_space=pltpu.SMEM)
WHOLE = pl.BlockSpec(memory_space=pltpu.VMEM)


def dot(a, b, dims=((1,), (0,))):
    return lax.dot_general(a, b, (dims, ((), ())), preferred_element_type=F32)


def query_kernel(tokens, weight, out):
    out[...] = dot(tokens[...], weight[...]).astype(BF16)


def attend_kernel(queries, source, out):
    for head in range(queries.shape[1] // HEAD_DIM):
        part = slice(head * HEAD_DIM, (head + 1) * HEAD_DIM)
        scores = dot(queries[:, part], source[0, :, part], ((1,), (1,)))
        top = jnp.max(scores, axis=1, keepdims=True)
        weights = jnp.exp((scores - top) * HEAD_DIM**-0.5)
        total = jnp.sum(weights, axis=1, keepdims=True)
        context = dot(weights.astype(BF16), source[1, :, part])
        out[:, part] = (context / total).astype(BF16)


def attend(queries, source, block):
    rows, width = queries.shape
    return pl.pallas_call(
        attend_kernel,
        grid=(rows // block,),
        in_specs=[
            pl.BlockSpec((block, width), lambda i: (i, 0)),
            pl.BlockSpec(source.shape, lambda i: (0, 0, 0)),
        ],
        out_specs=pl.BlockSpec((block, width), lambda i: (i, 0)),
        out_shape=jax.ShapeDtypeStruct((rows, width), BF16),
        compiler_params=PARAMS,
        name="attend",
    )(queries, source)


def route_kernel(experts, ids, choice, choice_t, dispatch, first, second):
    tokens = choice.shape[0]
    parts, slots = dispatch.shape[0], dispatch.shape[1]
    capacity = slots * parts // experts
    wide = lax.broadcasted_iota(jnp.int32, (tokens, experts), 1)
    tall = lax.broadcasted_iota(jnp.int32, (experts, tokens), 0)
    c0, c1 = choice[:, 0:1], choice[:, 1:2]
    r0, r1 = choice_t[0:1, :], choice_t[1:2, :]
    named = ((wide == c0) | (wide == c1)).astype(BF16)
    named_t = ((tall == r0) | (tall == r1)).astype(BF16)
    i = lax.broadcasted_iota(jnp.int32, (tokens, tokens), 0)
    j = lax.broadcasted_iota(jnp.int32, (tokens, tokens), 1)
    rank = dot((j < i).astype(BF16), named).astype(jnp.int32)
    rank_t = dot(named_t, (i < j).astype(BF16)).astype(jnp.int32)
    place0 = c0 * capacity + jnp.sum(jnp.where(wide == c0, rank, 0), axis=1, keepdims=True)
    place1 = c1 * capacity + jnp.sum(jnp.where(wide == c1, rank, 0), axis=1, keepdims=True)
    across0 = r0 * capacity + jnp.sum(jnp.where(tall == r0, rank_t, 0), axis=0, keepdims=True)
    across1 = r1 * capacity + jnp.sum(jnp.where(tall == r1, rank_t, 0), axis=0, keepdims=True)
    lane = lax.broadcasted_iota(jnp.int32, (tokens, slots), 1)
    row = lax.broadcasted_iota(jnp.int32, (slots, tokens), 0)
    for k in range(parts):
        base = (ids[0] ^ k) * capacity if parts > 1 else 0
        dispatch[k] = ((row + base == across0) | (row + base == across1)).astype(BF16)
        first[k] = (lane + base == place0).astype(BF16)
        second[k] = (lane + base == place1).astype(BF16)


def route(ids, choice, experts, parts, capacity):
    tokens = choice.shape[0]
    slots = experts * capacity // parts
    return pl.pallas_call(
        functools.partial(route_kernel, experts),
        in_specs=[SCALARS, WHOLE, WHOLE],
        out_specs=[WHOLE] * 3,
        out_shape=[
            jax.ShapeDtypeStruct((parts, slots, tokens), BF16),
            jax.ShapeDtypeStruct((parts, tokens, slots), BF16),
            jax.ShapeDtypeStruct((parts, tokens, slots), BF16),
        ],
        compiler_params=PARAMS,
        name="route",
    )(ids, choice, choice.T)


def state_kernel(count, away, *refs):
    ids, tokens, dispatch = refs[:3]
    contexts, weights = refs[3 : 3 + count], refs[3 + count : 3 + 2 * count]
    state = refs[3 + 2 * count]
    outs = refs[4 + 2 * count :]
    total = tokens[...].astype(F32)
    for context, weight in zip(contexts, weights):
        total += dot(context[...], weight[...])
    state[...] = total.astype(BF16)
    half = state.shape[1] // 2
    mine = state[:, pl.ds(pl.multiple_of((ids[1] & 1) * half, half), half)]
    for out, k in zip(outs, away):
        out[...] = dot(dispatch[k], mine).astype(BF16)


def make_state(ids, tokens, dispatch, contexts, weights, away):
    slots = dispatch.shape[1]
    features = tokens.shape[1]
    return pl.pallas_call(
        functools.partial(state_kernel, len(contexts), away),
        in_specs=[SCALARS] + [WHOLE] * (2 + 2 * len(contexts)),
        out_specs=[WHOLE] * (1 + len(away)),
        out_shape=[jax.ShapeDtypeStruct(tokens.shape, BF16)]
        + [jax.ShapeDtypeStruct((slots, features // 2), BF16)] * len(away),
        compiler_params=PARAMS,
        name="state",
    )(ids, tokens, dispatch, *contexts, *weights)


def home_kernel(experts, ids, state, dispatch, router, choice, own_a, own_b, gates, columns):
    half = own_a.shape[1]
    core = ids[1] & 1
    own_a[...] = dot(dispatch[0], state[:, pl.ds(pl.multiple_of(core * half, half), half)]).astype(BF16)
    own_b[...] = dot(dispatch[0], state[:, pl.ds(pl.multiple_of((1 - core) * half, half), half)]).astype(BF16)
    logits = dot(state[...], router[...])
    wide = lax.broadcasted_iota(jnp.int32, logits.shape, 1)
    first = jnp.sum(jnp.where(wide == choice[:, 0:1], logits, 0.0), axis=1, keepdims=True)
    second = jnp.sum(jnp.where(wide == choice[:, 1:2], logits, 0.0), axis=1, keepdims=True)
    gates[:, 0:1] = jax.nn.sigmoid(first - second)
    gates[:, 1:2] = jax.nn.sigmoid(second - first)
    width = columns.shape[1]
    columns[...] = state[:, pl.ds(pl.multiple_of(ids[1] * width, width), width)].astype(F32)


def at_home(ids, state, dispatch, router, choice, experts, width):
    tokens, features = state.shape
    slots = dispatch.shape[1]
    return pl.pallas_call(
        functools.partial(home_kernel, experts),
        in_specs=[SCALARS] + [WHOLE] * 4,
        out_specs=[WHOLE] * 4,
        out_shape=[
            jax.ShapeDtypeStruct((slots, features // 2), BF16),
            jax.ShapeDtypeStruct((slots, features // 2), BF16),
            jax.ShapeDtypeStruct((tokens, 2), F32),
            jax.ShapeDtypeStruct((tokens, width), F32),
        ],
        compiler_params=PARAMS,
        name="home",
    )(ids, state, dispatch, router, choice)


def expert_kernel(ids, mine, other, expand, shrink, keep, give, total):
    step, steps = pl.program_id(0), pl.num_programs(0)
    half = mine.shape[1]
    core = ids[1] & 1
    hidden = dot(mine[...], expand[pl.ds(pl.multiple_of(core * half, half), half), :])
    hidden += dot(other[...], expand[pl.ds(pl.multiple_of((1 - core) * half, half), half), :])
    hidden = jnp.maximum(hidden, 0.0).astype(BF16)
    product = dot(hidden, shrink[...])

    @pl.when(step == 0)
    def _():
        total[...] = product

    @pl.when(step > 0)
    def _():
        total[...] += product

    @pl.when(step == steps - 1)
    def _():
        parts = keep.shape[0]
        width = keep.shape[2]
        for j in range(parts):
            at = (ids[1] ^ (2 * j)) * width
            keep[j] = total[:, pl.ds(pl.multiple_of(at, width), width)]
            at = (ids[1] ^ (2 * j) ^ 1) * width
            give[j] = total[:, pl.ds(pl.multiple_of(at, width), width)].astype(BF16)


def run_expert(ids, mine, other, expand, shrink, parts):
    rows, half = mine.shape
    features, units = expand.shape
    tile = min(256, units)
    width = features // (2 * parts)
    return pl.pallas_call(
        expert_kernel,
        grid=(units // tile,),
        in_specs=[
            SCALARS,
            pl.BlockSpec((rows, half), lambda i: (0, 0)),
            pl.BlockSpec((rows, half), lambda i: (0, 0)),
            pl.BlockSpec((features, tile), lambda i: (0, i)),
            pl.BlockSpec((tile, features), lambda i: (i, 0)),
        ],
        out_specs=[pl.BlockSpec((parts, rows, width), lambda i: (0, 0, 0))] * 2,
        out_shape=[
            jax.ShapeDtypeStruct((parts, rows, width), F32),
            jax.ShapeDtypeStruct((parts, rows, width), BF16),
        ],
        scratch_shapes=[pltpu.VMEM((rows, features), F32)],
        compiler_params=PARAMS,
        name="expert",
    )(ids, mine, other, expand, shrink)


def combine_kernel(count, gates, base, first, second, *refs):
    parts, out = refs[:count], refs[count]
    total = parts[0][...].astype(F32)
    for part in parts[1:]:
        total += part[...].astype(F32)
    total = total.astype(BF16)
    result = base[...] + gates[:, 0:1] * dot(first[...], total) + gates[:, 1:2] * dot(second[...], total)
    out[...] = result.astype(out.dtype)


def combine(gates, base, first, second, parts, dtype):
    return pl.pallas_call(
        functools.partial(combine_kernel, len(parts)),
        in_specs=[WHOLE] * (4 + len(parts)),
        out_specs=WHOLE,
        out_shape=jax.ShapeDtypeStruct(base.shape, dtype),
        compiler_params=PARAMS,
        name="combine",
    )(gates, base, first, second, *parts)


def local(
    tokens,
    encoder_states,
    source_owner,
    query_weight,
    output_weight,
    router_weight,
    expert_choice,
    expand_weight,
    shrink_weight,
):
    token_count, features = tokens.shape
    groups = lax.axis_size("expert")
    slices = lax.axis_size("mp")
    here, column = lax.axis_index("expert"), lax.axis_index("mp")
    ids = jnp.stack([here, column]).astype(jnp.int32)
    width = features // slices
    experts = expand_weight.shape[0] * groups
    capacity = max(2, 3 * token_count // experts)
    direct = groups <= DIRECT
    pairs = slices // 2

    def hop(value, along_expert, along_mp):
        if along_expert == 0 and along_mp == 0:
            return value
        moves = [
            (e * slices + m, (e ^ along_expert) * slices + (m ^ along_mp))
            for e in range(groups)
            for m in range(slices)
        ]
        return lax.ppermute(value, ("expert", "mp"), moves)

    def spread(value):
        parts = value.reshape(groups, -1, value.shape[-1])
        return lax.all_to_all(parts, "expert", 0, 0, tiled=True).reshape(value.shape)

    steps = range(groups) if direct else [0]
    dispatch, first, second = route(ids, expert_choice, experts, len(steps), capacity)

    queries = pl.pallas_call(
        query_kernel,
        in_specs=[WHOLE] * 2,
        out_specs=WHOLE,
        out_shape=jax.ShapeDtypeStruct((token_count, width), BF16),
        compiler_params=PARAMS,
        name="query",
    )(tokens, query_weight)
    owner = source_owner[0]
    if direct:
        context = attend(queries, encoder_states[0], token_count)
        for k in range(1, groups):
            back = hop(attend(hop(queries, k, 0), encoder_states[0], token_count), k, 0)
            context = jnp.where(owner == here ^ k, back, context)
    else:
        asked = lax.all_gather(queries, "expert", axis=0, tiled=True)
        back = spread(attend(asked, encoder_states[0], token_count))
        context = lax.dynamic_slice_in_dim(back, owner * token_count, token_count, 0)

    weights = [output_weight]
    bit = 1
    while bit < slices:
        bit *= 2
    while bit > 1:
        bit //= 2
        weights = weights + [hop(weight, 0, bit) for weight in weights]
    order = [0]
    bit = slices
    while bit > 1:
        bit //= 2
        order = order + [index ^ bit for index in order]
    contexts = [hop(context, 0, index) for index in order]

    away = tuple(range(1, groups)) if direct else (0,)
    state, *leaving = make_state(ids, tokens, dispatch, contexts, weights, away)
    own_a, own_b, gates, columns = at_home(ids, state, dispatch, router_weight, expert_choice, experts, width)

    results = columns
    for k in steps:
        if not direct:
            mine = spread(leaving[0])
            other = hop(mine, 0, 1)
        elif k == 0:
            mine, other = own_a, own_b
        else:
            mine = hop(leaving[k - 1], k, 0)
            other = hop(mine, 0, 1)
        keep, give = run_expert(ids, mine, other, expand_weight[0], shrink_weight[0], pairs)
        summed = (keep + hop(give, 0, 1).astype(F32)).astype(BF16)
        parts = []
        for j in range(pairs):
            if direct:
                parts.append(hop(summed[j], k, 2 * j))
            else:
                parts.append(hop(spread(summed[j]), 0, 2 * j))
        last = k == steps[-1]
        results = combine(gates, results, first[k], second[k], parts, BF16 if last else F32)
    return results


def solution(mesh):
    return jax.shard_map(
        local,
        mesh=mesh,
        in_specs=(
            P(("groups", "expert"), None),
            P(("groups", "expert"), None, None, "mp"),
            P(("groups", "expert")),
            P(None, "mp"),
            P("mp", None),
            P(),
            P(("groups", "expert"), None),
            P("expert", None, "mp"),
            P("expert", "mp", None),
        ),
        out_specs=P(("groups", "expert"), "mp"),
        check_vma=False,
    )
```

time: 267 us -> 97.1 us (0.36)
  blocking collectives: 107 us -> 0 us
  waiting for transfers between devices: 108 us -> 37.1 us
  starting transfers between devices: 4.51 us -> 31.1 us
  Pallas kernels: 0 us -> 23.7 us
  matrix products: 14.2 us -> 0 us
  between operations: 14.2 us -> 0.99 us
  local copies, waits for them, and re-layouts: 14.9 us -> 3.62 us
  other arithmetic: 3.43 us -> 0.3 us
    psum x1 -> x0, blocking collectives: 58.5 us -> none  [local(): summed = lax.psum(partial_out, 'mp').astype(jnp.bfloat16)]
    all_gather x1 -> x0, waiting for transfers between devices: 48.1 us -> none  [local(): piece = lax.all_gather(encoder_states, 'expert', axis=0, tiled=True)]
    all_to_all x1 -> x0, blocking collectives: 42.2 us -> none  [local(): lax.all_to_all(outgoing.reshape(experts, capacity, features), 'expert', s...]
    all_to_all x1 -> x0, waiting for transfers between devices: 37.9 us -> none  [local(): lax.all_to_all(summed.reshape(groups, capacity, features), 'expert', spli...]
    ppermute x0 -> x29, waiting for transfers between devices: none -> 37.1 us  [hop(): return lax.ppermute(value, ('expert', 'mp'), moves)]
    ppermute x0 -> x29, starting transfers between devices: none -> 31.1 us  [hop(): return lax.ppermute(value, ('expert', 'mp'), moves)]
    pallas_call x0 -> x16, Pallas kernels: none -> 23.7 us  [the longest x4 14.7 us: run_expert(): pl.pallas_call(expert_kernel, grid=(units // tile,), in_specs=[SCALARS, p...]
    reduce_scatter x1 -> x0, waiting for transfers between devices: 21.3 us -> none  [local(): lax.psum_scatter(projected, 'mp', scatter_dimension=1, tiled=True)]
  transfers between devices with their start and end apart: 3 -> 29, of which waited for: 3 -> 8; matrix products, arithmetic and copies ran while one was open for 2% -> 1% of each run, Pallas kernels for 0% -> 22%
where the time goes in v1:
time: 97.1 us; the launch traced here: 96.8 us
  waiting for transfers between devices  37.1 us (38%)
  starting transfers between devices  31.1 us (32%)
  Pallas kernels  23.7 us (24%)
  local copies, waits for them, and re-layouts  3.62 us (4%)
  between operations  0.99 us (1%)
    ppermute x29, waiting for transfers between devices, hop(): return lax.ppermute(value, ('expert', 'mp'), moves)  37.1 us
    ppermute x29, starting transfers between devices, hop(): return lax.ppermute(value, ('expert', 'mp'), moves)  31.1 us
    pallas_call x4, Pallas kernels, run_expert(): pl.pallas_call(expert_kernel, grid=(units // tile,), in_specs=[SCALARS, p...  14.7 us
    unnamed x22, local copies, waits for them, and re-layouts  3.49 us
    pallas_call x4, Pallas kernels, attend(): pl.pallas_call(attend_kernel, grid=(rows // block,), in_specs=[pl.BlockSp...  3.1 us
  transfers between devices with their start and end apart: 29, of which 8 were waited for; matrix products, arithmetic and copies ran while one was open for 1% of the time, Pallas kernels for 22%

profile of v1, /device:TPU:0, one launch (start us, length us, event | category | flops | bytes accessed | tf_op | source)
XLA Modules:
  0.0 96.8 jit_solution(11859681644649322115)
XLA Ops:
  0.0 2.9 %collective-permute-start.9 = (bf16[256,1024]{1,0:T(8,128)(2,1)}, bf16[256,1024]{1,0:T(8,128)(2,1)S(1)}, u32[]{:S(2)}, u32[]{:S(2)}) collective-permute-start(bf16[256,1024]{1,0:T(8,128)(2,1)} %refs_7_.1), channel_id=1, source_target_pairs={{0,2},{1,3},{2,0},{3,1},{4,6},{5,7},{6,4},{7,5},{8,10},{9,11},{10,... | collective-permute-start | bytes 1572872 | tf_op jit(solution)/shard_map/ppermute | solution.py:264
  2.9 1.0 %copy-done.4 = bf16[256,1024]{1,0:T(8,128)(2,1)S(1)} copy-done((bf16[256,1024]{1,0:T(8,128)(2,1)S(1)}, bf16[256,1024]{1,0:T(8,128)(2,1)}, u32[]{:S(2)}) %copy-start.4) | copy-done | bytes 524312
  4.0 1.0 %copy-done.6 = bf16[1024,256]{1,0:T(8,128)(2,1)S(1)} copy-done((bf16[1024,256]{1,0:T(8,128)(2,1)S(1)}, bf16[1024,256]{1,0:T(8,128)(2,1)}, u32[]{:S(2)}) %copy-start.6) | copy-done | bytes 524312
  5.0 0.3 query.1.queries
  5.3 3.7 %collective-permute-start = (bf16[256,256]{1,0:T(8,128)(2,1)S(1)}, bf16[256,256]{1,0:T(8,128)(2,1)S(1)}, u32[]{:S(2)}, u32[]{:S(2)}) collective-permute-start(bf16[256,256]{1,0:T(8,128)(2,1)S(1)} %query.1.queries), channel_id=1, source_target_pairs={{0,12},{1,13},{2,14},{3,15},{4,8},{5,9},{6,10},{7,11},{8,4},{9,5},... | collective-permute-start | bytes 393224 | tf_op jit(solution)/shard_map/ppermute | solution.py:264
  9.0 0.0 collective-permute-start.2
  9.0 0.8 collective-permute-start.4
  9.8 0.0 collective-permute-start.10
  9.8 5.3 %collective-permute-done.9.refs_8_ = bf16[256,1024]{1,0:T(8,128)(2,1)S(1)} collective-permute-done((bf16[256,1024]{1,0:T(8,128)(2,1)}, bf16[256,1024]{1,0:T(8,128)(2,1)S(1)}, u32[]{:S(2)}, u32[]{:S(2)}) %collective-permute-start.9) | collective-permute-done | bytes 524320 | tf_op jit(solution)/shard_map/ppermute | solution.py:264
  15.1 0.0 collective-permute-start.11
  15.1 0.0 collective-permute-done.queries
  15.1 1.0 %copy-done.2 = bf16[1,2,512,256]{3,2,1,0:T(8,128)(2,1)S(1)} copy-done((bf16[1,2,512,256]{3,2,1,0:T(8,128)(2,1)S(1)}, bf16[1,2,512,256]{3,2,1,0:T(8,128)(2,1)}, u32[]{:S(2)}) %copy-start.2) | copy-done | bytes 524312
  16.1 0.8 attend.4
  16.9 3.9 %collective-permute-start.1 = (bf16[256,256]{1,0:T(8,128)(2,1)S(1)}, bf16[256,256]{1,0:T(8,128)(2,1)S(1)}, u32[]{:S(2)}, u32[]{:S(2)}) collective-permute-start(bf16[256,256]{1,0:T(8,128)(2,1)S(1)} %attend.4), channel_id=1, source_target_pairs={{0,12},{1,13},{2,14},{3,15},{4,8},{5,9},{6,10},{7,11},{8,4},{9,5},... | collective-permute-start | bytes 393224 | tf_op jit(solution)/shard_map/ppermute | solution.py:264
  20.8 0.0 collective-permute-done.2.queries
  20.8 0.8 attend.5
  21.6 1.1 %collective-permute-start.3 = (bf16[256,256]{1,0:T(8,128)(2,1)S(1)}, bf16[256,256]{1,0:T(8,128)(2,1)S(1)}, u32[]{:S(2)}, u32[]{:S(2)}) collective-permute-start(bf16[256,256]{1,0:T(8,128)(2,1)S(1)} %attend.5), channel_id=1, source_target_pairs={{0,8},{1,9},{2,10},{3,11},{4,12},{5,13},{6,14},{7,15},{8,0},{9,1},... | collective-permute-start | bytes 393224 | tf_op jit(solution)/shard_map/ppermute | solution.py:264
  22.8 0.0 collective-permute-done.4.queries
  22.8 0.8 attend.6
  23.5 1.0 %collective-permute-start.5 = (bf16[256,256]{1,0:T(8,128)(2,1)S(1)}, bf16[256,256]{1,0:T(8,128)(2,1)S(1)}, u32[]{:S(2)}, u32[]{:S(2)}) collective-permute-start(bf16[256,256]{1,0:T(8,128)(2,1)S(1)} %attend.6), channel_id=1, source_target_pairs={{0,4},{1,5},{2,6},{3,7},{4,0},{5,1},{6,2},{7,3},{8,12},{9,13},{10,... | collective-permute-start | bytes 393224 | tf_op jit(solution)/shard_map/ppermute | solution.py:264
  24.5 0.8 attend.7
  26.0 6.6 %collective-permute-done.3 = bf16[256,256]{1,0:T(8,128)(2,1)S(1)} collective-permute-done((bf16[256,256]{1,0:T(8,128)(2,1)S(1)}, bf16[256,256]{1,0:T(8,128)(2,1)S(1)}, u32[]{:S(2)}, u32[]{:S(2)}) %collective-permute-start.3) | collective-permute-done | bytes 131104 | tf_op jit(solution)/shard_map/ppermute | solution.py:264
  32.6 1.6 %collective-permute-start.6 = (bf16[256,256]{1,0:T(8,128)(2,1)S(1)}, bf16[256,256]{1,0:T(8,128)(2,1)S(1)}, u32[]{:S(2)}, u32[]{:S(2)}) collective-permute-start(bf16[256,256]{1,0:T(8,128)(2,1)S(1)} %select_select_fusion.refs_3_), channel_id=1, source_target_pairs={{0,2},{1,3},{2,0},{3,1},{4,6},{5,7},{6,4},{7,5},{8,10},{9,11},{10,... | collective-permute-start | bytes 393224 | tf_op jit(solution)/shard_map/ppermute | solution.py:264
  34.2 0.0 collective-permute-start.7
  34.2 0.7 collective-permute-start.8
  34.8 0.1 copy.10.choice
  35.0 0.2 copy.11.router
  35.2 0.1 pad_add_fusion.ids.refs_0_
  35.3 1.4 %route.1 = (bf16[4,192,256]{2,1,0:T(8,128)(2,1)S(1)}, bf16[4,256,192]{2,1,0:T(8,128)(2,1)S(1)}, bf16[4,256,192]{2,1,0:T(8,128)(2,1)S(1)}) custom-call(s32[2]{0:T(128)S(1)} %pad_add_fusion.ids.refs_0_, s32[256,2]{1,0:T(8,128)S(1)} %copy.10.choice, s32[2,256]{1,0:T(2,128)S(1)} %bitcast.54), custom_call_target="tpu_custom_call" | custom-call | tf_op jit(solution)/shard_map/route/pallas_call | solution.py:83
  36.6 1.5 %collective-permute-done.6.refs_4_ = bf16[256,256]{1,0:T(8,128)(2,1)S(1)} collective-permute-done((bf16[256,256]{1,0:T(8,128)(2,1)S(1)}, bf16[256,256]{1,0:T(8,128)(2,1)S(1)}, u32[]{:S(2)}, u32[]{:S(2)}) %collective-permute-start.6) | collective-permute-done | bytes 131104 | tf_op jit(solution)/shard_map/ppermute | solution.py:264
  38.1 1.8 %collective-permute-done.8.refs_6_ = bf16[256,256]{1,0:T(8,128)(2,1)S(1)} collective-permute-done((bf16[256,256]{1,0:T(8,128)(2,1)S(1)}, bf16[256,256]{1,0:T(8,128)(2,1)S(1)}, u32[]{:S(2)}, u32[]{:S(2)}) %collective-permute-start.8) | collective-permute-done | bytes 131104 | tf_op jit(solution)/shard_map/ppermute | solution.py:264
  40.0 0.0 copy-start
  40.0 0.0 copy-start.1
  40.0 1.6 %state.1 = (bf16[256,1024]{1,0:T(8,128)(2,1)S(1)}, bf16[192,512]{1,0:T(8,128)(2,1)S(1)}, bf16[192,512]{1,0:T(8,128)(2,1)S(1)}, bf16[192,512]{1,0:T(8,128)(2,1)S(1)}) custom-call(s32[2]{0:T(128)S(1)} %pad_add_fusion.ids.refs_0_, bf16[256,1024]{1,0:T(8,128)(2,1)S(1)} %copy-done.5, bf16[4,192,256]{2,1,0:T(8,128)(2,1)S(1)} %get-tuple-element.24.refs_2_.dispatch, ...), custom_call_target="tpu_custom_call" | custom-call | tf_op jit(solution)/shard_map/state/pallas_call | solution.py:115
  41.6 2.6 %collective-permute-start.24 = (bf16[192,512]{1,0:T(8,128)(2,1)S(1)}, bf16[192,512]{1,0:T(8,128)(2,1)S(1)}, u32[]{:S(2)}, u32[]{:S(2)}) collective-permute-start(bf16[192,512]{1,0:T(8,128)(2,1)S(1)} %get-tuple-element.40), channel_id=1, source_target_pairs={{0,12},{1,13},{2,14},{3,15},{4,8},{5,9},{6,10},{7,11},{8,4},{9,5},... | collective-permute-start | bytes 589832 | tf_op jit(solution)/shard_map/ppermute | solution.py:264
  44.2 1.8 %collective-permute-start.14 = (bf16[192,512]{1,0:T(8,128)(2,1)S(1)}, bf16[192,512]{1,0:T(8,128)(2,1)S(1)}, u32[]{:S(2)}, u32[]{:S(2)}) collective-permute-start(bf16[192,512]{1,0:T(8,128)(2,1)S(1)} %get-tuple-element.34), channel_id=1, source_target_pairs={{0,4},{1,5},{2,6},{3,7},{4,0},{5,1},{6,2},{7,3},{8,12},{9,13},{10,... | collective-permute-start | bytes 589832 | tf_op jit(solution)/shard_map/ppermute | solution.py:264
  46.1 1.0 %home.1 = (bf16[192,512]{1,0:T(8,128)(2,1)S(1)}, bf16[192,512]{1,0:T(8,128)(2,1)S(1)}, f32[256,2]{1,0:T(8,128)S(1)}, f32[256,256]{1,0:T(8,128)S(1)}) custom-call(s32[2]{0:T(128)S(1)} %pad_add_fusion.ids.refs_0_, bf16[256,1024]{1,0:T(8,128)(2,1)S(1)} %get-tuple-element.25.state, bf16[4,192,256]{2,1,0:T(8,128)(2,1)S(1)} %get-tuple-element.24.refs_2_.dispatch, ...), custom_call_target="tpu_custom_call" | custom-call | tf_op jit(solution)/shard_map/home/pallas_call | solution.py:144
  47.1 3.7 %expert.4 = (f32[2,192,256]{2,1,0:T(8,128)S(1)}, bf16[2,192,256]{2,1,0:T(8,128)(2,1)S(1)}) custom-call(s32[2]{0:T(128)S(1)} %pad_add_fusion.ids.refs_0_, bf16[192,512]{1,0:T(8,128)(2,1)S(1)} %get-tuple-element.30.mine, bf16[192,512]{1,0:T(8,128)(2,1)S(1)} %get-tuple-element.31.other, bf16[1024,1024]{1,0:T(8,128)(2,1)S(1)} %bitcast.42, ...), custom_call_target="tpu_custom_call" | custom-call | tf_op jit(solution)/shard_map/expert/pallas_call | solution.py:192
  50.8 0.1 collective-permute-start.12
  50.9 0.4 collective-permute-done.24.mine
  51.3 0.1 collective-permute-start.25
  51.4 9.6 %collective-permute-done.19.mine = bf16[192,512]{1,0:T(8,128)(2,1)S(1)} collective-permute-done((bf16[192,512]{1,0:T(8,128)(2,1)S(1)}, bf16[192,512]{1,0:T(8,128)(2,1)S(1)}, u32[]{:S(2)}, u32[]{:S(2)}) %collective-permute-start.19) | collective-permute-done | bytes 196640 | tf_op jit(solution)/shard_map/ppermute | solution.py:264
  61.0 0.5 collective-permute-start.15
  61.5 0.1 add_convert_fusion.3
  61.6 3.7 %expert.7 = (f32[2,192,256]{2,1,0:T(8,128)S(1)}, bf16[2,192,256]{2,1,0:T(8,128)(2,1)S(1)}) custom-call(s32[2]{0:T(128)S(1)} %pad_add_fusion.ids.refs_0_, bf16[192,512]{1,0:T(8,128)(2,1)S(1)} %collective-permute-done.24.mine, bf16[192,512]{1,0:T(8,128)(2,1)S(1)} %collective-permute-done.25.other, bf16[1024,1024]{1,0:T(8,128)(2,1)S(1)} %bitcast.43, ...), custom_call_target="tpu_custom_call" | custom-call | tf_op jit(solution)/shard_map/expert/pallas_call | solution.py:192
  65.3 0.1 collective-permute-start.26
  65.4 1.3 %collective-permute-start.13 = (bf16[192,256]{1,0:T(8,128)(2,1)S(1)}, bf16[192,256]{1,0:T(8,128)(2,1)S(1)}, u32[]{:S(2)}, u32[]{:S(2)}) collective-permute-start(bf16[192,256]{1,0:T(8,128)(2,1)S(1)} %get-tuple-element.57), channel_id=1, source_target_pairs={{0,2},{1,3},{2,0},{3,1},{4,6},{5,7},{6,4},{7,5},{8,10},{9,11},{10,... | collective-permute-start | bytes 294920 | tf_op jit(solution)/shard_map/ppermute | solution.py:264
  66.7 3.7 %expert.6 = (f32[2,192,256]{2,1,0:T(8,128)S(1)}, bf16[2,192,256]{2,1,0:T(8,128)(2,1)S(1)}) custom-call(s32[2]{0:T(128)S(1)} %pad_add_fusion.ids.refs_0_, bf16[192,512]{1,0:T(8,128)(2,1)S(1)} %collective-permute-done.19.mine, bf16[192,512]{1,0:T(8,128)(2,1)S(1)} %collective-permute-done.20.other, bf16[1024,1024]{1,0:T(8,128)(2,1)S(1)} %bitcast.44, ...), custom_call_target="tpu_custom_call" | custom-call | tf_op jit(solution)/shard_map/expert/pallas_call | solution.py:192
  70.3 0.1 collective-permute-start.21
  70.5 3.7 %expert.5 = (f32[2,192,256]{2,1,0:T(8,128)S(1)}, bf16[2,192,256]{2,1,0:T(8,128)(2,1)S(1)}) custom-call(s32[2]{0:T(128)S(1)} %pad_add_fusion.ids.refs_0_, bf16[192,512]{1,0:T(8,128)(2,1)S(1)} %collective-permute-done.14.mine, bf16[192,512]{1,0:T(8,128)(2,1)S(1)} %collective-permute-done.15.other, bf16[1024,1024]{1,0:T(8,128)(2,1)S(1)} %bitcast.45, ...), custom_call_target="tpu_custom_call" | custom-call | tf_op jit(solution)/shard_map/expert/pallas_call | solution.py:192
  74.2 0.5 collective-permute-start.16
  74.7 1.7 %collective-permute-start.27 = (bf16[192,256]{1,0:T(8,128)(2,1)S(1)}, bf16[192,256]{1,0:T(8,128)(2,1)S(1)}, u32[]{:S(2)}, u32[]{:S(2)}) collective-permute-start(bf16[192,256]{1,0:T(8,128)(2,1)S(1)} %get-tuple-element.52), channel_id=1, source_target_pairs={{0,12},{1,13},{2,14},{3,15},{4,8},{5,9},{6,10},{7,11},{8,4},{9,5},... | collective-permute-start | bytes 294920 | tf_op jit(solution)/shard_map/ppermute | solution.py:264
  76.4 2.5 %collective-permute-start.28 = (bf16[192,256]{1,0:T(8,128)(2,1)S(1)}, bf16[192,256]{1,0:T(8,128)(2,1)S(1)}, u32[]{:S(2)}, u32[]{:S(2)}) collective-permute-start(bf16[192,256]{1,0:T(8,128)(2,1)S(1)} %get-tuple-element.51), channel_id=1, source_target_pairs={{0,14},{1,15},{2,12},{3,13},{4,10},{5,11},{6,8},{7,9},{8,6},{9,7},... | collective-permute-start | bytes 294920 | tf_op jit(solution)/shard_map/ppermute | solution.py:264
  79.0 0.1 collective-permute-start.17
  79.1 2.7 %collective-permute-start.22 = (bf16[192,256]{1,0:T(8,128)(2,1)S(1)}, bf16[192,256]{1,0:T(8,128)(2,1)S(1)}, u32[]{:S(2)}, u32[]{:S(2)}) collective-permute-start(bf16[192,256]{1,0:T(8,128)(2,1)S(1)} %get-tuple-element.54), channel_id=1, source_target_pairs={{0,8},{1,9},{2,10},{3,11},{4,12},{5,13},{6,14},{7,15},{8,0},{9,1},... | collective-permute-start | bytes 294920 | tf_op jit(solution)/shard_map/ppermute | solution.py:264
  81.8 0.9 collective-permute-start.23
  82.7 4.1 %collective-permute-done.17.refs_0_ = bf16[192,256]{1,0:T(8,128)(2,1)S(1)} collective-permute-done((bf16[192,256]{1,0:T(8,128)(2,1)S(1)}, bf16[192,256]{1,0:T(8,128)(2,1)S(1)}, u32[]{:S(2)}, u32[]{:S(2)}) %collective-permute-start.17) | collective-permute-done | bytes 98336 | tf_op jit(solution)/shard_map/ppermute | solution.py:264
  86.8 0.5 collective-permute-start.18
  87.3 0.1 slice_bitcast_fusion
  87.4 0.2 combine.4.base
  87.6 7.8 %collective-permute-done.18.refs_1_ = bf16[192,256]{1,0:T(8,128)(2,1)S(1)} collective-permute-done((bf16[192,256]{1,0:T(8,128)(2,1)S(1)}, bf16[192,256]{1,0:T(8,128)(2,1)S(1)}, u32[]{:S(2)}, u32[]{:S(2)}) %collective-permute-start.18) | collective-permute-done | bytes 98336 | tf_op jit(solution)/shard_map/ppermute | solution.py:264
  95.4 0.2 combine.5.base
  95.7 0.2 combine.6.base
  95.9 0.9 combine.7
  (43 shorter events, 0.3 us)
Async XLA Ops:
  0.0 20.8 %copy-start.3 = (bf16[1,2,512,256]{3,2,1,0:T(8,128)(2,1)S(1)}, bf16[1,2,512,256]{3,2,1,0:T(8,128)(2,1)}, u32[]{:S(2)}) copy-start(bf16[1,2,512,256]{3,2,1,0:T(8,128)(2,1)} %param.10) | copy-start | bytes 1572868
  0.0 15.1 %collective-permute-start.9 = (bf16[256,1024]{1,0:T(8,128)(2,1)}, bf16[256,1024]{1,0:T(8,128)(2,1)S(1)}, u32[]{:S(2)}, u32[]{:S(2)}) collective-permute-start(bf16[256,1024]{1,0:T(8,128)(2,1)} %refs_7_.1), channel_id=1, source_target_pairs={{0,2},{1,3},{2,0},{3,1},{4,6},{5,7},{6,4},{7,5},{8,10},{9,11},{10,... | collective-permute-start | bytes 1572872 | tf_op jit(solution)/shard_map/ppermute | solution.py:264
  2.9 1.0 %copy-start.4 = (bf16[256,1024]{1,0:T(8,128)(2,1)S(1)}, bf16[256,1024]{1,0:T(8,128)(2,1)}, u32[]{:S(2)}) copy-start(bf16[256,1024]{1,0:T(8,128)(2,1)} %refs_1_.1) | copy-start | bytes 1572868
  4.0 1.0 %copy-start.6 = (bf16[1024,256]{1,0:T(8,128)(2,1)S(1)}, bf16[1024,256]{1,0:T(8,128)(2,1)}, u32[]{:S(2)}) copy-start(bf16[1024,256]{1,0:T(8,128)(2,1)} %weight.1) | copy-start | bytes 1572868
  5.0 29.8 %copy-start.8 = (s32[256,2]{0,1:T(2,128)S(1)}, s32[256,2]{0,1:T(2,128)}, u32[]{:S(2)}) copy-start(s32[256,2]{0,1:T(2,128)} %param.15) | copy-start | bytes 6148
  5.0 29.9 %copy-start.9 = (bf16[1024,4]{0,1:T(4,128)(2,1)S(1)}, bf16[1024,4]{0,1:T(4,128)(2,1)}, u32[]{:S(2)}) copy-start(bf16[1024,4]{0,1:T(4,128)(2,1)} %param.14) | copy-start | bytes 24580
  5.3 9.7 %collective-permute-start = (bf16[256,256]{1,0:T(8,128)(2,1)S(1)}, bf16[256,256]{1,0:T(8,128)(2,1)S(1)}, u32[]{:S(2)}, u32[]{:S(2)}) collective-permute-start(bf16[256,256]{1,0:T(8,128)(2,1)S(1)} %query.1.queries), channel_id=1, source_target_pairs={{0,12},{1,13},{2,14},{3,15},{4,8},{5,9},{6,10},{7,11},{8,4},{9,5},... | collective-permute-start | bytes 393224 | tf_op jit(solution)/shard_map/ppermute | solution.py:264
  9.0 11.8 %collective-permute-start.2 = (bf16[256,256]{1,0:T(8,128)(2,1)S(1)}, bf16[256,256]{1,0:T(8,128)(2,1)S(1)}, u32[]{:S(2)}, u32[]{:S(2)}) collective-permute-start(bf16[256,256]{1,0:T(8,128)(2,1)S(1)} %query.1.queries), channel_id=1, source_target_pairs={{0,8},{1,9},{2,10},{3,11},{4,12},{5,13},{6,14},{7,15},{8,0},{9,1},... | collective-permute-start | bytes 393224 | tf_op jit(solution)/shard_map/ppermute | solution.py:264
  9.0 13.8 %collective-permute-start.4 = (bf16[256,256]{1,0:T(8,128)(2,1)S(1)}, bf16[256,256]{1,0:T(8,128)(2,1)S(1)}, u32[]{:S(2)}, u32[]{:S(2)}) collective-permute-start(bf16[256,256]{1,0:T(8,128)(2,1)S(1)} %query.1.queries), channel_id=1, source_target_pairs={{0,4},{1,5},{2,6},{3,7},{4,0},{5,1},{6,2},{7,3},{8,12},{9,13},{10,... | collective-permute-start | bytes 393224 | tf_op jit(solution)/shard_map/ppermute | solution.py:264
  9.8 30.2 %collective-permute-start.10 = (bf16[256,1024]{1,0:T(8,128)(2,1)}, bf16[256,1024]{1,0:T(8,128)(2,1)S(1)}, u32[]{:S(2)}, u32[]{:S(2)}) collective-permute-start(bf16[256,1024]{1,0:T(8,128)(2,1)} %refs_7_.1), channel_id=1, source_target_pairs={{0,1},{1,0},{2,3},{3,2},{4,5},{5,4},{6,7},{7,6},{8,9},{9,8},{10,11... | collective-permute-start | bytes 1572872 | tf_op jit(solution)/shard_map/ppermute | solution.py:264
  15.1 24.9 %collective-permute-start.11 = (bf16[256,1024]{1,0:T(8,128)(2,1)S(1)}, bf16[256,1024]{1,0:T(8,128)(2,1)S(1)}, u32[]{:S(2)}, u32[]{:S(2)}) collective-permute-start(bf16[256,1024]{1,0:T(8,128)(2,1)S(1)} %collective-permute-done.9.refs_8_), channel_id=1, source_target_pairs={{0,1},{1,0},{2,3},{3,2},{4,5},{5,4},{6,7},{7,6},{8,9},{9,8},{10,11... | collective-permute-start | bytes 1572872 | tf_op jit(solution)/shard_map/ppermute | solution.py:264
  15.1 1.0 %copy-start.2 = (bf16[1,2,512,256]{3,2,1,0:T(8,128)(2,1)S(1)}, bf16[1,2,512,256]{3,2,1,0:T(8,128)(2,1)}, u32[]{:S(2)}) copy-start(bf16[1,2,512,256]{3,2,1,0:T(8,128)(2,1)} %param.10) | copy-start | bytes 1572868
  16.1 23.8 %copy-start.5 = (bf16[256,1024]{1,0:T(8,128)(2,1)S(1)}, bf16[256,1024]{1,0:T(8,128)(2,1)}, u32[]{:S(2)}) copy-start(bf16[256,1024]{1,0:T(8,128)(2,1)} %refs_1_.1) | copy-start | bytes 1572868
  16.1 23.8 %copy-start.7 = (bf16[256,1024]{1,0:T(8,128)(2,1)S(1)}, bf16[256,1024]{1,0:T(8,128)(2,1)}, u32[]{:S(2)}) copy-start(bf16[256,1024]{1,0:T(8,128)(2,1)} %refs_7_.1) | copy-start | bytes 1572868
  16.9 9.1 %collective-permute-start.1 = (bf16[256,256]{1,0:T(8,128)(2,1)S(1)}, bf16[256,256]{1,0:T(8,128)(2,1)S(1)}, u32[]{:S(2)}, u32[]{:S(2)}) collective-permute-start(bf16[256,256]{1,0:T(8,128)(2,1)S(1)} %attend.4), channel_id=1, source_target_pairs={{0,12},{1,13},{2,14},{3,15},{4,8},{5,9},{6,10},{7,11},{8,4},{9,5},... | collective-permute-start | bytes 393224 | tf_op jit(solution)/shard_map/ppermute | solution.py:264
  21.6 11.0 %collective-permute-start.3 = (bf16[256,256]{1,0:T(8,128)(2,1)S(1)}, bf16[256,256]{1,0:T(8,128)(2,1)S(1)}, u32[]{:S(2)}, u32[]{:S(2)}) collective-permute-start(bf16[256,256]{1,0:T(8,128)(2,1)S(1)} %attend.5), channel_id=1, source_target_pairs={{0,8},{1,9},{2,10},{3,11},{4,12},{5,13},{6,14},{7,15},{8,0},{9,1},... | collective-permute-start | bytes 393224 | tf_op jit(solution)/shard_map/ppermute | solution.py:264
  23.5 9.0 %collective-permute-start.5 = (bf16[256,256]{1,0:T(8,128)(2,1)S(1)}, bf16[256,256]{1,0:T(8,128)(2,1)S(1)}, u32[]{:S(2)}, u32[]{:S(2)}) collective-permute-start(bf16[256,256]{1,0:T(8,128)(2,1)S(1)} %attend.6), channel_id=1, source_target_pairs={{0,4},{1,5},{2,6},{3,7},{4,0},{5,1},{6,2},{7,3},{8,12},{9,13},{10,... | collective-permute-start | bytes 393224 | tf_op jit(solution)/shard_map/ppermute | solution.py:264
  32.6 5.5 %collective-permute-start.6 = (bf16[256,256]{1,0:T(8,128)(2,1)S(1)}, bf16[256,256]{1,0:T(8,128)(2,1)S(1)}, u32[]{:S(2)}, u32[]{:S(2)}) collective-permute-start(bf16[256,256]{1,0:T(8,128)(2,1)S(1)} %select_select_fusion.refs_3_), channel_id=1, source_target_pairs={{0,2},{1,3},{2,0},{3,1},{4,6},{5,7},{6,4},{7,5},{8,10},{9,11},{10,... | collective-permute-start | bytes 393224 | tf_op jit(solution)/shard_map/ppermute | solution.py:264
  34.2 4.0 %collective-permute-start.7 = (bf16[256,256]{1,0:T(8,128)(2,1)S(1)}, bf16[256,256]{1,0:T(8,128)(2,1)S(1)}, u32[]{:S(2)}, u32[]{:S(2)}) collective-permute-start(bf16[256,256]{1,0:T(8,128)(2,1)S(1)} %select_select_fusion.refs_3_), channel_id=1, source_target_pairs={{0,1},{1,0},{2,3},{3,2},{4,5},{5,4},{6,7},{7,6},{8,9},{9,8},{10,11... | collective-permute-start | bytes 393224 | tf_op jit(solution)/shard_map/ppermute | solution.py:264
  34.2 5.8 %collective-permute-start.8 = (bf16[256,256]{1,0:T(8,128)(2,1)S(1)}, bf16[256,256]{1,0:T(8,128)(2,1)S(1)}, u32[]{:S(2)}, u32[]{:S(2)}) collective-permute-start(bf16[256,256]{1,0:T(8,128)(2,1)S(1)} %select_select_fusion.refs_3_), channel_id=1, source_target_pairs={{0,3},{1,2},{2,1},{3,0},{4,7},{5,6},{6,5},{7,4},{8,11},{9,10},{10,... | collective-permute-start | bytes 393224 | tf_op jit(solution)/shard_map/ppermute | solution.py:264
  40.0 7.1 %copy-start = (bf16[1,1024,1024]{2,1,0:T(8,128)(2,1)S(1)}, bf16[1,1024,1024]{2,1,0:T(8,128)(2,1)}, u32[]{:S(2)}) copy-start(bf16[1,1024,1024]{2,1,0:T(8,128)(2,1)} %param.16) | copy-start | bytes 6291460
  40.0 7.1 %copy-start.1 = (bf16[1,1024,1024]{2,1,0:T(8,128)(2,1)S(1)}, bf16[1,1024,1024]{2,1,0:T(8,128)(2,1)}, u32[]{:S(2)}) copy-start(bf16[1,1024,1024]{2,1,0:T(8,128)(2,1)} %param.17) | copy-start | bytes 6291460
  41.6 9.7 %collective-permute-start.24 = (bf16[192,512]{1,0:T(8,128)(2,1)S(1)}, bf16[192,512]{1,0:T(8,128)(2,1)S(1)}, u32[]{:S(2)}, u32[]{:S(2)}) collective-permute-start(bf16[192,512]{1,0:T(8,128)(2,1)S(1)} %get-tuple-element.40), channel_id=1, source_target_pairs={{0,12},{1,13},{2,14},{3,15},{4,8},{5,9},{6,10},{7,11},{8,4},{9,5},... | collective-permute-start | bytes 589832 | tf_op jit(solution)/shard_map/ppermute | solution.py:264
  44.2 16.8 %collective-permute-start.19 = (bf16[192,512]{1,0:T(8,128)(2,1)S(1)}, bf16[192,512]{1,0:T(8,128)(2,1)S(1)}, u32[]{:S(2)}, u32[]{:S(2)}) collective-permute-start(bf16[192,512]{1,0:T(8,128)(2,1)S(1)} %get-tuple-element.37), channel_id=1, source_target_pairs={{0,8},{1,9},{2,10},{3,11},{4,12},{5,13},{6,14},{7,15},{8,0},{9,1},... | collective-permute-start | bytes 589832 | tf_op jit(solution)/shard_map/ppermute | solution.py:264
  44.2 16.8 %collective-permute-start.14 = (bf16[192,512]{1,0:T(8,128)(2,1)S(1)}, bf16[192,512]{1,0:T(8,128)(2,1)S(1)}, u32[]{:S(2)}, u32[]{:S(2)}) collective-permute-start(bf16[192,512]{1,0:T(8,128)(2,1)S(1)} %get-tuple-element.34), channel_id=1, source_target_pairs={{0,4},{1,5},{2,6},{3,7},{4,0},{5,1},{6,2},{7,3},{8,12},{9,13},{10,... | collective-permute-start | bytes 589832 | tf_op jit(solution)/shard_map/ppermute | solution.py:264
  50.8 10.7 %collective-permute-start.12 = (bf16[2,192,256]{2,1,0:T(8,128)(2,1)S(1)}, bf16[2,192,256]{2,1,0:T(8,128)(2,1)S(1)}, u32[]{:S(2)}, u32[]{:S(2)}) collective-permute-start(bf16[2,192,256]{2,1,0:T(8,128)(2,1)S(1)} %get-tuple-element.33), channel_id=1, source_target_pairs={{0,1},{1,0},{2,3},{3,2},{4,5},{5,4},{6,7},{7,6},{8,9},{9,8},{10,11... | collective-permute-start | bytes 589832 | tf_op jit(solution)/shard_map/ppermute | solution.py:264
  51.3 10.3 %collective-permute-start.25 = (bf16[192,512]{1,0:T(8,128)(2,1)S(1)}, bf16[192,512]{1,0:T(8,128)(2,1)S(1)}, u32[]{:S(2)}, u32[]{:S(2)}) collective-permute-start(bf16[192,512]{1,0:T(8,128)(2,1)S(1)} %collective-permute-done.24.mine), channel_id=1, source_target_pairs={{0,1},{1,0},{2,3},{3,2},{4,5},{5,4},{6,7},{7,6},{8,9},{9,8},{10,11... | collective-permute-start | bytes 589832 | tf_op jit(solution)/shard_map/ppermute | solution.py:264
  61.0 5.6 %collective-permute-start.20 = (bf16[192,512]{1,0:T(8,128)(2,1)S(1)}, bf16[192,512]{1,0:T(8,128)(2,1)S(1)}, u32[]{:S(2)}, u32[]{:S(2)}) collective-permute-start(bf16[192,512]{1,0:T(8,128)(2,1)S(1)} %collective-permute-done.19.mine), channel_id=1, source_target_pairs={{0,1},{1,0},{2,3},{3,2},{4,5},{5,4},{6,7},{7,6},{8,9},{9,8},{10,11... | collective-permute-start | bytes 589832 | tf_op jit(solution)/shard_map/ppermute | solution.py:264
  61.0 9.5 %collective-permute-start.15 = (bf16[192,512]{1,0:T(8,128)(2,1)S(1)}, bf16[192,512]{1,0:T(8,128)(2,1)S(1)}, u32[]{:S(2)}, u32[]{:S(2)}) collective-permute-start(bf16[192,512]{1,0:T(8,128)(2,1)S(1)} %collective-permute-done.14.mine), channel_id=1, source_target_pairs={{0,1},{1,0},{2,3},{3,2},{4,5},{5,4},{6,7},{7,6},{8,9},{9,8},{10,11... | collective-permute-start | bytes 589832 | tf_op jit(solution)/shard_map/ppermute | solution.py:264
  65.3 9.4 %collective-permute-start.26 = (bf16[2,192,256]{2,1,0:T(8,128)(2,1)S(1)}, bf16[2,192,256]{2,1,0:T(8,128)(2,1)S(1)}, u32[]{:S(2)}, u32[]{:S(2)}) collective-permute-start(bf16[2,192,256]{2,1,0:T(8,128)(2,1)S(1)} %get-tuple-element.42), channel_id=1, source_target_pairs={{0,1},{1,0},{2,3},{3,2},{4,5},{5,4},{6,7},{7,6},{8,9},{9,8},{10,11... | collective-permute-start | bytes 589832 | tf_op jit(solution)/shard_map/ppermute | solution.py:264
  65.4 16.4 %collective-permute-start.13 = (bf16[192,256]{1,0:T(8,128)(2,1)S(1)}, bf16[192,256]{1,0:T(8,128)(2,1)S(1)}, u32[]{:S(2)}, u32[]{:S(2)}) collective-permute-start(bf16[192,256]{1,0:T(8,128)(2,1)S(1)} %get-tuple-element.57), channel_id=1, source_target_pairs={{0,2},{1,3},{2,0},{3,1},{4,6},{5,7},{6,4},{7,5},{8,10},{9,11},{10,... | collective-permute-start | bytes 294920 | tf_op jit(solution)/shard_map/ppermute | solution.py:264
  70.3 8.7 %collective-permute-start.21 = (bf16[2,192,256]{2,1,0:T(8,128)(2,1)S(1)}, bf16[2,192,256]{2,1,0:T(8,128)(2,1)S(1)}, u32[]{:S(2)}, u32[]{:S(2)}) collective-permute-start(bf16[2,192,256]{2,1,0:T(8,128)(2,1)S(1)} %get-tuple-element.39), channel_id=1, source_target_pairs={{0,1},{1,0},{2,3},{3,2},{4,5},{5,4},{6,7},{7,6},{8,9},{9,8},{10,11... | collective-permute-start | bytes 589832 | tf_op jit(solution)/shard_map/ppermute | solution.py:264
  74.2 4.7 %collective-permute-start.16 = (bf16[2,192,256]{2,1,0:T(8,128)(2,1)S(1)}, bf16[2,192,256]{2,1,0:T(8,128)(2,1)S(1)}, u32[]{:S(2)}, u32[]{:S(2)}) collective-permute-start(bf16[2,192,256]{2,1,0:T(8,128)(2,1)S(1)} %get-tuple-element.36), channel_id=1, source_target_pairs={{0,1},{1,0},{2,3},{3,2},{4,5},{5,4},{6,7},{7,6},{8,9},{9,8},{10,11... | collective-permute-start | bytes 589832 | tf_op jit(solution)/shard_map/ppermute | solution.py:264
  74.7 21.2 %collective-permute-start.27 = (bf16[192,256]{1,0:T(8,128)(2,1)S(1)}, bf16[192,256]{1,0:T(8,128)(2,1)S(1)}, u32[]{:S(2)}, u32[]{:S(2)}) collective-permute-start(bf16[192,256]{1,0:T(8,128)(2,1)S(1)} %get-tuple-element.52), channel_id=1, source_target_pairs={{0,12},{1,13},{2,14},{3,15},{4,8},{5,9},{6,10},{7,11},{8,4},{9,5},... | collective-permute-start | bytes 294920 | tf_op jit(solution)/shard_map/ppermute | solution.py:264
  76.4 19.5 %collective-permute-start.28 = (bf16[192,256]{1,0:T(8,128)(2,1)S(1)}, bf16[192,256]{1,0:T(8,128)(2,1)S(1)}, u32[]{:S(2)}, u32[]{:S(2)}) collective-permute-start(bf16[192,256]{1,0:T(8,128)(2,1)S(1)} %get-tuple-element.51), channel_id=1, source_target_pairs={{0,14},{1,15},{2,12},{3,13},{4,10},{5,11},{6,8},{7,9},{8,6},{9,7},... | collective-permute-start | bytes 294920 | tf_op jit(solution)/shard_map/ppermute | solution.py:264
  79.0 7.9 %collective-permute-start.17 = (bf16[192,256]{1,0:T(8,128)(2,1)S(1)}, bf16[192,256]{1,0:T(8,128)(2,1)S(1)}, u32[]{:S(2)}, u32[]{:S(2)}) collective-permute-start(bf16[192,256]{1,0:T(8,128)(2,1)S(1)} %get-tuple-element.56), channel_id=1, source_target_pairs={{0,4},{1,5},{2,6},{3,7},{4,0},{5,1},{6,2},{7,3},{8,12},{9,13},{10,... | collective-permute-start | bytes 294920 | tf_op jit(solution)/shard_map/ppermute | solution.py:264
  79.1 16.5 %collective-permute-start.22 = (bf16[192,256]{1,0:T(8,128)(2,1)S(1)}, bf16[192,256]{1,0:T(8,128)(2,1)S(1)}, u32[]{:S(2)}, u32[]{:S(2)}) collective-permute-start(bf16[192,256]{1,0:T(8,128)(2,1)S(1)} %get-tuple-element.54), channel_id=1, source_target_pairs={{0,8},{1,9},{2,10},{3,11},{4,12},{5,13},{6,14},{7,15},{8,0},{9,1},... | collective-permute-start | bytes 294920 | tf_op jit(solution)/shard_map/ppermute | solution.py:264
  81.8 13.8 %collective-permute-start.23 = (bf16[192,256]{1,0:T(8,128)(2,1)S(1)}, bf16[192,256]{1,0:T(8,128)(2,1)S(1)}, u32[]{:S(2)}, u32[]{:S(2)}) collective-permute-start(bf16[192,256]{1,0:T(8,128)(2,1)S(1)} %get-tuple-element.53), channel_id=1, source_target_pairs={{0,10},{1,11},{2,8},{3,9},{4,14},{5,15},{6,12},{7,13},{8,2},{9,3},... | collective-permute-start | bytes 294920 | tf_op jit(solution)/shard_map/ppermute | solution.py:264
  86.8 8.6 %collective-permute-start.18 = (bf16[192,256]{1,0:T(8,128)(2,1)S(1)}, bf16[192,256]{1,0:T(8,128)(2,1)S(1)}, u32[]{:S(2)}, u32[]{:S(2)}) collective-permute-start(bf16[192,256]{1,0:T(8,128)(2,1)S(1)} %get-tuple-element.55), channel_id=1, source_target_pairs={{0,6},{1,7},{2,4},{3,5},{4,2},{5,3},{6,0},{7,1},{8,14},{9,15},{10,... | collective-permute-start | bytes 294920 | tf_op jit(solution)/shard_map/ppermute | solution.py:264

commit v2 on v1

--- a/solution.py
+++ b/solution.py
@@ -9,6 +9,8 @@
 
 HEAD_DIM = 128
 DIRECT = 8
+CUTS = 4
+TILE = 256
 F32, BF16 = jnp.float32, jnp.bfloat16
 PARAMS = pltpu.CompilerParams(vmem_limit_bytes=40 * 2**20)
 SCALARS = pl.BlockSpec(memory_space=pltpu.SMEM)
@@ -19,8 +21,73 @@
     return lax.dot_general(a, b, (dims, ((), ())), preferred_element_type=F32)
 
 
-def query_kernel(tokens, weight, out):
-    out[...] = dot(tokens[...], weight[...]).astype(BF16)
+def in_hbm(value):
+    return pltpu.with_memory_space_constraint(value, pltpu.HBM)
+
+
+def query_kernel(tokens, weight, out, tokens_here, weight_here, sems):
+    features = tokens.shape[1]
+    depth = features // CUTS
+    copies = []
+    for i in range(CUTS):
+        part = pl.ds(i * depth, depth)
+        copies.append(
+            (
+                pltpu.make_async_copy(tokens.at[:, part], tokens_here.at[:, part], sems.at[0, i]),
+                pltpu.make_async_copy(weight.at[part, :], weight_here.at[part, :], sems.at[1, i]),
+            )
+        )
+    for pair in copies:
+        for copy in pair:
+            copy.start()
+    total = jnp.zeros(out.shape, F32)
+    for i, pair in enumerate(copies):
+        for copy in pair:
+            copy.wait()
+        part = slice(i * depth, (i + 1) * depth)
+        total += dot(tokens_here[:, part], weight_here[part, :])
+    out[...] = total.astype(BF16)
+
+
+def ask(tokens, weight):
+    return pl.pallas_call(
+        query_kernel,
+        in_specs=[pl.BlockSpec(memory_space=pltpu.HBM)] * 2,
+        out_specs=WHOLE,
+        out_shape=jax.ShapeDtypeStruct((tokens.shape[0], weight.shape[1]), BF16),
+        scratch_shapes=[
+            pltpu.VMEM(tokens.shape, BF16),
+            pltpu.VMEM(weight.shape, BF16),
+            pltpu.SemaphoreType.DMA((2, CUTS)),
+        ],
+        compiler_params=PARAMS,
+        name="query",
+    )(in_hbm(tokens), in_hbm(weight))
+
+
+def stage_kernel(source, out, sems):
+    copies = [
+        pltpu.make_async_copy(source.at[:, rows], out.at[:, rows], sems.at[i])
+        for i, rows in enumerate(
+            pl.ds(i * (source.shape[1] // CUTS), source.shape[1] // CUTS) for i in range(CUTS)
+        )
+    ]
+    for copy in copies:
+        copy.start()
+    for copy in copies:
+        copy.wait()
+
+
+def stage(source):
+    return pl.pallas_call(
+        stage_kernel,
+        in_specs=[pl.BlockSpec(memory_space=pltpu.HBM)],
+        out_specs=WHOLE,
+        out_shape=jax.ShapeDtypeStruct(source.shape, source.dtype),
+        scratch_shapes=[pltpu.SemaphoreType.DMA((CUTS,))],
+        compiler_params=PARAMS,
+        name="stage",
+    )(in_hbm(source))
 
 
 def attend_kernel(queries, source, out):
@@ -36,6 +103,15 @@
 
 def attend(queries, source, block):
     rows, width = queries.shape
+    if rows == block:
+        return pl.pallas_call(
+            attend_kernel,
+            in_specs=[WHOLE] * 2,
+            out_specs=WHOLE,
+            out_shape=jax.ShapeDtypeStruct((rows, width), BF16),
+            compiler_params=PARAMS,
+            name="attend",
+        )(queries, source)
     return pl.pallas_call(
         attend_kernel,
         grid=(rows // block,),
@@ -94,7 +170,7 @@
     )(ids, choice, choice.T)
 
 
-def state_kernel(count, away, *refs):
+def state_kernel(count, leave, *refs):
     ids, tokens, dispatch = refs[:3]
     contexts, weights = refs[3 : 3 + count], refs[3 + count : 3 + 2 * count]
     state = refs[3 + 2 * count]
@@ -103,21 +179,21 @@
     for context, weight in zip(contexts, weights):
         total += dot(context[...], weight[...])
     state[...] = total.astype(BF16)
-    half = state.shape[1] // 2
-    mine = state[:, pl.ds(pl.multiple_of((ids[1] & 1) * half, half), half)]
-    for out, k in zip(outs, away):
-        out[...] = dot(dispatch[k], mine).astype(BF16)
-
-
-def make_state(ids, tokens, dispatch, contexts, weights, away):
+    for out, (k, cuts) in zip(outs, leave):
+        width = out.shape[1]
+        at = (ids[1] & (cuts - 1)) * width
+        out[...] = dot(dispatch[k], state[:, pl.ds(pl.multiple_of(at, width), width)]).astype(BF16)
+
+
+def make_state(ids, tokens, dispatch, contexts, weights, leave):
     slots = dispatch.shape[1]
     features = tokens.shape[1]
     return pl.pallas_call(
-        functools.partial(state_kernel, len(contexts), away),
+        functools.partial(state_kernel, len(contexts), leave),
         in_specs=[SCALARS] + [WHOLE] * (2 + 2 * len(contexts)),
-        out_specs=[WHOLE] * (1 + len(away)),
+        out_specs=[WHOLE] * (1 + len(leave)),
         out_shape=[jax.ShapeDtypeStruct(tokens.shape, BF16)]
-        + [jax.ShapeDtypeStruct((slots, features // 2), BF16)] * len(away),
+        + [jax.ShapeDtypeStruct((slots, features // cuts), BF16) for _, cuts in leave],
         compiler_params=PARAMS,
         name="state",
     )(ids, tokens, dispatch, *contexts, *weights)
@@ -156,58 +232,44 @@
     )(ids, state, dispatch, router, choice)
 
 
-def expert_kernel(ids, mine, other, expand, shrink, keep, give, total):
-    step, steps = pl.program_id(0), pl.num_programs(0)
-    half = mine.shape[1]
-    core = ids[1] & 1
-    hidden = dot(mine[...], expand[pl.ds(pl.multiple_of(core * half, half), half), :])
-    hidden += dot(other[...], expand[pl.ds(pl.multiple_of((1 - core) * half, half), half), :])
-    hidden = jnp.maximum(hidden, 0.0).astype(BF16)
-    product = dot(hidden, shrink[...])
-
-    @pl.when(step == 0)
-    def _():
-        total[...] = product
-
-    @pl.when(step > 0)
-    def _():
-        total[...] += product
-
-    @pl.when(step == steps - 1)
-    def _():
-        parts = keep.shape[0]
-        width = keep.shape[2]
-        for j in range(parts):
-            at = (ids[1] ^ (2 * j)) * width
-            keep[j] = total[:, pl.ds(pl.multiple_of(at, width), width)]
-            at = (ids[1] ^ (2 * j) ^ 1) * width
-            give[j] = total[:, pl.ds(pl.multiple_of(at, width), width)].astype(BF16)
-
-
-def run_expert(ids, mine, other, expand, shrink, parts):
-    rows, half = mine.shape
+def expert_kernel(order, *refs):
+    ids, pieces = refs[0], refs[1 : 1 + len(order)]
+    expand, shrink, keep, give, hidden = refs[1 + len(order) :]
+    cuts = len(order)
+    units = expand.shape[1]
+    tile = min(TILE, units)
+    for at in range(0, units, tile):
+        total = jnp.zeros((hidden.shape[0], tile), F32)
+        for index, piece in zip(order, pieces):
+            width = piece.shape[1]
+            rows = pl.ds(pl.multiple_of(((ids[1] & (cuts - 1)) ^ index) * width, width), width)
+            total += dot(piece[...], expand[rows, at : at + tile])
+        hidden[:, at : at + tile] = jnp.maximum(total, 0.0).astype(BF16)
+    width = keep.shape[2]
+    for j in range(keep.shape[0]):
+        at = pl.multiple_of((ids[1] ^ (2 * j) ^ 1) * width, width)
+        give[j] = dot(hidden[...], shrink[:, pl.ds(at, width)]).astype(BF16)
+    for j in range(keep.shape[0]):
+        at = pl.multiple_of((ids[1] ^ (2 * j)) * width, width)
+        keep[j] = dot(hidden[...], shrink[:, pl.ds(at, width)])
+
+
+def run_expert(ids, order, pieces, expand, shrink, parts):
+    rows = pieces[0].shape[0]
     features, units = expand.shape
-    tile = min(256, units)
     width = features // (2 * parts)
     return pl.pallas_call(
-        expert_kernel,
-        grid=(units // tile,),
-        in_specs=[
-            SCALARS,
-            pl.BlockSpec((rows, half), lambda i: (0, 0)),
-            pl.BlockSpec((rows, half), lambda i: (0, 0)),
-            pl.BlockSpec((features, tile), lambda i: (0, i)),
-            pl.BlockSpec((tile, features), lambda i: (i, 0)),
-        ],
-        out_specs=[pl.BlockSpec((parts, rows, width), lambda i: (0, 0, 0))] * 2,
+        functools.partial(expert_kernel, tuple(order)),
+        in_specs=[SCALARS] + [WHOLE] * (2 + len(pieces)),
+        out_specs=[WHOLE] * 2,
         out_shape=[
             jax.ShapeDtypeStruct((parts, rows, width), F32),
             jax.ShapeDtypeStruct((parts, rows, width), BF16),
         ],
-        scratch_shapes=[pltpu.VMEM((rows, features), F32)],
+        scratch_shapes=[pltpu.VMEM((rows, units), BF16)],
         compiler_params=PARAMS,
         name="expert",
-    )(ids, mine, other, expand, shrink)
+    )(ids, *pieces, expand, shrink)
 
 
 def combine_kernel(count, gates, base, first, second, *refs):
@@ -267,65 +329,72 @@
         parts = value.reshape(groups, -1, value.shape[-1])
         return lax.all_to_all(parts, "expert", 0, 0, tiled=True).reshape(value.shape)
 
+    def after(value, other):
+        return lax.optimization_barrier((value, other))[0]
+
     steps = range(groups) if direct else [0]
     dispatch, first, second = route(ids, expert_choice, experts, len(steps), capacity)
 
-    queries = pl.pallas_call(
-        query_kernel,
-        in_specs=[WHOLE] * 2,
-        out_specs=WHOLE,
-        out_shape=jax.ShapeDtypeStruct((token_count, width), BF16),
-        compiler_params=PARAMS,
-        name="query",
-    )(tokens, query_weight)
+    queries = ask(tokens, query_weight)
     owner = source_owner[0]
     if direct:
-        context = attend(queries, encoder_states[0], token_count)
-        for k in range(1, groups):
-            back = hop(attend(hop(queries, k, 0), encoder_states[0], token_count), k, 0)
+        source = stage(after(encoder_states[0], queries))
+        own = context = attend(queries, source, token_count)
+        for k in reversed(range(1, groups)):
+            asked = after(hop(queries, k, 0), own)
+            back = hop(attend(asked, source, token_count), k, 0)
             context = jnp.where(owner == here ^ k, back, context)
     else:
         asked = lax.all_gather(queries, "expert", axis=0, tiled=True)
         back = spread(attend(asked, encoder_states[0], token_count))
         context = lax.dynamic_slice_in_dim(back, owner * token_count, token_count, 0)
 
-    weights = [output_weight]
-    bit = 1
-    while bit < slices:
-        bit *= 2
-    while bit > 1:
-        bit //= 2
+    bits = []
+    while 2 ** len(bits) < slices:
+        bits.insert(0, 2 ** len(bits))
+    weights, order = [after(output_weight, source if direct else queries)], [0]
+    for bit in bits:
+        if bit == 1:
+            weights = [after(weight, context) for weight in weights]
         weights = weights + [hop(weight, 0, bit) for weight in weights]
-    order = [0]
-    bit = slices
-    while bit > 1:
-        bit //= 2
         order = order + [index ^ bit for index in order]
     contexts = [hop(context, 0, index) for index in order]
 
-    away = tuple(range(1, groups)) if direct else (0,)
-    state, *leaving = make_state(ids, tokens, dispatch, contexts, weights, away)
+    relayed = groups - 1 if direct and pairs > 1 and groups > 1 else -1
+    leave = tuple((k, slices if k == relayed else 2) for k in reversed(range(1, groups))) if direct else ((0, 2),)
+    state, *leaving = make_state(ids, tokens, dispatch, contexts, weights, leave)
+    leaving = {k: rows for (k, _), rows in zip(leave, leaving)}
     own_a, own_b, gates, columns = at_home(ids, state, dispatch, router_weight, expert_choice, experts, width)
 
     results = columns
-    for k in steps:
+    turns = [0, *reversed(range(1, groups))] if direct else [0]
+    for k in turns:
         if not direct:
             mine = spread(leaving[0])
-            other = hop(mine, 0, 1)
+            pieces, places = [mine, hop(mine, 0, 1)], [0, 1]
         elif k == 0:
-            mine, other = own_a, own_b
+            pieces, places = [own_a, own_b], [0, 1]
+        elif k == relayed:
+            pieces, places = [hop(leaving[k], k, 0)], [0]
+            for bit in bits:
+                pieces = pieces + [hop(piece, 0, bit) for piece in pieces]
+                places = places + [index ^ bit for index in places]
         else:
-            mine = hop(leaving[k - 1], k, 0)
-            other = hop(mine, 0, 1)
-        keep, give = run_expert(ids, mine, other, expand_weight[0], shrink_weight[0], pairs)
-        summed = (keep + hop(give, 0, 1).astype(F32)).astype(BF16)
-        parts = []
-        for j in range(pairs):
-            if direct:
-                parts.append(hop(summed[j], k, 2 * j))
-            else:
-                parts.append(hop(spread(summed[j]), 0, 2 * j))
-        last = k == steps[-1]
+            mine = hop(leaving[k], k, 0)
+            pieces, places = [mine, hop(mine, 0, 1)], [0, 1]
+        keep, give = run_expert(ids, places, pieces, expand_weight[0], shrink_weight[0], pairs)
+        summed = keep + hop(give, 0, 1).astype(F32)
+        if k == relayed:
+            total = summed[0]
+            for j in range(1, pairs):
+                total += hop(summed[j].astype(BF16), 0, 2 * j).astype(F32)
+            parts = [hop(total.astype(BF16), k, 0)]
+        else:
+            parts = []
+            for j in range(pairs):
+                part = summed[j].astype(BF16)
+                parts.append(hop(part, k, 2 * j) if direct else hop(spread(part), 0, 2 * j))
+        last = k == turns[-1]
         results = combine(gates, results, first[k], second[k], parts, BF16 if last else F32)
     return results
 

time: 97.1 us -> 91.3 us (0.940)
  Pallas kernels: 23.7 us -> 17.8 us
  local copies, waits for them, and re-layouts: 3.62 us -> 0.5 us
  waiting for transfers between devices: 37.1 us -> 39 us
  starting transfers between devices: 31.1 us -> 32.5 us
    pallas_call x10 -> x11, Pallas kernels: 19.7 us -> 13.8 us  [the longest x4 6.15 us: run_expert(): pl.pallas_call(functools.partial(expert_kernel, tuple(order)), in_specs=[...]
    unnamed x22 -> x14, local copies, waits for them, and re-layouts: 3.49 us -> 0.37 us
    ppermute x29 -> x31, waiting for transfers between devices: 37.1 us -> 39 us  [hop(): return lax.ppermute(value, ('expert', 'mp'), moves)]
    ppermute x29 -> x31, starting transfers between devices: 31.1 us -> 32.5 us  [hop(): return lax.ppermute(value, ('expert', 'mp'), moves)]
  transfers between devices with their start and end apart: 29 -> 31, of which waited for: 8 -> 10; matrix products, arithmetic and copies ran while one was open for 1% -> 1% of each run, Pallas kernels for 22% -> 14%
where the time goes in v2:
time: 91.3 us; the launch traced here: 91.2 us
  waiting for transfers between devices  39 us (43%)
  starting transfers between devices  32.5 us (36%)
  Pallas kernels  17.8 us (19%)
  between operations  1.01 us (1%)
    ppermute x31, waiting for transfers between devices, hop(): return lax.ppermute(value, ('expert', 'mp'), moves)  39 us
    ppermute x31, starting transfers between devices, hop(): return lax.ppermute(value, ('expert', 'mp'), moves)  32.5 us
    pallas_call x4, Pallas kernels, run_expert(): pl.pallas_call(functools.partial(expert_kernel, tuple(order)), in_specs=[...  6.15 us
    pallas_call x4, Pallas kernels, attend(): pl.pallas_call(attend_kernel, in_specs=[WHOLE] * 2, out_specs=WHOLE, out_...  3.1 us
    pallas_call x1, Pallas kernels, ask(): pl.pallas_call(query_kernel, in_specs=[pl.BlockSpec(memory_space=pltpu.HB...  1.83 us
  transfers between devices with their start and end apart: 31, of which 10 were waited for; matrix products, arithmetic and copies ran while one was open for 1% of the time, Pallas kernels for 14%

profile of v2, /device:TPU:0, one launch (start us, length us, event | category | flops | bytes accessed | tf_op | source)
XLA Modules:
  0.0 91.2 jit_solution(18370127269323631711)
XLA Ops:
  0.0 1.8 %query.1.queries = bf16[256,256]{1,0:T(8,128)(2,1)S(1)} custom-call(bf16[256,1024]{1,0:T(8,128)(2,1)} %refs_1_.1, bf16[1024,256]{1,0:T(8,128)(2,1)} %weight.1), custom_call_target="tpu_custom_call" | custom-call | tf_op jit(solution)/shard_map/query/pallas_call | solution.py:53
  1.8 1.1 %stage.1.source = bf16[2,512,256]{2,1,0:T(8,128)(2,1)S(1)} custom-call(bf16[2,512,256]{2,1,0:T(8,128)(2,1)} %bitcast.55), custom_call_target="tpu_custom_call" | custom-call | tf_op jit(solution)/shard_map/stage/pallas_call | solution.py:82
  3.0 0.0 copy-start.4
  3.0 3.0 %collective-permute-start.9 = (bf16[256,1024]{1,0:T(8,128)(2,1)S(1)}, bf16[256,1024]{1,0:T(8,128)(2,1)S(1)}, u32[]{:S(2)}, u32[]{:S(2)}) collective-permute-start(bf16[256,1024]{1,0:T(8,128)(2,1)S(1)} %copy-done.3), channel_id=1, source_target_pairs={{0,2},{1,3},{2,0},{3,1},{4,6},{5,7},{6,4},{7,5},{8,10},{9,11},{10,... | collective-permute-start | bytes 1572872 | tf_op jit(solution)/shard_map/ppermute | solution.py:326
  6.0 1.6 %collective-permute-start = (bf16[256,256]{1,0:T(8,128)(2,1)S(1)}, bf16[256,256]{1,0:T(8,128)(2,1)S(1)}, u32[]{:S(2)}, u32[]{:S(2)}) collective-permute-start(bf16[256,256]{1,0:T(8,128)(2,1)S(1)} %query.1.queries), channel_id=1, source_target_pairs={{0,4},{1,5},{2,6},{3,7},{4,0},{5,1},{6,2},{7,3},{8,12},{9,13},{10,... | collective-permute-start | bytes 393224 | tf_op jit(solution)/shard_map/ppermute | solution.py:326
  7.6 2.6 %collective-permute-start.2 = (bf16[256,256]{1,0:T(8,128)(2,1)S(1)}, bf16[256,256]{1,0:T(8,128)(2,1)S(1)}, u32[]{:S(2)}, u32[]{:S(2)}) collective-permute-start(bf16[256,256]{1,0:T(8,128)(2,1)S(1)} %query.1.queries), channel_id=1, source_target_pairs={{0,8},{1,9},{2,10},{3,11},{4,12},{5,13},{6,14},{7,15},{8,0},{9,1},... | collective-permute-start | bytes 393224 | tf_op jit(solution)/shard_map/ppermute | solution.py:326
  10.2 0.2 collective-permute-start.4
  10.4 0.8 attend.4
  11.2 1.3 %collective-permute-done.queries = bf16[256,256]{1,0:T(8,128)(2,1)S(1)} collective-permute-done((bf16[256,256]{1,0:T(8,128)(2,1)S(1)}, bf16[256,256]{1,0:T(8,128)(2,1)S(1)}, u32[]{:S(2)}, u32[]{:S(2)}) %collective-permute-start) | collective-permute-done | bytes 131104 | tf_op jit(solution)/shard_map/ppermute | solution.py:326
  12.5 0.8 attend.5
  13.2 0.7 collective-permute-start.1
  13.9 6.7 %collective-permute-done.2.queries = bf16[256,256]{1,0:T(8,128)(2,1)S(1)} collective-permute-done((bf16[256,256]{1,0:T(8,128)(2,1)S(1)}, bf16[256,256]{1,0:T(8,128)(2,1)S(1)}, u32[]{:S(2)}, u32[]{:S(2)}) %collective-permute-start.2) | collective-permute-done | bytes 131104 | tf_op jit(solution)/shard_map/ppermute | solution.py:326
  20.6 0.8 attend.6
  21.4 0.1 collective-permute-start.3
  21.5 0.8 attend.7
  22.3 3.3 %collective-permute-start.5 = (bf16[256,256]{1,0:T(8,128)(2,1)S(1)}, bf16[256,256]{1,0:T(8,128)(2,1)S(1)}, u32[]{:S(2)}, u32[]{:S(2)}) collective-permute-start(bf16[256,256]{1,0:T(8,128)(2,1)S(1)} %attend.7), channel_id=1, source_target_pairs={{0,12},{1,13},{2,14},{3,15},{4,8},{5,9},{6,10},{7,11},{8,4},{9,5},... | collective-permute-start | bytes 393224 | tf_op jit(solution)/shard_map/ppermute | solution.py:326
  26.2 5.3 %collective-permute-done.3 = bf16[256,256]{1,0:T(8,128)(2,1)S(1)} collective-permute-done((bf16[256,256]{1,0:T(8,128)(2,1)S(1)}, bf16[256,256]{1,0:T(8,128)(2,1)S(1)}, u32[]{:S(2)}, u32[]{:S(2)}) %collective-permute-start.3) | collective-permute-done | bytes 131104 | tf_op jit(solution)/shard_map/ppermute | solution.py:326
  31.5 0.1 collective-permute-start.10
  31.6 0.5 collective-permute-start.11
  32.1 0.5 collective-permute-start.6
  32.6 1.6 %collective-permute-start.8 = (bf16[256,256]{1,0:T(8,128)(2,1)S(1)}, bf16[256,256]{1,0:T(8,128)(2,1)S(1)}, u32[]{:S(2)}, u32[]{:S(2)}) collective-permute-start(bf16[256,256]{1,0:T(8,128)(2,1)S(1)} %select_select_fusion.refs_3_), channel_id=1, source_target_pairs={{0,3},{1,2},{2,1},{3,0},{4,7},{5,6},{6,5},{7,4},{8,11},{9,10},{10,... | collective-permute-start | bytes 393224 | tf_op jit(solution)/shard_map/ppermute | solution.py:326
  34.2 0.1 copy.10.choice
  34.4 0.2 copy.11.router
  34.6 0.1 pad_add_fusion.ids.refs_0_
  34.7 1.4 %route.1 = (bf16[4,192,256]{2,1,0:T(8,128)(2,1)S(1)}, bf16[4,256,192]{2,1,0:T(8,128)(2,1)S(1)}, bf16[4,256,192]{2,1,0:T(8,128)(2,1)S(1)}) custom-call(s32[2]{0:T(128)S(1)} %pad_add_fusion.ids.refs_0_, s32[256,2]{1,0:T(8,128)S(1)} %copy.10.choice, s32[2,256]{1,0:T(2,128)S(1)} %bitcast.54), custom_call_target="tpu_custom_call" | custom-call | tf_op jit(solution)/shard_map/route/pallas_call | solution.py:159
  36.0 2.4 %collective-permute-done.6.refs_4_ = bf16[256,256]{1,0:T(8,128)(2,1)S(1)} collective-permute-done((bf16[256,256]{1,0:T(8,128)(2,1)S(1)}, bf16[256,256]{1,0:T(8,128)(2,1)S(1)}, u32[]{:S(2)}, u32[]{:S(2)}) %collective-permute-start.6) | collective-permute-done | bytes 131104 | tf_op jit(solution)/shard_map/ppermute | solution.py:326
  38.5 1.1 %collective-permute-done.8.refs_6_ = bf16[256,256]{1,0:T(8,128)(2,1)S(1)} collective-permute-done((bf16[256,256]{1,0:T(8,128)(2,1)S(1)}, bf16[256,256]{1,0:T(8,128)(2,1)S(1)}, u32[]{:S(2)}, u32[]{:S(2)}) %collective-permute-start.8) | collective-permute-done | bytes 131104 | tf_op jit(solution)/shard_map/ppermute | solution.py:326
  39.5 0.0 copy-start
  39.5 0.0 copy-start.1
  39.6 1.6 %state.1 = (bf16[256,1024]{1,0:T(8,128)(2,1)S(1)}, bf16[192,256]{1,0:T(8,128)(2,1)S(1)}, bf16[192,512]{1,0:T(8,128)(2,1)S(1)}, bf16[192,512]{1,0:T(8,128)(2,1)S(1)}) custom-call(s32[2]{0:T(128)S(1)} %pad_add_fusion.ids.refs_0_, bf16[256,1024]{1,0:T(8,128)(2,1)S(1)} %copy-done.2, bf16[4,192,256]{2,1,0:T(8,128)(2,1)S(1)} %get-tuple-element.31.refs_2_.dispatch, ...), custom_call_target="tpu_custom_call" | custom-call | tf_op jit(solution)/shard_map/state/pallas_call | solution.py:191
  41.1 2.0 %collective-permute-start.26 = (bf16[192,512]{1,0:T(8,128)(2,1)S(1)}, bf16[192,512]{1,0:T(8,128)(2,1)S(1)}, u32[]{:S(2)}, u32[]{:S(2)}) collective-permute-start(bf16[192,512]{1,0:T(8,128)(2,1)S(1)} %get-tuple-element.54), channel_id=1, source_target_pairs={{0,4},{1,5},{2,6},{3,7},{4,0},{5,1},{6,2},{7,3},{8,12},{9,13},{10,... | collective-permute-start | bytes 589832 | tf_op jit(solution)/shard_map/ppermute | solution.py:326
  43.2 1.2 %collective-permute-start.21 = (bf16[192,512]{1,0:T(8,128)(2,1)S(1)}, bf16[192,512]{1,0:T(8,128)(2,1)S(1)}, u32[]{:S(2)}, u32[]{:S(2)}) collective-permute-start(bf16[192,512]{1,0:T(8,128)(2,1)S(1)} %get-tuple-element.51), channel_id=1, source_target_pairs={{0,8},{1,9},{2,10},{3,11},{4,12},{5,13},{6,14},{7,15},{8,0},{9,1},... | collective-permute-start | bytes 589832 | tf_op jit(solution)/shard_map/ppermute | solution.py:326
  44.4 1.4 %collective-permute-start.14 = (bf16[192,256]{1,0:T(8,128)(2,1)S(1)}, bf16[192,256]{1,0:T(8,128)(2,1)S(1)}, u32[]{:S(2)}, u32[]{:S(2)}) collective-permute-start(bf16[192,256]{1,0:T(8,128)(2,1)S(1)} %get-tuple-element.48), channel_id=1, source_target_pairs={{0,12},{1,13},{2,14},{3,15},{4,8},{5,9},{6,10},{7,11},{8,4},{9,5},... | collective-permute-start | bytes 294920 | tf_op jit(solution)/shard_map/ppermute | solution.py:326
  45.8 1.1 %home.1 = (bf16[192,512]{1,0:T(8,128)(2,1)S(1)}, bf16[192,512]{1,0:T(8,128)(2,1)S(1)}, f32[256,2]{1,0:T(8,128)S(1)}, f32[256,256]{1,0:T(8,128)S(1)}) custom-call(s32[2]{0:T(128)S(1)} %pad_add_fusion.ids.refs_0_, bf16[256,1024]{1,0:T(8,128)(2,1)S(1)} %get-tuple-element.39.state, bf16[4,192,256]{2,1,0:T(8,128)(2,1)S(1)} %get-tuple-element.31.refs_2_.dispatch, ...), custom_call_target="tpu_custom_call" | custom-call | tf_op jit(solution)/shard_map/home/pallas_call | solution.py:220
  46.9 1.5 %expert.4 = (f32[2,192,256]{2,1,0:T(8,128)S(1)}, bf16[2,192,256]{2,1,0:T(8,128)(2,1)S(1)}) custom-call(s32[2]{0:T(128)S(1)} %pad_add_fusion.ids.refs_0_, bf16[192,512]{1,0:T(8,128)(2,1)S(1)} %get-tuple-element.44.refs_1_, bf16[192,512]{1,0:T(8,128)(2,1)S(1)} %get-tuple-element.45.refs_2_, bf16[1024,1024]{1,0:T(8,128)(2,1)S(1)} %bitcast.46, ...), custom_call_target="tpu_custom_call" | custom-call | tf_op jit(solution)/shard_map/expert/pallas_call | solution.py:261
  48.4 0.2 collective-permute-start.12
  48.6 9.1 %collective-permute-done.14.refs_1_ = bf16[192,256]{1,0:T(8,128)(2,1)S(1)} collective-permute-done((bf16[192,256]{1,0:T(8,128)(2,1)S(1)}, bf16[192,256]{1,0:T(8,128)(2,1)S(1)}, u32[]{:S(2)}, u32[]{:S(2)}) %collective-permute-start.14) | collective-permute-done | bytes 98336 | tf_op jit(solution)/shard_map/ppermute | solution.py:326
  57.7 0.5 collective-permute-start.15
  58.2 0.5 collective-permute-start.27
  58.8 0.1 collective-permute-start.22
  58.8 3.5 %collective-permute-done.15.refs_2_ = bf16[192,256]{1,0:T(8,128)(2,1)S(1)} collective-permute-done((bf16[192,256]{1,0:T(8,128)(2,1)S(1)}, bf16[192,256]{1,0:T(8,128)(2,1)S(1)}, u32[]{:S(2)}, u32[]{:S(2)}) %collective-permute-start.15) | collective-permute-done | bytes 98336 | tf_op jit(solution)/shard_map/ppermute | solution.py:326
  62.3 0.1 add_convert_fusion.2
  62.4 1.2 %collective-permute-done.17.refs_4_ = bf16[192,256]{1,0:T(8,128)(2,1)S(1)} collective-permute-done((bf16[192,256]{1,0:T(8,128)(2,1)S(1)}, bf16[192,256]{1,0:T(8,128)(2,1)S(1)}, u32[]{:S(2)}, u32[]{:S(2)}) %collective-permute-start.17) | collective-permute-done | bytes 98336 | tf_op jit(solution)/shard_map/ppermute | solution.py:326
  63.6 1.5 %expert.5 = (f32[2,192,256]{2,1,0:T(8,128)S(1)}, bf16[2,192,256]{2,1,0:T(8,128)(2,1)S(1)}) custom-call(s32[2]{0:T(128)S(1)} %pad_add_fusion.ids.refs_0_, bf16[192,256]{1,0:T(8,128)(2,1)S(1)} %collective-permute-done.14.refs_1_, bf16[192,256]{1,0:T(8,128)(2,1)S(1)} %collective-permute-done.15.refs_2_, bf16[192,256]{1,0:T(8,128)(2,1)S(1)} %collective-permute-done.16.refs_3_, ...), custom_call_target="tpu_custom_call" | custom-call | tf_op jit(solution)/shard_map/expert/pallas_call | solution.py:261
  65.2 0.2 collective-permute-start.18
  65.4 0.6 collective-permute-start.13
  66.0 1.5 %expert.7 = (f32[2,192,256]{2,1,0:T(8,128)S(1)}, bf16[2,192,256]{2,1,0:T(8,128)(2,1)S(1)}) custom-call(s32[2]{0:T(128)S(1)} %pad_add_fusion.ids.refs_0_, bf16[192,512]{1,0:T(8,128)(2,1)S(1)} %collective-permute-done.26.refs_1_, bf16[192,512]{1,0:T(8,128)(2,1)S(1)} %collective-permute-done.27.refs_2_, bf16[1024,1024]{1,0:T(8,128)(2,1)S(1)} %bitcast.48, ...), custom_call_target="tpu_custom_call" | custom-call | tf_op jit(solution)/shard_map/expert/pallas_call | solution.py:261
  67.6 0.1 collective-permute-start.28
  67.7 1.5 %expert.6 = (f32[2,192,256]{2,1,0:T(8,128)S(1)}, bf16[2,192,256]{2,1,0:T(8,128)(2,1)S(1)}) custom-call(s32[2]{0:T(128)S(1)} %pad_add_fusion.ids.refs_0_, bf16[192,512]{1,0:T(8,128)(2,1)S(1)} %collective-permute-done.21.refs_1_, bf16[192,512]{1,0:T(8,128)(2,1)S(1)} %collective-permute-done.22.refs_2_, bf16[1024,1024]{1,0:T(8,128)(2,1)S(1)} %bitcast.49, ...), custom_call_target="tpu_custom_call" | custom-call | tf_op jit(solution)/shard_map/expert/pallas_call | solution.py:261
  69.2 0.5 collective-permute-start.23
  69.8 1.6 %collective-permute-start.19 = (bf16[192,256]{1,0:T(8,128)(2,1)S(1)}, bf16[192,256]{1,0:T(8,128)(2,1)S(1)}, u32[]{:S(2)}, u32[]{:S(2)}) collective-permute-start(bf16[192,256]{1,0:T(8,128)(2,1)S(1)} %fusion.2), channel_id=1, source_target_pairs={{0,2},{1,3},{2,0},{3,1},{4,6},{5,7},{6,4},{7,5},{8,10},{9,11},{10,... | collective-permute-start | bytes 294920 | tf_op jit(solution)/shard_map/ppermute | solution.py:326
  71.5 2.7 %collective-permute-start.29 = (bf16[192,256]{1,0:T(8,128)(2,1)S(1)}, bf16[192,256]{1,0:T(8,128)(2,1)S(1)}, u32[]{:S(2)}, u32[]{:S(2)}) collective-permute-start(bf16[192,256]{1,0:T(8,128)(2,1)S(1)} %get-tuple-element.66), channel_id=1, source_target_pairs={{0,4},{1,5},{2,6},{3,7},{4,0},{5,1},{6,2},{7,3},{8,12},{9,13},{10,... | collective-permute-start | bytes 294920 | tf_op jit(solution)/shard_map/ppermute | solution.py:326
  74.2 0.1 collective-permute-start.30
  74.2 0.1 add_convert_fusion.1
  74.3 3.2 %collective-permute-start.24 = (bf16[192,256]{1,0:T(8,128)(2,1)S(1)}, bf16[192,256]{1,0:T(8,128)(2,1)S(1)}, u32[]{:S(2)}, u32[]{:S(2)}) collective-permute-start(bf16[192,256]{1,0:T(8,128)(2,1)S(1)} %get-tuple-element.68), channel_id=1, source_target_pairs={{0,8},{1,9},{2,10},{3,11},{4,12},{5,13},{6,14},{7,15},{8,0},{9,1},... | collective-permute-start | bytes 294920 | tf_op jit(solution)/shard_map/ppermute | solution.py:326
  77.5 1.9 %collective-permute-start.25 = (bf16[192,256]{1,0:T(8,128)(2,1)S(1)}, bf16[192,256]{1,0:T(8,128)(2,1)S(1)}, u32[]{:S(2)}, u32[]{:S(2)}) collective-permute-start(bf16[192,256]{1,0:T(8,128)(2,1)S(1)} %get-tuple-element.67), channel_id=1, source_target_pairs={{0,10},{1,11},{2,8},{3,9},{4,14},{5,15},{6,12},{7,13},{8,2},{9,3},... | collective-permute-start | bytes 294920 | tf_op jit(solution)/shard_map/ppermute | solution.py:326
  79.4 1.5 %collective-permute-start.20 = (bf16[192,256]{1,0:T(8,128)(2,1)S(1)}, bf16[192,256]{1,0:T(8,128)(2,1)S(1)}, u32[]{:S(2)}, u32[]{:S(2)}) collective-permute-start(bf16[192,256]{1,0:T(8,128)(2,1)S(1)} %fusion.1), channel_id=1, source_target_pairs={{0,12},{1,13},{2,14},{3,15},{4,8},{5,9},{6,10},{7,11},{8,4},{9,5},... | collective-permute-start | bytes 294920 | tf_op jit(solution)/shard_map/ppermute | solution.py:326
  81.0 0.1 slice_bitcast_fusion.1
  81.0 0.2 combine.4.base
  81.3 6.5 %collective-permute-done.20.refs_0_ = bf16[192,256]{1,0:T(8,128)(2,1)S(1)} collective-permute-done((bf16[192,256]{1,0:T(8,128)(2,1)S(1)}, bf16[192,256]{1,0:T(8,128)(2,1)S(1)}, u32[]{:S(2)}, u32[]{:S(2)}) %collective-permute-start.20) | collective-permute-done | bytes 98336 | tf_op jit(solution)/shard_map/ppermute | solution.py:326
  87.8 0.2 combine.5.base
  88.0 2.0 %collective-permute-done.25.refs_1_ = bf16[192,256]{1,0:T(8,128)(2,1)S(1)} collective-permute-done((bf16[192,256]{1,0:T(8,128)(2,1)S(1)}, bf16[192,256]{1,0:T(8,128)(2,1)S(1)}, u32[]{:S(2)}, u32[]{:S(2)}) %collective-permute-start.25) | collective-permute-done | bytes 98336 | tf_op jit(solution)/shard_map/ppermute | solution.py:326
  90.0 0.2 combine.6.base
  90.3 0.9 combine.7
  (41 shorter events, 0.3 us)
Async XLA Ops:
  0.0 3.0 %copy-start.3 = (bf16[256,1024]{1,0:T(8,128)(2,1)S(1)}, bf16[256,1024]{1,0:T(8,128)(2,1)}, u32[]{:S(2)}) copy-start(bf16[256,1024]{1,0:T(8,128)(2,1)} %refs_7_) | copy-start | bytes 1572868
  3.0 31.3 %copy-start.4 = (s32[256,2]{0,1:T(2,128)S(1)}, s32[256,2]{0,1:T(2,128)}, u32[]{:S(2)}) copy-start(s32[256,2]{0,1:T(2,128)} %param.15) | copy-start | bytes 6148
  3.0 31.4 %copy-start.5 = (bf16[1024,4]{0,1:T(4,128)(2,1)S(1)}, bf16[1024,4]{0,1:T(4,128)(2,1)}, u32[]{:S(2)}) copy-start(bf16[1024,4]{0,1:T(4,128)(2,1)} %param.14) | copy-start | bytes 24580
  3.0 36.5 %copy-start.2 = (bf16[256,1024]{1,0:T(8,128)(2,1)S(1)}, bf16[256,1024]{1,0:T(8,128)(2,1)}, u32[]{:S(2)}) copy-start(bf16[256,1024]{1,0:T(8,128)(2,1)} %refs_1_.1) | copy-start | bytes 1572868
  3.0 28.6 %collective-permute-start.9 = (bf16[256,1024]{1,0:T(8,128)(2,1)S(1)}, bf16[256,1024]{1,0:T(8,128)(2,1)S(1)}, u32[]{:S(2)}, u32[]{:S(2)}) collective-permute-start(bf16[256,1024]{1,0:T(8,128)(2,1)S(1)} %copy-done.3), channel_id=1, source_target_pairs={{0,2},{1,3},{2,0},{3,1},{4,6},{5,7},{6,4},{7,5},{8,10},{9,11},{10,... | collective-permute-start | bytes 1572872 | tf_op jit(solution)/shard_map/ppermute | solution.py:326
  6.0 6.4 %collective-permute-start = (bf16[256,256]{1,0:T(8,128)(2,1)S(1)}, bf16[256,256]{1,0:T(8,128)(2,1)S(1)}, u32[]{:S(2)}, u32[]{:S(2)}) collective-permute-start(bf16[256,256]{1,0:T(8,128)(2,1)S(1)} %query.1.queries), channel_id=1, source_target_pairs={{0,4},{1,5},{2,6},{3,7},{4,0},{5,1},{6,2},{7,3},{8,12},{9,13},{10,... | collective-permute-start | bytes 393224 | tf_op jit(solution)/shard_map/ppermute | solution.py:326
  7.6 13.0 %collective-permute-start.2 = (bf16[256,256]{1,0:T(8,128)(2,1)S(1)}, bf16[256,256]{1,0:T(8,128)(2,1)S(1)}, u32[]{:S(2)}, u32[]{:S(2)}) collective-permute-start(bf16[256,256]{1,0:T(8,128)(2,1)S(1)} %query.1.queries), channel_id=1, source_target_pairs={{0,8},{1,9},{2,10},{3,11},{4,12},{5,13},{6,14},{7,15},{8,0},{9,1},... | collective-permute-start | bytes 393224 | tf_op jit(solution)/shard_map/ppermute | solution.py:326
  10.2 11.3 %collective-permute-start.4 = (bf16[256,256]{1,0:T(8,128)(2,1)S(1)}, bf16[256,256]{1,0:T(8,128)(2,1)S(1)}, u32[]{:S(2)}, u32[]{:S(2)}) collective-permute-start(bf16[256,256]{1,0:T(8,128)(2,1)S(1)} %query.1.queries), channel_id=1, source_target_pairs={{0,12},{1,13},{2,14},{3,15},{4,8},{5,9},{6,10},{7,11},{8,4},{9,5},... | collective-permute-start | bytes 393224 | tf_op jit(solution)/shard_map/ppermute | solution.py:326
  13.2 12.9 %collective-permute-start.1 = (bf16[256,256]{1,0:T(8,128)(2,1)S(1)}, bf16[256,256]{1,0:T(8,128)(2,1)S(1)}, u32[]{:S(2)}, u32[]{:S(2)}) collective-permute-start(bf16[256,256]{1,0:T(8,128)(2,1)S(1)} %attend.5), channel_id=1, source_target_pairs={{0,4},{1,5},{2,6},{3,7},{4,0},{5,1},{6,2},{7,3},{8,12},{9,13},{10,... | collective-permute-start | bytes 393224 | tf_op jit(solution)/shard_map/ppermute | solution.py:326
  21.4 10.1 %collective-permute-start.3 = (bf16[256,256]{1,0:T(8,128)(2,1)S(1)}, bf16[256,256]{1,0:T(8,128)(2,1)S(1)}, u32[]{:S(2)}, u32[]{:S(2)}) collective-permute-start(bf16[256,256]{1,0:T(8,128)(2,1)S(1)} %attend.6), channel_id=1, source_target_pairs={{0,8},{1,9},{2,10},{3,11},{4,12},{5,13},{6,14},{7,15},{8,0},{9,1},... | collective-permute-start | bytes 393224 | tf_op jit(solution)/shard_map/ppermute | solution.py:326
  22.3 9.2 %collective-permute-start.5 = (bf16[256,256]{1,0:T(8,128)(2,1)S(1)}, bf16[256,256]{1,0:T(8,128)(2,1)S(1)}, u32[]{:S(2)}, u32[]{:S(2)}) collective-permute-start(bf16[256,256]{1,0:T(8,128)(2,1)S(1)} %attend.7), channel_id=1, source_target_pairs={{0,12},{1,13},{2,14},{3,15},{4,8},{5,9},{6,10},{7,11},{8,4},{9,5},... | collective-permute-start | bytes 393224 | tf_op jit(solution)/shard_map/ppermute | solution.py:326
  31.5 8.0 %collective-permute-start.10 = (bf16[256,1024]{1,0:T(8,128)(2,1)S(1)}, bf16[256,1024]{1,0:T(8,128)(2,1)S(1)}, u32[]{:S(2)}, u32[]{:S(2)}) collective-permute-start(bf16[256,1024]{1,0:T(8,128)(2,1)S(1)} %copy-done.3), channel_id=1, source_target_pairs={{0,1},{1,0},{2,3},{3,2},{4,5},{5,4},{6,7},{7,6},{8,9},{9,8},{10,11... | collective-permute-start | bytes 1572872 | tf_op jit(solution)/shard_map/ppermute | solution.py:326
  31.6 7.9 %collective-permute-start.11 = (bf16[256,1024]{1,0:T(8,128)(2,1)S(1)}, bf16[256,1024]{1,0:T(8,128)(2,1)S(1)}, u32[]{:S(2)}, u32[]{:S(2)}) collective-permute-start(bf16[256,1024]{1,0:T(8,128)(2,1)S(1)} %collective-permute-done.9.refs_8_), channel_id=1, source_target_pairs={{0,1},{1,0},{2,3},{3,2},{4,5},{5,4},{6,7},{7,6},{8,9},{9,8},{10,11... | collective-permute-start | bytes 1572872 | tf_op jit(solution)/shard_map/ppermute | solution.py:326
  32.1 6.4 %collective-permute-start.6 = (bf16[256,256]{1,0:T(8,128)(2,1)S(1)}, bf16[256,256]{1,0:T(8,128)(2,1)S(1)}, u32[]{:S(2)}, u32[]{:S(2)}) collective-permute-start(bf16[256,256]{1,0:T(8,128)(2,1)S(1)} %select_select_fusion.refs_3_), channel_id=1, source_target_pairs={{0,2},{1,3},{2,0},{3,1},{4,6},{5,7},{6,4},{7,5},{8,10},{9,11},{10,... | collective-permute-start | bytes 393224 | tf_op jit(solution)/shard_map/ppermute | solution.py:326
  32.6 5.8 %collective-permute-start.7 = (bf16[256,256]{1,0:T(8,128)(2,1)S(1)}, bf16[256,256]{1,0:T(8,128)(2,1)S(1)}, u32[]{:S(2)}, u32[]{:S(2)}) collective-permute-start(bf16[256,256]{1,0:T(8,128)(2,1)S(1)} %select_select_fusion.refs_3_), channel_id=1, source_target_pairs={{0,1},{1,0},{2,3},{3,2},{4,5},{5,4},{6,7},{7,6},{8,9},{9,8},{10,11... | collective-permute-start | bytes 393224 | tf_op jit(solution)/shard_map/ppermute | solution.py:326
  32.6 6.9 %collective-permute-start.8 = (bf16[256,256]{1,0:T(8,128)(2,1)S(1)}, bf16[256,256]{1,0:T(8,128)(2,1)S(1)}, u32[]{:S(2)}, u32[]{:S(2)}) collective-permute-start(bf16[256,256]{1,0:T(8,128)(2,1)S(1)} %select_select_fusion.refs_3_), channel_id=1, source_target_pairs={{0,3},{1,2},{2,1},{3,0},{4,7},{5,6},{6,5},{7,4},{8,11},{9,10},{10,... | collective-permute-start | bytes 393224 | tf_op jit(solution)/shard_map/ppermute | solution.py:326
  39.5 7.3 %copy-start = (bf16[1,1024,1024]{2,1,0:T(8,128)(2,1)S(1)}, bf16[1,1024,1024]{2,1,0:T(8,128)(2,1)}, u32[]{:S(2)}) copy-start(bf16[1,1024,1024]{2,1,0:T(8,128)(2,1)} %param.16) | copy-start | bytes 6291460
  39.5 7.3 %copy-start.1 = (bf16[1,1024,1024]{2,1,0:T(8,128)(2,1)S(1)}, bf16[1,1024,1024]{2,1,0:T(8,128)(2,1)}, u32[]{:S(2)}) copy-start(bf16[1,1024,1024]{2,1,0:T(8,128)(2,1)} %param.17) | copy-start | bytes 6291460
  41.1 17.1 %collective-permute-start.26 = (bf16[192,512]{1,0:T(8,128)(2,1)S(1)}, bf16[192,512]{1,0:T(8,128)(2,1)S(1)}, u32[]{:S(2)}, u32[]{:S(2)}) collective-permute-start(bf16[192,512]{1,0:T(8,128)(2,1)S(1)} %get-tuple-element.54), channel_id=1, source_target_pairs={{0,4},{1,5},{2,6},{3,7},{4,0},{5,1},{6,2},{7,3},{8,12},{9,13},{10,... | collective-permute-start | bytes 589832 | tf_op jit(solution)/shard_map/ppermute | solution.py:326
  43.2 15.6 %collective-permute-start.21 = (bf16[192,512]{1,0:T(8,128)(2,1)S(1)}, bf16[192,512]{1,0:T(8,128)(2,1)S(1)}, u32[]{:S(2)}, u32[]{:S(2)}) collective-permute-start(bf16[192,512]{1,0:T(8,128)(2,1)S(1)} %get-tuple-element.51), channel_id=1, source_target_pairs={{0,8},{1,9},{2,10},{3,11},{4,12},{5,13},{6,14},{7,15},{8,0},{9,1},... | collective-permute-start | bytes 589832 | tf_op jit(solution)/shard_map/ppermute | solution.py:326
  44.4 13.3 %collective-permute-start.14 = (bf16[192,256]{1,0:T(8,128)(2,1)S(1)}, bf16[192,256]{1,0:T(8,128)(2,1)S(1)}, u32[]{:S(2)}, u32[]{:S(2)}) collective-permute-start(bf16[192,256]{1,0:T(8,128)(2,1)S(1)} %get-tuple-element.48), channel_id=1, source_target_pairs={{0,12},{1,13},{2,14},{3,15},{4,8},{5,9},{6,10},{7,11},{8,4},{9,5},... | collective-permute-start | bytes 294920 | tf_op jit(solution)/shard_map/ppermute | solution.py:326
  48.4 13.9 %collective-permute-start.12 = (bf16[2,192,256]{2,1,0:T(8,128)(2,1)S(1)}, bf16[2,192,256]{2,1,0:T(8,128)(2,1)S(1)}, u32[]{:S(2)}, u32[]{:S(2)}) collective-permute-start(bf16[2,192,256]{2,1,0:T(8,128)(2,1)S(1)} %get-tuple-element.47), channel_id=1, source_target_pairs={{0,1},{1,0},{2,3},{3,2},{4,5},{5,4},{6,7},{7,6},{8,9},{9,8},{10,11... | collective-permute-start | bytes 589832 | tf_op jit(solution)/shard_map/ppermute | solution.py:326
  57.7 4.6 %collective-permute-start.15 = (bf16[192,256]{1,0:T(8,128)(2,1)S(1)}, bf16[192,256]{1,0:T(8,128)(2,1)S(1)}, u32[]{:S(2)}, u32[]{:S(2)}) collective-permute-start(bf16[192,256]{1,0:T(8,128)(2,1)S(1)} %collective-permute-done.14.refs_1_), channel_id=1, source_target_pairs={{0,2},{1,3},{2,0},{3,1},{4,6},{5,7},{6,4},{7,5},{8,10},{9,11},{10,... | collective-permute-start | bytes 294920 | tf_op jit(solution)/shard_map/ppermute | solution.py:326
  58.2 4.1 %collective-permute-start.16 = (bf16[192,256]{1,0:T(8,128)(2,1)S(1)}, bf16[192,256]{1,0:T(8,128)(2,1)S(1)}, u32[]{:S(2)}, u32[]{:S(2)}) collective-permute-start(bf16[192,256]{1,0:T(8,128)(2,1)S(1)} %collective-permute-done.14.refs_1_), channel_id=1, source_target_pairs={{0,1},{1,0},{2,3},{3,2},{4,5},{5,4},{6,7},{7,6},{8,9},{9,8},{10,11... | collective-permute-start | bytes 294920 | tf_op jit(solution)/shard_map/ppermute | solution.py:326
  58.2 7.8 %collective-permute-start.27 = (bf16[192,512]{1,0:T(8,128)(2,1)S(1)}, bf16[192,512]{1,0:T(8,128)(2,1)S(1)}, u32[]{:S(2)}, u32[]{:S(2)}) collective-permute-start(bf16[192,512]{1,0:T(8,128)(2,1)S(1)} %collective-permute-done.26.refs_1_), channel_id=1, source_target_pairs={{0,1},{1,0},{2,3},{3,2},{4,5},{5,4},{6,7},{7,6},{8,9},{9,8},{10,11... | collective-permute-start | bytes 589832 | tf_op jit(solution)/shard_map/ppermute | solution.py:326
  58.8 8.9 %collective-permute-start.22 = (bf16[192,512]{1,0:T(8,128)(2,1)S(1)}, bf16[192,512]{1,0:T(8,128)(2,1)S(1)}, u32[]{:S(2)}, u32[]{:S(2)}) collective-permute-start(bf16[192,512]{1,0:T(8,128)(2,1)S(1)} %collective-permute-done.21.refs_1_), channel_id=1, source_target_pairs={{0,1},{1,0},{2,3},{3,2},{4,5},{5,4},{6,7},{7,6},{8,9},{9,8},{10,11... | collective-permute-start | bytes 589832 | tf_op jit(solution)/shard_map/ppermute | solution.py:326
  62.3 1.3 %collective-permute-start.17 = (bf16[192,256]{1,0:T(8,128)(2,1)S(1)}, bf16[192,256]{1,0:T(8,128)(2,1)S(1)}, u32[]{:S(2)}, u32[]{:S(2)}) collective-permute-start(bf16[192,256]{1,0:T(8,128)(2,1)S(1)} %collective-permute-done.15.refs_2_), channel_id=1, source_target_pairs={{0,1},{1,0},{2,3},{3,2},{4,5},{5,4},{6,7},{7,6},{8,9},{9,8},{10,11... | collective-permute-start | bytes 294920 | tf_op jit(solution)/shard_map/ppermute | solution.py:326
  65.2 4.6 %collective-permute-start.18 = (bf16[2,192,256]{2,1,0:T(8,128)(2,1)S(1)}, bf16[2,192,256]{2,1,0:T(8,128)(2,1)S(1)}, u32[]{:S(2)}, u32[]{:S(2)}) collective-permute-start(bf16[2,192,256]{2,1,0:T(8,128)(2,1)S(1)} %get-tuple-element.50), channel_id=1, source_target_pairs={{0,1},{1,0},{2,3},{3,2},{4,5},{5,4},{6,7},{7,6},{8,9},{9,8},{10,11... | collective-permute-start | bytes 589832 | tf_op jit(solution)/shard_map/ppermute | solution.py:326
  65.4 14.0 %collective-permute-start.13 = (bf16[192,256]{1,0:T(8,128)(2,1)S(1)}, bf16[192,256]{1,0:T(8,128)(2,1)S(1)}, u32[]{:S(2)}, u32[]{:S(2)}) collective-permute-start(bf16[192,256]{1,0:T(8,128)(2,1)S(1)} %get-tuple-element.69), channel_id=1, source_target_pairs={{0,2},{1,3},{2,0},{3,1},{4,6},{5,7},{6,4},{7,5},{8,10},{9,11},{10,... | collective-permute-start | bytes 294920 | tf_op jit(solution)/shard_map/ppermute | solution.py:326
  67.6 3.8 %collective-permute-start.28 = (bf16[2,192,256]{2,1,0:T(8,128)(2,1)S(1)}, bf16[2,192,256]{2,1,0:T(8,128)(2,1)S(1)}, u32[]{:S(2)}, u32[]{:S(2)}) collective-permute-start(bf16[2,192,256]{2,1,0:T(8,128)(2,1)S(1)} %get-tuple-element.56), channel_id=1, source_target_pairs={{0,1},{1,0},{2,3},{3,2},{4,5},{5,4},{6,7},{7,6},{8,9},{9,8},{10,11... | collective-permute-start | bytes 589832 | tf_op jit(solution)/shard_map/ppermute | solution.py:326
  69.2 5.0 %collective-permute-start.23 = (bf16[2,192,256]{2,1,0:T(8,128)(2,1)S(1)}, bf16[2,192,256]{2,1,0:T(8,128)(2,1)S(1)}, u32[]{:S(2)}, u32[]{:S(2)}) collective-permute-start(bf16[2,192,256]{2,1,0:T(8,128)(2,1)S(1)} %get-tuple-element.53), channel_id=1, source_target_pairs={{0,1},{1,0},{2,3},{3,2},{4,5},{5,4},{6,7},{7,6},{8,9},{9,8},{10,11... | collective-permute-start | bytes 589832 | tf_op jit(solution)/shard_map/ppermute | solution.py:326
  69.8 7.7 %collective-permute-start.19 = (bf16[192,256]{1,0:T(8,128)(2,1)S(1)}, bf16[192,256]{1,0:T(8,128)(2,1)S(1)}, u32[]{:S(2)}, u32[]{:S(2)}) collective-permute-start(bf16[192,256]{1,0:T(8,128)(2,1)S(1)} %fusion.2), channel_id=1, source_target_pairs={{0,2},{1,3},{2,0},{3,1},{4,6},{5,7},{6,4},{7,5},{8,10},{9,11},{10,... | collective-permute-start | bytes 294920 | tf_op jit(solution)/shard_map/ppermute | solution.py:326
  71.5 18.8 %collective-permute-start.29 = (bf16[192,256]{1,0:T(8,128)(2,1)S(1)}, bf16[192,256]{1,0:T(8,128)(2,1)S(1)}, u32[]{:S(2)}, u32[]{:S(2)}) collective-permute-start(bf16[192,256]{1,0:T(8,128)(2,1)S(1)} %get-tuple-element.66), channel_id=1, source_target_pairs={{0,4},{1,5},{2,6},{3,7},{4,0},{5,1},{6,2},{7,3},{8,12},{9,13},{10,... | collective-permute-start | bytes 294920 | tf_op jit(solution)/shard_map/ppermute | solution.py:326
  74.2 16.1 %collective-permute-start.30 = (bf16[192,256]{1,0:T(8,128)(2,1)S(1)}, bf16[192,256]{1,0:T(8,128)(2,1)S(1)}, u32[]{:S(2)}, u32[]{:S(2)}) collective-permute-start(bf16[192,256]{1,0:T(8,128)(2,1)S(1)} %get-tuple-element.65), channel_id=1, source_target_pairs={{0,6},{1,7},{2,4},{3,5},{4,2},{5,3},{6,0},{7,1},{8,14},{9,15},{10,... | collective-permute-start | bytes 294920 | tf_op jit(solution)/shard_map/ppermute | solution.py:326
  74.3 13.7 %collective-permute-start.24 = (bf16[192,256]{1,0:T(8,128)(2,1)S(1)}, bf16[192,256]{1,0:T(8,128)(2,1)S(1)}, u32[]{:S(2)}, u32[]{:S(2)}) collective-permute-start(bf16[192,256]{1,0:T(8,128)(2,1)S(1)} %get-tuple-element.68), channel_id=1, source_target_pairs={{0,8},{1,9},{2,10},{3,11},{4,12},{5,13},{6,14},{7,15},{8,0},{9,1},... | collective-permute-start | bytes 294920 | tf_op jit(solution)/shard_map/ppermute | solution.py:326
  77.5 12.5 %collective-permute-start.25 = (bf16[192,256]{1,0:T(8,128)(2,1)S(1)}, bf16[192,256]{1,0:T(8,128)(2,1)S(1)}, u32[]{:S(2)}, u32[]{:S(2)}) collective-permute-start(bf16[192,256]{1,0:T(8,128)(2,1)S(1)} %get-tuple-element.67), channel_id=1, source_target_pairs={{0,10},{1,11},{2,8},{3,9},{4,14},{5,15},{6,12},{7,13},{8,2},{9,3},... | collective-permute-start | bytes 294920 | tf_op jit(solution)/shard_map/ppermute | solution.py:326
  79.4 8.4 %collective-permute-start.20 = (bf16[192,256]{1,0:T(8,128)(2,1)S(1)}, bf16[192,256]{1,0:T(8,128)(2,1)S(1)}, u32[]{:S(2)}, u32[]{:S(2)}) collective-permute-start(bf16[192,256]{1,0:T(8,128)(2,1)S(1)} %fusion.1), channel_id=1, source_target_pairs={{0,12},{1,13},{2,14},{3,15},{4,8},{5,9},{6,10},{7,11},{8,4},{9,5},... | collective-permute-start | bytes 294920 | tf_op jit(solution)/shard_map/ppermute | solution.py:326

commit v3 on v2

--- a/solution.py
+++ b/solution.py
@@ -12,7 +12,8 @@
 CUTS = 4
 TILE = 256
 F32, BF16 = jnp.float32, jnp.bfloat16
-PARAMS = pltpu.CompilerParams(vmem_limit_bytes=40 * 2**20)
+PARAMS = pltpu.CompilerParams(vmem_limit_bytes=20 * 2**20)
+CHEAP = pl.CostEstimate(flops=0, bytes_accessed=0, transcendentals=0)
 SCALARS = pl.BlockSpec(memory_space=pltpu.SMEM)
 WHOLE = pl.BlockSpec(memory_space=pltpu.VMEM)
 
@@ -25,10 +26,10 @@
     return pltpu.with_memory_space_constraint(value, pltpu.HBM)
 
 
-def query_kernel(tokens, weight, out, tokens_here, weight_here, sems):
+def query_kernel(tokens, weight, source, out, staged, tokens_here, weight_here, sems):
     features = tokens.shape[1]
     depth = features // CUTS
-    copies = []
+    copies, later = [], []
     for i in range(CUTS):
         part = pl.ds(i * depth, depth)
         copies.append(
@@ -37,9 +38,13 @@
                 pltpu.make_async_copy(weight.at[part, :], weight_here.at[part, :], sems.at[1, i]),
             )
         )
+        rows = pl.ds(i * (source.shape[1] // CUTS), source.shape[1] // CUTS)
+        later.append(pltpu.make_async_copy(source.at[:, rows], staged.at[:, rows], sems.at[2, i]))
     for pair in copies:
         for copy in pair:
             copy.start()
+    for copy in later:
+        copy.start()
     total = jnp.zeros(out.shape, F32)
     for i, pair in enumerate(copies):
         for copy in pair:
@@ -47,47 +52,28 @@
         part = slice(i * depth, (i + 1) * depth)
         total += dot(tokens_here[:, part], weight_here[part, :])
     out[...] = total.astype(BF16)
-
-
-def ask(tokens, weight):
+    for copy in later:
+        copy.wait()
+
+
+def ask(tokens, weight, source):
     return pl.pallas_call(
         query_kernel,
-        in_specs=[pl.BlockSpec(memory_space=pltpu.HBM)] * 2,
-        out_specs=WHOLE,
-        out_shape=jax.ShapeDtypeStruct((tokens.shape[0], weight.shape[1]), BF16),
+        in_specs=[pl.BlockSpec(memory_space=pltpu.HBM)] * 3,
+        out_specs=[WHOLE] * 2,
+        out_shape=[
+            jax.ShapeDtypeStruct((tokens.shape[0], weight.shape[1]), BF16),
+            jax.ShapeDtypeStruct(source.shape, BF16),
+        ],
         scratch_shapes=[
             pltpu.VMEM(tokens.shape, BF16),
             pltpu.VMEM(weight.shape, BF16),
-            pltpu.SemaphoreType.DMA((2, CUTS)),
-        ],
-        compiler_params=PARAMS,
+            pltpu.SemaphoreType.DMA((3, CUTS)),
+        ],
+        compiler_params=PARAMS,
+        cost_estimate=CHEAP,
         name="query",
-    )(in_hbm(tokens), in_hbm(weight))
-
-
-def stage_kernel(source, out, sems):
-    copies = [
-        pltpu.make_async_copy(source.at[:, rows], out.at[:, rows], sems.at[i])
-        for i, rows in enumerate(
-            pl.ds(i * (source.shape[1] // CUTS), source.shape[1] // CUTS) for i in range(CUTS)
-        )
-    ]
-    for copy in copies:
-        copy.start()
-    for copy in copies:
-        copy.wait()
-
-
-def stage(source):
-    return pl.pallas_call(
-        stage_kernel,
-        in_specs=[pl.BlockSpec(memory_space=pltpu.HBM)],
-        out_specs=WHOLE,
-        out_shape=jax.ShapeDtypeStruct(source.shape, source.dtype),
-        scratch_shapes=[pltpu.SemaphoreType.DMA((CUTS,))],
-        compiler_params=PARAMS,
-        name="stage",
-    )(in_hbm(source))
+    )(in_hbm(tokens), in_hbm(weight), in_hbm(source))
 
 
 def attend_kernel(queries, source, out):
@@ -110,6 +96,7 @@
             out_specs=WHOLE,
             out_shape=jax.ShapeDtypeStruct((rows, width), BF16),
             compiler_params=PARAMS,
+        cost_estimate=CHEAP,
             name="attend",
         )(queries, source)
     return pl.pallas_call(
@@ -122,13 +109,15 @@
         out_specs=pl.BlockSpec((block, width), lambda i: (i, 0)),
         out_shape=jax.ShapeDtypeStruct((rows, width), BF16),
         compiler_params=PARAMS,
+        cost_estimate=CHEAP,
         name="attend",
     )(queries, source)
 
 
-def route_kernel(experts, ids, choice, choice_t, dispatch, first, second):
+def route_kernel(experts, parts, ids, choice, choice_t, *outs):
+    dispatch, first, second = outs[:parts], outs[parts : 2 * parts], outs[2 * parts :]
     tokens = choice.shape[0]
-    parts, slots = dispatch.shape[0], dispatch.shape[1]
+    slots = dispatch[0].shape[0]
     capacity = slots * parts // experts
     wide = lax.broadcasted_iota(jnp.int32, (tokens, experts), 1)
     tall = lax.broadcasted_iota(jnp.int32, (experts, tokens), 0)
@@ -148,62 +137,75 @@
     row = lax.broadcasted_iota(jnp.int32, (slots, tokens), 0)
     for k in range(parts):
         base = (ids[0] ^ k) * capacity if parts > 1 else 0
-        dispatch[k] = ((row + base == across0) | (row + base == across1)).astype(BF16)
-        first[k] = (lane + base == place0).astype(BF16)
-        second[k] = (lane + base == place1).astype(BF16)
+        dispatch[k][...] = ((row + base == across0) | (row + base == across1)).astype(BF16)
+        first[k][...] = (lane + base == place0).astype(BF16)
+        second[k][...] = (lane + base == place1).astype(BF16)
 
 
 def route(ids, choice, experts, parts, capacity):
     tokens = choice.shape[0]
     slots = experts * capacity // parts
-    return pl.pallas_call(
-        functools.partial(route_kernel, experts),
+    outs = pl.pallas_call(
+        functools.partial(route_kernel, experts, parts),
         in_specs=[SCALARS, WHOLE, WHOLE],
-        out_specs=[WHOLE] * 3,
-        out_shape=[
-            jax.ShapeDtypeStruct((parts, slots, tokens), BF16),
-            jax.ShapeDtypeStruct((parts, tokens, slots), BF16),
-            jax.ShapeDtypeStruct((parts, tokens, slots), BF16),
-        ],
-        compiler_params=PARAMS,
+        out_specs=[WHOLE] * (3 * parts),
+        out_shape=[jax.ShapeDtypeStruct((slots, tokens), BF16)] * parts
+        + [jax.ShapeDtypeStruct((tokens, slots), BF16)] * (2 * parts),
+        compiler_params=PARAMS,
+        cost_estimate=CHEAP,
         name="route",
     )(ids, choice, choice.T)
-
-
-def state_kernel(count, leave, *refs):
-    ids, tokens, dispatch = refs[:3]
-    contexts, weights = refs[3 : 3 + count], refs[3 + count : 3 + 2 * count]
-    state = refs[3 + 2 * count]
-    outs = refs[4 + 2 * count :]
+    return outs[:parts], outs[parts : 2 * parts], outs[2 * parts :]
+
+
+def state_kernel(count, *refs):
+    tokens, contexts, weights = refs[0], refs[1 : 1 + count], refs[1 + count : 1 + 2 * count]
+    ids, dispatch, state, out = refs[1 + 2 * count :]
     total = tokens[...].astype(F32)
     for context, weight in zip(contexts, weights):
         total += dot(context[...], weight[...])
     state[...] = total.astype(BF16)
-    for out, (k, cuts) in zip(outs, leave):
-        width = out.shape[1]
-        at = (ids[1] & (cuts - 1)) * width
-        out[...] = dot(dispatch[k], state[:, pl.ds(pl.multiple_of(at, width), width)]).astype(BF16)
-
-
-def make_state(ids, tokens, dispatch, contexts, weights, leave):
-    slots = dispatch.shape[1]
-    features = tokens.shape[1]
-    return pl.pallas_call(
-        functools.partial(state_kernel, len(contexts), leave),
-        in_specs=[SCALARS] + [WHOLE] * (2 + 2 * len(contexts)),
-        out_specs=[WHOLE] * (1 + len(leave)),
-        out_shape=[jax.ShapeDtypeStruct(tokens.shape, BF16)]
-        + [jax.ShapeDtypeStruct((slots, features // cuts), BF16) for _, cuts in leave],
-        compiler_params=PARAMS,
+    leave_kernel(ids, dispatch, state, out)
+
+
+def leave_kernel(ids, dispatch, state, out):
+    width = out.shape[1]
+    at = (ids[1] & (state.shape[1] // width - 1)) * width
+    out[...] = dot(dispatch[...], state[:, pl.ds(pl.multiple_of(at, width), width)]).astype(BF16)
+
+
+def make_state(ids, tokens, contexts, weights, dispatch, cuts):
+    return pl.pallas_call(
+        functools.partial(state_kernel, len(contexts)),
+        in_specs=[WHOLE] * (1 + 2 * len(contexts)) + [SCALARS, WHOLE],
+        out_specs=[WHOLE] * 2,
+        out_shape=[
+            jax.ShapeDtypeStruct(tokens.shape, BF16),
+            jax.ShapeDtypeStruct((dispatch.shape[0], tokens.shape[1] // cuts), BF16),
+        ],
+        compiler_params=PARAMS,
+        cost_estimate=CHEAP,
         name="state",
-    )(ids, tokens, dispatch, *contexts, *weights)
+    )(tokens, *contexts, *weights, ids, dispatch)
+
+
+def leave(ids, dispatch, state, cuts):
+    return pl.pallas_call(
+        leave_kernel,
+        in_specs=[SCALARS, WHOLE, WHOLE],
+        out_specs=WHOLE,
+        out_shape=jax.ShapeDtypeStruct((dispatch.shape[0], state.shape[1] // cuts), BF16),
+        compiler_params=PARAMS,
+        cost_estimate=CHEAP,
+        name="leave",
+    )(ids, dispatch, state)
 
 
 def home_kernel(experts, ids, state, dispatch, router, choice, own_a, own_b, gates, columns):
     half = own_a.shape[1]
     core = ids[1] & 1
-    own_a[...] = dot(dispatch[0], state[:, pl.ds(pl.multiple_of(core * half, half), half)]).astype(BF16)
-    own_b[...] = dot(dispatch[0], state[:, pl.ds(pl.multiple_of((1 - core) * half, half), half)]).astype(BF16)
+    own_a[...] = dot(dispatch[...], state[:, pl.ds(pl.multiple_of(core * half, half), half)]).astype(BF16)
+    own_b[...] = dot(dispatch[...], state[:, pl.ds(pl.multiple_of((1 - core) * half, half), half)]).astype(BF16)
     logits = dot(state[...], router[...])
     wide = lax.broadcasted_iota(jnp.int32, logits.shape, 1)
     first = jnp.sum(jnp.where(wide == choice[:, 0:1], logits, 0.0), axis=1, keepdims=True)
@@ -216,7 +218,7 @@
 
 def at_home(ids, state, dispatch, router, choice, experts, width):
     tokens, features = state.shape
-    slots = dispatch.shape[1]
+    slots = dispatch.shape[0]
     return pl.pallas_call(
         functools.partial(home_kernel, experts),
         in_specs=[SCALARS] + [WHOLE] * 4,
@@ -228,6 +230,7 @@
             jax.ShapeDtypeStruct((tokens, width), F32),
         ],
         compiler_params=PARAMS,
+        cost_estimate=CHEAP,
         name="home",
     )(ids, state, dispatch, router, choice)
 
@@ -268,6 +271,7 @@
         ],
         scratch_shapes=[pltpu.VMEM((rows, units), BF16)],
         compiler_params=PARAMS,
+        cost_estimate=CHEAP,
         name="expert",
     )(ids, *pieces, expand, shrink)
 
@@ -289,8 +293,16 @@
         out_specs=WHOLE,
         out_shape=jax.ShapeDtypeStruct(base.shape, dtype),
         compiler_params=PARAMS,
+        cost_estimate=CHEAP,
         name="combine",
     )(gates, base, first, second, *parts)
+
+
+def bits_of(count):
+    bits = []
+    while 2 ** len(bits) < count:
+        bits.insert(0, 2 ** len(bits))
+    return bits
 
 
 def local(
@@ -333,69 +345,98 @@
         return lax.optimization_barrier((value, other))[0]
 
     steps = range(groups) if direct else [0]
-    dispatch, first, second = route(ids, expert_choice, experts, len(steps), capacity)
-
-    queries = ask(tokens, query_weight)
+
+    queries, source = ask(tokens, query_weight, encoder_states[0])
     owner = source_owner[0]
+    expert_bits = bits_of(groups)
+    bits = bits_of(slices)
     if direct:
-        source = stage(after(encoder_states[0], queries))
         own = context = attend(queries, source, token_count)
-        for k in reversed(range(1, groups)):
-            asked = after(hop(queries, k, 0), own)
-            back = hop(attend(asked, source, token_count), k, 0)
-            context = jnp.where(owner == here ^ k, back, context)
+        asked, steps_of = [queries], [0]
+        for bit in expert_bits:
+            asked = asked + [hop(value if k == 0 else after(value, own), bit, 0) for k, value in zip(steps_of, asked)]
+            steps_of = steps_of + [k ^ bit for k in steps_of]
+        asked = dict(zip(steps_of, asked))
+        previous, backs = own, {}
+        for k in range(1, groups):
+            answer = attend(after(asked[k], previous), source, token_count)
+            backs[k] = hop(answer, k, 0)
+            previous = answer
+        for k in range(1, groups):
+            context = jnp.where(owner == here ^ k, backs[k], context)
     else:
         asked = lax.all_gather(queries, "expert", axis=0, tiled=True)
-        back = spread(attend(asked, encoder_states[0], token_count))
-        context = lax.dynamic_slice_in_dim(back, owner * token_count, token_count, 0)
-
-    bits = []
-    while 2 ** len(bits) < slices:
-        bits.insert(0, 2 ** len(bits))
-    weights, order = [after(output_weight, source if direct else queries)], [0]
+        previous = attend(asked, source, token_count)
+        context = lax.dynamic_slice_in_dim(spread(previous), owner * token_count, token_count, 0)
+
+    weights, order = [output_weight], [0]
     for bit in bits:
         if bit == 1:
-            weights = [after(weight, context) for weight in weights]
+            weights = [after(weight, previous) for weight in weights]
         weights = weights + [hop(weight, 0, bit) for weight in weights]
         order = order + [index ^ bit for index in order]
-    contexts = [hop(context, 0, index) for index in order]
-
-    relayed = groups - 1 if direct and pairs > 1 and groups > 1 else -1
-    leave = tuple((k, slices if k == relayed else 2) for k in reversed(range(1, groups))) if direct else ((0, 2),)
-    state, *leaving = make_state(ids, tokens, dispatch, contexts, weights, leave)
-    leaving = {k: rows for (k, _), rows in zip(leave, leaving)}
-    own_a, own_b, gates, columns = at_home(ids, state, dispatch, router_weight, expert_choice, experts, width)
+    dispatch, first, second = route(ids, after(expert_choice, context), experts, len(steps), capacity)
+    contexts = [context]
+    for bit in bits:
+        contexts = contexts + [hop(value if i == 0 else after(value, dispatch[0]), 0, bit) for i, value in enumerate(contexts)]
+
+    relayed = groups // 2 if direct and pairs > 1 and groups > 1 else -1
+    far = list(reversed(range(1, groups)))
+    sends = ([relayed] if relayed >= 0 else []) + [k for k in far if k != relayed] if direct else [0]
+    cuts = {k: slices if k == relayed else 2 for k in sends}
+    leaving = {}
+    for k in sends:
+        if not leaving:
+            state, leaving[k] = make_state(ids, tokens, contexts, weights, dispatch[k], cuts[k])
+            waited = state
+        else:
+            waited = leaving[k] = leave(ids, dispatch[k], after(state, waited), cuts[k])
+    own_a, own_b, gates, columns = at_home(
+        ids, after(state, waited), dispatch[0], router_weight, expert_choice, experts, width
+    )
 
     results = columns
-    turns = [0, *reversed(range(1, groups))] if direct else [0]
-    for k in turns:
-        if not direct:
-            mine = spread(leaving[0])
-            pieces, places = [mine, hop(mine, 0, 1)], [0, 1]
-        elif k == 0:
-            pieces, places = [own_a, own_b], [0, 1]
-        elif k == relayed:
-            pieces, places = [hop(leaving[k], k, 0)], [0]
-            for bit in bits:
-                pieces = pieces + [hop(piece, 0, bit) for piece in pieces]
-                places = places + [index ^ bit for index in places]
-        else:
-            mine = hop(leaving[k], k, 0)
-            pieces, places = [mine, hop(mine, 0, 1)], [0, 1]
-        keep, give = run_expert(ids, places, pieces, expand_weight[0], shrink_weight[0], pairs)
-        summed = keep + hop(give, 0, 1).astype(F32)
+    arrived = {k: hop(leaving[k], k, 0) for k in sends} if direct else {0: spread(leaving[0])}
+    turns = far if direct else [0]
+    inputs = {}
+    if relayed >= 0:
+        pieces, places = [arrived[relayed]], [0]
+        for bit in bits:
+            pieces = pieces + [hop(piece, 0, bit) for piece in pieces]
+            places = places + [index ^ bit for index in places]
+        inputs[relayed] = pieces, places
+
+    def sum_cores(keep, give):
+        return keep + hop(give, 0, 1).astype(F32)
+
+    def send_home(k, summed):
         if k == relayed:
             total = summed[0]
             for j in range(1, pairs):
                 total += hop(summed[j].astype(BF16), 0, 2 * j).astype(F32)
-            parts = [hop(total.astype(BF16), k, 0)]
+            return [hop(total.astype(BF16), k, 0)]
+        parts = [summed[j].astype(BF16) for j in range(pairs)]
+        return [hop(part, k, 2 * j) if direct else hop(spread(part), 0, 2 * j) for j, part in enumerate(parts)]
+
+    home = {}
+    turn_ids = ids
+    if direct:
+        keep, give = run_expert(ids, [0, 1], [own_a, own_b], expand_weight[0], shrink_weight[0], pairs)
+        turn_ids = after(ids, give)
+        home[0] = send_home(0, sum_cores(keep, after(give, arrived[sends[0]])))
+    for k in turns:
+        if k in inputs:
+            pieces, places = inputs[k]
         else:
-            parts = []
-            for j in range(pairs):
-                part = summed[j].astype(BF16)
-                parts.append(hop(part, k, 2 * j) if direct else hop(spread(part), 0, 2 * j))
-        last = k == turns[-1]
-        results = combine(gates, results, first[k], second[k], parts, BF16 if last else F32)
+            pieces, places = [arrived[k], hop(arrived[k], 0, 1)], [0, 1]
+        keep, give = run_expert(turn_ids, places, pieces, expand_weight[0], shrink_weight[0], pairs)
+        summed = sum_cores(keep, give)
+        home[k] = send_home(k, summed)
+        turn_ids = after(ids, give)
+    arrivals = ([0] if direct else []) + turns
+    for k in arrivals:
+        kind = BF16 if k == arrivals[-1] else F32
+        results = combine(gates, results, first[k], second[k], home[k], kind)
     return results
 
 

time: 91.3 us -> 94.2 us (1.032)
  waiting for transfers between devices: 39 us -> 21.6 us
  local copies, waits for them, and re-layouts: 0.5 us -> 15.6 us
  starting transfers between devices: 32.5 us -> 36.2 us
    ppermute x31, waiting for transfers between devices: 39 us -> 21.6 us  [hop(): return lax.ppermute(value, ('expert', 'mp'), moves)]
    unnamed x14 -> x62, local copies, waits for them, and re-layouts: 0.37 us -> 15.4 us
    ppermute x31, starting transfers between devices: 32.5 us -> 36.2 us  [hop(): return lax.ppermute(value, ('expert', 'mp'), moves)]
    pallas_call x3 -> x4, Pallas kernels: 4.05 us -> 4.91 us  [the longest x1 2.06 us: make_state(): pl.pallas_call(functools.partial(state_kernel, len(contexts)), in_specs=[...]
  transfers between devices with their start and end apart: 31 -> 31, of which waited for: 10 -> 10; matrix products, arithmetic and copies ran while one was open for 1% -> 1% of each run, Pallas kernels for 14% -> 17%
where the time goes in v3:
time: 94.2 us; the launch traced here: 93.5 us
  starting transfers between devices  36.2 us (38%)
  waiting for transfers between devices  21.6 us (23%)
  Pallas kernels  18.7 us (20%)
  local copies, waits for them, and re-layouts  15.6 us (17%)
  between operations  1.1 us (1%)
    ppermute x31, starting transfers between devices, hop(): return lax.ppermute(value, ('expert', 'mp'), moves)  36.2 us
    ppermute x31, waiting for transfers between devices, hop(): return lax.ppermute(value, ('expert', 'mp'), moves)  21.6 us
    unnamed x62, local copies, waits for them, and re-layouts  15.4 us
    pallas_call x4, Pallas kernels, run_expert(): pl.pallas_call(functools.partial(expert_kernel, tuple(order)), in_specs=[...  6.19 us
    pallas_call x4, Pallas kernels, attend(): pl.pallas_call(attend_kernel, in_specs=[WHOLE] * 2, out_specs=WHOLE, out_...  3.09 us
    pallas_call x1, Pallas kernels, make_state(): pl.pallas_call(functools.partial(state_kernel, len(contexts)), in_specs=[...  2.06 us
  transfers between devices with their start and end apart: 31, of which 10 were waited for; matrix products, arithmetic and copies ran while one was open for 1% of the time, Pallas kernels for 17%

profile of v3, /device:TPU:0, one launch (start us, length us, event | category | flops | bytes accessed | tf_op | source)
XLA Modules:
  0.0 93.5 jit_solution(4724011292669480668)
XLA Ops:
  0.0 2.9 %collective-permute-start.9 = (bf16[256,1024]{1,0:T(8,128)(2,1)}, bf16[256,1024]{1,0:T(8,128)(2,1)S(1)}, u32[]{:S(2)}, u32[]{:S(2)}) collective-permute-start(bf16[256,1024]{1,0:T(8,128)(2,1)} %refs_5_), channel_id=1, source_target_pairs={{0,2},{1,3},{2,0},{3,1},{4,6},{5,7},{6,4},{7,5},{8,10},{9,11},{10,... | collective-permute-start | bytes 1572872 | tf_op jit(solution)/shard_map/ppermute | solution.py:338
  2.9 1.9 %query.1 = (bf16[256,256]{1,0:T(8,128)(2,1)S(1)}, bf16[2,512,256]{2,1,0:T(8,128)(2,1)S(1)}) custom-call(bf16[256,1024]{1,0:T(8,128)(2,1)} %refs_0_.1, bf16[1024,256]{1,0:T(8,128)(2,1)} %weight.1, bf16[2,512,256]{2,1,0:T(8,128)(2,1)} %bitcast.39), custom_call_target="tpu_custom_call" | custom-call | tf_op jit(solution)/shard_map/query/pallas_call | solution.py:60
  4.8 2.7 %collective-permute-start = (bf16[256,256]{1,0:T(8,128)(2,1)S(1)}, bf16[256,256]{1,0:T(8,128)(2,1)S(1)}, u32[]{:S(2)}, u32[]{:S(2)}) collective-permute-start(bf16[256,256]{1,0:T(8,128)(2,1)S(1)} %get-tuple-element.48.queries), channel_id=1, source_target_pairs={{0,8},{1,9},{2,10},{3,11},{4,12},{5,13},{6,14},{7,15},{8,0},{9,1},... | collective-permute-start | bytes 393224 | tf_op jit(solution)/shard_map/ppermute | solution.py:338
  7.5 1.6 %collective-permute-start.2 = (bf16[256,256]{1,0:T(8,128)(2,1)S(1)}, bf16[256,256]{1,0:T(8,128)(2,1)S(1)}, u32[]{:S(2)}, u32[]{:S(2)}) collective-permute-start(bf16[256,256]{1,0:T(8,128)(2,1)S(1)} %get-tuple-element.48.queries), channel_id=1, source_target_pairs={{0,4},{1,5},{2,6},{3,7},{4,0},{5,1},{6,2},{7,3},{8,12},{9,13},{10,... | collective-permute-start | bytes 393224 | tf_op jit(solution)/shard_map/ppermute | solution.py:338
  9.1 0.8 attend.4
  9.9 3.8 %collective-permute-done.queries = bf16[256,256]{1,0:T(8,128)(2,1)S(1)} collective-permute-done((bf16[256,256]{1,0:T(8,128)(2,1)S(1)}, bf16[256,256]{1,0:T(8,128)(2,1)S(1)}, u32[]{:S(2)}, u32[]{:S(2)}) %collective-permute-start) | collective-permute-done | bytes 131104 | tf_op jit(solution)/shard_map/ppermute | solution.py:338
  13.7 0.6 collective-permute-start.1
  14.2 0.8 attend.5
  15.0 1.5 %collective-permute-start.5 = (bf16[256,256]{1,0:T(8,128)(2,1)S(1)}, bf16[256,256]{1,0:T(8,128)(2,1)S(1)}, u32[]{:S(2)}, u32[]{:S(2)}) collective-permute-start(bf16[256,256]{1,0:T(8,128)(2,1)S(1)} %attend.5), channel_id=1, source_target_pairs={{0,4},{1,5},{2,6},{3,7},{4,0},{5,1},{6,2},{7,3},{8,12},{9,13},{10,... | collective-permute-start | bytes 393224 | tf_op jit(solution)/shard_map/ppermute | solution.py:338
  16.6 0.8 attend.6
  17.3 2.0 %collective-permute-start.4 = (bf16[256,256]{1,0:T(8,128)(2,1)S(1)}, bf16[256,256]{1,0:T(8,128)(2,1)S(1)}, u32[]{:S(2)}, u32[]{:S(2)}) collective-permute-start(bf16[256,256]{1,0:T(8,128)(2,1)S(1)} %attend.6), channel_id=1, source_target_pairs={{0,8},{1,9},{2,10},{3,11},{4,12},{5,13},{6,14},{7,15},{8,0},{9,1},... | collective-permute-start | bytes 393224 | tf_op jit(solution)/shard_map/ppermute | solution.py:338
  19.3 0.5 collective-permute-done.1.queries
  19.9 0.8 attend.7
  20.6 3.6 %collective-permute-start.3 = (bf16[256,256]{1,0:T(8,128)(2,1)S(1)}, bf16[256,256]{1,0:T(8,128)(2,1)}, u32[]{:S(2)}, u32[]{:S(2)}) collective-permute-start(bf16[256,256]{1,0:T(8,128)(2,1)S(1)} %attend.7), channel_id=1, source_target_pairs={{0,12},{1,13},{2,14},{3,15},{4,8},{5,9},{6,10},{7,11},{8,4},{9,5},... | collective-permute-start | bytes 393224 | tf_op jit(solution)/shard_map/ppermute | solution.py:338
  24.3 0.5 collective-permute-start.11
  25.5 3.9 %collective-permute-done.3 = bf16[256,256]{1,0:T(8,128)(2,1)} collective-permute-done((bf16[256,256]{1,0:T(8,128)(2,1)S(1)}, bf16[256,256]{1,0:T(8,128)(2,1)}, u32[]{:S(2)}, u32[]{:S(2)}) %collective-permute-start.3) | collective-permute-done | bytes 131104 | tf_op jit(solution)/shard_map/ppermute | solution.py:338
  29.4 0.6 collective-permute-start.6
  30.2 1.4 %route.1 = (bf16[192,256]{1,0:T(8,128)(2,1)S(1)}, bf16[192,256]{1,0:T(8,128)(2,1)S(1)}, bf16[192,256]{1,0:T(8,128)(2,1)S(1)}, bf16[192,256]{1,0:T(8,128)(2,1)S(1...) custom-call(s32[2]{0:T(128)S(1)} %pad_add_fusion.ids.refs_9_.refs_0_, ...), custom_call_target="tpu_custom_call" | custom-call | tf_op jit(solution)/shard_map/route/pallas_call | solution.py:148
  31.6 0.6 copy-done.6
  32.3 0.6 copy-done.8
  32.9 0.6 copy-done.10
  33.6 0.6 copy-done.12
  34.2 0.7 copy-done.14
  34.9 0.7 copy-done.16
  35.5 0.6 copy-done.22
  36.1 0.6 copy-done.24
  36.8 0.7 copy-done.26
  37.4 0.5 collective-permute-start.8
  37.9 0.7 copy-done.18
  38.6 0.7 copy-done.20
  39.3 0.8 copy-done.4
  40.1 1.0 %copy-done.5 = bf16[256,1024]{1,0:T(8,128)(2,1)S(1)} copy-done((bf16[256,1024]{1,0:T(8,128)(2,1)S(1)}, bf16[256,1024]{1,0:T(8,128)(2,1)}, u32[]{:S(2)}) %copy-start.5) | copy-done | bytes 524312
  41.1 0.9 copy-done.19
  42.0 0.9 copy-done.21
  42.9 2.1 %state.1 = (bf16[256,1024]{1,0:T(8,128)(2,1)S(1)}, bf16[192,256]{1,0:T(8,128)(2,1)}) custom-call(bf16[256,1024]{1,0:T(8,128)(2,1)S(1)} %copy-done.2, bf16[256,256]{1,0:T(8,128)(2,1)S(1)} %select_select_fusion.refs_1_, bf16[256,256]{1,0:T(8,128)(2,1)S(1)} %copy-done.19, bf16[256,256]{1,0:T(8,128)(2,1)S(1)} %copy-done.21, ...), custom_call_target="tpu_custom_call" | custom-call | tf_op jit(solution)/shard_map/state/pallas_call | solution.py:178
  45.0 4.7 %collective-permute-start.12 = (bf16[192,256]{1,0:T(8,128)(2,1)}, bf16[192,256]{1,0:T(8,128)(2,1)S(1)}, u32[]{:S(2)}, u32[]{:S(2)}) collective-permute-start(bf16[192,256]{1,0:T(8,128)(2,1)} %get-tuple-element.74), channel_id=1, source_target_pairs={{0,8},{1,9},{2,10},{3,11},{4,12},{5,13},{6,14},{7,15},{8,0},{9,1},... | collective-permute-start | bytes 294920 | tf_op jit(solution)/shard_map/ppermute | solution.py:338
  50.0 0.9 copy-done.27
  50.9 0.7 leave.2
  51.7 0.7 collective-permute-start.15
  52.4 0.9 copy-done.25
  53.2 0.7 leave.3
  54.2 0.9 copy-done.23
  55.1 1.0 %home.1 = (bf16[192,512]{1,0:T(8,128)(2,1)S(1)}, bf16[192,512]{1,0:T(8,128)(2,1)S(1)}, f32[256,2]{1,0:T(8,128)S(1)}, f32[256,256]{1,0:T(8,128)S(1)}) custom-call(s32[2]{0:T(128)S(1)} %pad_add_fusion.ids.refs_9_.refs_0_, bf16[256,1024]{1,0:T(8,128)(2,1)S(1)} %get-tuple-element.65.state, bf16[192,256]{1,0:T(8,128)(2,1)S(1)} %copy-done.23, ...), custom_call_target="tpu_custom_call" | custom-call | tf_op jit(solution)/shard_map/home/pallas_call | solution.py:222
  56.2 1.6 %copy-done.1 = bf16[1,1024,1024]{2,1,0:T(8,128)(2,1)S(1)} copy-done((bf16[1,1024,1024]{2,1,0:T(8,128)(2,1)S(1)}, bf16[1,1024,1024]{2,1,0:T(8,128)(2,1)}, u32[]{:S(2)}) %copy-start.1) | copy-done | bytes 2097176
  57.8 1.5 %expert.4 = (f32[2,192,256]{2,1,0:T(8,128)S(1)}, bf16[2,192,256]{2,1,0:T(8,128)(2,1)S(1)}) custom-call(s32[2]{0:T(128)S(1)} %pad_add_fusion.ids.refs_9_.refs_0_, bf16[192,512]{1,0:T(8,128)(2,1)S(1)} %get-tuple-element.70.refs_1_, bf16[192,512]{1,0:T(8,128)(2,1)S(1)} %get-tuple-element.71.refs_2_, bf16[1024,1024]{1,0:T(8,128)(2,1)S(1)} %bitcast.30, ...), custom_call_target="tpu_custom_call" | custom-call | tf_op jit(solution)/shard_map/expert/pallas_call | solution.py:264
  59.4 1.6 %collective-permute-start.20 = (bf16[192,256]{1,0:T(8,128)(2,1)S(1)}, bf16[192,256]{1,0:T(8,128)(2,1)S(1)}, u32[]{:S(2)}, u32[]{:S(2)}) collective-permute-start(bf16[192,256]{1,0:T(8,128)(2,1)S(1)} %collective-permute-done.12.refs_1_), channel_id=1, source_target_pairs={{0,2},{1,3},{2,0},{3,1},{4,6},{5,7},{6,4},{7,5},{8,10},{9,11},{10,... | collective-permute-start | bytes 294920 | tf_op jit(solution)/shard_map/ppermute | solution.py:338
  61.1 0.3 collective-permute-done.15.refs_1_
  61.5 3.0 %collective-permute-done.26.refs_1_ = bf16[192,512]{1,0:T(8,128)(2,1)S(1)} collective-permute-done((bf16[192,512]{1,0:T(8,128)(2,1)S(1)}, bf16[192,512]{1,0:T(8,128)(2,1)S(1)}, u32[]{:S(2)}, u32[]{:S(2)}) %collective-permute-start.26) | collective-permute-done | bytes 196640 | tf_op jit(solution)/shard_map/ppermute | solution.py:338
  64.6 0.3 collective-permute-start.22
  65.0 1.5 %expert.5 = (f32[2,192,256]{2,1,0:T(8,128)S(1)}, bf16[2,192,256]{2,1,0:T(8,128)(2,1)S(1)}) custom-call(s32[2]{0:T(128)S(1)} %pad_add_fusion.ids.refs_9_.refs_0_, bf16[192,512]{1,0:T(8,128)(2,1)S(1)} %collective-permute-done.15.refs_1_, bf16[192,512]{1,0:T(8,128)(2,1)S(1)} %collective-permute-done.16.refs_2_, bf16[1024,1024]{1,0:T(8,128)(2,1)S(1)} %bitcast.31, ...), custom_call_target="tpu_custom_call" | custom-call | tf_op jit(solution)/shard_map/expert/pallas_call | solution.py:264
  66.8 1.6 %collective-permute-start.14 = (bf16[192,256]{1,0:T(8,128)(2,1)S(1)}, bf16[192,256]{1,0:T(8,128)(2,1)S(1)}, u32[]{:S(2)}, u32[]{:S(2)}) collective-permute-start(bf16[192,256]{1,0:T(8,128)(2,1)S(1)} %get-tuple-element.95), channel_id=1, source_target_pairs={{0,2},{1,3},{2,0},{3,1},{4,6},{5,7},{6,4},{7,5},{8,10},{9,11},{10,... | collective-permute-start | bytes 294920 | tf_op jit(solution)/shard_map/ppermute | solution.py:338
  68.4 1.6 %expert.6 = (f32[2,192,256]{2,1,0:T(8,128)S(1)}, bf16[2,192,256]{2,1,0:T(8,128)(2,1)S(1)}) custom-call(s32[2]{0:T(128)S(1)} %pad_add_fusion.ids.refs_9_.refs_0_, bf16[192,256]{1,0:T(8,128)(2,1)S(1)} %collective-permute-done.12.refs_1_, bf16[192,256]{1,0:T(8,128)(2,1)S(1)} %collective-permute-done.20.refs_2_, ...), custom_call_target="tpu_custom_call" | custom-call | tf_op jit(solution)/shard_map/expert/pallas_call | solution.py:264
  70.1 1.5 %expert.7 = (f32[2,192,256]{2,1,0:T(8,128)S(1)}, bf16[2,192,256]{2,1,0:T(8,128)(2,1)S(1)}) custom-call(s32[2]{0:T(128)S(1)} %pad_add_fusion.ids.refs_9_.refs_0_, bf16[192,512]{1,0:T(8,128)(2,1)S(1)} %collective-permute-done.26.refs_1_, bf16[192,512]{1,0:T(8,128)(2,1)S(1)} %collective-permute-done.27.refs_2_, bf16[1024,1024]{1,0:T(8,128)(2,1)S(1)} %bitcast.33, ...), custom_call_target="tpu_custom_call" | custom-call | tf_op jit(solution)/shard_map/expert/pallas_call | solution.py:264
  71.7 0.5 collective-permute-start.28
  72.3 3.2 %collective-permute-start.18 = (bf16[192,256]{1,0:T(8,128)(2,1)S(1)}, bf16[192,256]{1,0:T(8,128)(2,1)S(1)}, u32[]{:S(2)}, u32[]{:S(2)}) collective-permute-start(bf16[192,256]{1,0:T(8,128)(2,1)S(1)} %get-tuple-element.94), channel_id=1, source_target_pairs={{0,12},{1,13},{2,14},{3,15},{4,8},{5,9},{6,10},{7,11},{8,4},{9,5},... | collective-permute-start | bytes 294920 | tf_op jit(solution)/shard_map/ppermute | solution.py:338
  75.4 0.7 collective-permute-start.19
  76.2 1.6 %collective-permute-start.24 = (bf16[192,256]{1,0:T(8,128)(2,1)S(1)}, bf16[192,256]{1,0:T(8,128)(2,1)S(1)}, u32[]{:S(2)}, u32[]{:S(2)}) collective-permute-start(bf16[192,256]{1,0:T(8,128)(2,1)S(1)} %fusion.2), channel_id=1, source_target_pairs={{0,2},{1,3},{2,0},{3,1},{4,6},{5,7},{6,4},{7,5},{8,10},{9,11},{10,... | collective-permute-start | bytes 294920 | tf_op jit(solution)/shard_map/ppermute | solution.py:338
  77.9 5.2 %collective-permute-done.24 = bf16[192,256]{1,0:T(8,128)(2,1)S(1)} collective-permute-done((bf16[192,256]{1,0:T(8,128)(2,1)S(1)}, bf16[192,256]{1,0:T(8,128)(2,1)S(1)}, u32[]{:S(2)}, u32[]{:S(2)}) %collective-permute-start.24) | collective-permute-done | bytes 98336 | tf_op jit(solution)/shard_map/ppermute | solution.py:338
  83.1 3.1 %collective-permute-start.29 = (bf16[192,256]{1,0:T(8,128)(2,1)S(1)}, bf16[192,256]{1,0:T(8,128)(2,1)S(1)}, u32[]{:S(2)}, u32[]{:S(2)}) collective-permute-start(bf16[192,256]{1,0:T(8,128)(2,1)S(1)} %get-tuple-element.92), channel_id=1, source_target_pairs={{0,4},{1,5},{2,6},{3,7},{4,0},{5,1},{6,2},{7,3},{8,12},{9,13},{10,... | collective-permute-start | bytes 294920 | tf_op jit(solution)/shard_map/ppermute | solution.py:338
  86.2 0.8 collective-permute-start.30
  87.6 1.9 %collective-permute-done.25.refs_0_ = bf16[192,256]{1,0:T(8,128)(2,1)S(1)} collective-permute-done((bf16[192,256]{1,0:T(8,128)(2,1)S(1)}, bf16[192,256]{1,0:T(8,128)(2,1)S(1)}, u32[]{:S(2)}, u32[]{:S(2)}) %collective-permute-start.25) | collective-permute-done | bytes 98336 | tf_op jit(solution)/shard_map/ppermute | solution.py:338
  89.8 0.7 collective-permute-done.29.refs_0_
  90.5 2.1 %collective-permute-done.30.refs_1_ = bf16[192,256]{1,0:T(8,128)(2,1)S(1)} collective-permute-done((bf16[192,256]{1,0:T(8,128)(2,1)S(1)}, bf16[192,256]{1,0:T(8,128)(2,1)S(1)}, u32[]{:S(2)}, u32[]{:S(2)}) %collective-permute-start.30) | collective-permute-done | bytes 98336 | tf_op jit(solution)/shard_map/ppermute | solution.py:338
  92.6 0.9 combine.7
  (90 shorter events, 2.8 us)
Async XLA Ops:
  0.0 24.3 %collective-permute-start.9 = (bf16[256,1024]{1,0:T(8,128)(2,1)}, bf16[256,1024]{1,0:T(8,128)(2,1)S(1)}, u32[]{:S(2)}, u32[]{:S(2)}) collective-permute-start(bf16[256,1024]{1,0:T(8,128)(2,1)} %refs_5_), channel_id=1, source_target_pairs={{0,2},{1,3},{2,0},{3,1},{4,6},{5,7},{6,4},{7,5},{8,10},{9,11},{10,... | collective-permute-start | bytes 1572872 | tf_op jit(solution)/shard_map/ppermute | solution.py:338
  2.9 21.3 %copy-start.3 = (bf16[256,1024]{1,0:T(8,128)(2,1)S(1)}, bf16[256,1024]{1,0:T(8,128)(2,1)}, u32[]{:S(2)}) copy-start(bf16[256,1024]{1,0:T(8,128)(2,1)} %refs_5_) | copy-start | bytes 1572868
  4.8 25.3 %copy-start.28 = (s32[256,2]{0,1:T(2,128)S(1)}, s32[256,2]{0,1:T(2,128)}, u32[]{:S(2)}) copy-start(s32[256,2]{0,1:T(2,128)} %param.15) | copy-start | bytes 6148
  4.8 35.2 %copy-start.2 = (bf16[256,1024]{1,0:T(8,128)(2,1)S(1)}, bf16[256,1024]{1,0:T(8,128)(2,1)}, u32[]{:S(2)}) copy-start(bf16[256,1024]{1,0:T(8,128)(2,1)} %refs_0_.1) | copy-start | bytes 1572868
  4.8 8.8 %collective-permute-start = (bf16[256,256]{1,0:T(8,128)(2,1)S(1)}, bf16[256,256]{1,0:T(8,128)(2,1)S(1)}, u32[]{:S(2)}, u32[]{:S(2)}) collective-permute-start(bf16[256,256]{1,0:T(8,128)(2,1)S(1)} %get-tuple-element.48.queries), channel_id=1, source_target_pairs={{0,8},{1,9},{2,10},{3,11},{4,12},{5,13},{6,14},{7,15},{8,0},{9,1},... | collective-permute-start | bytes 393224 | tf_op jit(solution)/shard_map/ppermute | solution.py:338
  7.5 6.7 %collective-permute-start.2 = (bf16[256,256]{1,0:T(8,128)(2,1)S(1)}, bf16[256,256]{1,0:T(8,128)(2,1)S(1)}, u32[]{:S(2)}, u32[]{:S(2)}) collective-permute-start(bf16[256,256]{1,0:T(8,128)(2,1)S(1)} %get-tuple-element.48.queries), channel_id=1, source_target_pairs={{0,4},{1,5},{2,6},{3,7},{4,0},{5,1},{6,2},{7,3},{8,12},{9,13},{10,... | collective-permute-start | bytes 393224 | tf_op jit(solution)/shard_map/ppermute | solution.py:338
  13.7 6.2 %collective-permute-start.1 = (bf16[256,256]{1,0:T(8,128)(2,1)S(1)}, bf16[256,256]{1,0:T(8,128)(2,1)S(1)}, u32[]{:S(2)}, u32[]{:S(2)}) collective-permute-start(bf16[256,256]{1,0:T(8,128)(2,1)S(1)} %collective-permute-done.queries), channel_id=1, source_target_pairs={{0,4},{1,5},{2,6},{3,7},{4,0},{5,1},{6,2},{7,3},{8,12},{9,13},{10,... | collective-permute-start | bytes 393224 | tf_op jit(solution)/shard_map/ppermute | solution.py:338
  15.0 10.4 %collective-permute-start.5 = (bf16[256,256]{1,0:T(8,128)(2,1)S(1)}, bf16[256,256]{1,0:T(8,128)(2,1)S(1)}, u32[]{:S(2)}, u32[]{:S(2)}) collective-permute-start(bf16[256,256]{1,0:T(8,128)(2,1)S(1)} %attend.5), channel_id=1, source_target_pairs={{0,4},{1,5},{2,6},{3,7},{4,0},{5,1},{6,2},{7,3},{8,12},{9,13},{10,... | collective-permute-start | bytes 393224 | tf_op jit(solution)/shard_map/ppermute | solution.py:338
  17.3 8.1 %collective-permute-start.4 = (bf16[256,256]{1,0:T(8,128)(2,1)S(1)}, bf16[256,256]{1,0:T(8,128)(2,1)S(1)}, u32[]{:S(2)}, u32[]{:S(2)}) collective-permute-start(bf16[256,256]{1,0:T(8,128)(2,1)S(1)} %attend.6), channel_id=1, source_target_pairs={{0,8},{1,9},{2,10},{3,11},{4,12},{5,13},{6,14},{7,15},{8,0},{9,1},... | collective-permute-start | bytes 393224 | tf_op jit(solution)/shard_map/ppermute | solution.py:338
  20.6 8.7 %collective-permute-start.3 = (bf16[256,256]{1,0:T(8,128)(2,1)S(1)}, bf16[256,256]{1,0:T(8,128)(2,1)}, u32[]{:S(2)}, u32[]{:S(2)}) collective-permute-start(bf16[256,256]{1,0:T(8,128)(2,1)S(1)} %attend.7), channel_id=1, source_target_pairs={{0,12},{1,13},{2,14},{3,15},{4,8},{5,9},{6,10},{7,11},{8,4},{9,5},... | collective-permute-start | bytes 393224 | tf_op jit(solution)/shard_map/ppermute | solution.py:338
  24.3 15.0 %collective-permute-start.10 = (bf16[256,1024]{1,0:T(8,128)(2,1)S(1)}, bf16[256,1024]{1,0:T(8,128)(2,1)S(1)}, u32[]{:S(2)}, u32[]{:S(2)}) collective-permute-start(bf16[256,1024]{1,0:T(8,128)(2,1)S(1)} %copy-done.3), channel_id=1, source_target_pairs={{0,1},{1,0},{2,3},{3,2},{4,5},{5,4},{6,7},{7,6},{8,9},{9,8},{10,11... | collective-permute-start | bytes 1572872 | tf_op jit(solution)/shard_map/ppermute | solution.py:338
  24.3 15.0 %collective-permute-start.11 = (bf16[256,1024]{1,0:T(8,128)(2,1)S(1)}, bf16[256,1024]{1,0:T(8,128)(2,1)S(1)}, u32[]{:S(2)}, u32[]{:S(2)}) collective-permute-start(bf16[256,1024]{1,0:T(8,128)(2,1)S(1)} %collective-permute-done.9.refs_6_), channel_id=1, source_target_pairs={{0,1},{1,0},{2,3},{3,2},{4,5},{5,4},{6,7},{7,6},{8,9},{9,8},{10,11... | collective-permute-start | bytes 1572872 | tf_op jit(solution)/shard_map/ppermute | solution.py:338
  25.4 24.4 %copy-start.29 = (bf16[1024,4]{0,1:T(4,128)(2,1)S(1)}, bf16[1024,4]{0,1:T(4,128)(2,1)}, u32[]{:S(2)}) copy-start(bf16[1024,4]{0,1:T(4,128)(2,1)} %param.14) | copy-start | bytes 24580
  29.4 8.0 %collective-permute-start.6 = (bf16[256,256]{1,0:T(8,128)(2,1)S(1)}, bf16[256,256]{1,0:T(8,128)(2,1)S(1)}, u32[]{:S(2)}, u32[]{:S(2)}) collective-permute-start(bf16[256,256]{1,0:T(8,128)(2,1)S(1)} %select_select_fusion.refs_1_), channel_id=1, source_target_pairs={{0,2},{1,3},{2,0},{3,1},{4,6},{5,7},{6,4},{7,5},{8,10},{9,11},{10,... | collective-permute-start | bytes 393224 | tf_op jit(solution)/shard_map/ppermute | solution.py:338
  30.1 8.5 %collective-permute-start.7 = (bf16[256,256]{1,0:T(8,128)(2,1)S(1)}, bf16[256,256]{1,0:T(8,128)(2,1)S(1)}, u32[]{:S(2)}, u32[]{:S(2)}) collective-permute-start(bf16[256,256]{1,0:T(8,128)(2,1)S(1)} %select_select_fusion.refs_1_), channel_id=1, source_target_pairs={{0,1},{1,0},{2,3},{3,2},{4,5},{5,4},{6,7},{7,6},{8,9},{9,8},{10,11... | collective-permute-start | bytes 393224 | tf_op jit(solution)/shard_map/ppermute | solution.py:338
  31.6 0.7 copy-start.6
  32.3 0.6 copy-start.8
  32.9 0.6 copy-start.10
  33.6 0.6 copy-start.12
  34.2 0.7 copy-start.14
  34.9 0.7 copy-start.16
  35.5 0.6 copy-start.22
  36.1 0.6 copy-start.24
  36.8 0.7 copy-start.26
  37.4 1.8 %collective-permute-start.8 = (bf16[256,256]{1,0:T(8,128)(2,1)S(1)}, bf16[256,256]{1,0:T(8,128)(2,1)S(1)}, u32[]{:S(2)}, u32[]{:S(2)}) collective-permute-start(bf16[256,256]{1,0:T(8,128)(2,1)S(1)} %collective-permute-done.6.refs_2_), channel_id=1, source_target_pairs={{0,1},{1,0},{2,3},{3,2},{4,5},{5,4},{6,7},{7,6},{8,9},{9,8},{10,11... | collective-permute-start | bytes 393224 | tf_op jit(solution)/shard_map/ppermute | solution.py:338
  37.9 0.7 copy-start.18
  38.6 0.7 copy-start.20
  39.2 0.8 copy-start.4
  40.1 1.0 %copy-start.5 = (bf16[256,1024]{1,0:T(8,128)(2,1)S(1)}, bf16[256,1024]{1,0:T(8,128)(2,1)}, u32[]{:S(2)}) copy-start(bf16[256,1024]{1,0:T(8,128)(2,1)} %copy-done.4) | copy-start | bytes 1572868
  41.1 0.9 copy-start.19
  42.0 0.9 copy-start.21
  45.0 11.2 %copy-start = (bf16[1,1024,1024]{2,1,0:T(8,128)(2,1)S(1)}, bf16[1,1024,1024]{2,1,0:T(8,128)(2,1)}, u32[]{:S(2)}) copy-start(bf16[1,1024,1024]{2,1,0:T(8,128)(2,1)} %param.16) | copy-start | bytes 6291460
  45.0 14.3 %collective-permute-start.12 = (bf16[192,256]{1,0:T(8,128)(2,1)}, bf16[192,256]{1,0:T(8,128)(2,1)S(1)}, u32[]{:S(2)}, u32[]{:S(2)}) collective-permute-start(bf16[192,256]{1,0:T(8,128)(2,1)} %get-tuple-element.74), channel_id=1, source_target_pairs={{0,8},{1,9},{2,10},{3,11},{4,12},{5,13},{6,14},{7,15},{8,0},{9,1},... | collective-permute-start | bytes 294920 | tf_op jit(solution)/shard_map/ppermute | solution.py:338
  50.0 0.9 copy-start.27
  51.7 9.7 %collective-permute-start.15 = (bf16[192,512]{1,0:T(8,128)(2,1)S(1)}, bf16[192,512]{1,0:T(8,128)(2,1)S(1)}, u32[]{:S(2)}, u32[]{:S(2)}) collective-permute-start(bf16[192,512]{1,0:T(8,128)(2,1)S(1)} %leave.2), channel_id=1, source_target_pairs={{0,12},{1,13},{2,14},{3,15},{4,8},{5,9},{6,10},{7,11},{8,4},{9,5},... | collective-permute-start | bytes 589832 | tf_op jit(solution)/shard_map/ppermute | solution.py:338
  52.4 0.9 copy-start.25
  54.0 10.4 %collective-permute-start.26 = (bf16[192,512]{1,0:T(8,128)(2,1)S(1)}, bf16[192,512]{1,0:T(8,128)(2,1)S(1)}, u32[]{:S(2)}, u32[]{:S(2)}) collective-permute-start(bf16[192,512]{1,0:T(8,128)(2,1)S(1)} %leave.3), channel_id=1, source_target_pairs={{0,4},{1,5},{2,6},{3,7},{4,0},{5,1},{6,2},{7,3},{8,12},{9,13},{10,... | collective-permute-start | bytes 589832 | tf_op jit(solution)/shard_map/ppermute | solution.py:338
  54.2 0.9 copy-start.23
  56.2 1.6 %copy-start.1 = (bf16[1,1024,1024]{2,1,0:T(8,128)(2,1)S(1)}, bf16[1,1024,1024]{2,1,0:T(8,128)(2,1)}, u32[]{:S(2)}) copy-start(bf16[1,1024,1024]{2,1,0:T(8,128)(2,1)} %param.17) | copy-start | bytes 6291460
  59.3 5.6 %collective-permute-start.13 = (bf16[2,192,256]{2,1,0:T(8,128)(2,1)S(1)}, bf16[2,192,256]{2,1,0:T(8,128)(2,1)S(1)}, u32[]{:S(2)}, u32[]{:S(2)}) collective-permute-start(bf16[2,192,256]{2,1,0:T(8,128)(2,1)S(1)} %get-tuple-element.75), channel_id=1, source_target_pairs={{0,1},{1,0},{2,3},{3,2},{4,5},{5,4},{6,7},{7,6},{8,9},{9,8},{10,11... | collective-permute-start | bytes 589832 | tf_op jit(solution)/shard_map/ppermute | solution.py:338
  59.4 5.2 %collective-permute-start.20 = (bf16[192,256]{1,0:T(8,128)(2,1)S(1)}, bf16[192,256]{1,0:T(8,128)(2,1)S(1)}, u32[]{:S(2)}, u32[]{:S(2)}) collective-permute-start(bf16[192,256]{1,0:T(8,128)(2,1)S(1)} %collective-permute-done.12.refs_1_), channel_id=1, source_target_pairs={{0,2},{1,3},{2,0},{3,1},{4,6},{5,7},{6,4},{7,5},{8,10},{9,11},{10,... | collective-permute-start | bytes 294920 | tf_op jit(solution)/shard_map/ppermute | solution.py:338
  61.0 7.4 %collective-permute-start.21 = (bf16[192,256]{1,0:T(8,128)(2,1)S(1)}, bf16[192,256]{1,0:T(8,128)(2,1)S(1)}, u32[]{:S(2)}, u32[]{:S(2)}) collective-permute-start(bf16[192,256]{1,0:T(8,128)(2,1)S(1)} %collective-permute-done.12.refs_1_), channel_id=1, source_target_pairs={{0,1},{1,0},{2,3},{3,2},{4,5},{5,4},{6,7},{7,6},{8,9},{9,8},{10,11... | collective-permute-start | bytes 294920 | tf_op jit(solution)/shard_map/ppermute | solution.py:338
  61.4 3.6 %collective-permute-start.16 = (bf16[192,512]{1,0:T(8,128)(2,1)S(1)}, bf16[192,512]{1,0:T(8,128)(2,1)S(1)}, u32[]{:S(2)}, u32[]{:S(2)}) collective-permute-start(bf16[192,512]{1,0:T(8,128)(2,1)S(1)} %collective-permute-done.15.refs_1_), channel_id=1, source_target_pairs={{0,1},{1,0},{2,3},{3,2},{4,5},{5,4},{6,7},{7,6},{8,9},{9,8},{10,11... | collective-permute-start | bytes 589832 | tf_op jit(solution)/shard_map/ppermute | solution.py:338
  64.4 5.7 %collective-permute-start.27 = (bf16[192,512]{1,0:T(8,128)(2,1)S(1)}, bf16[192,512]{1,0:T(8,128)(2,1)S(1)}, u32[]{:S(2)}, u32[]{:S(2)}) collective-permute-start(bf16[192,512]{1,0:T(8,128)(2,1)S(1)} %collective-permute-done.26.refs_1_), channel_id=1, source_target_pairs={{0,1},{1,0},{2,3},{3,2},{4,5},{5,4},{6,7},{7,6},{8,9},{9,8},{10,11... | collective-permute-start | bytes 589832 | tf_op jit(solution)/shard_map/ppermute | solution.py:338
  64.6 3.8 %collective-permute-start.22 = (bf16[192,256]{1,0:T(8,128)(2,1)S(1)}, bf16[192,256]{1,0:T(8,128)(2,1)S(1)}, u32[]{:S(2)}, u32[]{:S(2)}) collective-permute-start(bf16[192,256]{1,0:T(8,128)(2,1)S(1)} %collective-permute-done.20.refs_2_), channel_id=1, source_target_pairs={{0,1},{1,0},{2,3},{3,2},{4,5},{5,4},{6,7},{7,6},{8,9},{9,8},{10,11... | collective-permute-start | bytes 294920 | tf_op jit(solution)/shard_map/ppermute | solution.py:338
  66.6 5.6 %collective-permute-start.17 = (bf16[2,192,256]{2,1,0:T(8,128)(2,1)S(1)}, bf16[2,192,256]{2,1,0:T(8,128)(2,1)S(1)}, u32[]{:S(2)}, u32[]{:S(2)}) collective-permute-start(bf16[2,192,256]{2,1,0:T(8,128)(2,1)S(1)} %get-tuple-element.80), channel_id=1, source_target_pairs={{0,1},{1,0},{2,3},{3,2},{4,5},{5,4},{6,7},{7,6},{8,9},{9,8},{10,11... | collective-permute-start | bytes 589832 | tf_op jit(solution)/shard_map/ppermute | solution.py:338
  66.8 19.4 %collective-permute-start.14 = (bf16[192,256]{1,0:T(8,128)(2,1)S(1)}, bf16[192,256]{1,0:T(8,128)(2,1)S(1)}, u32[]{:S(2)}, u32[]{:S(2)}) collective-permute-start(bf16[192,256]{1,0:T(8,128)(2,1)S(1)} %get-tuple-element.95), channel_id=1, source_target_pairs={{0,2},{1,3},{2,0},{3,1},{4,6},{5,7},{6,4},{7,5},{8,10},{9,11},{10,... | collective-permute-start | bytes 294920 | tf_op jit(solution)/shard_map/ppermute | solution.py:338
  70.0 6.2 %collective-permute-start.23 = (bf16[2,192,256]{2,1,0:T(8,128)(2,1)S(1)}, bf16[2,192,256]{2,1,0:T(8,128)(2,1)S(1)}, u32[]{:S(2)}, u32[]{:S(2)}) collective-permute-start(bf16[2,192,256]{2,1,0:T(8,128)(2,1)S(1)} %get-tuple-element.85), channel_id=1, source_target_pairs={{0,1},{1,0},{2,3},{3,2},{4,5},{5,4},{6,7},{7,6},{8,9},{9,8},{10,11... | collective-permute-start | bytes 589832 | tf_op jit(solution)/shard_map/ppermute | solution.py:338
  71.6 15.4 %copy-start.11 = (bf16[256,192]{1,0:T(8,128)(2,1)S(1)}, bf16[256,192]{1,0:T(8,128)(2,1)}, u32[]{:S(2)}) copy-start(bf16[256,192]{1,0:T(8,128)(2,1)} %copy-done.10) | copy-start | bytes 294916
  71.6 15.4 %copy-start.13 = (bf16[256,192]{1,0:T(8,128)(2,1)S(1)}, bf16[256,192]{1,0:T(8,128)(2,1)}, u32[]{:S(2)}) copy-start(bf16[256,192]{1,0:T(8,128)(2,1)} %copy-done.12) | copy-start | bytes 294916
  71.7 6.1 %collective-permute-start.28 = (bf16[2,192,256]{2,1,0:T(8,128)(2,1)S(1)}, bf16[2,192,256]{2,1,0:T(8,128)(2,1)S(1)}, u32[]{:S(2)}, u32[]{:S(2)}) collective-permute-start(bf16[2,192,256]{2,1,0:T(8,128)(2,1)S(1)} %get-tuple-element.90), channel_id=1, source_target_pairs={{0,1},{1,0},{2,3},{3,2},{4,5},{5,4},{6,7},{7,6},{8,9},{9,8},{10,11... | collective-permute-start | bytes 589832 | tf_op jit(solution)/shard_map/ppermute | solution.py:338
  72.2 15.1 %copy-start.7 = (bf16[256,192]{1,0:T(8,128)(2,1)S(1)}, bf16[256,192]{1,0:T(8,128)(2,1)}, u32[]{:S(2)}) copy-start(bf16[256,192]{1,0:T(8,128)(2,1)} %copy-done.6) | copy-start | bytes 294916
  72.2 15.1 %copy-start.9 = (bf16[256,192]{1,0:T(8,128)(2,1)S(1)}, bf16[256,192]{1,0:T(8,128)(2,1)}, u32[]{:S(2)}) copy-start(bf16[256,192]{1,0:T(8,128)(2,1)} %copy-done.8) | copy-start | bytes 294916
  72.3 15.1 %collective-permute-start.18 = (bf16[192,256]{1,0:T(8,128)(2,1)S(1)}, bf16[192,256]{1,0:T(8,128)(2,1)S(1)}, u32[]{:S(2)}, u32[]{:S(2)}) collective-permute-start(bf16[192,256]{1,0:T(8,128)(2,1)S(1)} %get-tuple-element.94), channel_id=1, source_target_pairs={{0,12},{1,13},{2,14},{3,15},{4,8},{5,9},{6,10},{7,11},{8,4},{9,5},... | collective-permute-start | bytes 294920 | tf_op jit(solution)/shard_map/ppermute | solution.py:338
  75.4 11.9 %collective-permute-start.19 = (bf16[192,256]{1,0:T(8,128)(2,1)S(1)}, bf16[192,256]{1,0:T(8,128)(2,1)S(1)}, u32[]{:S(2)}, u32[]{:S(2)}) collective-permute-start(bf16[192,256]{1,0:T(8,128)(2,1)S(1)} %get-tuple-element.93), channel_id=1, source_target_pairs={{0,14},{1,15},{2,12},{3,13},{4,10},{5,11},{6,8},{7,9},{8,6},{9,7},... | collective-permute-start | bytes 294920 | tf_op jit(solution)/shard_map/ppermute | solution.py:338
  76.2 13.3 %copy-start.15 = (bf16[256,192]{1,0:T(8,128)(2,1)S(1)}, bf16[256,192]{1,0:T(8,128)(2,1)}, u32[]{:S(2)}) copy-start(bf16[256,192]{1,0:T(8,128)(2,1)} %copy-done.14) | copy-start | bytes 294916
  76.2 13.3 %copy-start.17 = (bf16[256,192]{1,0:T(8,128)(2,1)S(1)}, bf16[256,192]{1,0:T(8,128)(2,1)}, u32[]{:S(2)}) copy-start(bf16[256,192]{1,0:T(8,128)(2,1)} %copy-done.16) | copy-start | bytes 294916
  76.2 6.8 %collective-permute-start.24 = (bf16[192,256]{1,0:T(8,128)(2,1)S(1)}, bf16[192,256]{1,0:T(8,128)(2,1)S(1)}, u32[]{:S(2)}, u32[]{:S(2)}) collective-permute-start(bf16[192,256]{1,0:T(8,128)(2,1)S(1)} %fusion.2), channel_id=1, source_target_pairs={{0,2},{1,3},{2,0},{3,1},{4,6},{5,7},{6,4},{7,5},{8,10},{9,11},{10,... | collective-permute-start | bytes 294920 | tf_op jit(solution)/shard_map/ppermute | solution.py:338
  83.0 6.5 %collective-permute-start.25 = (bf16[192,256]{1,0:T(8,128)(2,1)S(1)}, bf16[192,256]{1,0:T(8,128)(2,1)S(1)}, u32[]{:S(2)}, u32[]{:S(2)}) collective-permute-start(bf16[192,256]{1,0:T(8,128)(2,1)S(1)} %fusion.1), channel_id=1, source_target_pairs={{0,8},{1,9},{2,10},{3,11},{4,12},{5,13},{6,14},{7,15},{8,0},{9,1},... | collective-permute-start | bytes 294920 | tf_op jit(solution)/shard_map/ppermute | solution.py:338
  83.1 7.4 %collective-permute-start.29 = (bf16[192,256]{1,0:T(8,128)(2,1)S(1)}, bf16[192,256]{1,0:T(8,128)(2,1)S(1)}, u32[]{:S(2)}, u32[]{:S(2)}) collective-permute-start(bf16[192,256]{1,0:T(8,128)(2,1)S(1)} %get-tuple-element.92), channel_id=1, source_target_pairs={{0,4},{1,5},{2,6},{3,7},{4,0},{5,1},{6,2},{7,3},{8,12},{9,13},{10,... | collective-permute-start | bytes 294920 | tf_op jit(solution)/shard_map/ppermute | solution.py:338
  86.2 6.3 %collective-permute-start.30 = (bf16[192,256]{1,0:T(8,128)(2,1)S(1)}, bf16[192,256]{1,0:T(8,128)(2,1)S(1)}, u32[]{:S(2)}, u32[]{:S(2)}) collective-permute-start(bf16[192,256]{1,0:T(8,128)(2,1)S(1)} %get-tuple-element.91), channel_id=1, source_target_pairs={{0,6},{1,7},{2,4},{3,5},{4,2},{5,3},{6,0},{7,1},{8,14},{9,15},{10,... | collective-permute-start | bytes 294920 | tf_op jit(solution)/shard_map/ppermute | solution.py:338

commit v4 on v3

--- a/solution.py
+++ b/solution.py
@@ -114,19 +114,42 @@
     )(queries, source)
 
 
-def route_kernel(experts, parts, ids, choice, choice_t, *outs):
+def pick_kernel(ids, owner, *refs):
+    backs, out = refs[:-1], refs[-1]
+    for k, back in enumerate(backs):
+
+        @pl.when(owner[0] == ids[0] ^ k)
+        def _():
+            out[...] = back[...]
+
+
+def pick(ids, owner, backs):
+    return pl.pallas_call(
+        pick_kernel,
+        in_specs=[SCALARS] * 2 + [WHOLE] * len(backs),
+        out_specs=WHOLE,
+        out_shape=jax.ShapeDtypeStruct(backs[0].shape, BF16),
+        compiler_params=PARAMS,
+        cost_estimate=CHEAP,
+        name="pick",
+    )(ids, owner, *backs)
+
+
+def route_kernel(experts, parts, ids, choice_t, choice, *outs):
     dispatch, first, second = outs[:parts], outs[parts : 2 * parts], outs[2 * parts :]
-    tokens = choice.shape[0]
+    tokens = choice_t.shape[1]
     slots = dispatch[0].shape[0]
     capacity = slots * parts // experts
     wide = lax.broadcasted_iota(jnp.int32, (tokens, experts), 1)
     tall = lax.broadcasted_iota(jnp.int32, (experts, tokens), 0)
-    c0, c1 = choice[:, 0:1], choice[:, 1:2]
+    i = lax.broadcasted_iota(jnp.int32, (tokens, tokens), 0)
+    j = lax.broadcasted_iota(jnp.int32, (tokens, tokens), 1)
     r0, r1 = choice_t[0:1, :], choice_t[1:2, :]
+    turned = dot((i == j).astype(BF16), choice_t[...].astype(F32).astype(BF16), ((1,), (1,))).astype(jnp.int32)
+    choice[...] = turned
+    c0, c1 = turned[:, 0:1], turned[:, 1:2]
     named = ((wide == c0) | (wide == c1)).astype(BF16)
     named_t = ((tall == r0) | (tall == r1)).astype(BF16)
-    i = lax.broadcasted_iota(jnp.int32, (tokens, tokens), 0)
-    j = lax.broadcasted_iota(jnp.int32, (tokens, tokens), 1)
     rank = dot((j < i).astype(BF16), named).astype(jnp.int32)
     rank_t = dot(named_t, (i < j).astype(BF16)).astype(jnp.int32)
     place0 = c0 * capacity + jnp.sum(jnp.where(wide == c0, rank, 0), axis=1, keepdims=True)
@@ -147,15 +170,16 @@
     slots = experts * capacity // parts
     outs = pl.pallas_call(
         functools.partial(route_kernel, experts, parts),
-        in_specs=[SCALARS, WHOLE, WHOLE],
-        out_specs=[WHOLE] * (3 * parts),
-        out_shape=[jax.ShapeDtypeStruct((slots, tokens), BF16)] * parts
+        in_specs=[SCALARS, WHOLE],
+        out_specs=[WHOLE] * (1 + 3 * parts),
+        out_shape=[jax.ShapeDtypeStruct(choice.shape, jnp.int32)]
+        + [jax.ShapeDtypeStruct((slots, tokens), BF16)] * parts
         + [jax.ShapeDtypeStruct((tokens, slots), BF16)] * (2 * parts),
         compiler_params=PARAMS,
         cost_estimate=CHEAP,
         name="route",
-    )(ids, choice, choice.T)
-    return outs[:parts], outs[parts : 2 * parts], outs[2 * parts :]
+    )(ids, choice.T)
+    return outs[0], outs[1 : 1 + parts], outs[1 + parts : 1 + 2 * parts], outs[1 + 2 * parts :]
 
 
 def state_kernel(count, *refs):
@@ -206,7 +230,7 @@
     core = ids[1] & 1
     own_a[...] = dot(dispatch[...], state[:, pl.ds(pl.multiple_of(core * half, half), half)]).astype(BF16)
     own_b[...] = dot(dispatch[...], state[:, pl.ds(pl.multiple_of((1 - core) * half, half), half)]).astype(BF16)
-    logits = dot(state[...], router[...])
+    logits = dot(state[...], router[...], ((1,), (1,)))
     wide = lax.broadcasted_iota(jnp.int32, logits.shape, 1)
     first = jnp.sum(jnp.where(wide == choice[:, 0:1], logits, 0.0), axis=1, keepdims=True)
     second = jnp.sum(jnp.where(wide == choice[:, 1:2], logits, 0.0), axis=1, keepdims=True)
@@ -346,12 +370,11 @@
 
     steps = range(groups) if direct else [0]
 
-    queries, source = ask(tokens, query_weight, encoder_states[0])
-    owner = source_owner[0]
+    queries, source = ask(after(tokens, ids), query_weight, encoder_states[0])
     expert_bits = bits_of(groups)
     bits = bits_of(slices)
     if direct:
-        own = context = attend(queries, source, token_count)
+        own = attend(queries, source, token_count)
         asked, steps_of = [queries], [0]
         for bit in expert_bits:
             asked = asked + [hop(value if k == 0 else after(value, own), bit, 0) for k, value in zip(steps_of, asked)]
@@ -362,20 +385,19 @@
             answer = attend(after(asked[k], previous), source, token_count)
             backs[k] = hop(answer, k, 0)
             previous = answer
-        for k in range(1, groups):
-            context = jnp.where(owner == here ^ k, backs[k], context)
+        context = pick(ids, source_owner, [own] + [backs[k] for k in range(1, groups)])
     else:
         asked = lax.all_gather(queries, "expert", axis=0, tiled=True)
         previous = attend(asked, source, token_count)
-        context = lax.dynamic_slice_in_dim(spread(previous), owner * token_count, token_count, 0)
-
+        context = lax.dynamic_slice_in_dim(spread(previous), source_owner[0] * token_count, token_count, 0)
+
+    choice, dispatch, first, second = route(ids, after(expert_choice, context), experts, len(steps), capacity)
     weights, order = [output_weight], [0]
     for bit in bits:
         if bit == 1:
-            weights = [after(weight, previous) for weight in weights]
+            weights = [after(weight, dispatch[0]) for weight in weights]
         weights = weights + [hop(weight, 0, bit) for weight in weights]
         order = order + [index ^ bit for index in order]
-    dispatch, first, second = route(ids, after(expert_choice, context), experts, len(steps), capacity)
     contexts = [context]
     for bit in bits:
         contexts = contexts + [hop(value if i == 0 else after(value, dispatch[0]), 0, bit) for i, value in enumerate(contexts)]
@@ -392,12 +414,12 @@
         else:
             waited = leaving[k] = leave(ids, dispatch[k], after(state, waited), cuts[k])
     own_a, own_b, gates, columns = at_home(
-        ids, after(state, waited), dispatch[0], router_weight, expert_choice, experts, width
+        ids, after(state, waited), dispatch[0], router_weight.T, choice, experts, width
     )
 
     results = columns
     arrived = {k: hop(leaving[k], k, 0) for k in sends} if direct else {0: spread(leaving[0])}
-    turns = far if direct else [0]
+    turns = [k for k in far if k != relayed] + [k for k in far if k == relayed] if direct else [0]
     inputs = {}
     if relayed >= 0:
         pieces, places = [arrived[relayed]], [0]
@@ -418,25 +440,25 @@
         parts = [summed[j].astype(BF16) for j in range(pairs)]
         return [hop(part, k, 2 * j) if direct else hop(spread(part), 0, 2 * j) for j, part in enumerate(parts)]
 
-    home = {}
-    turn_ids = ids
+    def gather(k, results, parts, dtype):
+        return combine(gates, results, first[k], second[k], parts, dtype)
+
+    turn_ids, home = ids, {}
     if direct:
         keep, give = run_expert(ids, [0, 1], [own_a, own_b], expand_weight[0], shrink_weight[0], pairs)
-        turn_ids = after(ids, give)
-        home[0] = send_home(0, sum_cores(keep, after(give, arrived[sends[0]])))
+        parts = send_home(0, sum_cores(keep, after(give, arrived[sends[0]])))
+        results = gather(0, results, parts, F32)
+        turn_ids = after(ids, results)
     for k in turns:
         if k in inputs:
             pieces, places = inputs[k]
         else:
             pieces, places = [arrived[k], hop(arrived[k], 0, 1)], [0, 1]
         keep, give = run_expert(turn_ids, places, pieces, expand_weight[0], shrink_weight[0], pairs)
-        summed = sum_cores(keep, give)
-        home[k] = send_home(k, summed)
         turn_ids = after(ids, give)
-    arrivals = ([0] if direct else []) + turns
-    for k in arrivals:
-        kind = BF16 if k == arrivals[-1] else F32
-        results = combine(gates, results, first[k], second[k], home[k], kind)
+        home[k] = send_home(k, sum_cores(keep, give))
+    for k in turns:
+        results = gather(k, results, home[k], BF16 if k == turns[-1] else F32)
     return results
 
 

time: 94.2 us -> 90 us (0.955)
  local copies, waits for them, and re-layouts: 15.6 us -> 0.1 us
  waiting for transfers between devices: 21.6 us -> 35.8 us
  starting transfers between devices: 36.2 us -> 33.9 us
    unnamed x62 -> x12, local copies, waits for them, and re-layouts: 15.4 us -> 0.04 us
    ppermute x31, waiting for transfers between devices: 21.6 us -> 35.8 us  [hop(): return lax.ppermute(value, ('expert', 'mp'), moves)]
    ppermute x31, starting transfers between devices: 36.2 us -> 33.9 us  [hop(): return lax.ppermute(value, ('expert', 'mp'), moves)]
  transfers between devices with their start and end apart: 31 -> 31, of which waited for: 10 -> 11; matrix products, arithmetic and copies ran while one was open for 1% -> 0% of each run, Pallas kernels for 17% -> 17%
where the time goes in v4:
time: 90 us; the launch traced here: 89.8 us
  waiting for transfers between devices  35.8 us (40%)
  starting transfers between devices  33.9 us (38%)
  Pallas kernels  18.7 us (21%)
  between operations  1.04 us (1%)
    ppermute x31, waiting for transfers between devices, hop(): return lax.ppermute(value, ('expert', 'mp'), moves)  35.8 us
    ppermute x31, starting transfers between devices, hop(): return lax.ppermute(value, ('expert', 'mp'), moves)  33.9 us
    pallas_call x4, Pallas kernels, run_expert(): pl.pallas_call(functools.partial(expert_kernel, tuple(order)), in_specs=[...  6.16 us
    pallas_call x4, Pallas kernels, attend(): pl.pallas_call(attend_kernel, in_specs=[WHOLE] * 2, out_specs=WHOLE, out_...  3.09 us
    pallas_call x1, Pallas kernels, ask(): pl.pallas_call(query_kernel, in_specs=[pl.BlockSpec(memory_space=pltpu.HB...  1.81 us
  transfers between devices with their start and end apart: 31, of which 11 were waited for; matrix products, arithmetic and copies ran while one was open for 0% of the time, Pallas kernels for 17%

profile of v4, /device:TPU:0, one launch (start us, length us, event | category | flops | bytes accessed | tf_op | source)
XLA Modules:
  0.0 89.8 jit_solution(9412454410183992562)
XLA Ops:
  0.0 2.9 %collective-permute-start.9 = (bf16[256,1024]{1,0:T(8,128)(2,1)}, bf16[256,1024]{1,0:T(8,128)(2,1)S(1)}, u32[]{:S(2)}, u32[]{:S(2)}) collective-permute-start(bf16[256,1024]{1,0:T(8,128)(2,1)} %refs_5_), channel_id=1, source_target_pairs={{0,2},{1,3},{2,0},{3,1},{4,6},{5,7},{6,4},{7,5},{8,10},{9,11},{10,... | collective-permute-start | bytes 1572872 | tf_op jit(solution)/shard_map/ppermute | solution.py:362
  2.9 0.1 pad_add_fusion.ids.refs_9_.refs_0_
  3.0 1.8 %query.1 = (bf16[256,256]{1,0:T(8,128)(2,1)S(1)}, bf16[2,512,256]{2,1,0:T(8,128)(2,1)S(1)}) custom-call(bf16[256,1024]{1,0:T(8,128)(2,1)} %refs_0_.1, bf16[1024,256]{1,0:T(8,128)(2,1)} %weight.1, bf16[2,512,256]{2,1,0:T(8,128)(2,1)} %bitcast.37), custom_call_target="tpu_custom_call" | custom-call | tf_op jit(solution)/shard_map/query/pallas_call | solution.py:60
  4.8 0.0 copy-start.5
  4.8 0.0 copy-start.3
  4.9 0.0 copy-start.2
  4.9 2.6 %collective-permute-start.2 = (bf16[256,256]{1,0:T(8,128)(2,1)S(1)}, bf16[256,256]{1,0:T(8,128)(2,1)S(1)}, u32[]{:S(2)}, u32[]{:S(2)}) collective-permute-start(bf16[256,256]{1,0:T(8,128)(2,1)S(1)} %get-tuple-element.51.queries), channel_id=1, source_target_pairs={{0,8},{1,9},{2,10},{3,11},{4,12},{5,13},{6,14},{7,15},{8,0},{9,1},... | collective-permute-start | bytes 393224 | tf_op jit(solution)/shard_map/ppermute | solution.py:362
  7.5 1.6 %collective-permute-start = (bf16[256,256]{1,0:T(8,128)(2,1)S(1)}, bf16[256,256]{1,0:T(8,128)(2,1)S(1)}, u32[]{:S(2)}, u32[]{:S(2)}) collective-permute-start(bf16[256,256]{1,0:T(8,128)(2,1)S(1)} %get-tuple-element.51.queries), channel_id=1, source_target_pairs={{0,4},{1,5},{2,6},{3,7},{4,0},{5,1},{6,2},{7,3},{8,12},{9,13},{10,... | collective-permute-start | bytes 393224 | tf_op jit(solution)/shard_map/ppermute | solution.py:362
  9.1 0.8 attend.4.refs_0_
  9.9 3.8 %collective-permute-done.2.queries = bf16[256,256]{1,0:T(8,128)(2,1)S(1)} collective-permute-done((bf16[256,256]{1,0:T(8,128)(2,1)S(1)}, bf16[256,256]{1,0:T(8,128)(2,1)S(1)}, u32[]{:S(2)}, u32[]{:S(2)}) %collective-permute-start.2) | collective-permute-done | bytes 131104 | tf_op jit(solution)/shard_map/ppermute | solution.py:362
  13.7 0.6 collective-permute-start.4
  14.3 0.8 attend.5
  15.1 1.5 %collective-permute-start.1 = (bf16[256,256]{1,0:T(8,128)(2,1)S(1)}, bf16[256,256]{1,0:T(8,128)(2,1)S(1)}, u32[]{:S(2)}, u32[]{:S(2)}) collective-permute-start(bf16[256,256]{1,0:T(8,128)(2,1)S(1)} %attend.5), channel_id=1, source_target_pairs={{0,4},{1,5},{2,6},{3,7},{4,0},{5,1},{6,2},{7,3},{8,12},{9,13},{10,... | collective-permute-start | bytes 393224 | tf_op jit(solution)/shard_map/ppermute | solution.py:362
  16.6 0.8 attend.6
  17.4 2.0 %collective-permute-start.3 = (bf16[256,256]{1,0:T(8,128)(2,1)S(1)}, bf16[256,256]{1,0:T(8,128)(2,1)S(1)}, u32[]{:S(2)}, u32[]{:S(2)}) collective-permute-start(bf16[256,256]{1,0:T(8,128)(2,1)S(1)} %attend.6), channel_id=1, source_target_pairs={{0,8},{1,9},{2,10},{3,11},{4,12},{5,13},{6,14},{7,15},{8,0},{9,1},... | collective-permute-start | bytes 393224 | tf_op jit(solution)/shard_map/ppermute | solution.py:362
  19.4 0.5 collective-permute-done.4.queries
  19.9 0.8 attend.7
  20.7 3.6 %collective-permute-start.5 = (bf16[256,256]{1,0:T(8,128)(2,1)S(1)}, bf16[256,256]{1,0:T(8,128)(2,1)S(1)}, u32[]{:S(2)}, u32[]{:S(2)}) collective-permute-start(bf16[256,256]{1,0:T(8,128)(2,1)S(1)} %attend.7), channel_id=1, source_target_pairs={{0,12},{1,13},{2,14},{3,15},{4,8},{5,9},{6,10},{7,11},{8,4},{9,5},... | collective-permute-start | bytes 393224 | tf_op jit(solution)/shard_map/ppermute | solution.py:362
  25.0 4.3 %collective-permute-done.5.refs_3_ = bf16[256,256]{1,0:T(8,128)(2,1)S(1)} collective-permute-done((bf16[256,256]{1,0:T(8,128)(2,1)S(1)}, bf16[256,256]{1,0:T(8,128)(2,1)S(1)}, u32[]{:S(2)}, u32[]{:S(2)}) %collective-permute-start.5) | collective-permute-done | bytes 131104 | tf_op jit(solution)/shard_map/ppermute | solution.py:362
  29.3 0.6 pick.1.refs_1_
  29.9 1.5 %route.1 = (s32[256,2]{1,0:T(8,128)S(1)}, bf16[192,256]{1,0:T(8,128)(2,1)S(1)}, bf16[192,256]{1,0:T(8,128)(2,1)S(1)}, bf16[192,256]{1,0:T(8,128)(2,1)S(1)}, bf16...) custom-call(s32[2]{0:T(128)S(1)} %pad_add_fusion.ids.refs_9_.refs_0_, ...), custom_call_target="tpu_custom_call" | custom-call | tf_op jit(solution)/shard_map/route/pallas_call | solution.py:171
  31.4 0.1 collective-permute-start.10
  31.5 0.5 collective-permute-start.11
  32.0 0.5 collective-permute-start.6
  32.5 4.9 %collective-permute-done.6.refs_2_ = bf16[256,256]{1,0:T(8,128)(2,1)S(1)} collective-permute-done((bf16[256,256]{1,0:T(8,128)(2,1)S(1)}, bf16[256,256]{1,0:T(8,128)(2,1)S(1)}, u32[]{:S(2)}, u32[]{:S(2)}) %collective-permute-start.6) | collective-permute-done | bytes 131104 | tf_op jit(solution)/shard_map/ppermute | solution.py:362
  37.5 1.3 %collective-permute-done.8.refs_4_ = bf16[256,256]{1,0:T(8,128)(2,1)S(1)} collective-permute-done((bf16[256,256]{1,0:T(8,128)(2,1)S(1)}, bf16[256,256]{1,0:T(8,128)(2,1)S(1)}, u32[]{:S(2)}, u32[]{:S(2)}) %collective-permute-start.8) | collective-permute-done | bytes 131104 | tf_op jit(solution)/shard_map/ppermute | solution.py:362
  38.9 0.0 copy-start.1
  38.9 1.4 %state.1 = (bf16[256,1024]{1,0:T(8,128)(2,1)S(1)}, bf16[192,256]{1,0:T(8,128)(2,1)S(1)}) custom-call(bf16[256,1024]{1,0:T(8,128)(2,1)S(1)} %copy-done.2, bf16[256,256]{1,0:T(8,128)(2,1)S(1)} %pick.1.refs_1_, bf16[256,256]{1,0:T(8,128)(2,1)S(1)} %collective-permute-done.6.refs_2_, bf16[256,256]{1,0:T(8,128)(2,1)S(1)} %collective-permute-done.7.refs_3_, ...), custom_call_target="tpu_custom_call" | custom-call | tf_op jit(solution)/shard_map/state/pallas_call | solution.py:202
  40.3 4.8 %collective-permute-start.12 = (bf16[192,256]{1,0:T(8,128)(2,1)S(1)}, bf16[192,256]{1,0:T(8,128)(2,1)S(1)}, u32[]{:S(2)}, u32[]{:S(2)}) collective-permute-start(bf16[192,256]{1,0:T(8,128)(2,1)S(1)} %get-tuple-element.78), channel_id=1, source_target_pairs={{0,8},{1,9},{2,10},{3,11},{4,12},{5,13},{6,14},{7,15},{8,0},{9,1},... | collective-permute-start | bytes 294920 | tf_op jit(solution)/shard_map/ppermute | solution.py:362
  45.1 0.8 leave.2
  45.8 0.7 leave.3
  46.6 0.1 collective-permute-start.20
  46.7 1.5 %collective-permute-start.15 = (bf16[192,512]{1,0:T(8,128)(2,1)S(1)}, bf16[192,512]{1,0:T(8,128)(2,1)S(1)}, u32[]{:S(2)}, u32[]{:S(2)}) collective-permute-start(bf16[192,512]{1,0:T(8,128)(2,1)S(1)} %leave.2), channel_id=1, source_target_pairs={{0,12},{1,13},{2,14},{3,15},{4,8},{5,9},{6,10},{7,11},{8,4},{9,5},... | collective-permute-start | bytes 589832 | tf_op jit(solution)/shard_map/ppermute | solution.py:362
  48.1 1.0 %home.1 = (bf16[192,512]{1,0:T(8,128)(2,1)S(1)}, bf16[192,512]{1,0:T(8,128)(2,1)S(1)}, f32[256,2]{1,0:T(8,128)S(1)}, f32[256,256]{1,0:T(8,128)S(1)}) custom-call(s32[2]{0:T(128)S(1)} %pad_add_fusion.ids.refs_9_.refs_0_, bf16[256,1024]{1,0:T(8,128)(2,1)S(1)} %get-tuple-element.68.state, bf16[192,256]{1,0:T(8,128)(2,1)S(1)} %get-tuple-element.58.dispatch, ...), custom_call_target="tpu_custom_call" | custom-call | tf_op jit(solution)/shard_map/home/pallas_call | solution.py:246
  49.2 1.5 %expert.4 = (f32[2,192,256]{2,1,0:T(8,128)S(1)}, bf16[2,192,256]{2,1,0:T(8,128)(2,1)S(1)}) custom-call(s32[2]{0:T(128)S(1)} %pad_add_fusion.ids.refs_9_.refs_0_, bf16[192,512]{1,0:T(8,128)(2,1)S(1)} %get-tuple-element.74.refs_1_, bf16[192,512]{1,0:T(8,128)(2,1)S(1)} %get-tuple-element.75.refs_2_, bf16[1024,1024]{1,0:T(8,128)(2,1)S(1)} %bitcast.27, ...), custom_call_target="tpu_custom_call" | custom-call | tf_op jit(solution)/shard_map/expert/pallas_call | solution.py:288
  50.7 0.1 collective-permute-start.13
  50.8 0.6 collective-permute-start.25
  51.4 7.3 %collective-permute-done.20.refs_1_ = bf16[192,512]{1,0:T(8,128)(2,1)S(1)} collective-permute-done((bf16[192,512]{1,0:T(8,128)(2,1)S(1)}, bf16[192,512]{1,0:T(8,128)(2,1)S(1)}, u32[]{:S(2)}, u32[]{:S(2)}) %collective-permute-start.20) | collective-permute-done | bytes 196640 | tf_op jit(solution)/shard_map/ppermute | solution.py:362
  58.7 0.0 collective-permute-start.21
  58.7 0.5 collective-permute-start.16
  59.3 0.6 collective-permute-start.14
  59.9 0.5 collective-permute-start.27
  60.4 3.6 %collective-permute-done.14.refs_1_ = bf16[192,256]{1,0:T(8,128)(2,1)S(1)} collective-permute-done((bf16[192,256]{1,0:T(8,128)(2,1)S(1)}, bf16[192,256]{1,0:T(8,128)(2,1)S(1)}, u32[]{:S(2)}, u32[]{:S(2)}) %collective-permute-start.14) | collective-permute-done | bytes 98336 | tf_op jit(solution)/shard_map/ppermute | solution.py:362
  64.1 0.2 combine.4.base
  64.3 1.5 %expert.5 = (f32[2,192,256]{2,1,0:T(8,128)S(1)}, bf16[2,192,256]{2,1,0:T(8,128)(2,1)S(1)}) custom-call(s32[2]{0:T(128)S(1)} %pad_add_fusion.ids.refs_9_.refs_0_, bf16[192,512]{1,0:T(8,128)(2,1)S(1)} %collective-permute-done.15.refs_1_, bf16[192,512]{1,0:T(8,128)(2,1)S(1)} %collective-permute-done.16.refs_2_, bf16[1024,1024]{1,0:T(8,128)(2,1)S(1)} %bitcast.28, ...), custom_call_target="tpu_custom_call" | custom-call | tf_op jit(solution)/shard_map/expert/pallas_call | solution.py:288
  65.9 1.5 %expert.6 = (f32[2,192,256]{2,1,0:T(8,128)S(1)}, bf16[2,192,256]{2,1,0:T(8,128)(2,1)S(1)}) custom-call(s32[2]{0:T(128)S(1)} %pad_add_fusion.ids.refs_9_.refs_0_, bf16[192,512]{1,0:T(8,128)(2,1)S(1)} %collective-permute-done.20.refs_1_, bf16[192,512]{1,0:T(8,128)(2,1)S(1)} %collective-permute-done.21.refs_2_, bf16[1024,1024]{1,0:T(8,128)(2,1)S(1)} %bitcast.29, ...), custom_call_target="tpu_custom_call" | custom-call | tf_op jit(solution)/shard_map/expert/pallas_call | solution.py:288
  67.4 1.5 %expert.7 = (f32[2,192,256]{2,1,0:T(8,128)S(1)}, bf16[2,192,256]{2,1,0:T(8,128)(2,1)S(1)}) custom-call(s32[2]{0:T(128)S(1)} %pad_add_fusion.ids.refs_9_.refs_0_, bf16[192,256]{1,0:T(8,128)(2,1)S(1)} %collective-permute-done.12.refs_1_, bf16[192,256]{1,0:T(8,128)(2,1)S(1)} %collective-permute-done.25.refs_2_, ...), custom_call_target="tpu_custom_call" | custom-call | tf_op jit(solution)/shard_map/expert/pallas_call | solution.py:288
  69.0 0.1 collective-permute-start.28
  69.1 0.5 collective-permute-start.22
  69.6 0.1 collective-permute-start.17
  69.7 0.9 collective-permute-done.28
  70.6 0.6 collective-permute-start.29
  71.2 0.1 add_convert_fusion
  71.3 1.5 %collective-permute-start.24 = (bf16[192,256]{1,0:T(8,128)(2,1)S(1)}, bf16[192,256]{1,0:T(8,128)(2,1)S(1)}, u32[]{:S(2)}, u32[]{:S(2)}) collective-permute-start(bf16[192,256]{1,0:T(8,128)(2,1)S(1)} %get-tuple-element.95), channel_id=1, source_target_pairs={{0,6},{1,7},{2,4},{3,5},{4,2},{5,3},{6,0},{7,1},{8,14},{9,15},{10,... | collective-permute-start | bytes 294920 | tf_op jit(solution)/shard_map/ppermute | solution.py:362
  72.8 1.5 %collective-permute-start.23 = (bf16[192,256]{1,0:T(8,128)(2,1)S(1)}, bf16[192,256]{1,0:T(8,128)(2,1)S(1)}, u32[]{:S(2)}, u32[]{:S(2)}) collective-permute-start(bf16[192,256]{1,0:T(8,128)(2,1)S(1)} %get-tuple-element.96), channel_id=1, source_target_pairs={{0,4},{1,5},{2,6},{3,7},{4,0},{5,1},{6,2},{7,3},{8,12},{9,13},{10,... | collective-permute-start | bytes 294920 | tf_op jit(solution)/shard_map/ppermute | solution.py:362
  74.3 1.6 %collective-permute-start.19 = (bf16[192,256]{1,0:T(8,128)(2,1)S(1)}, bf16[192,256]{1,0:T(8,128)(2,1)S(1)}, u32[]{:S(2)}, u32[]{:S(2)}) collective-permute-start(bf16[192,256]{1,0:T(8,128)(2,1)S(1)} %get-tuple-element.97), channel_id=1, source_target_pairs={{0,14},{1,15},{2,12},{3,13},{4,10},{5,11},{6,8},{7,9},{8,6},{9,7},... | collective-permute-start | bytes 294920 | tf_op jit(solution)/shard_map/ppermute | solution.py:362
  76.0 2.3 %collective-permute-start.18 = (bf16[192,256]{1,0:T(8,128)(2,1)S(1)}, bf16[192,256]{1,0:T(8,128)(2,1)S(1)}, u32[]{:S(2)}, u32[]{:S(2)}) collective-permute-start(bf16[192,256]{1,0:T(8,128)(2,1)S(1)} %get-tuple-element.98), channel_id=1, source_target_pairs={{0,12},{1,13},{2,14},{3,15},{4,8},{5,9},{6,10},{7,11},{8,4},{9,5},... | collective-permute-start | bytes 294920 | tf_op jit(solution)/shard_map/ppermute | solution.py:362
  78.3 1.2 %collective-permute-start.30 = (bf16[192,256]{1,0:T(8,128)(2,1)S(1)}, bf16[192,256]{1,0:T(8,128)(2,1)S(1)}, u32[]{:S(2)}, u32[]{:S(2)}) collective-permute-start(bf16[192,256]{1,0:T(8,128)(2,1)S(1)} %fusion.1), channel_id=1, source_target_pairs={{0,8},{1,9},{2,10},{3,11},{4,12},{5,13},{6,14},{7,15},{8,0},{9,1},... | collective-permute-start | bytes 294920 | tf_op jit(solution)/shard_map/ppermute | solution.py:362
  79.4 3.3 %collective-permute-done.19.refs_1_ = bf16[192,256]{1,0:T(8,128)(2,1)S(1)} collective-permute-done((bf16[192,256]{1,0:T(8,128)(2,1)S(1)}, bf16[192,256]{1,0:T(8,128)(2,1)S(1)}, u32[]{:S(2)}, u32[]{:S(2)}) %collective-permute-start.19) | collective-permute-done | bytes 98336 | tf_op jit(solution)/shard_map/ppermute | solution.py:362
  82.7 1.7 %collective-permute-done.18.refs_0_ = bf16[192,256]{1,0:T(8,128)(2,1)S(1)} collective-permute-done((bf16[192,256]{1,0:T(8,128)(2,1)S(1)}, bf16[192,256]{1,0:T(8,128)(2,1)S(1)}, u32[]{:S(2)}, u32[]{:S(2)}) %collective-permute-start.18) | collective-permute-done | bytes 98336 | tf_op jit(solution)/shard_map/ppermute | solution.py:362
  84.4 0.2 combine.5.base
  84.6 0.2 combine.6.base
  84.9 4.1 %collective-permute-done.30.refs_0_ = bf16[192,256]{1,0:T(8,128)(2,1)S(1)} collective-permute-done((bf16[192,256]{1,0:T(8,128)(2,1)S(1)}, bf16[192,256]{1,0:T(8,128)(2,1)S(1)}, u32[]{:S(2)}, u32[]{:S(2)}) %collective-permute-start.30) | collective-permute-done | bytes 98336 | tf_op jit(solution)/shard_map/ppermute | solution.py:362
  89.0 0.9 combine.7
  (39 shorter events, 0.3 us)
Async XLA Ops:
  0.0 31.5 %collective-permute-start.9 = (bf16[256,1024]{1,0:T(8,128)(2,1)}, bf16[256,1024]{1,0:T(8,128)(2,1)S(1)}, u32[]{:S(2)}, u32[]{:S(2)}) collective-permute-start(bf16[256,1024]{1,0:T(8,128)(2,1)} %refs_5_), channel_id=1, source_target_pairs={{0,2},{1,3},{2,0},{3,1},{4,6},{5,7},{6,4},{7,5},{8,10},{9,11},{10,... | collective-permute-start | bytes 1572872 | tf_op jit(solution)/shard_map/ppermute | solution.py:362
  4.8 25.1 %copy-start.5 = (s32[256,2]{0,1:T(2,128)S(1)}, s32[256,2]{0,1:T(2,128)}, u32[]{:S(2)}) copy-start(s32[256,2]{0,1:T(2,128)} %param.15) | copy-start | bytes 6148
  4.8 26.6 %copy-start.3 = (bf16[256,1024]{1,0:T(8,128)(2,1)S(1)}, bf16[256,1024]{1,0:T(8,128)(2,1)}, u32[]{:S(2)}) copy-start(bf16[256,1024]{1,0:T(8,128)(2,1)} %refs_5_) | copy-start | bytes 1572868
  4.9 34.0 %copy-start.2 = (bf16[256,1024]{1,0:T(8,128)(2,1)S(1)}, bf16[256,1024]{1,0:T(8,128)(2,1)}, u32[]{:S(2)}) copy-start(bf16[256,1024]{1,0:T(8,128)(2,1)} %refs_0_.1) | copy-start | bytes 1572868
  4.9 8.8 %collective-permute-start.2 = (bf16[256,256]{1,0:T(8,128)(2,1)S(1)}, bf16[256,256]{1,0:T(8,128)(2,1)S(1)}, u32[]{:S(2)}, u32[]{:S(2)}) collective-permute-start(bf16[256,256]{1,0:T(8,128)(2,1)S(1)} %get-tuple-element.51.queries), channel_id=1, source_target_pairs={{0,8},{1,9},{2,10},{3,11},{4,12},{5,13},{6,14},{7,15},{8,0},{9,1},... | collective-permute-start | bytes 393224 | tf_op jit(solution)/shard_map/ppermute | solution.py:362
  7.5 6.8 %collective-permute-start = (bf16[256,256]{1,0:T(8,128)(2,1)S(1)}, bf16[256,256]{1,0:T(8,128)(2,1)S(1)}, u32[]{:S(2)}, u32[]{:S(2)}) collective-permute-start(bf16[256,256]{1,0:T(8,128)(2,1)S(1)} %get-tuple-element.51.queries), channel_id=1, source_target_pairs={{0,4},{1,5},{2,6},{3,7},{4,0},{5,1},{6,2},{7,3},{8,12},{9,13},{10,... | collective-permute-start | bytes 393224 | tf_op jit(solution)/shard_map/ppermute | solution.py:362
  13.7 6.2 %collective-permute-start.4 = (bf16[256,256]{1,0:T(8,128)(2,1)S(1)}, bf16[256,256]{1,0:T(8,128)(2,1)S(1)}, u32[]{:S(2)}, u32[]{:S(2)}) collective-permute-start(bf16[256,256]{1,0:T(8,128)(2,1)S(1)} %collective-permute-done.2.queries), channel_id=1, source_target_pairs={{0,4},{1,5},{2,6},{3,7},{4,0},{5,1},{6,2},{7,3},{8,12},{9,13},{10,... | collective-permute-start | bytes 393224 | tf_op jit(solution)/shard_map/ppermute | solution.py:362
  15.1 9.9 %collective-permute-start.1 = (bf16[256,256]{1,0:T(8,128)(2,1)S(1)}, bf16[256,256]{1,0:T(8,128)(2,1)S(1)}, u32[]{:S(2)}, u32[]{:S(2)}) collective-permute-start(bf16[256,256]{1,0:T(8,128)(2,1)S(1)} %attend.5), channel_id=1, source_target_pairs={{0,4},{1,5},{2,6},{3,7},{4,0},{5,1},{6,2},{7,3},{8,12},{9,13},{10,... | collective-permute-start | bytes 393224 | tf_op jit(solution)/shard_map/ppermute | solution.py:362
  17.4 7.6 %collective-permute-start.3 = (bf16[256,256]{1,0:T(8,128)(2,1)S(1)}, bf16[256,256]{1,0:T(8,128)(2,1)S(1)}, u32[]{:S(2)}, u32[]{:S(2)}) collective-permute-start(bf16[256,256]{1,0:T(8,128)(2,1)S(1)} %attend.6), channel_id=1, source_target_pairs={{0,8},{1,9},{2,10},{3,11},{4,12},{5,13},{6,14},{7,15},{8,0},{9,1},... | collective-permute-start | bytes 393224 | tf_op jit(solution)/shard_map/ppermute | solution.py:362
  20.7 8.6 %collective-permute-start.5 = (bf16[256,256]{1,0:T(8,128)(2,1)S(1)}, bf16[256,256]{1,0:T(8,128)(2,1)S(1)}, u32[]{:S(2)}, u32[]{:S(2)}) collective-permute-start(bf16[256,256]{1,0:T(8,128)(2,1)S(1)} %attend.7), channel_id=1, source_target_pairs={{0,12},{1,13},{2,14},{3,15},{4,8},{5,9},{6,10},{7,11},{8,4},{9,5},... | collective-permute-start | bytes 393224 | tf_op jit(solution)/shard_map/ppermute | solution.py:362
  31.4 7.4 %collective-permute-start.10 = (bf16[256,1024]{1,0:T(8,128)(2,1)S(1)}, bf16[256,1024]{1,0:T(8,128)(2,1)S(1)}, u32[]{:S(2)}, u32[]{:S(2)}) collective-permute-start(bf16[256,1024]{1,0:T(8,128)(2,1)S(1)} %copy-done.3), channel_id=1, source_target_pairs={{0,1},{1,0},{2,3},{3,2},{4,5},{5,4},{6,7},{7,6},{8,9},{9,8},{10,11... | collective-permute-start | bytes 1572872 | tf_op jit(solution)/shard_map/ppermute | solution.py:362
  31.5 7.3 %collective-permute-start.11 = (bf16[256,1024]{1,0:T(8,128)(2,1)S(1)}, bf16[256,1024]{1,0:T(8,128)(2,1)S(1)}, u32[]{:S(2)}, u32[]{:S(2)}) collective-permute-start(bf16[256,1024]{1,0:T(8,128)(2,1)S(1)} %collective-permute-done.9.refs_6_), channel_id=1, source_target_pairs={{0,1},{1,0},{2,3},{3,2},{4,5},{5,4},{6,7},{7,6},{8,9},{9,8},{10,11... | collective-permute-start | bytes 1572872 | tf_op jit(solution)/shard_map/ppermute | solution.py:362
  32.0 5.5 %collective-permute-start.6 = (bf16[256,256]{1,0:T(8,128)(2,1)S(1)}, bf16[256,256]{1,0:T(8,128)(2,1)S(1)}, u32[]{:S(2)}, u32[]{:S(2)}) collective-permute-start(bf16[256,256]{1,0:T(8,128)(2,1)S(1)} %pick.1.refs_1_), channel_id=1, source_target_pairs={{0,2},{1,3},{2,0},{3,1},{4,6},{5,7},{6,4},{7,5},{8,10},{9,11},{10,... | collective-permute-start | bytes 393224 | tf_op jit(solution)/shard_map/ppermute | solution.py:362
  32.5 5.0 %collective-permute-start.7 = (bf16[256,256]{1,0:T(8,128)(2,1)S(1)}, bf16[256,256]{1,0:T(8,128)(2,1)S(1)}, u32[]{:S(2)}, u32[]{:S(2)}) collective-permute-start(bf16[256,256]{1,0:T(8,128)(2,1)S(1)} %pick.1.refs_1_), channel_id=1, source_target_pairs={{0,1},{1,0},{2,3},{3,2},{4,5},{5,4},{6,7},{7,6},{8,9},{9,8},{10,11... | collective-permute-start | bytes 393224 | tf_op jit(solution)/shard_map/ppermute | solution.py:362
  37.5 1.3 %collective-permute-start.8 = (bf16[256,256]{1,0:T(8,128)(2,1)S(1)}, bf16[256,256]{1,0:T(8,128)(2,1)S(1)}, u32[]{:S(2)}, u32[]{:S(2)}) collective-permute-start(bf16[256,256]{1,0:T(8,128)(2,1)S(1)} %collective-permute-done.6.refs_2_), channel_id=1, source_target_pairs={{0,1},{1,0},{2,3},{3,2},{4,5},{5,4},{6,7},{7,6},{8,9},{9,8},{10,11... | collective-permute-start | bytes 393224 | tf_op jit(solution)/shard_map/ppermute | solution.py:362
  38.8 9.3 %copy-start.4 = (bf16[1024,4]{0,1:T(4,128)(2,1)S(1)}, bf16[1024,4]{0,1:T(4,128)(2,1)}, u32[]{:S(2)}) copy-start(bf16[1024,4]{0,1:T(4,128)(2,1)} %param.14) | copy-start | bytes 24580
  38.9 10.3 %copy-start = (bf16[1,1024,1024]{2,1,0:T(8,128)(2,1)S(1)}, bf16[1,1024,1024]{2,1,0:T(8,128)(2,1)}, u32[]{:S(2)}) copy-start(bf16[1,1024,1024]{2,1,0:T(8,128)(2,1)} %param.16) | copy-start | bytes 6291460
  38.9 10.3 %copy-start.1 = (bf16[1,1024,1024]{2,1,0:T(8,128)(2,1)S(1)}, bf16[1,1024,1024]{2,1,0:T(8,128)(2,1)}, u32[]{:S(2)}) copy-start(bf16[1,1024,1024]{2,1,0:T(8,128)(2,1)} %param.17) | copy-start | bytes 6291460
  40.3 10.4 %collective-permute-start.12 = (bf16[192,256]{1,0:T(8,128)(2,1)S(1)}, bf16[192,256]{1,0:T(8,128)(2,1)S(1)}, u32[]{:S(2)}, u32[]{:S(2)}) collective-permute-start(bf16[192,256]{1,0:T(8,128)(2,1)S(1)} %get-tuple-element.78), channel_id=1, source_target_pairs={{0,8},{1,9},{2,10},{3,11},{4,12},{5,13},{6,14},{7,15},{8,0},{9,1},... | collective-permute-start | bytes 294920 | tf_op jit(solution)/shard_map/ppermute | solution.py:362
  46.6 12.1 %collective-permute-start.20 = (bf16[192,512]{1,0:T(8,128)(2,1)S(1)}, bf16[192,512]{1,0:T(8,128)(2,1)S(1)}, u32[]{:S(2)}, u32[]{:S(2)}) collective-permute-start(bf16[192,512]{1,0:T(8,128)(2,1)S(1)} %leave.3), channel_id=1, source_target_pairs={{0,4},{1,5},{2,6},{3,7},{4,0},{5,1},{6,2},{7,3},{8,12},{9,13},{10,... | collective-permute-start | bytes 589832 | tf_op jit(solution)/shard_map/ppermute | solution.py:362
  46.7 12.1 %collective-permute-start.15 = (bf16[192,512]{1,0:T(8,128)(2,1)S(1)}, bf16[192,512]{1,0:T(8,128)(2,1)S(1)}, u32[]{:S(2)}, u32[]{:S(2)}) collective-permute-start(bf16[192,512]{1,0:T(8,128)(2,1)S(1)} %leave.2), channel_id=1, source_target_pairs={{0,12},{1,13},{2,14},{3,15},{4,8},{5,9},{6,10},{7,11},{8,4},{9,5},... | collective-permute-start | bytes 589832 | tf_op jit(solution)/shard_map/ppermute | solution.py:362
  50.7 8.5 %collective-permute-start.13 = (bf16[2,192,256]{2,1,0:T(8,128)(2,1)S(1)}, bf16[2,192,256]{2,1,0:T(8,128)(2,1)S(1)}, u32[]{:S(2)}, u32[]{:S(2)}) collective-permute-start(bf16[2,192,256]{2,1,0:T(8,128)(2,1)S(1)} %get-tuple-element.79), channel_id=1, source_target_pairs={{0,1},{1,0},{2,3},{3,2},{4,5},{5,4},{6,7},{7,6},{8,9},{9,8},{10,11... | collective-permute-start | bytes 589832 | tf_op jit(solution)/shard_map/ppermute | solution.py:362
  50.8 9.1 %collective-permute-start.25 = (bf16[192,256]{1,0:T(8,128)(2,1)S(1)}, bf16[192,256]{1,0:T(8,128)(2,1)S(1)}, u32[]{:S(2)}, u32[]{:S(2)}) collective-permute-start(bf16[192,256]{1,0:T(8,128)(2,1)S(1)} %collective-permute-done.12.refs_1_), channel_id=1, source_target_pairs={{0,2},{1,3},{2,0},{3,1},{4,6},{5,7},{6,4},{7,5},{8,10},{9,11},{10,... | collective-permute-start | bytes 294920 | tf_op jit(solution)/shard_map/ppermute | solution.py:362
  58.7 7.2 %collective-permute-start.21 = (bf16[192,512]{1,0:T(8,128)(2,1)S(1)}, bf16[192,512]{1,0:T(8,128)(2,1)S(1)}, u32[]{:S(2)}, u32[]{:S(2)}) collective-permute-start(bf16[192,512]{1,0:T(8,128)(2,1)S(1)} %collective-permute-done.20.refs_1_), channel_id=1, source_target_pairs={{0,1},{1,0},{2,3},{3,2},{4,5},{5,4},{6,7},{7,6},{8,9},{9,8},{10,11... | collective-permute-start | bytes 589832 | tf_op jit(solution)/shard_map/ppermute | solution.py:362
  58.7 5.6 %collective-permute-start.16 = (bf16[192,512]{1,0:T(8,128)(2,1)S(1)}, bf16[192,512]{1,0:T(8,128)(2,1)S(1)}, u32[]{:S(2)}, u32[]{:S(2)}) collective-permute-start(bf16[192,512]{1,0:T(8,128)(2,1)S(1)} %collective-permute-done.15.refs_1_), channel_id=1, source_target_pairs={{0,1},{1,0},{2,3},{3,2},{4,5},{5,4},{6,7},{7,6},{8,9},{9,8},{10,11... | collective-permute-start | bytes 589832 | tf_op jit(solution)/shard_map/ppermute | solution.py:362
  59.3 4.8 %collective-permute-start.14 = (bf16[192,256]{1,0:T(8,128)(2,1)S(1)}, bf16[192,256]{1,0:T(8,128)(2,1)S(1)}, u32[]{:S(2)}, u32[]{:S(2)}) collective-permute-start(bf16[192,256]{1,0:T(8,128)(2,1)S(1)} %get-tuple-element.99), channel_id=1, source_target_pairs={{0,2},{1,3},{2,0},{3,1},{4,6},{5,7},{6,4},{7,5},{8,10},{9,11},{10,... | collective-permute-start | bytes 294920 | tf_op jit(solution)/shard_map/ppermute | solution.py:362
  59.9 7.5 %collective-permute-start.26 = (bf16[192,256]{1,0:T(8,128)(2,1)S(1)}, bf16[192,256]{1,0:T(8,128)(2,1)S(1)}, u32[]{:S(2)}, u32[]{:S(2)}) collective-permute-start(bf16[192,256]{1,0:T(8,128)(2,1)S(1)} %collective-permute-done.12.refs_1_), channel_id=1, source_target_pairs={{0,1},{1,0},{2,3},{3,2},{4,5},{5,4},{6,7},{7,6},{8,9},{9,8},{10,11... | collective-permute-start | bytes 294920 | tf_op jit(solution)/shard_map/ppermute | solution.py:362
  59.9 7.5 %collective-permute-start.27 = (bf16[192,256]{1,0:T(8,128)(2,1)S(1)}, bf16[192,256]{1,0:T(8,128)(2,1)S(1)}, u32[]{:S(2)}, u32[]{:S(2)}) collective-permute-start(bf16[192,256]{1,0:T(8,128)(2,1)S(1)} %collective-permute-done.25.refs_2_), channel_id=1, source_target_pairs={{0,1},{1,0},{2,3},{3,2},{4,5},{5,4},{6,7},{7,6},{8,9},{9,8},{10,11... | collective-permute-start | bytes 294920 | tf_op jit(solution)/shard_map/ppermute | solution.py:362
  69.0 1.5 %collective-permute-start.28 = (bf16[2,192,256]{2,1,0:T(8,128)(2,1)S(1)}, bf16[2,192,256]{2,1,0:T(8,128)(2,1)S(1)}, u32[]{:S(2)}, u32[]{:S(2)}) collective-permute-start(bf16[2,192,256]{2,1,0:T(8,128)(2,1)S(1)} %get-tuple-element.94), channel_id=1, source_target_pairs={{0,1},{1,0},{2,3},{3,2},{4,5},{5,4},{6,7},{7,6},{8,9},{9,8},{10,11... | collective-permute-start | bytes 589832 | tf_op jit(solution)/shard_map/ppermute | solution.py:362
  69.1 2.1 %collective-permute-start.22 = (bf16[2,192,256]{2,1,0:T(8,128)(2,1)S(1)}, bf16[2,192,256]{2,1,0:T(8,128)(2,1)S(1)}, u32[]{:S(2)}, u32[]{:S(2)}) collective-permute-start(bf16[2,192,256]{2,1,0:T(8,128)(2,1)S(1)} %get-tuple-element.89), channel_id=1, source_target_pairs={{0,1},{1,0},{2,3},{3,2},{4,5},{5,4},{6,7},{7,6},{8,9},{9,8},{10,11... | collective-permute-start | bytes 589832 | tf_op jit(solution)/shard_map/ppermute | solution.py:362
  69.6 4.7 %collective-permute-start.17 = (bf16[2,192,256]{2,1,0:T(8,128)(2,1)S(1)}, bf16[2,192,256]{2,1,0:T(8,128)(2,1)S(1)}, u32[]{:S(2)}, u32[]{:S(2)}) collective-permute-start(bf16[2,192,256]{2,1,0:T(8,128)(2,1)S(1)} %get-tuple-element.84), channel_id=1, source_target_pairs={{0,1},{1,0},{2,3},{3,2},{4,5},{5,4},{6,7},{7,6},{8,9},{9,8},{10,11... | collective-permute-start | bytes 589832 | tf_op jit(solution)/shard_map/ppermute | solution.py:362
  70.6 7.7 %collective-permute-start.29 = (bf16[192,256]{1,0:T(8,128)(2,1)S(1)}, bf16[192,256]{1,0:T(8,128)(2,1)S(1)}, u32[]{:S(2)}, u32[]{:S(2)}) collective-permute-start(bf16[192,256]{1,0:T(8,128)(2,1)S(1)} %fusion.2), channel_id=1, source_target_pairs={{0,2},{1,3},{2,0},{3,1},{4,6},{5,7},{6,4},{7,5},{8,10},{9,11},{10,... | collective-permute-start | bytes 294920 | tf_op jit(solution)/shard_map/ppermute | solution.py:362
  71.3 13.3 %collective-permute-start.24 = (bf16[192,256]{1,0:T(8,128)(2,1)S(1)}, bf16[192,256]{1,0:T(8,128)(2,1)S(1)}, u32[]{:S(2)}, u32[]{:S(2)}) collective-permute-start(bf16[192,256]{1,0:T(8,128)(2,1)S(1)} %get-tuple-element.95), channel_id=1, source_target_pairs={{0,6},{1,7},{2,4},{3,5},{4,2},{5,3},{6,0},{7,1},{8,14},{9,15},{10,... | collective-permute-start | bytes 294920 | tf_op jit(solution)/shard_map/ppermute | solution.py:362
  72.8 11.8 %collective-permute-start.23 = (bf16[192,256]{1,0:T(8,128)(2,1)S(1)}, bf16[192,256]{1,0:T(8,128)(2,1)S(1)}, u32[]{:S(2)}, u32[]{:S(2)}) collective-permute-start(bf16[192,256]{1,0:T(8,128)(2,1)S(1)} %get-tuple-element.96), channel_id=1, source_target_pairs={{0,4},{1,5},{2,6},{3,7},{4,0},{5,1},{6,2},{7,3},{8,12},{9,13},{10,... | collective-permute-start | bytes 294920 | tf_op jit(solution)/shard_map/ppermute | solution.py:362
  74.3 8.3 %collective-permute-start.19 = (bf16[192,256]{1,0:T(8,128)(2,1)S(1)}, bf16[192,256]{1,0:T(8,128)(2,1)S(1)}, u32[]{:S(2)}, u32[]{:S(2)}) collective-permute-start(bf16[192,256]{1,0:T(8,128)(2,1)S(1)} %get-tuple-element.97), channel_id=1, source_target_pairs={{0,14},{1,15},{2,12},{3,13},{4,10},{5,11},{6,8},{7,9},{8,6},{9,7},... | collective-permute-start | bytes 294920 | tf_op jit(solution)/shard_map/ppermute | solution.py:362
  76.0 8.4 %collective-permute-start.18 = (bf16[192,256]{1,0:T(8,128)(2,1)S(1)}, bf16[192,256]{1,0:T(8,128)(2,1)S(1)}, u32[]{:S(2)}, u32[]{:S(2)}) collective-permute-start(bf16[192,256]{1,0:T(8,128)(2,1)S(1)} %get-tuple-element.98), channel_id=1, source_target_pairs={{0,12},{1,13},{2,14},{3,15},{4,8},{5,9},{6,10},{7,11},{8,4},{9,5},... | collective-permute-start | bytes 294920 | tf_op jit(solution)/shard_map/ppermute | solution.py:362
  78.3 10.7 %collective-permute-start.30 = (bf16[192,256]{1,0:T(8,128)(2,1)S(1)}, bf16[192,256]{1,0:T(8,128)(2,1)S(1)}, u32[]{:S(2)}, u32[]{:S(2)}) collective-permute-start(bf16[192,256]{1,0:T(8,128)(2,1)S(1)} %fusion.1), channel_id=1, source_target_pairs={{0,8},{1,9},{2,10},{3,11},{4,12},{5,13},{6,14},{7,15},{8,0},{9,1},... | collective-permute-start | bytes 294920 | tf_op jit(solution)/shard_map/ppermute | solution.py:362

commit v5 on v4

--- a/solution.py
+++ b/solution.py
@@ -182,47 +182,32 @@
     return outs[0], outs[1 : 1 + parts], outs[1 + parts : 1 + 2 * parts], outs[1 + 2 * parts :]
 
 
-def state_kernel(count, *refs):
-    tokens, contexts, weights = refs[0], refs[1 : 1 + count], refs[1 + count : 1 + 2 * count]
-    ids, dispatch, state, out = refs[1 + 2 * count :]
+def state_kernel(count, sends, *refs):
+    ids, tokens = refs[:2]
+    contexts, weights = refs[2 : 2 + count], refs[2 + count : 2 + 2 * count]
+    dispatch = refs[2 + 2 * count : 2 + 2 * count + sends]
+    state, outs = refs[2 + 2 * count + sends], refs[3 + 2 * count + sends :]
     total = tokens[...].astype(F32)
     for context, weight in zip(contexts, weights):
         total += dot(context[...], weight[...])
     state[...] = total.astype(BF16)
-    leave_kernel(ids, dispatch, state, out)
-
-
-def leave_kernel(ids, dispatch, state, out):
-    width = out.shape[1]
-    at = (ids[1] & (state.shape[1] // width - 1)) * width
-    out[...] = dot(dispatch[...], state[:, pl.ds(pl.multiple_of(at, width), width)]).astype(BF16)
+    for rows, out in zip(dispatch, outs):
+        width = out.shape[1]
+        at = (ids[1] & (state.shape[1] // width - 1)) * width
+        out[...] = dot(rows[...], state[:, pl.ds(pl.multiple_of(at, width), width)]).astype(BF16)
 
 
 def make_state(ids, tokens, contexts, weights, dispatch, cuts):
     return pl.pallas_call(
-        functools.partial(state_kernel, len(contexts)),
-        in_specs=[WHOLE] * (1 + 2 * len(contexts)) + [SCALARS, WHOLE],
-        out_specs=[WHOLE] * 2,
-        out_shape=[
-            jax.ShapeDtypeStruct(tokens.shape, BF16),
-            jax.ShapeDtypeStruct((dispatch.shape[0], tokens.shape[1] // cuts), BF16),
-        ],
+        functools.partial(state_kernel, len(contexts), len(dispatch)),
+        in_specs=[SCALARS] + [WHOLE] * (1 + 2 * len(contexts) + len(dispatch)),
+        out_specs=[WHOLE] * (1 + len(dispatch)),
+        out_shape=[jax.ShapeDtypeStruct(tokens.shape, BF16)]
+        + [jax.ShapeDtypeStruct((rows.shape[0], tokens.shape[1] // cut), BF16) for rows, cut in zip(dispatch, cuts)],
         compiler_params=PARAMS,
         cost_estimate=CHEAP,
         name="state",
-    )(tokens, *contexts, *weights, ids, dispatch)
-
-
-def leave(ids, dispatch, state, cuts):
-    return pl.pallas_call(
-        leave_kernel,
-        in_specs=[SCALARS, WHOLE, WHOLE],
-        out_specs=WHOLE,
-        out_shape=jax.ShapeDtypeStruct((dispatch.shape[0], state.shape[1] // cuts), BF16),
-        compiler_params=PARAMS,
-        cost_estimate=CHEAP,
-        name="leave",
-    )(ids, dispatch, state)
+    )(ids, tokens, *contexts, *weights, *dispatch)
 
 
 def home_kernel(experts, ids, state, dispatch, router, choice, own_a, own_b, gates, columns):
@@ -259,18 +244,21 @@
     )(ids, state, dispatch, router, choice)
 
 
-def expert_kernel(order, *refs):
-    ids, pieces = refs[0], refs[1 : 1 + len(order)]
-    expand, shrink, keep, give, hidden = refs[1 + len(order) :]
+def expert_kernel(order, blocks, *refs):
     cuts = len(order)
+    ids, pieces = refs[0], refs[1 : 1 + blocks * cuts]
+    expand, shrink, keep, give, rows_here, hidden = refs[1 + blocks * cuts :]
+    count, width = pieces[0].shape
+    for block in range(blocks):
+        for i in range(cuts):
+            rows_here[i, block * count : (block + 1) * count] = pieces[block * cuts + i][...]
     units = expand.shape[1]
     tile = min(TILE, units)
     for at in range(0, units, tile):
         total = jnp.zeros((hidden.shape[0], tile), F32)
-        for index, piece in zip(order, pieces):
-            width = piece.shape[1]
-            rows = pl.ds(pl.multiple_of(((ids[1] & (cuts - 1)) ^ index) * width, width), width)
-            total += dot(piece[...], expand[rows, at : at + tile])
+        for i, index in enumerate(order):
+            part = pl.ds(pl.multiple_of(((ids[1] & (cuts - 1)) ^ index) * width, width), width)
+            total += dot(rows_here[i], expand[part, at : at + tile])
         hidden[:, at : at + tile] = jnp.maximum(total, 0.0).astype(BF16)
     width = keep.shape[2]
     for j in range(keep.shape[0]):
@@ -281,19 +269,21 @@
         keep[j] = dot(hidden[...], shrink[:, pl.ds(at, width)])
 
 
-def run_expert(ids, order, pieces, expand, shrink, parts):
-    rows = pieces[0].shape[0]
+def run_expert(ids, order, blocks, expand, shrink, parts):
+    pieces = [piece for block in blocks for piece in block]
+    count, piece_width = pieces[0].shape
+    rows = count * len(blocks)
     features, units = expand.shape
     width = features // (2 * parts)
     return pl.pallas_call(
-        functools.partial(expert_kernel, tuple(order)),
+        functools.partial(expert_kernel, tuple(order), len(blocks)),
         in_specs=[SCALARS] + [WHOLE] * (2 + len(pieces)),
         out_specs=[WHOLE] * 2,
         out_shape=[
             jax.ShapeDtypeStruct((parts, rows, width), F32),
             jax.ShapeDtypeStruct((parts, rows, width), BF16),
         ],
-        scratch_shapes=[pltpu.VMEM((rows, units), BF16)],
+        scratch_shapes=[pltpu.VMEM((len(order), rows, piece_width), BF16), pltpu.VMEM((rows, units), BF16)],
         compiler_params=PARAMS,
         cost_estimate=CHEAP,
         name="expert",
@@ -350,6 +340,7 @@
     capacity = max(2, 3 * token_count // experts)
     direct = groups <= DIRECT
     pairs = slices // 2
+    slots = capacity if direct else experts * capacity
 
     def hop(value, along_expert, along_mp):
         if along_expert == 0 and along_mp == 0:
@@ -391,11 +382,11 @@
         previous = attend(asked, source, token_count)
         context = lax.dynamic_slice_in_dim(spread(previous), source_owner[0] * token_count, token_count, 0)
 
-    choice, dispatch, first, second = route(ids, after(expert_choice, context), experts, len(steps), capacity)
+    choice, dispatch, first, second = route(ids, after(expert_choice, previous), experts, len(steps), capacity)
     weights, order = [output_weight], [0]
     for bit in bits:
         if bit == 1:
-            weights = [after(weight, dispatch[0]) for weight in weights]
+            weights = [after(weight, context) for weight in weights]
         weights = weights + [hop(weight, 0, bit) for weight in weights]
         order = order + [index ^ bit for index in order]
     contexts = [context]
@@ -403,30 +394,14 @@
         contexts = contexts + [hop(value if i == 0 else after(value, dispatch[0]), 0, bit) for i, value in enumerate(contexts)]
 
     relayed = groups // 2 if direct and pairs > 1 and groups > 1 else -1
-    far = list(reversed(range(1, groups)))
-    sends = ([relayed] if relayed >= 0 else []) + [k for k in far if k != relayed] if direct else [0]
-    cuts = {k: slices if k == relayed else 2 for k in sends}
-    leaving = {}
-    for k in sends:
-        if not leaving:
-            state, leaving[k] = make_state(ids, tokens, contexts, weights, dispatch[k], cuts[k])
-            waited = state
-        else:
-            waited = leaving[k] = leave(ids, dispatch[k], after(state, waited), cuts[k])
+    rest = [k for k in reversed(range(1, groups)) if k != relayed]
+    sends = ([relayed] if relayed >= 0 else []) + rest if direct else [0]
+    cuts = [slices if k == relayed else 2 for k in sends]
+    state, *leaving = make_state(ids, tokens, contexts, weights, [dispatch[k] for k in sends], cuts)
     own_a, own_b, gates, columns = at_home(
-        ids, after(state, waited), dispatch[0], router_weight.T, choice, experts, width
+        ids, state, dispatch[0], router_weight.T, choice, experts, width
     )
-
-    results = columns
-    arrived = {k: hop(leaving[k], k, 0) for k in sends} if direct else {0: spread(leaving[0])}
-    turns = [k for k in far if k != relayed] + [k for k in far if k == relayed] if direct else [0]
-    inputs = {}
-    if relayed >= 0:
-        pieces, places = [arrived[relayed]], [0]
-        for bit in bits:
-            pieces = pieces + [hop(piece, 0, bit) for piece in pieces]
-            places = places + [index ^ bit for index in places]
-        inputs[relayed] = pieces, places
+    expert = functools.partial(run_expert, expand=expand_weight[0], shrink=shrink_weight[0], parts=pairs)
 
     def sum_cores(keep, give):
         return keep + hop(give, 0, 1).astype(F32)
@@ -440,25 +415,37 @@
         parts = [summed[j].astype(BF16) for j in range(pairs)]
         return [hop(part, k, 2 * j) if direct else hop(spread(part), 0, 2 * j) for j, part in enumerate(parts)]
 
-    def gather(k, results, parts, dtype):
-        return combine(gates, results, first[k], second[k], parts, dtype)
-
-    turn_ids, home = ids, {}
+    home = {}
     if direct:
-        keep, give = run_expert(ids, [0, 1], [own_a, own_b], expand_weight[0], shrink_weight[0], pairs)
-        parts = send_home(0, sum_cores(keep, after(give, arrived[sends[0]])))
-        results = gather(0, results, parts, F32)
-        turn_ids = after(ids, results)
-    for k in turns:
-        if k in inputs:
-            pieces, places = inputs[k]
-        else:
-            pieces, places = [arrived[k], hop(arrived[k], 0, 1)], [0, 1]
-        keep, give = run_expert(turn_ids, places, pieces, expand_weight[0], shrink_weight[0], pairs)
+        arrived = {k: hop(rows, k, 0) for k, rows in zip(sends, leaving)}
+        keep, give = expert(ids, [0, 1], [[own_a, own_b]])
+        if sends:
+            give = after(give, arrived[sends[0]])
+        home[0] = send_home(0, sum_cores(keep, give))
         turn_ids = after(ids, give)
-        home[k] = send_home(k, sum_cores(keep, give))
-    for k in turns:
-        results = gather(k, results, home[k], BF16 if k == turns[-1] else F32)
+        if rest:
+            mine = [arrived[k] for k in rest]
+            keep, give = expert(turn_ids, [0, 1], [[rows, hop(rows, 0, 1)] for rows in mine])
+            turn_ids = after(ids, give)
+            summed = sum_cores(keep, give)
+            for i, k in enumerate(rest):
+                home[k] = send_home(k, summed[:, i * slots : (i + 1) * slots])
+        if relayed >= 0:
+            pieces, places = [arrived[relayed]], [0]
+            for bit in bits:
+                pieces = pieces + [hop(piece, 0, bit) for piece in pieces]
+                places = places + [index ^ bit for index in places]
+            keep, give = expert(turn_ids, places, [pieces])
+            home[relayed] = send_home(relayed, sum_cores(keep, give))
+        order = [0] + rest + ([relayed] if relayed >= 0 else [])
+    else:
+        mine = spread(leaving[0])
+        keep, give = expert(ids, [0, 1], [[mine, hop(mine, 0, 1)]])
+        home[0] = send_home(0, sum_cores(keep, give))
+        order = [0]
+    results = columns
+    for k in order:
+        results = combine(gates, results, first[k], second[k], home[k], BF16 if k == order[-1] else F32)
     return results
 
 

time: 90 us -> 85.3 us (0.948)
  waiting for transfers between devices: 35.8 us -> 33.7 us
  Pallas kernels: 18.7 us -> 16.7 us
    ppermute x31 -> x30, waiting for transfers between devices: 35.8 us -> 33.7 us  [hop(): return lax.ppermute(value, ('expert', 'mp'), moves)]
    pallas_call x7 -> x4, Pallas kernels: 9.07 us -> 7.03 us  [the longest x3 5.45 us: run_expert(): pl.pallas_call(functools.partial(expert_kernel, tuple(order), len(blocks)...]
    ppermute x31 -> x30, starting transfers between devices: 33.9 us -> 33.4 us  [hop(): return lax.ppermute(value, ('expert', 'mp'), moves)]
  transfers between devices with their start and end apart: 31 -> 30, of which waited for: 11 -> 13; matrix products, arithmetic and copies ran while one was open for 0% -> 0% of each run, Pallas kernels for 17% -> 15%
where the time goes in v5:
time: 85.3 us; the launch traced here: 85.1 us
  waiting for transfers between devices  33.7 us (40%)
  starting transfers between devices  33.4 us (39%)
  Pallas kernels  16.7 us (20%)
  between operations  0.98 us (1%)
    ppermute x30, waiting for transfers between devices, hop(): return lax.ppermute(value, ('expert', 'mp'), moves)  33.7 us
    ppermute x30, starting transfers between devices, hop(): return lax.ppermute(value, ('expert', 'mp'), moves)  33.4 us
    pallas_call x3, Pallas kernels, run_expert(): pl.pallas_call(functools.partial(expert_kernel, tuple(order), len(blocks)...  5.45 us
    pallas_call x4, Pallas kernels, attend(): pl.pallas_call(attend_kernel, in_specs=[WHOLE] * 2, out_specs=WHOLE, out_...  3.09 us
    pallas_call x1, Pallas kernels, ask(): pl.pallas_call(query_kernel, in_specs=[pl.BlockSpec(memory_space=pltpu.HB...  1.81 us
  transfers between devices with their start and end apart: 30, of which 13 were waited for; matrix products, arithmetic and copies ran while one was open for 0% of the time, Pallas kernels for 15%

profile of v5, /device:TPU:0, one launch (start us, length us, event | category | flops | bytes accessed | tf_op | source)
XLA Modules:
  0.0 85.1 jit_solution(12565249378205206208)
XLA Ops:
  0.0 2.9 %collective-permute-start.9 = (bf16[256,1024]{1,0:T(8,128)(2,1)}, bf16[256,1024]{1,0:T(8,128)(2,1)S(1)}, u32[]{:S(2)}, u32[]{:S(2)}) collective-permute-start(bf16[256,1024]{1,0:T(8,128)(2,1)} %refs_6_), channel_id=1, source_target_pairs={{0,2},{1,3},{2,0},{3,1},{4,6},{5,7},{6,4},{7,5},{8,10},{9,11},{10,... | collective-permute-start | bytes 1572872 | tf_op jit(solution)/shard_map/ppermute | solution.py:353
  2.9 0.1 pad_add_fusion.ids.refs_0_
  3.0 1.8 %query.1 = (bf16[256,256]{1,0:T(8,128)(2,1)S(1)}, bf16[2,512,256]{2,1,0:T(8,128)(2,1)S(1)}) custom-call(bf16[256,1024]{1,0:T(8,128)(2,1)} %refs_1_.1, bf16[1024,256]{1,0:T(8,128)(2,1)} %weight.1, bf16[2,512,256]{2,1,0:T(8,128)(2,1)} %bitcast.35), custom_call_target="tpu_custom_call" | custom-call | tf_op jit(solution)/shard_map/query/pallas_call | solution.py:60
  4.8 0.0 copy-start.3
  4.8 0.0 copy-start.5
  4.9 0.0 copy-start.2
  4.9 2.6 %collective-permute-start.2 = (bf16[256,256]{1,0:T(8,128)(2,1)S(1)}, bf16[256,256]{1,0:T(8,128)(2,1)S(1)}, u32[]{:S(2)}, u32[]{:S(2)}) collective-permute-start(bf16[256,256]{1,0:T(8,128)(2,1)S(1)} %get-tuple-element.47.queries), channel_id=1, source_target_pairs={{0,8},{1,9},{2,10},{3,11},{4,12},{5,13},{6,14},{7,15},{8,0},{9,1},... | collective-permute-start | bytes 393224 | tf_op jit(solution)/shard_map/ppermute | solution.py:353
  7.5 1.6 %collective-permute-start = (bf16[256,256]{1,0:T(8,128)(2,1)S(1)}, bf16[256,256]{1,0:T(8,128)(2,1)S(1)}, u32[]{:S(2)}, u32[]{:S(2)}) collective-permute-start(bf16[256,256]{1,0:T(8,128)(2,1)S(1)} %get-tuple-element.47.queries), channel_id=1, source_target_pairs={{0,4},{1,5},{2,6},{3,7},{4,0},{5,1},{6,2},{7,3},{8,12},{9,13},{10,... | collective-permute-start | bytes 393224 | tf_op jit(solution)/shard_map/ppermute | solution.py:353
  9.1 0.8 attend.4.refs_0_
  9.9 3.8 %collective-permute-done.2.queries = bf16[256,256]{1,0:T(8,128)(2,1)S(1)} collective-permute-done((bf16[256,256]{1,0:T(8,128)(2,1)S(1)}, bf16[256,256]{1,0:T(8,128)(2,1)S(1)}, u32[]{:S(2)}, u32[]{:S(2)}) %collective-permute-start.2) | collective-permute-done | bytes 131104 | tf_op jit(solution)/shard_map/ppermute | solution.py:353
  13.7 0.6 collective-permute-start.4
  14.3 0.0 collective-permute-done.queries
  14.3 0.8 attend.5
  15.1 1.5 %collective-permute-start.1 = (bf16[256,256]{1,0:T(8,128)(2,1)S(1)}, bf16[256,256]{1,0:T(8,128)(2,1)S(1)}, u32[]{:S(2)}, u32[]{:S(2)}) collective-permute-start(bf16[256,256]{1,0:T(8,128)(2,1)S(1)} %attend.5), channel_id=1, source_target_pairs={{0,4},{1,5},{2,6},{3,7},{4,0},{5,1},{6,2},{7,3},{8,12},{9,13},{10,... | collective-permute-start | bytes 393224 | tf_op jit(solution)/shard_map/ppermute | solution.py:353
  16.6 0.8 attend.6
  17.4 2.0 %collective-permute-start.3 = (bf16[256,256]{1,0:T(8,128)(2,1)S(1)}, bf16[256,256]{1,0:T(8,128)(2,1)S(1)}, u32[]{:S(2)}, u32[]{:S(2)}) collective-permute-start(bf16[256,256]{1,0:T(8,128)(2,1)S(1)} %attend.6), channel_id=1, source_target_pairs={{0,8},{1,9},{2,10},{3,11},{4,12},{5,13},{6,14},{7,15},{8,0},{9,1},... | collective-permute-start | bytes 393224 | tf_op jit(solution)/shard_map/ppermute | solution.py:353
  19.4 0.5 collective-permute-done.4.queries
  19.9 0.8 attend.7
  20.7 0.0 copy-start.4
  20.7 3.6 %collective-permute-start.5 = (bf16[256,256]{1,0:T(8,128)(2,1)S(1)}, bf16[256,256]{1,0:T(8,128)(2,1)S(1)}, u32[]{:S(2)}, u32[]{:S(2)}) collective-permute-start(bf16[256,256]{1,0:T(8,128)(2,1)S(1)} %attend.7), channel_id=1, source_target_pairs={{0,12},{1,13},{2,14},{3,15},{4,8},{5,9},{6,10},{7,11},{8,4},{9,5},... | collective-permute-start | bytes 393224 | tf_op jit(solution)/shard_map/ppermute | solution.py:353
  25.0 4.3 %collective-permute-done.5.refs_3_ = bf16[256,256]{1,0:T(8,128)(2,1)S(1)} collective-permute-done((bf16[256,256]{1,0:T(8,128)(2,1)S(1)}, bf16[256,256]{1,0:T(8,128)(2,1)S(1)}, u32[]{:S(2)}, u32[]{:S(2)}) %collective-permute-start.5) | collective-permute-done | bytes 131104 | tf_op jit(solution)/shard_map/ppermute | solution.py:353
  29.3 0.6 pick.1.refs_2_
  29.9 0.1 collective-permute-start.10
  30.0 0.5 collective-permute-start.11
  30.5 0.5 collective-permute-start.6
  31.0 1.5 %route.1 = (s32[256,2]{1,0:T(8,128)S(1)}, bf16[192,256]{1,0:T(8,128)(2,1)S(1)}, bf16[192,256]{1,0:T(8,128)(2,1)S(1)}, bf16[192,256]{1,0:T(8,128)(2,1)S(1)}, bf16...) custom-call(s32[2]{0:T(128)S(1)} %pad_add_fusion.ids.refs_0_, ...), custom_call_target="tpu_custom_call" | custom-call | tf_op jit(solution)/shard_map/route/pallas_call | solution.py:171
  32.5 0.1 collective-permute-start.7
  32.6 3.4 %collective-permute-done.6.refs_3_ = bf16[256,256]{1,0:T(8,128)(2,1)S(1)} collective-permute-done((bf16[256,256]{1,0:T(8,128)(2,1)S(1)}, bf16[256,256]{1,0:T(8,128)(2,1)S(1)}, u32[]{:S(2)}, u32[]{:S(2)}) %collective-permute-start.6) | collective-permute-done | bytes 131104 | tf_op jit(solution)/shard_map/ppermute | solution.py:353
  36.0 1.3 %collective-permute-done.8.refs_5_ = bf16[256,256]{1,0:T(8,128)(2,1)S(1)} collective-permute-done((bf16[256,256]{1,0:T(8,128)(2,1)S(1)}, bf16[256,256]{1,0:T(8,128)(2,1)S(1)}, u32[]{:S(2)}, u32[]{:S(2)}) %collective-permute-start.8) | collective-permute-done | bytes 131104 | tf_op jit(solution)/shard_map/ppermute | solution.py:353
  37.3 0.0 copy-start
  37.3 0.0 copy-start.1
  37.4 1.6 %state.1 = (bf16[256,1024]{1,0:T(8,128)(2,1)S(1)}, bf16[192,256]{1,0:T(8,128)(2,1)S(1)}, bf16[192,512]{1,0:T(8,128)(2,1)S(1)}, bf16[192,512]{1,0:T(8,128)(2,1)S(1)}) custom-call(s32[2]{0:T(128)S(1)} %pad_add_fusion.ids.refs_0_, bf16[256,1024]{1,0:T(8,128)(2,1)S(1)} %copy-done.2, bf16[256,256]{1,0:T(8,128)(2,1)S(1)} %pick.1.refs_2_, ...), custom_call_target="tpu_custom_call" | custom-call | tf_op jit(solution)/shard_map/state/pallas_call | solution.py:201
  38.9 4.8 %collective-permute-start.12 = (bf16[192,256]{1,0:T(8,128)(2,1)S(1)}, bf16[192,256]{1,0:T(8,128)(2,1)S(1)}, u32[]{:S(2)}, u32[]{:S(2)}) collective-permute-start(bf16[192,256]{1,0:T(8,128)(2,1)S(1)} %get-tuple-element.71), channel_id=1, source_target_pairs={{0,8},{1,9},{2,10},{3,11},{4,12},{5,13},{6,14},{7,15},{8,0},{9,1},... | collective-permute-start | bytes 294920 | tf_op jit(solution)/shard_map/ppermute | solution.py:353
  43.7 0.7 collective-permute-start.15
  44.4 1.0 %home.1 = (bf16[192,512]{1,0:T(8,128)(2,1)S(1)}, bf16[192,512]{1,0:T(8,128)(2,1)S(1)}, f32[256,2]{1,0:T(8,128)S(1)}, f32[256,256]{1,0:T(8,128)S(1)}) custom-call(s32[2]{0:T(128)S(1)} %pad_add_fusion.ids.refs_0_, bf16[256,1024]{1,0:T(8,128)(2,1)S(1)} %get-tuple-element.61.state, bf16[192,256]{1,0:T(8,128)(2,1)S(1)} %get-tuple-element.54.dispatch, ...), custom_call_target="tpu_custom_call" | custom-call | tf_op jit(solution)/shard_map/home/pallas_call | solution.py:231
  45.4 1.5 %expert.3 = (f32[2,192,256]{2,1,0:T(8,128)S(1)}, bf16[2,192,256]{2,1,0:T(8,128)(2,1)S(1)}) custom-call(s32[2]{0:T(128)S(1)} %pad_add_fusion.ids.refs_0_, bf16[192,512]{1,0:T(8,128)(2,1)S(1)} %get-tuple-element.67.refs_1_, bf16[192,512]{1,0:T(8,128)(2,1)S(1)} %get-tuple-element.68.refs_2_, bf16[1024,1024]{1,0:T(8,128)(2,1)S(1)} %bitcast.27, ...), custom_call_target="tpu_custom_call" | custom-call | tf_op jit(solution)/shard_map/expert/pallas_call | solution.py:278
  47.0 6.6 %collective-permute-done.12.refs_1_ = bf16[192,256]{1,0:T(8,128)(2,1)S(1)} collective-permute-done((bf16[192,256]{1,0:T(8,128)(2,1)S(1)}, bf16[192,256]{1,0:T(8,128)(2,1)S(1)}, u32[]{:S(2)}, u32[]{:S(2)}) %collective-permute-start.12) | collective-permute-done | bytes 98336 | tf_op jit(solution)/shard_map/ppermute | solution.py:353
  53.6 0.5 collective-permute-start.24
  54.1 0.2 collective-permute-start.25
  54.3 0.3 collective-permute-start.16
  54.6 2.0 %collective-permute-done.17.refs_3_ = bf16[192,512]{1,0:T(8,128)(2,1)S(1)} collective-permute-done((bf16[192,512]{1,0:T(8,128)(2,1)S(1)}, bf16[192,512]{1,0:T(8,128)(2,1)S(1)}, u32[]{:S(2)}, u32[]{:S(2)}) %collective-permute-start.17) | collective-permute-done | bytes 196640 | tf_op jit(solution)/shard_map/ppermute | solution.py:353
  56.6 2.2 %collective-permute-done.24.refs_2_ = bf16[192,256]{1,0:T(8,128)(2,1)S(1)} collective-permute-done((bf16[192,256]{1,0:T(8,128)(2,1)S(1)}, bf16[192,256]{1,0:T(8,128)(2,1)S(1)}, u32[]{:S(2)}, u32[]{:S(2)}) %collective-permute-start.24) | collective-permute-done | bytes 98336 | tf_op jit(solution)/shard_map/ppermute | solution.py:353
  58.8 0.1 add_convert_fusion.1
  58.9 2.4 %expert.4 = (f32[2,384,256]{2,1,0:T(8,128)S(1)}, bf16[2,384,256]{2,1,0:T(8,128)(2,1)S(1)}) custom-call(s32[2]{0:T(128)S(1)} %pad_add_fusion.ids.refs_0_, bf16[192,512]{1,0:T(8,128)(2,1)S(1)} %collective-permute-done.15.refs_1_, bf16[192,512]{1,0:T(8,128)(2,1)S(1)} %collective-permute-done.16.refs_2_, bf16[192,512]{1,0:T(8,128)(2,1)S(1)} %collective-permute-done.17.refs_3_, ...), custom_call_target="tpu_custom_call" | custom-call | tf_op jit(solution)/shard_map/expert/pallas_call | solution.py:278
  61.3 1.5 %expert.5 = (f32[2,192,256]{2,1,0:T(8,128)S(1)}, bf16[2,192,256]{2,1,0:T(8,128)(2,1)S(1)}) custom-call(s32[2]{0:T(128)S(1)} %pad_add_fusion.ids.refs_0_, bf16[192,256]{1,0:T(8,128)(2,1)S(1)} %collective-permute-done.12.refs_1_, bf16[192,256]{1,0:T(8,128)(2,1)S(1)} %collective-permute-done.24.refs_2_, bf16[192,256]{1,0:T(8,128)(2,1)S(1)} %collective-permute-done.25.refs_3_, ...), custom_call_target="tpu_custom_call" | custom-call | tf_op jit(solution)/shard_map/expert/pallas_call | solution.py:278
  62.8 0.6 collective-permute-start.27
  63.4 0.6 collective-permute-start.14
  63.9 0.5 collective-permute-done.27
  64.5 1.1 %collective-permute-start.28 = (bf16[192,256]{1,0:T(8,128)(2,1)S(1)}, bf16[192,256]{1,0:T(8,128)(2,1)S(1)}, u32[]{:S(2)}, u32[]{:S(2)}) collective-permute-start(bf16[192,256]{1,0:T(8,128)(2,1)S(1)} %fusion.2), channel_id=1, source_target_pairs={{0,2},{1,3},{2,0},{3,1},{4,6},{5,7},{6,4},{7,5},{8,10},{9,11},{10,... | collective-permute-start | bytes 294920 | tf_op jit(solution)/shard_map/ppermute | solution.py:353
  65.6 0.0 collective-permute-done.19
  65.7 0.1 add_convert_fusion
  65.8 1.6 %collective-permute-start.23 = (bf16[192,256]{1,0:T(8,128)(2,1)S(1)}, bf16[192,256]{1,0:T(8,128)(2,1)S(1)}, u32[]{:S(2)}, u32[]{:S(2)}) collective-permute-start(bf16[192,256]{1,0:T(8,128)(2,1)S(1)} %get-tuple-element.87), channel_id=1, source_target_pairs={{0,6},{1,7},{2,4},{3,5},{4,2},{5,3},{6,0},{7,1},{8,14},{9,15},{10,... | collective-permute-start | bytes 294920 | tf_op jit(solution)/shard_map/ppermute | solution.py:353
  67.4 1.5 %collective-permute-start.22 = (bf16[192,256]{1,0:T(8,128)(2,1)S(1)}, bf16[192,256]{1,0:T(8,128)(2,1)S(1)}, u32[]{:S(2)}, u32[]{:S(2)}) collective-permute-start(bf16[192,256]{1,0:T(8,128)(2,1)S(1)} %get-tuple-element.88), channel_id=1, source_target_pairs={{0,4},{1,5},{2,6},{3,7},{4,0},{5,1},{6,2},{7,3},{8,12},{9,13},{10,... | collective-permute-start | bytes 294920 | tf_op jit(solution)/shard_map/ppermute | solution.py:353
  68.9 1.9 %collective-permute-start.21 = (bf16[192,256]{1,0:T(8,128)(2,1)S(1)}, bf16[192,256]{1,0:T(8,128)(2,1)S(1)}, u32[]{:S(2)}, u32[]{:S(2)}) collective-permute-start(bf16[192,256]{1,0:T(8,128)(2,1)S(1)} %get-tuple-element.89), channel_id=1, source_target_pairs={{0,14},{1,15},{2,12},{3,13},{4,10},{5,11},{6,8},{7,9},{8,6},{9,7},... | collective-permute-start | bytes 294920 | tf_op jit(solution)/shard_map/ppermute | solution.py:353
  70.8 1.5 %collective-permute-done.28 = bf16[192,256]{1,0:T(8,128)(2,1)S(1)} collective-permute-done((bf16[192,256]{1,0:T(8,128)(2,1)S(1)}, bf16[192,256]{1,0:T(8,128)(2,1)S(1)}, u32[]{:S(2)}, u32[]{:S(2)}) %collective-permute-start.28) | collective-permute-done | bytes 98336 | tf_op jit(solution)/shard_map/ppermute | solution.py:353
  72.3 1.9 %collective-permute-start.20 = (bf16[192,256]{1,0:T(8,128)(2,1)S(1)}, bf16[192,256]{1,0:T(8,128)(2,1)S(1)}, u32[]{:S(2)}, u32[]{:S(2)}) collective-permute-start(bf16[192,256]{1,0:T(8,128)(2,1)S(1)} %get-tuple-element.90), channel_id=1, source_target_pairs={{0,12},{1,13},{2,14},{3,15},{4,8},{5,9},{6,10},{7,11},{8,4},{9,5},... | collective-permute-start | bytes 294920 | tf_op jit(solution)/shard_map/ppermute | solution.py:353
  74.2 1.8 %collective-permute-start.29 = (bf16[192,256]{1,0:T(8,128)(2,1)S(1)}, bf16[192,256]{1,0:T(8,128)(2,1)S(1)}, u32[]{:S(2)}, u32[]{:S(2)}) collective-permute-start(bf16[192,256]{1,0:T(8,128)(2,1)S(1)} %fusion.1), channel_id=1, source_target_pairs={{0,8},{1,9},{2,10},{3,11},{4,12},{5,13},{6,14},{7,15},{8,0},{9,1},... | collective-permute-start | bytes 294920 | tf_op jit(solution)/shard_map/ppermute | solution.py:353
  76.1 0.2 combine.4.base
  76.3 0.7 collective-permute-done.21.refs_1_
  77.0 2.1 %collective-permute-done.20.refs_0_ = bf16[192,256]{1,0:T(8,128)(2,1)S(1)} collective-permute-done((bf16[192,256]{1,0:T(8,128)(2,1)S(1)}, bf16[192,256]{1,0:T(8,128)(2,1)S(1)}, u32[]{:S(2)}, u32[]{:S(2)}) %collective-permute-start.20) | collective-permute-done | bytes 98336 | tf_op jit(solution)/shard_map/ppermute | solution.py:353
  79.2 0.2 combine.5.base
  79.4 0.2 combine.6.base
  79.7 4.6 %collective-permute-done.29.refs_0_ = bf16[192,256]{1,0:T(8,128)(2,1)S(1)} collective-permute-done((bf16[192,256]{1,0:T(8,128)(2,1)S(1)}, bf16[192,256]{1,0:T(8,128)(2,1)S(1)}, u32[]{:S(2)}, u32[]{:S(2)}) %collective-permute-start.29) | collective-permute-done | bytes 98336 | tf_op jit(solution)/shard_map/ppermute | solution.py:353
  84.2 0.9 %combine.7 = bf16[256,256]{1,0:T(8,128)(2,1)} custom-call(f32[256,2]{1,0:T(8,128)S(1)} %get-tuple-element.63.gates, f32[256,256]{1,0:T(8,128)S(1)} %combine.6.base, bf16[256,192]{1,0:T(8,128)(2,1)S(1)} %get-tuple-element.82.first, bf16[256,192]{1,0:T(8,128)(2,1)S(1)} %get-tuple-element.83.second, bf16[192,256]{1,0:T(8,128)(2,1)S(1)} %collective-permute-done.29.refs_0_), custom_call_target="tpu_custom_call" | custom-call | tf_op jit(solution)/shard_map/combine/pallas_call | solution.py:304
  (32 shorter events, 0.2 us)
Async XLA Ops:
  0.0 30.0 %collective-permute-start.9 = (bf16[256,1024]{1,0:T(8,128)(2,1)}, bf16[256,1024]{1,0:T(8,128)(2,1)S(1)}, u32[]{:S(2)}, u32[]{:S(2)}) collective-permute-start(bf16[256,1024]{1,0:T(8,128)(2,1)} %refs_6_), channel_id=1, source_target_pairs={{0,2},{1,3},{2,0},{3,1},{4,6},{5,7},{6,4},{7,5},{8,10},{9,11},{10,... | collective-permute-start | bytes 1572872 | tf_op jit(solution)/shard_map/ppermute | solution.py:353
  4.8 25.1 %copy-start.3 = (bf16[256,1024]{1,0:T(8,128)(2,1)S(1)}, bf16[256,1024]{1,0:T(8,128)(2,1)}, u32[]{:S(2)}) copy-start(bf16[256,1024]{1,0:T(8,128)(2,1)} %refs_6_) | copy-start | bytes 1572868
  4.8 26.2 %copy-start.5 = (s32[256,2]{0,1:T(2,128)S(1)}, s32[256,2]{0,1:T(2,128)}, u32[]{:S(2)}) copy-start(s32[256,2]{0,1:T(2,128)} %param.15) | copy-start | bytes 6148
  4.9 32.5 %copy-start.2 = (bf16[256,1024]{1,0:T(8,128)(2,1)S(1)}, bf16[256,1024]{1,0:T(8,128)(2,1)}, u32[]{:S(2)}) copy-start(bf16[256,1024]{1,0:T(8,128)(2,1)} %refs_1_.1) | copy-start | bytes 1572868
  4.9 8.8 %collective-permute-start.2 = (bf16[256,256]{1,0:T(8,128)(2,1)S(1)}, bf16[256,256]{1,0:T(8,128)(2,1)S(1)}, u32[]{:S(2)}, u32[]{:S(2)}) collective-permute-start(bf16[256,256]{1,0:T(8,128)(2,1)S(1)} %get-tuple-element.47.queries), channel_id=1, source_target_pairs={{0,8},{1,9},{2,10},{3,11},{4,12},{5,13},{6,14},{7,15},{8,0},{9,1},... | collective-permute-start | bytes 393224 | tf_op jit(solution)/shard_map/ppermute | solution.py:353
  7.5 6.8 %collective-permute-start = (bf16[256,256]{1,0:T(8,128)(2,1)S(1)}, bf16[256,256]{1,0:T(8,128)(2,1)S(1)}, u32[]{:S(2)}, u32[]{:S(2)}) collective-permute-start(bf16[256,256]{1,0:T(8,128)(2,1)S(1)} %get-tuple-element.47.queries), channel_id=1, source_target_pairs={{0,4},{1,5},{2,6},{3,7},{4,0},{5,1},{6,2},{7,3},{8,12},{9,13},{10,... | collective-permute-start | bytes 393224 | tf_op jit(solution)/shard_map/ppermute | solution.py:353
  13.7 6.2 %collective-permute-start.4 = (bf16[256,256]{1,0:T(8,128)(2,1)S(1)}, bf16[256,256]{1,0:T(8,128)(2,1)S(1)}, u32[]{:S(2)}, u32[]{:S(2)}) collective-permute-start(bf16[256,256]{1,0:T(8,128)(2,1)S(1)} %collective-permute-done.2.queries), channel_id=1, source_target_pairs={{0,4},{1,5},{2,6},{3,7},{4,0},{5,1},{6,2},{7,3},{8,12},{9,13},{10,... | collective-permute-start | bytes 393224 | tf_op jit(solution)/shard_map/ppermute | solution.py:353
  15.1 9.9 %collective-permute-start.1 = (bf16[256,256]{1,0:T(8,128)(2,1)S(1)}, bf16[256,256]{1,0:T(8,128)(2,1)S(1)}, u32[]{:S(2)}, u32[]{:S(2)}) collective-permute-start(bf16[256,256]{1,0:T(8,128)(2,1)S(1)} %attend.5), channel_id=1, source_target_pairs={{0,4},{1,5},{2,6},{3,7},{4,0},{5,1},{6,2},{7,3},{8,12},{9,13},{10,... | collective-permute-start | bytes 393224 | tf_op jit(solution)/shard_map/ppermute | solution.py:353
  17.4 7.6 %collective-permute-start.3 = (bf16[256,256]{1,0:T(8,128)(2,1)S(1)}, bf16[256,256]{1,0:T(8,128)(2,1)S(1)}, u32[]{:S(2)}, u32[]{:S(2)}) collective-permute-start(bf16[256,256]{1,0:T(8,128)(2,1)S(1)} %attend.6), channel_id=1, source_target_pairs={{0,8},{1,9},{2,10},{3,11},{4,12},{5,13},{6,14},{7,15},{8,0},{9,1},... | collective-permute-start | bytes 393224 | tf_op jit(solution)/shard_map/ppermute | solution.py:353
  20.7 23.7 %copy-start.4 = (bf16[1024,4]{0,1:T(4,128)(2,1)S(1)}, bf16[1024,4]{0,1:T(4,128)(2,1)}, u32[]{:S(2)}) copy-start(bf16[1024,4]{0,1:T(4,128)(2,1)} %param.14) | copy-start | bytes 24580
  20.7 8.6 %collective-permute-start.5 = (bf16[256,256]{1,0:T(8,128)(2,1)S(1)}, bf16[256,256]{1,0:T(8,128)(2,1)S(1)}, u32[]{:S(2)}, u32[]{:S(2)}) collective-permute-start(bf16[256,256]{1,0:T(8,128)(2,1)S(1)} %attend.7), channel_id=1, source_target_pairs={{0,12},{1,13},{2,14},{3,15},{4,8},{5,9},{6,10},{7,11},{8,4},{9,5},... | collective-permute-start | bytes 393224 | tf_op jit(solution)/shard_map/ppermute | solution.py:353
  29.9 7.4 %collective-permute-start.10 = (bf16[256,1024]{1,0:T(8,128)(2,1)S(1)}, bf16[256,1024]{1,0:T(8,128)(2,1)S(1)}, u32[]{:S(2)}, u32[]{:S(2)}) collective-permute-start(bf16[256,1024]{1,0:T(8,128)(2,1)S(1)} %copy-done.3), channel_id=1, source_target_pairs={{0,1},{1,0},{2,3},{3,2},{4,5},{5,4},{6,7},{7,6},{8,9},{9,8},{10,11... | collective-permute-start | bytes 1572872 | tf_op jit(solution)/shard_map/ppermute | solution.py:353
  30.0 7.3 %collective-permute-start.11 = (bf16[256,1024]{1,0:T(8,128)(2,1)S(1)}, bf16[256,1024]{1,0:T(8,128)(2,1)S(1)}, u32[]{:S(2)}, u32[]{:S(2)}) collective-permute-start(bf16[256,1024]{1,0:T(8,128)(2,1)S(1)} %collective-permute-done.9.refs_7_), channel_id=1, source_target_pairs={{0,1},{1,0},{2,3},{3,2},{4,5},{5,4},{6,7},{7,6},{8,9},{9,8},{10,11... | collective-permute-start | bytes 1572872 | tf_op jit(solution)/shard_map/ppermute | solution.py:353
  30.5 5.5 %collective-permute-start.6 = (bf16[256,256]{1,0:T(8,128)(2,1)S(1)}, bf16[256,256]{1,0:T(8,128)(2,1)S(1)}, u32[]{:S(2)}, u32[]{:S(2)}) collective-permute-start(bf16[256,256]{1,0:T(8,128)(2,1)S(1)} %pick.1.refs_2_), channel_id=1, source_target_pairs={{0,2},{1,3},{2,0},{3,1},{4,6},{5,7},{6,4},{7,5},{8,10},{9,11},{10,... | collective-permute-start | bytes 393224 | tf_op jit(solution)/shard_map/ppermute | solution.py:353
  32.5 3.5 %collective-permute-start.7 = (bf16[256,256]{1,0:T(8,128)(2,1)S(1)}, bf16[256,256]{1,0:T(8,128)(2,1)S(1)}, u32[]{:S(2)}, u32[]{:S(2)}) collective-permute-start(bf16[256,256]{1,0:T(8,128)(2,1)S(1)} %pick.1.refs_2_), channel_id=1, source_target_pairs={{0,1},{1,0},{2,3},{3,2},{4,5},{5,4},{6,7},{7,6},{8,9},{9,8},{10,11... | collective-permute-start | bytes 393224 | tf_op jit(solution)/shard_map/ppermute | solution.py:353
  36.0 1.3 %collective-permute-start.8 = (bf16[256,256]{1,0:T(8,128)(2,1)S(1)}, bf16[256,256]{1,0:T(8,128)(2,1)S(1)}, u32[]{:S(2)}, u32[]{:S(2)}) collective-permute-start(bf16[256,256]{1,0:T(8,128)(2,1)S(1)} %collective-permute-done.6.refs_3_), channel_id=1, source_target_pairs={{0,1},{1,0},{2,3},{3,2},{4,5},{5,4},{6,7},{7,6},{8,9},{9,8},{10,11... | collective-permute-start | bytes 393224 | tf_op jit(solution)/shard_map/ppermute | solution.py:353
  37.3 8.1 %copy-start = (bf16[1,1024,1024]{2,1,0:T(8,128)(2,1)S(1)}, bf16[1,1024,1024]{2,1,0:T(8,128)(2,1)}, u32[]{:S(2)}) copy-start(bf16[1,1024,1024]{2,1,0:T(8,128)(2,1)} %param.16) | copy-start | bytes 6291460
  37.3 8.1 %copy-start.1 = (bf16[1,1024,1024]{2,1,0:T(8,128)(2,1)S(1)}, bf16[1,1024,1024]{2,1,0:T(8,128)(2,1)}, u32[]{:S(2)}) copy-start(bf16[1,1024,1024]{2,1,0:T(8,128)(2,1)} %param.17) | copy-start | bytes 6291460
  38.9 14.6 %collective-permute-start.12 = (bf16[192,256]{1,0:T(8,128)(2,1)S(1)}, bf16[192,256]{1,0:T(8,128)(2,1)S(1)}, u32[]{:S(2)}, u32[]{:S(2)}) collective-permute-start(bf16[192,256]{1,0:T(8,128)(2,1)S(1)} %get-tuple-element.71), channel_id=1, source_target_pairs={{0,8},{1,9},{2,10},{3,11},{4,12},{5,13},{6,14},{7,15},{8,0},{9,1},... | collective-permute-start | bytes 294920 | tf_op jit(solution)/shard_map/ppermute | solution.py:353
  43.7 10.6 %collective-permute-start.15 = (bf16[192,512]{1,0:T(8,128)(2,1)S(1)}, bf16[192,512]{1,0:T(8,128)(2,1)S(1)}, u32[]{:S(2)}, u32[]{:S(2)}) collective-permute-start(bf16[192,512]{1,0:T(8,128)(2,1)S(1)} %get-tuple-element.76), channel_id=1, source_target_pairs={{0,12},{1,13},{2,14},{3,15},{4,8},{5,9},{6,10},{7,11},{8,4},{9,5},... | collective-permute-start | bytes 589832 | tf_op jit(solution)/shard_map/ppermute | solution.py:353
  44.4 12.3 %collective-permute-start.17 = (bf16[192,512]{1,0:T(8,128)(2,1)S(1)}, bf16[192,512]{1,0:T(8,128)(2,1)S(1)}, u32[]{:S(2)}, u32[]{:S(2)}) collective-permute-start(bf16[192,512]{1,0:T(8,128)(2,1)S(1)} %get-tuple-element.77), channel_id=1, source_target_pairs={{0,4},{1,5},{2,6},{3,7},{4,0},{5,1},{6,2},{7,3},{8,12},{9,13},{10,... | collective-permute-start | bytes 589832 | tf_op jit(solution)/shard_map/ppermute | solution.py:353
  53.6 5.2 %collective-permute-start.13 = (bf16[2,192,256]{2,1,0:T(8,128)(2,1)S(1)}, bf16[2,192,256]{2,1,0:T(8,128)(2,1)S(1)}, u32[]{:S(2)}, u32[]{:S(2)}) collective-permute-start(bf16[2,192,256]{2,1,0:T(8,128)(2,1)S(1)} %get-tuple-element.72), channel_id=1, source_target_pairs={{0,1},{1,0},{2,3},{3,2},{4,5},{5,4},{6,7},{7,6},{8,9},{9,8},{10,11... | collective-permute-start | bytes 589832 | tf_op jit(solution)/shard_map/ppermute | solution.py:353
  53.6 5.2 %collective-permute-start.24 = (bf16[192,256]{1,0:T(8,128)(2,1)S(1)}, bf16[192,256]{1,0:T(8,128)(2,1)S(1)}, u32[]{:S(2)}, u32[]{:S(2)}) collective-permute-start(bf16[192,256]{1,0:T(8,128)(2,1)S(1)} %collective-permute-done.12.refs_1_), channel_id=1, source_target_pairs={{0,2},{1,3},{2,0},{3,1},{4,6},{5,7},{6,4},{7,5},{8,10},{9,11},{10,... | collective-permute-start | bytes 294920 | tf_op jit(solution)/shard_map/ppermute | solution.py:353
  54.1 7.2 %collective-permute-start.25 = (bf16[192,256]{1,0:T(8,128)(2,1)S(1)}, bf16[192,256]{1,0:T(8,128)(2,1)S(1)}, u32[]{:S(2)}, u32[]{:S(2)}) collective-permute-start(bf16[192,256]{1,0:T(8,128)(2,1)S(1)} %collective-permute-done.12.refs_1_), channel_id=1, source_target_pairs={{0,1},{1,0},{2,3},{3,2},{4,5},{5,4},{6,7},{7,6},{8,9},{9,8},{10,11... | collective-permute-start | bytes 294920 | tf_op jit(solution)/shard_map/ppermute | solution.py:353
  54.3 4.6 %collective-permute-start.16 = (bf16[192,512]{1,0:T(8,128)(2,1)S(1)}, bf16[192,512]{1,0:T(8,128)(2,1)S(1)}, u32[]{:S(2)}, u32[]{:S(2)}) collective-permute-start(bf16[192,512]{1,0:T(8,128)(2,1)S(1)} %collective-permute-done.15.refs_1_), channel_id=1, source_target_pairs={{0,1},{1,0},{2,3},{3,2},{4,5},{5,4},{6,7},{7,6},{8,9},{9,8},{10,11... | collective-permute-start | bytes 589832 | tf_op jit(solution)/shard_map/ppermute | solution.py:353
  56.6 2.3 %collective-permute-start.18 = (bf16[192,512]{1,0:T(8,128)(2,1)S(1)}, bf16[192,512]{1,0:T(8,128)(2,1)S(1)}, u32[]{:S(2)}, u32[]{:S(2)}) collective-permute-start(bf16[192,512]{1,0:T(8,128)(2,1)S(1)} %collective-permute-done.17.refs_3_), channel_id=1, source_target_pairs={{0,1},{1,0},{2,3},{3,2},{4,5},{5,4},{6,7},{7,6},{8,9},{9,8},{10,11... | collective-permute-start | bytes 589832 | tf_op jit(solution)/shard_map/ppermute | solution.py:353
  58.8 2.5 %collective-permute-start.26 = (bf16[192,256]{1,0:T(8,128)(2,1)S(1)}, bf16[192,256]{1,0:T(8,128)(2,1)S(1)}, u32[]{:S(2)}, u32[]{:S(2)}) collective-permute-start(bf16[192,256]{1,0:T(8,128)(2,1)S(1)} %collective-permute-done.24.refs_2_), channel_id=1, source_target_pairs={{0,1},{1,0},{2,3},{3,2},{4,5},{5,4},{6,7},{7,6},{8,9},{9,8},{10,11... | collective-permute-start | bytes 294920 | tf_op jit(solution)/shard_map/ppermute | solution.py:353
  62.8 1.6 %collective-permute-start.27 = (bf16[2,192,256]{2,1,0:T(8,128)(2,1)S(1)}, bf16[2,192,256]{2,1,0:T(8,128)(2,1)S(1)}, u32[]{:S(2)}, u32[]{:S(2)}) collective-permute-start(bf16[2,192,256]{2,1,0:T(8,128)(2,1)S(1)} %get-tuple-element.86), channel_id=1, source_target_pairs={{0,1},{1,0},{2,3},{3,2},{4,5},{5,4},{6,7},{7,6},{8,9},{9,8},{10,11... | collective-permute-start | bytes 589832 | tf_op jit(solution)/shard_map/ppermute | solution.py:353
  63.4 10.8 %collective-permute-start.14 = (bf16[192,256]{1,0:T(8,128)(2,1)S(1)}, bf16[192,256]{1,0:T(8,128)(2,1)S(1)}, u32[]{:S(2)}, u32[]{:S(2)}) collective-permute-start(bf16[192,256]{1,0:T(8,128)(2,1)S(1)} %get-tuple-element.91), channel_id=1, source_target_pairs={{0,2},{1,3},{2,0},{3,1},{4,6},{5,7},{6,4},{7,5},{8,10},{9,11},{10,... | collective-permute-start | bytes 294920 | tf_op jit(solution)/shard_map/ppermute | solution.py:353
  63.9 1.7 %collective-permute-start.19 = (bf16[2,384,256]{2,1,0:T(8,128)(2,1)S(1)}, bf16[2,384,256]{2,1,0:T(8,128)(2,1)S(1)}, u32[]{:S(2)}, u32[]{:S(2)}) collective-permute-start(bf16[2,384,256]{2,1,0:T(8,128)(2,1)S(1)} %get-tuple-element.79), channel_id=1, source_target_pairs={{0,1},{1,0},{2,3},{3,2},{4,5},{5,4},{6,7},{7,6},{8,9},{9,8},{10,11... | collective-permute-start | bytes 1179656 | tf_op jit(solution)/shard_map/ppermute | solution.py:353
  64.5 7.8 %collective-permute-start.28 = (bf16[192,256]{1,0:T(8,128)(2,1)S(1)}, bf16[192,256]{1,0:T(8,128)(2,1)S(1)}, u32[]{:S(2)}, u32[]{:S(2)}) collective-permute-start(bf16[192,256]{1,0:T(8,128)(2,1)S(1)} %fusion.2), channel_id=1, source_target_pairs={{0,2},{1,3},{2,0},{3,1},{4,6},{5,7},{6,4},{7,5},{8,10},{9,11},{10,... | collective-permute-start | bytes 294920 | tf_op jit(solution)/shard_map/ppermute | solution.py:353
  65.8 13.6 %collective-permute-start.23 = (bf16[192,256]{1,0:T(8,128)(2,1)S(1)}, bf16[192,256]{1,0:T(8,128)(2,1)S(1)}, u32[]{:S(2)}, u32[]{:S(2)}) collective-permute-start(bf16[192,256]{1,0:T(8,128)(2,1)S(1)} %get-tuple-element.87), channel_id=1, source_target_pairs={{0,6},{1,7},{2,4},{3,5},{4,2},{5,3},{6,0},{7,1},{8,14},{9,15},{10,... | collective-permute-start | bytes 294920 | tf_op jit(solution)/shard_map/ppermute | solution.py:353
  67.4 12.0 %collective-permute-start.22 = (bf16[192,256]{1,0:T(8,128)(2,1)S(1)}, bf16[192,256]{1,0:T(8,128)(2,1)S(1)}, u32[]{:S(2)}, u32[]{:S(2)}) collective-permute-start(bf16[192,256]{1,0:T(8,128)(2,1)S(1)} %get-tuple-element.88), channel_id=1, source_target_pairs={{0,4},{1,5},{2,6},{3,7},{4,0},{5,1},{6,2},{7,3},{8,12},{9,13},{10,... | collective-permute-start | bytes 294920 | tf_op jit(solution)/shard_map/ppermute | solution.py:353
  68.9 8.1 %collective-permute-start.21 = (bf16[192,256]{1,0:T(8,128)(2,1)S(1)}, bf16[192,256]{1,0:T(8,128)(2,1)S(1)}, u32[]{:S(2)}, u32[]{:S(2)}) collective-permute-start(bf16[192,256]{1,0:T(8,128)(2,1)S(1)} %get-tuple-element.89), channel_id=1, source_target_pairs={{0,14},{1,15},{2,12},{3,13},{4,10},{5,11},{6,8},{7,9},{8,6},{9,7},... | collective-permute-start | bytes 294920 | tf_op jit(solution)/shard_map/ppermute | solution.py:353
  72.3 6.9 %collective-permute-start.20 = (bf16[192,256]{1,0:T(8,128)(2,1)S(1)}, bf16[192,256]{1,0:T(8,128)(2,1)S(1)}, u32[]{:S(2)}, u32[]{:S(2)}) collective-permute-start(bf16[192,256]{1,0:T(8,128)(2,1)S(1)} %get-tuple-element.90), channel_id=1, source_target_pairs={{0,12},{1,13},{2,14},{3,15},{4,8},{5,9},{6,10},{7,11},{8,4},{9,5},... | collective-permute-start | bytes 294920 | tf_op jit(solution)/shard_map/ppermute | solution.py:353
  74.2 10.0 %collective-permute-start.29 = (bf16[192,256]{1,0:T(8,128)(2,1)S(1)}, bf16[192,256]{1,0:T(8,128)(2,1)S(1)}, u32[]{:S(2)}, u32[]{:S(2)}) collective-permute-start(bf16[192,256]{1,0:T(8,128)(2,1)S(1)} %fusion.1), channel_id=1, source_target_pairs={{0,8},{1,9},{2,10},{3,11},{4,12},{5,13},{6,14},{7,15},{8,0},{9,1},... | collective-permute-start | bytes 294920 | tf_op jit(solution)/shard_map/ppermute | solution.py:353

commit v6 on v5

--- a/solution.py
+++ b/solution.py
@@ -244,21 +244,23 @@
     )(ids, state, dispatch, router, choice)
 
 
-def expert_kernel(order, blocks, *refs):
-    cuts = len(order)
-    ids, pieces = refs[0], refs[1 : 1 + blocks * cuts]
-    expand, shrink, keep, give, rows_here, hidden = refs[1 + blocks * cuts :]
-    count, width = pieces[0].shape
-    for block in range(blocks):
-        for i in range(cuts):
-            rows_here[i, block * count : (block + 1) * count] = pieces[block * cuts + i][...]
+def expert_kernel(orders, *refs):
+    blocks, at = [], 1
+    for order in orders:
+        blocks.append(refs[at : at + len(order)])
+        at += len(order)
+    ids = refs[0]
+    expand, shrink, keep, give, rows_here, hidden = refs[at:]
+    count = blocks[0][0].shape[0]
+    for block, (order, pieces) in enumerate(zip(orders, blocks)):
+        for index, piece in zip(order, pieces):
+            width = piece.shape[1]
+            part = pl.ds(pl.multiple_of(((ids[1] & (len(order) - 1)) ^ index) * width, width), width)
+            rows_here[block * count : (block + 1) * count, part] = piece[...]
     units = expand.shape[1]
     tile = min(TILE, units)
     for at in range(0, units, tile):
-        total = jnp.zeros((hidden.shape[0], tile), F32)
-        for i, index in enumerate(order):
-            part = pl.ds(pl.multiple_of(((ids[1] & (cuts - 1)) ^ index) * width, width), width)
-            total += dot(rows_here[i], expand[part, at : at + tile])
+        total = dot(rows_here[...], expand[:, at : at + tile])
         hidden[:, at : at + tile] = jnp.maximum(total, 0.0).astype(BF16)
     width = keep.shape[2]
     for j in range(keep.shape[0]):
@@ -269,21 +271,20 @@
         keep[j] = dot(hidden[...], shrink[:, pl.ds(at, width)])
 
 
-def run_expert(ids, order, blocks, expand, shrink, parts):
+def run_expert(ids, orders, blocks, expand, shrink, parts):
     pieces = [piece for block in blocks for piece in block]
-    count, piece_width = pieces[0].shape
-    rows = count * len(blocks)
+    rows = pieces[0].shape[0] * len(blocks)
     features, units = expand.shape
     width = features // (2 * parts)
     return pl.pallas_call(
-        functools.partial(expert_kernel, tuple(order), len(blocks)),
+        functools.partial(expert_kernel, tuple(map(tuple, orders))),
         in_specs=[SCALARS] + [WHOLE] * (2 + len(pieces)),
         out_specs=[WHOLE] * 2,
         out_shape=[
             jax.ShapeDtypeStruct((parts, rows, width), F32),
             jax.ShapeDtypeStruct((parts, rows, width), BF16),
         ],
-        scratch_shapes=[pltpu.VMEM((len(order), rows, piece_width), BF16), pltpu.VMEM((rows, units), BF16)],
+        scratch_shapes=[pltpu.VMEM((rows, features), BF16), pltpu.VMEM((rows, units), BF16)],
         compiler_params=PARAMS,
         cost_estimate=CHEAP,
         name="expert",
@@ -376,17 +377,19 @@
             answer = attend(after(asked[k], previous), source, token_count)
             backs[k] = hop(answer, k, 0)
             previous = answer
+        swap_after = backs.get(1, own)
         context = pick(ids, source_owner, [own] + [backs[k] for k in range(1, groups)])
     else:
         asked = lax.all_gather(queries, "expert", axis=0, tiled=True)
         previous = attend(asked, source, token_count)
+        swap_after = previous
         context = lax.dynamic_slice_in_dim(spread(previous), source_owner[0] * token_count, token_count, 0)
 
     choice, dispatch, first, second = route(ids, after(expert_choice, previous), experts, len(steps), capacity)
     weights, order = [output_weight], [0]
     for bit in bits:
         if bit == 1:
-            weights = [after(weight, context) for weight in weights]
+            weights = [after(weight, swap_after) for weight in weights]
         weights = weights + [hop(weight, 0, bit) for weight in weights]
         order = order + [index ^ bit for index in order]
     contexts = [context]
@@ -406,42 +409,47 @@
     def sum_cores(keep, give):
         return keep + hop(give, 0, 1).astype(F32)
 
-    def send_home(k, summed):
-        if k == relayed:
+    def send_home(k, summed, earlier=None):
+        if k > 1:
             total = summed[0]
             for j in range(1, pairs):
-                total += hop(summed[j].astype(BF16), 0, 2 * j).astype(F32)
-            return [hop(total.astype(BF16), k, 0)]
+                other = hop(summed[j].astype(BF16), 0, 2 * j)
+                total += (other if earlier is None else after(other, earlier)).astype(F32)
+            return [total.astype(BF16)]
         parts = [summed[j].astype(BF16) for j in range(pairs)]
         return [hop(part, k, 2 * j) if direct else hop(spread(part), 0, 2 * j) for j, part in enumerate(parts)]
 
     home = {}
     if direct:
         arrived = {k: hop(rows, k, 0) for k, rows in zip(sends, leaving)}
-        keep, give = expert(ids, [0, 1], [[own_a, own_b]])
+        keep, give = expert(ids, [[0, 1]], [[own_a, own_b]])
+        turn_ids = after(ids, give)
+        used = {k: after(rows, give) for k, rows in arrived.items()}
         if sends:
             give = after(give, arrived[sends[0]])
         home[0] = send_home(0, sum_cores(keep, give))
-        turn_ids = after(ids, give)
-        if rest:
-            mine = [arrived[k] for k in rest]
-            keep, give = expert(turn_ids, [0, 1], [[rows, hop(rows, 0, 1)] for rows in mine])
-            turn_ids = after(ids, give)
-            summed = sum_cores(keep, give)
-            for i, k in enumerate(rest):
-                home[k] = send_home(k, summed[:, i * slots : (i + 1) * slots])
-        if relayed >= 0:
-            pieces, places = [arrived[relayed]], [0]
-            for bit in bits:
+        order = [*rest, relayed] if relayed >= 0 else rest
+        blocks, orders = [], []
+        for k in order:
+            pieces, places = [used[k]], [0]
+            for bit in bits if k == relayed else [1]:
                 pieces = pieces + [hop(piece, 0, bit) for piece in pieces]
                 places = places + [index ^ bit for index in places]
-            keep, give = expert(turn_ids, places, [pieces])
-            home[relayed] = send_home(relayed, sum_cores(keep, give))
-        order = [0] + rest + ([relayed] if relayed >= 0 else [])
+            blocks.append(pieces)
+            orders.append(places)
+        if order:
+            summed = sum_cores(*expert(turn_ids, orders, blocks))
+            earlier = None
+            for k in sorted(order, reverse=True):
+                i = order.index(k)
+                home[k] = send_home(k, summed[:, i * slots : (i + 1) * slots], earlier)
+                if k > 1:
+                    earlier = home[k][0]
+                    home[k] = [hop(earlier, k, 0)]
+        order = [0] + sorted(order, key=lambda k: (k > 1, -k))
     else:
         mine = spread(leaving[0])
-        keep, give = expert(ids, [0, 1], [[mine, hop(mine, 0, 1)]])
-        home[0] = send_home(0, sum_cores(keep, give))
+        home[0] = send_home(0, sum_cores(*expert(ids, [[0, 1]], [[mine, hop(mine, 0, 1)]])))
         order = [0]
     results = columns
     for k in order:

time: 85.3 us -> 90.6 us (1.062)
  waiting for transfers between devices: 33.7 us -> 42.9 us
  starting transfers between devices: 33.4 us -> 30.2 us
    ppermute x30 -> x29, waiting for transfers between devices: 33.7 us -> 42.9 us  [hop(): return lax.ppermute(value, ('expert', 'mp'), moves)]
    ppermute x30 -> x29, starting transfers between devices: 33.4 us -> 30.2 us  [hop(): return lax.ppermute(value, ('expert', 'mp'), moves)]
    pallas_call x3 -> x2, Pallas kernels: 5.45 us -> 4.8 us  [run_expert(): pl.pallas_call(functools.partial(expert_kernel, tuple(map(tuple, orders))...]
  transfers between devices with their start and end apart: 30 -> 29, of which waited for: 13 -> 14; matrix products, arithmetic and copies ran while one was open for 0% -> 0% of each run, Pallas kernels for 15% -> 11%
where the time goes in v6:
time: 90.6 us; the launch traced here: 90.5 us
  waiting for transfers between devices  42.9 us (47%)
  starting transfers between devices  30.2 us (33%)
  Pallas kernels  16 us (18%)
  between operations  0.91 us (1%)
    ppermute x29, waiting for transfers between devices, hop(): return lax.ppermute(value, ('expert', 'mp'), moves)  42.9 us
    ppermute x29, starting transfers between devices, hop(): return lax.ppermute(value, ('expert', 'mp'), moves)  30.2 us
    pallas_call x2, Pallas kernels, run_expert(): pl.pallas_call(functools.partial(expert_kernel, tuple(map(tuple, orders))...  4.8 us
    pallas_call x4, Pallas kernels, attend(): pl.pallas_call(attend_kernel, in_specs=[WHOLE] * 2, out_specs=WHOLE, out_...  3.1 us
    pallas_call x1, Pallas kernels, ask(): pl.pallas_call(query_kernel, in_specs=[pl.BlockSpec(memory_space=pltpu.HB...  1.81 us
  transfers between devices with their start and end apart: 29, of which 14 were waited for; matrix products, arithmetic and copies ran while one was open for 0% of the time, Pallas kernels for 11%

profile of v6, /device:TPU:0, one launch (start us, length us, event | category | flops | bytes accessed | tf_op | source)
XLA Modules:
  0.0 90.5 jit_solution(12919150810380499229)
XLA Ops:
  0.0 2.9 %collective-permute-start.9 = (bf16[256,1024]{1,0:T(8,128)(2,1)}, bf16[256,1024]{1,0:T(8,128)(2,1)S(1)}, u32[]{:S(2)}, u32[]{:S(2)}) collective-permute-start(bf16[256,1024]{1,0:T(8,128)(2,1)} %refs_6_), channel_id=1, source_target_pairs={{0,2},{1,3},{2,0},{3,1},{4,6},{5,7},{6,4},{7,5},{8,10},{9,11},{10,... | collective-permute-start | bytes 1572872 | tf_op jit(solution)/shard_map/ppermute | solution.py:354
  2.9 0.1 pad_add_fusion.ids.refs_0_
  3.0 1.8 %query.1 = (bf16[256,256]{1,0:T(8,128)(2,1)S(1)}, bf16[2,512,256]{2,1,0:T(8,128)(2,1)S(1)}) custom-call(bf16[256,1024]{1,0:T(8,128)(2,1)} %refs_1_.1, bf16[1024,256]{1,0:T(8,128)(2,1)} %weight.1, bf16[2,512,256]{2,1,0:T(8,128)(2,1)} %bitcast.37), custom_call_target="tpu_custom_call" | custom-call | tf_op jit(solution)/shard_map/query/pallas_call | solution.py:60
  4.8 0.0 copy-start.3
  4.8 1.6 %collective-permute-start = (bf16[256,256]{1,0:T(8,128)(2,1)S(1)}, bf16[256,256]{1,0:T(8,128)(2,1)S(1)}, u32[]{:S(2)}, u32[]{:S(2)}) collective-permute-start(bf16[256,256]{1,0:T(8,128)(2,1)S(1)} %get-tuple-element.48.queries), channel_id=1, source_target_pairs={{0,4},{1,5},{2,6},{3,7},{4,0},{5,1},{6,2},{7,3},{8,12},{9,13},{10,... | collective-permute-start | bytes 393224 | tf_op jit(solution)/shard_map/ppermute | solution.py:354
  6.5 2.6 %collective-permute-start.2 = (bf16[256,256]{1,0:T(8,128)(2,1)S(1)}, bf16[256,256]{1,0:T(8,128)(2,1)S(1)}, u32[]{:S(2)}, u32[]{:S(2)}) collective-permute-start(bf16[256,256]{1,0:T(8,128)(2,1)S(1)} %get-tuple-element.48.queries), channel_id=1, source_target_pairs={{0,8},{1,9},{2,10},{3,11},{4,12},{5,13},{6,14},{7,15},{8,0},{9,1},... | collective-permute-start | bytes 393224 | tf_op jit(solution)/shard_map/ppermute | solution.py:354
  9.1 0.8 attend.4.refs_0_
  9.9 1.7 %collective-permute-done.queries = bf16[256,256]{1,0:T(8,128)(2,1)S(1)} collective-permute-done((bf16[256,256]{1,0:T(8,128)(2,1)S(1)}, bf16[256,256]{1,0:T(8,128)(2,1)S(1)}, u32[]{:S(2)}, u32[]{:S(2)}) %collective-permute-start) | collective-permute-done | bytes 131104 | tf_op jit(solution)/shard_map/ppermute | solution.py:354
  11.6 0.8 attend.5
  12.4 0.0 copy-start.5
  12.4 0.0 copy-start.2
  12.4 0.4 collective-permute-start.1
  12.8 2.2 %collective-permute-done.2.queries = bf16[256,256]{1,0:T(8,128)(2,1)S(1)} collective-permute-done((bf16[256,256]{1,0:T(8,128)(2,1)S(1)}, bf16[256,256]{1,0:T(8,128)(2,1)S(1)}, u32[]{:S(2)}, u32[]{:S(2)}) %collective-permute-start.2) | collective-permute-done | bytes 131104 | tf_op jit(solution)/shard_map/ppermute | solution.py:354
  15.0 0.2 collective-permute-start.4
  15.3 2.2 %collective-permute-done.1.refs_1_ = bf16[256,256]{1,0:T(8,128)(2,1)S(1)} collective-permute-done((bf16[256,256]{1,0:T(8,128)(2,1)S(1)}, bf16[256,256]{1,0:T(8,128)(2,1)S(1)}, u32[]{:S(2)}, u32[]{:S(2)}) %collective-permute-start.1) | collective-permute-done | bytes 131104 | tf_op jit(solution)/shard_map/ppermute | solution.py:354
  17.5 0.0 collective-permute-done.9.refs_7_
  17.5 0.5 collective-permute-start.11
  18.0 0.8 attend.6
  18.8 2.9 %collective-permute-start.3 = (bf16[256,256]{1,0:T(8,128)(2,1)S(1)}, bf16[256,256]{1,0:T(8,128)(2,1)S(1)}, u32[]{:S(2)}, u32[]{:S(2)}) collective-permute-start(bf16[256,256]{1,0:T(8,128)(2,1)S(1)} %attend.6), channel_id=1, source_target_pairs={{0,8},{1,9},{2,10},{3,11},{4,12},{5,13},{6,14},{7,15},{8,0},{9,1},... | collective-permute-start | bytes 393224 | tf_op jit(solution)/shard_map/ppermute | solution.py:354
  21.7 0.8 attend.7
  22.5 1.4 %collective-permute-start.5 = (bf16[256,256]{1,0:T(8,128)(2,1)S(1)}, bf16[256,256]{1,0:T(8,128)(2,1)S(1)}, u32[]{:S(2)}, u32[]{:S(2)}) collective-permute-start(bf16[256,256]{1,0:T(8,128)(2,1)S(1)} %attend.7), channel_id=1, source_target_pairs={{0,12},{1,13},{2,14},{3,15},{4,8},{5,9},{6,10},{7,11},{8,4},{9,5},... | collective-permute-start | bytes 393224 | tf_op jit(solution)/shard_map/ppermute | solution.py:354
  24.5 7.2 %collective-permute-done.3.refs_2_ = bf16[256,256]{1,0:T(8,128)(2,1)S(1)} collective-permute-done((bf16[256,256]{1,0:T(8,128)(2,1)S(1)}, bf16[256,256]{1,0:T(8,128)(2,1)S(1)}, u32[]{:S(2)}, u32[]{:S(2)}) %collective-permute-start.3) | collective-permute-done | bytes 131104 | tf_op jit(solution)/shard_map/ppermute | solution.py:354
  31.7 0.6 pick.1.refs_2_
  32.3 0.6 collective-permute-start.6
  32.9 1.5 %route.1 = (s32[256,2]{1,0:T(8,128)S(1)}, bf16[192,256]{1,0:T(8,128)(2,1)S(1)}, bf16[192,256]{1,0:T(8,128)(2,1)S(1)}, bf16[192,256]{1,0:T(8,128)(2,1)S(1)}, bf16...) custom-call(s32[2]{0:T(128)S(1)} %pad_add_fusion.ids.refs_0_, ...), custom_call_target="tpu_custom_call" | custom-call | tf_op jit(solution)/shard_map/route/pallas_call | solution.py:171
  34.4 0.1 collective-permute-start.7
  34.5 2.8 %collective-permute-done.6.refs_3_ = bf16[256,256]{1,0:T(8,128)(2,1)S(1)} collective-permute-done((bf16[256,256]{1,0:T(8,128)(2,1)S(1)}, bf16[256,256]{1,0:T(8,128)(2,1)S(1)}, u32[]{:S(2)}, u32[]{:S(2)}) %collective-permute-start.6) | collective-permute-done | bytes 131104 | tf_op jit(solution)/shard_map/ppermute | solution.py:354
  37.3 0.0 collective-permute-start.8
  37.3 0.0 collective-permute-done.7.refs_4_
  37.3 1.3 %collective-permute-done.8.refs_5_ = bf16[256,256]{1,0:T(8,128)(2,1)S(1)} collective-permute-done((bf16[256,256]{1,0:T(8,128)(2,1)S(1)}, bf16[256,256]{1,0:T(8,128)(2,1)S(1)}, u32[]{:S(2)}, u32[]{:S(2)}) %collective-permute-start.8) | collective-permute-done | bytes 131104 | tf_op jit(solution)/shard_map/ppermute | solution.py:354
  38.7 0.0 copy-start
  38.7 0.0 copy-start.1
  38.7 1.6 %state.1 = (bf16[256,1024]{1,0:T(8,128)(2,1)S(1)}, bf16[192,256]{1,0:T(8,128)(2,1)S(1)}, bf16[192,512]{1,0:T(8,128)(2,1)S(1)}, bf16[192,512]{1,0:T(8,128)(2,1)S(1)}) custom-call(s32[2]{0:T(128)S(1)} %pad_add_fusion.ids.refs_0_, bf16[256,1024]{1,0:T(8,128)(2,1)S(1)} %copy-done.2, bf16[256,256]{1,0:T(8,128)(2,1)S(1)} %pick.1.refs_2_, ...), custom_call_target="tpu_custom_call" | custom-call | tf_op jit(solution)/shard_map/state/pallas_call | solution.py:201
  40.3 3.4 %collective-permute-start.17 = (bf16[192,512]{1,0:T(8,128)(2,1)S(1)}, bf16[192,512]{1,0:T(8,128)(2,1)S(1)}, u32[]{:S(2)}, u32[]{:S(2)}) collective-permute-start(bf16[192,512]{1,0:T(8,128)(2,1)S(1)} %get-tuple-element.79), channel_id=1, source_target_pairs={{0,4},{1,5},{2,6},{3,7},{4,0},{5,1},{6,2},{7,3},{8,12},{9,13},{10,... | collective-permute-start | bytes 589832 | tf_op jit(solution)/shard_map/ppermute | solution.py:354
  43.7 3.4 %collective-permute-start.15 = (bf16[192,512]{1,0:T(8,128)(2,1)S(1)}, bf16[192,512]{1,0:T(8,128)(2,1)S(1)}, u32[]{:S(2)}, u32[]{:S(2)}) collective-permute-start(bf16[192,512]{1,0:T(8,128)(2,1)S(1)} %get-tuple-element.77), channel_id=1, source_target_pairs={{0,12},{1,13},{2,14},{3,15},{4,8},{5,9},{6,10},{7,11},{8,4},{9,5},... | collective-permute-start | bytes 589832 | tf_op jit(solution)/shard_map/ppermute | solution.py:354
  47.1 1.0 %home.1 = (bf16[192,512]{1,0:T(8,128)(2,1)S(1)}, bf16[192,512]{1,0:T(8,128)(2,1)S(1)}, f32[256,2]{1,0:T(8,128)S(1)}, f32[256,256]{1,0:T(8,128)S(1)}) custom-call(s32[2]{0:T(128)S(1)} %pad_add_fusion.ids.refs_0_, bf16[256,1024]{1,0:T(8,128)(2,1)S(1)} %get-tuple-element.62.state, bf16[192,256]{1,0:T(8,128)(2,1)S(1)} %get-tuple-element.55.dispatch, ...), custom_call_target="tpu_custom_call" | custom-call | tf_op jit(solution)/shard_map/home/pallas_call | solution.py:231
  48.2 1.6 %expert.2 = (f32[2,192,256]{2,1,0:T(8,128)S(1)}, bf16[2,192,256]{2,1,0:T(8,128)(2,1)S(1)}) custom-call(s32[2]{0:T(128)S(1)} %pad_add_fusion.ids.refs_0_, bf16[192,512]{1,0:T(8,128)(2,1)S(1)} %get-tuple-element.68.refs_1_, bf16[192,512]{1,0:T(8,128)(2,1)S(1)} %get-tuple-element.69.refs_2_, bf16[1024,1024]{1,0:T(8,128)(2,1)S(1)} %bitcast.31, ...), custom_call_target="tpu_custom_call" | custom-call | tf_op jit(solution)/shard_map/expert/pallas_call | solution.py:279
  49.7 9.6 %collective-permute-done.12.refs_5_ = bf16[192,256]{1,0:T(8,128)(2,1)S(1)} collective-permute-done((bf16[192,256]{1,0:T(8,128)(2,1)S(1)}, bf16[192,256]{1,0:T(8,128)(2,1)S(1)}, u32[]{:S(2)}, u32[]{:S(2)}) %collective-permute-start.12) | collective-permute-done | bytes 98336 | tf_op jit(solution)/shard_map/ppermute | solution.py:354
  59.4 0.5 collective-permute-start.19
  59.9 0.5 collective-permute-start.18
  60.4 0.1 collective-permute-start.20
  60.5 3.5 %collective-permute-done.19.refs_6_ = bf16[192,256]{1,0:T(8,128)(2,1)S(1)} collective-permute-done((bf16[192,256]{1,0:T(8,128)(2,1)S(1)}, bf16[192,256]{1,0:T(8,128)(2,1)S(1)}, u32[]{:S(2)}, u32[]{:S(2)}) %collective-permute-start.19) | collective-permute-done | bytes 98336 | tf_op jit(solution)/shard_map/ppermute | solution.py:354
  64.0 1.3 %collective-permute-done.21.refs_8_ = bf16[192,256]{1,0:T(8,128)(2,1)S(1)} collective-permute-done((bf16[192,256]{1,0:T(8,128)(2,1)S(1)}, bf16[192,256]{1,0:T(8,128)(2,1)S(1)}, u32[]{:S(2)}, u32[]{:S(2)}) %collective-permute-start.21) | collective-permute-done | bytes 98336 | tf_op jit(solution)/shard_map/ppermute | solution.py:354
  65.3 3.2 %expert.3 = (f32[2,576,256]{2,1,0:T(8,128)S(1)}, bf16[2,576,256]{2,1,0:T(8,128)(2,1)S(1)}) custom-call(s32[2]{0:T(128)S(1)} %pad_add_fusion.ids.refs_0_, bf16[192,512]{1,0:T(8,128)(2,1)S(1)} %collective-permute-done.15.refs_1_, bf16[192,512]{1,0:T(8,128)(2,1)S(1)} %collective-permute-done.16.refs_2_, bf16[192,512]{1,0:T(8,128)(2,1)S(1)} %collective-permute-done.17.refs_3_, ...), custom_call_target="tpu_custom_call" | custom-call | tf_op jit(solution)/shard_map/expert/pallas_call | solution.py:279
  68.5 0.2 collective-permute-start.22
  68.8 0.4 collective-permute-start.13
  69.1 1.8 %collective-permute-done.13 = bf16[2,192,256]{2,1,0:T(8,128)(2,1)S(1)} collective-permute-done((bf16[2,192,256]{2,1,0:T(8,128)(2,1)S(1)}, bf16[2,192,256]{2,1,0:T(8,128)(2,1)S(1)}, u32[]{:S(2)}, u32[]{:S(2)}) %collective-permute-start.13) | collective-permute-done | bytes 196640 | tf_op jit(solution)/shard_map/ppermute | solution.py:354
  70.9 0.1 add_convert_fusion
  71.0 0.2 fusion.4
  71.2 0.6 collective-permute-start.25
  71.8 1.6 %collective-permute-start.14 = (bf16[192,256]{1,0:T(8,128)(2,1)S(1)}, bf16[192,256]{1,0:T(8,128)(2,1)S(1)}, u32[]{:S(2)}, u32[]{:S(2)}) collective-permute-start(bf16[192,256]{1,0:T(8,128)(2,1)S(1)} %get-tuple-element.95), channel_id=1, source_target_pairs={{0,2},{1,3},{2,0},{3,1},{4,6},{5,7},{6,4},{7,5},{8,10},{9,11},{10,... | collective-permute-start | bytes 294920 | tf_op jit(solution)/shard_map/ppermute | solution.py:354
  73.4 0.5 collective-permute-start.27
  73.9 0.8 collective-permute-start.24
  74.7 2.2 %collective-permute-start.23 = (bf16[192,256]{1,0:T(8,128)(2,1)S(1)}, bf16[192,256]{1,0:T(8,128)(2,1)S(1)}, u32[]{:S(2)}, u32[]{:S(2)}) collective-permute-start(bf16[192,256]{1,0:T(8,128)(2,1)S(1)} %get-tuple-element.94), channel_id=1, source_target_pairs={{0,4},{1,5},{2,6},{3,7},{4,0},{5,1},{6,2},{7,3},{8,12},{9,13},{10,... | collective-permute-start | bytes 294920 | tf_op jit(solution)/shard_map/ppermute | solution.py:354
  76.9 1.1 %collective-permute-done.25 = bf16[192,256]{1,0:T(8,128)(2,1)S(1)} collective-permute-done((bf16[192,256]{1,0:T(8,128)(2,1)S(1)}, bf16[192,256]{1,0:T(8,128)(2,1)S(1)}, u32[]{:S(2)}, u32[]{:S(2)}) %collective-permute-start.25) | collective-permute-done | bytes 98336 | tf_op jit(solution)/shard_map/ppermute | solution.py:354
  78.0 2.7 %collective-permute-start.26 = (bf16[192,256]{1,0:T(8,128)(2,1)S(1)}, bf16[192,256]{1,0:T(8,128)(2,1)S(1)}, u32[]{:S(2)}, u32[]{:S(2)}) collective-permute-start(bf16[192,256]{1,0:T(8,128)(2,1)S(1)} %fusion.3), channel_id=1, source_target_pairs={{0,12},{1,13},{2,14},{3,15},{4,8},{5,9},{6,10},{7,11},{8,4},{9,5},... | collective-permute-start | bytes 294920 | tf_op jit(solution)/shard_map/ppermute | solution.py:354
  80.7 1.8 %collective-permute-done.27 = bf16[192,256]{1,0:T(8,128)(2,1)S(1)} collective-permute-done((bf16[192,256]{1,0:T(8,128)(2,1)S(1)}, bf16[192,256]{1,0:T(8,128)(2,1)S(1)}, u32[]{:S(2)}, u32[]{:S(2)}) %collective-permute-start.27) | collective-permute-done | bytes 98336 | tf_op jit(solution)/shard_map/ppermute | solution.py:354
  82.5 0.1 collective-permute-start.28
  82.6 0.2 combine.4.base
  82.8 0.2 combine.5.base
  83.1 1.4 %collective-permute-done.26.refs_0_ = bf16[192,256]{1,0:T(8,128)(2,1)S(1)} collective-permute-done((bf16[192,256]{1,0:T(8,128)(2,1)S(1)}, bf16[192,256]{1,0:T(8,128)(2,1)S(1)}, u32[]{:S(2)}, u32[]{:S(2)}) %collective-permute-start.26) | collective-permute-done | bytes 98336 | tf_op jit(solution)/shard_map/ppermute | solution.py:354
  84.5 0.2 combine.6.base
  84.7 4.9 %collective-permute-done.28.refs_0_ = bf16[192,256]{1,0:T(8,128)(2,1)S(1)} collective-permute-done((bf16[192,256]{1,0:T(8,128)(2,1)S(1)}, bf16[192,256]{1,0:T(8,128)(2,1)S(1)}, u32[]{:S(2)}, u32[]{:S(2)}) %collective-permute-start.28) | collective-permute-done | bytes 98336 | tf_op jit(solution)/shard_map/ppermute | solution.py:354
  89.6 0.9 combine.7
  (28 shorter events, 0.1 us)
Async XLA Ops:
  0.0 17.5 %collective-permute-start.9 = (bf16[256,1024]{1,0:T(8,128)(2,1)}, bf16[256,1024]{1,0:T(8,128)(2,1)S(1)}, u32[]{:S(2)}, u32[]{:S(2)}) collective-permute-start(bf16[256,1024]{1,0:T(8,128)(2,1)} %refs_6_), channel_id=1, source_target_pairs={{0,2},{1,3},{2,0},{3,1},{4,6},{5,7},{6,4},{7,5},{8,10},{9,11},{10,... | collective-permute-start | bytes 1572872 | tf_op jit(solution)/shard_map/ppermute | solution.py:354
  4.8 12.7 %copy-start.3 = (bf16[256,1024]{1,0:T(8,128)(2,1)S(1)}, bf16[256,1024]{1,0:T(8,128)(2,1)}, u32[]{:S(2)}) copy-start(bf16[256,1024]{1,0:T(8,128)(2,1)} %refs_6_) | copy-start | bytes 1572868
  4.8 6.7 %collective-permute-start = (bf16[256,256]{1,0:T(8,128)(2,1)S(1)}, bf16[256,256]{1,0:T(8,128)(2,1)S(1)}, u32[]{:S(2)}, u32[]{:S(2)}) collective-permute-start(bf16[256,256]{1,0:T(8,128)(2,1)S(1)} %get-tuple-element.48.queries), channel_id=1, source_target_pairs={{0,4},{1,5},{2,6},{3,7},{4,0},{5,1},{6,2},{7,3},{8,12},{9,13},{10,... | collective-permute-start | bytes 393224 | tf_op jit(solution)/shard_map/ppermute | solution.py:354
  6.5 8.5 %collective-permute-start.2 = (bf16[256,256]{1,0:T(8,128)(2,1)S(1)}, bf16[256,256]{1,0:T(8,128)(2,1)S(1)}, u32[]{:S(2)}, u32[]{:S(2)}) collective-permute-start(bf16[256,256]{1,0:T(8,128)(2,1)S(1)} %get-tuple-element.48.queries), channel_id=1, source_target_pairs={{0,8},{1,9},{2,10},{3,11},{4,12},{5,13},{6,14},{7,15},{8,0},{9,1},... | collective-permute-start | bytes 393224 | tf_op jit(solution)/shard_map/ppermute | solution.py:354
  12.4 20.5 %copy-start.5 = (s32[256,2]{0,1:T(2,128)S(1)}, s32[256,2]{0,1:T(2,128)}, u32[]{:S(2)}) copy-start(s32[256,2]{0,1:T(2,128)} %param.15) | copy-start | bytes 6148
  12.4 26.3 %copy-start.2 = (bf16[256,1024]{1,0:T(8,128)(2,1)S(1)}, bf16[256,1024]{1,0:T(8,128)(2,1)}, u32[]{:S(2)}) copy-start(bf16[256,1024]{1,0:T(8,128)(2,1)} %refs_1_.1) | copy-start | bytes 1572868
  12.4 5.1 %collective-permute-start.1 = (bf16[256,256]{1,0:T(8,128)(2,1)S(1)}, bf16[256,256]{1,0:T(8,128)(2,1)S(1)}, u32[]{:S(2)}, u32[]{:S(2)}) collective-permute-start(bf16[256,256]{1,0:T(8,128)(2,1)S(1)} %attend.5), channel_id=1, source_target_pairs={{0,4},{1,5},{2,6},{3,7},{4,0},{5,1},{6,2},{7,3},{8,12},{9,13},{10,... | collective-permute-start | bytes 393224 | tf_op jit(solution)/shard_map/ppermute | solution.py:354
  15.0 6.7 %collective-permute-start.4 = (bf16[256,256]{1,0:T(8,128)(2,1)S(1)}, bf16[256,256]{1,0:T(8,128)(2,1)S(1)}, u32[]{:S(2)}, u32[]{:S(2)}) collective-permute-start(bf16[256,256]{1,0:T(8,128)(2,1)S(1)} %collective-permute-done.2.queries), channel_id=1, source_target_pairs={{0,4},{1,5},{2,6},{3,7},{4,0},{5,1},{6,2},{7,3},{8,12},{9,13},{10,... | collective-permute-start | bytes 393224 | tf_op jit(solution)/shard_map/ppermute | solution.py:354
  17.5 21.2 %collective-permute-start.10 = (bf16[256,1024]{1,0:T(8,128)(2,1)S(1)}, bf16[256,1024]{1,0:T(8,128)(2,1)S(1)}, u32[]{:S(2)}, u32[]{:S(2)}) collective-permute-start(bf16[256,1024]{1,0:T(8,128)(2,1)S(1)} %copy-done.3), channel_id=1, source_target_pairs={{0,1},{1,0},{2,3},{3,2},{4,5},{5,4},{6,7},{7,6},{8,9},{9,8},{10,11... | collective-permute-start | bytes 1572872 | tf_op jit(solution)/shard_map/ppermute | solution.py:354
  17.5 21.2 %collective-permute-start.11 = (bf16[256,1024]{1,0:T(8,128)(2,1)S(1)}, bf16[256,1024]{1,0:T(8,128)(2,1)S(1)}, u32[]{:S(2)}, u32[]{:S(2)}) collective-permute-start(bf16[256,1024]{1,0:T(8,128)(2,1)S(1)} %collective-permute-done.9.refs_7_), channel_id=1, source_target_pairs={{0,1},{1,0},{2,3},{3,2},{4,5},{5,4},{6,7},{7,6},{8,9},{9,8},{10,11... | collective-permute-start | bytes 1572872 | tf_op jit(solution)/shard_map/ppermute | solution.py:354
  18.8 12.9 %collective-permute-start.3 = (bf16[256,256]{1,0:T(8,128)(2,1)S(1)}, bf16[256,256]{1,0:T(8,128)(2,1)S(1)}, u32[]{:S(2)}, u32[]{:S(2)}) collective-permute-start(bf16[256,256]{1,0:T(8,128)(2,1)S(1)} %attend.6), channel_id=1, source_target_pairs={{0,8},{1,9},{2,10},{3,11},{4,12},{5,13},{6,14},{7,15},{8,0},{9,1},... | collective-permute-start | bytes 393224 | tf_op jit(solution)/shard_map/ppermute | solution.py:354
  22.5 9.2 %collective-permute-start.5 = (bf16[256,256]{1,0:T(8,128)(2,1)S(1)}, bf16[256,256]{1,0:T(8,128)(2,1)S(1)}, u32[]{:S(2)}, u32[]{:S(2)}) collective-permute-start(bf16[256,256]{1,0:T(8,128)(2,1)S(1)} %attend.7), channel_id=1, source_target_pairs={{0,12},{1,13},{2,14},{3,15},{4,8},{5,9},{6,10},{7,11},{8,4},{9,5},... | collective-permute-start | bytes 393224 | tf_op jit(solution)/shard_map/ppermute | solution.py:354
  31.7 15.4 %copy-start.4 = (bf16[1024,4]{0,1:T(4,128)(2,1)S(1)}, bf16[1024,4]{0,1:T(4,128)(2,1)}, u32[]{:S(2)}) copy-start(bf16[1024,4]{0,1:T(4,128)(2,1)} %param.14) | copy-start | bytes 24580
  32.3 5.0 %collective-permute-start.6 = (bf16[256,256]{1,0:T(8,128)(2,1)S(1)}, bf16[256,256]{1,0:T(8,128)(2,1)S(1)}, u32[]{:S(2)}, u32[]{:S(2)}) collective-permute-start(bf16[256,256]{1,0:T(8,128)(2,1)S(1)} %pick.1.refs_2_), channel_id=1, source_target_pairs={{0,2},{1,3},{2,0},{3,1},{4,6},{5,7},{6,4},{7,5},{8,10},{9,11},{10,... | collective-permute-start | bytes 393224 | tf_op jit(solution)/shard_map/ppermute | solution.py:354
  34.4 2.9 %collective-permute-start.7 = (bf16[256,256]{1,0:T(8,128)(2,1)S(1)}, bf16[256,256]{1,0:T(8,128)(2,1)S(1)}, u32[]{:S(2)}, u32[]{:S(2)}) collective-permute-start(bf16[256,256]{1,0:T(8,128)(2,1)S(1)} %pick.1.refs_2_), channel_id=1, source_target_pairs={{0,1},{1,0},{2,3},{3,2},{4,5},{5,4},{6,7},{7,6},{8,9},{9,8},{10,11... | collective-permute-start | bytes 393224 | tf_op jit(solution)/shard_map/ppermute | solution.py:354
  37.3 1.3 %collective-permute-start.8 = (bf16[256,256]{1,0:T(8,128)(2,1)S(1)}, bf16[256,256]{1,0:T(8,128)(2,1)S(1)}, u32[]{:S(2)}, u32[]{:S(2)}) collective-permute-start(bf16[256,256]{1,0:T(8,128)(2,1)S(1)} %collective-permute-done.6.refs_3_), channel_id=1, source_target_pairs={{0,1},{1,0},{2,3},{3,2},{4,5},{5,4},{6,7},{7,6},{8,9},{9,8},{10,11... | collective-permute-start | bytes 393224 | tf_op jit(solution)/shard_map/ppermute | solution.py:354
  38.7 9.5 %copy-start = (bf16[1,1024,1024]{2,1,0:T(8,128)(2,1)S(1)}, bf16[1,1024,1024]{2,1,0:T(8,128)(2,1)}, u32[]{:S(2)}) copy-start(bf16[1,1024,1024]{2,1,0:T(8,128)(2,1)} %param.16) | copy-start | bytes 6291460
  38.7 9.5 %copy-start.1 = (bf16[1,1024,1024]{2,1,0:T(8,128)(2,1)S(1)}, bf16[1,1024,1024]{2,1,0:T(8,128)(2,1)}, u32[]{:S(2)}) copy-start(bf16[1,1024,1024]{2,1,0:T(8,128)(2,1)} %param.17) | copy-start | bytes 6291460
  40.3 19.6 %collective-permute-start.17 = (bf16[192,512]{1,0:T(8,128)(2,1)S(1)}, bf16[192,512]{1,0:T(8,128)(2,1)S(1)}, u32[]{:S(2)}, u32[]{:S(2)}) collective-permute-start(bf16[192,512]{1,0:T(8,128)(2,1)S(1)} %get-tuple-element.79), channel_id=1, source_target_pairs={{0,4},{1,5},{2,6},{3,7},{4,0},{5,1},{6,2},{7,3},{8,12},{9,13},{10,... | collective-permute-start | bytes 589832 | tf_op jit(solution)/shard_map/ppermute | solution.py:354
  43.7 16.2 %collective-permute-start.15 = (bf16[192,512]{1,0:T(8,128)(2,1)S(1)}, bf16[192,512]{1,0:T(8,128)(2,1)S(1)}, u32[]{:S(2)}, u32[]{:S(2)}) collective-permute-start(bf16[192,512]{1,0:T(8,128)(2,1)S(1)} %get-tuple-element.77), channel_id=1, source_target_pairs={{0,12},{1,13},{2,14},{3,15},{4,8},{5,9},{6,10},{7,11},{8,4},{9,5},... | collective-permute-start | bytes 589832 | tf_op jit(solution)/shard_map/ppermute | solution.py:354
  47.1 12.3 %collective-permute-start.12 = (bf16[192,256]{1,0:T(8,128)(2,1)S(1)}, bf16[192,256]{1,0:T(8,128)(2,1)S(1)}, u32[]{:S(2)}, u32[]{:S(2)}) collective-permute-start(bf16[192,256]{1,0:T(8,128)(2,1)S(1)} %get-tuple-element.72), channel_id=1, source_target_pairs={{0,8},{1,9},{2,10},{3,11},{4,12},{5,13},{6,14},{7,15},{8,0},{9,1},... | collective-permute-start | bytes 294920 | tf_op jit(solution)/shard_map/ppermute | solution.py:354
  59.4 4.6 %collective-permute-start.19 = (bf16[192,256]{1,0:T(8,128)(2,1)S(1)}, bf16[192,256]{1,0:T(8,128)(2,1)S(1)}, u32[]{:S(2)}, u32[]{:S(2)}) collective-permute-start(bf16[192,256]{1,0:T(8,128)(2,1)S(1)} %collective-permute-done.12.refs_5_), channel_id=1, source_target_pairs={{0,2},{1,3},{2,0},{3,1},{4,6},{5,7},{6,4},{7,5},{8,10},{9,11},{10,... | collective-permute-start | bytes 294920 | tf_op jit(solution)/shard_map/ppermute | solution.py:354
  59.9 5.4 %collective-permute-start.16 = (bf16[192,512]{1,0:T(8,128)(2,1)S(1)}, bf16[192,512]{1,0:T(8,128)(2,1)S(1)}, u32[]{:S(2)}, u32[]{:S(2)}) collective-permute-start(bf16[192,512]{1,0:T(8,128)(2,1)S(1)} %collective-permute-done.15.refs_1_), channel_id=1, source_target_pairs={{0,1},{1,0},{2,3},{3,2},{4,5},{5,4},{6,7},{7,6},{8,9},{9,8},{10,11... | collective-permute-start | bytes 589832 | tf_op jit(solution)/shard_map/ppermute | solution.py:354
  59.9 5.4 %collective-permute-start.18 = (bf16[192,512]{1,0:T(8,128)(2,1)S(1)}, bf16[192,512]{1,0:T(8,128)(2,1)S(1)}, u32[]{:S(2)}, u32[]{:S(2)}) collective-permute-start(bf16[192,512]{1,0:T(8,128)(2,1)S(1)} %collective-permute-done.17.refs_3_), channel_id=1, source_target_pairs={{0,1},{1,0},{2,3},{3,2},{4,5},{5,4},{6,7},{7,6},{8,9},{9,8},{10,11... | collective-permute-start | bytes 589832 | tf_op jit(solution)/shard_map/ppermute | solution.py:354
  60.4 3.6 %collective-permute-start.20 = (bf16[192,256]{1,0:T(8,128)(2,1)S(1)}, bf16[192,256]{1,0:T(8,128)(2,1)S(1)}, u32[]{:S(2)}, u32[]{:S(2)}) collective-permute-start(bf16[192,256]{1,0:T(8,128)(2,1)S(1)} %collective-permute-done.12.refs_5_), channel_id=1, source_target_pairs={{0,1},{1,0},{2,3},{3,2},{4,5},{5,4},{6,7},{7,6},{8,9},{9,8},{10,11... | collective-permute-start | bytes 294920 | tf_op jit(solution)/shard_map/ppermute | solution.py:354
  64.0 1.3 %collective-permute-start.21 = (bf16[192,256]{1,0:T(8,128)(2,1)S(1)}, bf16[192,256]{1,0:T(8,128)(2,1)S(1)}, u32[]{:S(2)}, u32[]{:S(2)}) collective-permute-start(bf16[192,256]{1,0:T(8,128)(2,1)S(1)} %collective-permute-done.19.refs_6_), channel_id=1, source_target_pairs={{0,1},{1,0},{2,3},{3,2},{4,5},{5,4},{6,7},{7,6},{8,9},{9,8},{10,11... | collective-permute-start | bytes 294920 | tf_op jit(solution)/shard_map/ppermute | solution.py:354
  68.5 2.4 %collective-permute-start.22 = (bf16[2,576,256]{2,1,0:T(8,128)(2,1)S(1)}, bf16[2,576,256]{2,1,0:T(8,128)(2,1)S(1)}, u32[]{:S(2)}, u32[]{:S(2)}) collective-permute-start(bf16[2,576,256]{2,1,0:T(8,128)(2,1)S(1)} %get-tuple-element.83), channel_id=1, source_target_pairs={{0,1},{1,0},{2,3},{3,2},{4,5},{5,4},{6,7},{7,6},{8,9},{9,8},{10,11... | collective-permute-start | bytes 1769480 | tf_op jit(solution)/shard_map/ppermute | solution.py:354
  68.8 2.1 %collective-permute-start.13 = (bf16[2,192,256]{2,1,0:T(8,128)(2,1)S(1)}, bf16[2,192,256]{2,1,0:T(8,128)(2,1)S(1)}, u32[]{:S(2)}, u32[]{:S(2)}) collective-permute-start(bf16[2,192,256]{2,1,0:T(8,128)(2,1)S(1)} %get-tuple-element.73), channel_id=1, source_target_pairs={{0,1},{1,0},{2,3},{3,2},{4,5},{5,4},{6,7},{7,6},{8,9},{9,8},{10,11... | collective-permute-start | bytes 589832 | tf_op jit(solution)/shard_map/ppermute | solution.py:354
  71.2 6.8 %collective-permute-start.25 = (bf16[192,256]{1,0:T(8,128)(2,1)S(1)}, bf16[192,256]{1,0:T(8,128)(2,1)S(1)}, u32[]{:S(2)}, u32[]{:S(2)}) collective-permute-start(bf16[192,256]{1,0:T(8,128)(2,1)S(1)} %get-tuple-element.92), channel_id=1, source_target_pairs={{0,2},{1,3},{2,0},{3,1},{4,6},{5,7},{6,4},{7,5},{8,10},{9,11},{10,... | collective-permute-start | bytes 294920 | tf_op jit(solution)/shard_map/ppermute | solution.py:354
  71.8 10.8 %collective-permute-start.14 = (bf16[192,256]{1,0:T(8,128)(2,1)S(1)}, bf16[192,256]{1,0:T(8,128)(2,1)S(1)}, u32[]{:S(2)}, u32[]{:S(2)}) collective-permute-start(bf16[192,256]{1,0:T(8,128)(2,1)S(1)} %get-tuple-element.95), channel_id=1, source_target_pairs={{0,2},{1,3},{2,0},{3,1},{4,6},{5,7},{6,4},{7,5},{8,10},{9,11},{10,... | collective-permute-start | bytes 294920 | tf_op jit(solution)/shard_map/ppermute | solution.py:354
  73.4 9.1 %collective-permute-start.27 = (bf16[192,256]{1,0:T(8,128)(2,1)S(1)}, bf16[192,256]{1,0:T(8,128)(2,1)S(1)}, u32[]{:S(2)}, u32[]{:S(2)}) collective-permute-start(bf16[192,256]{1,0:T(8,128)(2,1)S(1)} %get-tuple-element.91), channel_id=1, source_target_pairs={{0,2},{1,3},{2,0},{3,1},{4,6},{5,7},{6,4},{7,5},{8,10},{9,11},{10,... | collective-permute-start | bytes 294920 | tf_op jit(solution)/shard_map/ppermute | solution.py:354
  73.9 8.9 %collective-permute-start.24 = (bf16[192,256]{1,0:T(8,128)(2,1)S(1)}, bf16[192,256]{1,0:T(8,128)(2,1)S(1)}, u32[]{:S(2)}, u32[]{:S(2)}) collective-permute-start(bf16[192,256]{1,0:T(8,128)(2,1)S(1)} %get-tuple-element.93), channel_id=1, source_target_pairs={{0,6},{1,7},{2,4},{3,5},{4,2},{5,3},{6,0},{7,1},{8,14},{9,15},{10,... | collective-permute-start | bytes 294920 | tf_op jit(solution)/shard_map/ppermute | solution.py:354
  74.7 8.2 %collective-permute-start.23 = (bf16[192,256]{1,0:T(8,128)(2,1)S(1)}, bf16[192,256]{1,0:T(8,128)(2,1)S(1)}, u32[]{:S(2)}, u32[]{:S(2)}) collective-permute-start(bf16[192,256]{1,0:T(8,128)(2,1)S(1)} %get-tuple-element.94), channel_id=1, source_target_pairs={{0,4},{1,5},{2,6},{3,7},{4,0},{5,1},{6,2},{7,3},{8,12},{9,13},{10,... | collective-permute-start | bytes 294920 | tf_op jit(solution)/shard_map/ppermute | solution.py:354
  78.0 6.5 %collective-permute-start.26 = (bf16[192,256]{1,0:T(8,128)(2,1)S(1)}, bf16[192,256]{1,0:T(8,128)(2,1)S(1)}, u32[]{:S(2)}, u32[]{:S(2)}) collective-permute-start(bf16[192,256]{1,0:T(8,128)(2,1)S(1)} %fusion.3), channel_id=1, source_target_pairs={{0,12},{1,13},{2,14},{3,15},{4,8},{5,9},{6,10},{7,11},{8,4},{9,5},... | collective-permute-start | bytes 294920 | tf_op jit(solution)/shard_map/ppermute | solution.py:354
  82.5 7.1 %collective-permute-start.28 = (bf16[192,256]{1,0:T(8,128)(2,1)S(1)}, bf16[192,256]{1,0:T(8,128)(2,1)S(1)}, u32[]{:S(2)}, u32[]{:S(2)}) collective-permute-start(bf16[192,256]{1,0:T(8,128)(2,1)S(1)} %fusion.1), channel_id=1, source_target_pairs={{0,8},{1,9},{2,10},{3,11},{4,12},{5,13},{6,14},{7,15},{8,0},{9,1},... | collective-permute-start | bytes 294920 | tf_op jit(solution)/shard_map/ppermute | solution.py:354

commit v7 on v5

--- a/solution.py
+++ b/solution.py
@@ -372,10 +372,9 @@
             steps_of = steps_of + [k ^ bit for k in steps_of]
         asked = dict(zip(steps_of, asked))
         previous, backs = own, {}
-        for k in range(1, groups):
-            answer = attend(after(asked[k], previous), source, token_count)
+        for k in sorted(range(1, groups), key=lambda k: (k & (k - 1) != 0, -k)):
+            answer = previous = attend(after(asked[k], previous), source, token_count)
             backs[k] = hop(answer, k, 0)
-            previous = answer
         context = pick(ids, source_owner, [own] + [backs[k] for k in range(1, groups)])
     else:
         asked = lax.all_gather(queries, "expert", axis=0, tiled=True)
@@ -437,7 +436,7 @@
                 places = places + [index ^ bit for index in places]
             keep, give = expert(turn_ids, places, [pieces])
             home[relayed] = send_home(relayed, sum_cores(keep, give))
-        order = [0] + rest + ([relayed] if relayed >= 0 else [])
+        order = [0] + rest[::-1] + ([relayed] if relayed >= 0 else [])
     else:
         mine = spread(leaving[0])
         keep, give = expert(ids, [0, 1], [[mine, hop(mine, 0, 1)]])

time: 85.3 us -> 82 us (0.961)
  waiting for transfers between devices: 33.7 us -> 30.1 us
    ppermute x30, waiting for transfers between devices: 33.7 us -> 30.1 us  [hop(): return lax.ppermute(value, ('expert', 'mp'), moves)]
  transfers between devices with their start and end apart: 30 -> 30, of which waited for: 13 -> 11; matrix products, arithmetic and copies ran while one was open for 0% -> 0% of each run, Pallas kernels for 15% -> 15%
where the time goes in v7:
time: 82 us; the launch traced here: 81.8 us
  starting transfers between devices  33.6 us (41%)
  waiting for transfers between devices  30.1 us (37%)
  Pallas kernels  16.7 us (20%)
  between operations  1 us (1%)
    ppermute x30, starting transfers between devices, hop(): return lax.ppermute(value, ('expert', 'mp'), moves)  33.6 us
    ppermute x30, waiting for transfers between devices, hop(): return lax.ppermute(value, ('expert', 'mp'), moves)  30.1 us
    pallas_call x3, Pallas kernels, run_expert(): pl.pallas_call(functools.partial(expert_kernel, tuple(order), len(blocks)...  5.45 us
    pallas_call x4, Pallas kernels, attend(): pl.pallas_call(attend_kernel, in_specs=[WHOLE] * 2, out_specs=WHOLE, out_...  3.1 us
    pallas_call x1, Pallas kernels, ask(): pl.pallas_call(query_kernel, in_specs=[pl.BlockSpec(memory_space=pltpu.HB...  1.81 us
  transfers between devices with their start and end apart: 30, of which 11 were waited for; matrix products, arithmetic and copies ran while one was open for 0% of the time, Pallas kernels for 15%

profile of v7, /device:TPU:0, one launch (start us, length us, event | category | flops | bytes accessed | tf_op | source)
XLA Modules:
  0.0 81.8 jit_solution(835100837215047298)
XLA Ops:
  0.0 2.9 %collective-permute-start.9 = (bf16[256,1024]{1,0:T(8,128)(2,1)}, bf16[256,1024]{1,0:T(8,128)(2,1)S(1)}, u32[]{:S(2)}, u32[]{:S(2)}) collective-permute-start(bf16[256,1024]{1,0:T(8,128)(2,1)} %refs_6_), channel_id=1, source_target_pairs={{0,2},{1,3},{2,0},{3,1},{4,6},{5,7},{6,4},{7,5},{8,10},{9,11},{10,... | collective-permute-start | bytes 1572872 | tf_op jit(solution)/shard_map/ppermute | solution.py:353
  2.9 0.1 pad_add_fusion.ids.refs_0_
  3.0 1.8 %query.1 = (bf16[256,256]{1,0:T(8,128)(2,1)S(1)}, bf16[2,512,256]{2,1,0:T(8,128)(2,1)S(1)}) custom-call(bf16[256,1024]{1,0:T(8,128)(2,1)} %refs_1_.1, bf16[1024,256]{1,0:T(8,128)(2,1)} %weight.1, bf16[2,512,256]{2,1,0:T(8,128)(2,1)} %bitcast.35), custom_call_target="tpu_custom_call" | custom-call | tf_op jit(solution)/shard_map/query/pallas_call | solution.py:60
  4.8 0.0 copy-start.3
  4.8 0.0 copy-start.5
  4.9 0.0 copy-start.2
  4.9 2.6 %collective-permute-start.1 = (bf16[256,256]{1,0:T(8,128)(2,1)S(1)}, bf16[256,256]{1,0:T(8,128)(2,1)S(1)}, u32[]{:S(2)}, u32[]{:S(2)}) collective-permute-start(bf16[256,256]{1,0:T(8,128)(2,1)S(1)} %get-tuple-element.46.queries), channel_id=1, source_target_pairs={{0,8},{1,9},{2,10},{3,11},{4,12},{5,13},{6,14},{7,15},{8,0},{9,1},... | collective-permute-start | bytes 393224 | tf_op jit(solution)/shard_map/ppermute | solution.py:353
  7.5 1.6 %collective-permute-start = (bf16[256,256]{1,0:T(8,128)(2,1)S(1)}, bf16[256,256]{1,0:T(8,128)(2,1)S(1)}, u32[]{:S(2)}, u32[]{:S(2)}) collective-permute-start(bf16[256,256]{1,0:T(8,128)(2,1)S(1)} %get-tuple-element.46.queries), channel_id=1, source_target_pairs={{0,4},{1,5},{2,6},{3,7},{4,0},{5,1},{6,2},{7,3},{8,12},{9,13},{10,... | collective-permute-start | bytes 393224 | tf_op jit(solution)/shard_map/ppermute | solution.py:353
  9.1 0.8 attend.4.refs_0_
  9.9 3.8 %collective-permute-done.1.queries = bf16[256,256]{1,0:T(8,128)(2,1)S(1)} collective-permute-done((bf16[256,256]{1,0:T(8,128)(2,1)S(1)}, bf16[256,256]{1,0:T(8,128)(2,1)S(1)}, u32[]{:S(2)}, u32[]{:S(2)}) %collective-permute-start.1) | collective-permute-done | bytes 131104 | tf_op jit(solution)/shard_map/ppermute | solution.py:353
  13.7 0.6 collective-permute-start.4
  14.3 0.8 attend.5
  15.1 3.4 %collective-permute-start.3 = (bf16[256,256]{1,0:T(8,128)(2,1)S(1)}, bf16[256,256]{1,0:T(8,128)(2,1)S(1)}, u32[]{:S(2)}, u32[]{:S(2)}) collective-permute-start(bf16[256,256]{1,0:T(8,128)(2,1)S(1)} %attend.5), channel_id=1, source_target_pairs={{0,8},{1,9},{2,10},{3,11},{4,12},{5,13},{6,14},{7,15},{8,0},{9,1},... | collective-permute-start | bytes 393224 | tf_op jit(solution)/shard_map/ppermute | solution.py:353
  18.5 0.0 collective-permute-done.queries
  18.5 0.8 attend.6
  19.3 0.1 collective-permute-start.2
  19.4 0.8 attend.7
  20.2 0.0 copy-start.4
  20.2 5.7 %collective-permute-start.5 = (bf16[256,256]{1,0:T(8,128)(2,1)S(1)}, bf16[256,256]{1,0:T(8,128)(2,1)S(1)}, u32[]{:S(2)}, u32[]{:S(2)}) collective-permute-start(bf16[256,256]{1,0:T(8,128)(2,1)S(1)} %attend.7), channel_id=1, source_target_pairs={{0,12},{1,13},{2,14},{3,15},{4,8},{5,9},{6,10},{7,11},{8,4},{9,5},... | collective-permute-start | bytes 393224 | tf_op jit(solution)/shard_map/ppermute | solution.py:353
  26.5 0.0 collective-permute-done.3.refs_2_
  26.5 2.8 %collective-permute-done.5.refs_3_ = bf16[256,256]{1,0:T(8,128)(2,1)S(1)} collective-permute-done((bf16[256,256]{1,0:T(8,128)(2,1)S(1)}, bf16[256,256]{1,0:T(8,128)(2,1)S(1)}, u32[]{:S(2)}, u32[]{:S(2)}) %collective-permute-start.5) | collective-permute-done | bytes 131104 | tf_op jit(solution)/shard_map/ppermute | solution.py:353
  29.3 0.6 pick.1.refs_2_
  29.9 0.1 collective-permute-start.10
  30.0 0.0 collective-permute-done.9.refs_7_
  30.0 0.5 collective-permute-start.11
  30.5 0.5 collective-permute-start.6
  31.1 1.5 %route.1 = (s32[256,2]{1,0:T(8,128)S(1)}, bf16[192,256]{1,0:T(8,128)(2,1)S(1)}, bf16[192,256]{1,0:T(8,128)(2,1)S(1)}, bf16[192,256]{1,0:T(8,128)(2,1)S(1)}, bf16...) custom-call(s32[2]{0:T(128)S(1)} %pad_add_fusion.ids.refs_0_, ...), custom_call_target="tpu_custom_call" | custom-call | tf_op jit(solution)/shard_map/route/pallas_call | solution.py:171
  32.6 0.1 collective-permute-start.7
  32.6 3.4 %collective-permute-done.6.refs_3_ = bf16[256,256]{1,0:T(8,128)(2,1)S(1)} collective-permute-done((bf16[256,256]{1,0:T(8,128)(2,1)S(1)}, bf16[256,256]{1,0:T(8,128)(2,1)S(1)}, u32[]{:S(2)}, u32[]{:S(2)}) %collective-permute-start.6) | collective-permute-done | bytes 131104 | tf_op jit(solution)/shard_map/ppermute | solution.py:353
  36.0 0.0 collective-permute-start.8
  36.0 1.3 %collective-permute-done.8.refs_5_ = bf16[256,256]{1,0:T(8,128)(2,1)S(1)} collective-permute-done((bf16[256,256]{1,0:T(8,128)(2,1)S(1)}, bf16[256,256]{1,0:T(8,128)(2,1)S(1)}, u32[]{:S(2)}, u32[]{:S(2)}) %collective-permute-start.8) | collective-permute-done | bytes 131104 | tf_op jit(solution)/shard_map/ppermute | solution.py:353
  37.4 0.0 copy-start
  37.4 0.0 copy-start.1
  37.4 1.6 %state.1 = (bf16[256,1024]{1,0:T(8,128)(2,1)S(1)}, bf16[192,256]{1,0:T(8,128)(2,1)S(1)}, bf16[192,512]{1,0:T(8,128)(2,1)S(1)}, bf16[192,512]{1,0:T(8,128)(2,1)S(1)}) custom-call(s32[2]{0:T(128)S(1)} %pad_add_fusion.ids.refs_0_, bf16[256,1024]{1,0:T(8,128)(2,1)S(1)} %copy-done.2, bf16[256,256]{1,0:T(8,128)(2,1)S(1)} %pick.1.refs_2_, ...), custom_call_target="tpu_custom_call" | custom-call | tf_op jit(solution)/shard_map/state/pallas_call | solution.py:201
  39.0 2.6 %collective-permute-start.12 = (bf16[192,256]{1,0:T(8,128)(2,1)S(1)}, bf16[192,256]{1,0:T(8,128)(2,1)S(1)}, u32[]{:S(2)}, u32[]{:S(2)}) collective-permute-start(bf16[192,256]{1,0:T(8,128)(2,1)S(1)} %get-tuple-element.69), channel_id=1, source_target_pairs={{0,8},{1,9},{2,10},{3,11},{4,12},{5,13},{6,14},{7,15},{8,0},{9,1},... | collective-permute-start | bytes 294920 | tf_op jit(solution)/shard_map/ppermute | solution.py:353
  41.5 1.4 %collective-permute-start.15 = (bf16[192,512]{1,0:T(8,128)(2,1)S(1)}, bf16[192,512]{1,0:T(8,128)(2,1)S(1)}, u32[]{:S(2)}, u32[]{:S(2)}) collective-permute-start(bf16[192,512]{1,0:T(8,128)(2,1)S(1)} %get-tuple-element.74), channel_id=1, source_target_pairs={{0,12},{1,13},{2,14},{3,15},{4,8},{5,9},{6,10},{7,11},{8,4},{9,5},... | collective-permute-start | bytes 589832 | tf_op jit(solution)/shard_map/ppermute | solution.py:353
  43.0 0.0 collective-permute-start.17
  43.0 1.0 %home.1 = (bf16[192,512]{1,0:T(8,128)(2,1)S(1)}, bf16[192,512]{1,0:T(8,128)(2,1)S(1)}, f32[256,2]{1,0:T(8,128)S(1)}, f32[256,256]{1,0:T(8,128)S(1)}) custom-call(s32[2]{0:T(128)S(1)} %pad_add_fusion.ids.refs_0_, bf16[256,1024]{1,0:T(8,128)(2,1)S(1)} %get-tuple-element.59.state, bf16[192,256]{1,0:T(8,128)(2,1)S(1)} %get-tuple-element.52.dispatch, ...), custom_call_target="tpu_custom_call" | custom-call | tf_op jit(solution)/shard_map/home/pallas_call | solution.py:231
  44.0 1.5 %expert.3 = (f32[2,192,256]{2,1,0:T(8,128)S(1)}, bf16[2,192,256]{2,1,0:T(8,128)(2,1)S(1)}) custom-call(s32[2]{0:T(128)S(1)} %pad_add_fusion.ids.refs_0_, bf16[192,512]{1,0:T(8,128)(2,1)S(1)} %get-tuple-element.65.refs_1_, bf16[192,512]{1,0:T(8,128)(2,1)S(1)} %get-tuple-element.66.refs_2_, bf16[1024,1024]{1,0:T(8,128)(2,1)S(1)} %bitcast.27, ...), custom_call_target="tpu_custom_call" | custom-call | tf_op jit(solution)/shard_map/expert/pallas_call | solution.py:278
  45.6 6.4 %collective-permute-done.12.refs_1_ = bf16[192,256]{1,0:T(8,128)(2,1)S(1)} collective-permute-done((bf16[192,256]{1,0:T(8,128)(2,1)S(1)}, bf16[192,256]{1,0:T(8,128)(2,1)S(1)}, u32[]{:S(2)}, u32[]{:S(2)}) %collective-permute-start.12) | collective-permute-done | bytes 98336 | tf_op jit(solution)/shard_map/ppermute | solution.py:353
  52.0 0.5 collective-permute-start.24
  52.5 0.2 collective-permute-start.25
  52.7 0.3 collective-permute-start.16
  53.0 1.6 %collective-permute-done.17.refs_3_ = bf16[192,512]{1,0:T(8,128)(2,1)S(1)} collective-permute-done((bf16[192,512]{1,0:T(8,128)(2,1)S(1)}, bf16[192,512]{1,0:T(8,128)(2,1)S(1)}, u32[]{:S(2)}, u32[]{:S(2)}) %collective-permute-start.17) | collective-permute-done | bytes 196640 | tf_op jit(solution)/shard_map/ppermute | solution.py:353
  54.6 2.6 %collective-permute-done.24.refs_2_ = bf16[192,256]{1,0:T(8,128)(2,1)S(1)} collective-permute-done((bf16[192,256]{1,0:T(8,128)(2,1)S(1)}, bf16[192,256]{1,0:T(8,128)(2,1)S(1)}, u32[]{:S(2)}, u32[]{:S(2)}) %collective-permute-start.24) | collective-permute-done | bytes 98336 | tf_op jit(solution)/shard_map/ppermute | solution.py:353
  57.2 0.1 add_convert_fusion.1
  57.3 2.4 %expert.4 = (f32[2,384,256]{2,1,0:T(8,128)S(1)}, bf16[2,384,256]{2,1,0:T(8,128)(2,1)S(1)}) custom-call(s32[2]{0:T(128)S(1)} %pad_add_fusion.ids.refs_0_, bf16[192,512]{1,0:T(8,128)(2,1)S(1)} %collective-permute-done.15.refs_1_, bf16[192,512]{1,0:T(8,128)(2,1)S(1)} %collective-permute-done.16.refs_2_, bf16[192,512]{1,0:T(8,128)(2,1)S(1)} %collective-permute-done.17.refs_3_, ...), custom_call_target="tpu_custom_call" | custom-call | tf_op jit(solution)/shard_map/expert/pallas_call | solution.py:278
  59.6 1.5 %expert.5 = (f32[2,192,256]{2,1,0:T(8,128)S(1)}, bf16[2,192,256]{2,1,0:T(8,128)(2,1)S(1)}) custom-call(s32[2]{0:T(128)S(1)} %pad_add_fusion.ids.refs_0_, bf16[192,256]{1,0:T(8,128)(2,1)S(1)} %collective-permute-done.12.refs_1_, bf16[192,256]{1,0:T(8,128)(2,1)S(1)} %collective-permute-done.24.refs_2_, bf16[192,256]{1,0:T(8,128)(2,1)S(1)} %collective-permute-done.25.refs_3_, ...), custom_call_target="tpu_custom_call" | custom-call | tf_op jit(solution)/shard_map/expert/pallas_call | solution.py:278
  61.2 0.6 collective-permute-start.27
  61.8 0.6 collective-permute-start.14
  62.4 0.5 collective-permute-done.27
  62.9 1.1 %collective-permute-start.28 = (bf16[192,256]{1,0:T(8,128)(2,1)S(1)}, bf16[192,256]{1,0:T(8,128)(2,1)S(1)}, u32[]{:S(2)}, u32[]{:S(2)}) collective-permute-start(bf16[192,256]{1,0:T(8,128)(2,1)S(1)} %fusion.2), channel_id=1, source_target_pairs={{0,2},{1,3},{2,0},{3,1},{4,6},{5,7},{6,4},{7,5},{8,10},{9,11},{10,... | collective-permute-start | bytes 294920 | tf_op jit(solution)/shard_map/ppermute | solution.py:353
  64.0 0.1 collective-permute-done.19
  64.1 0.1 add_convert_fusion
  64.2 3.7 %collective-permute-start.23 = (bf16[192,256]{1,0:T(8,128)(2,1)S(1)}, bf16[192,256]{1,0:T(8,128)(2,1)S(1)}, u32[]{:S(2)}, u32[]{:S(2)}) collective-permute-start(bf16[192,256]{1,0:T(8,128)(2,1)S(1)} %get-tuple-element.85), channel_id=1, source_target_pairs={{0,14},{1,15},{2,12},{3,13},{4,10},{5,11},{6,8},{7,9},{8,6},{9,7},... | collective-permute-start | bytes 294920 | tf_op jit(solution)/shard_map/ppermute | solution.py:353
  67.9 1.1 %collective-permute-start.22 = (bf16[192,256]{1,0:T(8,128)(2,1)S(1)}, bf16[192,256]{1,0:T(8,128)(2,1)S(1)}, u32[]{:S(2)}, u32[]{:S(2)}) collective-permute-start(bf16[192,256]{1,0:T(8,128)(2,1)S(1)} %get-tuple-element.86), channel_id=1, source_target_pairs={{0,12},{1,13},{2,14},{3,15},{4,8},{5,9},{6,10},{7,11},{8,4},{9,5},... | collective-permute-start | bytes 294920 | tf_op jit(solution)/shard_map/ppermute | solution.py:353
  69.1 2.0 %collective-permute-start.20 = (bf16[192,256]{1,0:T(8,128)(2,1)S(1)}, bf16[192,256]{1,0:T(8,128)(2,1)S(1)}, u32[]{:S(2)}, u32[]{:S(2)}) collective-permute-start(bf16[192,256]{1,0:T(8,128)(2,1)S(1)} %get-tuple-element.88), channel_id=1, source_target_pairs={{0,4},{1,5},{2,6},{3,7},{4,0},{5,1},{6,2},{7,3},{8,12},{9,13},{10,... | collective-permute-start | bytes 294920 | tf_op jit(solution)/shard_map/ppermute | solution.py:353
  71.1 1.4 %collective-permute-start.29 = (bf16[192,256]{1,0:T(8,128)(2,1)S(1)}, bf16[192,256]{1,0:T(8,128)(2,1)S(1)}, u32[]{:S(2)}, u32[]{:S(2)}) collective-permute-start(bf16[192,256]{1,0:T(8,128)(2,1)S(1)} %fusion.1), channel_id=1, source_target_pairs={{0,8},{1,9},{2,10},{3,11},{4,12},{5,13},{6,14},{7,15},{8,0},{9,1},... | collective-permute-start | bytes 294920 | tf_op jit(solution)/shard_map/ppermute | solution.py:353
  72.5 0.2 combine.4.base
  72.8 4.1 %collective-permute-done.21.refs_1_ = bf16[192,256]{1,0:T(8,128)(2,1)S(1)} collective-permute-done((bf16[192,256]{1,0:T(8,128)(2,1)S(1)}, bf16[192,256]{1,0:T(8,128)(2,1)S(1)}, u32[]{:S(2)}, u32[]{:S(2)}) %collective-permute-start.21) | collective-permute-done | bytes 98336 | tf_op jit(solution)/shard_map/ppermute | solution.py:353
  76.9 3.5 %collective-permute-done.20.refs_0_ = bf16[192,256]{1,0:T(8,128)(2,1)S(1)} collective-permute-done((bf16[192,256]{1,0:T(8,128)(2,1)S(1)}, bf16[192,256]{1,0:T(8,128)(2,1)S(1)}, u32[]{:S(2)}, u32[]{:S(2)}) %collective-permute-start.20) | collective-permute-done | bytes 98336 | tf_op jit(solution)/shard_map/ppermute | solution.py:353
  80.4 0.2 combine.5.base
  80.7 0.2 combine.6.base
  80.9 0.9 %combine.7 = bf16[256,256]{1,0:T(8,128)(2,1)} custom-call(f32[256,2]{1,0:T(8,128)S(1)} %get-tuple-element.61.gates, f32[256,256]{1,0:T(8,128)S(1)} %combine.6.base, bf16[256,192]{1,0:T(8,128)(2,1)S(1)} %get-tuple-element.80.first, bf16[256,192]{1,0:T(8,128)(2,1)S(1)} %get-tuple-element.81.second, bf16[192,256]{1,0:T(8,128)(2,1)S(1)} %collective-permute-done.29.refs_0_), custom_call_target="tpu_custom_call" | custom-call | tf_op jit(solution)/shard_map/combine/pallas_call | solution.py:304
  (32 shorter events, 0.2 us)
Async XLA Ops:
  0.0 30.0 %collective-permute-start.9 = (bf16[256,1024]{1,0:T(8,128)(2,1)}, bf16[256,1024]{1,0:T(8,128)(2,1)S(1)}, u32[]{:S(2)}, u32[]{:S(2)}) collective-permute-start(bf16[256,1024]{1,0:T(8,128)(2,1)} %refs_6_), channel_id=1, source_target_pairs={{0,2},{1,3},{2,0},{3,1},{4,6},{5,7},{6,4},{7,5},{8,10},{9,11},{10,... | collective-permute-start | bytes 1572872 | tf_op jit(solution)/shard_map/ppermute | solution.py:353
  4.8 25.1 %copy-start.3 = (bf16[256,1024]{1,0:T(8,128)(2,1)S(1)}, bf16[256,1024]{1,0:T(8,128)(2,1)}, u32[]{:S(2)}) copy-start(bf16[256,1024]{1,0:T(8,128)(2,1)} %refs_6_) | copy-start | bytes 1572868
  4.8 26.2 %copy-start.5 = (s32[256,2]{0,1:T(2,128)S(1)}, s32[256,2]{0,1:T(2,128)}, u32[]{:S(2)}) copy-start(s32[256,2]{0,1:T(2,128)} %param.15) | copy-start | bytes 6148
  4.9 32.5 %copy-start.2 = (bf16[256,1024]{1,0:T(8,128)(2,1)S(1)}, bf16[256,1024]{1,0:T(8,128)(2,1)}, u32[]{:S(2)}) copy-start(bf16[256,1024]{1,0:T(8,128)(2,1)} %refs_1_.1) | copy-start | bytes 1572868
  4.9 8.8 %collective-permute-start.1 = (bf16[256,256]{1,0:T(8,128)(2,1)S(1)}, bf16[256,256]{1,0:T(8,128)(2,1)S(1)}, u32[]{:S(2)}, u32[]{:S(2)}) collective-permute-start(bf16[256,256]{1,0:T(8,128)(2,1)S(1)} %get-tuple-element.46.queries), channel_id=1, source_target_pairs={{0,8},{1,9},{2,10},{3,11},{4,12},{5,13},{6,14},{7,15},{8,0},{9,1},... | collective-permute-start | bytes 393224 | tf_op jit(solution)/shard_map/ppermute | solution.py:353
  7.5 11.0 %collective-permute-start = (bf16[256,256]{1,0:T(8,128)(2,1)S(1)}, bf16[256,256]{1,0:T(8,128)(2,1)S(1)}, u32[]{:S(2)}, u32[]{:S(2)}) collective-permute-start(bf16[256,256]{1,0:T(8,128)(2,1)S(1)} %get-tuple-element.46.queries), channel_id=1, source_target_pairs={{0,4},{1,5},{2,6},{3,7},{4,0},{5,1},{6,2},{7,3},{8,12},{9,13},{10,... | collective-permute-start | bytes 393224 | tf_op jit(solution)/shard_map/ppermute | solution.py:353
  13.7 5.7 %collective-permute-start.4 = (bf16[256,256]{1,0:T(8,128)(2,1)S(1)}, bf16[256,256]{1,0:T(8,128)(2,1)S(1)}, u32[]{:S(2)}, u32[]{:S(2)}) collective-permute-start(bf16[256,256]{1,0:T(8,128)(2,1)S(1)} %collective-permute-done.1.queries), channel_id=1, source_target_pairs={{0,4},{1,5},{2,6},{3,7},{4,0},{5,1},{6,2},{7,3},{8,12},{9,13},{10,... | collective-permute-start | bytes 393224 | tf_op jit(solution)/shard_map/ppermute | solution.py:353
  15.1 11.4 %collective-permute-start.3 = (bf16[256,256]{1,0:T(8,128)(2,1)S(1)}, bf16[256,256]{1,0:T(8,128)(2,1)S(1)}, u32[]{:S(2)}, u32[]{:S(2)}) collective-permute-start(bf16[256,256]{1,0:T(8,128)(2,1)S(1)} %attend.5), channel_id=1, source_target_pairs={{0,8},{1,9},{2,10},{3,11},{4,12},{5,13},{6,14},{7,15},{8,0},{9,1},... | collective-permute-start | bytes 393224 | tf_op jit(solution)/shard_map/ppermute | solution.py:353
  19.3 7.2 %collective-permute-start.2 = (bf16[256,256]{1,0:T(8,128)(2,1)S(1)}, bf16[256,256]{1,0:T(8,128)(2,1)S(1)}, u32[]{:S(2)}, u32[]{:S(2)}) collective-permute-start(bf16[256,256]{1,0:T(8,128)(2,1)S(1)} %attend.6), channel_id=1, source_target_pairs={{0,4},{1,5},{2,6},{3,7},{4,0},{5,1},{6,2},{7,3},{8,12},{9,13},{10,... | collective-permute-start | bytes 393224 | tf_op jit(solution)/shard_map/ppermute | solution.py:353
  20.2 22.8 %copy-start.4 = (bf16[1024,4]{0,1:T(4,128)(2,1)S(1)}, bf16[1024,4]{0,1:T(4,128)(2,1)}, u32[]{:S(2)}) copy-start(bf16[1024,4]{0,1:T(4,128)(2,1)} %param.14) | copy-start | bytes 24580
  20.2 9.2 %collective-permute-start.5 = (bf16[256,256]{1,0:T(8,128)(2,1)S(1)}, bf16[256,256]{1,0:T(8,128)(2,1)S(1)}, u32[]{:S(2)}, u32[]{:S(2)}) collective-permute-start(bf16[256,256]{1,0:T(8,128)(2,1)S(1)} %attend.7), channel_id=1, source_target_pairs={{0,12},{1,13},{2,14},{3,15},{4,8},{5,9},{6,10},{7,11},{8,4},{9,5},... | collective-permute-start | bytes 393224 | tf_op jit(solution)/shard_map/ppermute | solution.py:353
  29.9 7.4 %collective-permute-start.10 = (bf16[256,1024]{1,0:T(8,128)(2,1)S(1)}, bf16[256,1024]{1,0:T(8,128)(2,1)S(1)}, u32[]{:S(2)}, u32[]{:S(2)}) collective-permute-start(bf16[256,1024]{1,0:T(8,128)(2,1)S(1)} %copy-done.3), channel_id=1, source_target_pairs={{0,1},{1,0},{2,3},{3,2},{4,5},{5,4},{6,7},{7,6},{8,9},{9,8},{10,11... | collective-permute-start | bytes 1572872 | tf_op jit(solution)/shard_map/ppermute | solution.py:353
  30.0 7.3 %collective-permute-start.11 = (bf16[256,1024]{1,0:T(8,128)(2,1)S(1)}, bf16[256,1024]{1,0:T(8,128)(2,1)S(1)}, u32[]{:S(2)}, u32[]{:S(2)}) collective-permute-start(bf16[256,1024]{1,0:T(8,128)(2,1)S(1)} %collective-permute-done.9.refs_7_), channel_id=1, source_target_pairs={{0,1},{1,0},{2,3},{3,2},{4,5},{5,4},{6,7},{7,6},{8,9},{9,8},{10,11... | collective-permute-start | bytes 1572872 | tf_op jit(solution)/shard_map/ppermute | solution.py:353
  30.5 5.5 %collective-permute-start.6 = (bf16[256,256]{1,0:T(8,128)(2,1)S(1)}, bf16[256,256]{1,0:T(8,128)(2,1)S(1)}, u32[]{:S(2)}, u32[]{:S(2)}) collective-permute-start(bf16[256,256]{1,0:T(8,128)(2,1)S(1)} %pick.1.refs_2_), channel_id=1, source_target_pairs={{0,2},{1,3},{2,0},{3,1},{4,6},{5,7},{6,4},{7,5},{8,10},{9,11},{10,... | collective-permute-start | bytes 393224 | tf_op jit(solution)/shard_map/ppermute | solution.py:353
  32.6 3.5 %collective-permute-start.7 = (bf16[256,256]{1,0:T(8,128)(2,1)S(1)}, bf16[256,256]{1,0:T(8,128)(2,1)S(1)}, u32[]{:S(2)}, u32[]{:S(2)}) collective-permute-start(bf16[256,256]{1,0:T(8,128)(2,1)S(1)} %pick.1.refs_2_), channel_id=1, source_target_pairs={{0,1},{1,0},{2,3},{3,2},{4,5},{5,4},{6,7},{7,6},{8,9},{9,8},{10,11... | collective-permute-start | bytes 393224 | tf_op jit(solution)/shard_map/ppermute | solution.py:353
  36.0 1.3 %collective-permute-start.8 = (bf16[256,256]{1,0:T(8,128)(2,1)S(1)}, bf16[256,256]{1,0:T(8,128)(2,1)S(1)}, u32[]{:S(2)}, u32[]{:S(2)}) collective-permute-start(bf16[256,256]{1,0:T(8,128)(2,1)S(1)} %collective-permute-done.6.refs_3_), channel_id=1, source_target_pairs={{0,1},{1,0},{2,3},{3,2},{4,5},{5,4},{6,7},{7,6},{8,9},{9,8},{10,11... | collective-permute-start | bytes 393224 | tf_op jit(solution)/shard_map/ppermute | solution.py:353
  37.4 6.6 %copy-start = (bf16[1,1024,1024]{2,1,0:T(8,128)(2,1)S(1)}, bf16[1,1024,1024]{2,1,0:T(8,128)(2,1)}, u32[]{:S(2)}) copy-start(bf16[1,1024,1024]{2,1,0:T(8,128)(2,1)} %param.16) | copy-start | bytes 6291460
  37.4 6.6 %copy-start.1 = (bf16[1,1024,1024]{2,1,0:T(8,128)(2,1)S(1)}, bf16[1,1024,1024]{2,1,0:T(8,128)(2,1)}, u32[]{:S(2)}) copy-start(bf16[1,1024,1024]{2,1,0:T(8,128)(2,1)} %param.17) | copy-start | bytes 6291460
  39.0 13.0 %collective-permute-start.12 = (bf16[192,256]{1,0:T(8,128)(2,1)S(1)}, bf16[192,256]{1,0:T(8,128)(2,1)S(1)}, u32[]{:S(2)}, u32[]{:S(2)}) collective-permute-start(bf16[192,256]{1,0:T(8,128)(2,1)S(1)} %get-tuple-element.69), channel_id=1, source_target_pairs={{0,8},{1,9},{2,10},{3,11},{4,12},{5,13},{6,14},{7,15},{8,0},{9,1},... | collective-permute-start | bytes 294920 | tf_op jit(solution)/shard_map/ppermute | solution.py:353
  41.5 11.2 %collective-permute-start.15 = (bf16[192,512]{1,0:T(8,128)(2,1)S(1)}, bf16[192,512]{1,0:T(8,128)(2,1)S(1)}, u32[]{:S(2)}, u32[]{:S(2)}) collective-permute-start(bf16[192,512]{1,0:T(8,128)(2,1)S(1)} %get-tuple-element.74), channel_id=1, source_target_pairs={{0,12},{1,13},{2,14},{3,15},{4,8},{5,9},{6,10},{7,11},{8,4},{9,5},... | collective-permute-start | bytes 589832 | tf_op jit(solution)/shard_map/ppermute | solution.py:353
  43.0 11.6 %collective-permute-start.17 = (bf16[192,512]{1,0:T(8,128)(2,1)S(1)}, bf16[192,512]{1,0:T(8,128)(2,1)S(1)}, u32[]{:S(2)}, u32[]{:S(2)}) collective-permute-start(bf16[192,512]{1,0:T(8,128)(2,1)S(1)} %get-tuple-element.75), channel_id=1, source_target_pairs={{0,4},{1,5},{2,6},{3,7},{4,0},{5,1},{6,2},{7,3},{8,12},{9,13},{10,... | collective-permute-start | bytes 589832 | tf_op jit(solution)/shard_map/ppermute | solution.py:353
  52.0 5.2 %collective-permute-start.13 = (bf16[2,192,256]{2,1,0:T(8,128)(2,1)S(1)}, bf16[2,192,256]{2,1,0:T(8,128)(2,1)S(1)}, u32[]{:S(2)}, u32[]{:S(2)}) collective-permute-start(bf16[2,192,256]{2,1,0:T(8,128)(2,1)S(1)} %get-tuple-element.70), channel_id=1, source_target_pairs={{0,1},{1,0},{2,3},{3,2},{4,5},{5,4},{6,7},{7,6},{8,9},{9,8},{10,11... | collective-permute-start | bytes 589832 | tf_op jit(solution)/shard_map/ppermute | solution.py:353
  52.0 5.2 %collective-permute-start.24 = (bf16[192,256]{1,0:T(8,128)(2,1)S(1)}, bf16[192,256]{1,0:T(8,128)(2,1)S(1)}, u32[]{:S(2)}, u32[]{:S(2)}) collective-permute-start(bf16[192,256]{1,0:T(8,128)(2,1)S(1)} %collective-permute-done.12.refs_1_), channel_id=1, source_target_pairs={{0,2},{1,3},{2,0},{3,1},{4,6},{5,7},{6,4},{7,5},{8,10},{9,11},{10,... | collective-permute-start | bytes 294920 | tf_op jit(solution)/shard_map/ppermute | solution.py:353
  52.5 7.1 %collective-permute-start.25 = (bf16[192,256]{1,0:T(8,128)(2,1)S(1)}, bf16[192,256]{1,0:T(8,128)(2,1)S(1)}, u32[]{:S(2)}, u32[]{:S(2)}) collective-permute-start(bf16[192,256]{1,0:T(8,128)(2,1)S(1)} %collective-permute-done.12.refs_1_), channel_id=1, source_target_pairs={{0,1},{1,0},{2,3},{3,2},{4,5},{5,4},{6,7},{7,6},{8,9},{9,8},{10,11... | collective-permute-start | bytes 294920 | tf_op jit(solution)/shard_map/ppermute | solution.py:353
  52.7 4.5 %collective-permute-start.16 = (bf16[192,512]{1,0:T(8,128)(2,1)S(1)}, bf16[192,512]{1,0:T(8,128)(2,1)S(1)}, u32[]{:S(2)}, u32[]{:S(2)}) collective-permute-start(bf16[192,512]{1,0:T(8,128)(2,1)S(1)} %collective-permute-done.15.refs_1_), channel_id=1, source_target_pairs={{0,1},{1,0},{2,3},{3,2},{4,5},{5,4},{6,7},{7,6},{8,9},{9,8},{10,11... | collective-permute-start | bytes 589832 | tf_op jit(solution)/shard_map/ppermute | solution.py:353
  54.6 2.7 %collective-permute-start.18 = (bf16[192,512]{1,0:T(8,128)(2,1)S(1)}, bf16[192,512]{1,0:T(8,128)(2,1)S(1)}, u32[]{:S(2)}, u32[]{:S(2)}) collective-permute-start(bf16[192,512]{1,0:T(8,128)(2,1)S(1)} %collective-permute-done.17.refs_3_), channel_id=1, source_target_pairs={{0,1},{1,0},{2,3},{3,2},{4,5},{5,4},{6,7},{7,6},{8,9},{9,8},{10,11... | collective-permute-start | bytes 589832 | tf_op jit(solution)/shard_map/ppermute | solution.py:353
  57.2 2.5 %collective-permute-start.26 = (bf16[192,256]{1,0:T(8,128)(2,1)S(1)}, bf16[192,256]{1,0:T(8,128)(2,1)S(1)}, u32[]{:S(2)}, u32[]{:S(2)}) collective-permute-start(bf16[192,256]{1,0:T(8,128)(2,1)S(1)} %collective-permute-done.24.refs_2_), channel_id=1, source_target_pairs={{0,1},{1,0},{2,3},{3,2},{4,5},{5,4},{6,7},{7,6},{8,9},{9,8},{10,11... | collective-permute-start | bytes 294920 | tf_op jit(solution)/shard_map/ppermute | solution.py:353
  61.2 1.6 %collective-permute-start.27 = (bf16[2,192,256]{2,1,0:T(8,128)(2,1)S(1)}, bf16[2,192,256]{2,1,0:T(8,128)(2,1)S(1)}, u32[]{:S(2)}, u32[]{:S(2)}) collective-permute-start(bf16[2,192,256]{2,1,0:T(8,128)(2,1)S(1)} %get-tuple-element.84), channel_id=1, source_target_pairs={{0,1},{1,0},{2,3},{3,2},{4,5},{5,4},{6,7},{7,6},{8,9},{9,8},{10,11... | collective-permute-start | bytes 589832 | tf_op jit(solution)/shard_map/ppermute | solution.py:353
  61.8 9.3 %collective-permute-start.14 = (bf16[192,256]{1,0:T(8,128)(2,1)S(1)}, bf16[192,256]{1,0:T(8,128)(2,1)S(1)}, u32[]{:S(2)}, u32[]{:S(2)}) collective-permute-start(bf16[192,256]{1,0:T(8,128)(2,1)S(1)} %get-tuple-element.89), channel_id=1, source_target_pairs={{0,2},{1,3},{2,0},{3,1},{4,6},{5,7},{6,4},{7,5},{8,10},{9,11},{10,... | collective-permute-start | bytes 294920 | tf_op jit(solution)/shard_map/ppermute | solution.py:353
  62.4 1.7 %collective-permute-start.19 = (bf16[2,384,256]{2,1,0:T(8,128)(2,1)S(1)}, bf16[2,384,256]{2,1,0:T(8,128)(2,1)S(1)}, u32[]{:S(2)}, u32[]{:S(2)}) collective-permute-start(bf16[2,384,256]{2,1,0:T(8,128)(2,1)S(1)} %get-tuple-element.77), channel_id=1, source_target_pairs={{0,1},{1,0},{2,3},{3,2},{4,5},{5,4},{6,7},{7,6},{8,9},{9,8},{10,11... | collective-permute-start | bytes 1179656 | tf_op jit(solution)/shard_map/ppermute | solution.py:353
  62.9 6.2 %collective-permute-start.28 = (bf16[192,256]{1,0:T(8,128)(2,1)S(1)}, bf16[192,256]{1,0:T(8,128)(2,1)S(1)}, u32[]{:S(2)}, u32[]{:S(2)}) collective-permute-start(bf16[192,256]{1,0:T(8,128)(2,1)S(1)} %fusion.2), channel_id=1, source_target_pairs={{0,2},{1,3},{2,0},{3,1},{4,6},{5,7},{6,4},{7,5},{8,10},{9,11},{10,... | collective-permute-start | bytes 294920 | tf_op jit(solution)/shard_map/ppermute | solution.py:353
  64.2 16.4 %collective-permute-start.23 = (bf16[192,256]{1,0:T(8,128)(2,1)S(1)}, bf16[192,256]{1,0:T(8,128)(2,1)S(1)}, u32[]{:S(2)}, u32[]{:S(2)}) collective-permute-start(bf16[192,256]{1,0:T(8,128)(2,1)S(1)} %get-tuple-element.85), channel_id=1, source_target_pairs={{0,14},{1,15},{2,12},{3,13},{4,10},{5,11},{6,8},{7,9},{8,6},{9,7},... | collective-permute-start | bytes 294920 | tf_op jit(solution)/shard_map/ppermute | solution.py:353
  67.9 12.7 %collective-permute-start.22 = (bf16[192,256]{1,0:T(8,128)(2,1)S(1)}, bf16[192,256]{1,0:T(8,128)(2,1)S(1)}, u32[]{:S(2)}, u32[]{:S(2)}) collective-permute-start(bf16[192,256]{1,0:T(8,128)(2,1)S(1)} %get-tuple-element.86), channel_id=1, source_target_pairs={{0,12},{1,13},{2,14},{3,15},{4,8},{5,9},{6,10},{7,11},{8,4},{9,5},... | collective-permute-start | bytes 294920 | tf_op jit(solution)/shard_map/ppermute | solution.py:353
  69.1 7.8 %collective-permute-start.21 = (bf16[192,256]{1,0:T(8,128)(2,1)S(1)}, bf16[192,256]{1,0:T(8,128)(2,1)S(1)}, u32[]{:S(2)}, u32[]{:S(2)}) collective-permute-start(bf16[192,256]{1,0:T(8,128)(2,1)S(1)} %get-tuple-element.87), channel_id=1, source_target_pairs={{0,6},{1,7},{2,4},{3,5},{4,2},{5,3},{6,0},{7,1},{8,14},{9,15},{10,... | collective-permute-start | bytes 294920 | tf_op jit(solution)/shard_map/ppermute | solution.py:353
  69.1 11.3 %collective-permute-start.20 = (bf16[192,256]{1,0:T(8,128)(2,1)S(1)}, bf16[192,256]{1,0:T(8,128)(2,1)S(1)}, u32[]{:S(2)}, u32[]{:S(2)}) collective-permute-start(bf16[192,256]{1,0:T(8,128)(2,1)S(1)} %get-tuple-element.88), channel_id=1, source_target_pairs={{0,4},{1,5},{2,6},{3,7},{4,0},{5,1},{6,2},{7,3},{8,12},{9,13},{10,... | collective-permute-start | bytes 294920 | tf_op jit(solution)/shard_map/ppermute | solution.py:353
  71.1 9.8 %collective-permute-start.29 = (bf16[192,256]{1,0:T(8,128)(2,1)S(1)}, bf16[192,256]{1,0:T(8,128)(2,1)S(1)}, u32[]{:S(2)}, u32[]{:S(2)}) collective-permute-start(bf16[192,256]{1,0:T(8,128)(2,1)S(1)} %fusion.1), channel_id=1, source_target_pairs={{0,8},{1,9},{2,10},{3,11},{4,12},{5,13},{6,14},{7,15},{8,0},{9,1},... | collective-permute-start | bytes 294920 | tf_op jit(solution)/shard_map/ppermute | solution.py:353

commit v8 on v6

--- a/solution.py
+++ b/solution.py
@@ -373,33 +373,29 @@
             steps_of = steps_of + [k ^ bit for k in steps_of]
         asked = dict(zip(steps_of, asked))
         previous, backs = own, {}
-        for k in range(1, groups):
-            answer = attend(after(asked[k], previous), source, token_count)
+        for k in sorted(range(1, groups), key=lambda k: (k & (k - 1) != 0, -k)):
+            answer = previous = attend(after(asked[k], previous), source, token_count)
             backs[k] = hop(answer, k, 0)
-            previous = answer
-        swap_after = backs.get(1, own)
         context = pick(ids, source_owner, [own] + [backs[k] for k in range(1, groups)])
     else:
         asked = lax.all_gather(queries, "expert", axis=0, tiled=True)
         previous = attend(asked, source, token_count)
-        swap_after = previous
         context = lax.dynamic_slice_in_dim(spread(previous), source_owner[0] * token_count, token_count, 0)
 
     choice, dispatch, first, second = route(ids, after(expert_choice, previous), experts, len(steps), capacity)
     weights, order = [output_weight], [0]
     for bit in bits:
         if bit == 1:
-            weights = [after(weight, swap_after) for weight in weights]
+            weights = [after(weight, context) for weight in weights]
         weights = weights + [hop(weight, 0, bit) for weight in weights]
         order = order + [index ^ bit for index in order]
     contexts = [context]
     for bit in bits:
         contexts = contexts + [hop(value if i == 0 else after(value, dispatch[0]), 0, bit) for i, value in enumerate(contexts)]
 
-    relayed = groups // 2 if direct and pairs > 1 and groups > 1 else -1
-    rest = [k for k in reversed(range(1, groups)) if k != relayed]
-    sends = ([relayed] if relayed >= 0 else []) + rest if direct else [0]
-    cuts = [slices if k == relayed else 2 for k in sends]
+    far = set(range(2, groups)) if direct and pairs > 1 else set()
+    sends = [k for k in range(2, groups)] + ([1] if groups > 1 else []) if direct else [0]
+    cuts = [slices if k in far else 2 for k in sends]
     state, *leaving = make_state(ids, tokens, contexts, weights, [dispatch[k] for k in sends], cuts)
     own_a, own_b, gates, columns = at_home(
         ids, state, dispatch[0], router_weight.T, choice, experts, width
@@ -409,48 +405,43 @@
     def sum_cores(keep, give):
         return keep + hop(give, 0, 1).astype(F32)
 
-    def send_home(k, summed, earlier=None):
-        if k > 1:
+    def send_home(k, summed):
+        if k in far:
             total = summed[0]
             for j in range(1, pairs):
-                other = hop(summed[j].astype(BF16), 0, 2 * j)
-                total += (other if earlier is None else after(other, earlier)).astype(F32)
-            return [total.astype(BF16)]
+                total += hop(summed[j].astype(BF16), 0, 2 * j).astype(F32)
+            return [hop(total.astype(BF16), k, 0)]
         parts = [summed[j].astype(BF16) for j in range(pairs)]
         return [hop(part, k, 2 * j) if direct else hop(spread(part), 0, 2 * j) for j, part in enumerate(parts)]
 
-    home = {}
+    home, order = {}, [0]
     if direct:
         arrived = {k: hop(rows, k, 0) for k, rows in zip(sends, leaving)}
         keep, give = expert(ids, [[0, 1]], [[own_a, own_b]])
         turn_ids = after(ids, give)
-        used = {k: after(rows, give) for k, rows in arrived.items()}
         if sends:
             give = after(give, arrived[sends[0]])
         home[0] = send_home(0, sum_cores(keep, give))
-        order = [*rest, relayed] if relayed >= 0 else rest
-        blocks, orders = [], []
-        for k in order:
-            pieces, places = [used[k]], [0]
-            for bit in bits if k == relayed else [1]:
-                pieces = pieces + [hop(piece, 0, bit) for piece in pieces]
-                places = places + [index ^ bit for index in places]
-            blocks.append(pieces)
-            orders.append(places)
-        if order:
-            summed = sum_cores(*expert(turn_ids, orders, blocks))
-            earlier = None
-            for k in sorted(order, reverse=True):
-                i = order.index(k)
-                home[k] = send_home(k, summed[:, i * slots : (i + 1) * slots], earlier)
-                if k > 1:
-                    earlier = home[k][0]
-                    home[k] = [hop(earlier, k, 0)]
-        order = [0] + sorted(order, key=lambda k: (k > 1, -k))
+        turns = [[k for k in sends if k < groups - 1], [groups - 1]] if groups > 2 else [sends]
+        for turn in turns:
+            blocks, orders = [], []
+            for k in turn:
+                pieces, places = [arrived[k]], [0]
+                for bit in bits if k in far else [1]:
+                    pieces = pieces + [hop(piece, 0, bit) for piece in pieces]
+                    places = places + [index ^ bit for index in places]
+                blocks.append(pieces)
+                orders.append(places)
+            if turn:
+                keep, give = expert(turn_ids, orders, blocks)
+                turn_ids = after(ids, give)
+                summed = sum_cores(keep, give)
+                for i, k in enumerate(turn):
+                    home[k] = send_home(k, summed[:, i * slots : (i + 1) * slots])
+        order = [0] + sorted(sends)
     else:
         mine = spread(leaving[0])
         home[0] = send_home(0, sum_cores(*expert(ids, [[0, 1]], [[mine, hop(mine, 0, 1)]])))
-        order = [0]
     results = columns
     for k in order:
         results = combine(gates, results, first[k], second[k], home[k], BF16 if k == order[-1] else F32)

time: 90.6 us -> 82.5 us (0.911)
  waiting for transfers between devices: 42.9 us -> 29.7 us
  starting transfers between devices: 30.2 us -> 34.7 us
    ppermute x29 -> x32, waiting for transfers between devices: 42.9 us -> 29.7 us  [hop(): return lax.ppermute(value, ('expert', 'mp'), moves)]
    ppermute x29 -> x32, starting transfers between devices: 30.2 us -> 34.7 us  [hop(): return lax.ppermute(value, ('expert', 'mp'), moves)]
    pallas_call x2 -> x3, Pallas kernels: 4.8 us -> 5.52 us  [run_expert(): pl.pallas_call(functools.partial(expert_kernel, tuple(map(tuple, orders))...]
  transfers between devices with their start and end apart: 29 -> 32, of which waited for: 14 -> 13; matrix products, arithmetic and copies ran while one was open for 0% -> 0% of each run, Pallas kernels for 11% -> 17%
where the time goes in v8:
time: 82.5 us; the launch traced here: 82.4 us
  starting transfers between devices  34.7 us (42%)
  waiting for transfers between devices  29.7 us (36%)
  Pallas kernels  16.7 us (20%)
  between operations  0.98 us (1%)
    ppermute x32, starting transfers between devices, hop(): return lax.ppermute(value, ('expert', 'mp'), moves)  34.7 us
    ppermute x32, waiting for transfers between devices, hop(): return lax.ppermute(value, ('expert', 'mp'), moves)  29.7 us
    pallas_call x3, Pallas kernels, run_expert(): pl.pallas_call(functools.partial(expert_kernel, tuple(map(tuple, orders))...  5.52 us
    pallas_call x4, Pallas kernels, attend(): pl.pallas_call(attend_kernel, in_specs=[WHOLE] * 2, out_specs=WHOLE, out_...  3.1 us
    pallas_call x1, Pallas kernels, ask(): pl.pallas_call(query_kernel, in_specs=[pl.BlockSpec(memory_space=pltpu.HB...  1.81 us
  transfers between devices with their start and end apart: 32, of which 13 were waited for; matrix products, arithmetic and copies ran while one was open for 0% of the time, Pallas kernels for 17%

profile of v8, /device:TPU:0, one launch (start us, length us, event | category | flops | bytes accessed | tf_op | source)
XLA Modules:
  0.0 82.4 jit_solution(9787516236868605989)
XLA Ops:
  0.0 2.9 %collective-permute-start.9 = (bf16[256,1024]{1,0:T(8,128)(2,1)}, bf16[256,1024]{1,0:T(8,128)(2,1)S(1)}, u32[]{:S(2)}, u32[]{:S(2)}) collective-permute-start(bf16[256,1024]{1,0:T(8,128)(2,1)} %refs_6_), channel_id=1, source_target_pairs={{0,2},{1,3},{2,0},{3,1},{4,6},{5,7},{6,4},{7,5},{8,10},{9,11},{10,... | collective-permute-start | bytes 1572872 | tf_op jit(solution)/shard_map/ppermute | solution.py:354
  2.9 0.1 pad_add_fusion.ids.refs_0_
  3.0 1.8 %query.1 = (bf16[256,256]{1,0:T(8,128)(2,1)S(1)}, bf16[2,512,256]{2,1,0:T(8,128)(2,1)S(1)}) custom-call(bf16[256,1024]{1,0:T(8,128)(2,1)} %refs_1_.1, bf16[1024,256]{1,0:T(8,128)(2,1)} %weight.1, bf16[2,512,256]{2,1,0:T(8,128)(2,1)} %bitcast.39), custom_call_target="tpu_custom_call" | custom-call | tf_op jit(solution)/shard_map/query/pallas_call | solution.py:60
  4.8 0.0 copy-start.3
  4.8 0.0 copy-start.5
  4.9 0.0 copy-start.2
  4.9 2.6 %collective-permute-start.1 = (bf16[256,256]{1,0:T(8,128)(2,1)S(1)}, bf16[256,256]{1,0:T(8,128)(2,1)S(1)}, u32[]{:S(2)}, u32[]{:S(2)}) collective-permute-start(bf16[256,256]{1,0:T(8,128)(2,1)S(1)} %get-tuple-element.46.queries), channel_id=1, source_target_pairs={{0,8},{1,9},{2,10},{3,11},{4,12},{5,13},{6,14},{7,15},{8,0},{9,1},... | collective-permute-start | bytes 393224 | tf_op jit(solution)/shard_map/ppermute | solution.py:354
  7.5 1.6 %collective-permute-start = (bf16[256,256]{1,0:T(8,128)(2,1)S(1)}, bf16[256,256]{1,0:T(8,128)(2,1)S(1)}, u32[]{:S(2)}, u32[]{:S(2)}) collective-permute-start(bf16[256,256]{1,0:T(8,128)(2,1)S(1)} %get-tuple-element.46.queries), channel_id=1, source_target_pairs={{0,4},{1,5},{2,6},{3,7},{4,0},{5,1},{6,2},{7,3},{8,12},{9,13},{10,... | collective-permute-start | bytes 393224 | tf_op jit(solution)/shard_map/ppermute | solution.py:354
  9.1 0.8 attend.4.refs_0_
  9.9 3.8 %collective-permute-done.1.queries = bf16[256,256]{1,0:T(8,128)(2,1)S(1)} collective-permute-done((bf16[256,256]{1,0:T(8,128)(2,1)S(1)}, bf16[256,256]{1,0:T(8,128)(2,1)S(1)}, u32[]{:S(2)}, u32[]{:S(2)}) %collective-permute-start.1) | collective-permute-done | bytes 131104 | tf_op jit(solution)/shard_map/ppermute | solution.py:354
  13.7 0.6 collective-permute-start.4
  14.3 0.8 attend.5
  15.1 3.4 %collective-permute-start.3 = (bf16[256,256]{1,0:T(8,128)(2,1)S(1)}, bf16[256,256]{1,0:T(8,128)(2,1)S(1)}, u32[]{:S(2)}, u32[]{:S(2)}) collective-permute-start(bf16[256,256]{1,0:T(8,128)(2,1)S(1)} %attend.5), channel_id=1, source_target_pairs={{0,8},{1,9},{2,10},{3,11},{4,12},{5,13},{6,14},{7,15},{8,0},{9,1},... | collective-permute-start | bytes 393224 | tf_op jit(solution)/shard_map/ppermute | solution.py:354
  18.5 0.8 attend.6
  19.3 0.1 collective-permute-start.2
  19.4 0.0 collective-permute-done.4.queries
  19.4 0.8 attend.7
  20.2 0.0 copy-start.4
  20.2 5.7 %collective-permute-start.5 = (bf16[256,256]{1,0:T(8,128)(2,1)S(1)}, bf16[256,256]{1,0:T(8,128)(2,1)S(1)}, u32[]{:S(2)}, u32[]{:S(2)}) collective-permute-start(bf16[256,256]{1,0:T(8,128)(2,1)S(1)} %attend.7), channel_id=1, source_target_pairs={{0,12},{1,13},{2,14},{3,15},{4,8},{5,9},{6,10},{7,11},{8,4},{9,5},... | collective-permute-start | bytes 393224 | tf_op jit(solution)/shard_map/ppermute | solution.py:354
  26.5 2.8 %collective-permute-done.5.refs_3_ = bf16[256,256]{1,0:T(8,128)(2,1)S(1)} collective-permute-done((bf16[256,256]{1,0:T(8,128)(2,1)S(1)}, bf16[256,256]{1,0:T(8,128)(2,1)S(1)}, u32[]{:S(2)}, u32[]{:S(2)}) %collective-permute-start.5) | collective-permute-done | bytes 131104 | tf_op jit(solution)/shard_map/ppermute | solution.py:354
  29.3 0.6 pick.1.refs_2_
  29.9 0.1 collective-permute-start.10
  30.0 0.5 collective-permute-start.11
  30.5 0.5 collective-permute-start.6
  31.1 1.5 %route.1 = (s32[256,2]{1,0:T(8,128)S(1)}, bf16[192,256]{1,0:T(8,128)(2,1)S(1)}, bf16[192,256]{1,0:T(8,128)(2,1)S(1)}, bf16[192,256]{1,0:T(8,128)(2,1)S(1)}, bf16...) custom-call(s32[2]{0:T(128)S(1)} %pad_add_fusion.ids.refs_0_, ...), custom_call_target="tpu_custom_call" | custom-call | tf_op jit(solution)/shard_map/route/pallas_call | solution.py:171
  32.6 0.1 collective-permute-start.7
  32.6 3.4 %collective-permute-done.6.refs_3_ = bf16[256,256]{1,0:T(8,128)(2,1)S(1)} collective-permute-done((bf16[256,256]{1,0:T(8,128)(2,1)S(1)}, bf16[256,256]{1,0:T(8,128)(2,1)S(1)}, u32[]{:S(2)}, u32[]{:S(2)}) %collective-permute-start.6) | collective-permute-done | bytes 131104 | tf_op jit(solution)/shard_map/ppermute | solution.py:354
  36.0 1.3 %collective-permute-done.8.refs_5_ = bf16[256,256]{1,0:T(8,128)(2,1)S(1)} collective-permute-done((bf16[256,256]{1,0:T(8,128)(2,1)S(1)}, bf16[256,256]{1,0:T(8,128)(2,1)S(1)}, u32[]{:S(2)}, u32[]{:S(2)}) %collective-permute-start.8) | collective-permute-done | bytes 131104 | tf_op jit(solution)/shard_map/ppermute | solution.py:354
  37.4 0.0 copy-start
  37.4 0.0 copy-start.1
  37.4 1.5 %state.1 = (bf16[256,1024]{1,0:T(8,128)(2,1)S(1)}, bf16[192,256]{1,0:T(8,128)(2,1)S(1)}, bf16[192,256]{1,0:T(8,128)(2,1)S(1)}, bf16[192,512]{1,0:T(8,128)(2,1)S(1)}) custom-call(s32[2]{0:T(128)S(1)} %pad_add_fusion.ids.refs_0_, bf16[256,1024]{1,0:T(8,128)(2,1)S(1)} %copy-done.2, bf16[256,256]{1,0:T(8,128)(2,1)S(1)} %pick.1.refs_2_, ...), custom_call_target="tpu_custom_call" | custom-call | tf_op jit(solution)/shard_map/state/pallas_call | solution.py:201
  38.9 2.6 %collective-permute-start.12 = (bf16[192,256]{1,0:T(8,128)(2,1)S(1)}, bf16[192,256]{1,0:T(8,128)(2,1)S(1)}, u32[]{:S(2)}, u32[]{:S(2)}) collective-permute-start(bf16[192,256]{1,0:T(8,128)(2,1)S(1)} %get-tuple-element.69), channel_id=1, source_target_pairs={{0,8},{1,9},{2,10},{3,11},{4,12},{5,13},{6,14},{7,15},{8,0},{9,1},... | collective-permute-start | bytes 294920 | tf_op jit(solution)/shard_map/ppermute | solution.py:354
  41.5 1.4 %collective-permute-start.25 = (bf16[192,256]{1,0:T(8,128)(2,1)S(1)}, bf16[192,256]{1,0:T(8,128)(2,1)S(1)}, u32[]{:S(2)}, u32[]{:S(2)}) collective-permute-start(bf16[192,256]{1,0:T(8,128)(2,1)S(1)} %get-tuple-element.82), channel_id=1, source_target_pairs={{0,12},{1,13},{2,14},{3,15},{4,8},{5,9},{6,10},{7,11},{8,4},{9,5},... | collective-permute-start | bytes 294920 | tf_op jit(solution)/shard_map/ppermute | solution.py:354
  42.9 0.0 collective-permute-start.18
  42.9 1.0 %home.1 = (bf16[192,512]{1,0:T(8,128)(2,1)S(1)}, bf16[192,512]{1,0:T(8,128)(2,1)S(1)}, f32[256,2]{1,0:T(8,128)S(1)}, f32[256,256]{1,0:T(8,128)S(1)}) custom-call(s32[2]{0:T(128)S(1)} %pad_add_fusion.ids.refs_0_, bf16[256,1024]{1,0:T(8,128)(2,1)S(1)} %get-tuple-element.59.state, bf16[192,256]{1,0:T(8,128)(2,1)S(1)} %get-tuple-element.52.dispatch, ...), custom_call_target="tpu_custom_call" | custom-call | tf_op jit(solution)/shard_map/home/pallas_call | solution.py:231
  44.0 1.5 %expert.3 = (f32[2,192,256]{2,1,0:T(8,128)S(1)}, bf16[2,192,256]{2,1,0:T(8,128)(2,1)S(1)}) custom-call(s32[2]{0:T(128)S(1)} %pad_add_fusion.ids.refs_0_, bf16[192,512]{1,0:T(8,128)(2,1)S(1)} %get-tuple-element.65.refs_1_, bf16[192,512]{1,0:T(8,128)(2,1)S(1)} %get-tuple-element.66.refs_2_, bf16[1024,1024]{1,0:T(8,128)(2,1)S(1)} %bitcast.31, ...), custom_call_target="tpu_custom_call" | custom-call | tf_op jit(solution)/shard_map/expert/pallas_call | solution.py:279
  45.5 4.2 %collective-permute-done.12.refs_1_ = bf16[192,256]{1,0:T(8,128)(2,1)S(1)} collective-permute-done((bf16[192,256]{1,0:T(8,128)(2,1)S(1)}, bf16[192,256]{1,0:T(8,128)(2,1)S(1)}, u32[]{:S(2)}, u32[]{:S(2)}) %collective-permute-start.12) | collective-permute-done | bytes 98336 | tf_op jit(solution)/shard_map/ppermute | solution.py:354
  49.8 0.5 collective-permute-start.15
  50.3 1.5 %collective-permute-start.26 = (bf16[192,256]{1,0:T(8,128)(2,1)S(1)}, bf16[192,256]{1,0:T(8,128)(2,1)S(1)}, u32[]{:S(2)}, u32[]{:S(2)}) collective-permute-start(bf16[192,256]{1,0:T(8,128)(2,1)S(1)} %collective-permute-done.25.refs_1_), channel_id=1, source_target_pairs={{0,2},{1,3},{2,0},{3,1},{4,6},{5,7},{6,4},{7,5},{8,10},{9,11},{10,... | collective-permute-start | bytes 294920 | tf_op jit(solution)/shard_map/ppermute | solution.py:354
  51.8 0.6 collective-permute-done.18.refs_5_
  52.4 3.0 %collective-permute-done.15.refs_2_ = bf16[192,256]{1,0:T(8,128)(2,1)S(1)} collective-permute-done((bf16[192,256]{1,0:T(8,128)(2,1)S(1)}, bf16[192,256]{1,0:T(8,128)(2,1)S(1)}, u32[]{:S(2)}, u32[]{:S(2)}) %collective-permute-start.15) | collective-permute-done | bytes 98336 | tf_op jit(solution)/shard_map/ppermute | solution.py:354
  55.4 1.7 %collective-permute-done.26.refs_2_ = bf16[192,256]{1,0:T(8,128)(2,1)S(1)} collective-permute-done((bf16[192,256]{1,0:T(8,128)(2,1)S(1)}, bf16[192,256]{1,0:T(8,128)(2,1)S(1)}, u32[]{:S(2)}, u32[]{:S(2)}) %collective-permute-start.26) | collective-permute-done | bytes 98336 | tf_op jit(solution)/shard_map/ppermute | solution.py:354
  57.1 0.5 collective-permute-start.28
  57.7 0.7 collective-permute-done.17.refs_4_
  58.4 2.4 %expert.4 = (f32[2,384,256]{2,1,0:T(8,128)S(1)}, bf16[2,384,256]{2,1,0:T(8,128)(2,1)S(1)}) custom-call(s32[2]{0:T(128)S(1)} %pad_add_fusion.ids.refs_0_, bf16[192,256]{1,0:T(8,128)(2,1)S(1)} %collective-permute-done.12.refs_1_, bf16[192,256]{1,0:T(8,128)(2,1)S(1)} %collective-permute-done.15.refs_2_, bf16[192,256]{1,0:T(8,128)(2,1)S(1)} %collective-permute-done.16.refs_3_, ...), custom_call_target="tpu_custom_call" | custom-call | tf_op jit(solution)/shard_map/expert/pallas_call | solution.py:279
  60.8 0.2 collective-permute-start.20
  61.1 1.6 %expert.5 = (f32[2,192,256]{2,1,0:T(8,128)S(1)}, bf16[2,192,256]{2,1,0:T(8,128)(2,1)S(1)}) custom-call(s32[2]{0:T(128)S(1)} %pad_add_fusion.ids.refs_0_, bf16[192,256]{1,0:T(8,128)(2,1)S(1)} %collective-permute-done.25.refs_1_, bf16[192,256]{1,0:T(8,128)(2,1)S(1)} %collective-permute-done.26.refs_2_, bf16[192,256]{1,0:T(8,128)(2,1)S(1)} %collective-permute-done.27.refs_3_, ...), custom_call_target="tpu_custom_call" | custom-call | tf_op jit(solution)/shard_map/expert/pallas_call | solution.py:279
  62.6 0.4 collective-permute-start.29
  63.1 0.6 collective-permute-start.14
  63.7 0.5 collective-permute-done.29
  64.2 0.1 fusion.5
  64.3 1.1 %collective-permute-start.23 = (bf16[192,256]{1,0:T(8,128)(2,1)S(1)}, bf16[192,256]{1,0:T(8,128)(2,1)S(1)}, u32[]{:S(2)}, u32[]{:S(2)}) collective-permute-start(bf16[192,256]{1,0:T(8,128)(2,1)S(1)} %get-tuple-element.87), channel_id=1, source_target_pairs={{0,2},{1,3},{2,0},{3,1},{4,6},{5,7},{6,4},{7,5},{8,10},{9,11},{10,... | collective-permute-start | bytes 294920 | tf_op jit(solution)/shard_map/ppermute | solution.py:354
  65.4 1.1 %collective-permute-start.30 = (bf16[192,256]{1,0:T(8,128)(2,1)S(1)}, bf16[192,256]{1,0:T(8,128)(2,1)S(1)}, u32[]{:S(2)}, u32[]{:S(2)}) collective-permute-start(bf16[192,256]{1,0:T(8,128)(2,1)S(1)} %fusion.4), channel_id=1, source_target_pairs={{0,2},{1,3},{2,0},{3,1},{4,6},{5,7},{6,4},{7,5},{8,10},{9,11},{10,... | collective-permute-start | bytes 294920 | tf_op jit(solution)/shard_map/ppermute | solution.py:354
  66.5 0.3 collective-permute-start.22
  66.8 2.1 %collective-permute-start.21 = (bf16[192,256]{1,0:T(8,128)(2,1)S(1)}, bf16[192,256]{1,0:T(8,128)(2,1)S(1)}, u32[]{:S(2)}, u32[]{:S(2)}) collective-permute-start(bf16[192,256]{1,0:T(8,128)(2,1)S(1)} %get-tuple-element.89), channel_id=1, source_target_pairs={{0,4},{1,5},{2,6},{3,7},{4,0},{5,1},{6,2},{7,3},{8,12},{9,13},{10,... | collective-permute-start | bytes 294920 | tf_op jit(solution)/shard_map/ppermute | solution.py:354
  69.0 3.7 %collective-permute-done.23 = bf16[192,256]{1,0:T(8,128)(2,1)S(1)} collective-permute-done((bf16[192,256]{1,0:T(8,128)(2,1)S(1)}, bf16[192,256]{1,0:T(8,128)(2,1)S(1)}, u32[]{:S(2)}, u32[]{:S(2)}) %collective-permute-start.23) | collective-permute-done | bytes 98336 | tf_op jit(solution)/shard_map/ppermute | solution.py:354
  72.7 1.4 %collective-permute-start.24 = (bf16[192,256]{1,0:T(8,128)(2,1)S(1)}, bf16[192,256]{1,0:T(8,128)(2,1)S(1)}, u32[]{:S(2)}, u32[]{:S(2)}) collective-permute-start(bf16[192,256]{1,0:T(8,128)(2,1)S(1)} %fusion.3), channel_id=1, source_target_pairs={{0,8},{1,9},{2,10},{3,11},{4,12},{5,13},{6,14},{7,15},{8,0},{9,1},... | collective-permute-start | bytes 294920 | tf_op jit(solution)/shard_map/ppermute | solution.py:354
  74.1 0.2 collective-permute-done.30
  74.3 2.8 %collective-permute-start.31 = (bf16[192,256]{1,0:T(8,128)(2,1)S(1)}, bf16[192,256]{1,0:T(8,128)(2,1)S(1)}, u32[]{:S(2)}, u32[]{:S(2)}) collective-permute-start(bf16[192,256]{1,0:T(8,128)(2,1)S(1)} %fusion.1), channel_id=1, source_target_pairs={{0,12},{1,13},{2,14},{3,15},{4,8},{5,9},{6,10},{7,11},{8,4},{9,5},... | collective-permute-start | bytes 294920 | tf_op jit(solution)/shard_map/ppermute | solution.py:354
  77.1 0.2 combine.4.base
  77.4 0.2 combine.5.base
  77.6 3.6 %collective-permute-done.24.refs_0_ = bf16[192,256]{1,0:T(8,128)(2,1)S(1)} collective-permute-done((bf16[192,256]{1,0:T(8,128)(2,1)S(1)}, bf16[192,256]{1,0:T(8,128)(2,1)S(1)}, u32[]{:S(2)}, u32[]{:S(2)}) %collective-permute-start.24) | collective-permute-done | bytes 98336 | tf_op jit(solution)/shard_map/ppermute | solution.py:354
  81.2 0.2 combine.6.base
  81.5 0.9 %combine.7 = bf16[256,256]{1,0:T(8,128)(2,1)} custom-call(f32[256,2]{1,0:T(8,128)S(1)} %get-tuple-element.61.gates, f32[256,256]{1,0:T(8,128)S(1)} %combine.6.base, bf16[256,192]{1,0:T(8,128)(2,1)S(1)} %get-tuple-element.79.first, bf16[256,192]{1,0:T(8,128)(2,1)S(1)} %get-tuple-element.80.second, bf16[192,256]{1,0:T(8,128)(2,1)S(1)} %collective-permute-done.31.refs_0_), custom_call_target="tpu_custom_call" | custom-call | tf_op jit(solution)/shard_map/combine/pallas_call | solution.py:305
  (37 shorter events, 0.2 us)
Async XLA Ops:
  0.0 30.0 %collective-permute-start.9 = (bf16[256,1024]{1,0:T(8,128)(2,1)}, bf16[256,1024]{1,0:T(8,128)(2,1)S(1)}, u32[]{:S(2)}, u32[]{:S(2)}) collective-permute-start(bf16[256,1024]{1,0:T(8,128)(2,1)} %refs_6_), channel_id=1, source_target_pairs={{0,2},{1,3},{2,0},{3,1},{4,6},{5,7},{6,4},{7,5},{8,10},{9,11},{10,... | collective-permute-start | bytes 1572872 | tf_op jit(solution)/shard_map/ppermute | solution.py:354
  4.8 25.1 %copy-start.3 = (bf16[256,1024]{1,0:T(8,128)(2,1)S(1)}, bf16[256,1024]{1,0:T(8,128)(2,1)}, u32[]{:S(2)}) copy-start(bf16[256,1024]{1,0:T(8,128)(2,1)} %refs_6_) | copy-start | bytes 1572868
  4.8 26.2 %copy-start.5 = (s32[256,2]{0,1:T(2,128)S(1)}, s32[256,2]{0,1:T(2,128)}, u32[]{:S(2)}) copy-start(s32[256,2]{0,1:T(2,128)} %param.15) | copy-start | bytes 6148
  4.9 32.5 %copy-start.2 = (bf16[256,1024]{1,0:T(8,128)(2,1)S(1)}, bf16[256,1024]{1,0:T(8,128)(2,1)}, u32[]{:S(2)}) copy-start(bf16[256,1024]{1,0:T(8,128)(2,1)} %refs_1_.1) | copy-start | bytes 1572868
  4.9 8.8 %collective-permute-start.1 = (bf16[256,256]{1,0:T(8,128)(2,1)S(1)}, bf16[256,256]{1,0:T(8,128)(2,1)S(1)}, u32[]{:S(2)}, u32[]{:S(2)}) collective-permute-start(bf16[256,256]{1,0:T(8,128)(2,1)S(1)} %get-tuple-element.46.queries), channel_id=1, source_target_pairs={{0,8},{1,9},{2,10},{3,11},{4,12},{5,13},{6,14},{7,15},{8,0},{9,1},... | collective-permute-start | bytes 393224 | tf_op jit(solution)/shard_map/ppermute | solution.py:354
  7.5 11.0 %collective-permute-start = (bf16[256,256]{1,0:T(8,128)(2,1)S(1)}, bf16[256,256]{1,0:T(8,128)(2,1)S(1)}, u32[]{:S(2)}, u32[]{:S(2)}) collective-permute-start(bf16[256,256]{1,0:T(8,128)(2,1)S(1)} %get-tuple-element.46.queries), channel_id=1, source_target_pairs={{0,4},{1,5},{2,6},{3,7},{4,0},{5,1},{6,2},{7,3},{8,12},{9,13},{10,... | collective-permute-start | bytes 393224 | tf_op jit(solution)/shard_map/ppermute | solution.py:354
  13.7 5.7 %collective-permute-start.4 = (bf16[256,256]{1,0:T(8,128)(2,1)S(1)}, bf16[256,256]{1,0:T(8,128)(2,1)S(1)}, u32[]{:S(2)}, u32[]{:S(2)}) collective-permute-start(bf16[256,256]{1,0:T(8,128)(2,1)S(1)} %collective-permute-done.1.queries), channel_id=1, source_target_pairs={{0,4},{1,5},{2,6},{3,7},{4,0},{5,1},{6,2},{7,3},{8,12},{9,13},{10,... | collective-permute-start | bytes 393224 | tf_op jit(solution)/shard_map/ppermute | solution.py:354
  15.1 11.4 %collective-permute-start.3 = (bf16[256,256]{1,0:T(8,128)(2,1)S(1)}, bf16[256,256]{1,0:T(8,128)(2,1)S(1)}, u32[]{:S(2)}, u32[]{:S(2)}) collective-permute-start(bf16[256,256]{1,0:T(8,128)(2,1)S(1)} %attend.5), channel_id=1, source_target_pairs={{0,8},{1,9},{2,10},{3,11},{4,12},{5,13},{6,14},{7,15},{8,0},{9,1},... | collective-permute-start | bytes 393224 | tf_op jit(solution)/shard_map/ppermute | solution.py:354
  19.3 7.2 %collective-permute-start.2 = (bf16[256,256]{1,0:T(8,128)(2,1)S(1)}, bf16[256,256]{1,0:T(8,128)(2,1)S(1)}, u32[]{:S(2)}, u32[]{:S(2)}) collective-permute-start(bf16[256,256]{1,0:T(8,128)(2,1)S(1)} %attend.6), channel_id=1, source_target_pairs={{0,4},{1,5},{2,6},{3,7},{4,0},{5,1},{6,2},{7,3},{8,12},{9,13},{10,... | collective-permute-start | bytes 393224 | tf_op jit(solution)/shard_map/ppermute | solution.py:354
  20.2 22.8 %copy-start.4 = (bf16[1024,4]{0,1:T(4,128)(2,1)S(1)}, bf16[1024,4]{0,1:T(4,128)(2,1)}, u32[]{:S(2)}) copy-start(bf16[1024,4]{0,1:T(4,128)(2,1)} %param.14) | copy-start | bytes 24580
  20.2 9.2 %collective-permute-start.5 = (bf16[256,256]{1,0:T(8,128)(2,1)S(1)}, bf16[256,256]{1,0:T(8,128)(2,1)S(1)}, u32[]{:S(2)}, u32[]{:S(2)}) collective-permute-start(bf16[256,256]{1,0:T(8,128)(2,1)S(1)} %attend.7), channel_id=1, source_target_pairs={{0,12},{1,13},{2,14},{3,15},{4,8},{5,9},{6,10},{7,11},{8,4},{9,5},... | collective-permute-start | bytes 393224 | tf_op jit(solution)/shard_map/ppermute | solution.py:354
  29.9 7.4 %collective-permute-start.10 = (bf16[256,1024]{1,0:T(8,128)(2,1)S(1)}, bf16[256,1024]{1,0:T(8,128)(2,1)S(1)}, u32[]{:S(2)}, u32[]{:S(2)}) collective-permute-start(bf16[256,1024]{1,0:T(8,128)(2,1)S(1)} %copy-done.3), channel_id=1, source_target_pairs={{0,1},{1,0},{2,3},{3,2},{4,5},{5,4},{6,7},{7,6},{8,9},{9,8},{10,11... | collective-permute-start | bytes 1572872 | tf_op jit(solution)/shard_map/ppermute | solution.py:354
  30.0 7.3 %collective-permute-start.11 = (bf16[256,1024]{1,0:T(8,128)(2,1)S(1)}, bf16[256,1024]{1,0:T(8,128)(2,1)S(1)}, u32[]{:S(2)}, u32[]{:S(2)}) collective-permute-start(bf16[256,1024]{1,0:T(8,128)(2,1)S(1)} %collective-permute-done.9.refs_7_), channel_id=1, source_target_pairs={{0,1},{1,0},{2,3},{3,2},{4,5},{5,4},{6,7},{7,6},{8,9},{9,8},{10,11... | collective-permute-start | bytes 1572872 | tf_op jit(solution)/shard_map/ppermute | solution.py:354
  30.5 5.5 %collective-permute-start.6 = (bf16[256,256]{1,0:T(8,128)(2,1)S(1)}, bf16[256,256]{1,0:T(8,128)(2,1)S(1)}, u32[]{:S(2)}, u32[]{:S(2)}) collective-permute-start(bf16[256,256]{1,0:T(8,128)(2,1)S(1)} %pick.1.refs_2_), channel_id=1, source_target_pairs={{0,2},{1,3},{2,0},{3,1},{4,6},{5,7},{6,4},{7,5},{8,10},{9,11},{10,... | collective-permute-start | bytes 393224 | tf_op jit(solution)/shard_map/ppermute | solution.py:354
  32.6 3.5 %collective-permute-start.7 = (bf16[256,256]{1,0:T(8,128)(2,1)S(1)}, bf16[256,256]{1,0:T(8,128)(2,1)S(1)}, u32[]{:S(2)}, u32[]{:S(2)}) collective-permute-start(bf16[256,256]{1,0:T(8,128)(2,1)S(1)} %pick.1.refs_2_), channel_id=1, source_target_pairs={{0,1},{1,0},{2,3},{3,2},{4,5},{5,4},{6,7},{7,6},{8,9},{9,8},{10,11... | collective-permute-start | bytes 393224 | tf_op jit(solution)/shard_map/ppermute | solution.py:354
  36.0 1.3 %collective-permute-start.8 = (bf16[256,256]{1,0:T(8,128)(2,1)S(1)}, bf16[256,256]{1,0:T(8,128)(2,1)S(1)}, u32[]{:S(2)}, u32[]{:S(2)}) collective-permute-start(bf16[256,256]{1,0:T(8,128)(2,1)S(1)} %collective-permute-done.6.refs_3_), channel_id=1, source_target_pairs={{0,1},{1,0},{2,3},{3,2},{4,5},{5,4},{6,7},{7,6},{8,9},{9,8},{10,11... | collective-permute-start | bytes 393224 | tf_op jit(solution)/shard_map/ppermute | solution.py:354
  37.4 6.6 %copy-start = (bf16[1,1024,1024]{2,1,0:T(8,128)(2,1)S(1)}, bf16[1,1024,1024]{2,1,0:T(8,128)(2,1)}, u32[]{:S(2)}) copy-start(bf16[1,1024,1024]{2,1,0:T(8,128)(2,1)} %param.16) | copy-start | bytes 6291460
  37.4 6.6 %copy-start.1 = (bf16[1,1024,1024]{2,1,0:T(8,128)(2,1)S(1)}, bf16[1,1024,1024]{2,1,0:T(8,128)(2,1)}, u32[]{:S(2)}) copy-start(bf16[1,1024,1024]{2,1,0:T(8,128)(2,1)} %param.17) | copy-start | bytes 6291460
  38.9 10.9 %collective-permute-start.12 = (bf16[192,256]{1,0:T(8,128)(2,1)S(1)}, bf16[192,256]{1,0:T(8,128)(2,1)S(1)}, u32[]{:S(2)}, u32[]{:S(2)}) collective-permute-start(bf16[192,256]{1,0:T(8,128)(2,1)S(1)} %get-tuple-element.69), channel_id=1, source_target_pairs={{0,8},{1,9},{2,10},{3,11},{4,12},{5,13},{6,14},{7,15},{8,0},{9,1},... | collective-permute-start | bytes 294920 | tf_op jit(solution)/shard_map/ppermute | solution.py:354
  41.5 8.8 %collective-permute-start.25 = (bf16[192,256]{1,0:T(8,128)(2,1)S(1)}, bf16[192,256]{1,0:T(8,128)(2,1)S(1)}, u32[]{:S(2)}, u32[]{:S(2)}) collective-permute-start(bf16[192,256]{1,0:T(8,128)(2,1)S(1)} %get-tuple-element.82), channel_id=1, source_target_pairs={{0,12},{1,13},{2,14},{3,15},{4,8},{5,9},{6,10},{7,11},{8,4},{9,5},... | collective-permute-start | bytes 294920 | tf_op jit(solution)/shard_map/ppermute | solution.py:354
  42.9 9.5 %collective-permute-start.18 = (bf16[192,512]{1,0:T(8,128)(2,1)S(1)}, bf16[192,512]{1,0:T(8,128)(2,1)S(1)}, u32[]{:S(2)}, u32[]{:S(2)}) collective-permute-start(bf16[192,512]{1,0:T(8,128)(2,1)S(1)} %get-tuple-element.74), channel_id=1, source_target_pairs={{0,4},{1,5},{2,6},{3,7},{4,0},{5,1},{6,2},{7,3},{8,12},{9,13},{10,... | collective-permute-start | bytes 589832 | tf_op jit(solution)/shard_map/ppermute | solution.py:354
  49.8 7.3 %collective-permute-start.13 = (bf16[2,192,256]{2,1,0:T(8,128)(2,1)S(1)}, bf16[2,192,256]{2,1,0:T(8,128)(2,1)S(1)}, u32[]{:S(2)}, u32[]{:S(2)}) collective-permute-start(bf16[2,192,256]{2,1,0:T(8,128)(2,1)S(1)} %get-tuple-element.70), channel_id=1, source_target_pairs={{0,1},{1,0},{2,3},{3,2},{4,5},{5,4},{6,7},{7,6},{8,9},{9,8},{10,11... | collective-permute-start | bytes 589832 | tf_op jit(solution)/shard_map/ppermute | solution.py:354
  49.8 5.6 %collective-permute-start.15 = (bf16[192,256]{1,0:T(8,128)(2,1)S(1)}, bf16[192,256]{1,0:T(8,128)(2,1)S(1)}, u32[]{:S(2)}, u32[]{:S(2)}) collective-permute-start(bf16[192,256]{1,0:T(8,128)(2,1)S(1)} %collective-permute-done.12.refs_1_), channel_id=1, source_target_pairs={{0,2},{1,3},{2,0},{3,1},{4,6},{5,7},{6,4},{7,5},{8,10},{9,11},{10,... | collective-permute-start | bytes 294920 | tf_op jit(solution)/shard_map/ppermute | solution.py:354
  50.3 6.8 %collective-permute-start.26 = (bf16[192,256]{1,0:T(8,128)(2,1)S(1)}, bf16[192,256]{1,0:T(8,128)(2,1)S(1)}, u32[]{:S(2)}, u32[]{:S(2)}) collective-permute-start(bf16[192,256]{1,0:T(8,128)(2,1)S(1)} %collective-permute-done.25.refs_1_), channel_id=1, source_target_pairs={{0,2},{1,3},{2,0},{3,1},{4,6},{5,7},{6,4},{7,5},{8,10},{9,11},{10,... | collective-permute-start | bytes 294920 | tf_op jit(solution)/shard_map/ppermute | solution.py:354
  51.8 5.8 %collective-permute-start.16 = (bf16[192,256]{1,0:T(8,128)(2,1)S(1)}, bf16[192,256]{1,0:T(8,128)(2,1)S(1)}, u32[]{:S(2)}, u32[]{:S(2)}) collective-permute-start(bf16[192,256]{1,0:T(8,128)(2,1)S(1)} %collective-permute-done.12.refs_1_), channel_id=1, source_target_pairs={{0,1},{1,0},{2,3},{3,2},{4,5},{5,4},{6,7},{7,6},{8,9},{9,8},{10,11... | collective-permute-start | bytes 294920 | tf_op jit(solution)/shard_map/ppermute | solution.py:354
  52.4 8.6 %collective-permute-start.27 = (bf16[192,256]{1,0:T(8,128)(2,1)S(1)}, bf16[192,256]{1,0:T(8,128)(2,1)S(1)}, u32[]{:S(2)}, u32[]{:S(2)}) collective-permute-start(bf16[192,256]{1,0:T(8,128)(2,1)S(1)} %collective-permute-done.25.refs_1_), channel_id=1, source_target_pairs={{0,1},{1,0},{2,3},{3,2},{4,5},{5,4},{6,7},{7,6},{8,9},{9,8},{10,11... | collective-permute-start | bytes 294920 | tf_op jit(solution)/shard_map/ppermute | solution.py:354
  55.4 3.0 %collective-permute-start.19 = (bf16[192,512]{1,0:T(8,128)(2,1)S(1)}, bf16[192,512]{1,0:T(8,128)(2,1)S(1)}, u32[]{:S(2)}, u32[]{:S(2)}) collective-permute-start(bf16[192,512]{1,0:T(8,128)(2,1)S(1)} %collective-permute-done.18.refs_5_), channel_id=1, source_target_pairs={{0,1},{1,0},{2,3},{3,2},{4,5},{5,4},{6,7},{7,6},{8,9},{9,8},{10,11... | collective-permute-start | bytes 589832 | tf_op jit(solution)/shard_map/ppermute | solution.py:354
  57.1 1.3 %collective-permute-start.17 = (bf16[192,256]{1,0:T(8,128)(2,1)S(1)}, bf16[192,256]{1,0:T(8,128)(2,1)S(1)}, u32[]{:S(2)}, u32[]{:S(2)}) collective-permute-start(bf16[192,256]{1,0:T(8,128)(2,1)S(1)} %collective-permute-done.15.refs_2_), channel_id=1, source_target_pairs={{0,1},{1,0},{2,3},{3,2},{4,5},{5,4},{6,7},{7,6},{8,9},{9,8},{10,11... | collective-permute-start | bytes 294920 | tf_op jit(solution)/shard_map/ppermute | solution.py:354
  57.1 3.9 %collective-permute-start.28 = (bf16[192,256]{1,0:T(8,128)(2,1)S(1)}, bf16[192,256]{1,0:T(8,128)(2,1)S(1)}, u32[]{:S(2)}, u32[]{:S(2)}) collective-permute-start(bf16[192,256]{1,0:T(8,128)(2,1)S(1)} %collective-permute-done.26.refs_2_), channel_id=1, source_target_pairs={{0,1},{1,0},{2,3},{3,2},{4,5},{5,4},{6,7},{7,6},{8,9},{9,8},{10,11... | collective-permute-start | bytes 294920 | tf_op jit(solution)/shard_map/ppermute | solution.py:354
  60.8 3.3 %collective-permute-start.20 = (bf16[2,384,256]{2,1,0:T(8,128)(2,1)S(1)}, bf16[2,384,256]{2,1,0:T(8,128)(2,1)S(1)}, u32[]{:S(2)}, u32[]{:S(2)}) collective-permute-start(bf16[2,384,256]{2,1,0:T(8,128)(2,1)S(1)} %get-tuple-element.76), channel_id=1, source_target_pairs={{0,1},{1,0},{2,3},{3,2},{4,5},{5,4},{6,7},{7,6},{8,9},{9,8},{10,11... | collective-permute-start | bytes 1179656 | tf_op jit(solution)/shard_map/ppermute | solution.py:354
  62.6 1.5 %collective-permute-start.29 = (bf16[2,192,256]{2,1,0:T(8,128)(2,1)S(1)}, bf16[2,192,256]{2,1,0:T(8,128)(2,1)S(1)}, u32[]{:S(2)}, u32[]{:S(2)}) collective-permute-start(bf16[2,192,256]{2,1,0:T(8,128)(2,1)S(1)} %get-tuple-element.84), channel_id=1, source_target_pairs={{0,1},{1,0},{2,3},{3,2},{4,5},{5,4},{6,7},{7,6},{8,9},{9,8},{10,11... | collective-permute-start | bytes 589832 | tf_op jit(solution)/shard_map/ppermute | solution.py:354
  63.1 14.0 %collective-permute-start.14 = (bf16[192,256]{1,0:T(8,128)(2,1)S(1)}, bf16[192,256]{1,0:T(8,128)(2,1)S(1)}, u32[]{:S(2)}, u32[]{:S(2)}) collective-permute-start(bf16[192,256]{1,0:T(8,128)(2,1)S(1)} %get-tuple-element.90), channel_id=1, source_target_pairs={{0,2},{1,3},{2,0},{3,1},{4,6},{5,7},{6,4},{7,5},{8,10},{9,11},{10,... | collective-permute-start | bytes 294920 | tf_op jit(solution)/shard_map/ppermute | solution.py:354
  64.3 8.4 %collective-permute-start.23 = (bf16[192,256]{1,0:T(8,128)(2,1)S(1)}, bf16[192,256]{1,0:T(8,128)(2,1)S(1)}, u32[]{:S(2)}, u32[]{:S(2)}) collective-permute-start(bf16[192,256]{1,0:T(8,128)(2,1)S(1)} %get-tuple-element.87), channel_id=1, source_target_pairs={{0,2},{1,3},{2,0},{3,1},{4,6},{5,7},{6,4},{7,5},{8,10},{9,11},{10,... | collective-permute-start | bytes 294920 | tf_op jit(solution)/shard_map/ppermute | solution.py:354
  65.4 8.9 %collective-permute-start.30 = (bf16[192,256]{1,0:T(8,128)(2,1)S(1)}, bf16[192,256]{1,0:T(8,128)(2,1)S(1)}, u32[]{:S(2)}, u32[]{:S(2)}) collective-permute-start(bf16[192,256]{1,0:T(8,128)(2,1)S(1)} %fusion.4), channel_id=1, source_target_pairs={{0,2},{1,3},{2,0},{3,1},{4,6},{5,7},{6,4},{7,5},{8,10},{9,11},{10,... | collective-permute-start | bytes 294920 | tf_op jit(solution)/shard_map/ppermute | solution.py:354
  66.5 10.8 %collective-permute-start.22 = (bf16[192,256]{1,0:T(8,128)(2,1)S(1)}, bf16[192,256]{1,0:T(8,128)(2,1)S(1)}, u32[]{:S(2)}, u32[]{:S(2)}) collective-permute-start(bf16[192,256]{1,0:T(8,128)(2,1)S(1)} %get-tuple-element.88), channel_id=1, source_target_pairs={{0,6},{1,7},{2,4},{3,5},{4,2},{5,3},{6,0},{7,1},{8,14},{9,15},{10,... | collective-permute-start | bytes 294920 | tf_op jit(solution)/shard_map/ppermute | solution.py:354
  66.8 10.5 %collective-permute-start.21 = (bf16[192,256]{1,0:T(8,128)(2,1)S(1)}, bf16[192,256]{1,0:T(8,128)(2,1)S(1)}, u32[]{:S(2)}, u32[]{:S(2)}) collective-permute-start(bf16[192,256]{1,0:T(8,128)(2,1)S(1)} %get-tuple-element.89), channel_id=1, source_target_pairs={{0,4},{1,5},{2,6},{3,7},{4,0},{5,1},{6,2},{7,3},{8,12},{9,13},{10,... | collective-permute-start | bytes 294920 | tf_op jit(solution)/shard_map/ppermute | solution.py:354
  72.7 8.5 %collective-permute-start.24 = (bf16[192,256]{1,0:T(8,128)(2,1)S(1)}, bf16[192,256]{1,0:T(8,128)(2,1)S(1)}, u32[]{:S(2)}, u32[]{:S(2)}) collective-permute-start(bf16[192,256]{1,0:T(8,128)(2,1)S(1)} %fusion.3), channel_id=1, source_target_pairs={{0,8},{1,9},{2,10},{3,11},{4,12},{5,13},{6,14},{7,15},{8,0},{9,1},... | collective-permute-start | bytes 294920 | tf_op jit(solution)/shard_map/ppermute | solution.py:354
  74.3 7.1 %collective-permute-start.31 = (bf16[192,256]{1,0:T(8,128)(2,1)S(1)}, bf16[192,256]{1,0:T(8,128)(2,1)S(1)}, u32[]{:S(2)}, u32[]{:S(2)}) collective-permute-start(bf16[192,256]{1,0:T(8,128)(2,1)S(1)} %fusion.1), channel_id=1, source_target_pairs={{0,12},{1,13},{2,14},{3,15},{4,8},{5,9},{6,10},{7,11},{8,4},{9,5},... | collective-permute-start | bytes 294920 | tf_op jit(solution)/shard_map/ppermute | solution.py:354

commit v9 on v8

--- a/solution.py
+++ b/solution.py
@@ -405,13 +405,16 @@
     def sum_cores(keep, give):
         return keep + hop(give, 0, 1).astype(F32)
 
-    def send_home(k, summed):
-        if k in far:
-            total = summed[0]
-            for j in range(1, pairs):
-                total += hop(summed[j].astype(BF16), 0, 2 * j).astype(F32)
-            return [hop(total.astype(BF16), k, 0)]
+    def sum_slices(summed):
+        total = summed[0]
+        for j in range(1, pairs):
+            total += hop(summed[j].astype(BF16), 0, 2 * j).astype(F32)
+        return total.astype(BF16)
+
+    def send_home(k, summed, wait=None):
         parts = [summed[j].astype(BF16) for j in range(pairs)]
+        if wait is not None:
+            parts = parts[:1] + [after(part, wait) for part in parts[1:]]
         return [hop(part, k, 2 * j) if direct else hop(spread(part), 0, 2 * j) for j, part in enumerate(parts)]
 
     home, order = {}, [0]
@@ -421,7 +424,8 @@
         turn_ids = after(ids, give)
         if sends:
             give = after(give, arrived[sends[0]])
-        home[0] = send_home(0, sum_cores(keep, give))
+        own_sum, wait = sum_cores(keep, give), None
+        turn_ids = after(ids, own_sum)
         turns = [[k for k in sends if k < groups - 1], [groups - 1]] if groups > 2 else [sends]
         for turn in turns:
             blocks, orders = [], []
@@ -437,7 +441,14 @@
                 turn_ids = after(ids, give)
                 summed = sum_cores(keep, give)
                 for i, k in enumerate(turn):
-                    home[k] = send_home(k, summed[:, i * slots : (i + 1) * slots])
+                    rows = summed[:, i * slots : (i + 1) * slots]
+                    if k in far:
+                        total = sum_slices(rows)
+                        wait = total if wait is None else wait
+                        home[k] = [hop(total, k, 0)]
+                    else:
+                        home[k] = send_home(k, rows)
+        home[0] = send_home(0, own_sum, wait)
         order = [0] + sorted(sends)
     else:
         mine = spread(leaving[0])

time: 82.5 us -> 81.9 us (level)
  transfers between devices with their start and end apart: 32 -> 32, of which waited for: 13 -> 15; matrix products, arithmetic and copies ran while one was open for 0% -> 0% of each run, Pallas kernels for 17% -> 17%
where the time goes in v9:
time: 81.9 us; the launch traced here: 81.7 us
  starting transfers between devices  34 us (42%)
  waiting for transfers between devices  29.7 us (36%)
  Pallas kernels  16.7 us (20%)
  between operations  0.98 us (1%)
    ppermute x32, starting transfers between devices, hop(): return lax.ppermute(value, ('expert', 'mp'), moves)  34 us
    ppermute x32, waiting for transfers between devices, hop(): return lax.ppermute(value, ('expert', 'mp'), moves)  29.7 us
    pallas_call x3, Pallas kernels, run_expert(): pl.pallas_call(functools.partial(expert_kernel, tuple(map(tuple, orders))...  5.52 us
    pallas_call x4, Pallas kernels, attend(): pl.pallas_call(attend_kernel, in_specs=[WHOLE] * 2, out_specs=WHOLE, out_...  3.1 us
    pallas_call x1, Pallas kernels, ask(): pl.pallas_call(query_kernel, in_specs=[pl.BlockSpec(memory_space=pltpu.HB...  1.81 us
  transfers between devices with their start and end apart: 32, of which 15 were waited for; matrix products, arithmetic and copies ran while one was open for 0% of the time, Pallas kernels for 17%

profile of v9, /device:TPU:0, one launch (start us, length us, event | category | flops | bytes accessed | tf_op | source)
XLA Modules:
  0.0 81.7 jit_solution(6661219418634498727)
XLA Ops:
  0.0 2.9 %collective-permute-start.9 = (bf16[256,1024]{1,0:T(8,128)(2,1)}, bf16[256,1024]{1,0:T(8,128)(2,1)S(1)}, u32[]{:S(2)}, u32[]{:S(2)}) collective-permute-start(bf16[256,1024]{1,0:T(8,128)(2,1)} %refs_6_), channel_id=1, source_target_pairs={{0,2},{1,3},{2,0},{3,1},{4,6},{5,7},{6,4},{7,5},{8,10},{9,11},{10,... | collective-permute-start | bytes 1572872 | tf_op jit(solution)/shard_map/ppermute | solution.py:354
  2.9 0.1 pad_add_fusion.ids.refs_0_
  3.0 1.8 %query.1 = (bf16[256,256]{1,0:T(8,128)(2,1)S(1)}, bf16[2,512,256]{2,1,0:T(8,128)(2,1)S(1)}) custom-call(bf16[256,1024]{1,0:T(8,128)(2,1)} %refs_1_.1, bf16[1024,256]{1,0:T(8,128)(2,1)} %weight.1, bf16[2,512,256]{2,1,0:T(8,128)(2,1)} %bitcast.39), custom_call_target="tpu_custom_call" | custom-call | tf_op jit(solution)/shard_map/query/pallas_call | solution.py:60
  4.8 0.0 copy-start.3
  4.8 0.0 copy-start.5
  4.9 0.0 copy-start.2
  4.9 2.6 %collective-permute-start.1 = (bf16[256,256]{1,0:T(8,128)(2,1)S(1)}, bf16[256,256]{1,0:T(8,128)(2,1)S(1)}, u32[]{:S(2)}, u32[]{:S(2)}) collective-permute-start(bf16[256,256]{1,0:T(8,128)(2,1)S(1)} %get-tuple-element.47.queries), channel_id=1, source_target_pairs={{0,8},{1,9},{2,10},{3,11},{4,12},{5,13},{6,14},{7,15},{8,0},{9,1},... | collective-permute-start | bytes 393224 | tf_op jit(solution)/shard_map/ppermute | solution.py:354
  7.5 1.6 %collective-permute-start = (bf16[256,256]{1,0:T(8,128)(2,1)S(1)}, bf16[256,256]{1,0:T(8,128)(2,1)S(1)}, u32[]{:S(2)}, u32[]{:S(2)}) collective-permute-start(bf16[256,256]{1,0:T(8,128)(2,1)S(1)} %get-tuple-element.47.queries), channel_id=1, source_target_pairs={{0,4},{1,5},{2,6},{3,7},{4,0},{5,1},{6,2},{7,3},{8,12},{9,13},{10,... | collective-permute-start | bytes 393224 | tf_op jit(solution)/shard_map/ppermute | solution.py:354
  9.1 0.8 attend.4.refs_0_
  9.9 3.8 %collective-permute-done.1.queries = bf16[256,256]{1,0:T(8,128)(2,1)S(1)} collective-permute-done((bf16[256,256]{1,0:T(8,128)(2,1)S(1)}, bf16[256,256]{1,0:T(8,128)(2,1)S(1)}, u32[]{:S(2)}, u32[]{:S(2)}) %collective-permute-start.1) | collective-permute-done | bytes 131104 | tf_op jit(solution)/shard_map/ppermute | solution.py:354
  13.7 0.6 collective-permute-start.4
  14.3 0.8 attend.5
  15.1 3.4 %collective-permute-start.3 = (bf16[256,256]{1,0:T(8,128)(2,1)S(1)}, bf16[256,256]{1,0:T(8,128)(2,1)S(1)}, u32[]{:S(2)}, u32[]{:S(2)}) collective-permute-start(bf16[256,256]{1,0:T(8,128)(2,1)S(1)} %attend.5), channel_id=1, source_target_pairs={{0,8},{1,9},{2,10},{3,11},{4,12},{5,13},{6,14},{7,15},{8,0},{9,1},... | collective-permute-start | bytes 393224 | tf_op jit(solution)/shard_map/ppermute | solution.py:354
  18.5 0.0 collective-permute-done.queries
  18.5 0.8 attend.6
  19.3 0.1 collective-permute-start.2
  19.4 0.8 attend.7
  20.2 0.0 copy-start.4
  20.2 5.7 %collective-permute-start.5 = (bf16[256,256]{1,0:T(8,128)(2,1)S(1)}, bf16[256,256]{1,0:T(8,128)(2,1)S(1)}, u32[]{:S(2)}, u32[]{:S(2)}) collective-permute-start(bf16[256,256]{1,0:T(8,128)(2,1)S(1)} %attend.7), channel_id=1, source_target_pairs={{0,12},{1,13},{2,14},{3,15},{4,8},{5,9},{6,10},{7,11},{8,4},{9,5},... | collective-permute-start | bytes 393224 | tf_op jit(solution)/shard_map/ppermute | solution.py:354
  26.5 2.8 %collective-permute-done.5.refs_3_ = bf16[256,256]{1,0:T(8,128)(2,1)S(1)} collective-permute-done((bf16[256,256]{1,0:T(8,128)(2,1)S(1)}, bf16[256,256]{1,0:T(8,128)(2,1)S(1)}, u32[]{:S(2)}, u32[]{:S(2)}) %collective-permute-start.5) | collective-permute-done | bytes 131104 | tf_op jit(solution)/shard_map/ppermute | solution.py:354
  29.3 0.6 pick.1.refs_2_
  29.9 0.1 collective-permute-start.10
  30.0 0.5 collective-permute-start.11
  30.5 0.5 collective-permute-start.6
  31.1 1.5 %route.1 = (s32[256,2]{1,0:T(8,128)S(1)}, bf16[192,256]{1,0:T(8,128)(2,1)S(1)}, bf16[192,256]{1,0:T(8,128)(2,1)S(1)}, bf16[192,256]{1,0:T(8,128)(2,1)S(1)}, bf16...) custom-call(s32[2]{0:T(128)S(1)} %pad_add_fusion.ids.refs_0_, ...), custom_call_target="tpu_custom_call" | custom-call | tf_op jit(solution)/shard_map/route/pallas_call | solution.py:171
  32.6 0.1 collective-permute-start.7
  32.6 3.4 %collective-permute-done.6.refs_3_ = bf16[256,256]{1,0:T(8,128)(2,1)S(1)} collective-permute-done((bf16[256,256]{1,0:T(8,128)(2,1)S(1)}, bf16[256,256]{1,0:T(8,128)(2,1)S(1)}, u32[]{:S(2)}, u32[]{:S(2)}) %collective-permute-start.6) | collective-permute-done | bytes 131104 | tf_op jit(solution)/shard_map/ppermute | solution.py:354
  36.0 1.3 %collective-permute-done.8.refs_5_ = bf16[256,256]{1,0:T(8,128)(2,1)S(1)} collective-permute-done((bf16[256,256]{1,0:T(8,128)(2,1)S(1)}, bf16[256,256]{1,0:T(8,128)(2,1)S(1)}, u32[]{:S(2)}, u32[]{:S(2)}) %collective-permute-start.8) | collective-permute-done | bytes 131104 | tf_op jit(solution)/shard_map/ppermute | solution.py:354
  37.4 0.0 copy-start
  37.4 0.0 copy-start.1
  37.4 1.5 %state.1 = (bf16[256,1024]{1,0:T(8,128)(2,1)S(1)}, bf16[192,256]{1,0:T(8,128)(2,1)S(1)}, bf16[192,256]{1,0:T(8,128)(2,1)S(1)}, bf16[192,512]{1,0:T(8,128)(2,1)S(1)}) custom-call(s32[2]{0:T(128)S(1)} %pad_add_fusion.ids.refs_0_, bf16[256,1024]{1,0:T(8,128)(2,1)S(1)} %copy-done.2, bf16[256,256]{1,0:T(8,128)(2,1)S(1)} %pick.1.refs_2_, ...), custom_call_target="tpu_custom_call" | custom-call | tf_op jit(solution)/shard_map/state/pallas_call | solution.py:201
  38.9 2.6 %collective-permute-start.12 = (bf16[192,256]{1,0:T(8,128)(2,1)S(1)}, bf16[192,256]{1,0:T(8,128)(2,1)S(1)}, u32[]{:S(2)}, u32[]{:S(2)}) collective-permute-start(bf16[192,256]{1,0:T(8,128)(2,1)S(1)} %get-tuple-element.70), channel_id=1, source_target_pairs={{0,8},{1,9},{2,10},{3,11},{4,12},{5,13},{6,14},{7,15},{8,0},{9,1},... | collective-permute-start | bytes 294920 | tf_op jit(solution)/shard_map/ppermute | solution.py:354
  41.5 1.4 %collective-permute-start.25 = (bf16[192,256]{1,0:T(8,128)(2,1)S(1)}, bf16[192,256]{1,0:T(8,128)(2,1)S(1)}, u32[]{:S(2)}, u32[]{:S(2)}) collective-permute-start(bf16[192,256]{1,0:T(8,128)(2,1)S(1)} %get-tuple-element.84), channel_id=1, source_target_pairs={{0,12},{1,13},{2,14},{3,15},{4,8},{5,9},{6,10},{7,11},{8,4},{9,5},... | collective-permute-start | bytes 294920 | tf_op jit(solution)/shard_map/ppermute | solution.py:354
  42.9 0.0 collective-permute-start.17
  42.9 1.0 %home.1 = (bf16[192,512]{1,0:T(8,128)(2,1)S(1)}, bf16[192,512]{1,0:T(8,128)(2,1)S(1)}, f32[256,2]{1,0:T(8,128)S(1)}, f32[256,256]{1,0:T(8,128)S(1)}) custom-call(s32[2]{0:T(128)S(1)} %pad_add_fusion.ids.refs_0_, bf16[256,1024]{1,0:T(8,128)(2,1)S(1)} %get-tuple-element.60.state, bf16[192,256]{1,0:T(8,128)(2,1)S(1)} %get-tuple-element.53.dispatch, ...), custom_call_target="tpu_custom_call" | custom-call | tf_op jit(solution)/shard_map/home/pallas_call | solution.py:231
  44.0 1.5 %expert.3 = (f32[2,192,256]{2,1,0:T(8,128)S(1)}, bf16[2,192,256]{2,1,0:T(8,128)(2,1)S(1)}) custom-call(s32[2]{0:T(128)S(1)} %pad_add_fusion.ids.refs_0_, bf16[192,512]{1,0:T(8,128)(2,1)S(1)} %get-tuple-element.66.refs_1_, bf16[192,512]{1,0:T(8,128)(2,1)S(1)} %get-tuple-element.67.refs_2_, bf16[1024,1024]{1,0:T(8,128)(2,1)S(1)} %bitcast.31, ...), custom_call_target="tpu_custom_call" | custom-call | tf_op jit(solution)/shard_map/expert/pallas_call | solution.py:279
  45.5 4.2 %collective-permute-done.12.refs_1_ = bf16[192,256]{1,0:T(8,128)(2,1)S(1)} collective-permute-done((bf16[192,256]{1,0:T(8,128)(2,1)S(1)}, bf16[192,256]{1,0:T(8,128)(2,1)S(1)}, u32[]{:S(2)}, u32[]{:S(2)}) %collective-permute-start.12) | collective-permute-done | bytes 98336 | tf_op jit(solution)/shard_map/ppermute | solution.py:354
  49.8 0.5 collective-permute-start.14
  50.3 1.5 %collective-permute-start.26 = (bf16[192,256]{1,0:T(8,128)(2,1)S(1)}, bf16[192,256]{1,0:T(8,128)(2,1)S(1)}, u32[]{:S(2)}, u32[]{:S(2)}) collective-permute-start(bf16[192,256]{1,0:T(8,128)(2,1)S(1)} %collective-permute-done.25.refs_1_), channel_id=1, source_target_pairs={{0,2},{1,3},{2,0},{3,1},{4,6},{5,7},{6,4},{7,5},{8,10},{9,11},{10,... | collective-permute-start | bytes 294920 | tf_op jit(solution)/shard_map/ppermute | solution.py:354
  51.8 0.6 collective-permute-done.17.refs_5_
  52.4 3.0 %collective-permute-done.14.refs_2_ = bf16[192,256]{1,0:T(8,128)(2,1)S(1)} collective-permute-done((bf16[192,256]{1,0:T(8,128)(2,1)S(1)}, bf16[192,256]{1,0:T(8,128)(2,1)S(1)}, u32[]{:S(2)}, u32[]{:S(2)}) %collective-permute-start.14) | collective-permute-done | bytes 98336 | tf_op jit(solution)/shard_map/ppermute | solution.py:354
  55.4 1.7 %collective-permute-done.26.refs_2_ = bf16[192,256]{1,0:T(8,128)(2,1)S(1)} collective-permute-done((bf16[192,256]{1,0:T(8,128)(2,1)S(1)}, bf16[192,256]{1,0:T(8,128)(2,1)S(1)}, u32[]{:S(2)}, u32[]{:S(2)}) %collective-permute-start.26) | collective-permute-done | bytes 98336 | tf_op jit(solution)/shard_map/ppermute | solution.py:354
  57.1 0.5 collective-permute-start.28
  57.7 0.7 collective-permute-done.16.refs_4_
  58.4 2.4 %expert.4 = (f32[2,384,256]{2,1,0:T(8,128)S(1)}, bf16[2,384,256]{2,1,0:T(8,128)(2,1)S(1)}) custom-call(s32[2]{0:T(128)S(1)} %pad_add_fusion.ids.refs_0_, bf16[192,256]{1,0:T(8,128)(2,1)S(1)} %collective-permute-done.12.refs_1_, bf16[192,256]{1,0:T(8,128)(2,1)S(1)} %collective-permute-done.14.refs_2_, bf16[192,256]{1,0:T(8,128)(2,1)S(1)} %collective-permute-done.15.refs_3_, ...), custom_call_target="tpu_custom_call" | custom-call | tf_op jit(solution)/shard_map/expert/pallas_call | solution.py:279
  60.8 0.2 collective-permute-start.19
  61.1 1.6 %expert.5 = (f32[2,192,256]{2,1,0:T(8,128)S(1)}, bf16[2,192,256]{2,1,0:T(8,128)(2,1)S(1)}) custom-call(s32[2]{0:T(128)S(1)} %pad_add_fusion.ids.refs_0_, bf16[192,256]{1,0:T(8,128)(2,1)S(1)} %collective-permute-done.25.refs_1_, bf16[192,256]{1,0:T(8,128)(2,1)S(1)} %collective-permute-done.26.refs_2_, bf16[192,256]{1,0:T(8,128)(2,1)S(1)} %collective-permute-done.27.refs_3_, ...), custom_call_target="tpu_custom_call" | custom-call | tf_op jit(solution)/shard_map/expert/pallas_call | solution.py:279
  62.6 0.4 collective-permute-start.29
  63.1 1.1 %collective-permute-done.29 = bf16[2,192,256]{2,1,0:T(8,128)(2,1)S(1)} collective-permute-done((bf16[2,192,256]{2,1,0:T(8,128)(2,1)S(1)}, bf16[2,192,256]{2,1,0:T(8,128)(2,1)S(1)}, u32[]{:S(2)}, u32[]{:S(2)}) %collective-permute-start.29) | collective-permute-done | bytes 196640 | tf_op jit(solution)/shard_map/ppermute | solution.py:354
  64.2 0.1 fusion.5
  64.3 0.6 collective-permute-start.20
  65.0 1.6 %collective-permute-start.30 = (bf16[192,256]{1,0:T(8,128)(2,1)S(1)}, bf16[192,256]{1,0:T(8,128)(2,1)S(1)}, u32[]{:S(2)}, u32[]{:S(2)}) collective-permute-start(bf16[192,256]{1,0:T(8,128)(2,1)S(1)} %fusion.4), channel_id=1, source_target_pairs={{0,2},{1,3},{2,0},{3,1},{4,6},{5,7},{6,4},{7,5},{8,10},{9,11},{10,... | collective-permute-start | bytes 294920 | tf_op jit(solution)/shard_map/ppermute | solution.py:354
  66.5 2.0 %collective-permute-start.22 = (bf16[192,256]{1,0:T(8,128)(2,1)S(1)}, bf16[192,256]{1,0:T(8,128)(2,1)S(1)}, u32[]{:S(2)}, u32[]{:S(2)}) collective-permute-start(bf16[192,256]{1,0:T(8,128)(2,1)S(1)} %get-tuple-element.90), channel_id=1, source_target_pairs={{0,4},{1,5},{2,6},{3,7},{4,0},{5,1},{6,2},{7,3},{8,12},{9,13},{10,... | collective-permute-start | bytes 294920 | tf_op jit(solution)/shard_map/ppermute | solution.py:354
  68.5 2.6 %collective-permute-done.20 = bf16[192,256]{1,0:T(8,128)(2,1)S(1)} collective-permute-done((bf16[192,256]{1,0:T(8,128)(2,1)S(1)}, bf16[192,256]{1,0:T(8,128)(2,1)S(1)}, u32[]{:S(2)}, u32[]{:S(2)}) %collective-permute-start.20) | collective-permute-done | bytes 98336 | tf_op jit(solution)/shard_map/ppermute | solution.py:354
  71.2 1.8 %collective-permute-start.24 = (bf16[192,256]{1,0:T(8,128)(2,1)S(1)}, bf16[192,256]{1,0:T(8,128)(2,1)S(1)}, u32[]{:S(2)}, u32[]{:S(2)}) collective-permute-start(bf16[192,256]{1,0:T(8,128)(2,1)S(1)} %fusion.3), channel_id=1, source_target_pairs={{0,8},{1,9},{2,10},{3,11},{4,12},{5,13},{6,14},{7,15},{8,0},{9,1},... | collective-permute-start | bytes 294920 | tf_op jit(solution)/shard_map/ppermute | solution.py:354
  73.0 1.2 %collective-permute-done.30 = bf16[192,256]{1,0:T(8,128)(2,1)S(1)} collective-permute-done((bf16[192,256]{1,0:T(8,128)(2,1)S(1)}, bf16[192,256]{1,0:T(8,128)(2,1)S(1)}, u32[]{:S(2)}, u32[]{:S(2)}) %collective-permute-start.30) | collective-permute-done | bytes 98336 | tf_op jit(solution)/shard_map/ppermute | solution.py:354
  74.2 2.8 %collective-permute-start.31 = (bf16[192,256]{1,0:T(8,128)(2,1)S(1)}, bf16[192,256]{1,0:T(8,128)(2,1)S(1)}, u32[]{:S(2)}, u32[]{:S(2)}) collective-permute-start(bf16[192,256]{1,0:T(8,128)(2,1)S(1)} %fusion.1), channel_id=1, source_target_pairs={{0,12},{1,13},{2,14},{3,15},{4,8},{5,9},{6,10},{7,11},{8,4},{9,5},... | collective-permute-start | bytes 294920 | tf_op jit(solution)/shard_map/ppermute | solution.py:354
  77.0 0.6 collective-permute-done.21.refs_1_
  77.6 0.2 combine.4.base
  77.9 0.2 combine.5.base
  78.1 1.4 %collective-permute-done.24.refs_0_ = bf16[192,256]{1,0:T(8,128)(2,1)S(1)} collective-permute-done((bf16[192,256]{1,0:T(8,128)(2,1)S(1)}, bf16[192,256]{1,0:T(8,128)(2,1)S(1)}, u32[]{:S(2)}, u32[]{:S(2)}) %collective-permute-start.24) | collective-permute-done | bytes 98336 | tf_op jit(solution)/shard_map/ppermute | solution.py:354
  79.5 0.2 combine.6.base
  79.7 1.1 %collective-permute-done.31.refs_0_ = bf16[192,256]{1,0:T(8,128)(2,1)S(1)} collective-permute-done((bf16[192,256]{1,0:T(8,128)(2,1)S(1)}, bf16[192,256]{1,0:T(8,128)(2,1)S(1)}, u32[]{:S(2)}, u32[]{:S(2)}) %collective-permute-start.31) | collective-permute-done | bytes 98336 | tf_op jit(solution)/shard_map/ppermute | solution.py:354
  80.8 0.9 %combine.7 = bf16[256,256]{1,0:T(8,128)(2,1)} custom-call(f32[256,2]{1,0:T(8,128)S(1)} %get-tuple-element.62.gates, f32[256,256]{1,0:T(8,128)S(1)} %combine.6.base, bf16[256,192]{1,0:T(8,128)(2,1)S(1)} %get-tuple-element.81.first, bf16[256,192]{1,0:T(8,128)(2,1)S(1)} %get-tuple-element.82.second, bf16[192,256]{1,0:T(8,128)(2,1)S(1)} %collective-permute-done.31.refs_0_), custom_call_target="tpu_custom_call" | custom-call | tf_op jit(solution)/shard_map/combine/pallas_call | solution.py:305
  (37 shorter events, 0.2 us)
Async XLA Ops:
  0.0 30.0 %collective-permute-start.9 = (bf16[256,1024]{1,0:T(8,128)(2,1)}, bf16[256,1024]{1,0:T(8,128)(2,1)S(1)}, u32[]{:S(2)}, u32[]{:S(2)}) collective-permute-start(bf16[256,1024]{1,0:T(8,128)(2,1)} %refs_6_), channel_id=1, source_target_pairs={{0,2},{1,3},{2,0},{3,1},{4,6},{5,7},{6,4},{7,5},{8,10},{9,11},{10,... | collective-permute-start | bytes 1572872 | tf_op jit(solution)/shard_map/ppermute | solution.py:354
  4.8 25.1 %copy-start.3 = (bf16[256,1024]{1,0:T(8,128)(2,1)S(1)}, bf16[256,1024]{1,0:T(8,128)(2,1)}, u32[]{:S(2)}) copy-start(bf16[256,1024]{1,0:T(8,128)(2,1)} %refs_6_) | copy-start | bytes 1572868
  4.8 26.2 %copy-start.5 = (s32[256,2]{0,1:T(2,128)S(1)}, s32[256,2]{0,1:T(2,128)}, u32[]{:S(2)}) copy-start(s32[256,2]{0,1:T(2,128)} %param.15) | copy-start | bytes 6148
  4.9 32.5 %copy-start.2 = (bf16[256,1024]{1,0:T(8,128)(2,1)S(1)}, bf16[256,1024]{1,0:T(8,128)(2,1)}, u32[]{:S(2)}) copy-start(bf16[256,1024]{1,0:T(8,128)(2,1)} %refs_1_.1) | copy-start | bytes 1572868
  4.9 8.8 %collective-permute-start.1 = (bf16[256,256]{1,0:T(8,128)(2,1)S(1)}, bf16[256,256]{1,0:T(8,128)(2,1)S(1)}, u32[]{:S(2)}, u32[]{:S(2)}) collective-permute-start(bf16[256,256]{1,0:T(8,128)(2,1)S(1)} %get-tuple-element.47.queries), channel_id=1, source_target_pairs={{0,8},{1,9},{2,10},{3,11},{4,12},{5,13},{6,14},{7,15},{8,0},{9,1},... | collective-permute-start | bytes 393224 | tf_op jit(solution)/shard_map/ppermute | solution.py:354
  7.5 11.0 %collective-permute-start = (bf16[256,256]{1,0:T(8,128)(2,1)S(1)}, bf16[256,256]{1,0:T(8,128)(2,1)S(1)}, u32[]{:S(2)}, u32[]{:S(2)}) collective-permute-start(bf16[256,256]{1,0:T(8,128)(2,1)S(1)} %get-tuple-element.47.queries), channel_id=1, source_target_pairs={{0,4},{1,5},{2,6},{3,7},{4,0},{5,1},{6,2},{7,3},{8,12},{9,13},{10,... | collective-permute-start | bytes 393224 | tf_op jit(solution)/shard_map/ppermute | solution.py:354
  13.7 5.7 %collective-permute-start.4 = (bf16[256,256]{1,0:T(8,128)(2,1)S(1)}, bf16[256,256]{1,0:T(8,128)(2,1)S(1)}, u32[]{:S(2)}, u32[]{:S(2)}) collective-permute-start(bf16[256,256]{1,0:T(8,128)(2,1)S(1)} %collective-permute-done.1.queries), channel_id=1, source_target_pairs={{0,4},{1,5},{2,6},{3,7},{4,0},{5,1},{6,2},{7,3},{8,12},{9,13},{10,... | collective-permute-start | bytes 393224 | tf_op jit(solution)/shard_map/ppermute | solution.py:354
  15.1 11.4 %collective-permute-start.3 = (bf16[256,256]{1,0:T(8,128)(2,1)S(1)}, bf16[256,256]{1,0:T(8,128)(2,1)S(1)}, u32[]{:S(2)}, u32[]{:S(2)}) collective-permute-start(bf16[256,256]{1,0:T(8,128)(2,1)S(1)} %attend.5), channel_id=1, source_target_pairs={{0,8},{1,9},{2,10},{3,11},{4,12},{5,13},{6,14},{7,15},{8,0},{9,1},... | collective-permute-start | bytes 393224 | tf_op jit(solution)/shard_map/ppermute | solution.py:354
  19.3 7.2 %collective-permute-start.2 = (bf16[256,256]{1,0:T(8,128)(2,1)S(1)}, bf16[256,256]{1,0:T(8,128)(2,1)S(1)}, u32[]{:S(2)}, u32[]{:S(2)}) collective-permute-start(bf16[256,256]{1,0:T(8,128)(2,1)S(1)} %attend.6), channel_id=1, source_target_pairs={{0,4},{1,5},{2,6},{3,7},{4,0},{5,1},{6,2},{7,3},{8,12},{9,13},{10,... | collective-permute-start | bytes 393224 | tf_op jit(solution)/shard_map/ppermute | solution.py:354
  20.2 22.8 %copy-start.4 = (bf16[1024,4]{0,1:T(4,128)(2,1)S(1)}, bf16[1024,4]{0,1:T(4,128)(2,1)}, u32[]{:S(2)}) copy-start(bf16[1024,4]{0,1:T(4,128)(2,1)} %param.14) | copy-start | bytes 24580
  20.2 9.2 %collective-permute-start.5 = (bf16[256,256]{1,0:T(8,128)(2,1)S(1)}, bf16[256,256]{1,0:T(8,128)(2,1)S(1)}, u32[]{:S(2)}, u32[]{:S(2)}) collective-permute-start(bf16[256,256]{1,0:T(8,128)(2,1)S(1)} %attend.7), channel_id=1, source_target_pairs={{0,12},{1,13},{2,14},{3,15},{4,8},{5,9},{6,10},{7,11},{8,4},{9,5},... | collective-permute-start | bytes 393224 | tf_op jit(solution)/shard_map/ppermute | solution.py:354
  29.9 7.4 %collective-permute-start.10 = (bf16[256,1024]{1,0:T(8,128)(2,1)S(1)}, bf16[256,1024]{1,0:T(8,128)(2,1)S(1)}, u32[]{:S(2)}, u32[]{:S(2)}) collective-permute-start(bf16[256,1024]{1,0:T(8,128)(2,1)S(1)} %copy-done.3), channel_id=1, source_target_pairs={{0,1},{1,0},{2,3},{3,2},{4,5},{5,4},{6,7},{7,6},{8,9},{9,8},{10,11... | collective-permute-start | bytes 1572872 | tf_op jit(solution)/shard_map/ppermute | solution.py:354
  30.0 7.3 %collective-permute-start.11 = (bf16[256,1024]{1,0:T(8,128)(2,1)S(1)}, bf16[256,1024]{1,0:T(8,128)(2,1)S(1)}, u32[]{:S(2)}, u32[]{:S(2)}) collective-permute-start(bf16[256,1024]{1,0:T(8,128)(2,1)S(1)} %collective-permute-done.9.refs_7_), channel_id=1, source_target_pairs={{0,1},{1,0},{2,3},{3,2},{4,5},{5,4},{6,7},{7,6},{8,9},{9,8},{10,11... | collective-permute-start | bytes 1572872 | tf_op jit(solution)/shard_map/ppermute | solution.py:354
  30.5 5.5 %collective-permute-start.6 = (bf16[256,256]{1,0:T(8,128)(2,1)S(1)}, bf16[256,256]{1,0:T(8,128)(2,1)S(1)}, u32[]{:S(2)}, u32[]{:S(2)}) collective-permute-start(bf16[256,256]{1,0:T(8,128)(2,1)S(1)} %pick.1.refs_2_), channel_id=1, source_target_pairs={{0,2},{1,3},{2,0},{3,1},{4,6},{5,7},{6,4},{7,5},{8,10},{9,11},{10,... | collective-permute-start | bytes 393224 | tf_op jit(solution)/shard_map/ppermute | solution.py:354
  32.6 3.5 %collective-permute-start.7 = (bf16[256,256]{1,0:T(8,128)(2,1)S(1)}, bf16[256,256]{1,0:T(8,128)(2,1)S(1)}, u32[]{:S(2)}, u32[]{:S(2)}) collective-permute-start(bf16[256,256]{1,0:T(8,128)(2,1)S(1)} %pick.1.refs_2_), channel_id=1, source_target_pairs={{0,1},{1,0},{2,3},{3,2},{4,5},{5,4},{6,7},{7,6},{8,9},{9,8},{10,11... | collective-permute-start | bytes 393224 | tf_op jit(solution)/shard_map/ppermute | solution.py:354
  36.0 1.3 %collective-permute-start.8 = (bf16[256,256]{1,0:T(8,128)(2,1)S(1)}, bf16[256,256]{1,0:T(8,128)(2,1)S(1)}, u32[]{:S(2)}, u32[]{:S(2)}) collective-permute-start(bf16[256,256]{1,0:T(8,128)(2,1)S(1)} %collective-permute-done.6.refs_3_), channel_id=1, source_target_pairs={{0,1},{1,0},{2,3},{3,2},{4,5},{5,4},{6,7},{7,6},{8,9},{9,8},{10,11... | collective-permute-start | bytes 393224 | tf_op jit(solution)/shard_map/ppermute | solution.py:354
  37.4 6.6 %copy-start = (bf16[1,1024,1024]{2,1,0:T(8,128)(2,1)S(1)}, bf16[1,1024,1024]{2,1,0:T(8,128)(2,1)}, u32[]{:S(2)}) copy-start(bf16[1,1024,1024]{2,1,0:T(8,128)(2,1)} %param.16) | copy-start | bytes 6291460
  37.4 6.6 %copy-start.1 = (bf16[1,1024,1024]{2,1,0:T(8,128)(2,1)S(1)}, bf16[1,1024,1024]{2,1,0:T(8,128)(2,1)}, u32[]{:S(2)}) copy-start(bf16[1,1024,1024]{2,1,0:T(8,128)(2,1)} %param.17) | copy-start | bytes 6291460
  38.9 10.9 %collective-permute-start.12 = (bf16[192,256]{1,0:T(8,128)(2,1)S(1)}, bf16[192,256]{1,0:T(8,128)(2,1)S(1)}, u32[]{:S(2)}, u32[]{:S(2)}) collective-permute-start(bf16[192,256]{1,0:T(8,128)(2,1)S(1)} %get-tuple-element.70), channel_id=1, source_target_pairs={{0,8},{1,9},{2,10},{3,11},{4,12},{5,13},{6,14},{7,15},{8,0},{9,1},... | collective-permute-start | bytes 294920 | tf_op jit(solution)/shard_map/ppermute | solution.py:354
  41.5 8.8 %collective-permute-start.25 = (bf16[192,256]{1,0:T(8,128)(2,1)S(1)}, bf16[192,256]{1,0:T(8,128)(2,1)S(1)}, u32[]{:S(2)}, u32[]{:S(2)}) collective-permute-start(bf16[192,256]{1,0:T(8,128)(2,1)S(1)} %get-tuple-element.84), channel_id=1, source_target_pairs={{0,12},{1,13},{2,14},{3,15},{4,8},{5,9},{6,10},{7,11},{8,4},{9,5},... | collective-permute-start | bytes 294920 | tf_op jit(solution)/shard_map/ppermute | solution.py:354
  42.9 9.5 %collective-permute-start.17 = (bf16[192,512]{1,0:T(8,128)(2,1)S(1)}, bf16[192,512]{1,0:T(8,128)(2,1)S(1)}, u32[]{:S(2)}, u32[]{:S(2)}) collective-permute-start(bf16[192,512]{1,0:T(8,128)(2,1)S(1)} %get-tuple-element.73), channel_id=1, source_target_pairs={{0,4},{1,5},{2,6},{3,7},{4,0},{5,1},{6,2},{7,3},{8,12},{9,13},{10,... | collective-permute-start | bytes 589832 | tf_op jit(solution)/shard_map/ppermute | solution.py:354
  49.8 7.3 %collective-permute-start.13 = (bf16[2,192,256]{2,1,0:T(8,128)(2,1)S(1)}, bf16[2,192,256]{2,1,0:T(8,128)(2,1)S(1)}, u32[]{:S(2)}, u32[]{:S(2)}) collective-permute-start(bf16[2,192,256]{2,1,0:T(8,128)(2,1)S(1)} %get-tuple-element.71), channel_id=1, source_target_pairs={{0,1},{1,0},{2,3},{3,2},{4,5},{5,4},{6,7},{7,6},{8,9},{9,8},{10,11... | collective-permute-start | bytes 589832 | tf_op jit(solution)/shard_map/ppermute | solution.py:354
  49.8 5.6 %collective-permute-start.14 = (bf16[192,256]{1,0:T(8,128)(2,1)S(1)}, bf16[192,256]{1,0:T(8,128)(2,1)S(1)}, u32[]{:S(2)}, u32[]{:S(2)}) collective-permute-start(bf16[192,256]{1,0:T(8,128)(2,1)S(1)} %collective-permute-done.12.refs_1_), channel_id=1, source_target_pairs={{0,2},{1,3},{2,0},{3,1},{4,6},{5,7},{6,4},{7,5},{8,10},{9,11},{10,... | collective-permute-start | bytes 294920 | tf_op jit(solution)/shard_map/ppermute | solution.py:354
  50.3 6.8 %collective-permute-start.26 = (bf16[192,256]{1,0:T(8,128)(2,1)S(1)}, bf16[192,256]{1,0:T(8,128)(2,1)S(1)}, u32[]{:S(2)}, u32[]{:S(2)}) collective-permute-start(bf16[192,256]{1,0:T(8,128)(2,1)S(1)} %collective-permute-done.25.refs_1_), channel_id=1, source_target_pairs={{0,2},{1,3},{2,0},{3,1},{4,6},{5,7},{6,4},{7,5},{8,10},{9,11},{10,... | collective-permute-start | bytes 294920 | tf_op jit(solution)/shard_map/ppermute | solution.py:354
  51.8 5.8 %collective-permute-start.15 = (bf16[192,256]{1,0:T(8,128)(2,1)S(1)}, bf16[192,256]{1,0:T(8,128)(2,1)S(1)}, u32[]{:S(2)}, u32[]{:S(2)}) collective-permute-start(bf16[192,256]{1,0:T(8,128)(2,1)S(1)} %collective-permute-done.12.refs_1_), channel_id=1, source_target_pairs={{0,1},{1,0},{2,3},{3,2},{4,5},{5,4},{6,7},{7,6},{8,9},{9,8},{10,11... | collective-permute-start | bytes 294920 | tf_op jit(solution)/shard_map/ppermute | solution.py:354
  52.4 8.6 %collective-permute-start.27 = (bf16[192,256]{1,0:T(8,128)(2,1)S(1)}, bf16[192,256]{1,0:T(8,128)(2,1)S(1)}, u32[]{:S(2)}, u32[]{:S(2)}) collective-permute-start(bf16[192,256]{1,0:T(8,128)(2,1)S(1)} %collective-permute-done.25.refs_1_), channel_id=1, source_target_pairs={{0,1},{1,0},{2,3},{3,2},{4,5},{5,4},{6,7},{7,6},{8,9},{9,8},{10,11... | collective-permute-start | bytes 294920 | tf_op jit(solution)/shard_map/ppermute | solution.py:354
  55.4 3.0 %collective-permute-start.18 = (bf16[192,512]{1,0:T(8,128)(2,1)S(1)}, bf16[192,512]{1,0:T(8,128)(2,1)S(1)}, u32[]{:S(2)}, u32[]{:S(2)}) collective-permute-start(bf16[192,512]{1,0:T(8,128)(2,1)S(1)} %collective-permute-done.17.refs_5_), channel_id=1, source_target_pairs={{0,1},{1,0},{2,3},{3,2},{4,5},{5,4},{6,7},{7,6},{8,9},{9,8},{10,11... | collective-permute-start | bytes 589832 | tf_op jit(solution)/shard_map/ppermute | solution.py:354
  57.1 1.3 %collective-permute-start.16 = (bf16[192,256]{1,0:T(8,128)(2,1)S(1)}, bf16[192,256]{1,0:T(8,128)(2,1)S(1)}, u32[]{:S(2)}, u32[]{:S(2)}) collective-permute-start(bf16[192,256]{1,0:T(8,128)(2,1)S(1)} %collective-permute-done.14.refs_2_), channel_id=1, source_target_pairs={{0,1},{1,0},{2,3},{3,2},{4,5},{5,4},{6,7},{7,6},{8,9},{9,8},{10,11... | collective-permute-start | bytes 294920 | tf_op jit(solution)/shard_map/ppermute | solution.py:354
  57.1 3.9 %collective-permute-start.28 = (bf16[192,256]{1,0:T(8,128)(2,1)S(1)}, bf16[192,256]{1,0:T(8,128)(2,1)S(1)}, u32[]{:S(2)}, u32[]{:S(2)}) collective-permute-start(bf16[192,256]{1,0:T(8,128)(2,1)S(1)} %collective-permute-done.26.refs_2_), channel_id=1, source_target_pairs={{0,1},{1,0},{2,3},{3,2},{4,5},{5,4},{6,7},{7,6},{8,9},{9,8},{10,11... | collective-permute-start | bytes 294920 | tf_op jit(solution)/shard_map/ppermute | solution.py:354
  60.8 3.3 %collective-permute-start.19 = (bf16[2,384,256]{2,1,0:T(8,128)(2,1)S(1)}, bf16[2,384,256]{2,1,0:T(8,128)(2,1)S(1)}, u32[]{:S(2)}, u32[]{:S(2)}) collective-permute-start(bf16[2,384,256]{2,1,0:T(8,128)(2,1)S(1)} %get-tuple-element.75), channel_id=1, source_target_pairs={{0,1},{1,0},{2,3},{3,2},{4,5},{5,4},{6,7},{7,6},{8,9},{9,8},{10,11... | collective-permute-start | bytes 1179656 | tf_op jit(solution)/shard_map/ppermute | solution.py:354
  62.6 1.5 %collective-permute-start.29 = (bf16[2,192,256]{2,1,0:T(8,128)(2,1)S(1)}, bf16[2,192,256]{2,1,0:T(8,128)(2,1)S(1)}, u32[]{:S(2)}, u32[]{:S(2)}) collective-permute-start(bf16[2,192,256]{2,1,0:T(8,128)(2,1)S(1)} %get-tuple-element.86), channel_id=1, source_target_pairs={{0,1},{1,0},{2,3},{3,2},{4,5},{5,4},{6,7},{7,6},{8,9},{9,8},{10,11... | collective-permute-start | bytes 589832 | tf_op jit(solution)/shard_map/ppermute | solution.py:354
  64.3 6.8 %collective-permute-start.20 = (bf16[192,256]{1,0:T(8,128)(2,1)S(1)}, bf16[192,256]{1,0:T(8,128)(2,1)S(1)}, u32[]{:S(2)}, u32[]{:S(2)}) collective-permute-start(bf16[192,256]{1,0:T(8,128)(2,1)S(1)} %get-tuple-element.91), channel_id=1, source_target_pairs={{0,2},{1,3},{2,0},{3,1},{4,6},{5,7},{6,4},{7,5},{8,10},{9,11},{10,... | collective-permute-start | bytes 294920 | tf_op jit(solution)/shard_map/ppermute | solution.py:354
  65.0 9.3 %collective-permute-start.30 = (bf16[192,256]{1,0:T(8,128)(2,1)S(1)}, bf16[192,256]{1,0:T(8,128)(2,1)S(1)}, u32[]{:S(2)}, u32[]{:S(2)}) collective-permute-start(bf16[192,256]{1,0:T(8,128)(2,1)S(1)} %fusion.4), channel_id=1, source_target_pairs={{0,2},{1,3},{2,0},{3,1},{4,6},{5,7},{6,4},{7,5},{8,10},{9,11},{10,... | collective-permute-start | bytes 294920 | tf_op jit(solution)/shard_map/ppermute | solution.py:354
  66.5 11.3 %collective-permute-start.23 = (bf16[192,256]{1,0:T(8,128)(2,1)S(1)}, bf16[192,256]{1,0:T(8,128)(2,1)S(1)}, u32[]{:S(2)}, u32[]{:S(2)}) collective-permute-start(bf16[192,256]{1,0:T(8,128)(2,1)S(1)} %get-tuple-element.89), channel_id=1, source_target_pairs={{0,6},{1,7},{2,4},{3,5},{4,2},{5,3},{6,0},{7,1},{8,14},{9,15},{10,... | collective-permute-start | bytes 294920 | tf_op jit(solution)/shard_map/ppermute | solution.py:354
  66.5 11.4 %collective-permute-start.22 = (bf16[192,256]{1,0:T(8,128)(2,1)S(1)}, bf16[192,256]{1,0:T(8,128)(2,1)S(1)}, u32[]{:S(2)}, u32[]{:S(2)}) collective-permute-start(bf16[192,256]{1,0:T(8,128)(2,1)S(1)} %get-tuple-element.90), channel_id=1, source_target_pairs={{0,4},{1,5},{2,6},{3,7},{4,0},{5,1},{6,2},{7,3},{8,12},{9,13},{10,... | collective-permute-start | bytes 294920 | tf_op jit(solution)/shard_map/ppermute | solution.py:354
  71.2 8.3 %collective-permute-start.24 = (bf16[192,256]{1,0:T(8,128)(2,1)S(1)}, bf16[192,256]{1,0:T(8,128)(2,1)S(1)}, u32[]{:S(2)}, u32[]{:S(2)}) collective-permute-start(bf16[192,256]{1,0:T(8,128)(2,1)S(1)} %fusion.3), channel_id=1, source_target_pairs={{0,8},{1,9},{2,10},{3,11},{4,12},{5,13},{6,14},{7,15},{8,0},{9,1},... | collective-permute-start | bytes 294920 | tf_op jit(solution)/shard_map/ppermute | solution.py:354
  73.0 4.6 %collective-permute-start.21 = (bf16[192,256]{1,0:T(8,128)(2,1)S(1)}, bf16[192,256]{1,0:T(8,128)(2,1)S(1)}, u32[]{:S(2)}, u32[]{:S(2)}) collective-permute-start(bf16[192,256]{1,0:T(8,128)(2,1)S(1)} %get-tuple-element.76), channel_id=1, source_target_pairs={{0,2},{1,3},{2,0},{3,1},{4,6},{5,7},{6,4},{7,5},{8,10},{9,11},{10,... | collective-permute-start | bytes 294920 | tf_op jit(solution)/shard_map/ppermute | solution.py:354
  74.2 6.6 %collective-permute-start.31 = (bf16[192,256]{1,0:T(8,128)(2,1)S(1)}, bf16[192,256]{1,0:T(8,128)(2,1)S(1)}, u32[]{:S(2)}, u32[]{:S(2)}) collective-permute-start(bf16[192,256]{1,0:T(8,128)(2,1)S(1)} %fusion.1), channel_id=1, source_target_pairs={{0,12},{1,13},{2,14},{3,15},{4,8},{5,9},{6,10},{7,11},{8,4},{9,5},... | collective-permute-start | bytes 294920 | tf_op jit(solution)/shard_map/ppermute | solution.py:354

commit v10 on v9

--- a/solution.py
+++ b/solution.py
@@ -14,7 +14,6 @@
 F32, BF16 = jnp.float32, jnp.bfloat16
 PARAMS = pltpu.CompilerParams(vmem_limit_bytes=20 * 2**20)
 CHEAP = pl.CostEstimate(flops=0, bytes_accessed=0, transcendentals=0)
-SCALARS = pl.BlockSpec(memory_space=pltpu.SMEM)
 WHOLE = pl.BlockSpec(memory_space=pltpu.VMEM)
 
 
@@ -24,6 +23,10 @@
 
 def in_hbm(value):
     return pltpu.with_memory_space_constraint(value, pltpu.HBM)
+
+
+def position():
+    return lax.axis_index("expert"), lax.axis_index("mp")
 
 
 def query_kernel(tokens, weight, source, out, staged, tokens_here, weight_here, sems):
@@ -114,28 +117,29 @@
     )(queries, source)
 
 
-def pick_kernel(ids, owner, *refs):
+def pick_kernel(owner, *refs):
     backs, out = refs[:-1], refs[-1]
-    for k, back in enumerate(backs):
-
-        @pl.when(owner[0] == ids[0] ^ k)
-        def _():
-            out[...] = back[...]
-
-
-def pick(ids, owner, backs):
+    here, _ = position()
+    names = jnp.broadcast_to(owner[0:1, 0:1], out.shape)
+    total = backs[0][...].astype(F32)
+    for k in range(1, len(backs)):
+        total = jnp.where(names == here ^ k, backs[k][...].astype(F32), total)
+    out[...] = total.astype(BF16)
+
+
+def pick(owner, backs):
     return pl.pallas_call(
         pick_kernel,
-        in_specs=[SCALARS] * 2 + [WHOLE] * len(backs),
+        in_specs=[WHOLE] * (1 + len(backs)),
         out_specs=WHOLE,
         out_shape=jax.ShapeDtypeStruct(backs[0].shape, BF16),
         compiler_params=PARAMS,
         cost_estimate=CHEAP,
         name="pick",
-    )(ids, owner, *backs)
-
-
-def route_kernel(experts, parts, ids, choice_t, choice, *outs):
+    )(owner, *backs)
+
+
+def route_kernel(experts, parts, choice_t, choice, *outs):
     dispatch, first, second = outs[:parts], outs[parts : 2 * parts], outs[2 * parts :]
     tokens = choice_t.shape[1]
     slots = dispatch[0].shape[0]
@@ -159,18 +163,18 @@
     lane = lax.broadcasted_iota(jnp.int32, (tokens, slots), 1)
     row = lax.broadcasted_iota(jnp.int32, (slots, tokens), 0)
     for k in range(parts):
-        base = (ids[0] ^ k) * capacity if parts > 1 else 0
+        base = (position()[0] ^ k) * capacity if parts > 1 else 0
         dispatch[k][...] = ((row + base == across0) | (row + base == across1)).astype(BF16)
         first[k][...] = (lane + base == place0).astype(BF16)
         second[k][...] = (lane + base == place1).astype(BF16)
 
 
-def route(ids, choice, experts, parts, capacity):
+def route(choice, experts, parts, capacity):
     tokens = choice.shape[0]
     slots = experts * capacity // parts
     outs = pl.pallas_call(
         functools.partial(route_kernel, experts, parts),
-        in_specs=[SCALARS, WHOLE],
+        in_specs=[WHOLE],
         out_specs=[WHOLE] * (1 + 3 * parts),
         out_shape=[jax.ShapeDtypeStruct(choice.shape, jnp.int32)]
         + [jax.ShapeDtypeStruct((slots, tokens), BF16)] * parts
@@ -178,41 +182,45 @@
         compiler_params=PARAMS,
         cost_estimate=CHEAP,
         name="route",
-    )(ids, choice.T)
+    )(choice.T)
     return outs[0], outs[1 : 1 + parts], outs[1 + parts : 1 + 2 * parts], outs[1 + 2 * parts :]
 
 
 def state_kernel(count, sends, *refs):
-    ids, tokens = refs[:2]
-    contexts, weights = refs[2 : 2 + count], refs[2 + count : 2 + 2 * count]
-    dispatch = refs[2 + 2 * count : 2 + 2 * count + sends]
-    state, outs = refs[2 + 2 * count + sends], refs[3 + 2 * count + sends :]
-    total = tokens[...].astype(F32)
-    for context, weight in zip(contexts, weights):
-        total += dot(context[...], weight[...])
-    state[...] = total.astype(BF16)
+    tokens = refs[0]
+    contexts, weights = refs[1 : 1 + count], refs[1 + count : 1 + 2 * count]
+    dispatch = refs[1 + 2 * count : 1 + 2 * count + sends]
+    state, outs = refs[1 + 2 * count + sends], refs[2 + 2 * count + sends :]
+    tile = min(TILE, state.shape[1])
+    for at in range(0, state.shape[1], tile):
+        part = slice(at, at + tile)
+        total = tokens[:, part].astype(F32)
+        for context, weight in zip(contexts, weights):
+            total += dot(context[...], weight[:, part])
+        state[:, part] = total.astype(BF16)
     for rows, out in zip(dispatch, outs):
         width = out.shape[1]
-        at = (ids[1] & (state.shape[1] // width - 1)) * width
+        at = (position()[1] & (state.shape[1] // width - 1)) * width
         out[...] = dot(rows[...], state[:, pl.ds(pl.multiple_of(at, width), width)]).astype(BF16)
 
 
-def make_state(ids, tokens, contexts, weights, dispatch, cuts):
+def make_state(tokens, contexts, weights, dispatch, cuts):
     return pl.pallas_call(
         functools.partial(state_kernel, len(contexts), len(dispatch)),
-        in_specs=[SCALARS] + [WHOLE] * (1 + 2 * len(contexts) + len(dispatch)),
+        in_specs=[WHOLE] * (1 + 2 * len(contexts) + len(dispatch)),
         out_specs=[WHOLE] * (1 + len(dispatch)),
         out_shape=[jax.ShapeDtypeStruct(tokens.shape, BF16)]
         + [jax.ShapeDtypeStruct((rows.shape[0], tokens.shape[1] // cut), BF16) for rows, cut in zip(dispatch, cuts)],
         compiler_params=PARAMS,
         cost_estimate=CHEAP,
         name="state",
-    )(ids, tokens, *contexts, *weights, *dispatch)
-
-
-def home_kernel(experts, ids, state, dispatch, router, choice, own_a, own_b, gates, columns):
+    )(tokens, *contexts, *weights, *dispatch)
+
+
+def home_kernel(experts, state, dispatch, router, choice, own_a, own_b, gates, columns):
     half = own_a.shape[1]
-    core = ids[1] & 1
+    column = position()[1]
+    core = column & 1
     own_a[...] = dot(dispatch[...], state[:, pl.ds(pl.multiple_of(core * half, half), half)]).astype(BF16)
     own_b[...] = dot(dispatch[...], state[:, pl.ds(pl.multiple_of((1 - core) * half, half), half)]).astype(BF16)
     logits = dot(state[...], router[...], ((1,), (1,)))
@@ -222,15 +230,15 @@
     gates[:, 0:1] = jax.nn.sigmoid(first - second)
     gates[:, 1:2] = jax.nn.sigmoid(second - first)
     width = columns.shape[1]
-    columns[...] = state[:, pl.ds(pl.multiple_of(ids[1] * width, width), width)].astype(F32)
-
-
-def at_home(ids, state, dispatch, router, choice, experts, width):
+    columns[...] = state[:, pl.ds(pl.multiple_of(column * width, width), width)].astype(F32)
+
+
+def at_home(state, dispatch, router, choice, experts, width):
     tokens, features = state.shape
     slots = dispatch.shape[0]
     return pl.pallas_call(
         functools.partial(home_kernel, experts),
-        in_specs=[SCALARS] + [WHOLE] * 4,
+        in_specs=[WHOLE] * 4,
         out_specs=[WHOLE] * 4,
         out_shape=[
             jax.ShapeDtypeStruct((slots, features // 2), BF16),
@@ -241,21 +249,21 @@
         compiler_params=PARAMS,
         cost_estimate=CHEAP,
         name="home",
-    )(ids, state, dispatch, router, choice)
+    )(state, dispatch, router, choice)
 
 
 def expert_kernel(orders, *refs):
-    blocks, at = [], 1
+    blocks, at = [], 0
     for order in orders:
         blocks.append(refs[at : at + len(order)])
         at += len(order)
-    ids = refs[0]
+    column = position()[1]
     expand, shrink, keep, give, rows_here, hidden = refs[at:]
     count = blocks[0][0].shape[0]
     for block, (order, pieces) in enumerate(zip(orders, blocks)):
         for index, piece in zip(order, pieces):
             width = piece.shape[1]
-            part = pl.ds(pl.multiple_of(((ids[1] & (len(order) - 1)) ^ index) * width, width), width)
+            part = pl.ds(pl.multiple_of(((column & (len(order) - 1)) ^ index) * width, width), width)
             rows_here[block * count : (block + 1) * count, part] = piece[...]
     units = expand.shape[1]
     tile = min(TILE, units)
@@ -264,21 +272,21 @@
         hidden[:, at : at + tile] = jnp.maximum(total, 0.0).astype(BF16)
     width = keep.shape[2]
     for j in range(keep.shape[0]):
-        at = pl.multiple_of((ids[1] ^ (2 * j) ^ 1) * width, width)
+        at = pl.multiple_of((column ^ (2 * j) ^ 1) * width, width)
         give[j] = dot(hidden[...], shrink[:, pl.ds(at, width)]).astype(BF16)
     for j in range(keep.shape[0]):
-        at = pl.multiple_of((ids[1] ^ (2 * j)) * width, width)
+        at = pl.multiple_of((column ^ (2 * j)) * width, width)
         keep[j] = dot(hidden[...], shrink[:, pl.ds(at, width)])
 
 
-def run_expert(ids, orders, blocks, expand, shrink, parts):
+def run_expert(orders, blocks, expand, shrink, parts):
     pieces = [piece for block in blocks for piece in block]
     rows = pieces[0].shape[0] * len(blocks)
     features, units = expand.shape
     width = features // (2 * parts)
     return pl.pallas_call(
         functools.partial(expert_kernel, tuple(map(tuple, orders))),
-        in_specs=[SCALARS] + [WHOLE] * (2 + len(pieces)),
+        in_specs=[WHOLE] * (2 + len(pieces)),
         out_specs=[WHOLE] * 2,
         out_shape=[
             jax.ShapeDtypeStruct((parts, rows, width), F32),
@@ -288,7 +296,7 @@
         compiler_params=PARAMS,
         cost_estimate=CHEAP,
         name="expert",
-    )(ids, *pieces, expand, shrink)
+    )(*pieces, expand, shrink)
 
 
 def combine_kernel(count, gates, base, first, second, *refs):
@@ -335,7 +343,7 @@
     groups = lax.axis_size("expert")
     slices = lax.axis_size("mp")
     here, column = lax.axis_index("expert"), lax.axis_index("mp")
-    ids = jnp.stack([here, column]).astype(jnp.int32)
+    owner_rows = jnp.broadcast_to(source_owner[:, None], (8, 128))
     width = features // slices
     experts = expand_weight.shape[0] * groups
     capacity = max(2, 3 * token_count // experts)
@@ -362,7 +370,7 @@
 
     steps = range(groups) if direct else [0]
 
-    queries, source = ask(after(tokens, ids), query_weight, encoder_states[0])
+    queries, source = ask(after(tokens, owner_rows), query_weight, encoder_states[0])
     expert_bits = bits_of(groups)
     bits = bits_of(slices)
     if direct:
@@ -376,13 +384,13 @@
         for k in sorted(range(1, groups), key=lambda k: (k & (k - 1) != 0, -k)):
             answer = previous = attend(after(asked[k], previous), source, token_count)
             backs[k] = hop(answer, k, 0)
-        context = pick(ids, source_owner, [own] + [backs[k] for k in range(1, groups)])
+        context = pick(owner_rows, [own] + [backs[k] for k in range(1, groups)])
     else:
         asked = lax.all_gather(queries, "expert", axis=0, tiled=True)
         previous = attend(asked, source, token_count)
         context = lax.dynamic_slice_in_dim(spread(previous), source_owner[0] * token_count, token_count, 0)
 
-    choice, dispatch, first, second = route(ids, after(expert_choice, previous), experts, len(steps), capacity)
+    choice, dispatch, first, second = route(after(expert_choice, previous), experts, len(steps), capacity)
     weights, order = [output_weight], [0]
     for bit in bits:
         if bit == 1:
@@ -396,9 +404,9 @@
     far = set(range(2, groups)) if direct and pairs > 1 else set()
     sends = [k for k in range(2, groups)] + ([1] if groups > 1 else []) if direct else [0]
     cuts = [slices if k in far else 2 for k in sends]
-    state, *leaving = make_state(ids, tokens, contexts, weights, [dispatch[k] for k in sends], cuts)
+    state, *leaving = make_state(tokens, contexts, weights, [dispatch[k] for k in sends], cuts)
     own_a, own_b, gates, columns = at_home(
-        ids, state, dispatch[0], router_weight.T, choice, experts, width
+        state, dispatch[0], router_weight.T, choice, experts, width
     )
     expert = functools.partial(run_expert, expand=expand_weight[0], shrink=shrink_weight[0], parts=pairs)
 
@@ -420,12 +428,11 @@
     home, order = {}, [0]
     if direct:
         arrived = {k: hop(rows, k, 0) for k, rows in zip(sends, leaving)}
-        keep, give = expert(ids, [[0, 1]], [[own_a, own_b]])
-        turn_ids = after(ids, give)
+        keep, give = expert([[0, 1]], [[own_a, own_b]])
         if sends:
             give = after(give, arrived[sends[0]])
         own_sum, wait = sum_cores(keep, give), None
-        turn_ids = after(ids, own_sum)
+        earlier = own_sum
         turns = [[k for k in sends if k < groups - 1], [groups - 1]] if groups > 2 else [sends]
         for turn in turns:
             blocks, orders = [], []
@@ -437,8 +444,9 @@
                 blocks.append(pieces)
                 orders.append(places)
             if turn:
-                keep, give = expert(turn_ids, orders, blocks)
-                turn_ids = after(ids, give)
+                blocks[0][0] = after(blocks[0][0], earlier)
+                keep, give = expert(orders, blocks)
+                earlier = give
                 summed = sum_cores(keep, give)
                 for i, k in enumerate(turn):
                     rows = summed[:, i * slots : (i + 1) * slots]
@@ -452,7 +460,7 @@
         order = [0] + sorted(sends)
     else:
         mine = spread(leaving[0])
-        home[0] = send_home(0, sum_cores(*expert(ids, [[0, 1]], [[mine, hop(mine, 0, 1)]])))
+        home[0] = send_home(0, sum_cores(*expert([[0, 1]], [[mine, hop(mine, 0, 1)]])))
     results = columns
     for k in order:
         results = combine(gates, results, first[k], second[k], home[k], BF16 if k == order[-1] else F32)

time: 81.9 us -> 80.3 us (0.980)
  Pallas kernels: 16.7 us -> 12.9 us
  waiting for transfers between devices: 29.7 us -> 31.9 us
    ppermute x32, waiting for transfers between devices: 29.7 us -> 31.9 us  [hop(): return lax.ppermute(value, ('expert', 'mp'), moves)]
    pallas_call x3, Pallas kernels: 5.52 us -> 3.88 us  [run_expert(): pl.pallas_call(functools.partial(expert_kernel, tuple(map(tuple, orders))...]
    pallas_call x2, Pallas kernels: 1.61 us -> 0.63 us  [the longest x1 0.52 us: at_home(): pl.pallas_call(functools.partial(home_kernel, experts), in_specs=[WHOLE]...]
  transfers between devices with their start and end apart: 32 -> 32, of which waited for: 15 -> 15; matrix products, arithmetic and copies ran while one was open for 0% -> 0% of each run, Pallas kernels for 17% -> 14%
where the time goes in v10:
time: 80.3 us; the launch traced here: 80.2 us
  starting transfers between devices  34 us (42%)
  waiting for transfers between devices  31.9 us (40%)
  Pallas kernels  12.9 us (16%)
  between operations  0.97 us (1%)
    ppermute x32, starting transfers between devices, hop(): return lax.ppermute(value, ('expert', 'mp'), moves)  34 us
    ppermute x32, waiting for transfers between devices, hop(): return lax.ppermute(value, ('expert', 'mp'), moves)  31.9 us
    pallas_call x3, Pallas kernels, run_expert(): pl.pallas_call(functools.partial(expert_kernel, tuple(map(tuple, orders))...  3.88 us
    pallas_call x4, Pallas kernels, attend(): pl.pallas_call(attend_kernel, in_specs=[WHOLE] * 2, out_specs=WHOLE, out_...  3.09 us
    pallas_call x1, Pallas kernels, ask(): pl.pallas_call(query_kernel, in_specs=[pl.BlockSpec(memory_space=pltpu.HB...  1.82 us
  transfers between devices with their start and end apart: 32, of which 15 were waited for; matrix products, arithmetic and copies ran while one was open for 0% of the time, Pallas kernels for 14%

profile of v10, /device:TPU:0, one launch (start us, length us, event | category | flops | bytes accessed | tf_op | source)
XLA Modules:
  0.0 80.2 jit_solution(15551774165771676703)
XLA Ops:
  0.0 2.9 %collective-permute-start.9 = (bf16[256,1024]{1,0:T(8,128)(2,1)}, bf16[256,1024]{1,0:T(8,128)(2,1)S(1)}, u32[]{:S(2)}, u32[]{:S(2)}) collective-permute-start(bf16[256,1024]{1,0:T(8,128)(2,1)} %refs_5_), channel_id=1, source_target_pairs={{0,2},{1,3},{2,0},{3,1},{4,6},{5,7},{6,4},{7,5},{8,10},{9,11},{10,... | collective-permute-start | bytes 1572872 | tf_op jit(solution)/shard_map/ppermute | solution.py:362
  3.6 1.8 %query.1 = (bf16[256,256]{1,0:T(8,128)(2,1)S(1)}, bf16[2,512,256]{2,1,0:T(8,128)(2,1)S(1)}) custom-call(bf16[256,1024]{1,0:T(8,128)(2,1)} %refs_0_.1, bf16[1024,256]{1,0:T(8,128)(2,1)} %weight.1, bf16[2,512,256]{2,1,0:T(8,128)(2,1)} %bitcast.39), custom_call_target="tpu_custom_call" | custom-call | tf_op jit(solution)/shard_map/query/pallas_call | solution.py:63
  5.4 0.0 copy-start.3
  5.4 0.0 copy-start.5
  5.5 0.0 copy-start.2
  5.5 2.7 %collective-permute-start.1 = (bf16[256,256]{1,0:T(8,128)(2,1)S(1)}, bf16[256,256]{1,0:T(8,128)(2,1)S(1)}, u32[]{:S(2)}, u32[]{:S(2)}) collective-permute-start(bf16[256,256]{1,0:T(8,128)(2,1)S(1)} %get-tuple-element.47.queries), channel_id=1, source_target_pairs={{0,8},{1,9},{2,10},{3,11},{4,12},{5,13},{6,14},{7,15},{8,0},{9,1},... | collective-permute-start | bytes 393224 | tf_op jit(solution)/shard_map/ppermute | solution.py:362
  8.1 1.6 %collective-permute-start = (bf16[256,256]{1,0:T(8,128)(2,1)S(1)}, bf16[256,256]{1,0:T(8,128)(2,1)S(1)}, u32[]{:S(2)}, u32[]{:S(2)}) collective-permute-start(bf16[256,256]{1,0:T(8,128)(2,1)S(1)} %get-tuple-element.47.queries), channel_id=1, source_target_pairs={{0,4},{1,5},{2,6},{3,7},{4,0},{5,1},{6,2},{7,3},{8,12},{9,13},{10,... | collective-permute-start | bytes 393224 | tf_op jit(solution)/shard_map/ppermute | solution.py:362
  9.7 0.8 attend.4.refs_0_
  10.5 3.8 %collective-permute-done.1.queries = bf16[256,256]{1,0:T(8,128)(2,1)S(1)} collective-permute-done((bf16[256,256]{1,0:T(8,128)(2,1)S(1)}, bf16[256,256]{1,0:T(8,128)(2,1)S(1)}, u32[]{:S(2)}, u32[]{:S(2)}) %collective-permute-start.1) | collective-permute-done | bytes 131104 | tf_op jit(solution)/shard_map/ppermute | solution.py:362
  14.3 0.6 collective-permute-start.4
  14.9 0.8 attend.5
  15.6 3.4 %collective-permute-start.3 = (bf16[256,256]{1,0:T(8,128)(2,1)S(1)}, bf16[256,256]{1,0:T(8,128)(2,1)S(1)}, u32[]{:S(2)}, u32[]{:S(2)}) collective-permute-start(bf16[256,256]{1,0:T(8,128)(2,1)S(1)} %attend.5), channel_id=1, source_target_pairs={{0,8},{1,9},{2,10},{3,11},{4,12},{5,13},{6,14},{7,15},{8,0},{9,1},... | collective-permute-start | bytes 393224 | tf_op jit(solution)/shard_map/ppermute | solution.py:362
  19.1 0.8 attend.6
  19.9 0.1 collective-permute-start.2
  20.0 0.0 collective-permute-done.4.queries
  20.0 0.8 attend.7
  20.7 0.0 copy-start.4
  20.8 5.7 %collective-permute-start.5 = (bf16[256,256]{1,0:T(8,128)(2,1)S(1)}, bf16[256,256]{1,0:T(8,128)(2,1)S(1)}, u32[]{:S(2)}, u32[]{:S(2)}) collective-permute-start(bf16[256,256]{1,0:T(8,128)(2,1)S(1)} %attend.7), channel_id=1, source_target_pairs={{0,12},{1,13},{2,14},{3,15},{4,8},{5,9},{6,10},{7,11},{8,4},{9,5},... | collective-permute-start | bytes 393224 | tf_op jit(solution)/shard_map/ppermute | solution.py:362
  26.4 0.0 collective-permute-done.3.refs_2_
  26.4 3.5 %collective-permute-done.5.refs_3_ = bf16[256,256]{1,0:T(8,128)(2,1)S(1)} collective-permute-done((bf16[256,256]{1,0:T(8,128)(2,1)S(1)}, bf16[256,256]{1,0:T(8,128)(2,1)S(1)}, u32[]{:S(2)}, u32[]{:S(2)}) %collective-permute-start.5) | collective-permute-done | bytes 131104 | tf_op jit(solution)/shard_map/ppermute | solution.py:362
  29.9 0.1 pick.1.refs_1_
  30.1 0.1 collective-permute-start.10
  30.2 0.5 collective-permute-start.11
  30.6 0.5 collective-permute-start.6
  31.2 1.0 %route.1 = (s32[256,2]{1,0:T(8,128)S(1)}, bf16[192,256]{1,0:T(8,128)(2,1)S(1)}, bf16[192,256]{1,0:T(8,128)(2,1)S(1)}, bf16[192,256]{1,0:T(8,128)(2,1)S(1)}, bf16...) custom-call(s32[2,256]{1,0:T(2,128)S(1)} %bitcast.38), custom_call_target="tpu_custom_call" | custom-call | tf_op jit(solution)/shard_map/route/pallas_call | solution.py:175
  32.1 0.1 collective-permute-start.7
  32.2 3.9 %collective-permute-done.6.refs_2_ = bf16[256,256]{1,0:T(8,128)(2,1)S(1)} collective-permute-done((bf16[256,256]{1,0:T(8,128)(2,1)S(1)}, bf16[256,256]{1,0:T(8,128)(2,1)S(1)}, u32[]{:S(2)}, u32[]{:S(2)}) %collective-permute-start.6) | collective-permute-done | bytes 131104 | tf_op jit(solution)/shard_map/ppermute | solution.py:362
  36.1 1.3 %collective-permute-done.8.refs_4_ = bf16[256,256]{1,0:T(8,128)(2,1)S(1)} collective-permute-done((bf16[256,256]{1,0:T(8,128)(2,1)S(1)}, bf16[256,256]{1,0:T(8,128)(2,1)S(1)}, u32[]{:S(2)}, u32[]{:S(2)}) %collective-permute-start.8) | collective-permute-done | bytes 131104 | tf_op jit(solution)/shard_map/ppermute | solution.py:362
  37.5 0.0 copy-start
  37.5 0.0 copy-start.1
  37.5 1.0 %state.1 = (bf16[256,1024]{1,0:T(8,128)(2,1)S(1)}, bf16[192,256]{1,0:T(8,128)(2,1)S(1)}, bf16[192,256]{1,0:T(8,128)(2,1)S(1)}, bf16[192,512]{1,0:T(8,128)(2,1)S(1)}) custom-call(bf16[256,1024]{1,0:T(8,128)(2,1)S(1)} %copy-done.2, bf16[256,256]{1,0:T(8,128)(2,1)S(1)} %pick.1.refs_1_, bf16[256,256]{1,0:T(8,128)(2,1)S(1)} %collective-permute-done.6.refs_2_, ...), custom_call_target="tpu_custom_call" | custom-call | tf_op jit(solution)/shard_map/state/pallas_call | solution.py:208
  38.5 2.6 %collective-permute-start.12 = (bf16[192,256]{1,0:T(8,128)(2,1)S(1)}, bf16[192,256]{1,0:T(8,128)(2,1)S(1)}, u32[]{:S(2)}, u32[]{:S(2)}) collective-permute-start(bf16[192,256]{1,0:T(8,128)(2,1)S(1)} %get-tuple-element.70), channel_id=1, source_target_pairs={{0,8},{1,9},{2,10},{3,11},{4,12},{5,13},{6,14},{7,15},{8,0},{9,1},... | collective-permute-start | bytes 294920 | tf_op jit(solution)/shard_map/ppermute | solution.py:362
  41.1 1.4 %collective-permute-start.25 = (bf16[192,256]{1,0:T(8,128)(2,1)S(1)}, bf16[192,256]{1,0:T(8,128)(2,1)S(1)}, u32[]{:S(2)}, u32[]{:S(2)}) collective-permute-start(bf16[192,256]{1,0:T(8,128)(2,1)S(1)} %get-tuple-element.83), channel_id=1, source_target_pairs={{0,12},{1,13},{2,14},{3,15},{4,8},{5,9},{6,10},{7,11},{8,4},{9,5},... | collective-permute-start | bytes 294920 | tf_op jit(solution)/shard_map/ppermute | solution.py:362
  42.5 0.0 collective-permute-start.17
  42.5 0.5 home.1
  43.1 1.0 %expert.3 = (f32[2,192,256]{2,1,0:T(8,128)S(1)}, bf16[2,192,256]{2,1,0:T(8,128)(2,1)S(1)}) custom-call(bf16[192,512]{1,0:T(8,128)(2,1)S(1)} %get-tuple-element.66.refs_0_, bf16[192,512]{1,0:T(8,128)(2,1)S(1)} %get-tuple-element.67.refs_1_, bf16[1024,1024]{1,0:T(8,128)(2,1)S(1)} %bitcast.31, bf16[1024,1024]{1,0:T(8,128)(2,1)S(1)} %bitcast.34), custom_call_target="tpu_custom_call" | custom-call | tf_op jit(solution)/shard_map/expert/pallas_call | solution.py:287
  44.1 5.3 %collective-permute-done.12.refs_0_ = bf16[192,256]{1,0:T(8,128)(2,1)S(1)} collective-permute-done((bf16[192,256]{1,0:T(8,128)(2,1)S(1)}, bf16[192,256]{1,0:T(8,128)(2,1)S(1)}, u32[]{:S(2)}, u32[]{:S(2)}) %collective-permute-start.12) | collective-permute-done | bytes 98336 | tf_op jit(solution)/shard_map/ppermute | solution.py:362
  49.4 0.5 collective-permute-start.14
  49.9 1.5 %collective-permute-start.26 = (bf16[192,256]{1,0:T(8,128)(2,1)S(1)}, bf16[192,256]{1,0:T(8,128)(2,1)S(1)}, u32[]{:S(2)}, u32[]{:S(2)}) collective-permute-start(bf16[192,256]{1,0:T(8,128)(2,1)S(1)} %collective-permute-done.25.refs_0_), channel_id=1, source_target_pairs={{0,2},{1,3},{2,0},{3,1},{4,6},{5,7},{6,4},{7,5},{8,10},{9,11},{10,... | collective-permute-start | bytes 294920 | tf_op jit(solution)/shard_map/ppermute | solution.py:362
  51.4 0.6 collective-permute-done.17.refs_4_
  52.0 3.0 %collective-permute-done.14.refs_1_ = bf16[192,256]{1,0:T(8,128)(2,1)S(1)} collective-permute-done((bf16[192,256]{1,0:T(8,128)(2,1)S(1)}, bf16[192,256]{1,0:T(8,128)(2,1)S(1)}, u32[]{:S(2)}, u32[]{:S(2)}) %collective-permute-start.14) | collective-permute-done | bytes 98336 | tf_op jit(solution)/shard_map/ppermute | solution.py:362
  55.0 1.7 %collective-permute-done.26.refs_1_ = bf16[192,256]{1,0:T(8,128)(2,1)S(1)} collective-permute-done((bf16[192,256]{1,0:T(8,128)(2,1)S(1)}, bf16[192,256]{1,0:T(8,128)(2,1)S(1)}, u32[]{:S(2)}, u32[]{:S(2)}) %collective-permute-start.26) | collective-permute-done | bytes 98336 | tf_op jit(solution)/shard_map/ppermute | solution.py:362
  56.7 0.5 collective-permute-start.28
  57.3 0.7 collective-permute-done.16.refs_3_
  58.0 1.9 %expert.4 = (f32[2,384,256]{2,1,0:T(8,128)S(1)}, bf16[2,384,256]{2,1,0:T(8,128)(2,1)S(1)}) custom-call(bf16[192,256]{1,0:T(8,128)(2,1)S(1)} %collective-permute-done.12.refs_0_, bf16[192,256]{1,0:T(8,128)(2,1)S(1)} %collective-permute-done.14.refs_1_, bf16[192,256]{1,0:T(8,128)(2,1)S(1)} %collective-permute-done.15.refs_2_, ...), custom_call_target="tpu_custom_call" | custom-call | tf_op jit(solution)/shard_map/expert/pallas_call | solution.py:287
  59.9 0.2 collective-permute-start.19
  60.1 1.0 %expert.5 = (f32[2,192,256]{2,1,0:T(8,128)S(1)}, bf16[2,192,256]{2,1,0:T(8,128)(2,1)S(1)}) custom-call(bf16[192,256]{1,0:T(8,128)(2,1)S(1)} %collective-permute-done.25.refs_0_, bf16[192,256]{1,0:T(8,128)(2,1)S(1)} %collective-permute-done.26.refs_1_, bf16[192,256]{1,0:T(8,128)(2,1)S(1)} %collective-permute-done.27.refs_2_, ...), custom_call_target="tpu_custom_call" | custom-call | tf_op jit(solution)/shard_map/expert/pallas_call | solution.py:287
  61.1 0.4 collective-permute-start.29
  61.5 1.1 %collective-permute-done.29 = bf16[2,192,256]{2,1,0:T(8,128)(2,1)S(1)} collective-permute-done((bf16[2,192,256]{2,1,0:T(8,128)(2,1)S(1)}, bf16[2,192,256]{2,1,0:T(8,128)(2,1)S(1)}, u32[]{:S(2)}, u32[]{:S(2)}) %collective-permute-start.29) | collective-permute-done | bytes 196640 | tf_op jit(solution)/shard_map/ppermute | solution.py:362
  62.7 0.1 fusion.5
  62.8 0.6 collective-permute-start.20
  63.4 1.5 %collective-permute-start.30 = (bf16[192,256]{1,0:T(8,128)(2,1)S(1)}, bf16[192,256]{1,0:T(8,128)(2,1)S(1)}, u32[]{:S(2)}, u32[]{:S(2)}) collective-permute-start(bf16[192,256]{1,0:T(8,128)(2,1)S(1)} %fusion.4), channel_id=1, source_target_pairs={{0,2},{1,3},{2,0},{3,1},{4,6},{5,7},{6,4},{7,5},{8,10},{9,11},{10,... | collective-permute-start | bytes 294920 | tf_op jit(solution)/shard_map/ppermute | solution.py:362
  65.0 2.0 %collective-permute-start.22 = (bf16[192,256]{1,0:T(8,128)(2,1)S(1)}, bf16[192,256]{1,0:T(8,128)(2,1)S(1)}, u32[]{:S(2)}, u32[]{:S(2)}) collective-permute-start(bf16[192,256]{1,0:T(8,128)(2,1)S(1)} %get-tuple-element.90), channel_id=1, source_target_pairs={{0,4},{1,5},{2,6},{3,7},{4,0},{5,1},{6,2},{7,3},{8,12},{9,13},{10,... | collective-permute-start | bytes 294920 | tf_op jit(solution)/shard_map/ppermute | solution.py:362
  67.0 2.6 %collective-permute-done.20 = bf16[192,256]{1,0:T(8,128)(2,1)S(1)} collective-permute-done((bf16[192,256]{1,0:T(8,128)(2,1)S(1)}, bf16[192,256]{1,0:T(8,128)(2,1)S(1)}, u32[]{:S(2)}, u32[]{:S(2)}) %collective-permute-start.20) | collective-permute-done | bytes 98336 | tf_op jit(solution)/shard_map/ppermute | solution.py:362
  69.6 1.8 %collective-permute-start.24 = (bf16[192,256]{1,0:T(8,128)(2,1)S(1)}, bf16[192,256]{1,0:T(8,128)(2,1)S(1)}, u32[]{:S(2)}, u32[]{:S(2)}) collective-permute-start(bf16[192,256]{1,0:T(8,128)(2,1)S(1)} %fusion.3), channel_id=1, source_target_pairs={{0,8},{1,9},{2,10},{3,11},{4,12},{5,13},{6,14},{7,15},{8,0},{9,1},... | collective-permute-start | bytes 294920 | tf_op jit(solution)/shard_map/ppermute | solution.py:362
  71.5 1.2 %collective-permute-done.30 = bf16[192,256]{1,0:T(8,128)(2,1)S(1)} collective-permute-done((bf16[192,256]{1,0:T(8,128)(2,1)S(1)}, bf16[192,256]{1,0:T(8,128)(2,1)S(1)}, u32[]{:S(2)}, u32[]{:S(2)}) %collective-permute-start.30) | collective-permute-done | bytes 98336 | tf_op jit(solution)/shard_map/ppermute | solution.py:362
  72.7 2.7 %collective-permute-start.31 = (bf16[192,256]{1,0:T(8,128)(2,1)S(1)}, bf16[192,256]{1,0:T(8,128)(2,1)S(1)}, u32[]{:S(2)}, u32[]{:S(2)}) collective-permute-start(bf16[192,256]{1,0:T(8,128)(2,1)S(1)} %fusion.1), channel_id=1, source_target_pairs={{0,12},{1,13},{2,14},{3,15},{4,8},{5,9},{6,10},{7,11},{8,4},{9,5},... | collective-permute-start | bytes 294920 | tf_op jit(solution)/shard_map/ppermute | solution.py:362
  75.5 0.6 collective-permute-done.21.refs_1_
  76.1 0.2 combine.4.base
  76.3 0.2 combine.5.base
  76.6 1.4 %collective-permute-done.24.refs_0_ = bf16[192,256]{1,0:T(8,128)(2,1)S(1)} collective-permute-done((bf16[192,256]{1,0:T(8,128)(2,1)S(1)}, bf16[192,256]{1,0:T(8,128)(2,1)S(1)}, u32[]{:S(2)}, u32[]{:S(2)}) %collective-permute-start.24) | collective-permute-done | bytes 98336 | tf_op jit(solution)/shard_map/ppermute | solution.py:362
  78.0 0.2 combine.6.base
  78.3 1.0 %collective-permute-done.31.refs_0_ = bf16[192,256]{1,0:T(8,128)(2,1)S(1)} collective-permute-done((bf16[192,256]{1,0:T(8,128)(2,1)S(1)}, bf16[192,256]{1,0:T(8,128)(2,1)S(1)}, u32[]{:S(2)}, u32[]{:S(2)}) %collective-permute-start.31) | collective-permute-done | bytes 98336 | tf_op jit(solution)/shard_map/ppermute | solution.py:362
  79.3 0.9 %combine.7 = bf16[256,256]{1,0:T(8,128)(2,1)} custom-call(f32[256,2]{1,0:T(8,128)S(1)} %get-tuple-element.62.gates, f32[256,256]{1,0:T(8,128)S(1)} %combine.6.base, bf16[256,192]{1,0:T(8,128)(2,1)S(1)} %get-tuple-element.81.first, bf16[256,192]{1,0:T(8,128)(2,1)S(1)} %get-tuple-element.82.second, bf16[192,256]{1,0:T(8,128)(2,1)S(1)} %collective-permute-done.31.refs_0_), custom_call_target="tpu_custom_call" | custom-call | tf_op jit(solution)/shard_map/combine/pallas_call | solution.py:313
  (37 shorter events, 0.2 us)
Async XLA Ops:
  0.0 30.1 %collective-permute-start.9 = (bf16[256,1024]{1,0:T(8,128)(2,1)}, bf16[256,1024]{1,0:T(8,128)(2,1)S(1)}, u32[]{:S(2)}, u32[]{:S(2)}) collective-permute-start(bf16[256,1024]{1,0:T(8,128)(2,1)} %refs_5_), channel_id=1, source_target_pairs={{0,2},{1,3},{2,0},{3,1},{4,6},{5,7},{6,4},{7,5},{8,10},{9,11},{10,... | collective-permute-start | bytes 1572872 | tf_op jit(solution)/shard_map/ppermute | solution.py:362
  5.4 24.6 %copy-start.3 = (bf16[256,1024]{1,0:T(8,128)(2,1)S(1)}, bf16[256,1024]{1,0:T(8,128)(2,1)}, u32[]{:S(2)}) copy-start(bf16[256,1024]{1,0:T(8,128)(2,1)} %refs_5_) | copy-start | bytes 1572868
  5.4 25.7 %copy-start.5 = (s32[256,2]{0,1:T(2,128)S(1)}, s32[256,2]{0,1:T(2,128)}, u32[]{:S(2)}) copy-start(s32[256,2]{0,1:T(2,128)} %param.15) | copy-start | bytes 6148
  5.5 32.0 %copy-start.2 = (bf16[256,1024]{1,0:T(8,128)(2,1)S(1)}, bf16[256,1024]{1,0:T(8,128)(2,1)}, u32[]{:S(2)}) copy-start(bf16[256,1024]{1,0:T(8,128)(2,1)} %refs_0_.1) | copy-start | bytes 1572868
  5.5 8.8 %collective-permute-start.1 = (bf16[256,256]{1,0:T(8,128)(2,1)S(1)}, bf16[256,256]{1,0:T(8,128)(2,1)S(1)}, u32[]{:S(2)}, u32[]{:S(2)}) collective-permute-start(bf16[256,256]{1,0:T(8,128)(2,1)S(1)} %get-tuple-element.47.queries), channel_id=1, source_target_pairs={{0,8},{1,9},{2,10},{3,11},{4,12},{5,13},{6,14},{7,15},{8,0},{9,1},... | collective-permute-start | bytes 393224 | tf_op jit(solution)/shard_map/ppermute | solution.py:362
  8.1 11.0 %collective-permute-start = (bf16[256,256]{1,0:T(8,128)(2,1)S(1)}, bf16[256,256]{1,0:T(8,128)(2,1)S(1)}, u32[]{:S(2)}, u32[]{:S(2)}) collective-permute-start(bf16[256,256]{1,0:T(8,128)(2,1)S(1)} %get-tuple-element.47.queries), channel_id=1, source_target_pairs={{0,4},{1,5},{2,6},{3,7},{4,0},{5,1},{6,2},{7,3},{8,12},{9,13},{10,... | collective-permute-start | bytes 393224 | tf_op jit(solution)/shard_map/ppermute | solution.py:362
  14.3 5.7 %collective-permute-start.4 = (bf16[256,256]{1,0:T(8,128)(2,1)S(1)}, bf16[256,256]{1,0:T(8,128)(2,1)S(1)}, u32[]{:S(2)}, u32[]{:S(2)}) collective-permute-start(bf16[256,256]{1,0:T(8,128)(2,1)S(1)} %collective-permute-done.1.queries), channel_id=1, source_target_pairs={{0,4},{1,5},{2,6},{3,7},{4,0},{5,1},{6,2},{7,3},{8,12},{9,13},{10,... | collective-permute-start | bytes 393224 | tf_op jit(solution)/shard_map/ppermute | solution.py:362
  15.6 10.8 %collective-permute-start.3 = (bf16[256,256]{1,0:T(8,128)(2,1)S(1)}, bf16[256,256]{1,0:T(8,128)(2,1)S(1)}, u32[]{:S(2)}, u32[]{:S(2)}) collective-permute-start(bf16[256,256]{1,0:T(8,128)(2,1)S(1)} %attend.5), channel_id=1, source_target_pairs={{0,8},{1,9},{2,10},{3,11},{4,12},{5,13},{6,14},{7,15},{8,0},{9,1},... | collective-permute-start | bytes 393224 | tf_op jit(solution)/shard_map/ppermute | solution.py:362
  19.9 6.6 %collective-permute-start.2 = (bf16[256,256]{1,0:T(8,128)(2,1)S(1)}, bf16[256,256]{1,0:T(8,128)(2,1)S(1)}, u32[]{:S(2)}, u32[]{:S(2)}) collective-permute-start(bf16[256,256]{1,0:T(8,128)(2,1)S(1)} %attend.6), channel_id=1, source_target_pairs={{0,4},{1,5},{2,6},{3,7},{4,0},{5,1},{6,2},{7,3},{8,12},{9,13},{10,... | collective-permute-start | bytes 393224 | tf_op jit(solution)/shard_map/ppermute | solution.py:362
  20.7 21.8 %copy-start.4 = (bf16[1024,4]{0,1:T(4,128)(2,1)S(1)}, bf16[1024,4]{0,1:T(4,128)(2,1)}, u32[]{:S(2)}) copy-start(bf16[1024,4]{0,1:T(4,128)(2,1)} %param.14) | copy-start | bytes 24580
  20.8 9.2 %collective-permute-start.5 = (bf16[256,256]{1,0:T(8,128)(2,1)S(1)}, bf16[256,256]{1,0:T(8,128)(2,1)S(1)}, u32[]{:S(2)}, u32[]{:S(2)}) collective-permute-start(bf16[256,256]{1,0:T(8,128)(2,1)S(1)} %attend.7), channel_id=1, source_target_pairs={{0,12},{1,13},{2,14},{3,15},{4,8},{5,9},{6,10},{7,11},{8,4},{9,5},... | collective-permute-start | bytes 393224 | tf_op jit(solution)/shard_map/ppermute | solution.py:362
  30.1 7.4 %collective-permute-start.10 = (bf16[256,1024]{1,0:T(8,128)(2,1)S(1)}, bf16[256,1024]{1,0:T(8,128)(2,1)S(1)}, u32[]{:S(2)}, u32[]{:S(2)}) collective-permute-start(bf16[256,1024]{1,0:T(8,128)(2,1)S(1)} %copy-done.3), channel_id=1, source_target_pairs={{0,1},{1,0},{2,3},{3,2},{4,5},{5,4},{6,7},{7,6},{8,9},{9,8},{10,11... | collective-permute-start | bytes 1572872 | tf_op jit(solution)/shard_map/ppermute | solution.py:362
  30.2 7.3 %collective-permute-start.11 = (bf16[256,1024]{1,0:T(8,128)(2,1)S(1)}, bf16[256,1024]{1,0:T(8,128)(2,1)S(1)}, u32[]{:S(2)}, u32[]{:S(2)}) collective-permute-start(bf16[256,1024]{1,0:T(8,128)(2,1)S(1)} %collective-permute-done.9.refs_6_), channel_id=1, source_target_pairs={{0,1},{1,0},{2,3},{3,2},{4,5},{5,4},{6,7},{7,6},{8,9},{9,8},{10,11... | collective-permute-start | bytes 1572872 | tf_op jit(solution)/shard_map/ppermute | solution.py:362
  30.6 5.5 %collective-permute-start.6 = (bf16[256,256]{1,0:T(8,128)(2,1)S(1)}, bf16[256,256]{1,0:T(8,128)(2,1)S(1)}, u32[]{:S(2)}, u32[]{:S(2)}) collective-permute-start(bf16[256,256]{1,0:T(8,128)(2,1)S(1)} %pick.1.refs_1_), channel_id=1, source_target_pairs={{0,2},{1,3},{2,0},{3,1},{4,6},{5,7},{6,4},{7,5},{8,10},{9,11},{10,... | collective-permute-start | bytes 393224 | tf_op jit(solution)/shard_map/ppermute | solution.py:362
  32.1 4.0 %collective-permute-start.7 = (bf16[256,256]{1,0:T(8,128)(2,1)S(1)}, bf16[256,256]{1,0:T(8,128)(2,1)S(1)}, u32[]{:S(2)}, u32[]{:S(2)}) collective-permute-start(bf16[256,256]{1,0:T(8,128)(2,1)S(1)} %pick.1.refs_1_), channel_id=1, source_target_pairs={{0,1},{1,0},{2,3},{3,2},{4,5},{5,4},{6,7},{7,6},{8,9},{9,8},{10,11... | collective-permute-start | bytes 393224 | tf_op jit(solution)/shard_map/ppermute | solution.py:362
  36.1 1.3 %collective-permute-start.8 = (bf16[256,256]{1,0:T(8,128)(2,1)S(1)}, bf16[256,256]{1,0:T(8,128)(2,1)S(1)}, u32[]{:S(2)}, u32[]{:S(2)}) collective-permute-start(bf16[256,256]{1,0:T(8,128)(2,1)S(1)} %collective-permute-done.6.refs_2_), channel_id=1, source_target_pairs={{0,1},{1,0},{2,3},{3,2},{4,5},{5,4},{6,7},{7,6},{8,9},{9,8},{10,11... | collective-permute-start | bytes 393224 | tf_op jit(solution)/shard_map/ppermute | solution.py:362
  37.5 5.5 %copy-start = (bf16[1,1024,1024]{2,1,0:T(8,128)(2,1)S(1)}, bf16[1,1024,1024]{2,1,0:T(8,128)(2,1)}, u32[]{:S(2)}) copy-start(bf16[1,1024,1024]{2,1,0:T(8,128)(2,1)} %param.16) | copy-start | bytes 6291460
  37.5 5.5 %copy-start.1 = (bf16[1,1024,1024]{2,1,0:T(8,128)(2,1)S(1)}, bf16[1,1024,1024]{2,1,0:T(8,128)(2,1)}, u32[]{:S(2)}) copy-start(bf16[1,1024,1024]{2,1,0:T(8,128)(2,1)} %param.17) | copy-start | bytes 6291460
  38.5 10.9 %collective-permute-start.12 = (bf16[192,256]{1,0:T(8,128)(2,1)S(1)}, bf16[192,256]{1,0:T(8,128)(2,1)S(1)}, u32[]{:S(2)}, u32[]{:S(2)}) collective-permute-start(bf16[192,256]{1,0:T(8,128)(2,1)S(1)} %get-tuple-element.70), channel_id=1, source_target_pairs={{0,8},{1,9},{2,10},{3,11},{4,12},{5,13},{6,14},{7,15},{8,0},{9,1},... | collective-permute-start | bytes 294920 | tf_op jit(solution)/shard_map/ppermute | solution.py:362
  41.1 8.9 %collective-permute-start.25 = (bf16[192,256]{1,0:T(8,128)(2,1)S(1)}, bf16[192,256]{1,0:T(8,128)(2,1)S(1)}, u32[]{:S(2)}, u32[]{:S(2)}) collective-permute-start(bf16[192,256]{1,0:T(8,128)(2,1)S(1)} %get-tuple-element.83), channel_id=1, source_target_pairs={{0,12},{1,13},{2,14},{3,15},{4,8},{5,9},{6,10},{7,11},{8,4},{9,5},... | collective-permute-start | bytes 294920 | tf_op jit(solution)/shard_map/ppermute | solution.py:362
  42.5 9.5 %collective-permute-start.17 = (bf16[192,512]{1,0:T(8,128)(2,1)S(1)}, bf16[192,512]{1,0:T(8,128)(2,1)S(1)}, u32[]{:S(2)}, u32[]{:S(2)}) collective-permute-start(bf16[192,512]{1,0:T(8,128)(2,1)S(1)} %get-tuple-element.73), channel_id=1, source_target_pairs={{0,4},{1,5},{2,6},{3,7},{4,0},{5,1},{6,2},{7,3},{8,12},{9,13},{10,... | collective-permute-start | bytes 589832 | tf_op jit(solution)/shard_map/ppermute | solution.py:362
  49.4 7.3 %collective-permute-start.13 = (bf16[2,192,256]{2,1,0:T(8,128)(2,1)S(1)}, bf16[2,192,256]{2,1,0:T(8,128)(2,1)S(1)}, u32[]{:S(2)}, u32[]{:S(2)}) collective-permute-start(bf16[2,192,256]{2,1,0:T(8,128)(2,1)S(1)} %get-tuple-element.71), channel_id=1, source_target_pairs={{0,1},{1,0},{2,3},{3,2},{4,5},{5,4},{6,7},{7,6},{8,9},{9,8},{10,11... | collective-permute-start | bytes 589832 | tf_op jit(solution)/shard_map/ppermute | solution.py:362
  49.4 5.6 %collective-permute-start.14 = (bf16[192,256]{1,0:T(8,128)(2,1)S(1)}, bf16[192,256]{1,0:T(8,128)(2,1)S(1)}, u32[]{:S(2)}, u32[]{:S(2)}) collective-permute-start(bf16[192,256]{1,0:T(8,128)(2,1)S(1)} %collective-permute-done.12.refs_0_), channel_id=1, source_target_pairs={{0,2},{1,3},{2,0},{3,1},{4,6},{5,7},{6,4},{7,5},{8,10},{9,11},{10,... | collective-permute-start | bytes 294920 | tf_op jit(solution)/shard_map/ppermute | solution.py:362
  49.9 6.8 %collective-permute-start.26 = (bf16[192,256]{1,0:T(8,128)(2,1)S(1)}, bf16[192,256]{1,0:T(8,128)(2,1)S(1)}, u32[]{:S(2)}, u32[]{:S(2)}) collective-permute-start(bf16[192,256]{1,0:T(8,128)(2,1)S(1)} %collective-permute-done.25.refs_0_), channel_id=1, source_target_pairs={{0,2},{1,3},{2,0},{3,1},{4,6},{5,7},{6,4},{7,5},{8,10},{9,11},{10,... | collective-permute-start | bytes 294920 | tf_op jit(solution)/shard_map/ppermute | solution.py:362
  51.4 5.8 %collective-permute-start.15 = (bf16[192,256]{1,0:T(8,128)(2,1)S(1)}, bf16[192,256]{1,0:T(8,128)(2,1)S(1)}, u32[]{:S(2)}, u32[]{:S(2)}) collective-permute-start(bf16[192,256]{1,0:T(8,128)(2,1)S(1)} %collective-permute-done.12.refs_0_), channel_id=1, source_target_pairs={{0,1},{1,0},{2,3},{3,2},{4,5},{5,4},{6,7},{7,6},{8,9},{9,8},{10,11... | collective-permute-start | bytes 294920 | tf_op jit(solution)/shard_map/ppermute | solution.py:362
  52.0 8.1 %collective-permute-start.27 = (bf16[192,256]{1,0:T(8,128)(2,1)S(1)}, bf16[192,256]{1,0:T(8,128)(2,1)S(1)}, u32[]{:S(2)}, u32[]{:S(2)}) collective-permute-start(bf16[192,256]{1,0:T(8,128)(2,1)S(1)} %collective-permute-done.25.refs_0_), channel_id=1, source_target_pairs={{0,1},{1,0},{2,3},{3,2},{4,5},{5,4},{6,7},{7,6},{8,9},{9,8},{10,11... | collective-permute-start | bytes 294920 | tf_op jit(solution)/shard_map/ppermute | solution.py:362
  55.0 3.0 %collective-permute-start.18 = (bf16[192,512]{1,0:T(8,128)(2,1)S(1)}, bf16[192,512]{1,0:T(8,128)(2,1)S(1)}, u32[]{:S(2)}, u32[]{:S(2)}) collective-permute-start(bf16[192,512]{1,0:T(8,128)(2,1)S(1)} %collective-permute-done.17.refs_4_), channel_id=1, source_target_pairs={{0,1},{1,0},{2,3},{3,2},{4,5},{5,4},{6,7},{7,6},{8,9},{9,8},{10,11... | collective-permute-start | bytes 589832 | tf_op jit(solution)/shard_map/ppermute | solution.py:362
  56.7 1.3 %collective-permute-start.16 = (bf16[192,256]{1,0:T(8,128)(2,1)S(1)}, bf16[192,256]{1,0:T(8,128)(2,1)S(1)}, u32[]{:S(2)}, u32[]{:S(2)}) collective-permute-start(bf16[192,256]{1,0:T(8,128)(2,1)S(1)} %collective-permute-done.14.refs_1_), channel_id=1, source_target_pairs={{0,1},{1,0},{2,3},{3,2},{4,5},{5,4},{6,7},{7,6},{8,9},{9,8},{10,11... | collective-permute-start | bytes 294920 | tf_op jit(solution)/shard_map/ppermute | solution.py:362
  56.7 3.4 %collective-permute-start.28 = (bf16[192,256]{1,0:T(8,128)(2,1)S(1)}, bf16[192,256]{1,0:T(8,128)(2,1)S(1)}, u32[]{:S(2)}, u32[]{:S(2)}) collective-permute-start(bf16[192,256]{1,0:T(8,128)(2,1)S(1)} %collective-permute-done.26.refs_1_), channel_id=1, source_target_pairs={{0,1},{1,0},{2,3},{3,2},{4,5},{5,4},{6,7},{7,6},{8,9},{9,8},{10,11... | collective-permute-start | bytes 294920 | tf_op jit(solution)/shard_map/ppermute | solution.py:362
  59.9 2.8 %collective-permute-start.19 = (bf16[2,384,256]{2,1,0:T(8,128)(2,1)S(1)}, bf16[2,384,256]{2,1,0:T(8,128)(2,1)S(1)}, u32[]{:S(2)}, u32[]{:S(2)}) collective-permute-start(bf16[2,384,256]{2,1,0:T(8,128)(2,1)S(1)} %get-tuple-element.75), channel_id=1, source_target_pairs={{0,1},{1,0},{2,3},{3,2},{4,5},{5,4},{6,7},{7,6},{8,9},{9,8},{10,11... | collective-permute-start | bytes 1179656 | tf_op jit(solution)/shard_map/ppermute | solution.py:362
  61.1 1.5 %collective-permute-start.29 = (bf16[2,192,256]{2,1,0:T(8,128)(2,1)S(1)}, bf16[2,192,256]{2,1,0:T(8,128)(2,1)S(1)}, u32[]{:S(2)}, u32[]{:S(2)}) collective-permute-start(bf16[2,192,256]{2,1,0:T(8,128)(2,1)S(1)} %get-tuple-element.86), channel_id=1, source_target_pairs={{0,1},{1,0},{2,3},{3,2},{4,5},{5,4},{6,7},{7,6},{8,9},{9,8},{10,11... | collective-permute-start | bytes 589832 | tf_op jit(solution)/shard_map/ppermute | solution.py:362
  62.8 6.8 %collective-permute-start.20 = (bf16[192,256]{1,0:T(8,128)(2,1)S(1)}, bf16[192,256]{1,0:T(8,128)(2,1)S(1)}, u32[]{:S(2)}, u32[]{:S(2)}) collective-permute-start(bf16[192,256]{1,0:T(8,128)(2,1)S(1)} %get-tuple-element.91), channel_id=1, source_target_pairs={{0,2},{1,3},{2,0},{3,1},{4,6},{5,7},{6,4},{7,5},{8,10},{9,11},{10,... | collective-permute-start | bytes 294920 | tf_op jit(solution)/shard_map/ppermute | solution.py:362
  63.4 9.3 %collective-permute-start.30 = (bf16[192,256]{1,0:T(8,128)(2,1)S(1)}, bf16[192,256]{1,0:T(8,128)(2,1)S(1)}, u32[]{:S(2)}, u32[]{:S(2)}) collective-permute-start(bf16[192,256]{1,0:T(8,128)(2,1)S(1)} %fusion.4), channel_id=1, source_target_pairs={{0,2},{1,3},{2,0},{3,1},{4,6},{5,7},{6,4},{7,5},{8,10},{9,11},{10,... | collective-permute-start | bytes 294920 | tf_op jit(solution)/shard_map/ppermute | solution.py:362
  65.0 11.3 %collective-permute-start.23 = (bf16[192,256]{1,0:T(8,128)(2,1)S(1)}, bf16[192,256]{1,0:T(8,128)(2,1)S(1)}, u32[]{:S(2)}, u32[]{:S(2)}) collective-permute-start(bf16[192,256]{1,0:T(8,128)(2,1)S(1)} %get-tuple-element.89), channel_id=1, source_target_pairs={{0,6},{1,7},{2,4},{3,5},{4,2},{5,3},{6,0},{7,1},{8,14},{9,15},{10,... | collective-permute-start | bytes 294920 | tf_op jit(solution)/shard_map/ppermute | solution.py:362
  65.0 11.3 %collective-permute-start.22 = (bf16[192,256]{1,0:T(8,128)(2,1)S(1)}, bf16[192,256]{1,0:T(8,128)(2,1)S(1)}, u32[]{:S(2)}, u32[]{:S(2)}) collective-permute-start(bf16[192,256]{1,0:T(8,128)(2,1)S(1)} %get-tuple-element.90), channel_id=1, source_target_pairs={{0,4},{1,5},{2,6},{3,7},{4,0},{5,1},{6,2},{7,3},{8,12},{9,13},{10,... | collective-permute-start | bytes 294920 | tf_op jit(solution)/shard_map/ppermute | solution.py:362
  69.6 8.4 %collective-permute-start.24 = (bf16[192,256]{1,0:T(8,128)(2,1)S(1)}, bf16[192,256]{1,0:T(8,128)(2,1)S(1)}, u32[]{:S(2)}, u32[]{:S(2)}) collective-permute-start(bf16[192,256]{1,0:T(8,128)(2,1)S(1)} %fusion.3), channel_id=1, source_target_pairs={{0,8},{1,9},{2,10},{3,11},{4,12},{5,13},{6,14},{7,15},{8,0},{9,1},... | collective-permute-start | bytes 294920 | tf_op jit(solution)/shard_map/ppermute | solution.py:362
  71.4 4.6 %collective-permute-start.21 = (bf16[192,256]{1,0:T(8,128)(2,1)S(1)}, bf16[192,256]{1,0:T(8,128)(2,1)S(1)}, u32[]{:S(2)}, u32[]{:S(2)}) collective-permute-start(bf16[192,256]{1,0:T(8,128)(2,1)S(1)} %get-tuple-element.76), channel_id=1, source_target_pairs={{0,2},{1,3},{2,0},{3,1},{4,6},{5,7},{6,4},{7,5},{8,10},{9,11},{10,... | collective-permute-start | bytes 294920 | tf_op jit(solution)/shard_map/ppermute | solution.py:362
  72.7 6.6 %collective-permute-start.31 = (bf16[192,256]{1,0:T(8,128)(2,1)S(1)}, bf16[192,256]{1,0:T(8,128)(2,1)S(1)}, u32[]{:S(2)}, u32[]{:S(2)}) collective-permute-start(bf16[192,256]{1,0:T(8,128)(2,1)S(1)} %fusion.1), channel_id=1, source_target_pairs={{0,12},{1,13},{2,14},{3,15},{4,8},{5,9},{6,10},{7,11},{8,4},{9,5},... | collective-permute-start | bytes 294920 | tf_op jit(solution)/shard_map/ppermute | solution.py:362

commit v11 on v10

--- a/solution.py
+++ b/solution.py
@@ -343,7 +343,6 @@
     groups = lax.axis_size("expert")
     slices = lax.axis_size("mp")
     here, column = lax.axis_index("expert"), lax.axis_index("mp")
-    owner_rows = jnp.broadcast_to(source_owner[:, None], (8, 128))
     width = features // slices
     experts = expand_weight.shape[0] * groups
     capacity = max(2, 3 * token_count // experts)
@@ -370,7 +369,7 @@
 
     steps = range(groups) if direct else [0]
 
-    queries, source = ask(after(tokens, owner_rows), query_weight, encoder_states[0])
+    queries, source = ask(tokens, query_weight, encoder_states[0])
     expert_bits = bits_of(groups)
     bits = bits_of(slices)
     if direct:
@@ -384,7 +383,7 @@
         for k in sorted(range(1, groups), key=lambda k: (k & (k - 1) != 0, -k)):
             answer = previous = attend(after(asked[k], previous), source, token_count)
             backs[k] = hop(answer, k, 0)
-        context = pick(owner_rows, [own] + [backs[k] for k in range(1, groups)])
+        context = pick(source_owner.reshape(1, 1), [own] + [backs[k] for k in range(1, groups)])
     else:
         asked = lax.all_gather(queries, "expert", axis=0, tiled=True)
         previous = attend(asked, source, token_count)
@@ -413,10 +412,11 @@
     def sum_cores(keep, give):
         return keep + hop(give, 0, 1).astype(F32)
 
-    def sum_slices(summed):
+    def sum_slices(summed, wait):
         total = summed[0]
         for j in range(1, pairs):
-            total += hop(summed[j].astype(BF16), 0, 2 * j).astype(F32)
+            part = summed[j].astype(BF16)
+            total += hop(part if wait is None else after(part, wait), 0, 2 * j).astype(F32)
         return total.astype(BF16)
 
     def send_home(k, summed, wait=None):
@@ -434,6 +434,7 @@
         own_sum, wait = sum_cores(keep, give), None
         earlier = own_sum
         turns = [[k for k in sends if k < groups - 1], [groups - 1]] if groups > 2 else [sends]
+        give, relay = None, None
         for turn in turns:
             blocks, orders = [], []
             for k in turn:
@@ -441,6 +442,8 @@
                 for bit in bits if k in far else [1]:
                     pieces = pieces + [hop(piece, 0, bit) for piece in pieces]
                     places = places + [index ^ bit for index in places]
+                    if bit > 1:
+                        relay = pieces[-1]
                 blocks.append(pieces)
                 orders.append(places)
             if turn:
@@ -451,13 +454,14 @@
                 for i, k in enumerate(turn):
                     rows = summed[:, i * slots : (i + 1) * slots]
                     if k in far:
-                        total = sum_slices(rows)
-                        wait = total if wait is None else wait
-                        home[k] = [hop(total, k, 0)]
+                        wait = sum_slices(rows, wait)
+                        home[k] = [hop(wait, k, 0)]
                     else:
-                        home[k] = send_home(k, rows)
+                        near = k, rows
+        if sends and 1 not in far:
+            home[near[0]] = send_home(*near, wait)
         home[0] = send_home(0, own_sum, wait)
-        order = [0] + sorted(sends)
+        order = sorted(sends, key=lambda k: (k == 1, k)) + [0]
     else:
         mine = spread(leaving[0])
         home[0] = send_home(0, sum_cores(*expert([[0, 1]], [[mine, hop(mine, 0, 1)]])))

time: 80.3 us -> 82.2 us (1.024)
  waiting for transfers between devices: 31.9 us -> 34.7 us
  starting transfers between devices: 34 us -> 33.1 us
    ppermute x32, waiting for transfers between devices: 31.9 us -> 34.7 us  [hop(): return lax.ppermute(value, ('expert', 'mp'), moves)]
    ppermute x32, starting transfers between devices: 34 us -> 33.1 us  [hop(): return lax.ppermute(value, ('expert', 'mp'), moves)]
  transfers between devices with their start and end apart: 32 -> 32, of which waited for: 15 -> 16; matrix products, arithmetic and copies ran while one was open for 0% -> 0% of each run, Pallas kernels for 14% -> 12%
where the time goes in v11:
time: 82.2 us; the launch traced here: 82.1 us
  waiting for transfers between devices  34.7 us (42%)
  starting transfers between devices  33.1 us (40%)
  Pallas kernels  13 us (16%)
  between operations  0.98 us (1%)
    ppermute x32, waiting for transfers between devices, hop(): return lax.ppermute(value, ('expert', 'mp'), moves)  34.7 us
    ppermute x32, starting transfers between devices, hop(): return lax.ppermute(value, ('expert', 'mp'), moves)  33.1 us
    pallas_call x3, Pallas kernels, run_expert(): pl.pallas_call(functools.partial(expert_kernel, tuple(map(tuple, orders))...  3.88 us
    pallas_call x4, Pallas kernels, attend(): pl.pallas_call(attend_kernel, in_specs=[WHOLE] * 2, out_specs=WHOLE, out_...  3.09 us
    pallas_call x1, Pallas kernels, ask(): pl.pallas_call(query_kernel, in_specs=[pl.BlockSpec(memory_space=pltpu.HB...  1.81 us
  transfers between devices with their start and end apart: 32, of which 16 were waited for; matrix products, arithmetic and copies ran while one was open for 0% of the time, Pallas kernels for 12%

profile of v11, /device:TPU:0, one launch (start us, length us, event | category | flops | bytes accessed | tf_op | source)
XLA Modules:
  0.0 82.1 jit_solution(8628842098282396891)
XLA Ops:
  0.0 2.9 %collective-permute-start.9 = (bf16[256,1024]{1,0:T(8,128)(2,1)}, bf16[256,1024]{1,0:T(8,128)(2,1)S(1)}, u32[]{:S(2)}, u32[]{:S(2)}) collective-permute-start(bf16[256,1024]{1,0:T(8,128)(2,1)} %refs_5_), channel_id=1, source_target_pairs={{0,2},{1,3},{2,0},{3,1},{4,6},{5,7},{6,4},{7,5},{8,10},{9,11},{10,... | collective-permute-start | bytes 1572872 | tf_op jit(solution)/shard_map/ppermute | solution.py:361
  2.9 1.8 %query.1 = (bf16[256,256]{1,0:T(8,128)(2,1)S(1)}, bf16[2,512,256]{2,1,0:T(8,128)(2,1)S(1)}) custom-call(bf16[256,1024]{1,0:T(8,128)(2,1)} %refs_0_.1, bf16[1024,256]{1,0:T(8,128)(2,1)} %weight.1, bf16[2,512,256]{2,1,0:T(8,128)(2,1)} %bitcast.39), custom_call_target="tpu_custom_call" | custom-call | tf_op jit(solution)/shard_map/query/pallas_call | solution.py:63
  4.8 0.0 copy-start.3
  4.8 0.0 copy-start.5
  4.8 0.0 copy-start.2
  4.8 2.6 %collective-permute-start.1 = (bf16[256,256]{1,0:T(8,128)(2,1)S(1)}, bf16[256,256]{1,0:T(8,128)(2,1)S(1)}, u32[]{:S(2)}, u32[]{:S(2)}) collective-permute-start(bf16[256,256]{1,0:T(8,128)(2,1)S(1)} %get-tuple-element.47.queries), channel_id=1, source_target_pairs={{0,8},{1,9},{2,10},{3,11},{4,12},{5,13},{6,14},{7,15},{8,0},{9,1},... | collective-permute-start | bytes 393224 | tf_op jit(solution)/shard_map/ppermute | solution.py:361
  7.4 1.6 %collective-permute-start = (bf16[256,256]{1,0:T(8,128)(2,1)S(1)}, bf16[256,256]{1,0:T(8,128)(2,1)S(1)}, u32[]{:S(2)}, u32[]{:S(2)}) collective-permute-start(bf16[256,256]{1,0:T(8,128)(2,1)S(1)} %get-tuple-element.47.queries), channel_id=1, source_target_pairs={{0,4},{1,5},{2,6},{3,7},{4,0},{5,1},{6,2},{7,3},{8,12},{9,13},{10,... | collective-permute-start | bytes 393224 | tf_op jit(solution)/shard_map/ppermute | solution.py:361
  9.0 0.8 attend.4.refs_0_
  9.8 3.8 %collective-permute-done.1.queries = bf16[256,256]{1,0:T(8,128)(2,1)S(1)} collective-permute-done((bf16[256,256]{1,0:T(8,128)(2,1)S(1)}, bf16[256,256]{1,0:T(8,128)(2,1)S(1)}, u32[]{:S(2)}, u32[]{:S(2)}) %collective-permute-start.1) | collective-permute-done | bytes 131104 | tf_op jit(solution)/shard_map/ppermute | solution.py:361
  13.6 0.6 collective-permute-start.4
  14.2 0.8 attend.5
  15.0 3.4 %collective-permute-start.3 = (bf16[256,256]{1,0:T(8,128)(2,1)S(1)}, bf16[256,256]{1,0:T(8,128)(2,1)S(1)}, u32[]{:S(2)}, u32[]{:S(2)}) collective-permute-start(bf16[256,256]{1,0:T(8,128)(2,1)S(1)} %attend.5), channel_id=1, source_target_pairs={{0,8},{1,9},{2,10},{3,11},{4,12},{5,13},{6,14},{7,15},{8,0},{9,1},... | collective-permute-start | bytes 393224 | tf_op jit(solution)/shard_map/ppermute | solution.py:361
  18.4 0.8 attend.6
  19.2 0.1 collective-permute-start.2
  19.3 0.8 attend.7
  20.1 0.0 copy-start.4
  20.1 5.7 %collective-permute-start.5 = (bf16[256,256]{1,0:T(8,128)(2,1)S(1)}, bf16[256,256]{1,0:T(8,128)(2,1)S(1)}, u32[]{:S(2)}, u32[]{:S(2)}) collective-permute-start(bf16[256,256]{1,0:T(8,128)(2,1)S(1)} %attend.7), channel_id=1, source_target_pairs={{0,12},{1,13},{2,14},{3,15},{4,8},{5,9},{6,10},{7,11},{8,4},{9,5},... | collective-permute-start | bytes 393224 | tf_op jit(solution)/shard_map/ppermute | solution.py:361
  26.4 2.8 %collective-permute-done.5.refs_3_ = bf16[256,256]{1,0:T(8,128)(2,1)S(1)} collective-permute-done((bf16[256,256]{1,0:T(8,128)(2,1)S(1)}, bf16[256,256]{1,0:T(8,128)(2,1)S(1)}, u32[]{:S(2)}, u32[]{:S(2)}) %collective-permute-start.5) | collective-permute-done | bytes 131104 | tf_op jit(solution)/shard_map/ppermute | solution.py:361
  29.3 0.1 pick.1.refs_1_
  29.4 0.1 collective-permute-start.10
  29.5 0.5 collective-permute-start.11
  30.0 0.5 collective-permute-start.6
  30.5 1.0 %route.1 = (s32[256,2]{1,0:T(8,128)S(1)}, bf16[192,256]{1,0:T(8,128)(2,1)S(1)}, bf16[192,256]{1,0:T(8,128)(2,1)S(1)}, bf16[192,256]{1,0:T(8,128)(2,1)S(1)}, bf16...) custom-call(s32[2,256]{1,0:T(2,128)S(1)} %bitcast.38), custom_call_target="tpu_custom_call" | custom-call | tf_op jit(solution)/shard_map/route/pallas_call | solution.py:175
  31.5 0.1 collective-permute-start.7
  31.6 3.9 %collective-permute-done.6.refs_2_ = bf16[256,256]{1,0:T(8,128)(2,1)S(1)} collective-permute-done((bf16[256,256]{1,0:T(8,128)(2,1)S(1)}, bf16[256,256]{1,0:T(8,128)(2,1)S(1)}, u32[]{:S(2)}, u32[]{:S(2)}) %collective-permute-start.6) | collective-permute-done | bytes 131104 | tf_op jit(solution)/shard_map/ppermute | solution.py:361
  35.5 1.3 %collective-permute-done.8.refs_4_ = bf16[256,256]{1,0:T(8,128)(2,1)S(1)} collective-permute-done((bf16[256,256]{1,0:T(8,128)(2,1)S(1)}, bf16[256,256]{1,0:T(8,128)(2,1)S(1)}, u32[]{:S(2)}, u32[]{:S(2)}) %collective-permute-start.8) | collective-permute-done | bytes 131104 | tf_op jit(solution)/shard_map/ppermute | solution.py:361
  36.9 0.0 copy-start
  36.9 1.0 %state.1 = (bf16[256,1024]{1,0:T(8,128)(2,1)S(1)}, bf16[192,256]{1,0:T(8,128)(2,1)S(1)}, bf16[192,256]{1,0:T(8,128)(2,1)S(1)}, bf16[192,512]{1,0:T(8,128)(2,1)S(1)}) custom-call(bf16[256,1024]{1,0:T(8,128)(2,1)S(1)} %copy-done.2, bf16[256,256]{1,0:T(8,128)(2,1)S(1)} %pick.1.refs_1_, bf16[256,256]{1,0:T(8,128)(2,1)S(1)} %collective-permute-done.6.refs_2_, ...), custom_call_target="tpu_custom_call" | custom-call | tf_op jit(solution)/shard_map/state/pallas_call | solution.py:208
  37.9 2.6 %collective-permute-start.12 = (bf16[192,256]{1,0:T(8,128)(2,1)S(1)}, bf16[192,256]{1,0:T(8,128)(2,1)S(1)}, u32[]{:S(2)}, u32[]{:S(2)}) collective-permute-start(bf16[192,256]{1,0:T(8,128)(2,1)S(1)} %get-tuple-element.66), channel_id=1, source_target_pairs={{0,8},{1,9},{2,10},{3,11},{4,12},{5,13},{6,14},{7,15},{8,0},{9,1},... | collective-permute-start | bytes 294920 | tf_op jit(solution)/shard_map/ppermute | solution.py:361
  40.4 1.4 %collective-permute-start.22 = (bf16[192,256]{1,0:T(8,128)(2,1)S(1)}, bf16[192,256]{1,0:T(8,128)(2,1)S(1)}, u32[]{:S(2)}, u32[]{:S(2)}) collective-permute-start(bf16[192,256]{1,0:T(8,128)(2,1)S(1)} %get-tuple-element.78), channel_id=1, source_target_pairs={{0,12},{1,13},{2,14},{3,15},{4,8},{5,9},{6,10},{7,11},{8,4},{9,5},... | collective-permute-start | bytes 294920 | tf_op jit(solution)/shard_map/ppermute | solution.py:361
  41.8 0.0 collective-permute-start.17
  41.9 0.5 home.1
  42.4 1.0 %expert.3 = (f32[2,192,256]{2,1,0:T(8,128)S(1)}, bf16[2,192,256]{2,1,0:T(8,128)(2,1)S(1)}) custom-call(bf16[192,512]{1,0:T(8,128)(2,1)S(1)} %get-tuple-element.67.refs_0_, bf16[192,512]{1,0:T(8,128)(2,1)S(1)} %get-tuple-element.68.refs_1_, bf16[1024,1024]{1,0:T(8,128)(2,1)S(1)} %bitcast.31, bf16[1024,1024]{1,0:T(8,128)(2,1)S(1)} %bitcast.34), custom_call_target="tpu_custom_call" | custom-call | tf_op jit(solution)/shard_map/expert/pallas_call | solution.py:287
  43.4 5.3 %collective-permute-done.12.refs_0_ = bf16[192,256]{1,0:T(8,128)(2,1)S(1)} collective-permute-done((bf16[192,256]{1,0:T(8,128)(2,1)S(1)}, bf16[192,256]{1,0:T(8,128)(2,1)S(1)}, u32[]{:S(2)}, u32[]{:S(2)}) %collective-permute-start.12) | collective-permute-done | bytes 98336 | tf_op jit(solution)/shard_map/ppermute | solution.py:361
  48.7 0.5 collective-permute-start.14
  49.3 1.5 %collective-permute-start.23 = (bf16[192,256]{1,0:T(8,128)(2,1)S(1)}, bf16[192,256]{1,0:T(8,128)(2,1)S(1)}, u32[]{:S(2)}, u32[]{:S(2)}) collective-permute-start(bf16[192,256]{1,0:T(8,128)(2,1)S(1)} %collective-permute-done.22.refs_0_), channel_id=1, source_target_pairs={{0,2},{1,3},{2,0},{3,1},{4,6},{5,7},{6,4},{7,5},{8,10},{9,11},{10,... | collective-permute-start | bytes 294920 | tf_op jit(solution)/shard_map/ppermute | solution.py:361
  50.8 0.6 collective-permute-done.17.refs_4_
  51.4 3.0 %collective-permute-done.14.refs_1_ = bf16[192,256]{1,0:T(8,128)(2,1)S(1)} collective-permute-done((bf16[192,256]{1,0:T(8,128)(2,1)S(1)}, bf16[192,256]{1,0:T(8,128)(2,1)S(1)}, u32[]{:S(2)}, u32[]{:S(2)}) %collective-permute-start.14) | collective-permute-done | bytes 98336 | tf_op jit(solution)/shard_map/ppermute | solution.py:361
  54.3 1.7 %collective-permute-done.23.refs_1_ = bf16[192,256]{1,0:T(8,128)(2,1)S(1)} collective-permute-done((bf16[192,256]{1,0:T(8,128)(2,1)S(1)}, bf16[192,256]{1,0:T(8,128)(2,1)S(1)}, u32[]{:S(2)}, u32[]{:S(2)}) %collective-permute-start.23) | collective-permute-done | bytes 98336 | tf_op jit(solution)/shard_map/ppermute | solution.py:361
  56.1 0.5 collective-permute-start.25
  56.6 0.1 convert_add_fusion.2
  56.6 0.7 collective-permute-done.16.refs_3_
  57.4 1.9 %expert.4 = (f32[2,384,256]{2,1,0:T(8,128)S(1)}, bf16[2,384,256]{2,1,0:T(8,128)(2,1)S(1)}) custom-call(bf16[192,256]{1,0:T(8,128)(2,1)S(1)} %collective-permute-done.12.refs_0_, bf16[192,256]{1,0:T(8,128)(2,1)S(1)} %collective-permute-done.14.refs_1_, bf16[192,256]{1,0:T(8,128)(2,1)S(1)} %collective-permute-done.15.refs_2_, ...), custom_call_target="tpu_custom_call" | custom-call | tf_op jit(solution)/shard_map/expert/pallas_call | solution.py:287
  59.2 1.0 %expert.5 = (f32[2,192,256]{2,1,0:T(8,128)S(1)}, bf16[2,192,256]{2,1,0:T(8,128)(2,1)S(1)}) custom-call(bf16[192,256]{1,0:T(8,128)(2,1)S(1)} %collective-permute-done.22.refs_0_, bf16[192,256]{1,0:T(8,128)(2,1)S(1)} %collective-permute-done.23.refs_1_, bf16[192,256]{1,0:T(8,128)(2,1)S(1)} %collective-permute-done.24.refs_2_, ...), custom_call_target="tpu_custom_call" | custom-call | tf_op jit(solution)/shard_map/expert/pallas_call | solution.py:287
  60.3 0.2 collective-permute-start.26
  60.5 0.4 collective-permute-start.19
  60.8 0.9 %collective-permute-done.26 = bf16[2,192,256]{2,1,0:T(8,128)(2,1)S(1)} collective-permute-done((bf16[2,192,256]{2,1,0:T(8,128)(2,1)S(1)}, bf16[2,192,256]{2,1,0:T(8,128)(2,1)S(1)}, u32[]{:S(2)}, u32[]{:S(2)}) %collective-permute-start.26) | collective-permute-done | bytes 196640 | tf_op jit(solution)/shard_map/ppermute | solution.py:361
  61.8 0.5 collective-permute-done.19
  62.3 0.1 fusion.5
  62.5 0.6 collective-permute-start.20
  63.1 4.4 %collective-permute-done.20 = bf16[192,256]{1,0:T(8,128)(2,1)S(1)} collective-permute-done((bf16[192,256]{1,0:T(8,128)(2,1)S(1)}, bf16[192,256]{1,0:T(8,128)(2,1)S(1)}, u32[]{:S(2)}, u32[]{:S(2)}) %collective-permute-start.20) | collective-permute-done | bytes 98336 | tf_op jit(solution)/shard_map/ppermute | solution.py:361
  67.5 0.6 collective-permute-start.27
  68.2 0.1 collective-permute-start.29
  68.2 3.3 %collective-permute-start.21 = (bf16[192,256]{1,0:T(8,128)(2,1)S(1)}, bf16[192,256]{1,0:T(8,128)(2,1)S(1)}, u32[]{:S(2)}, u32[]{:S(2)}) collective-permute-start(bf16[192,256]{1,0:T(8,128)(2,1)S(1)} %fusion.3), channel_id=1, source_target_pairs={{0,8},{1,9},{2,10},{3,11},{4,12},{5,13},{6,14},{7,15},{8,0},{9,1},... | collective-permute-start | bytes 294920 | tf_op jit(solution)/shard_map/ppermute | solution.py:361
  71.5 0.7 collective-permute-done.27
  72.2 2.7 %collective-permute-start.28 = (bf16[192,256]{1,0:T(8,128)(2,1)S(1)}, bf16[192,256]{1,0:T(8,128)(2,1)S(1)}, u32[]{:S(2)}, u32[]{:S(2)}) collective-permute-start(bf16[192,256]{1,0:T(8,128)(2,1)S(1)} %fusion.1), channel_id=1, source_target_pairs={{0,12},{1,13},{2,14},{3,15},{4,8},{5,9},{6,10},{7,11},{8,4},{9,5},... | collective-permute-start | bytes 294920 | tf_op jit(solution)/shard_map/ppermute | solution.py:361
  75.0 0.6 collective-permute-start.31
  75.5 2.0 %collective-permute-done.21.refs_0_ = bf16[192,256]{1,0:T(8,128)(2,1)S(1)} collective-permute-done((bf16[192,256]{1,0:T(8,128)(2,1)S(1)}, bf16[192,256]{1,0:T(8,128)(2,1)S(1)}, u32[]{:S(2)}, u32[]{:S(2)}) %collective-permute-start.21) | collective-permute-done | bytes 98336 | tf_op jit(solution)/shard_map/ppermute | solution.py:361
  77.5 0.2 combine.4.base
  77.7 1.1 %collective-permute-done.28.refs_0_ = bf16[192,256]{1,0:T(8,128)(2,1)S(1)} collective-permute-done((bf16[192,256]{1,0:T(8,128)(2,1)S(1)}, bf16[192,256]{1,0:T(8,128)(2,1)S(1)}, u32[]{:S(2)}, u32[]{:S(2)}) %collective-permute-start.28) | collective-permute-done | bytes 98336 | tf_op jit(solution)/shard_map/ppermute | solution.py:361
  78.8 0.2 combine.5.base
  79.1 1.9 %collective-permute-done.30.refs_1_ = bf16[192,256]{1,0:T(8,128)(2,1)S(1)} collective-permute-done((bf16[192,256]{1,0:T(8,128)(2,1)S(1)}, bf16[192,256]{1,0:T(8,128)(2,1)S(1)}, u32[]{:S(2)}, u32[]{:S(2)}) %collective-permute-start.30) | collective-permute-done | bytes 98336 | tf_op jit(solution)/shard_map/ppermute | solution.py:361
  80.9 0.2 combine.6.base
  81.2 0.9 %combine.7 = bf16[256,256]{1,0:T(8,128)(2,1)} custom-call(f32[256,2]{1,0:T(8,128)S(1)} %get-tuple-element.62.gates, f32[256,256]{1,0:T(8,128)S(1)} %combine.6.base, bf16[256,192]{1,0:T(8,128)(2,1)S(1)} %get-tuple-element.86.first, bf16[256,192]{1,0:T(8,128)(2,1)S(1)} %get-tuple-element.87.second, bf16[192,256]{1,0:T(8,128)(2,1)S(1)} %get-tuple-element.95.refs_0_, ...), custom_call_target="tpu_custom_call" | custom-call | tf_op jit(solution)/shard_map/combine/pallas_call | solution.py:313
  (36 shorter events, 0.2 us)
Async XLA Ops:
  0.0 29.5 %collective-permute-start.9 = (bf16[256,1024]{1,0:T(8,128)(2,1)}, bf16[256,1024]{1,0:T(8,128)(2,1)S(1)}, u32[]{:S(2)}, u32[]{:S(2)}) collective-permute-start(bf16[256,1024]{1,0:T(8,128)(2,1)} %refs_5_), channel_id=1, source_target_pairs={{0,2},{1,3},{2,0},{3,1},{4,6},{5,7},{6,4},{7,5},{8,10},{9,11},{10,... | collective-permute-start | bytes 1572872 | tf_op jit(solution)/shard_map/ppermute | solution.py:361
  4.8 24.7 %copy-start.3 = (bf16[256,1024]{1,0:T(8,128)(2,1)S(1)}, bf16[256,1024]{1,0:T(8,128)(2,1)}, u32[]{:S(2)}) copy-start(bf16[256,1024]{1,0:T(8,128)(2,1)} %refs_5_) | copy-start | bytes 1572868
  4.8 25.8 %copy-start.5 = (s32[256,2]{0,1:T(2,128)S(1)}, s32[256,2]{0,1:T(2,128)}, u32[]{:S(2)}) copy-start(s32[256,2]{0,1:T(2,128)} %param.15) | copy-start | bytes 6148
  4.8 32.1 %copy-start.2 = (bf16[256,1024]{1,0:T(8,128)(2,1)S(1)}, bf16[256,1024]{1,0:T(8,128)(2,1)}, u32[]{:S(2)}) copy-start(bf16[256,1024]{1,0:T(8,128)(2,1)} %refs_0_.1) | copy-start | bytes 1572868
  4.8 8.8 %collective-permute-start.1 = (bf16[256,256]{1,0:T(8,128)(2,1)S(1)}, bf16[256,256]{1,0:T(8,128)(2,1)S(1)}, u32[]{:S(2)}, u32[]{:S(2)}) collective-permute-start(bf16[256,256]{1,0:T(8,128)(2,1)S(1)} %get-tuple-element.47.queries), channel_id=1, source_target_pairs={{0,8},{1,9},{2,10},{3,11},{4,12},{5,13},{6,14},{7,15},{8,0},{9,1},... | collective-permute-start | bytes 393224 | tf_op jit(solution)/shard_map/ppermute | solution.py:361
  7.4 11.0 %collective-permute-start = (bf16[256,256]{1,0:T(8,128)(2,1)S(1)}, bf16[256,256]{1,0:T(8,128)(2,1)S(1)}, u32[]{:S(2)}, u32[]{:S(2)}) collective-permute-start(bf16[256,256]{1,0:T(8,128)(2,1)S(1)} %get-tuple-element.47.queries), channel_id=1, source_target_pairs={{0,4},{1,5},{2,6},{3,7},{4,0},{5,1},{6,2},{7,3},{8,12},{9,13},{10,... | collective-permute-start | bytes 393224 | tf_op jit(solution)/shard_map/ppermute | solution.py:361
  13.6 5.7 %collective-permute-start.4 = (bf16[256,256]{1,0:T(8,128)(2,1)S(1)}, bf16[256,256]{1,0:T(8,128)(2,1)S(1)}, u32[]{:S(2)}, u32[]{:S(2)}) collective-permute-start(bf16[256,256]{1,0:T(8,128)(2,1)S(1)} %collective-permute-done.1.queries), channel_id=1, source_target_pairs={{0,4},{1,5},{2,6},{3,7},{4,0},{5,1},{6,2},{7,3},{8,12},{9,13},{10,... | collective-permute-start | bytes 393224 | tf_op jit(solution)/shard_map/ppermute | solution.py:361
  15.0 11.4 %collective-permute-start.3 = (bf16[256,256]{1,0:T(8,128)(2,1)S(1)}, bf16[256,256]{1,0:T(8,128)(2,1)S(1)}, u32[]{:S(2)}, u32[]{:S(2)}) collective-permute-start(bf16[256,256]{1,0:T(8,128)(2,1)S(1)} %attend.5), channel_id=1, source_target_pairs={{0,8},{1,9},{2,10},{3,11},{4,12},{5,13},{6,14},{7,15},{8,0},{9,1},... | collective-permute-start | bytes 393224 | tf_op jit(solution)/shard_map/ppermute | solution.py:361
  19.2 7.2 %collective-permute-start.2 = (bf16[256,256]{1,0:T(8,128)(2,1)S(1)}, bf16[256,256]{1,0:T(8,128)(2,1)S(1)}, u32[]{:S(2)}, u32[]{:S(2)}) collective-permute-start(bf16[256,256]{1,0:T(8,128)(2,1)S(1)} %attend.6), channel_id=1, source_target_pairs={{0,4},{1,5},{2,6},{3,7},{4,0},{5,1},{6,2},{7,3},{8,12},{9,13},{10,... | collective-permute-start | bytes 393224 | tf_op jit(solution)/shard_map/ppermute | solution.py:361
  20.1 21.8 %copy-start.4 = (bf16[1024,4]{0,1:T(4,128)(2,1)S(1)}, bf16[1024,4]{0,1:T(4,128)(2,1)}, u32[]{:S(2)}) copy-start(bf16[1024,4]{0,1:T(4,128)(2,1)} %param.14) | copy-start | bytes 24580
  20.1 9.2 %collective-permute-start.5 = (bf16[256,256]{1,0:T(8,128)(2,1)S(1)}, bf16[256,256]{1,0:T(8,128)(2,1)S(1)}, u32[]{:S(2)}, u32[]{:S(2)}) collective-permute-start(bf16[256,256]{1,0:T(8,128)(2,1)S(1)} %attend.7), channel_id=1, source_target_pairs={{0,12},{1,13},{2,14},{3,15},{4,8},{5,9},{6,10},{7,11},{8,4},{9,5},... | collective-permute-start | bytes 393224 | tf_op jit(solution)/shard_map/ppermute | solution.py:361
  29.4 7.4 %collective-permute-start.10 = (bf16[256,1024]{1,0:T(8,128)(2,1)S(1)}, bf16[256,1024]{1,0:T(8,128)(2,1)S(1)}, u32[]{:S(2)}, u32[]{:S(2)}) collective-permute-start(bf16[256,1024]{1,0:T(8,128)(2,1)S(1)} %copy-done.3), channel_id=1, source_target_pairs={{0,1},{1,0},{2,3},{3,2},{4,5},{5,4},{6,7},{7,6},{8,9},{9,8},{10,11... | collective-permute-start | bytes 1572872 | tf_op jit(solution)/shard_map/ppermute | solution.py:361
  29.5 7.3 %collective-permute-start.11 = (bf16[256,1024]{1,0:T(8,128)(2,1)S(1)}, bf16[256,1024]{1,0:T(8,128)(2,1)S(1)}, u32[]{:S(2)}, u32[]{:S(2)}) collective-permute-start(bf16[256,1024]{1,0:T(8,128)(2,1)S(1)} %collective-permute-done.9.refs_6_), channel_id=1, source_target_pairs={{0,1},{1,0},{2,3},{3,2},{4,5},{5,4},{6,7},{7,6},{8,9},{9,8},{10,11... | collective-permute-start | bytes 1572872 | tf_op jit(solution)/shard_map/ppermute | solution.py:361
  30.0 5.5 %collective-permute-start.6 = (bf16[256,256]{1,0:T(8,128)(2,1)S(1)}, bf16[256,256]{1,0:T(8,128)(2,1)S(1)}, u32[]{:S(2)}, u32[]{:S(2)}) collective-permute-start(bf16[256,256]{1,0:T(8,128)(2,1)S(1)} %pick.1.refs_1_), channel_id=1, source_target_pairs={{0,2},{1,3},{2,0},{3,1},{4,6},{5,7},{6,4},{7,5},{8,10},{9,11},{10,... | collective-permute-start | bytes 393224 | tf_op jit(solution)/shard_map/ppermute | solution.py:361
  31.5 4.0 %collective-permute-start.7 = (bf16[256,256]{1,0:T(8,128)(2,1)S(1)}, bf16[256,256]{1,0:T(8,128)(2,1)S(1)}, u32[]{:S(2)}, u32[]{:S(2)}) collective-permute-start(bf16[256,256]{1,0:T(8,128)(2,1)S(1)} %pick.1.refs_1_), channel_id=1, source_target_pairs={{0,1},{1,0},{2,3},{3,2},{4,5},{5,4},{6,7},{7,6},{8,9},{9,8},{10,11... | collective-permute-start | bytes 393224 | tf_op jit(solution)/shard_map/ppermute | solution.py:361
  35.5 1.3 %collective-permute-start.8 = (bf16[256,256]{1,0:T(8,128)(2,1)S(1)}, bf16[256,256]{1,0:T(8,128)(2,1)S(1)}, u32[]{:S(2)}, u32[]{:S(2)}) collective-permute-start(bf16[256,256]{1,0:T(8,128)(2,1)S(1)} %collective-permute-done.6.refs_2_), channel_id=1, source_target_pairs={{0,1},{1,0},{2,3},{3,2},{4,5},{5,4},{6,7},{7,6},{8,9},{9,8},{10,11... | collective-permute-start | bytes 393224 | tf_op jit(solution)/shard_map/ppermute | solution.py:361
  36.9 5.5 %copy-start = (bf16[1,1024,1024]{2,1,0:T(8,128)(2,1)S(1)}, bf16[1,1024,1024]{2,1,0:T(8,128)(2,1)}, u32[]{:S(2)}) copy-start(bf16[1,1024,1024]{2,1,0:T(8,128)(2,1)} %param.16) | copy-start | bytes 6291460
  36.9 5.5 %copy-start.1 = (bf16[1,1024,1024]{2,1,0:T(8,128)(2,1)S(1)}, bf16[1,1024,1024]{2,1,0:T(8,128)(2,1)}, u32[]{:S(2)}) copy-start(bf16[1,1024,1024]{2,1,0:T(8,128)(2,1)} %param.17) | copy-start | bytes 6291460
  37.9 10.9 %collective-permute-start.12 = (bf16[192,256]{1,0:T(8,128)(2,1)S(1)}, bf16[192,256]{1,0:T(8,128)(2,1)S(1)}, u32[]{:S(2)}, u32[]{:S(2)}) collective-permute-start(bf16[192,256]{1,0:T(8,128)(2,1)S(1)} %get-tuple-element.66), channel_id=1, source_target_pairs={{0,8},{1,9},{2,10},{3,11},{4,12},{5,13},{6,14},{7,15},{8,0},{9,1},... | collective-permute-start | bytes 294920 | tf_op jit(solution)/shard_map/ppermute | solution.py:361
  40.4 8.9 %collective-permute-start.22 = (bf16[192,256]{1,0:T(8,128)(2,1)S(1)}, bf16[192,256]{1,0:T(8,128)(2,1)S(1)}, u32[]{:S(2)}, u32[]{:S(2)}) collective-permute-start(bf16[192,256]{1,0:T(8,128)(2,1)S(1)} %get-tuple-element.78), channel_id=1, source_target_pairs={{0,12},{1,13},{2,14},{3,15},{4,8},{5,9},{6,10},{7,11},{8,4},{9,5},... | collective-permute-start | bytes 294920 | tf_op jit(solution)/shard_map/ppermute | solution.py:361
  41.8 9.5 %collective-permute-start.17 = (bf16[192,512]{1,0:T(8,128)(2,1)S(1)}, bf16[192,512]{1,0:T(8,128)(2,1)S(1)}, u32[]{:S(2)}, u32[]{:S(2)}) collective-permute-start(bf16[192,512]{1,0:T(8,128)(2,1)S(1)} %get-tuple-element.73), channel_id=1, source_target_pairs={{0,4},{1,5},{2,6},{3,7},{4,0},{5,1},{6,2},{7,3},{8,12},{9,13},{10,... | collective-permute-start | bytes 589832 | tf_op jit(solution)/shard_map/ppermute | solution.py:361
  48.7 7.3 %collective-permute-start.13 = (bf16[2,192,256]{2,1,0:T(8,128)(2,1)S(1)}, bf16[2,192,256]{2,1,0:T(8,128)(2,1)S(1)}, u32[]{:S(2)}, u32[]{:S(2)}) collective-permute-start(bf16[2,192,256]{2,1,0:T(8,128)(2,1)S(1)} %get-tuple-element.71), channel_id=1, source_target_pairs={{0,1},{1,0},{2,3},{3,2},{4,5},{5,4},{6,7},{7,6},{8,9},{9,8},{10,11... | collective-permute-start | bytes 589832 | tf_op jit(solution)/shard_map/ppermute | solution.py:361
  48.7 5.6 %collective-permute-start.14 = (bf16[192,256]{1,0:T(8,128)(2,1)S(1)}, bf16[192,256]{1,0:T(8,128)(2,1)S(1)}, u32[]{:S(2)}, u32[]{:S(2)}) collective-permute-start(bf16[192,256]{1,0:T(8,128)(2,1)S(1)} %collective-permute-done.12.refs_0_), channel_id=1, source_target_pairs={{0,2},{1,3},{2,0},{3,1},{4,6},{5,7},{6,4},{7,5},{8,10},{9,11},{10,... | collective-permute-start | bytes 294920 | tf_op jit(solution)/shard_map/ppermute | solution.py:361
  49.3 6.8 %collective-permute-start.23 = (bf16[192,256]{1,0:T(8,128)(2,1)S(1)}, bf16[192,256]{1,0:T(8,128)(2,1)S(1)}, u32[]{:S(2)}, u32[]{:S(2)}) collective-permute-start(bf16[192,256]{1,0:T(8,128)(2,1)S(1)} %collective-permute-done.22.refs_0_), channel_id=1, source_target_pairs={{0,2},{1,3},{2,0},{3,1},{4,6},{5,7},{6,4},{7,5},{8,10},{9,11},{10,... | collective-permute-start | bytes 294920 | tf_op jit(solution)/shard_map/ppermute | solution.py:361
  50.8 5.9 %collective-permute-start.15 = (bf16[192,256]{1,0:T(8,128)(2,1)S(1)}, bf16[192,256]{1,0:T(8,128)(2,1)S(1)}, u32[]{:S(2)}, u32[]{:S(2)}) collective-permute-start(bf16[192,256]{1,0:T(8,128)(2,1)S(1)} %collective-permute-done.12.refs_0_), channel_id=1, source_target_pairs={{0,1},{1,0},{2,3},{3,2},{4,5},{5,4},{6,7},{7,6},{8,9},{9,8},{10,11... | collective-permute-start | bytes 294920 | tf_op jit(solution)/shard_map/ppermute | solution.py:361
  51.4 7.9 %collective-permute-start.24 = (bf16[192,256]{1,0:T(8,128)(2,1)S(1)}, bf16[192,256]{1,0:T(8,128)(2,1)S(1)}, u32[]{:S(2)}, u32[]{:S(2)}) collective-permute-start(bf16[192,256]{1,0:T(8,128)(2,1)S(1)} %collective-permute-done.22.refs_0_), channel_id=1, source_target_pairs={{0,1},{1,0},{2,3},{3,2},{4,5},{5,4},{6,7},{7,6},{8,9},{9,8},{10,11... | collective-permute-start | bytes 294920 | tf_op jit(solution)/shard_map/ppermute | solution.py:361
  54.3 3.0 %collective-permute-start.18 = (bf16[192,512]{1,0:T(8,128)(2,1)S(1)}, bf16[192,512]{1,0:T(8,128)(2,1)S(1)}, u32[]{:S(2)}, u32[]{:S(2)}) collective-permute-start(bf16[192,512]{1,0:T(8,128)(2,1)S(1)} %collective-permute-done.17.refs_4_), channel_id=1, source_target_pairs={{0,1},{1,0},{2,3},{3,2},{4,5},{5,4},{6,7},{7,6},{8,9},{9,8},{10,11... | collective-permute-start | bytes 589832 | tf_op jit(solution)/shard_map/ppermute | solution.py:361
  56.0 1.3 %collective-permute-start.16 = (bf16[192,256]{1,0:T(8,128)(2,1)S(1)}, bf16[192,256]{1,0:T(8,128)(2,1)S(1)}, u32[]{:S(2)}, u32[]{:S(2)}) collective-permute-start(bf16[192,256]{1,0:T(8,128)(2,1)S(1)} %collective-permute-done.14.refs_1_), channel_id=1, source_target_pairs={{0,1},{1,0},{2,3},{3,2},{4,5},{5,4},{6,7},{7,6},{8,9},{9,8},{10,11... | collective-permute-start | bytes 294920 | tf_op jit(solution)/shard_map/ppermute | solution.py:361
  56.1 3.2 %collective-permute-start.25 = (bf16[192,256]{1,0:T(8,128)(2,1)S(1)}, bf16[192,256]{1,0:T(8,128)(2,1)S(1)}, u32[]{:S(2)}, u32[]{:S(2)}) collective-permute-start(bf16[192,256]{1,0:T(8,128)(2,1)S(1)} %collective-permute-done.23.refs_1_), channel_id=1, source_target_pairs={{0,1},{1,0},{2,3},{3,2},{4,5},{5,4},{6,7},{7,6},{8,9},{9,8},{10,11... | collective-permute-start | bytes 294920 | tf_op jit(solution)/shard_map/ppermute | solution.py:361
  60.3 1.5 %collective-permute-start.26 = (bf16[2,192,256]{2,1,0:T(8,128)(2,1)S(1)}, bf16[2,192,256]{2,1,0:T(8,128)(2,1)S(1)}, u32[]{:S(2)}, u32[]{:S(2)}) collective-permute-start(bf16[2,192,256]{2,1,0:T(8,128)(2,1)S(1)} %get-tuple-element.81), channel_id=1, source_target_pairs={{0,1},{1,0},{2,3},{3,2},{4,5},{5,4},{6,7},{7,6},{8,9},{9,8},{10,11... | collective-permute-start | bytes 589832 | tf_op jit(solution)/shard_map/ppermute | solution.py:361
  60.5 1.9 %collective-permute-start.19 = (bf16[2,384,256]{2,1,0:T(8,128)(2,1)S(1)}, bf16[2,384,256]{2,1,0:T(8,128)(2,1)S(1)}, u32[]{:S(2)}, u32[]{:S(2)}) collective-permute-start(bf16[2,384,256]{2,1,0:T(8,128)(2,1)S(1)} %get-tuple-element.75), channel_id=1, source_target_pairs={{0,1},{1,0},{2,3},{3,2},{4,5},{5,4},{6,7},{7,6},{8,9},{9,8},{10,11... | collective-permute-start | bytes 1179656 | tf_op jit(solution)/shard_map/ppermute | solution.py:361
  62.5 5.0 %collective-permute-start.20 = (bf16[192,256]{1,0:T(8,128)(2,1)S(1)}, bf16[192,256]{1,0:T(8,128)(2,1)S(1)}, u32[]{:S(2)}, u32[]{:S(2)}) collective-permute-start(bf16[192,256]{1,0:T(8,128)(2,1)S(1)} %get-tuple-element.93), channel_id=1, source_target_pairs={{0,2},{1,3},{2,0},{3,1},{4,6},{5,7},{6,4},{7,5},{8,10},{9,11},{10,... | collective-permute-start | bytes 294920 | tf_op jit(solution)/shard_map/ppermute | solution.py:361
  67.5 4.7 %collective-permute-start.27 = (bf16[192,256]{1,0:T(8,128)(2,1)S(1)}, bf16[192,256]{1,0:T(8,128)(2,1)S(1)}, u32[]{:S(2)}, u32[]{:S(2)}) collective-permute-start(bf16[192,256]{1,0:T(8,128)(2,1)S(1)} %fusion.4), channel_id=1, source_target_pairs={{0,2},{1,3},{2,0},{3,1},{4,6},{5,7},{6,4},{7,5},{8,10},{9,11},{10,... | collective-permute-start | bytes 294920 | tf_op jit(solution)/shard_map/ppermute | solution.py:361
  68.2 10.9 %collective-permute-start.29 = (bf16[192,256]{1,0:T(8,128)(2,1)S(1)}, bf16[192,256]{1,0:T(8,128)(2,1)S(1)}, u32[]{:S(2)}, u32[]{:S(2)}) collective-permute-start(bf16[192,256]{1,0:T(8,128)(2,1)S(1)} %get-tuple-element.92), channel_id=1, source_target_pairs={{0,4},{1,5},{2,6},{3,7},{4,0},{5,1},{6,2},{7,3},{8,12},{9,13},{10,... | collective-permute-start | bytes 294920 | tf_op jit(solution)/shard_map/ppermute | solution.py:361
  68.2 9.3 %collective-permute-start.21 = (bf16[192,256]{1,0:T(8,128)(2,1)S(1)}, bf16[192,256]{1,0:T(8,128)(2,1)S(1)}, u32[]{:S(2)}, u32[]{:S(2)}) collective-permute-start(bf16[192,256]{1,0:T(8,128)(2,1)S(1)} %fusion.3), channel_id=1, source_target_pairs={{0,8},{1,9},{2,10},{3,11},{4,12},{5,13},{6,14},{7,15},{8,0},{9,1},... | collective-permute-start | bytes 294920 | tf_op jit(solution)/shard_map/ppermute | solution.py:361
  72.2 6.6 %collective-permute-start.28 = (bf16[192,256]{1,0:T(8,128)(2,1)S(1)}, bf16[192,256]{1,0:T(8,128)(2,1)S(1)}, u32[]{:S(2)}, u32[]{:S(2)}) collective-permute-start(bf16[192,256]{1,0:T(8,128)(2,1)S(1)} %fusion.1), channel_id=1, source_target_pairs={{0,12},{1,13},{2,14},{3,15},{4,8},{5,9},{6,10},{7,11},{8,4},{9,5},... | collective-permute-start | bytes 294920 | tf_op jit(solution)/shard_map/ppermute | solution.py:361
  75.0 6.0 %collective-permute-start.30 = (bf16[192,256]{1,0:T(8,128)(2,1)S(1)}, bf16[192,256]{1,0:T(8,128)(2,1)S(1)}, u32[]{:S(2)}, u32[]{:S(2)}) collective-permute-start(bf16[192,256]{1,0:T(8,128)(2,1)S(1)} %get-tuple-element.85), channel_id=1, source_target_pairs={{0,6},{1,7},{2,4},{3,5},{4,2},{5,3},{6,0},{7,1},{8,14},{9,15},{10,... | collective-permute-start | bytes 294920 | tf_op jit(solution)/shard_map/ppermute | solution.py:361
  75.0 6.2 %collective-permute-start.31 = (bf16[192,256]{1,0:T(8,128)(2,1)S(1)}, bf16[192,256]{1,0:T(8,128)(2,1)S(1)}, u32[]{:S(2)}, u32[]{:S(2)}) collective-permute-start(bf16[192,256]{1,0:T(8,128)(2,1)S(1)} %get-tuple-element.88), channel_id=1, source_target_pairs={{0,2},{1,3},{2,0},{3,1},{4,6},{5,7},{6,4},{7,5},{8,10},{9,11},{10,... | collective-permute-start | bytes 294920 | tf_op jit(solution)/shard_map/ppermute | solution.py:361

commit v12 on v10

--- a/solution.py
+++ b/solution.py
@@ -1,4 +1,5 @@
 import functools
+import math
 
 import jax
 import jax.numpy as jnp
@@ -8,6 +9,7 @@
 from jax.sharding import PartitionSpec as P
 
 HEAD_DIM = 128
+SHARPNESS = HEAD_DIM**-0.5 * math.log2(math.e)
 DIRECT = 8
 CUTS = 4
 TILE = 256
@@ -84,10 +86,10 @@
         part = slice(head * HEAD_DIM, (head + 1) * HEAD_DIM)
         scores = dot(queries[:, part], source[0, :, part], ((1,), (1,)))
         top = jnp.max(scores, axis=1, keepdims=True)
-        weights = jnp.exp((scores - top) * HEAD_DIM**-0.5)
-        total = jnp.sum(weights, axis=1, keepdims=True)
-        context = dot(weights.astype(BF16), source[1, :, part])
-        out[:, part] = (context / total).astype(BF16)
+        weights = jnp.exp2((scores - top) * SHARPNESS).astype(BF16)
+        values = jnp.concatenate([source[1, :, part], jnp.ones((source.shape[1], HEAD_DIM), BF16)], axis=1)
+        summed = dot(weights, values)
+        out[:, part] = (summed[:, :HEAD_DIM] / summed[:, HEAD_DIM:]).astype(BF16)
 
 
 def attend(queries, source, block):
@@ -343,7 +345,6 @@
     groups = lax.axis_size("expert")
     slices = lax.axis_size("mp")
     here, column = lax.axis_index("expert"), lax.axis_index("mp")
-    owner_rows = jnp.broadcast_to(source_owner[:, None], (8, 128))
     width = features // slices
     experts = expand_weight.shape[0] * groups
     capacity = max(2, 3 * token_count // experts)
@@ -370,7 +371,7 @@
 
     steps = range(groups) if direct else [0]
 
-    queries, source = ask(after(tokens, owner_rows), query_weight, encoder_states[0])
+    queries, source = ask(tokens, query_weight, encoder_states[0])
     expert_bits = bits_of(groups)
     bits = bits_of(slices)
     if direct:
@@ -384,7 +385,7 @@
         for k in sorted(range(1, groups), key=lambda k: (k & (k - 1) != 0, -k)):
             answer = previous = attend(after(asked[k], previous), source, token_count)
             backs[k] = hop(answer, k, 0)
-        context = pick(owner_rows, [own] + [backs[k] for k in range(1, groups)])
+        context = pick(source_owner.reshape(1, 1), [own] + [backs[k] for k in range(1, groups)])
     else:
         asked = lax.all_gather(queries, "expert", axis=0, tiled=True)
         previous = attend(asked, source, token_count)
@@ -430,7 +431,7 @@
         arrived = {k: hop(rows, k, 0) for k, rows in zip(sends, leaving)}
         keep, give = expert([[0, 1]], [[own_a, own_b]])
         if sends:
-            give = after(give, arrived[sends[0]])
+            give = after(give, arrived[groups - 1])
         own_sum, wait = sum_cores(keep, give), None
         earlier = own_sum
         turns = [[k for k in sends if k < groups - 1], [groups - 1]] if groups > 2 else [sends]
@@ -439,6 +440,8 @@
             for k in turn:
                 pieces, places = [arrived[k]], [0]
                 for bit in bits if k in far else [1]:
+                    if bit == 1 and wait is not None:
+                        pieces = [after(piece, earlier) for piece in pieces]
                     pieces = pieces + [hop(piece, 0, bit) for piece in pieces]
                     places = places + [index ^ bit for index in places]
                 blocks.append(pieces)

time: 80.3 us -> 80.1 us (level)
  starting transfers between devices: 34 us -> 33 us
  waiting for transfers between devices: 31.9 us -> 32.9 us
    ppermute x32, starting transfers between devices: 34 us -> 33 us  [hop(): return lax.ppermute(value, ('expert', 'mp'), moves)]
    ppermute x32, waiting for transfers between devices: 31.9 us -> 32.9 us  [hop(): return lax.ppermute(value, ('expert', 'mp'), moves)]
  transfers between devices with their start and end apart: 32 -> 32, of which waited for: 15 -> 16; matrix products, arithmetic and copies ran while one was open for 0% -> 0% of each run, Pallas kernels for 14% -> 14%
where the time goes in v12:
time: 80.1 us; the launch traced here: 79.9 us
  starting transfers between devices  33 us (41%)
  waiting for transfers between devices  32.9 us (41%)
  Pallas kernels  12.7 us (16%)
  between operations  0.98 us (1%)
    ppermute x32, starting transfers between devices, hop(): return lax.ppermute(value, ('expert', 'mp'), moves)  33 us
    ppermute x32, waiting for transfers between devices, hop(): return lax.ppermute(value, ('expert', 'mp'), moves)  32.9 us
    pallas_call x3, Pallas kernels, run_expert(): pl.pallas_call(functools.partial(expert_kernel, tuple(map(tuple, orders))...  3.88 us
    pallas_call x4, Pallas kernels, attend(): pl.pallas_call(attend_kernel, in_specs=[WHOLE] * 2, out_specs=WHOLE, out_...  2.8 us
    pallas_call x1, Pallas kernels, ask(): pl.pallas_call(query_kernel, in_specs=[pl.BlockSpec(memory_space=pltpu.HB...  1.81 us
  transfers between devices with their start and end apart: 32, of which 16 were waited for; matrix products, arithmetic and copies ran while one was open for 0% of the time, Pallas kernels for 14%

profile of v12, /device:TPU:0, one launch (start us, length us, event | category | flops | bytes accessed | tf_op | source)
XLA Modules:
  0.0 79.9 jit_solution(8476456123852018741)
XLA Ops:
  0.0 2.9 %collective-permute-start.9 = (bf16[256,1024]{1,0:T(8,128)(2,1)}, bf16[256,1024]{1,0:T(8,128)(2,1)S(1)}, u32[]{:S(2)}, u32[]{:S(2)}) collective-permute-start(bf16[256,1024]{1,0:T(8,128)(2,1)} %refs_5_), channel_id=1, source_target_pairs={{0,2},{1,3},{2,0},{3,1},{4,6},{5,7},{6,4},{7,5},{8,10},{9,11},{10,... | collective-permute-start | bytes 1572872 | tf_op jit(solution)/shard_map/ppermute | solution.py:363
  2.9 1.8 %query.1 = (bf16[256,256]{1,0:T(8,128)(2,1)S(1)}, bf16[2,512,256]{2,1,0:T(8,128)(2,1)S(1)}) custom-call(bf16[256,1024]{1,0:T(8,128)(2,1)} %refs_0_.1, bf16[1024,256]{1,0:T(8,128)(2,1)} %weight.1, bf16[2,512,256]{2,1,0:T(8,128)(2,1)} %bitcast.39), custom_call_target="tpu_custom_call" | custom-call | tf_op jit(solution)/shard_map/query/pallas_call | solution.py:65
  4.8 0.0 copy-start.3
  4.8 0.0 copy-start.5
  4.8 0.0 copy-start.2
  4.8 2.6 %collective-permute-start.1 = (bf16[256,256]{1,0:T(8,128)(2,1)S(1)}, bf16[256,256]{1,0:T(8,128)(2,1)S(1)}, u32[]{:S(2)}, u32[]{:S(2)}) collective-permute-start(bf16[256,256]{1,0:T(8,128)(2,1)S(1)} %get-tuple-element.47.queries), channel_id=1, source_target_pairs={{0,8},{1,9},{2,10},{3,11},{4,12},{5,13},{6,14},{7,15},{8,0},{9,1},... | collective-permute-start | bytes 393224 | tf_op jit(solution)/shard_map/ppermute | solution.py:363
  7.4 1.6 %collective-permute-start = (bf16[256,256]{1,0:T(8,128)(2,1)S(1)}, bf16[256,256]{1,0:T(8,128)(2,1)S(1)}, u32[]{:S(2)}, u32[]{:S(2)}) collective-permute-start(bf16[256,256]{1,0:T(8,128)(2,1)S(1)} %get-tuple-element.47.queries), channel_id=1, source_target_pairs={{0,4},{1,5},{2,6},{3,7},{4,0},{5,1},{6,2},{7,3},{8,12},{9,13},{10,... | collective-permute-start | bytes 393224 | tf_op jit(solution)/shard_map/ppermute | solution.py:363
  9.0 0.7 attend.4.refs_0_
  9.7 3.9 %collective-permute-done.1.queries = bf16[256,256]{1,0:T(8,128)(2,1)S(1)} collective-permute-done((bf16[256,256]{1,0:T(8,128)(2,1)S(1)}, bf16[256,256]{1,0:T(8,128)(2,1)S(1)}, u32[]{:S(2)}, u32[]{:S(2)}) %collective-permute-start.1) | collective-permute-done | bytes 131104 | tf_op jit(solution)/shard_map/ppermute | solution.py:363
  13.6 0.6 collective-permute-start.4
  14.2 0.7 attend.5
  14.9 3.4 %collective-permute-start.3 = (bf16[256,256]{1,0:T(8,128)(2,1)S(1)}, bf16[256,256]{1,0:T(8,128)(2,1)S(1)}, u32[]{:S(2)}, u32[]{:S(2)}) collective-permute-start(bf16[256,256]{1,0:T(8,128)(2,1)S(1)} %attend.5), channel_id=1, source_target_pairs={{0,8},{1,9},{2,10},{3,11},{4,12},{5,13},{6,14},{7,15},{8,0},{9,1},... | collective-permute-start | bytes 393224 | tf_op jit(solution)/shard_map/ppermute | solution.py:363
  18.4 0.7 attend.6
  19.1 0.1 collective-permute-start.2
  19.1 0.7 attend.7
  19.9 0.0 copy-start.4
  19.9 5.9 %collective-permute-start.5 = (bf16[256,256]{1,0:T(8,128)(2,1)S(1)}, bf16[256,256]{1,0:T(8,128)(2,1)S(1)}, u32[]{:S(2)}, u32[]{:S(2)}) collective-permute-start(bf16[256,256]{1,0:T(8,128)(2,1)S(1)} %attend.7), channel_id=1, source_target_pairs={{0,12},{1,13},{2,14},{3,15},{4,8},{5,9},{6,10},{7,11},{8,4},{9,5},... | collective-permute-start | bytes 393224 | tf_op jit(solution)/shard_map/ppermute | solution.py:363
  26.4 2.8 %collective-permute-done.5.refs_3_ = bf16[256,256]{1,0:T(8,128)(2,1)S(1)} collective-permute-done((bf16[256,256]{1,0:T(8,128)(2,1)S(1)}, bf16[256,256]{1,0:T(8,128)(2,1)S(1)}, u32[]{:S(2)}, u32[]{:S(2)}) %collective-permute-start.5) | collective-permute-done | bytes 131104 | tf_op jit(solution)/shard_map/ppermute | solution.py:363
  29.3 0.1 pick.1.refs_1_
  29.4 0.1 collective-permute-start.10
  29.5 0.5 collective-permute-start.11
  30.0 0.5 collective-permute-start.6
  30.6 1.0 %route.1 = (s32[256,2]{1,0:T(8,128)S(1)}, bf16[192,256]{1,0:T(8,128)(2,1)S(1)}, bf16[192,256]{1,0:T(8,128)(2,1)S(1)}, bf16[192,256]{1,0:T(8,128)(2,1)S(1)}, bf16...) custom-call(s32[2,256]{1,0:T(2,128)S(1)} %bitcast.38), custom_call_target="tpu_custom_call" | custom-call | tf_op jit(solution)/shard_map/route/pallas_call | solution.py:177
  31.5 0.1 collective-permute-start.7
  31.6 3.9 %collective-permute-done.6.refs_2_ = bf16[256,256]{1,0:T(8,128)(2,1)S(1)} collective-permute-done((bf16[256,256]{1,0:T(8,128)(2,1)S(1)}, bf16[256,256]{1,0:T(8,128)(2,1)S(1)}, u32[]{:S(2)}, u32[]{:S(2)}) %collective-permute-start.6) | collective-permute-done | bytes 131104 | tf_op jit(solution)/shard_map/ppermute | solution.py:363
  35.5 1.3 %collective-permute-done.8.refs_4_ = bf16[256,256]{1,0:T(8,128)(2,1)S(1)} collective-permute-done((bf16[256,256]{1,0:T(8,128)(2,1)S(1)}, bf16[256,256]{1,0:T(8,128)(2,1)S(1)}, u32[]{:S(2)}, u32[]{:S(2)}) %collective-permute-start.8) | collective-permute-done | bytes 131104 | tf_op jit(solution)/shard_map/ppermute | solution.py:363
  36.9 0.0 copy-start.1
  36.9 1.0 %state.1 = (bf16[256,1024]{1,0:T(8,128)(2,1)S(1)}, bf16[192,256]{1,0:T(8,128)(2,1)S(1)}, bf16[192,256]{1,0:T(8,128)(2,1)S(1)}, bf16[192,512]{1,0:T(8,128)(2,1)S(1)}) custom-call(bf16[256,1024]{1,0:T(8,128)(2,1)S(1)} %copy-done.2, bf16[256,256]{1,0:T(8,128)(2,1)S(1)} %pick.1.refs_1_, bf16[256,256]{1,0:T(8,128)(2,1)S(1)} %collective-permute-done.6.refs_2_, ...), custom_call_target="tpu_custom_call" | custom-call | tf_op jit(solution)/shard_map/state/pallas_call | solution.py:210
  37.9 3.4 %collective-permute-start.12 = (bf16[192,256]{1,0:T(8,128)(2,1)S(1)}, bf16[192,256]{1,0:T(8,128)(2,1)S(1)}, u32[]{:S(2)}, u32[]{:S(2)}) collective-permute-start(bf16[192,256]{1,0:T(8,128)(2,1)S(1)} %get-tuple-element.70), channel_id=1, source_target_pairs={{0,12},{1,13},{2,14},{3,15},{4,8},{5,9},{6,10},{7,11},{8,4},{9,5},... | collective-permute-start | bytes 294920 | tf_op jit(solution)/shard_map/ppermute | solution.py:363
  41.2 1.1 %collective-permute-start.18 = (bf16[192,512]{1,0:T(8,128)(2,1)S(1)}, bf16[192,512]{1,0:T(8,128)(2,1)S(1)}, u32[]{:S(2)}, u32[]{:S(2)}) collective-permute-start(bf16[192,512]{1,0:T(8,128)(2,1)S(1)} %get-tuple-element.74), channel_id=1, source_target_pairs={{0,4},{1,5},{2,6},{3,7},{4,0},{5,1},{6,2},{7,3},{8,12},{9,13},{10,... | collective-permute-start | bytes 589832 | tf_op jit(solution)/shard_map/ppermute | solution.py:363
  42.3 0.5 home.1
  42.9 1.0 %expert.3 = (f32[2,192,256]{2,1,0:T(8,128)S(1)}, bf16[2,192,256]{2,1,0:T(8,128)(2,1)S(1)}) custom-call(bf16[192,512]{1,0:T(8,128)(2,1)S(1)} %get-tuple-element.66.refs_0_, bf16[192,512]{1,0:T(8,128)(2,1)S(1)} %get-tuple-element.67.refs_1_, bf16[1024,1024]{1,0:T(8,128)(2,1)S(1)} %bitcast.31, bf16[1024,1024]{1,0:T(8,128)(2,1)S(1)} %bitcast.34), custom_call_target="tpu_custom_call" | custom-call | tf_op jit(solution)/shard_map/expert/pallas_call | solution.py:289
  43.9 1.6 %collective-permute-done.12.refs_0_ = bf16[192,256]{1,0:T(8,128)(2,1)S(1)} collective-permute-done((bf16[192,256]{1,0:T(8,128)(2,1)S(1)}, bf16[192,256]{1,0:T(8,128)(2,1)S(1)}, u32[]{:S(2)}, u32[]{:S(2)}) %collective-permute-start.12) | collective-permute-done | bytes 98336 | tf_op jit(solution)/shard_map/ppermute | solution.py:363
  45.5 4.6 %collective-permute-done.14.refs_0_ = bf16[192,256]{1,0:T(8,128)(2,1)S(1)} collective-permute-done((bf16[192,256]{1,0:T(8,128)(2,1)S(1)}, bf16[192,256]{1,0:T(8,128)(2,1)S(1)}, u32[]{:S(2)}, u32[]{:S(2)}) %collective-permute-start.14) | collective-permute-done | bytes 98336 | tf_op jit(solution)/shard_map/ppermute | solution.py:363
  50.1 0.5 collective-permute-start.15
  50.7 1.5 %collective-permute-start.26 = (bf16[192,256]{1,0:T(8,128)(2,1)S(1)}, bf16[192,256]{1,0:T(8,128)(2,1)S(1)}, u32[]{:S(2)}, u32[]{:S(2)}) collective-permute-start(bf16[192,256]{1,0:T(8,128)(2,1)S(1)} %collective-permute-done.12.refs_0_), channel_id=1, source_target_pairs={{0,2},{1,3},{2,0},{3,1},{4,6},{5,7},{6,4},{7,5},{8,10},{9,11},{10,... | collective-permute-start | bytes 294920 | tf_op jit(solution)/shard_map/ppermute | solution.py:363
  52.1 0.5 collective-permute-start.19
  52.6 2.4 %collective-permute-done.15.refs_1_ = bf16[192,256]{1,0:T(8,128)(2,1)S(1)} collective-permute-done((bf16[192,256]{1,0:T(8,128)(2,1)S(1)}, bf16[192,256]{1,0:T(8,128)(2,1)S(1)}, u32[]{:S(2)}, u32[]{:S(2)}) %collective-permute-start.15) | collective-permute-done | bytes 98336 | tf_op jit(solution)/shard_map/ppermute | solution.py:363
  55.1 1.2 %collective-permute-done.17.refs_3_ = bf16[192,256]{1,0:T(8,128)(2,1)S(1)} collective-permute-done((bf16[192,256]{1,0:T(8,128)(2,1)S(1)}, bf16[192,256]{1,0:T(8,128)(2,1)S(1)}, u32[]{:S(2)}, u32[]{:S(2)}) %collective-permute-start.17) | collective-permute-done | bytes 98336 | tf_op jit(solution)/shard_map/ppermute | solution.py:363
  56.4 1.9 %expert.4 = (f32[2,384,256]{2,1,0:T(8,128)S(1)}, bf16[2,384,256]{2,1,0:T(8,128)(2,1)S(1)}) custom-call(bf16[192,256]{1,0:T(8,128)(2,1)S(1)} %collective-permute-done.14.refs_0_, bf16[192,256]{1,0:T(8,128)(2,1)S(1)} %collective-permute-done.15.refs_1_, bf16[192,256]{1,0:T(8,128)(2,1)S(1)} %collective-permute-done.16.refs_2_, ...), custom_call_target="tpu_custom_call" | custom-call | tf_op jit(solution)/shard_map/expert/pallas_call | solution.py:289
  58.3 0.2 collective-permute-start.27
  58.5 0.4 collective-permute-start.28
  58.8 0.2 collective-permute-start.20
  59.0 0.6 collective-permute-done.27.refs_2_
  59.6 0.2 collective-permute-done.28.refs_3_
  59.8 1.0 %expert.5 = (f32[2,192,256]{2,1,0:T(8,128)S(1)}, bf16[2,192,256]{2,1,0:T(8,128)(2,1)S(1)}) custom-call(bf16[192,256]{1,0:T(8,128)(2,1)S(1)} %collective-permute-done.12.refs_0_, bf16[192,256]{1,0:T(8,128)(2,1)S(1)} %collective-permute-done.26.refs_1_, bf16[192,256]{1,0:T(8,128)(2,1)S(1)} %collective-permute-done.27.refs_2_, ...), custom_call_target="tpu_custom_call" | custom-call | tf_op jit(solution)/shard_map/expert/pallas_call | solution.py:289
  60.8 0.4 collective-permute-start.29
  61.2 1.1 %collective-permute-done.29 = bf16[2,192,256]{2,1,0:T(8,128)(2,1)S(1)} collective-permute-done((bf16[2,192,256]{2,1,0:T(8,128)(2,1)S(1)}, bf16[2,192,256]{2,1,0:T(8,128)(2,1)S(1)}, u32[]{:S(2)}, u32[]{:S(2)}) %collective-permute-start.29) | collective-permute-done | bytes 196640 | tf_op jit(solution)/shard_map/ppermute | solution.py:363
  62.4 0.1 fusion.5
  62.5 0.8 collective-permute-start.21
  63.3 1.4 %collective-permute-start.30 = (bf16[192,256]{1,0:T(8,128)(2,1)S(1)}, bf16[192,256]{1,0:T(8,128)(2,1)S(1)}, u32[]{:S(2)}, u32[]{:S(2)}) collective-permute-start(bf16[192,256]{1,0:T(8,128)(2,1)S(1)} %fusion.4), channel_id=1, source_target_pairs={{0,2},{1,3},{2,0},{3,1},{4,6},{5,7},{6,4},{7,5},{8,10},{9,11},{10,... | collective-permute-start | bytes 294920 | tf_op jit(solution)/shard_map/ppermute | solution.py:363
  64.7 2.2 %collective-permute-start.23 = (bf16[192,256]{1,0:T(8,128)(2,1)S(1)}, bf16[192,256]{1,0:T(8,128)(2,1)S(1)}, u32[]{:S(2)}, u32[]{:S(2)}) collective-permute-start(bf16[192,256]{1,0:T(8,128)(2,1)S(1)} %get-tuple-element.92), channel_id=1, source_target_pairs={{0,4},{1,5},{2,6},{3,7},{4,0},{5,1},{6,2},{7,3},{8,12},{9,13},{10,... | collective-permute-start | bytes 294920 | tf_op jit(solution)/shard_map/ppermute | solution.py:363
  66.9 2.4 %collective-permute-done.21 = bf16[192,256]{1,0:T(8,128)(2,1)S(1)} collective-permute-done((bf16[192,256]{1,0:T(8,128)(2,1)S(1)}, bf16[192,256]{1,0:T(8,128)(2,1)S(1)}, u32[]{:S(2)}, u32[]{:S(2)}) %collective-permute-start.21) | collective-permute-done | bytes 98336 | tf_op jit(solution)/shard_map/ppermute | solution.py:363
  69.3 0.4 collective-permute-start.25
  69.8 0.4 collective-permute-start.22
  70.2 2.2 %collective-permute-done.30 = bf16[192,256]{1,0:T(8,128)(2,1)S(1)} collective-permute-done((bf16[192,256]{1,0:T(8,128)(2,1)S(1)}, bf16[192,256]{1,0:T(8,128)(2,1)S(1)}, u32[]{:S(2)}, u32[]{:S(2)}) %collective-permute-start.30) | collective-permute-done | bytes 98336 | tf_op jit(solution)/shard_map/ppermute | solution.py:363
  72.4 1.3 %collective-permute-start.31 = (bf16[192,256]{1,0:T(8,128)(2,1)S(1)}, bf16[192,256]{1,0:T(8,128)(2,1)S(1)}, u32[]{:S(2)}, u32[]{:S(2)}) collective-permute-start(bf16[192,256]{1,0:T(8,128)(2,1)S(1)} %fusion.1), channel_id=1, source_target_pairs={{0,12},{1,13},{2,14},{3,15},{4,8},{5,9},{6,10},{7,11},{8,4},{9,5},... | collective-permute-start | bytes 294920 | tf_op jit(solution)/shard_map/ppermute | solution.py:363
  73.8 0.6 collective-permute-done.22.refs_1_
  74.4 0.2 combine.4.base
  74.6 0.2 combine.5.base
  74.9 2.6 %collective-permute-done.25.refs_0_ = bf16[192,256]{1,0:T(8,128)(2,1)S(1)} collective-permute-done((bf16[192,256]{1,0:T(8,128)(2,1)S(1)}, bf16[192,256]{1,0:T(8,128)(2,1)S(1)}, u32[]{:S(2)}, u32[]{:S(2)}) %collective-permute-start.25) | collective-permute-done | bytes 98336 | tf_op jit(solution)/shard_map/ppermute | solution.py:363
  77.5 0.2 combine.6.base
  77.7 1.3 %collective-permute-done.31.refs_0_ = bf16[192,256]{1,0:T(8,128)(2,1)S(1)} collective-permute-done((bf16[192,256]{1,0:T(8,128)(2,1)S(1)}, bf16[192,256]{1,0:T(8,128)(2,1)S(1)}, u32[]{:S(2)}, u32[]{:S(2)}) %collective-permute-start.31) | collective-permute-done | bytes 98336 | tf_op jit(solution)/shard_map/ppermute | solution.py:363
  79.0 0.9 %combine.7 = bf16[256,256]{1,0:T(8,128)(2,1)} custom-call(f32[256,2]{1,0:T(8,128)S(1)} %get-tuple-element.62.gates, f32[256,256]{1,0:T(8,128)S(1)} %combine.6.base, bf16[256,192]{1,0:T(8,128)(2,1)S(1)} %get-tuple-element.82.first, bf16[256,192]{1,0:T(8,128)(2,1)S(1)} %get-tuple-element.83.second, bf16[192,256]{1,0:T(8,128)(2,1)S(1)} %collective-permute-done.31.refs_0_), custom_call_target="tpu_custom_call" | custom-call | tf_op jit(solution)/shard_map/combine/pallas_call | solution.py:315
  (36 shorter events, 0.2 us)
Async XLA Ops:
  0.0 29.5 %collective-permute-start.9 = (bf16[256,1024]{1,0:T(8,128)(2,1)}, bf16[256,1024]{1,0:T(8,128)(2,1)S(1)}, u32[]{:S(2)}, u32[]{:S(2)}) collective-permute-start(bf16[256,1024]{1,0:T(8,128)(2,1)} %refs_5_), channel_id=1, source_target_pairs={{0,2},{1,3},{2,0},{3,1},{4,6},{5,7},{6,4},{7,5},{8,10},{9,11},{10,... | collective-permute-start | bytes 1572872 | tf_op jit(solution)/shard_map/ppermute | solution.py:363
  4.8 24.7 %copy-start.3 = (bf16[256,1024]{1,0:T(8,128)(2,1)S(1)}, bf16[256,1024]{1,0:T(8,128)(2,1)}, u32[]{:S(2)}) copy-start(bf16[256,1024]{1,0:T(8,128)(2,1)} %refs_5_) | copy-start | bytes 1572868
  4.8 25.8 %copy-start.5 = (s32[256,2]{0,1:T(2,128)S(1)}, s32[256,2]{0,1:T(2,128)}, u32[]{:S(2)}) copy-start(s32[256,2]{0,1:T(2,128)} %param.15) | copy-start | bytes 6148
  4.8 32.1 %copy-start.2 = (bf16[256,1024]{1,0:T(8,128)(2,1)S(1)}, bf16[256,1024]{1,0:T(8,128)(2,1)}, u32[]{:S(2)}) copy-start(bf16[256,1024]{1,0:T(8,128)(2,1)} %refs_0_.1) | copy-start | bytes 1572868
  4.8 8.8 %collective-permute-start.1 = (bf16[256,256]{1,0:T(8,128)(2,1)S(1)}, bf16[256,256]{1,0:T(8,128)(2,1)S(1)}, u32[]{:S(2)}, u32[]{:S(2)}) collective-permute-start(bf16[256,256]{1,0:T(8,128)(2,1)S(1)} %get-tuple-element.47.queries), channel_id=1, source_target_pairs={{0,8},{1,9},{2,10},{3,11},{4,12},{5,13},{6,14},{7,15},{8,0},{9,1},... | collective-permute-start | bytes 393224 | tf_op jit(solution)/shard_map/ppermute | solution.py:363
  7.4 10.9 %collective-permute-start = (bf16[256,256]{1,0:T(8,128)(2,1)S(1)}, bf16[256,256]{1,0:T(8,128)(2,1)S(1)}, u32[]{:S(2)}, u32[]{:S(2)}) collective-permute-start(bf16[256,256]{1,0:T(8,128)(2,1)S(1)} %get-tuple-element.47.queries), channel_id=1, source_target_pairs={{0,4},{1,5},{2,6},{3,7},{4,0},{5,1},{6,2},{7,3},{8,12},{9,13},{10,... | collective-permute-start | bytes 393224 | tf_op jit(solution)/shard_map/ppermute | solution.py:363
  13.6 5.5 %collective-permute-start.4 = (bf16[256,256]{1,0:T(8,128)(2,1)S(1)}, bf16[256,256]{1,0:T(8,128)(2,1)S(1)}, u32[]{:S(2)}, u32[]{:S(2)}) collective-permute-start(bf16[256,256]{1,0:T(8,128)(2,1)S(1)} %collective-permute-done.1.queries), channel_id=1, source_target_pairs={{0,4},{1,5},{2,6},{3,7},{4,0},{5,1},{6,2},{7,3},{8,12},{9,13},{10,... | collective-permute-start | bytes 393224 | tf_op jit(solution)/shard_map/ppermute | solution.py:363
  14.9 11.5 %collective-permute-start.3 = (bf16[256,256]{1,0:T(8,128)(2,1)S(1)}, bf16[256,256]{1,0:T(8,128)(2,1)S(1)}, u32[]{:S(2)}, u32[]{:S(2)}) collective-permute-start(bf16[256,256]{1,0:T(8,128)(2,1)S(1)} %attend.5), channel_id=1, source_target_pairs={{0,8},{1,9},{2,10},{3,11},{4,12},{5,13},{6,14},{7,15},{8,0},{9,1},... | collective-permute-start | bytes 393224 | tf_op jit(solution)/shard_map/ppermute | solution.py:363
  19.1 7.4 %collective-permute-start.2 = (bf16[256,256]{1,0:T(8,128)(2,1)S(1)}, bf16[256,256]{1,0:T(8,128)(2,1)S(1)}, u32[]{:S(2)}, u32[]{:S(2)}) collective-permute-start(bf16[256,256]{1,0:T(8,128)(2,1)S(1)} %attend.6), channel_id=1, source_target_pairs={{0,4},{1,5},{2,6},{3,7},{4,0},{5,1},{6,2},{7,3},{8,12},{9,13},{10,... | collective-permute-start | bytes 393224 | tf_op jit(solution)/shard_map/ppermute | solution.py:363
  19.9 22.5 %copy-start.4 = (bf16[1024,4]{0,1:T(4,128)(2,1)S(1)}, bf16[1024,4]{0,1:T(4,128)(2,1)}, u32[]{:S(2)}) copy-start(bf16[1024,4]{0,1:T(4,128)(2,1)} %param.14) | copy-start | bytes 24580
  19.9 9.4 %collective-permute-start.5 = (bf16[256,256]{1,0:T(8,128)(2,1)S(1)}, bf16[256,256]{1,0:T(8,128)(2,1)S(1)}, u32[]{:S(2)}, u32[]{:S(2)}) collective-permute-start(bf16[256,256]{1,0:T(8,128)(2,1)S(1)} %attend.7), channel_id=1, source_target_pairs={{0,12},{1,13},{2,14},{3,15},{4,8},{5,9},{6,10},{7,11},{8,4},{9,5},... | collective-permute-start | bytes 393224 | tf_op jit(solution)/shard_map/ppermute | solution.py:363
  29.4 7.4 %collective-permute-start.10 = (bf16[256,1024]{1,0:T(8,128)(2,1)S(1)}, bf16[256,1024]{1,0:T(8,128)(2,1)S(1)}, u32[]{:S(2)}, u32[]{:S(2)}) collective-permute-start(bf16[256,1024]{1,0:T(8,128)(2,1)S(1)} %copy-done.3), channel_id=1, source_target_pairs={{0,1},{1,0},{2,3},{3,2},{4,5},{5,4},{6,7},{7,6},{8,9},{9,8},{10,11... | collective-permute-start | bytes 1572872 | tf_op jit(solution)/shard_map/ppermute | solution.py:363
  29.5 7.3 %collective-permute-start.11 = (bf16[256,1024]{1,0:T(8,128)(2,1)S(1)}, bf16[256,1024]{1,0:T(8,128)(2,1)S(1)}, u32[]{:S(2)}, u32[]{:S(2)}) collective-permute-start(bf16[256,1024]{1,0:T(8,128)(2,1)S(1)} %collective-permute-done.9.refs_6_), channel_id=1, source_target_pairs={{0,1},{1,0},{2,3},{3,2},{4,5},{5,4},{6,7},{7,6},{8,9},{9,8},{10,11... | collective-permute-start | bytes 1572872 | tf_op jit(solution)/shard_map/ppermute | solution.py:363
  30.0 5.5 %collective-permute-start.6 = (bf16[256,256]{1,0:T(8,128)(2,1)S(1)}, bf16[256,256]{1,0:T(8,128)(2,1)S(1)}, u32[]{:S(2)}, u32[]{:S(2)}) collective-permute-start(bf16[256,256]{1,0:T(8,128)(2,1)S(1)} %pick.1.refs_1_), channel_id=1, source_target_pairs={{0,2},{1,3},{2,0},{3,1},{4,6},{5,7},{6,4},{7,5},{8,10},{9,11},{10,... | collective-permute-start | bytes 393224 | tf_op jit(solution)/shard_map/ppermute | solution.py:363
  31.5 4.0 %collective-permute-start.7 = (bf16[256,256]{1,0:T(8,128)(2,1)S(1)}, bf16[256,256]{1,0:T(8,128)(2,1)S(1)}, u32[]{:S(2)}, u32[]{:S(2)}) collective-permute-start(bf16[256,256]{1,0:T(8,128)(2,1)S(1)} %pick.1.refs_1_), channel_id=1, source_target_pairs={{0,1},{1,0},{2,3},{3,2},{4,5},{5,4},{6,7},{7,6},{8,9},{9,8},{10,11... | collective-permute-start | bytes 393224 | tf_op jit(solution)/shard_map/ppermute | solution.py:363
  35.5 1.3 %collective-permute-start.8 = (bf16[256,256]{1,0:T(8,128)(2,1)S(1)}, bf16[256,256]{1,0:T(8,128)(2,1)S(1)}, u32[]{:S(2)}, u32[]{:S(2)}) collective-permute-start(bf16[256,256]{1,0:T(8,128)(2,1)S(1)} %collective-permute-done.6.refs_2_), channel_id=1, source_target_pairs={{0,1},{1,0},{2,3},{3,2},{4,5},{5,4},{6,7},{7,6},{8,9},{9,8},{10,11... | collective-permute-start | bytes 393224 | tf_op jit(solution)/shard_map/ppermute | solution.py:363
  36.9 6.0 %copy-start = (bf16[1,1024,1024]{2,1,0:T(8,128)(2,1)S(1)}, bf16[1,1024,1024]{2,1,0:T(8,128)(2,1)}, u32[]{:S(2)}) copy-start(bf16[1,1024,1024]{2,1,0:T(8,128)(2,1)} %param.16) | copy-start | bytes 6291460
  36.9 6.0 %copy-start.1 = (bf16[1,1024,1024]{2,1,0:T(8,128)(2,1)S(1)}, bf16[1,1024,1024]{2,1,0:T(8,128)(2,1)}, u32[]{:S(2)}) copy-start(bf16[1,1024,1024]{2,1,0:T(8,128)(2,1)} %param.17) | copy-start | bytes 6291460
  37.9 7.6 %collective-permute-start.12 = (bf16[192,256]{1,0:T(8,128)(2,1)S(1)}, bf16[192,256]{1,0:T(8,128)(2,1)S(1)}, u32[]{:S(2)}, u32[]{:S(2)}) collective-permute-start(bf16[192,256]{1,0:T(8,128)(2,1)S(1)} %get-tuple-element.70), channel_id=1, source_target_pairs={{0,12},{1,13},{2,14},{3,15},{4,8},{5,9},{6,10},{7,11},{8,4},{9,5},... | collective-permute-start | bytes 294920 | tf_op jit(solution)/shard_map/ppermute | solution.py:363
  41.2 8.9 %collective-permute-start.14 = (bf16[192,256]{1,0:T(8,128)(2,1)S(1)}, bf16[192,256]{1,0:T(8,128)(2,1)S(1)}, u32[]{:S(2)}, u32[]{:S(2)}) collective-permute-start(bf16[192,256]{1,0:T(8,128)(2,1)S(1)} %get-tuple-element.72), channel_id=1, source_target_pairs={{0,8},{1,9},{2,10},{3,11},{4,12},{5,13},{6,14},{7,15},{8,0},{9,1},... | collective-permute-start | bytes 294920 | tf_op jit(solution)/shard_map/ppermute | solution.py:363
  41.2 10.9 %collective-permute-start.18 = (bf16[192,512]{1,0:T(8,128)(2,1)S(1)}, bf16[192,512]{1,0:T(8,128)(2,1)S(1)}, u32[]{:S(2)}, u32[]{:S(2)}) collective-permute-start(bf16[192,512]{1,0:T(8,128)(2,1)S(1)} %get-tuple-element.74), channel_id=1, source_target_pairs={{0,4},{1,5},{2,6},{3,7},{4,0},{5,1},{6,2},{7,3},{8,12},{9,13},{10,... | collective-permute-start | bytes 589832 | tf_op jit(solution)/shard_map/ppermute | solution.py:363
  45.5 9.6 %collective-permute-start.13 = (bf16[2,192,256]{2,1,0:T(8,128)(2,1)S(1)}, bf16[2,192,256]{2,1,0:T(8,128)(2,1)S(1)}, u32[]{:S(2)}, u32[]{:S(2)}) collective-permute-start(bf16[2,192,256]{2,1,0:T(8,128)(2,1)S(1)} %get-tuple-element.71), channel_id=1, source_target_pairs={{0,1},{1,0},{2,3},{3,2},{4,5},{5,4},{6,7},{7,6},{8,9},{9,8},{10,11... | collective-permute-start | bytes 589832 | tf_op jit(solution)/shard_map/ppermute | solution.py:363
  50.1 5.0 %collective-permute-start.15 = (bf16[192,256]{1,0:T(8,128)(2,1)S(1)}, bf16[192,256]{1,0:T(8,128)(2,1)S(1)}, u32[]{:S(2)}, u32[]{:S(2)}) collective-permute-start(bf16[192,256]{1,0:T(8,128)(2,1)S(1)} %collective-permute-done.14.refs_0_), channel_id=1, source_target_pairs={{0,2},{1,3},{2,0},{3,1},{4,6},{5,7},{6,4},{7,5},{8,10},{9,11},{10,... | collective-permute-start | bytes 294920 | tf_op jit(solution)/shard_map/ppermute | solution.py:363
  50.7 7.6 %collective-permute-start.26 = (bf16[192,256]{1,0:T(8,128)(2,1)S(1)}, bf16[192,256]{1,0:T(8,128)(2,1)S(1)}, u32[]{:S(2)}, u32[]{:S(2)}) collective-permute-start(bf16[192,256]{1,0:T(8,128)(2,1)S(1)} %collective-permute-done.12.refs_0_), channel_id=1, source_target_pairs={{0,2},{1,3},{2,0},{3,1},{4,6},{5,7},{6,4},{7,5},{8,10},{9,11},{10,... | collective-permute-start | bytes 294920 | tf_op jit(solution)/shard_map/ppermute | solution.py:363
  52.1 3.0 %collective-permute-start.16 = (bf16[192,256]{1,0:T(8,128)(2,1)S(1)}, bf16[192,256]{1,0:T(8,128)(2,1)S(1)}, u32[]{:S(2)}, u32[]{:S(2)}) collective-permute-start(bf16[192,256]{1,0:T(8,128)(2,1)S(1)} %collective-permute-done.14.refs_0_), channel_id=1, source_target_pairs={{0,1},{1,0},{2,3},{3,2},{4,5},{5,4},{6,7},{7,6},{8,9},{9,8},{10,11... | collective-permute-start | bytes 294920 | tf_op jit(solution)/shard_map/ppermute | solution.py:363
  52.1 4.2 %collective-permute-start.19 = (bf16[192,512]{1,0:T(8,128)(2,1)S(1)}, bf16[192,512]{1,0:T(8,128)(2,1)S(1)}, u32[]{:S(2)}, u32[]{:S(2)}) collective-permute-start(bf16[192,512]{1,0:T(8,128)(2,1)S(1)} %collective-permute-done.18.refs_4_), channel_id=1, source_target_pairs={{0,1},{1,0},{2,3},{3,2},{4,5},{5,4},{6,7},{7,6},{8,9},{9,8},{10,11... | collective-permute-start | bytes 589832 | tf_op jit(solution)/shard_map/ppermute | solution.py:363
  55.1 1.3 %collective-permute-start.17 = (bf16[192,256]{1,0:T(8,128)(2,1)S(1)}, bf16[192,256]{1,0:T(8,128)(2,1)S(1)}, u32[]{:S(2)}, u32[]{:S(2)}) collective-permute-start(bf16[192,256]{1,0:T(8,128)(2,1)S(1)} %collective-permute-done.15.refs_1_), channel_id=1, source_target_pairs={{0,1},{1,0},{2,3},{3,2},{4,5},{5,4},{6,7},{7,6},{8,9},{9,8},{10,11... | collective-permute-start | bytes 294920 | tf_op jit(solution)/shard_map/ppermute | solution.py:363
  58.3 1.4 %collective-permute-start.27 = (bf16[192,256]{1,0:T(8,128)(2,1)S(1)}, bf16[192,256]{1,0:T(8,128)(2,1)S(1)}, u32[]{:S(2)}, u32[]{:S(2)}) collective-permute-start(bf16[192,256]{1,0:T(8,128)(2,1)S(1)} %collective-permute-done.12.refs_0_), channel_id=1, source_target_pairs={{0,1},{1,0},{2,3},{3,2},{4,5},{5,4},{6,7},{7,6},{8,9},{9,8},{10,11... | collective-permute-start | bytes 294920 | tf_op jit(solution)/shard_map/ppermute | solution.py:363
  58.5 1.3 %collective-permute-start.28 = (bf16[192,256]{1,0:T(8,128)(2,1)S(1)}, bf16[192,256]{1,0:T(8,128)(2,1)S(1)}, u32[]{:S(2)}, u32[]{:S(2)}) collective-permute-start(bf16[192,256]{1,0:T(8,128)(2,1)S(1)} %collective-permute-done.26.refs_1_), channel_id=1, source_target_pairs={{0,1},{1,0},{2,3},{3,2},{4,5},{5,4},{6,7},{7,6},{8,9},{9,8},{10,11... | collective-permute-start | bytes 294920 | tf_op jit(solution)/shard_map/ppermute | solution.py:363
  58.8 3.5 %collective-permute-start.20 = (bf16[2,384,256]{2,1,0:T(8,128)(2,1)S(1)}, bf16[2,384,256]{2,1,0:T(8,128)(2,1)S(1)}, u32[]{:S(2)}, u32[]{:S(2)}) collective-permute-start(bf16[2,384,256]{2,1,0:T(8,128)(2,1)S(1)} %get-tuple-element.76), channel_id=1, source_target_pairs={{0,1},{1,0},{2,3},{3,2},{4,5},{5,4},{6,7},{7,6},{8,9},{9,8},{10,11... | collective-permute-start | bytes 1179656 | tf_op jit(solution)/shard_map/ppermute | solution.py:363
  60.8 1.5 %collective-permute-start.29 = (bf16[2,192,256]{2,1,0:T(8,128)(2,1)S(1)}, bf16[2,192,256]{2,1,0:T(8,128)(2,1)S(1)}, u32[]{:S(2)}, u32[]{:S(2)}) collective-permute-start(bf16[2,192,256]{2,1,0:T(8,128)(2,1)S(1)} %get-tuple-element.88), channel_id=1, source_target_pairs={{0,1},{1,0},{2,3},{3,2},{4,5},{5,4},{6,7},{7,6},{8,9},{9,8},{10,11... | collective-permute-start | bytes 589832 | tf_op jit(solution)/shard_map/ppermute | solution.py:363
  62.5 6.8 %collective-permute-start.21 = (bf16[192,256]{1,0:T(8,128)(2,1)S(1)}, bf16[192,256]{1,0:T(8,128)(2,1)S(1)}, u32[]{:S(2)}, u32[]{:S(2)}) collective-permute-start(bf16[192,256]{1,0:T(8,128)(2,1)S(1)} %get-tuple-element.93), channel_id=1, source_target_pairs={{0,2},{1,3},{2,0},{3,1},{4,6},{5,7},{6,4},{7,5},{8,10},{9,11},{10,... | collective-permute-start | bytes 294920 | tf_op jit(solution)/shard_map/ppermute | solution.py:363
  63.3 9.1 %collective-permute-start.30 = (bf16[192,256]{1,0:T(8,128)(2,1)S(1)}, bf16[192,256]{1,0:T(8,128)(2,1)S(1)}, u32[]{:S(2)}, u32[]{:S(2)}) collective-permute-start(bf16[192,256]{1,0:T(8,128)(2,1)S(1)} %fusion.4), channel_id=1, source_target_pairs={{0,2},{1,3},{2,0},{3,1},{4,6},{5,7},{6,4},{7,5},{8,10},{9,11},{10,... | collective-permute-start | bytes 294920 | tf_op jit(solution)/shard_map/ppermute | solution.py:363
  64.7 9.9 %collective-permute-start.24 = (bf16[192,256]{1,0:T(8,128)(2,1)S(1)}, bf16[192,256]{1,0:T(8,128)(2,1)S(1)}, u32[]{:S(2)}, u32[]{:S(2)}) collective-permute-start(bf16[192,256]{1,0:T(8,128)(2,1)S(1)} %get-tuple-element.91), channel_id=1, source_target_pairs={{0,6},{1,7},{2,4},{3,5},{4,2},{5,3},{6,0},{7,1},{8,14},{9,15},{10,... | collective-permute-start | bytes 294920 | tf_op jit(solution)/shard_map/ppermute | solution.py:363
  64.7 9.9 %collective-permute-start.23 = (bf16[192,256]{1,0:T(8,128)(2,1)S(1)}, bf16[192,256]{1,0:T(8,128)(2,1)S(1)}, u32[]{:S(2)}, u32[]{:S(2)}) collective-permute-start(bf16[192,256]{1,0:T(8,128)(2,1)S(1)} %get-tuple-element.92), channel_id=1, source_target_pairs={{0,4},{1,5},{2,6},{3,7},{4,0},{5,1},{6,2},{7,3},{8,12},{9,13},{10,... | collective-permute-start | bytes 294920 | tf_op jit(solution)/shard_map/ppermute | solution.py:363
  69.3 8.2 %collective-permute-start.25 = (bf16[192,256]{1,0:T(8,128)(2,1)S(1)}, bf16[192,256]{1,0:T(8,128)(2,1)S(1)}, u32[]{:S(2)}, u32[]{:S(2)}) collective-permute-start(bf16[192,256]{1,0:T(8,128)(2,1)S(1)} %fusion.3), channel_id=1, source_target_pairs={{0,8},{1,9},{2,10},{3,11},{4,12},{5,13},{6,14},{7,15},{8,0},{9,1},... | collective-permute-start | bytes 294920 | tf_op jit(solution)/shard_map/ppermute | solution.py:363
  69.8 4.6 %collective-permute-start.22 = (bf16[192,256]{1,0:T(8,128)(2,1)S(1)}, bf16[192,256]{1,0:T(8,128)(2,1)S(1)}, u32[]{:S(2)}, u32[]{:S(2)}) collective-permute-start(bf16[192,256]{1,0:T(8,128)(2,1)S(1)} %get-tuple-element.77), channel_id=1, source_target_pairs={{0,2},{1,3},{2,0},{3,1},{4,6},{5,7},{6,4},{7,5},{8,10},{9,11},{10,... | collective-permute-start | bytes 294920 | tf_op jit(solution)/shard_map/ppermute | solution.py:363
  72.4 6.6 %collective-permute-start.31 = (bf16[192,256]{1,0:T(8,128)(2,1)S(1)}, bf16[192,256]{1,0:T(8,128)(2,1)S(1)}, u32[]{:S(2)}, u32[]{:S(2)}) collective-permute-start(bf16[192,256]{1,0:T(8,128)(2,1)S(1)} %fusion.1), channel_id=1, source_target_pairs={{0,12},{1,13},{2,14},{3,15},{4,8},{5,9},{6,10},{7,11},{8,4},{9,5},... | collective-permute-start | bytes 294920 | tf_op jit(solution)/shard_map/ppermute | solution.py:363

commit v13 on v12

--- a/solution.py
+++ b/solution.py
@@ -414,12 +414,6 @@
     def sum_cores(keep, give):
         return keep + hop(give, 0, 1).astype(F32)
 
-    def sum_slices(summed):
-        total = summed[0]
-        for j in range(1, pairs):
-            total += hop(summed[j].astype(BF16), 0, 2 * j).astype(F32)
-        return total.astype(BF16)
-
     def send_home(k, summed, wait=None):
         parts = [summed[j].astype(BF16) for j in range(pairs)]
         if wait is not None:
@@ -433,32 +427,48 @@
         if sends:
             give = after(give, arrived[groups - 1])
         own_sum, wait = sum_cores(keep, give), None
-        earlier = own_sum
+        earlier = [own_sum]
+        crossing, started, relays = {}, None, {}
+        for k in sends:
+            pieces, places = [arrived[k]], [0]
+            for bit in bits[:-1] if k in far else []:
+                pieces = pieces + [hop(piece, 0, bit) for piece in pieces]
+                places = places + [index ^ bit for index in places]
+            relays[k] = pieces, places
+            if k in far:
+                earlier.append(pieces[-1])
         turns = [[k for k in sends if k < groups - 1], [groups - 1]] if groups > 2 else [sends]
         for turn in turns:
             blocks, orders = [], []
             for k in turn:
-                pieces, places = [arrived[k]], [0]
-                for bit in bits if k in far else [1]:
-                    if bit == 1 and wait is not None:
-                        pieces = [after(piece, earlier) for piece in pieces]
-                    pieces = pieces + [hop(piece, 0, bit) for piece in pieces]
-                    places = places + [index ^ bit for index in places]
+                pieces, places = relays[k]
+                if started is not None:
+                    pieces = [after(piece, started) for piece in pieces]
+                pieces = pieces + [hop(piece, 0, 1) for piece in pieces]
+                places = places + [index ^ 1 for index in places]
                 blocks.append(pieces)
                 orders.append(places)
             if turn:
-                blocks[0][0] = after(blocks[0][0], earlier)
+                for value in earlier:
+                    blocks[0][0] = after(blocks[0][0], value)
                 keep, give = expert(orders, blocks)
-                earlier = give
                 summed = sum_cores(keep, give)
+                earlier, started = [summed], give
                 for i, k in enumerate(turn):
                     rows = summed[:, i * slots : (i + 1) * slots]
                     if k in far:
-                        total = sum_slices(rows)
-                        wait = total if wait is None else wait
-                        home[k] = [hop(total, k, 0)]
+                        crossed = [hop(rows[j].astype(BF16), 0, 2 * j) for j in range(1, pairs)]
+                        crossing[k] = [rows[0]] + crossed
                     else:
-                        home[k] = send_home(k, rows)
+                        near = k, rows
+        for k, (total, *crossed) in crossing.items():
+            for part in crossed:
+                total += (part if k == groups - 1 else after(part, summed)).astype(F32)
+            total = total.astype(BF16)
+            wait = total if wait is None else wait
+            home[k] = [hop(total, k, 0)]
+        if sends:
+            home[near[0]] = send_home(near[0], after(near[1], give))
         home[0] = send_home(0, own_sum, wait)
         order = [0] + sorted(sends)
     else:

time: 80.1 us -> 78.4 us (0.979)
  waiting for transfers between devices: 32.9 us -> 30.9 us
    ppermute x32, waiting for transfers between devices: 32.9 us -> 30.9 us  [hop(): return lax.ppermute(value, ('expert', 'mp'), moves)]
  transfers between devices with their start and end apart: 32 -> 32, of which waited for: 16 -> 15; matrix products, arithmetic and copies ran while one was open for 0% -> 0% of each run, Pallas kernels for 14% -> 11%
where the time goes in v13:
time: 78.4 us; the launch traced here: 78.2 us
  starting transfers between devices  33.3 us (42%)
  waiting for transfers between devices  30.9 us (39%)
  Pallas kernels  12.7 us (16%)
  between operations  1 us (1%)
    ppermute x32, starting transfers between devices, hop(): return lax.ppermute(value, ('expert', 'mp'), moves)  33.3 us
    ppermute x32, waiting for transfers between devices, hop(): return lax.ppermute(value, ('expert', 'mp'), moves)  30.9 us
    pallas_call x3, Pallas kernels, run_expert(): pl.pallas_call(functools.partial(expert_kernel, tuple(map(tuple, orders))...  3.88 us
    pallas_call x4, Pallas kernels, attend(): pl.pallas_call(attend_kernel, in_specs=[WHOLE] * 2, out_specs=WHOLE, out_...  2.8 us
    pallas_call x1, Pallas kernels, ask(): pl.pallas_call(query_kernel, in_specs=[pl.BlockSpec(memory_space=pltpu.HB...  1.81 us
    pallas_call x4, Pallas kernels, combine(): pl.pallas_call(functools.partial(combine_kernel, len(parts)), in_specs=[W...  1.59 us
  transfers between devices with their start and end apart: 32, of which 15 were waited for; matrix products, arithmetic and copies ran while one was open for 0% of the time, Pallas kernels for 11%

profile of v13, /device:TPU:0, one launch (start us, length us, event | category | flops | bytes accessed | tf_op | source)
XLA Modules:
  0.0 78.2 jit_solution(14933797216210091695)
XLA Ops:
  0.0 2.9 %collective-permute-start.9 = (bf16[256,1024]{1,0:T(8,128)(2,1)}, bf16[256,1024]{1,0:T(8,128)(2,1)S(1)}, u32[]{:S(2)}, u32[]{:S(2)}) collective-permute-start(bf16[256,1024]{1,0:T(8,128)(2,1)} %refs_5_), channel_id=1, source_target_pairs={{0,2},{1,3},{2,0},{3,1},{4,6},{5,7},{6,4},{7,5},{8,10},{9,11},{10,... | collective-permute-start | bytes 1572872 | tf_op jit(solution)/shard_map/ppermute | solution.py:363
  2.9 1.8 %query.1 = (bf16[256,256]{1,0:T(8,128)(2,1)S(1)}, bf16[2,512,256]{2,1,0:T(8,128)(2,1)S(1)}) custom-call(bf16[256,1024]{1,0:T(8,128)(2,1)} %refs_0_.1, bf16[1024,256]{1,0:T(8,128)(2,1)} %weight.1, bf16[2,512,256]{2,1,0:T(8,128)(2,1)} %bitcast.39), custom_call_target="tpu_custom_call" | custom-call | tf_op jit(solution)/shard_map/query/pallas_call | solution.py:65
  4.8 0.0 copy-start.3
  4.8 0.0 copy-start.5
  4.8 0.0 copy-start.2
  4.8 2.6 %collective-permute-start.1 = (bf16[256,256]{1,0:T(8,128)(2,1)S(1)}, bf16[256,256]{1,0:T(8,128)(2,1)S(1)}, u32[]{:S(2)}, u32[]{:S(2)}) collective-permute-start(bf16[256,256]{1,0:T(8,128)(2,1)S(1)} %get-tuple-element.51.queries), channel_id=1, source_target_pairs={{0,8},{1,9},{2,10},{3,11},{4,12},{5,13},{6,14},{7,15},{8,0},{9,1},... | collective-permute-start | bytes 393224 | tf_op jit(solution)/shard_map/ppermute | solution.py:363
  7.4 1.6 %collective-permute-start = (bf16[256,256]{1,0:T(8,128)(2,1)S(1)}, bf16[256,256]{1,0:T(8,128)(2,1)S(1)}, u32[]{:S(2)}, u32[]{:S(2)}) collective-permute-start(bf16[256,256]{1,0:T(8,128)(2,1)S(1)} %get-tuple-element.51.queries), channel_id=1, source_target_pairs={{0,4},{1,5},{2,6},{3,7},{4,0},{5,1},{6,2},{7,3},{8,12},{9,13},{10,... | collective-permute-start | bytes 393224 | tf_op jit(solution)/shard_map/ppermute | solution.py:363
  9.0 0.7 attend.4.refs_0_
  9.7 3.9 %collective-permute-done.1.queries = bf16[256,256]{1,0:T(8,128)(2,1)S(1)} collective-permute-done((bf16[256,256]{1,0:T(8,128)(2,1)S(1)}, bf16[256,256]{1,0:T(8,128)(2,1)S(1)}, u32[]{:S(2)}, u32[]{:S(2)}) %collective-permute-start.1) | collective-permute-done | bytes 131104 | tf_op jit(solution)/shard_map/ppermute | solution.py:363
  13.6 0.6 collective-permute-start.4
  14.2 0.7 attend.5
  14.9 3.4 %collective-permute-start.3 = (bf16[256,256]{1,0:T(8,128)(2,1)S(1)}, bf16[256,256]{1,0:T(8,128)(2,1)S(1)}, u32[]{:S(2)}, u32[]{:S(2)}) collective-permute-start(bf16[256,256]{1,0:T(8,128)(2,1)S(1)} %attend.5), channel_id=1, source_target_pairs={{0,8},{1,9},{2,10},{3,11},{4,12},{5,13},{6,14},{7,15},{8,0},{9,1},... | collective-permute-start | bytes 393224 | tf_op jit(solution)/shard_map/ppermute | solution.py:363
  18.4 0.7 attend.6
  19.1 0.1 collective-permute-start.2
  19.1 0.7 attend.7
  19.9 0.0 copy-start.4
  19.9 5.9 %collective-permute-start.5 = (bf16[256,256]{1,0:T(8,128)(2,1)S(1)}, bf16[256,256]{1,0:T(8,128)(2,1)S(1)}, u32[]{:S(2)}, u32[]{:S(2)}) collective-permute-start(bf16[256,256]{1,0:T(8,128)(2,1)S(1)} %attend.7), channel_id=1, source_target_pairs={{0,12},{1,13},{2,14},{3,15},{4,8},{5,9},{6,10},{7,11},{8,4},{9,5},... | collective-permute-start | bytes 393224 | tf_op jit(solution)/shard_map/ppermute | solution.py:363
  26.4 2.8 %collective-permute-done.5.refs_3_ = bf16[256,256]{1,0:T(8,128)(2,1)S(1)} collective-permute-done((bf16[256,256]{1,0:T(8,128)(2,1)S(1)}, bf16[256,256]{1,0:T(8,128)(2,1)S(1)}, u32[]{:S(2)}, u32[]{:S(2)}) %collective-permute-start.5) | collective-permute-done | bytes 131104 | tf_op jit(solution)/shard_map/ppermute | solution.py:363
  29.3 0.1 pick.1.refs_1_
  29.4 0.1 collective-permute-start.10
  29.5 0.5 collective-permute-start.11
  30.0 0.5 collective-permute-start.6
  30.6 1.0 %route.1 = (s32[256,2]{1,0:T(8,128)S(1)}, bf16[192,256]{1,0:T(8,128)(2,1)S(1)}, bf16[192,256]{1,0:T(8,128)(2,1)S(1)}, bf16[192,256]{1,0:T(8,128)(2,1)S(1)}, bf16...) custom-call(s32[2,256]{1,0:T(2,128)S(1)} %bitcast.38), custom_call_target="tpu_custom_call" | custom-call | tf_op jit(solution)/shard_map/route/pallas_call | solution.py:177
  31.5 0.1 collective-permute-start.7
  31.6 3.9 %collective-permute-done.6.refs_2_ = bf16[256,256]{1,0:T(8,128)(2,1)S(1)} collective-permute-done((bf16[256,256]{1,0:T(8,128)(2,1)S(1)}, bf16[256,256]{1,0:T(8,128)(2,1)S(1)}, u32[]{:S(2)}, u32[]{:S(2)}) %collective-permute-start.6) | collective-permute-done | bytes 131104 | tf_op jit(solution)/shard_map/ppermute | solution.py:363
  35.5 1.3 %collective-permute-done.8.refs_4_ = bf16[256,256]{1,0:T(8,128)(2,1)S(1)} collective-permute-done((bf16[256,256]{1,0:T(8,128)(2,1)S(1)}, bf16[256,256]{1,0:T(8,128)(2,1)S(1)}, u32[]{:S(2)}, u32[]{:S(2)}) %collective-permute-start.8) | collective-permute-done | bytes 131104 | tf_op jit(solution)/shard_map/ppermute | solution.py:363
  36.9 1.0 %state.1 = (bf16[256,1024]{1,0:T(8,128)(2,1)S(1)}, bf16[192,256]{1,0:T(8,128)(2,1)S(1)}, bf16[192,256]{1,0:T(8,128)(2,1)S(1)}, bf16[192,512]{1,0:T(8,128)(2,1)S(1)}) custom-call(bf16[256,1024]{1,0:T(8,128)(2,1)S(1)} %copy-done.2, bf16[256,256]{1,0:T(8,128)(2,1)S(1)} %pick.1.refs_1_, bf16[256,256]{1,0:T(8,128)(2,1)S(1)} %collective-permute-done.6.refs_2_, ...), custom_call_target="tpu_custom_call" | custom-call | tf_op jit(solution)/shard_map/state/pallas_call | solution.py:210
  37.9 3.4 %collective-permute-start.12 = (bf16[192,256]{1,0:T(8,128)(2,1)S(1)}, bf16[192,256]{1,0:T(8,128)(2,1)S(1)}, u32[]{:S(2)}, u32[]{:S(2)}) collective-permute-start(bf16[192,256]{1,0:T(8,128)(2,1)S(1)} %get-tuple-element.74), channel_id=1, source_target_pairs={{0,12},{1,13},{2,14},{3,15},{4,8},{5,9},{6,10},{7,11},{8,4},{9,5},... | collective-permute-start | bytes 294920 | tf_op jit(solution)/shard_map/ppermute | solution.py:363
  41.2 1.1 %collective-permute-start.19 = (bf16[192,512]{1,0:T(8,128)(2,1)S(1)}, bf16[192,512]{1,0:T(8,128)(2,1)S(1)}, u32[]{:S(2)}, u32[]{:S(2)}) collective-permute-start(bf16[192,512]{1,0:T(8,128)(2,1)S(1)} %get-tuple-element.80), channel_id=1, source_target_pairs={{0,4},{1,5},{2,6},{3,7},{4,0},{5,1},{6,2},{7,3},{8,12},{9,13},{10,... | collective-permute-start | bytes 589832 | tf_op jit(solution)/shard_map/ppermute | solution.py:363
  42.3 0.5 home.1
  42.9 1.0 %expert.3 = (f32[2,192,256]{2,1,0:T(8,128)S(1)}, bf16[2,192,256]{2,1,0:T(8,128)(2,1)S(1)}) custom-call(bf16[192,512]{1,0:T(8,128)(2,1)S(1)} %get-tuple-element.70.refs_0_, bf16[192,512]{1,0:T(8,128)(2,1)S(1)} %get-tuple-element.71.refs_1_, bf16[1024,1024]{1,0:T(8,128)(2,1)S(1)} %bitcast.31, bf16[1024,1024]{1,0:T(8,128)(2,1)S(1)} %bitcast.34), custom_call_target="tpu_custom_call" | custom-call | tf_op jit(solution)/shard_map/expert/pallas_call | solution.py:289
  43.9 1.6 %collective-permute-done.12.refs_0_ = bf16[192,256]{1,0:T(8,128)(2,1)S(1)} collective-permute-done((bf16[192,256]{1,0:T(8,128)(2,1)S(1)}, bf16[192,256]{1,0:T(8,128)(2,1)S(1)}, u32[]{:S(2)}, u32[]{:S(2)}) %collective-permute-start.12) | collective-permute-done | bytes 98336 | tf_op jit(solution)/shard_map/ppermute | solution.py:363
  45.5 4.6 %collective-permute-done.14.refs_0_ = bf16[192,256]{1,0:T(8,128)(2,1)S(1)} collective-permute-done((bf16[192,256]{1,0:T(8,128)(2,1)S(1)}, bf16[192,256]{1,0:T(8,128)(2,1)S(1)}, u32[]{:S(2)}, u32[]{:S(2)}) %collective-permute-start.14) | collective-permute-done | bytes 98336 | tf_op jit(solution)/shard_map/ppermute | solution.py:363
  50.1 0.5 collective-permute-start.15
  50.7 1.5 %collective-permute-start.16 = (bf16[192,256]{1,0:T(8,128)(2,1)S(1)}, bf16[192,256]{1,0:T(8,128)(2,1)S(1)}, u32[]{:S(2)}, u32[]{:S(2)}) collective-permute-start(bf16[192,256]{1,0:T(8,128)(2,1)S(1)} %collective-permute-done.12.refs_0_), channel_id=1, source_target_pairs={{0,2},{1,3},{2,0},{3,1},{4,6},{5,7},{6,4},{7,5},{8,10},{9,11},{10,... | collective-permute-start | bytes 294920 | tf_op jit(solution)/shard_map/ppermute | solution.py:363
  52.1 0.5 collective-permute-start.20
  52.6 2.4 %collective-permute-done.15.refs_1_ = bf16[192,256]{1,0:T(8,128)(2,1)S(1)} collective-permute-done((bf16[192,256]{1,0:T(8,128)(2,1)S(1)}, bf16[192,256]{1,0:T(8,128)(2,1)S(1)}, u32[]{:S(2)}, u32[]{:S(2)}) %collective-permute-start.15) | collective-permute-done | bytes 98336 | tf_op jit(solution)/shard_map/ppermute | solution.py:363
  55.1 0.1 convert_add_fusion.2
  55.1 1.0 %collective-permute-done.16.refs_1_ = bf16[192,256]{1,0:T(8,128)(2,1)S(1)} collective-permute-done((bf16[192,256]{1,0:T(8,128)(2,1)S(1)}, bf16[192,256]{1,0:T(8,128)(2,1)S(1)}, u32[]{:S(2)}, u32[]{:S(2)}) %collective-permute-start.16) | collective-permute-done | bytes 98336 | tf_op jit(solution)/shard_map/ppermute | solution.py:363
  56.1 0.2 collective-permute-done.18.refs_3_
  56.4 1.9 %expert.4 = (f32[2,384,256]{2,1,0:T(8,128)S(1)}, bf16[2,384,256]{2,1,0:T(8,128)(2,1)S(1)}) custom-call(bf16[192,256]{1,0:T(8,128)(2,1)S(1)} %collective-permute-done.14.refs_0_, bf16[192,256]{1,0:T(8,128)(2,1)S(1)} %collective-permute-done.15.refs_1_, bf16[192,256]{1,0:T(8,128)(2,1)S(1)} %collective-permute-done.17.refs_2_, ...), custom_call_target="tpu_custom_call" | custom-call | tf_op jit(solution)/shard_map/expert/pallas_call | solution.py:289
  58.2 0.2 collective-permute-start.21
  58.5 0.4 collective-permute-start.23
  58.9 0.2 collective-permute-start.24
  59.1 1.0 %collective-permute-done.21 = bf16[2,384,256]{2,1,0:T(8,128)(2,1)S(1)} collective-permute-done((bf16[2,384,256]{2,1,0:T(8,128)(2,1)S(1)}, bf16[2,384,256]{2,1,0:T(8,128)(2,1)S(1)}, u32[]{:S(2)}, u32[]{:S(2)}) %collective-permute-start.21) | collective-permute-done | bytes 393248 | tf_op jit(solution)/shard_map/ppermute | solution.py:363
  60.0 0.1 convert_add_fusion
  60.2 0.8 collective-permute-start.22
  61.0 1.0 %expert.5 = (f32[2,192,256]{2,1,0:T(8,128)S(1)}, bf16[2,192,256]{2,1,0:T(8,128)(2,1)S(1)}) custom-call(bf16[192,256]{1,0:T(8,128)(2,1)S(1)} %collective-permute-done.12.refs_0_, bf16[192,256]{1,0:T(8,128)(2,1)S(1)} %collective-permute-done.16.refs_1_, bf16[192,256]{1,0:T(8,128)(2,1)S(1)} %collective-permute-done.23.refs_2_, ...), custom_call_target="tpu_custom_call" | custom-call | tf_op jit(solution)/shard_map/expert/pallas_call | solution.py:289
  62.0 0.1 collective-permute-start.25
  62.1 1.0 %collective-permute-start.28 = (bf16[192,256]{1,0:T(8,128)(2,1)S(1)}, bf16[192,256]{1,0:T(8,128)(2,1)S(1)}, u32[]{:S(2)}, u32[]{:S(2)}) collective-permute-start(bf16[192,256]{1,0:T(8,128)(2,1)S(1)} %get-tuple-element.97), channel_id=1, source_target_pairs={{0,6},{1,7},{2,4},{3,5},{4,2},{5,3},{6,0},{7,1},{8,14},{9,15},{10,... | collective-permute-start | bytes 294920 | tf_op jit(solution)/shard_map/ppermute | solution.py:363
  63.1 1.8 %collective-permute-start.27 = (bf16[192,256]{1,0:T(8,128)(2,1)S(1)}, bf16[192,256]{1,0:T(8,128)(2,1)S(1)}, u32[]{:S(2)}, u32[]{:S(2)}) collective-permute-start(bf16[192,256]{1,0:T(8,128)(2,1)S(1)} %get-tuple-element.98), channel_id=1, source_target_pairs={{0,4},{1,5},{2,6},{3,7},{4,0},{5,1},{6,2},{7,3},{8,12},{9,13},{10,... | collective-permute-start | bytes 294920 | tf_op jit(solution)/shard_map/ppermute | solution.py:363
  65.0 0.1 collective-permute-done.22
  65.1 0.7 collective-permute-start.30
  65.8 0.1 collective-permute-start.29
  65.9 1.4 %collective-permute-start.26 = (bf16[192,256]{1,0:T(8,128)(2,1)S(1)}, bf16[192,256]{1,0:T(8,128)(2,1)S(1)}, u32[]{:S(2)}, u32[]{:S(2)}) collective-permute-start(bf16[192,256]{1,0:T(8,128)(2,1)S(1)} %get-tuple-element.89), channel_id=1, source_target_pairs={{0,2},{1,3},{2,0},{3,1},{4,6},{5,7},{6,4},{7,5},{8,10},{9,11},{10,... | collective-permute-start | bytes 294920 | tf_op jit(solution)/shard_map/ppermute | solution.py:363
  67.3 3.5 %collective-permute-done.30 = bf16[192,256]{1,0:T(8,128)(2,1)S(1)} collective-permute-done((bf16[192,256]{1,0:T(8,128)(2,1)S(1)}, bf16[192,256]{1,0:T(8,128)(2,1)S(1)}, u32[]{:S(2)}, u32[]{:S(2)}) %collective-permute-start.30) | collective-permute-done | bytes 98336 | tf_op jit(solution)/shard_map/ppermute | solution.py:363
  70.8 1.3 %collective-permute-start.31 = (bf16[192,256]{1,0:T(8,128)(2,1)S(1)}, bf16[192,256]{1,0:T(8,128)(2,1)S(1)}, u32[]{:S(2)}, u32[]{:S(2)}) collective-permute-start(bf16[192,256]{1,0:T(8,128)(2,1)S(1)} %fusion.1), channel_id=1, source_target_pairs={{0,12},{1,13},{2,14},{3,15},{4,8},{5,9},{6,10},{7,11},{8,4},{9,5},... | collective-permute-start | bytes 294920 | tf_op jit(solution)/shard_map/ppermute | solution.py:363
  72.1 0.3 collective-permute-done.26.refs_1_
  72.5 0.2 combine.4.base
  72.7 0.2 combine.5.base
  73.0 0.6 collective-permute-done.29.refs_0_
  73.5 0.2 combine.6.base
  73.8 3.5 %collective-permute-done.31.refs_0_ = bf16[192,256]{1,0:T(8,128)(2,1)S(1)} collective-permute-done((bf16[192,256]{1,0:T(8,128)(2,1)S(1)}, bf16[192,256]{1,0:T(8,128)(2,1)S(1)}, u32[]{:S(2)}, u32[]{:S(2)}) %collective-permute-start.31) | collective-permute-done | bytes 98336 | tf_op jit(solution)/shard_map/ppermute | solution.py:363
  77.3 0.9 %combine.7 = bf16[256,256]{1,0:T(8,128)(2,1)} custom-call(f32[256,2]{1,0:T(8,128)S(1)} %get-tuple-element.66.gates, f32[256,256]{1,0:T(8,128)S(1)} %combine.6.base, bf16[256,192]{1,0:T(8,128)(2,1)S(1)} %get-tuple-element.95.first, bf16[256,192]{1,0:T(8,128)(2,1)S(1)} %get-tuple-element.96.second, bf16[192,256]{1,0:T(8,128)(2,1)S(1)} %collective-permute-done.31.refs_0_), custom_call_target="tpu_custom_call" | custom-call | tf_op jit(solution)/shard_map/combine/pallas_call | solution.py:315
  (38 shorter events, 0.2 us)
Async XLA Ops:
  0.0 29.5 %collective-permute-start.9 = (bf16[256,1024]{1,0:T(8,128)(2,1)}, bf16[256,1024]{1,0:T(8,128)(2,1)S(1)}, u32[]{:S(2)}, u32[]{:S(2)}) collective-permute-start(bf16[256,1024]{1,0:T(8,128)(2,1)} %refs_5_), channel_id=1, source_target_pairs={{0,2},{1,3},{2,0},{3,1},{4,6},{5,7},{6,4},{7,5},{8,10},{9,11},{10,... | collective-permute-start | bytes 1572872 | tf_op jit(solution)/shard_map/ppermute | solution.py:363
  4.8 24.7 %copy-start.3 = (bf16[256,1024]{1,0:T(8,128)(2,1)S(1)}, bf16[256,1024]{1,0:T(8,128)(2,1)}, u32[]{:S(2)}) copy-start(bf16[256,1024]{1,0:T(8,128)(2,1)} %refs_5_) | copy-start | bytes 1572868
  4.8 25.8 %copy-start.5 = (s32[256,2]{0,1:T(2,128)S(1)}, s32[256,2]{0,1:T(2,128)}, u32[]{:S(2)}) copy-start(s32[256,2]{0,1:T(2,128)} %param.15) | copy-start | bytes 6148
  4.8 32.1 %copy-start.2 = (bf16[256,1024]{1,0:T(8,128)(2,1)S(1)}, bf16[256,1024]{1,0:T(8,128)(2,1)}, u32[]{:S(2)}) copy-start(bf16[256,1024]{1,0:T(8,128)(2,1)} %refs_0_.1) | copy-start | bytes 1572868
  4.8 8.8 %collective-permute-start.1 = (bf16[256,256]{1,0:T(8,128)(2,1)S(1)}, bf16[256,256]{1,0:T(8,128)(2,1)S(1)}, u32[]{:S(2)}, u32[]{:S(2)}) collective-permute-start(bf16[256,256]{1,0:T(8,128)(2,1)S(1)} %get-tuple-element.51.queries), channel_id=1, source_target_pairs={{0,8},{1,9},{2,10},{3,11},{4,12},{5,13},{6,14},{7,15},{8,0},{9,1},... | collective-permute-start | bytes 393224 | tf_op jit(solution)/shard_map/ppermute | solution.py:363
  7.4 10.9 %collective-permute-start = (bf16[256,256]{1,0:T(8,128)(2,1)S(1)}, bf16[256,256]{1,0:T(8,128)(2,1)S(1)}, u32[]{:S(2)}, u32[]{:S(2)}) collective-permute-start(bf16[256,256]{1,0:T(8,128)(2,1)S(1)} %get-tuple-element.51.queries), channel_id=1, source_target_pairs={{0,4},{1,5},{2,6},{3,7},{4,0},{5,1},{6,2},{7,3},{8,12},{9,13},{10,... | collective-permute-start | bytes 393224 | tf_op jit(solution)/shard_map/ppermute | solution.py:363
  13.6 5.5 %collective-permute-start.4 = (bf16[256,256]{1,0:T(8,128)(2,1)S(1)}, bf16[256,256]{1,0:T(8,128)(2,1)S(1)}, u32[]{:S(2)}, u32[]{:S(2)}) collective-permute-start(bf16[256,256]{1,0:T(8,128)(2,1)S(1)} %collective-permute-done.1.queries), channel_id=1, source_target_pairs={{0,4},{1,5},{2,6},{3,7},{4,0},{5,1},{6,2},{7,3},{8,12},{9,13},{10,... | collective-permute-start | bytes 393224 | tf_op jit(solution)/shard_map/ppermute | solution.py:363
  14.9 11.5 %collective-permute-start.3 = (bf16[256,256]{1,0:T(8,128)(2,1)S(1)}, bf16[256,256]{1,0:T(8,128)(2,1)S(1)}, u32[]{:S(2)}, u32[]{:S(2)}) collective-permute-start(bf16[256,256]{1,0:T(8,128)(2,1)S(1)} %attend.5), channel_id=1, source_target_pairs={{0,8},{1,9},{2,10},{3,11},{4,12},{5,13},{6,14},{7,15},{8,0},{9,1},... | collective-permute-start | bytes 393224 | tf_op jit(solution)/shard_map/ppermute | solution.py:363
  19.1 7.4 %collective-permute-start.2 = (bf16[256,256]{1,0:T(8,128)(2,1)S(1)}, bf16[256,256]{1,0:T(8,128)(2,1)S(1)}, u32[]{:S(2)}, u32[]{:S(2)}) collective-permute-start(bf16[256,256]{1,0:T(8,128)(2,1)S(1)} %attend.6), channel_id=1, source_target_pairs={{0,4},{1,5},{2,6},{3,7},{4,0},{5,1},{6,2},{7,3},{8,12},{9,13},{10,... | collective-permute-start | bytes 393224 | tf_op jit(solution)/shard_map/ppermute | solution.py:363
  19.9 22.5 %copy-start.4 = (bf16[1024,4]{0,1:T(4,128)(2,1)S(1)}, bf16[1024,4]{0,1:T(4,128)(2,1)}, u32[]{:S(2)}) copy-start(bf16[1024,4]{0,1:T(4,128)(2,1)} %param.14) | copy-start | bytes 24580
  19.9 9.4 %collective-permute-start.5 = (bf16[256,256]{1,0:T(8,128)(2,1)S(1)}, bf16[256,256]{1,0:T(8,128)(2,1)S(1)}, u32[]{:S(2)}, u32[]{:S(2)}) collective-permute-start(bf16[256,256]{1,0:T(8,128)(2,1)S(1)} %attend.7), channel_id=1, source_target_pairs={{0,12},{1,13},{2,14},{3,15},{4,8},{5,9},{6,10},{7,11},{8,4},{9,5},... | collective-permute-start | bytes 393224 | tf_op jit(solution)/shard_map/ppermute | solution.py:363
  29.4 7.4 %collective-permute-start.10 = (bf16[256,1024]{1,0:T(8,128)(2,1)S(1)}, bf16[256,1024]{1,0:T(8,128)(2,1)S(1)}, u32[]{:S(2)}, u32[]{:S(2)}) collective-permute-start(bf16[256,1024]{1,0:T(8,128)(2,1)S(1)} %copy-done.3), channel_id=1, source_target_pairs={{0,1},{1,0},{2,3},{3,2},{4,5},{5,4},{6,7},{7,6},{8,9},{9,8},{10,11... | collective-permute-start | bytes 1572872 | tf_op jit(solution)/shard_map/ppermute | solution.py:363
  29.5 7.3 %collective-permute-start.11 = (bf16[256,1024]{1,0:T(8,128)(2,1)S(1)}, bf16[256,1024]{1,0:T(8,128)(2,1)S(1)}, u32[]{:S(2)}, u32[]{:S(2)}) collective-permute-start(bf16[256,1024]{1,0:T(8,128)(2,1)S(1)} %collective-permute-done.9.refs_6_), channel_id=1, source_target_pairs={{0,1},{1,0},{2,3},{3,2},{4,5},{5,4},{6,7},{7,6},{8,9},{9,8},{10,11... | collective-permute-start | bytes 1572872 | tf_op jit(solution)/shard_map/ppermute | solution.py:363
  30.0 5.5 %collective-permute-start.6 = (bf16[256,256]{1,0:T(8,128)(2,1)S(1)}, bf16[256,256]{1,0:T(8,128)(2,1)S(1)}, u32[]{:S(2)}, u32[]{:S(2)}) collective-permute-start(bf16[256,256]{1,0:T(8,128)(2,1)S(1)} %pick.1.refs_1_), channel_id=1, source_target_pairs={{0,2},{1,3},{2,0},{3,1},{4,6},{5,7},{6,4},{7,5},{8,10},{9,11},{10,... | collective-permute-start | bytes 393224 | tf_op jit(solution)/shard_map/ppermute | solution.py:363
  31.5 4.0 %collective-permute-start.7 = (bf16[256,256]{1,0:T(8,128)(2,1)S(1)}, bf16[256,256]{1,0:T(8,128)(2,1)S(1)}, u32[]{:S(2)}, u32[]{:S(2)}) collective-permute-start(bf16[256,256]{1,0:T(8,128)(2,1)S(1)} %pick.1.refs_1_), channel_id=1, source_target_pairs={{0,1},{1,0},{2,3},{3,2},{4,5},{5,4},{6,7},{7,6},{8,9},{9,8},{10,11... | collective-permute-start | bytes 393224 | tf_op jit(solution)/shard_map/ppermute | solution.py:363
  35.5 1.3 %collective-permute-start.8 = (bf16[256,256]{1,0:T(8,128)(2,1)S(1)}, bf16[256,256]{1,0:T(8,128)(2,1)S(1)}, u32[]{:S(2)}, u32[]{:S(2)}) collective-permute-start(bf16[256,256]{1,0:T(8,128)(2,1)S(1)} %collective-permute-done.6.refs_2_), channel_id=1, source_target_pairs={{0,1},{1,0},{2,3},{3,2},{4,5},{5,4},{6,7},{7,6},{8,9},{9,8},{10,11... | collective-permute-start | bytes 393224 | tf_op jit(solution)/shard_map/ppermute | solution.py:363
  36.9 6.0 %copy-start = (bf16[1,1024,1024]{2,1,0:T(8,128)(2,1)S(1)}, bf16[1,1024,1024]{2,1,0:T(8,128)(2,1)}, u32[]{:S(2)}) copy-start(bf16[1,1024,1024]{2,1,0:T(8,128)(2,1)} %param.16) | copy-start | bytes 6291460
  36.9 6.0 %copy-start.1 = (bf16[1,1024,1024]{2,1,0:T(8,128)(2,1)S(1)}, bf16[1,1024,1024]{2,1,0:T(8,128)(2,1)}, u32[]{:S(2)}) copy-start(bf16[1,1024,1024]{2,1,0:T(8,128)(2,1)} %param.17) | copy-start | bytes 6291460
  37.9 7.6 %collective-permute-start.12 = (bf16[192,256]{1,0:T(8,128)(2,1)S(1)}, bf16[192,256]{1,0:T(8,128)(2,1)S(1)}, u32[]{:S(2)}, u32[]{:S(2)}) collective-permute-start(bf16[192,256]{1,0:T(8,128)(2,1)S(1)} %get-tuple-element.74), channel_id=1, source_target_pairs={{0,12},{1,13},{2,14},{3,15},{4,8},{5,9},{6,10},{7,11},{8,4},{9,5},... | collective-permute-start | bytes 294920 | tf_op jit(solution)/shard_map/ppermute | solution.py:363
  41.2 8.9 %collective-permute-start.14 = (bf16[192,256]{1,0:T(8,128)(2,1)S(1)}, bf16[192,256]{1,0:T(8,128)(2,1)S(1)}, u32[]{:S(2)}, u32[]{:S(2)}) collective-permute-start(bf16[192,256]{1,0:T(8,128)(2,1)S(1)} %get-tuple-element.76), channel_id=1, source_target_pairs={{0,8},{1,9},{2,10},{3,11},{4,12},{5,13},{6,14},{7,15},{8,0},{9,1},... | collective-permute-start | bytes 294920 | tf_op jit(solution)/shard_map/ppermute | solution.py:363
  41.2 10.9 %collective-permute-start.19 = (bf16[192,512]{1,0:T(8,128)(2,1)S(1)}, bf16[192,512]{1,0:T(8,128)(2,1)S(1)}, u32[]{:S(2)}, u32[]{:S(2)}) collective-permute-start(bf16[192,512]{1,0:T(8,128)(2,1)S(1)} %get-tuple-element.80), channel_id=1, source_target_pairs={{0,4},{1,5},{2,6},{3,7},{4,0},{5,1},{6,2},{7,3},{8,12},{9,13},{10,... | collective-permute-start | bytes 589832 | tf_op jit(solution)/shard_map/ppermute | solution.py:363
  45.5 9.6 %collective-permute-start.13 = (bf16[2,192,256]{2,1,0:T(8,128)(2,1)S(1)}, bf16[2,192,256]{2,1,0:T(8,128)(2,1)S(1)}, u32[]{:S(2)}, u32[]{:S(2)}) collective-permute-start(bf16[2,192,256]{2,1,0:T(8,128)(2,1)S(1)} %get-tuple-element.75), channel_id=1, source_target_pairs={{0,1},{1,0},{2,3},{3,2},{4,5},{5,4},{6,7},{7,6},{8,9},{9,8},{10,11... | collective-permute-start | bytes 589832 | tf_op jit(solution)/shard_map/ppermute | solution.py:363
  50.1 5.0 %collective-permute-start.15 = (bf16[192,256]{1,0:T(8,128)(2,1)S(1)}, bf16[192,256]{1,0:T(8,128)(2,1)S(1)}, u32[]{:S(2)}, u32[]{:S(2)}) collective-permute-start(bf16[192,256]{1,0:T(8,128)(2,1)S(1)} %collective-permute-done.14.refs_0_), channel_id=1, source_target_pairs={{0,2},{1,3},{2,0},{3,1},{4,6},{5,7},{6,4},{7,5},{8,10},{9,11},{10,... | collective-permute-start | bytes 294920 | tf_op jit(solution)/shard_map/ppermute | solution.py:363
  50.7 5.5 %collective-permute-start.16 = (bf16[192,256]{1,0:T(8,128)(2,1)S(1)}, bf16[192,256]{1,0:T(8,128)(2,1)S(1)}, u32[]{:S(2)}, u32[]{:S(2)}) collective-permute-start(bf16[192,256]{1,0:T(8,128)(2,1)S(1)} %collective-permute-done.12.refs_0_), channel_id=1, source_target_pairs={{0,2},{1,3},{2,0},{3,1},{4,6},{5,7},{6,4},{7,5},{8,10},{9,11},{10,... | collective-permute-start | bytes 294920 | tf_op jit(solution)/shard_map/ppermute | solution.py:363
  52.1 4.0 %collective-permute-start.17 = (bf16[192,256]{1,0:T(8,128)(2,1)S(1)}, bf16[192,256]{1,0:T(8,128)(2,1)S(1)}, u32[]{:S(2)}, u32[]{:S(2)}) collective-permute-start(bf16[192,256]{1,0:T(8,128)(2,1)S(1)} %collective-permute-done.14.refs_0_), channel_id=1, source_target_pairs={{0,1},{1,0},{2,3},{3,2},{4,5},{5,4},{6,7},{7,6},{8,9},{9,8},{10,11... | collective-permute-start | bytes 294920 | tf_op jit(solution)/shard_map/ppermute | solution.py:363
  52.1 4.2 %collective-permute-start.20 = (bf16[192,512]{1,0:T(8,128)(2,1)S(1)}, bf16[192,512]{1,0:T(8,128)(2,1)S(1)}, u32[]{:S(2)}, u32[]{:S(2)}) collective-permute-start(bf16[192,512]{1,0:T(8,128)(2,1)S(1)} %collective-permute-done.19.refs_4_), channel_id=1, source_target_pairs={{0,1},{1,0},{2,3},{3,2},{4,5},{5,4},{6,7},{7,6},{8,9},{9,8},{10,11... | collective-permute-start | bytes 589832 | tf_op jit(solution)/shard_map/ppermute | solution.py:363
  55.1 1.3 %collective-permute-start.18 = (bf16[192,256]{1,0:T(8,128)(2,1)S(1)}, bf16[192,256]{1,0:T(8,128)(2,1)S(1)}, u32[]{:S(2)}, u32[]{:S(2)}) collective-permute-start(bf16[192,256]{1,0:T(8,128)(2,1)S(1)} %collective-permute-done.15.refs_1_), channel_id=1, source_target_pairs={{0,1},{1,0},{2,3},{3,2},{4,5},{5,4},{6,7},{7,6},{8,9},{9,8},{10,11... | collective-permute-start | bytes 294920 | tf_op jit(solution)/shard_map/ppermute | solution.py:363
  58.2 1.8 %collective-permute-start.21 = (bf16[2,384,256]{2,1,0:T(8,128)(2,1)S(1)}, bf16[2,384,256]{2,1,0:T(8,128)(2,1)S(1)}, u32[]{:S(2)}, u32[]{:S(2)}) collective-permute-start(bf16[2,384,256]{2,1,0:T(8,128)(2,1)S(1)} %get-tuple-element.82), channel_id=1, source_target_pairs={{0,1},{1,0},{2,3},{3,2},{4,5},{5,4},{6,7},{7,6},{8,9},{9,8},{10,11... | collective-permute-start | bytes 1179656 | tf_op jit(solution)/shard_map/ppermute | solution.py:363
  58.5 2.5 %collective-permute-start.23 = (bf16[192,256]{1,0:T(8,128)(2,1)S(1)}, bf16[192,256]{1,0:T(8,128)(2,1)S(1)}, u32[]{:S(2)}, u32[]{:S(2)}) collective-permute-start(bf16[192,256]{1,0:T(8,128)(2,1)S(1)} %collective-permute-done.12.refs_0_), channel_id=1, source_target_pairs={{0,1},{1,0},{2,3},{3,2},{4,5},{5,4},{6,7},{7,6},{8,9},{9,8},{10,11... | collective-permute-start | bytes 294920 | tf_op jit(solution)/shard_map/ppermute | solution.py:363
  58.9 2.1 %collective-permute-start.24 = (bf16[192,256]{1,0:T(8,128)(2,1)S(1)}, bf16[192,256]{1,0:T(8,128)(2,1)S(1)}, u32[]{:S(2)}, u32[]{:S(2)}) collective-permute-start(bf16[192,256]{1,0:T(8,128)(2,1)S(1)} %collective-permute-done.16.refs_1_), channel_id=1, source_target_pairs={{0,1},{1,0},{2,3},{3,2},{4,5},{5,4},{6,7},{7,6},{8,9},{9,8},{10,11... | collective-permute-start | bytes 294920 | tf_op jit(solution)/shard_map/ppermute | solution.py:363
  60.2 4.9 %collective-permute-start.22 = (bf16[192,256]{1,0:T(8,128)(2,1)S(1)}, bf16[192,256]{1,0:T(8,128)(2,1)S(1)}, u32[]{:S(2)}, u32[]{:S(2)}) collective-permute-start(bf16[192,256]{1,0:T(8,128)(2,1)S(1)} %fusion.4), channel_id=1, source_target_pairs={{0,2},{1,3},{2,0},{3,1},{4,6},{5,7},{6,4},{7,5},{8,10},{9,11},{10,... | collective-permute-start | bytes 294920 | tf_op jit(solution)/shard_map/ppermute | solution.py:363
  62.0 2.9 %collective-permute-start.25 = (bf16[2,192,256]{2,1,0:T(8,128)(2,1)S(1)}, bf16[2,192,256]{2,1,0:T(8,128)(2,1)S(1)}, u32[]{:S(2)}, u32[]{:S(2)}) collective-permute-start(bf16[2,192,256]{2,1,0:T(8,128)(2,1)S(1)} %get-tuple-element.87), channel_id=1, source_target_pairs={{0,1},{1,0},{2,3},{3,2},{4,5},{5,4},{6,7},{7,6},{8,9},{9,8},{10,11... | collective-permute-start | bytes 589832 | tf_op jit(solution)/shard_map/ppermute | solution.py:363
  62.1 10.6 %collective-permute-start.28 = (bf16[192,256]{1,0:T(8,128)(2,1)S(1)}, bf16[192,256]{1,0:T(8,128)(2,1)S(1)}, u32[]{:S(2)}, u32[]{:S(2)}) collective-permute-start(bf16[192,256]{1,0:T(8,128)(2,1)S(1)} %get-tuple-element.97), channel_id=1, source_target_pairs={{0,6},{1,7},{2,4},{3,5},{4,2},{5,3},{6,0},{7,1},{8,14},{9,15},{10,... | collective-permute-start | bytes 294920 | tf_op jit(solution)/shard_map/ppermute | solution.py:363
  63.1 9.6 %collective-permute-start.27 = (bf16[192,256]{1,0:T(8,128)(2,1)S(1)}, bf16[192,256]{1,0:T(8,128)(2,1)S(1)}, u32[]{:S(2)}, u32[]{:S(2)}) collective-permute-start(bf16[192,256]{1,0:T(8,128)(2,1)S(1)} %get-tuple-element.98), channel_id=1, source_target_pairs={{0,4},{1,5},{2,6},{3,7},{4,0},{5,1},{6,2},{7,3},{8,12},{9,13},{10,... | collective-permute-start | bytes 294920 | tf_op jit(solution)/shard_map/ppermute | solution.py:363
  65.1 5.7 %collective-permute-start.30 = (bf16[192,256]{1,0:T(8,128)(2,1)S(1)}, bf16[192,256]{1,0:T(8,128)(2,1)S(1)}, u32[]{:S(2)}, u32[]{:S(2)}) collective-permute-start(bf16[192,256]{1,0:T(8,128)(2,1)S(1)} %fusion.5), channel_id=1, source_target_pairs={{0,2},{1,3},{2,0},{3,1},{4,6},{5,7},{6,4},{7,5},{8,10},{9,11},{10,... | collective-permute-start | bytes 294920 | tf_op jit(solution)/shard_map/ppermute | solution.py:363
  65.8 7.7 %collective-permute-start.29 = (bf16[192,256]{1,0:T(8,128)(2,1)S(1)}, bf16[192,256]{1,0:T(8,128)(2,1)S(1)}, u32[]{:S(2)}, u32[]{:S(2)}) collective-permute-start(bf16[192,256]{1,0:T(8,128)(2,1)S(1)} %fusion.3), channel_id=1, source_target_pairs={{0,8},{1,9},{2,10},{3,11},{4,12},{5,13},{6,14},{7,15},{8,0},{9,1},... | collective-permute-start | bytes 294920 | tf_op jit(solution)/shard_map/ppermute | solution.py:363
  65.9 6.5 %collective-permute-start.26 = (bf16[192,256]{1,0:T(8,128)(2,1)S(1)}, bf16[192,256]{1,0:T(8,128)(2,1)S(1)}, u32[]{:S(2)}, u32[]{:S(2)}) collective-permute-start(bf16[192,256]{1,0:T(8,128)(2,1)S(1)} %get-tuple-element.89), channel_id=1, source_target_pairs={{0,2},{1,3},{2,0},{3,1},{4,6},{5,7},{6,4},{7,5},{8,10},{9,11},{10,... | collective-permute-start | bytes 294920 | tf_op jit(solution)/shard_map/ppermute | solution.py:363
  70.8 6.5 %collective-permute-start.31 = (bf16[192,256]{1,0:T(8,128)(2,1)S(1)}, bf16[192,256]{1,0:T(8,128)(2,1)S(1)}, u32[]{:S(2)}, u32[]{:S(2)}) collective-permute-start(bf16[192,256]{1,0:T(8,128)(2,1)S(1)} %fusion.1), channel_id=1, source_target_pairs={{0,12},{1,13},{2,14},{3,15},{4,8},{5,9},{6,10},{7,11},{8,4},{9,5},... | collective-permute-start | bytes 294920 | tf_op jit(solution)/shard_map/ppermute | solution.py:363

commit v14 on v13

--- a/solution.py
+++ b/solution.py
@@ -437,6 +437,8 @@
             relays[k] = pieces, places
             if k in far:
                 earlier.append(pieces[-1])
+                wait = pieces[-1]
+        home[0] = send_home(0, own_sum, wait)
         turns = [[k for k in sends if k < groups - 1], [groups - 1]] if groups > 2 else [sends]
         for turn in turns:
             blocks, orders = [], []
@@ -465,11 +467,9 @@
             for part in crossed:
                 total += (part if k == groups - 1 else after(part, summed)).astype(F32)
             total = total.astype(BF16)
-            wait = total if wait is None else wait
             home[k] = [hop(total, k, 0)]
         if sends:
             home[near[0]] = send_home(near[0], after(near[1], give))
-        home[0] = send_home(0, own_sum, wait)
         order = [0] + sorted(sends)
     else:
         mine = spread(leaving[0])

time: 78.4 us -> 78.3 us (level)
  transfers between devices with their start and end apart: 32 -> 32, of which waited for: 15 -> 14; matrix products, arithmetic and copies ran while one was open for 0% -> 0% of each run, Pallas kernels for 11% -> 11%
where the time goes in v14:
time: 78.3 us; the launch traced here: 78.1 us
  starting transfers between devices  32.8 us (42%)
  waiting for transfers between devices  31.4 us (40%)
  Pallas kernels  12.7 us (16%)
  between operations  1 us (1%)
    ppermute x32, starting transfers between devices, hop(): return lax.ppermute(value, ('expert', 'mp'), moves)  32.8 us
    ppermute x32, waiting for transfers between devices, hop(): return lax.ppermute(value, ('expert', 'mp'), moves)  31.4 us
    pallas_call x3, Pallas kernels, run_expert(): pl.pallas_call(functools.partial(expert_kernel, tuple(map(tuple, orders))...  3.88 us
    pallas_call x4, Pallas kernels, attend(): pl.pallas_call(attend_kernel, in_specs=[WHOLE] * 2, out_specs=WHOLE, out_...  2.8 us
    pallas_call x1, Pallas kernels, ask(): pl.pallas_call(query_kernel, in_specs=[pl.BlockSpec(memory_space=pltpu.HB...  1.81 us
    pallas_call x4, Pallas kernels, combine(): pl.pallas_call(functools.partial(combine_kernel, len(parts)), in_specs=[W...  1.59 us
  transfers between devices with their start and end apart: 32, of which 14 were waited for; matrix products, arithmetic and copies ran while one was open for 0% of the time, Pallas kernels for 11%

profile of v14, /device:TPU:0, one launch (start us, length us, event | category | flops | bytes accessed | tf_op | source)
XLA Modules:
  0.0 78.1 jit_solution(18414609059179849020)
XLA Ops:
  0.0 2.9 %collective-permute-start.9 = (bf16[256,1024]{1,0:T(8,128)(2,1)}, bf16[256,1024]{1,0:T(8,128)(2,1)S(1)}, u32[]{:S(2)}, u32[]{:S(2)}) collective-permute-start(bf16[256,1024]{1,0:T(8,128)(2,1)} %refs_5_), channel_id=1, source_target_pairs={{0,2},{1,3},{2,0},{3,1},{4,6},{5,7},{6,4},{7,5},{8,10},{9,11},{10,... | collective-permute-start | bytes 1572872 | tf_op jit(solution)/shard_map/ppermute | solution.py:363
  2.9 1.8 %query.1 = (bf16[256,256]{1,0:T(8,128)(2,1)S(1)}, bf16[2,512,256]{2,1,0:T(8,128)(2,1)S(1)}) custom-call(bf16[256,1024]{1,0:T(8,128)(2,1)} %refs_0_.1, bf16[1024,256]{1,0:T(8,128)(2,1)} %weight.1, bf16[2,512,256]{2,1,0:T(8,128)(2,1)} %bitcast.39), custom_call_target="tpu_custom_call" | custom-call | tf_op jit(solution)/shard_map/query/pallas_call | solution.py:65
  4.8 0.0 copy-start.3
  4.8 0.0 copy-start.5
  4.8 0.0 copy-start.2
  4.8 2.6 %collective-permute-start.1 = (bf16[256,256]{1,0:T(8,128)(2,1)S(1)}, bf16[256,256]{1,0:T(8,128)(2,1)S(1)}, u32[]{:S(2)}, u32[]{:S(2)}) collective-permute-start(bf16[256,256]{1,0:T(8,128)(2,1)S(1)} %get-tuple-element.51.queries), channel_id=1, source_target_pairs={{0,8},{1,9},{2,10},{3,11},{4,12},{5,13},{6,14},{7,15},{8,0},{9,1},... | collective-permute-start | bytes 393224 | tf_op jit(solution)/shard_map/ppermute | solution.py:363
  7.4 1.6 %collective-permute-start = (bf16[256,256]{1,0:T(8,128)(2,1)S(1)}, bf16[256,256]{1,0:T(8,128)(2,1)S(1)}, u32[]{:S(2)}, u32[]{:S(2)}) collective-permute-start(bf16[256,256]{1,0:T(8,128)(2,1)S(1)} %get-tuple-element.51.queries), channel_id=1, source_target_pairs={{0,4},{1,5},{2,6},{3,7},{4,0},{5,1},{6,2},{7,3},{8,12},{9,13},{10,... | collective-permute-start | bytes 393224 | tf_op jit(solution)/shard_map/ppermute | solution.py:363
  9.0 0.7 attend.4.refs_0_
  9.7 3.9 %collective-permute-done.1.queries = bf16[256,256]{1,0:T(8,128)(2,1)S(1)} collective-permute-done((bf16[256,256]{1,0:T(8,128)(2,1)S(1)}, bf16[256,256]{1,0:T(8,128)(2,1)S(1)}, u32[]{:S(2)}, u32[]{:S(2)}) %collective-permute-start.1) | collective-permute-done | bytes 131104 | tf_op jit(solution)/shard_map/ppermute | solution.py:363
  13.6 0.6 collective-permute-start.4
  14.2 0.7 attend.5
  14.9 3.4 %collective-permute-start.3 = (bf16[256,256]{1,0:T(8,128)(2,1)S(1)}, bf16[256,256]{1,0:T(8,128)(2,1)S(1)}, u32[]{:S(2)}, u32[]{:S(2)}) collective-permute-start(bf16[256,256]{1,0:T(8,128)(2,1)S(1)} %attend.5), channel_id=1, source_target_pairs={{0,8},{1,9},{2,10},{3,11},{4,12},{5,13},{6,14},{7,15},{8,0},{9,1},... | collective-permute-start | bytes 393224 | tf_op jit(solution)/shard_map/ppermute | solution.py:363
  18.4 0.7 attend.6
  19.1 0.1 collective-permute-start.2
  19.1 0.7 attend.7
  19.9 0.0 copy-start.4
  19.9 5.9 %collective-permute-start.5 = (bf16[256,256]{1,0:T(8,128)(2,1)S(1)}, bf16[256,256]{1,0:T(8,128)(2,1)S(1)}, u32[]{:S(2)}, u32[]{:S(2)}) collective-permute-start(bf16[256,256]{1,0:T(8,128)(2,1)S(1)} %attend.7), channel_id=1, source_target_pairs={{0,12},{1,13},{2,14},{3,15},{4,8},{5,9},{6,10},{7,11},{8,4},{9,5},... | collective-permute-start | bytes 393224 | tf_op jit(solution)/shard_map/ppermute | solution.py:363
  26.4 2.8 %collective-permute-done.5.refs_3_ = bf16[256,256]{1,0:T(8,128)(2,1)S(1)} collective-permute-done((bf16[256,256]{1,0:T(8,128)(2,1)S(1)}, bf16[256,256]{1,0:T(8,128)(2,1)S(1)}, u32[]{:S(2)}, u32[]{:S(2)}) %collective-permute-start.5) | collective-permute-done | bytes 131104 | tf_op jit(solution)/shard_map/ppermute | solution.py:363
  29.3 0.1 pick.1.refs_1_
  29.4 0.1 collective-permute-start.10
  29.5 0.5 collective-permute-start.11
  30.0 0.5 collective-permute-start.6
  30.6 1.0 %route.1 = (s32[256,2]{1,0:T(8,128)S(1)}, bf16[192,256]{1,0:T(8,128)(2,1)S(1)}, bf16[192,256]{1,0:T(8,128)(2,1)S(1)}, bf16[192,256]{1,0:T(8,128)(2,1)S(1)}, bf16...) custom-call(s32[2,256]{1,0:T(2,128)S(1)} %bitcast.38), custom_call_target="tpu_custom_call" | custom-call | tf_op jit(solution)/shard_map/route/pallas_call | solution.py:177
  31.5 0.1 collective-permute-start.7
  31.6 3.9 %collective-permute-done.6.refs_2_ = bf16[256,256]{1,0:T(8,128)(2,1)S(1)} collective-permute-done((bf16[256,256]{1,0:T(8,128)(2,1)S(1)}, bf16[256,256]{1,0:T(8,128)(2,1)S(1)}, u32[]{:S(2)}, u32[]{:S(2)}) %collective-permute-start.6) | collective-permute-done | bytes 131104 | tf_op jit(solution)/shard_map/ppermute | solution.py:363
  35.5 1.3 %collective-permute-done.8.refs_4_ = bf16[256,256]{1,0:T(8,128)(2,1)S(1)} collective-permute-done((bf16[256,256]{1,0:T(8,128)(2,1)S(1)}, bf16[256,256]{1,0:T(8,128)(2,1)S(1)}, u32[]{:S(2)}, u32[]{:S(2)}) %collective-permute-start.8) | collective-permute-done | bytes 131104 | tf_op jit(solution)/shard_map/ppermute | solution.py:363
  36.9 0.0 copy-start
  36.9 1.0 %state.1 = (bf16[256,1024]{1,0:T(8,128)(2,1)S(1)}, bf16[192,256]{1,0:T(8,128)(2,1)S(1)}, bf16[192,256]{1,0:T(8,128)(2,1)S(1)}, bf16[192,512]{1,0:T(8,128)(2,1)S(1)}) custom-call(bf16[256,1024]{1,0:T(8,128)(2,1)S(1)} %copy-done.2, bf16[256,256]{1,0:T(8,128)(2,1)S(1)} %pick.1.refs_1_, bf16[256,256]{1,0:T(8,128)(2,1)S(1)} %collective-permute-done.6.refs_2_, ...), custom_call_target="tpu_custom_call" | custom-call | tf_op jit(solution)/shard_map/state/pallas_call | solution.py:210
  37.9 3.4 %collective-permute-start.12 = (bf16[192,256]{1,0:T(8,128)(2,1)S(1)}, bf16[192,256]{1,0:T(8,128)(2,1)S(1)}, u32[]{:S(2)}, u32[]{:S(2)}) collective-permute-start(bf16[192,256]{1,0:T(8,128)(2,1)S(1)} %get-tuple-element.74), channel_id=1, source_target_pairs={{0,12},{1,13},{2,14},{3,15},{4,8},{5,9},{6,10},{7,11},{8,4},{9,5},... | collective-permute-start | bytes 294920 | tf_op jit(solution)/shard_map/ppermute | solution.py:363
  41.2 1.1 %collective-permute-start.20 = (bf16[192,512]{1,0:T(8,128)(2,1)S(1)}, bf16[192,512]{1,0:T(8,128)(2,1)S(1)}, u32[]{:S(2)}, u32[]{:S(2)}) collective-permute-start(bf16[192,512]{1,0:T(8,128)(2,1)S(1)} %get-tuple-element.83), channel_id=1, source_target_pairs={{0,4},{1,5},{2,6},{3,7},{4,0},{5,1},{6,2},{7,3},{8,12},{9,13},{10,... | collective-permute-start | bytes 589832 | tf_op jit(solution)/shard_map/ppermute | solution.py:363
  42.3 0.5 home.1
  42.9 1.0 %expert.3 = (f32[2,192,256]{2,1,0:T(8,128)S(1)}, bf16[2,192,256]{2,1,0:T(8,128)(2,1)S(1)}) custom-call(bf16[192,512]{1,0:T(8,128)(2,1)S(1)} %get-tuple-element.70.refs_0_, bf16[192,512]{1,0:T(8,128)(2,1)S(1)} %get-tuple-element.71.refs_1_, bf16[1024,1024]{1,0:T(8,128)(2,1)S(1)} %bitcast.31, bf16[1024,1024]{1,0:T(8,128)(2,1)S(1)} %bitcast.34), custom_call_target="tpu_custom_call" | custom-call | tf_op jit(solution)/shard_map/expert/pallas_call | solution.py:289
  43.9 1.6 %collective-permute-done.12.refs_0_ = bf16[192,256]{1,0:T(8,128)(2,1)S(1)} collective-permute-done((bf16[192,256]{1,0:T(8,128)(2,1)S(1)}, bf16[192,256]{1,0:T(8,128)(2,1)S(1)}, u32[]{:S(2)}, u32[]{:S(2)}) %collective-permute-start.12) | collective-permute-done | bytes 98336 | tf_op jit(solution)/shard_map/ppermute | solution.py:363
  45.5 4.6 %collective-permute-done.16.refs_0_ = bf16[192,256]{1,0:T(8,128)(2,1)S(1)} collective-permute-done((bf16[192,256]{1,0:T(8,128)(2,1)S(1)}, bf16[192,256]{1,0:T(8,128)(2,1)S(1)}, u32[]{:S(2)}, u32[]{:S(2)}) %collective-permute-start.16) | collective-permute-done | bytes 98336 | tf_op jit(solution)/shard_map/ppermute | solution.py:363
  50.1 0.5 collective-permute-start.17
  50.7 1.5 %collective-permute-start.14 = (bf16[192,256]{1,0:T(8,128)(2,1)S(1)}, bf16[192,256]{1,0:T(8,128)(2,1)S(1)}, u32[]{:S(2)}, u32[]{:S(2)}) collective-permute-start(bf16[192,256]{1,0:T(8,128)(2,1)S(1)} %collective-permute-done.12.refs_0_), channel_id=1, source_target_pairs={{0,2},{1,3},{2,0},{3,1},{4,6},{5,7},{6,4},{7,5},{8,10},{9,11},{10,... | collective-permute-start | bytes 294920 | tf_op jit(solution)/shard_map/ppermute | solution.py:363
  52.1 0.5 collective-permute-start.21
  52.6 2.4 %collective-permute-done.17.refs_1_ = bf16[192,256]{1,0:T(8,128)(2,1)S(1)} collective-permute-done((bf16[192,256]{1,0:T(8,128)(2,1)S(1)}, bf16[192,256]{1,0:T(8,128)(2,1)S(1)}, u32[]{:S(2)}, u32[]{:S(2)}) %collective-permute-start.17) | collective-permute-done | bytes 98336 | tf_op jit(solution)/shard_map/ppermute | solution.py:363
  55.1 0.1 convert_add_fusion.2
  55.1 1.0 %collective-permute-done.14.refs_1_ = bf16[192,256]{1,0:T(8,128)(2,1)S(1)} collective-permute-done((bf16[192,256]{1,0:T(8,128)(2,1)S(1)}, bf16[192,256]{1,0:T(8,128)(2,1)S(1)}, u32[]{:S(2)}, u32[]{:S(2)}) %collective-permute-start.14) | collective-permute-done | bytes 98336 | tf_op jit(solution)/shard_map/ppermute | solution.py:363
  56.1 0.2 collective-permute-done.19.refs_3_
  56.4 1.9 %expert.4 = (f32[2,384,256]{2,1,0:T(8,128)S(1)}, bf16[2,384,256]{2,1,0:T(8,128)(2,1)S(1)}) custom-call(bf16[192,256]{1,0:T(8,128)(2,1)S(1)} %collective-permute-done.16.refs_0_, bf16[192,256]{1,0:T(8,128)(2,1)S(1)} %collective-permute-done.17.refs_1_, bf16[192,256]{1,0:T(8,128)(2,1)S(1)} %collective-permute-done.18.refs_2_, ...), custom_call_target="tpu_custom_call" | custom-call | tf_op jit(solution)/shard_map/expert/pallas_call | solution.py:289
  58.2 0.2 collective-permute-start.22
  58.5 0.8 %collective-permute-start.15 = (bf16[192,256]{1,0:T(8,128)(2,1)S(1)}, bf16[192,256]{1,0:T(8,128)(2,1)S(1)}, u32[]{:S(2)}, u32[]{:S(2)}) collective-permute-start(bf16[192,256]{1,0:T(8,128)(2,1)S(1)} %get-tuple-element.76), channel_id=1, source_target_pairs={{0,2},{1,3},{2,0},{3,1},{4,6},{5,7},{6,4},{7,5},{8,10},{9,11},{10,... | collective-permute-start | bytes 294920 | tf_op jit(solution)/shard_map/ppermute | solution.py:363
  59.3 0.1 collective-permute-start.23
  59.3 0.4 collective-permute-start.24
  59.8 0.2 collective-permute-done.22
  60.0 0.1 convert_add_fusion
  60.2 1.1 %collective-permute-start.27 = (bf16[192,256]{1,0:T(8,128)(2,1)S(1)}, bf16[192,256]{1,0:T(8,128)(2,1)S(1)}, u32[]{:S(2)}, u32[]{:S(2)}) collective-permute-start(bf16[192,256]{1,0:T(8,128)(2,1)S(1)} %fusion.4), channel_id=1, source_target_pairs={{0,2},{1,3},{2,0},{3,1},{4,6},{5,7},{6,4},{7,5},{8,10},{9,11},{10,... | collective-permute-start | bytes 294920 | tf_op jit(solution)/shard_map/ppermute | solution.py:363
  61.3 1.0 %expert.5 = (f32[2,192,256]{2,1,0:T(8,128)S(1)}, bf16[2,192,256]{2,1,0:T(8,128)(2,1)S(1)}) custom-call(bf16[192,256]{1,0:T(8,128)(2,1)S(1)} %collective-permute-done.12.refs_0_, bf16[192,256]{1,0:T(8,128)(2,1)S(1)} %collective-permute-done.14.refs_1_, bf16[192,256]{1,0:T(8,128)(2,1)S(1)} %collective-permute-done.23.refs_2_, ...), custom_call_target="tpu_custom_call" | custom-call | tf_op jit(solution)/shard_map/expert/pallas_call | solution.py:289
  62.3 0.1 collective-permute-start.28
  62.4 0.7 collective-permute-start.26
  63.1 1.9 %collective-permute-start.25 = (bf16[192,256]{1,0:T(8,128)(2,1)S(1)}, bf16[192,256]{1,0:T(8,128)(2,1)S(1)}, u32[]{:S(2)}, u32[]{:S(2)}) collective-permute-start(bf16[192,256]{1,0:T(8,128)(2,1)S(1)} %get-tuple-element.98), channel_id=1, source_target_pairs={{0,4},{1,5},{2,6},{3,7},{4,0},{5,1},{6,2},{7,3},{8,12},{9,13},{10,... | collective-permute-start | bytes 294920 | tf_op jit(solution)/shard_map/ppermute | solution.py:363
  65.1 0.6 collective-permute-done.27
  65.7 0.7 collective-permute-start.30
  66.4 0.1 collective-permute-start.29
  66.5 4.2 %collective-permute-done.30 = bf16[192,256]{1,0:T(8,128)(2,1)S(1)} collective-permute-done((bf16[192,256]{1,0:T(8,128)(2,1)S(1)}, bf16[192,256]{1,0:T(8,128)(2,1)S(1)}, u32[]{:S(2)}, u32[]{:S(2)}) %collective-permute-start.30) | collective-permute-done | bytes 98336 | tf_op jit(solution)/shard_map/ppermute | solution.py:363
  70.7 1.3 %collective-permute-start.31 = (bf16[192,256]{1,0:T(8,128)(2,1)S(1)}, bf16[192,256]{1,0:T(8,128)(2,1)S(1)}, u32[]{:S(2)}, u32[]{:S(2)}) collective-permute-start(bf16[192,256]{1,0:T(8,128)(2,1)S(1)} %fusion.1), channel_id=1, source_target_pairs={{0,12},{1,13},{2,14},{3,15},{4,8},{5,9},{6,10},{7,11},{8,4},{9,5},... | collective-permute-start | bytes 294920 | tf_op jit(solution)/shard_map/ppermute | solution.py:363
  72.1 0.2 combine.4.base
  72.3 0.2 combine.5.base
  72.6 1.1 %collective-permute-done.29.refs_0_ = bf16[192,256]{1,0:T(8,128)(2,1)S(1)} collective-permute-done((bf16[192,256]{1,0:T(8,128)(2,1)S(1)}, bf16[192,256]{1,0:T(8,128)(2,1)S(1)}, u32[]{:S(2)}, u32[]{:S(2)}) %collective-permute-start.29) | collective-permute-done | bytes 98336 | tf_op jit(solution)/shard_map/ppermute | solution.py:363
  73.6 0.2 combine.6.base
  73.9 3.4 %collective-permute-done.31.refs_0_ = bf16[192,256]{1,0:T(8,128)(2,1)S(1)} collective-permute-done((bf16[192,256]{1,0:T(8,128)(2,1)S(1)}, bf16[192,256]{1,0:T(8,128)(2,1)S(1)}, u32[]{:S(2)}, u32[]{:S(2)}) %collective-permute-start.31) | collective-permute-done | bytes 98336 | tf_op jit(solution)/shard_map/ppermute | solution.py:363
  77.3 0.9 %combine.7 = bf16[256,256]{1,0:T(8,128)(2,1)} custom-call(f32[256,2]{1,0:T(8,128)S(1)} %get-tuple-element.66.gates, f32[256,256]{1,0:T(8,128)S(1)} %combine.6.base, bf16[256,192]{1,0:T(8,128)(2,1)S(1)} %get-tuple-element.95.first, bf16[256,192]{1,0:T(8,128)(2,1)S(1)} %get-tuple-element.96.second, bf16[192,256]{1,0:T(8,128)(2,1)S(1)} %collective-permute-done.31.refs_0_), custom_call_target="tpu_custom_call" | custom-call | tf_op jit(solution)/shard_map/combine/pallas_call | solution.py:315
  (38 shorter events, 0.2 us)
Async XLA Ops:
  0.0 29.5 %collective-permute-start.9 = (bf16[256,1024]{1,0:T(8,128)(2,1)}, bf16[256,1024]{1,0:T(8,128)(2,1)S(1)}, u32[]{:S(2)}, u32[]{:S(2)}) collective-permute-start(bf16[256,1024]{1,0:T(8,128)(2,1)} %refs_5_), channel_id=1, source_target_pairs={{0,2},{1,3},{2,0},{3,1},{4,6},{5,7},{6,4},{7,5},{8,10},{9,11},{10,... | collective-permute-start | bytes 1572872 | tf_op jit(solution)/shard_map/ppermute | solution.py:363
  4.8 24.7 %copy-start.3 = (bf16[256,1024]{1,0:T(8,128)(2,1)S(1)}, bf16[256,1024]{1,0:T(8,128)(2,1)}, u32[]{:S(2)}) copy-start(bf16[256,1024]{1,0:T(8,128)(2,1)} %refs_5_) | copy-start | bytes 1572868
  4.8 25.8 %copy-start.5 = (s32[256,2]{0,1:T(2,128)S(1)}, s32[256,2]{0,1:T(2,128)}, u32[]{:S(2)}) copy-start(s32[256,2]{0,1:T(2,128)} %param.15) | copy-start | bytes 6148
  4.8 32.1 %copy-start.2 = (bf16[256,1024]{1,0:T(8,128)(2,1)S(1)}, bf16[256,1024]{1,0:T(8,128)(2,1)}, u32[]{:S(2)}) copy-start(bf16[256,1024]{1,0:T(8,128)(2,1)} %refs_0_.1) | copy-start | bytes 1572868
  4.8 8.8 %collective-permute-start.1 = (bf16[256,256]{1,0:T(8,128)(2,1)S(1)}, bf16[256,256]{1,0:T(8,128)(2,1)S(1)}, u32[]{:S(2)}, u32[]{:S(2)}) collective-permute-start(bf16[256,256]{1,0:T(8,128)(2,1)S(1)} %get-tuple-element.51.queries), channel_id=1, source_target_pairs={{0,8},{1,9},{2,10},{3,11},{4,12},{5,13},{6,14},{7,15},{8,0},{9,1},... | collective-permute-start | bytes 393224 | tf_op jit(solution)/shard_map/ppermute | solution.py:363
  7.4 10.9 %collective-permute-start = (bf16[256,256]{1,0:T(8,128)(2,1)S(1)}, bf16[256,256]{1,0:T(8,128)(2,1)S(1)}, u32[]{:S(2)}, u32[]{:S(2)}) collective-permute-start(bf16[256,256]{1,0:T(8,128)(2,1)S(1)} %get-tuple-element.51.queries), channel_id=1, source_target_pairs={{0,4},{1,5},{2,6},{3,7},{4,0},{5,1},{6,2},{7,3},{8,12},{9,13},{10,... | collective-permute-start | bytes 393224 | tf_op jit(solution)/shard_map/ppermute | solution.py:363
  13.6 5.5 %collective-permute-start.4 = (bf16[256,256]{1,0:T(8,128)(2,1)S(1)}, bf16[256,256]{1,0:T(8,128)(2,1)S(1)}, u32[]{:S(2)}, u32[]{:S(2)}) collective-permute-start(bf16[256,256]{1,0:T(8,128)(2,1)S(1)} %collective-permute-done.1.queries), channel_id=1, source_target_pairs={{0,4},{1,5},{2,6},{3,7},{4,0},{5,1},{6,2},{7,3},{8,12},{9,13},{10,... | collective-permute-start | bytes 393224 | tf_op jit(solution)/shard_map/ppermute | solution.py:363
  14.9 11.5 %collective-permute-start.3 = (bf16[256,256]{1,0:T(8,128)(2,1)S(1)}, bf16[256,256]{1,0:T(8,128)(2,1)S(1)}, u32[]{:S(2)}, u32[]{:S(2)}) collective-permute-start(bf16[256,256]{1,0:T(8,128)(2,1)S(1)} %attend.5), channel_id=1, source_target_pairs={{0,8},{1,9},{2,10},{3,11},{4,12},{5,13},{6,14},{7,15},{8,0},{9,1},... | collective-permute-start | bytes 393224 | tf_op jit(solution)/shard_map/ppermute | solution.py:363
  19.1 7.4 %collective-permute-start.2 = (bf16[256,256]{1,0:T(8,128)(2,1)S(1)}, bf16[256,256]{1,0:T(8,128)(2,1)S(1)}, u32[]{:S(2)}, u32[]{:S(2)}) collective-permute-start(bf16[256,256]{1,0:T(8,128)(2,1)S(1)} %attend.6), channel_id=1, source_target_pairs={{0,4},{1,5},{2,6},{3,7},{4,0},{5,1},{6,2},{7,3},{8,12},{9,13},{10,... | collective-permute-start | bytes 393224 | tf_op jit(solution)/shard_map/ppermute | solution.py:363
  19.9 22.5 %copy-start.4 = (bf16[1024,4]{0,1:T(4,128)(2,1)S(1)}, bf16[1024,4]{0,1:T(4,128)(2,1)}, u32[]{:S(2)}) copy-start(bf16[1024,4]{0,1:T(4,128)(2,1)} %param.14) | copy-start | bytes 24580
  19.9 9.4 %collective-permute-start.5 = (bf16[256,256]{1,0:T(8,128)(2,1)S(1)}, bf16[256,256]{1,0:T(8,128)(2,1)S(1)}, u32[]{:S(2)}, u32[]{:S(2)}) collective-permute-start(bf16[256,256]{1,0:T(8,128)(2,1)S(1)} %attend.7), channel_id=1, source_target_pairs={{0,12},{1,13},{2,14},{3,15},{4,8},{5,9},{6,10},{7,11},{8,4},{9,5},... | collective-permute-start | bytes 393224 | tf_op jit(solution)/shard_map/ppermute | solution.py:363
  29.4 7.4 %collective-permute-start.10 = (bf16[256,1024]{1,0:T(8,128)(2,1)S(1)}, bf16[256,1024]{1,0:T(8,128)(2,1)S(1)}, u32[]{:S(2)}, u32[]{:S(2)}) collective-permute-start(bf16[256,1024]{1,0:T(8,128)(2,1)S(1)} %copy-done.3), channel_id=1, source_target_pairs={{0,1},{1,0},{2,3},{3,2},{4,5},{5,4},{6,7},{7,6},{8,9},{9,8},{10,11... | collective-permute-start | bytes 1572872 | tf_op jit(solution)/shard_map/ppermute | solution.py:363
  29.5 7.3 %collective-permute-start.11 = (bf16[256,1024]{1,0:T(8,128)(2,1)S(1)}, bf16[256,1024]{1,0:T(8,128)(2,1)S(1)}, u32[]{:S(2)}, u32[]{:S(2)}) collective-permute-start(bf16[256,1024]{1,0:T(8,128)(2,1)S(1)} %collective-permute-done.9.refs_6_), channel_id=1, source_target_pairs={{0,1},{1,0},{2,3},{3,2},{4,5},{5,4},{6,7},{7,6},{8,9},{9,8},{10,11... | collective-permute-start | bytes 1572872 | tf_op jit(solution)/shard_map/ppermute | solution.py:363
  30.0 5.5 %collective-permute-start.6 = (bf16[256,256]{1,0:T(8,128)(2,1)S(1)}, bf16[256,256]{1,0:T(8,128)(2,1)S(1)}, u32[]{:S(2)}, u32[]{:S(2)}) collective-permute-start(bf16[256,256]{1,0:T(8,128)(2,1)S(1)} %pick.1.refs_1_), channel_id=1, source_target_pairs={{0,2},{1,3},{2,0},{3,1},{4,6},{5,7},{6,4},{7,5},{8,10},{9,11},{10,... | collective-permute-start | bytes 393224 | tf_op jit(solution)/shard_map/ppermute | solution.py:363
  31.5 4.0 %collective-permute-start.7 = (bf16[256,256]{1,0:T(8,128)(2,1)S(1)}, bf16[256,256]{1,0:T(8,128)(2,1)S(1)}, u32[]{:S(2)}, u32[]{:S(2)}) collective-permute-start(bf16[256,256]{1,0:T(8,128)(2,1)S(1)} %pick.1.refs_1_), channel_id=1, source_target_pairs={{0,1},{1,0},{2,3},{3,2},{4,5},{5,4},{6,7},{7,6},{8,9},{9,8},{10,11... | collective-permute-start | bytes 393224 | tf_op jit(solution)/shard_map/ppermute | solution.py:363
  35.5 1.3 %collective-permute-start.8 = (bf16[256,256]{1,0:T(8,128)(2,1)S(1)}, bf16[256,256]{1,0:T(8,128)(2,1)S(1)}, u32[]{:S(2)}, u32[]{:S(2)}) collective-permute-start(bf16[256,256]{1,0:T(8,128)(2,1)S(1)} %collective-permute-done.6.refs_2_), channel_id=1, source_target_pairs={{0,1},{1,0},{2,3},{3,2},{4,5},{5,4},{6,7},{7,6},{8,9},{9,8},{10,11... | collective-permute-start | bytes 393224 | tf_op jit(solution)/shard_map/ppermute | solution.py:363
  36.9 6.0 %copy-start = (bf16[1,1024,1024]{2,1,0:T(8,128)(2,1)S(1)}, bf16[1,1024,1024]{2,1,0:T(8,128)(2,1)}, u32[]{:S(2)}) copy-start(bf16[1,1024,1024]{2,1,0:T(8,128)(2,1)} %param.16) | copy-start | bytes 6291460
  36.9 6.0 %copy-start.1 = (bf16[1,1024,1024]{2,1,0:T(8,128)(2,1)S(1)}, bf16[1,1024,1024]{2,1,0:T(8,128)(2,1)}, u32[]{:S(2)}) copy-start(bf16[1,1024,1024]{2,1,0:T(8,128)(2,1)} %param.17) | copy-start | bytes 6291460
  37.9 7.6 %collective-permute-start.12 = (bf16[192,256]{1,0:T(8,128)(2,1)S(1)}, bf16[192,256]{1,0:T(8,128)(2,1)S(1)}, u32[]{:S(2)}, u32[]{:S(2)}) collective-permute-start(bf16[192,256]{1,0:T(8,128)(2,1)S(1)} %get-tuple-element.74), channel_id=1, source_target_pairs={{0,12},{1,13},{2,14},{3,15},{4,8},{5,9},{6,10},{7,11},{8,4},{9,5},... | collective-permute-start | bytes 294920 | tf_op jit(solution)/shard_map/ppermute | solution.py:363
  41.2 8.9 %collective-permute-start.16 = (bf16[192,256]{1,0:T(8,128)(2,1)S(1)}, bf16[192,256]{1,0:T(8,128)(2,1)S(1)}, u32[]{:S(2)}, u32[]{:S(2)}) collective-permute-start(bf16[192,256]{1,0:T(8,128)(2,1)S(1)} %get-tuple-element.79), channel_id=1, source_target_pairs={{0,8},{1,9},{2,10},{3,11},{4,12},{5,13},{6,14},{7,15},{8,0},{9,1},... | collective-permute-start | bytes 294920 | tf_op jit(solution)/shard_map/ppermute | solution.py:363
  41.2 10.9 %collective-permute-start.20 = (bf16[192,512]{1,0:T(8,128)(2,1)S(1)}, bf16[192,512]{1,0:T(8,128)(2,1)S(1)}, u32[]{:S(2)}, u32[]{:S(2)}) collective-permute-start(bf16[192,512]{1,0:T(8,128)(2,1)S(1)} %get-tuple-element.83), channel_id=1, source_target_pairs={{0,4},{1,5},{2,6},{3,7},{4,0},{5,1},{6,2},{7,3},{8,12},{9,13},{10,... | collective-permute-start | bytes 589832 | tf_op jit(solution)/shard_map/ppermute | solution.py:363
  45.5 9.6 %collective-permute-start.13 = (bf16[2,192,256]{2,1,0:T(8,128)(2,1)S(1)}, bf16[2,192,256]{2,1,0:T(8,128)(2,1)S(1)}, u32[]{:S(2)}, u32[]{:S(2)}) collective-permute-start(bf16[2,192,256]{2,1,0:T(8,128)(2,1)S(1)} %get-tuple-element.75), channel_id=1, source_target_pairs={{0,1},{1,0},{2,3},{3,2},{4,5},{5,4},{6,7},{7,6},{8,9},{9,8},{10,11... | collective-permute-start | bytes 589832 | tf_op jit(solution)/shard_map/ppermute | solution.py:363
  50.1 5.0 %collective-permute-start.17 = (bf16[192,256]{1,0:T(8,128)(2,1)S(1)}, bf16[192,256]{1,0:T(8,128)(2,1)S(1)}, u32[]{:S(2)}, u32[]{:S(2)}) collective-permute-start(bf16[192,256]{1,0:T(8,128)(2,1)S(1)} %collective-permute-done.16.refs_0_), channel_id=1, source_target_pairs={{0,2},{1,3},{2,0},{3,1},{4,6},{5,7},{6,4},{7,5},{8,10},{9,11},{10,... | collective-permute-start | bytes 294920 | tf_op jit(solution)/shard_map/ppermute | solution.py:363
  50.7 5.5 %collective-permute-start.14 = (bf16[192,256]{1,0:T(8,128)(2,1)S(1)}, bf16[192,256]{1,0:T(8,128)(2,1)S(1)}, u32[]{:S(2)}, u32[]{:S(2)}) collective-permute-start(bf16[192,256]{1,0:T(8,128)(2,1)S(1)} %collective-permute-done.12.refs_0_), channel_id=1, source_target_pairs={{0,2},{1,3},{2,0},{3,1},{4,6},{5,7},{6,4},{7,5},{8,10},{9,11},{10,... | collective-permute-start | bytes 294920 | tf_op jit(solution)/shard_map/ppermute | solution.py:363
  52.1 4.0 %collective-permute-start.18 = (bf16[192,256]{1,0:T(8,128)(2,1)S(1)}, bf16[192,256]{1,0:T(8,128)(2,1)S(1)}, u32[]{:S(2)}, u32[]{:S(2)}) collective-permute-start(bf16[192,256]{1,0:T(8,128)(2,1)S(1)} %collective-permute-done.16.refs_0_), channel_id=1, source_target_pairs={{0,1},{1,0},{2,3},{3,2},{4,5},{5,4},{6,7},{7,6},{8,9},{9,8},{10,11... | collective-permute-start | bytes 294920 | tf_op jit(solution)/shard_map/ppermute | solution.py:363
  52.1 4.2 %collective-permute-start.21 = (bf16[192,512]{1,0:T(8,128)(2,1)S(1)}, bf16[192,512]{1,0:T(8,128)(2,1)S(1)}, u32[]{:S(2)}, u32[]{:S(2)}) collective-permute-start(bf16[192,512]{1,0:T(8,128)(2,1)S(1)} %collective-permute-done.20.refs_4_), channel_id=1, source_target_pairs={{0,1},{1,0},{2,3},{3,2},{4,5},{5,4},{6,7},{7,6},{8,9},{9,8},{10,11... | collective-permute-start | bytes 589832 | tf_op jit(solution)/shard_map/ppermute | solution.py:363
  55.1 1.3 %collective-permute-start.19 = (bf16[192,256]{1,0:T(8,128)(2,1)S(1)}, bf16[192,256]{1,0:T(8,128)(2,1)S(1)}, u32[]{:S(2)}, u32[]{:S(2)}) collective-permute-start(bf16[192,256]{1,0:T(8,128)(2,1)S(1)} %collective-permute-done.17.refs_1_), channel_id=1, source_target_pairs={{0,1},{1,0},{2,3},{3,2},{4,5},{5,4},{6,7},{7,6},{8,9},{9,8},{10,11... | collective-permute-start | bytes 294920 | tf_op jit(solution)/shard_map/ppermute | solution.py:363
  58.2 1.8 %collective-permute-start.22 = (bf16[2,384,256]{2,1,0:T(8,128)(2,1)S(1)}, bf16[2,384,256]{2,1,0:T(8,128)(2,1)S(1)}, u32[]{:S(2)}, u32[]{:S(2)}) collective-permute-start(bf16[2,384,256]{2,1,0:T(8,128)(2,1)S(1)} %get-tuple-element.85), channel_id=1, source_target_pairs={{0,1},{1,0},{2,3},{3,2},{4,5},{5,4},{6,7},{7,6},{8,9},{9,8},{10,11... | collective-permute-start | bytes 1179656 | tf_op jit(solution)/shard_map/ppermute | solution.py:363
  58.5 13.6 %collective-permute-start.15 = (bf16[192,256]{1,0:T(8,128)(2,1)S(1)}, bf16[192,256]{1,0:T(8,128)(2,1)S(1)}, u32[]{:S(2)}, u32[]{:S(2)}) collective-permute-start(bf16[192,256]{1,0:T(8,128)(2,1)S(1)} %get-tuple-element.76), channel_id=1, source_target_pairs={{0,2},{1,3},{2,0},{3,1},{4,6},{5,7},{6,4},{7,5},{8,10},{9,11},{10,... | collective-permute-start | bytes 294920 | tf_op jit(solution)/shard_map/ppermute | solution.py:363
  59.3 2.0 %collective-permute-start.23 = (bf16[192,256]{1,0:T(8,128)(2,1)S(1)}, bf16[192,256]{1,0:T(8,128)(2,1)S(1)}, u32[]{:S(2)}, u32[]{:S(2)}) collective-permute-start(bf16[192,256]{1,0:T(8,128)(2,1)S(1)} %collective-permute-done.12.refs_0_), channel_id=1, source_target_pairs={{0,1},{1,0},{2,3},{3,2},{4,5},{5,4},{6,7},{7,6},{8,9},{9,8},{10,11... | collective-permute-start | bytes 294920 | tf_op jit(solution)/shard_map/ppermute | solution.py:363
  59.3 2.0 %collective-permute-start.24 = (bf16[192,256]{1,0:T(8,128)(2,1)S(1)}, bf16[192,256]{1,0:T(8,128)(2,1)S(1)}, u32[]{:S(2)}, u32[]{:S(2)}) collective-permute-start(bf16[192,256]{1,0:T(8,128)(2,1)S(1)} %collective-permute-done.14.refs_1_), channel_id=1, source_target_pairs={{0,1},{1,0},{2,3},{3,2},{4,5},{5,4},{6,7},{7,6},{8,9},{9,8},{10,11... | collective-permute-start | bytes 294920 | tf_op jit(solution)/shard_map/ppermute | solution.py:363
  60.2 5.5 %collective-permute-start.27 = (bf16[192,256]{1,0:T(8,128)(2,1)S(1)}, bf16[192,256]{1,0:T(8,128)(2,1)S(1)}, u32[]{:S(2)}, u32[]{:S(2)}) collective-permute-start(bf16[192,256]{1,0:T(8,128)(2,1)S(1)} %fusion.4), channel_id=1, source_target_pairs={{0,2},{1,3},{2,0},{3,1},{4,6},{5,7},{6,4},{7,5},{8,10},{9,11},{10,... | collective-permute-start | bytes 294920 | tf_op jit(solution)/shard_map/ppermute | solution.py:363
  62.3 2.7 %collective-permute-start.28 = (bf16[2,192,256]{2,1,0:T(8,128)(2,1)S(1)}, bf16[2,192,256]{2,1,0:T(8,128)(2,1)S(1)}, u32[]{:S(2)}, u32[]{:S(2)}) collective-permute-start(bf16[2,192,256]{2,1,0:T(8,128)(2,1)S(1)} %get-tuple-element.89), channel_id=1, source_target_pairs={{0,1},{1,0},{2,3},{3,2},{4,5},{5,4},{6,7},{7,6},{8,9},{9,8},{10,11... | collective-permute-start | bytes 589832 | tf_op jit(solution)/shard_map/ppermute | solution.py:363
  62.4 9.9 %collective-permute-start.26 = (bf16[192,256]{1,0:T(8,128)(2,1)S(1)}, bf16[192,256]{1,0:T(8,128)(2,1)S(1)}, u32[]{:S(2)}, u32[]{:S(2)}) collective-permute-start(bf16[192,256]{1,0:T(8,128)(2,1)S(1)} %get-tuple-element.97), channel_id=1, source_target_pairs={{0,6},{1,7},{2,4},{3,5},{4,2},{5,3},{6,0},{7,1},{8,14},{9,15},{10,... | collective-permute-start | bytes 294920 | tf_op jit(solution)/shard_map/ppermute | solution.py:363
  63.1 9.2 %collective-permute-start.25 = (bf16[192,256]{1,0:T(8,128)(2,1)S(1)}, bf16[192,256]{1,0:T(8,128)(2,1)S(1)}, u32[]{:S(2)}, u32[]{:S(2)}) collective-permute-start(bf16[192,256]{1,0:T(8,128)(2,1)S(1)} %get-tuple-element.98), channel_id=1, source_target_pairs={{0,4},{1,5},{2,6},{3,7},{4,0},{5,1},{6,2},{7,3},{8,12},{9,13},{10,... | collective-permute-start | bytes 294920 | tf_op jit(solution)/shard_map/ppermute | solution.py:363
  65.7 5.0 %collective-permute-start.30 = (bf16[192,256]{1,0:T(8,128)(2,1)S(1)}, bf16[192,256]{1,0:T(8,128)(2,1)S(1)}, u32[]{:S(2)}, u32[]{:S(2)}) collective-permute-start(bf16[192,256]{1,0:T(8,128)(2,1)S(1)} %fusion.5), channel_id=1, source_target_pairs={{0,2},{1,3},{2,0},{3,1},{4,6},{5,7},{6,4},{7,5},{8,10},{9,11},{10,... | collective-permute-start | bytes 294920 | tf_op jit(solution)/shard_map/ppermute | solution.py:363
  66.4 7.2 %collective-permute-start.29 = (bf16[192,256]{1,0:T(8,128)(2,1)S(1)}, bf16[192,256]{1,0:T(8,128)(2,1)S(1)}, u32[]{:S(2)}, u32[]{:S(2)}) collective-permute-start(bf16[192,256]{1,0:T(8,128)(2,1)S(1)} %fusion.3), channel_id=1, source_target_pairs={{0,8},{1,9},{2,10},{3,11},{4,12},{5,13},{6,14},{7,15},{8,0},{9,1},... | collective-permute-start | bytes 294920 | tf_op jit(solution)/shard_map/ppermute | solution.py:363
  70.7 6.5 %collective-permute-start.31 = (bf16[192,256]{1,0:T(8,128)(2,1)S(1)}, bf16[192,256]{1,0:T(8,128)(2,1)S(1)}, u32[]{:S(2)}, u32[]{:S(2)}) collective-permute-start(bf16[192,256]{1,0:T(8,128)(2,1)S(1)} %fusion.1), channel_id=1, source_target_pairs={{0,12},{1,13},{2,14},{3,15},{4,8},{5,9},{6,10},{7,11},{8,4},{9,5},... | collective-permute-start | bytes 294920 | tf_op jit(solution)/shard_map/ppermute | solution.py:363

commit v15 on v14

--- a/solution.py
+++ b/solution.py
@@ -404,7 +404,8 @@
 
     far = set(range(2, groups)) if direct and pairs > 1 else set()
     sends = [k for k in range(2, groups)] + ([1] if groups > 1 else []) if direct else [0]
-    cuts = [slices if k in far else 2 for k in sends]
+    relayed = {groups - 1} & far
+    cuts = [slices if k in relayed else 2 for k in sends]
     state, *leaving = make_state(tokens, contexts, weights, [dispatch[k] for k in sends], cuts)
     own_a, own_b, gates, columns = at_home(
         state, dispatch[0], router_weight.T, choice, experts, width
@@ -431,11 +432,11 @@
         crossing, started, relays = {}, None, {}
         for k in sends:
             pieces, places = [arrived[k]], [0]
-            for bit in bits[:-1] if k in far else []:
+            for bit in bits[:-1] if k in relayed else []:
                 pieces = pieces + [hop(piece, 0, bit) for piece in pieces]
                 places = places + [index ^ bit for index in places]
             relays[k] = pieces, places
-            if k in far:
+            if k in relayed:
                 earlier.append(pieces[-1])
                 wait = pieces[-1]
         home[0] = send_home(0, own_sum, wait)

time: 78.3 us -> 78 us (level)
  starting transfers between devices: 32.8 us -> 31.2 us
  waiting for transfers between devices: 31.4 us -> 32.6 us
    ppermute x32 -> x30, starting transfers between devices: 32.8 us -> 31.2 us  [hop(): return lax.ppermute(value, ('expert', 'mp'), moves)]
    ppermute x32 -> x30, waiting for transfers between devices: 31.4 us -> 32.6 us  [hop(): return lax.ppermute(value, ('expert', 'mp'), moves)]
  transfers between devices with their start and end apart: 32 -> 30, of which waited for: 14 -> 13; matrix products, arithmetic and copies ran while one was open for 0% -> 0% of each run, Pallas kernels for 11% -> 12%
where the time goes in v15:
time: 78 us; the launch traced here: 77.9 us
  waiting for transfers between devices  32.6 us (42%)
  starting transfers between devices  31.2 us (40%)
  Pallas kernels  12.8 us (16%)
  between operations  1 us (1%)
    ppermute x30, waiting for transfers between devices, hop(): return lax.ppermute(value, ('expert', 'mp'), moves)  32.6 us
    ppermute x30, starting transfers between devices, hop(): return lax.ppermute(value, ('expert', 'mp'), moves)  31.2 us
    pallas_call x3, Pallas kernels, run_expert(): pl.pallas_call(functools.partial(expert_kernel, tuple(map(tuple, orders))...  3.87 us
    pallas_call x4, Pallas kernels, attend(): pl.pallas_call(attend_kernel, in_specs=[WHOLE] * 2, out_specs=WHOLE, out_...  2.8 us
    pallas_call x1, Pallas kernels, ask(): pl.pallas_call(query_kernel, in_specs=[pl.BlockSpec(memory_space=pltpu.HB...  1.81 us
    pallas_call x4, Pallas kernels, combine(): pl.pallas_call(functools.partial(combine_kernel, len(parts)), in_specs=[W...  1.59 us
  transfers between devices with their start and end apart: 30, of which 13 were waited for; matrix products, arithmetic and copies ran while one was open for 0% of the time, Pallas kernels for 12%

profile of v15, /device:TPU:0, one launch (start us, length us, event | category | flops | bytes accessed | tf_op | source)
XLA Modules:
  0.0 77.9 jit_solution(1342086132370370996)
XLA Ops:
  0.0 2.9 %collective-permute-start.9 = (bf16[256,1024]{1,0:T(8,128)(2,1)}, bf16[256,1024]{1,0:T(8,128)(2,1)S(1)}, u32[]{:S(2)}, u32[]{:S(2)}) collective-permute-start(bf16[256,1024]{1,0:T(8,128)(2,1)} %refs_5_), channel_id=1, source_target_pairs={{0,2},{1,3},{2,0},{3,1},{4,6},{5,7},{6,4},{7,5},{8,10},{9,11},{10,... | collective-permute-start | bytes 1572872 | tf_op jit(solution)/shard_map/ppermute | solution.py:363
  2.9 1.8 %query.1 = (bf16[256,256]{1,0:T(8,128)(2,1)S(1)}, bf16[2,512,256]{2,1,0:T(8,128)(2,1)S(1)}) custom-call(bf16[256,1024]{1,0:T(8,128)(2,1)} %refs_0_.1, bf16[1024,256]{1,0:T(8,128)(2,1)} %weight.1, bf16[2,512,256]{2,1,0:T(8,128)(2,1)} %bitcast.39), custom_call_target="tpu_custom_call" | custom-call | tf_op jit(solution)/shard_map/query/pallas_call | solution.py:65
  4.8 0.0 copy-start.3
  4.8 0.0 copy-start.5
  4.8 0.0 copy-start.2
  4.8 2.6 %collective-permute-start.1 = (bf16[256,256]{1,0:T(8,128)(2,1)S(1)}, bf16[256,256]{1,0:T(8,128)(2,1)S(1)}, u32[]{:S(2)}, u32[]{:S(2)}) collective-permute-start(bf16[256,256]{1,0:T(8,128)(2,1)S(1)} %get-tuple-element.50.queries), channel_id=1, source_target_pairs={{0,8},{1,9},{2,10},{3,11},{4,12},{5,13},{6,14},{7,15},{8,0},{9,1},... | collective-permute-start | bytes 393224 | tf_op jit(solution)/shard_map/ppermute | solution.py:363
  7.4 1.6 %collective-permute-start = (bf16[256,256]{1,0:T(8,128)(2,1)S(1)}, bf16[256,256]{1,0:T(8,128)(2,1)S(1)}, u32[]{:S(2)}, u32[]{:S(2)}) collective-permute-start(bf16[256,256]{1,0:T(8,128)(2,1)S(1)} %get-tuple-element.50.queries), channel_id=1, source_target_pairs={{0,4},{1,5},{2,6},{3,7},{4,0},{5,1},{6,2},{7,3},{8,12},{9,13},{10,... | collective-permute-start | bytes 393224 | tf_op jit(solution)/shard_map/ppermute | solution.py:363
  9.0 0.7 attend.4.refs_0_
  9.7 3.9 %collective-permute-done.1.queries = bf16[256,256]{1,0:T(8,128)(2,1)S(1)} collective-permute-done((bf16[256,256]{1,0:T(8,128)(2,1)S(1)}, bf16[256,256]{1,0:T(8,128)(2,1)S(1)}, u32[]{:S(2)}, u32[]{:S(2)}) %collective-permute-start.1) | collective-permute-done | bytes 131104 | tf_op jit(solution)/shard_map/ppermute | solution.py:363
  13.6 0.6 collective-permute-start.4
  14.2 0.7 attend.5
  14.9 3.4 %collective-permute-start.3 = (bf16[256,256]{1,0:T(8,128)(2,1)S(1)}, bf16[256,256]{1,0:T(8,128)(2,1)S(1)}, u32[]{:S(2)}, u32[]{:S(2)}) collective-permute-start(bf16[256,256]{1,0:T(8,128)(2,1)S(1)} %attend.5), channel_id=1, source_target_pairs={{0,8},{1,9},{2,10},{3,11},{4,12},{5,13},{6,14},{7,15},{8,0},{9,1},... | collective-permute-start | bytes 393224 | tf_op jit(solution)/shard_map/ppermute | solution.py:363
  18.4 0.0 collective-permute-done.queries
  18.4 0.7 attend.6
  19.1 0.1 collective-permute-start.2
  19.1 0.7 attend.7
  19.9 0.0 copy-start.4
  19.9 5.9 %collective-permute-start.5 = (bf16[256,256]{1,0:T(8,128)(2,1)S(1)}, bf16[256,256]{1,0:T(8,128)(2,1)S(1)}, u32[]{:S(2)}, u32[]{:S(2)}) collective-permute-start(bf16[256,256]{1,0:T(8,128)(2,1)S(1)} %attend.7), channel_id=1, source_target_pairs={{0,12},{1,13},{2,14},{3,15},{4,8},{5,9},{6,10},{7,11},{8,4},{9,5},... | collective-permute-start | bytes 393224 | tf_op jit(solution)/shard_map/ppermute | solution.py:363
  26.4 0.0 collective-permute-done.3.refs_2_
  26.4 0.0 collective-permute-done.2.refs_1_
  26.4 2.8 %collective-permute-done.5.refs_3_ = bf16[256,256]{1,0:T(8,128)(2,1)S(1)} collective-permute-done((bf16[256,256]{1,0:T(8,128)(2,1)S(1)}, bf16[256,256]{1,0:T(8,128)(2,1)S(1)}, u32[]{:S(2)}, u32[]{:S(2)}) %collective-permute-start.5) | collective-permute-done | bytes 131104 | tf_op jit(solution)/shard_map/ppermute | solution.py:363
  29.3 0.1 pick.1.refs_1_
  29.4 0.1 collective-permute-start.10
  29.5 0.5 collective-permute-start.11
  30.0 0.5 collective-permute-start.6
  30.6 1.0 %route.1 = (s32[256,2]{1,0:T(8,128)S(1)}, bf16[192,256]{1,0:T(8,128)(2,1)S(1)}, bf16[192,256]{1,0:T(8,128)(2,1)S(1)}, bf16[192,256]{1,0:T(8,128)(2,1)S(1)}, bf16...) custom-call(s32[2,256]{1,0:T(2,128)S(1)} %bitcast.38), custom_call_target="tpu_custom_call" | custom-call | tf_op jit(solution)/shard_map/route/pallas_call | solution.py:177
  31.5 0.1 collective-permute-start.7
  31.6 3.9 %collective-permute-done.6.refs_2_ = bf16[256,256]{1,0:T(8,128)(2,1)S(1)} collective-permute-done((bf16[256,256]{1,0:T(8,128)(2,1)S(1)}, bf16[256,256]{1,0:T(8,128)(2,1)S(1)}, u32[]{:S(2)}, u32[]{:S(2)}) %collective-permute-start.6) | collective-permute-done | bytes 131104 | tf_op jit(solution)/shard_map/ppermute | solution.py:363
  35.5 1.3 %collective-permute-done.8.refs_4_ = bf16[256,256]{1,0:T(8,128)(2,1)S(1)} collective-permute-done((bf16[256,256]{1,0:T(8,128)(2,1)S(1)}, bf16[256,256]{1,0:T(8,128)(2,1)S(1)}, u32[]{:S(2)}, u32[]{:S(2)}) %collective-permute-start.8) | collective-permute-done | bytes 131104 | tf_op jit(solution)/shard_map/ppermute | solution.py:363
  36.9 0.0 copy-start
  36.9 0.0 copy-start.1
  36.9 1.1 %state.1 = (bf16[256,1024]{1,0:T(8,128)(2,1)S(1)}, bf16[192,512]{1,0:T(8,128)(2,1)S(1)}, bf16[192,256]{1,0:T(8,128)(2,1)S(1)}, bf16[192,512]{1,0:T(8,128)(2,1)S(1)}) custom-call(bf16[256,1024]{1,0:T(8,128)(2,1)S(1)} %copy-done.2, bf16[256,256]{1,0:T(8,128)(2,1)S(1)} %pick.1.refs_1_, bf16[256,256]{1,0:T(8,128)(2,1)S(1)} %collective-permute-done.6.refs_2_, ...), custom_call_target="tpu_custom_call" | custom-call | tf_op jit(solution)/shard_map/state/pallas_call | solution.py:210
  38.0 3.4 %collective-permute-start.12 = (bf16[192,256]{1,0:T(8,128)(2,1)S(1)}, bf16[192,256]{1,0:T(8,128)(2,1)S(1)}, u32[]{:S(2)}, u32[]{:S(2)}) collective-permute-start(bf16[192,256]{1,0:T(8,128)(2,1)S(1)} %get-tuple-element.73), channel_id=1, source_target_pairs={{0,12},{1,13},{2,14},{3,15},{4,8},{5,9},{6,10},{7,11},{8,4},{9,5},... | collective-permute-start | bytes 294920 | tf_op jit(solution)/shard_map/ppermute | solution.py:363
  41.4 1.1 %collective-permute-start.18 = (bf16[192,512]{1,0:T(8,128)(2,1)S(1)}, bf16[192,512]{1,0:T(8,128)(2,1)S(1)}, u32[]{:S(2)}, u32[]{:S(2)}) collective-permute-start(bf16[192,512]{1,0:T(8,128)(2,1)S(1)} %get-tuple-element.81), channel_id=1, source_target_pairs={{0,4},{1,5},{2,6},{3,7},{4,0},{5,1},{6,2},{7,3},{8,12},{9,13},{10,... | collective-permute-start | bytes 589832 | tf_op jit(solution)/shard_map/ppermute | solution.py:363
  42.4 0.5 home.1
  43.0 1.0 %expert.3 = (f32[2,192,256]{2,1,0:T(8,128)S(1)}, bf16[2,192,256]{2,1,0:T(8,128)(2,1)S(1)}) custom-call(bf16[192,512]{1,0:T(8,128)(2,1)S(1)} %get-tuple-element.69.refs_0_, bf16[192,512]{1,0:T(8,128)(2,1)S(1)} %get-tuple-element.70.refs_1_, bf16[1024,1024]{1,0:T(8,128)(2,1)S(1)} %bitcast.31, bf16[1024,1024]{1,0:T(8,128)(2,1)S(1)} %bitcast.34), custom_call_target="tpu_custom_call" | custom-call | tf_op jit(solution)/shard_map/expert/pallas_call | solution.py:289
  44.0 1.6 %collective-permute-done.12.refs_0_ = bf16[192,256]{1,0:T(8,128)(2,1)S(1)} collective-permute-done((bf16[192,256]{1,0:T(8,128)(2,1)S(1)}, bf16[192,256]{1,0:T(8,128)(2,1)S(1)}, u32[]{:S(2)}, u32[]{:S(2)}) %collective-permute-start.12) | collective-permute-done | bytes 98336 | tf_op jit(solution)/shard_map/ppermute | solution.py:363
  45.6 0.5 collective-permute-start.14
  46.1 8.2 %collective-permute-done.16.refs_0_ = bf16[192,512]{1,0:T(8,128)(2,1)S(1)} collective-permute-done((bf16[192,512]{1,0:T(8,128)(2,1)S(1)}, bf16[192,512]{1,0:T(8,128)(2,1)S(1)}, u32[]{:S(2)}, u32[]{:S(2)}) %collective-permute-start.16) | collective-permute-done | bytes 196640 | tf_op jit(solution)/shard_map/ppermute | solution.py:363
  54.3 0.5 collective-permute-start.19
  54.9 0.9 %collective-permute-done.17.refs_1_ = bf16[192,512]{1,0:T(8,128)(2,1)S(1)} collective-permute-done((bf16[192,512]{1,0:T(8,128)(2,1)S(1)}, bf16[192,512]{1,0:T(8,128)(2,1)S(1)}, u32[]{:S(2)}, u32[]{:S(2)}) %collective-permute-start.17) | collective-permute-done | bytes 196640 | tf_op jit(solution)/shard_map/ppermute | solution.py:363
  55.8 0.3 collective-permute-done.19.refs_3_
  56.0 1.8 %expert.4 = (f32[2,384,256]{2,1,0:T(8,128)S(1)}, bf16[2,384,256]{2,1,0:T(8,128)(2,1)S(1)}) custom-call(bf16[192,512]{1,0:T(8,128)(2,1)S(1)} %collective-permute-done.16.refs_0_, bf16[192,512]{1,0:T(8,128)(2,1)S(1)} %collective-permute-done.17.refs_1_, bf16[192,512]{1,0:T(8,128)(2,1)S(1)} %collective-permute-done.18.refs_2_, ...), custom_call_target="tpu_custom_call" | custom-call | tf_op jit(solution)/shard_map/expert/pallas_call | solution.py:289
  57.9 0.3 collective-permute-start.20
  58.2 0.6 collective-permute-start.15
  58.8 0.5 collective-permute-start.22
  59.3 0.4 collective-permute-done.20
  59.7 0.1 convert_add_fusion
  59.8 1.2 %collective-permute-start.25 = (bf16[192,256]{1,0:T(8,128)(2,1)S(1)}, bf16[192,256]{1,0:T(8,128)(2,1)S(1)}, u32[]{:S(2)}, u32[]{:S(2)}) collective-permute-start(bf16[192,256]{1,0:T(8,128)(2,1)S(1)} %fusion.4), channel_id=1, source_target_pairs={{0,2},{1,3},{2,0},{3,1},{4,6},{5,7},{6,4},{7,5},{8,10},{9,11},{10,... | collective-permute-start | bytes 294920 | tf_op jit(solution)/shard_map/ppermute | solution.py:363
  61.0 1.0 %expert.5 = (f32[2,192,256]{2,1,0:T(8,128)S(1)}, bf16[2,192,256]{2,1,0:T(8,128)(2,1)S(1)}) custom-call(bf16[192,256]{1,0:T(8,128)(2,1)S(1)} %collective-permute-done.12.refs_0_, bf16[192,256]{1,0:T(8,128)(2,1)S(1)} %collective-permute-done.14.refs_1_, bf16[192,256]{1,0:T(8,128)(2,1)S(1)} %collective-permute-done.21.refs_2_, ...), custom_call_target="tpu_custom_call" | custom-call | tf_op jit(solution)/shard_map/expert/pallas_call | solution.py:289
  62.0 0.1 collective-permute-start.26
  62.1 1.0 %collective-permute-start.24 = (bf16[192,256]{1,0:T(8,128)(2,1)S(1)}, bf16[192,256]{1,0:T(8,128)(2,1)S(1)}, u32[]{:S(2)}, u32[]{:S(2)}) collective-permute-start(bf16[192,256]{1,0:T(8,128)(2,1)S(1)} %get-tuple-element.95), channel_id=1, source_target_pairs={{0,6},{1,7},{2,4},{3,5},{4,2},{5,3},{6,0},{7,1},{8,14},{9,15},{10,... | collective-permute-start | bytes 294920 | tf_op jit(solution)/shard_map/ppermute | solution.py:363
  63.2 1.6 %collective-permute-start.23 = (bf16[192,256]{1,0:T(8,128)(2,1)S(1)}, bf16[192,256]{1,0:T(8,128)(2,1)S(1)}, u32[]{:S(2)}, u32[]{:S(2)}) collective-permute-start(bf16[192,256]{1,0:T(8,128)(2,1)S(1)} %get-tuple-element.96), channel_id=1, source_target_pairs={{0,4},{1,5},{2,6},{3,7},{4,0},{5,1},{6,2},{7,3},{8,12},{9,13},{10,... | collective-permute-start | bytes 294920 | tf_op jit(solution)/shard_map/ppermute | solution.py:363
  64.8 0.5 collective-permute-done.25
  65.3 0.5 collective-permute-start.28
  65.9 0.1 collective-permute-start.27
  66.0 4.4 %collective-permute-done.28 = bf16[192,256]{1,0:T(8,128)(2,1)S(1)} collective-permute-done((bf16[192,256]{1,0:T(8,128)(2,1)S(1)}, bf16[192,256]{1,0:T(8,128)(2,1)S(1)}, u32[]{:S(2)}, u32[]{:S(2)}) %collective-permute-start.28) | collective-permute-done | bytes 98336 | tf_op jit(solution)/shard_map/ppermute | solution.py:363
  70.4 1.5 %collective-permute-start.29 = (bf16[192,256]{1,0:T(8,128)(2,1)S(1)}, bf16[192,256]{1,0:T(8,128)(2,1)S(1)}, u32[]{:S(2)}, u32[]{:S(2)}) collective-permute-start(bf16[192,256]{1,0:T(8,128)(2,1)S(1)} %fusion.1), channel_id=1, source_target_pairs={{0,12},{1,13},{2,14},{3,15},{4,8},{5,9},{6,10},{7,11},{8,4},{9,5},... | collective-permute-start | bytes 294920 | tf_op jit(solution)/shard_map/ppermute | solution.py:363
  71.9 0.2 combine.4.base
  72.2 0.2 combine.5.base
  72.4 1.2 %collective-permute-done.27.refs_0_ = bf16[192,256]{1,0:T(8,128)(2,1)S(1)} collective-permute-done((bf16[192,256]{1,0:T(8,128)(2,1)S(1)}, bf16[192,256]{1,0:T(8,128)(2,1)S(1)}, u32[]{:S(2)}, u32[]{:S(2)}) %collective-permute-start.27) | collective-permute-done | bytes 98336 | tf_op jit(solution)/shard_map/ppermute | solution.py:363
  73.6 0.2 combine.6.base
  73.9 3.1 %collective-permute-done.29.refs_0_ = bf16[192,256]{1,0:T(8,128)(2,1)S(1)} collective-permute-done((bf16[192,256]{1,0:T(8,128)(2,1)S(1)}, bf16[192,256]{1,0:T(8,128)(2,1)S(1)}, u32[]{:S(2)}, u32[]{:S(2)}) %collective-permute-start.29) | collective-permute-done | bytes 98336 | tf_op jit(solution)/shard_map/ppermute | solution.py:363
  77.0 0.9 %combine.7 = bf16[256,256]{1,0:T(8,128)(2,1)} custom-call(f32[256,2]{1,0:T(8,128)S(1)} %get-tuple-element.65.gates, f32[256,256]{1,0:T(8,128)S(1)} %combine.6.base, bf16[256,192]{1,0:T(8,128)(2,1)S(1)} %get-tuple-element.93.first, bf16[256,192]{1,0:T(8,128)(2,1)S(1)} %get-tuple-element.94.second, bf16[192,256]{1,0:T(8,128)(2,1)S(1)} %collective-permute-done.29.refs_0_), custom_call_target="tpu_custom_call" | custom-call | tf_op jit(solution)/shard_map/combine/pallas_call | solution.py:315
  (34 shorter events, 0.3 us)
Async XLA Ops:
  0.0 29.5 %collective-permute-start.9 = (bf16[256,1024]{1,0:T(8,128)(2,1)}, bf16[256,1024]{1,0:T(8,128)(2,1)S(1)}, u32[]{:S(2)}, u32[]{:S(2)}) collective-permute-start(bf16[256,1024]{1,0:T(8,128)(2,1)} %refs_5_), channel_id=1, source_target_pairs={{0,2},{1,3},{2,0},{3,1},{4,6},{5,7},{6,4},{7,5},{8,10},{9,11},{10,... | collective-permute-start | bytes 1572872 | tf_op jit(solution)/shard_map/ppermute | solution.py:363
  4.8 24.7 %copy-start.3 = (bf16[256,1024]{1,0:T(8,128)(2,1)S(1)}, bf16[256,1024]{1,0:T(8,128)(2,1)}, u32[]{:S(2)}) copy-start(bf16[256,1024]{1,0:T(8,128)(2,1)} %refs_5_) | copy-start | bytes 1572868
  4.8 25.8 %copy-start.5 = (s32[256,2]{0,1:T(2,128)S(1)}, s32[256,2]{0,1:T(2,128)}, u32[]{:S(2)}) copy-start(s32[256,2]{0,1:T(2,128)} %param.15) | copy-start | bytes 6148
  4.8 32.1 %copy-start.2 = (bf16[256,1024]{1,0:T(8,128)(2,1)S(1)}, bf16[256,1024]{1,0:T(8,128)(2,1)}, u32[]{:S(2)}) copy-start(bf16[256,1024]{1,0:T(8,128)(2,1)} %refs_0_.1) | copy-start | bytes 1572868
  4.8 8.8 %collective-permute-start.1 = (bf16[256,256]{1,0:T(8,128)(2,1)S(1)}, bf16[256,256]{1,0:T(8,128)(2,1)S(1)}, u32[]{:S(2)}, u32[]{:S(2)}) collective-permute-start(bf16[256,256]{1,0:T(8,128)(2,1)S(1)} %get-tuple-element.50.queries), channel_id=1, source_target_pairs={{0,8},{1,9},{2,10},{3,11},{4,12},{5,13},{6,14},{7,15},{8,0},{9,1},... | collective-permute-start | bytes 393224 | tf_op jit(solution)/shard_map/ppermute | solution.py:363
  7.4 10.9 %collective-permute-start = (bf16[256,256]{1,0:T(8,128)(2,1)S(1)}, bf16[256,256]{1,0:T(8,128)(2,1)S(1)}, u32[]{:S(2)}, u32[]{:S(2)}) collective-permute-start(bf16[256,256]{1,0:T(8,128)(2,1)S(1)} %get-tuple-element.50.queries), channel_id=1, source_target_pairs={{0,4},{1,5},{2,6},{3,7},{4,0},{5,1},{6,2},{7,3},{8,12},{9,13},{10,... | collective-permute-start | bytes 393224 | tf_op jit(solution)/shard_map/ppermute | solution.py:363
  13.6 5.5 %collective-permute-start.4 = (bf16[256,256]{1,0:T(8,128)(2,1)S(1)}, bf16[256,256]{1,0:T(8,128)(2,1)S(1)}, u32[]{:S(2)}, u32[]{:S(2)}) collective-permute-start(bf16[256,256]{1,0:T(8,128)(2,1)S(1)} %collective-permute-done.1.queries), channel_id=1, source_target_pairs={{0,4},{1,5},{2,6},{3,7},{4,0},{5,1},{6,2},{7,3},{8,12},{9,13},{10,... | collective-permute-start | bytes 393224 | tf_op jit(solution)/shard_map/ppermute | solution.py:363
  14.9 11.5 %collective-permute-start.3 = (bf16[256,256]{1,0:T(8,128)(2,1)S(1)}, bf16[256,256]{1,0:T(8,128)(2,1)S(1)}, u32[]{:S(2)}, u32[]{:S(2)}) collective-permute-start(bf16[256,256]{1,0:T(8,128)(2,1)S(1)} %attend.5), channel_id=1, source_target_pairs={{0,8},{1,9},{2,10},{3,11},{4,12},{5,13},{6,14},{7,15},{8,0},{9,1},... | collective-permute-start | bytes 393224 | tf_op jit(solution)/shard_map/ppermute | solution.py:363
  19.1 7.4 %collective-permute-start.2 = (bf16[256,256]{1,0:T(8,128)(2,1)S(1)}, bf16[256,256]{1,0:T(8,128)(2,1)S(1)}, u32[]{:S(2)}, u32[]{:S(2)}) collective-permute-start(bf16[256,256]{1,0:T(8,128)(2,1)S(1)} %attend.6), channel_id=1, source_target_pairs={{0,4},{1,5},{2,6},{3,7},{4,0},{5,1},{6,2},{7,3},{8,12},{9,13},{10,... | collective-permute-start | bytes 393224 | tf_op jit(solution)/shard_map/ppermute | solution.py:363
  19.9 22.6 %copy-start.4 = (bf16[1024,4]{0,1:T(4,128)(2,1)S(1)}, bf16[1024,4]{0,1:T(4,128)(2,1)}, u32[]{:S(2)}) copy-start(bf16[1024,4]{0,1:T(4,128)(2,1)} %param.14) | copy-start | bytes 24580
  19.9 9.4 %collective-permute-start.5 = (bf16[256,256]{1,0:T(8,128)(2,1)S(1)}, bf16[256,256]{1,0:T(8,128)(2,1)S(1)}, u32[]{:S(2)}, u32[]{:S(2)}) collective-permute-start(bf16[256,256]{1,0:T(8,128)(2,1)S(1)} %attend.7), channel_id=1, source_target_pairs={{0,12},{1,13},{2,14},{3,15},{4,8},{5,9},{6,10},{7,11},{8,4},{9,5},... | collective-permute-start | bytes 393224 | tf_op jit(solution)/shard_map/ppermute | solution.py:363
  29.4 7.4 %collective-permute-start.10 = (bf16[256,1024]{1,0:T(8,128)(2,1)S(1)}, bf16[256,1024]{1,0:T(8,128)(2,1)S(1)}, u32[]{:S(2)}, u32[]{:S(2)}) collective-permute-start(bf16[256,1024]{1,0:T(8,128)(2,1)S(1)} %copy-done.3), channel_id=1, source_target_pairs={{0,1},{1,0},{2,3},{3,2},{4,5},{5,4},{6,7},{7,6},{8,9},{9,8},{10,11... | collective-permute-start | bytes 1572872 | tf_op jit(solution)/shard_map/ppermute | solution.py:363
  29.5 7.3 %collective-permute-start.11 = (bf16[256,1024]{1,0:T(8,128)(2,1)S(1)}, bf16[256,1024]{1,0:T(8,128)(2,1)S(1)}, u32[]{:S(2)}, u32[]{:S(2)}) collective-permute-start(bf16[256,1024]{1,0:T(8,128)(2,1)S(1)} %collective-permute-done.9.refs_6_), channel_id=1, source_target_pairs={{0,1},{1,0},{2,3},{3,2},{4,5},{5,4},{6,7},{7,6},{8,9},{9,8},{10,11... | collective-permute-start | bytes 1572872 | tf_op jit(solution)/shard_map/ppermute | solution.py:363
  30.0 5.5 %collective-permute-start.6 = (bf16[256,256]{1,0:T(8,128)(2,1)S(1)}, bf16[256,256]{1,0:T(8,128)(2,1)S(1)}, u32[]{:S(2)}, u32[]{:S(2)}) collective-permute-start(bf16[256,256]{1,0:T(8,128)(2,1)S(1)} %pick.1.refs_1_), channel_id=1, source_target_pairs={{0,2},{1,3},{2,0},{3,1},{4,6},{5,7},{6,4},{7,5},{8,10},{9,11},{10,... | collective-permute-start | bytes 393224 | tf_op jit(solution)/shard_map/ppermute | solution.py:363
  31.5 4.0 %collective-permute-start.7 = (bf16[256,256]{1,0:T(8,128)(2,1)S(1)}, bf16[256,256]{1,0:T(8,128)(2,1)S(1)}, u32[]{:S(2)}, u32[]{:S(2)}) collective-permute-start(bf16[256,256]{1,0:T(8,128)(2,1)S(1)} %pick.1.refs_1_), channel_id=1, source_target_pairs={{0,1},{1,0},{2,3},{3,2},{4,5},{5,4},{6,7},{7,6},{8,9},{9,8},{10,11... | collective-permute-start | bytes 393224 | tf_op jit(solution)/shard_map/ppermute | solution.py:363
  35.5 1.3 %collective-permute-start.8 = (bf16[256,256]{1,0:T(8,128)(2,1)S(1)}, bf16[256,256]{1,0:T(8,128)(2,1)S(1)}, u32[]{:S(2)}, u32[]{:S(2)}) collective-permute-start(bf16[256,256]{1,0:T(8,128)(2,1)S(1)} %collective-permute-done.6.refs_2_), channel_id=1, source_target_pairs={{0,1},{1,0},{2,3},{3,2},{4,5},{5,4},{6,7},{7,6},{8,9},{9,8},{10,11... | collective-permute-start | bytes 393224 | tf_op jit(solution)/shard_map/ppermute | solution.py:363
  36.9 6.1 %copy-start = (bf16[1,1024,1024]{2,1,0:T(8,128)(2,1)S(1)}, bf16[1,1024,1024]{2,1,0:T(8,128)(2,1)}, u32[]{:S(2)}) copy-start(bf16[1,1024,1024]{2,1,0:T(8,128)(2,1)} %param.16) | copy-start | bytes 6291460
  36.9 6.1 %copy-start.1 = (bf16[1,1024,1024]{2,1,0:T(8,128)(2,1)S(1)}, bf16[1,1024,1024]{2,1,0:T(8,128)(2,1)}, u32[]{:S(2)}) copy-start(bf16[1,1024,1024]{2,1,0:T(8,128)(2,1)} %param.17) | copy-start | bytes 6291460
  38.0 7.6 %collective-permute-start.12 = (bf16[192,256]{1,0:T(8,128)(2,1)S(1)}, bf16[192,256]{1,0:T(8,128)(2,1)S(1)}, u32[]{:S(2)}, u32[]{:S(2)}) collective-permute-start(bf16[192,256]{1,0:T(8,128)(2,1)S(1)} %get-tuple-element.73), channel_id=1, source_target_pairs={{0,12},{1,13},{2,14},{3,15},{4,8},{5,9},{6,10},{7,11},{8,4},{9,5},... | collective-permute-start | bytes 294920 | tf_op jit(solution)/shard_map/ppermute | solution.py:363
  41.3 13.0 %collective-permute-start.16 = (bf16[192,512]{1,0:T(8,128)(2,1)S(1)}, bf16[192,512]{1,0:T(8,128)(2,1)S(1)}, u32[]{:S(2)}, u32[]{:S(2)}) collective-permute-start(bf16[192,512]{1,0:T(8,128)(2,1)S(1)} %get-tuple-element.78), channel_id=1, source_target_pairs={{0,8},{1,9},{2,10},{3,11},{4,12},{5,13},{6,14},{7,15},{8,0},{9,1},... | collective-permute-start | bytes 589832 | tf_op jit(solution)/shard_map/ppermute | solution.py:363
  41.4 13.0 %collective-permute-start.18 = (bf16[192,512]{1,0:T(8,128)(2,1)S(1)}, bf16[192,512]{1,0:T(8,128)(2,1)S(1)}, u32[]{:S(2)}, u32[]{:S(2)}) collective-permute-start(bf16[192,512]{1,0:T(8,128)(2,1)S(1)} %get-tuple-element.81), channel_id=1, source_target_pairs={{0,4},{1,5},{2,6},{3,7},{4,0},{5,1},{6,2},{7,3},{8,12},{9,13},{10,... | collective-permute-start | bytes 589832 | tf_op jit(solution)/shard_map/ppermute | solution.py:363
  45.6 9.3 %collective-permute-start.13 = (bf16[2,192,256]{2,1,0:T(8,128)(2,1)S(1)}, bf16[2,192,256]{2,1,0:T(8,128)(2,1)S(1)}, u32[]{:S(2)}, u32[]{:S(2)}) collective-permute-start(bf16[2,192,256]{2,1,0:T(8,128)(2,1)S(1)} %get-tuple-element.74), channel_id=1, source_target_pairs={{0,1},{1,0},{2,3},{3,2},{4,5},{5,4},{6,7},{7,6},{8,9},{9,8},{10,11... | collective-permute-start | bytes 589832 | tf_op jit(solution)/shard_map/ppermute | solution.py:363
  45.6 9.3 %collective-permute-start.14 = (bf16[192,256]{1,0:T(8,128)(2,1)S(1)}, bf16[192,256]{1,0:T(8,128)(2,1)S(1)}, u32[]{:S(2)}, u32[]{:S(2)}) collective-permute-start(bf16[192,256]{1,0:T(8,128)(2,1)S(1)} %collective-permute-done.12.refs_0_), channel_id=1, source_target_pairs={{0,2},{1,3},{2,0},{3,1},{4,6},{5,7},{6,4},{7,5},{8,10},{9,11},{10,... | collective-permute-start | bytes 294920 | tf_op jit(solution)/shard_map/ppermute | solution.py:363
  54.3 1.4 %collective-permute-start.17 = (bf16[192,512]{1,0:T(8,128)(2,1)S(1)}, bf16[192,512]{1,0:T(8,128)(2,1)S(1)}, u32[]{:S(2)}, u32[]{:S(2)}) collective-permute-start(bf16[192,512]{1,0:T(8,128)(2,1)S(1)} %collective-permute-done.16.refs_0_), channel_id=1, source_target_pairs={{0,1},{1,0},{2,3},{3,2},{4,5},{5,4},{6,7},{7,6},{8,9},{9,8},{10,11... | collective-permute-start | bytes 589832 | tf_op jit(solution)/shard_map/ppermute | solution.py:363
  54.3 1.7 %collective-permute-start.19 = (bf16[192,512]{1,0:T(8,128)(2,1)S(1)}, bf16[192,512]{1,0:T(8,128)(2,1)S(1)}, u32[]{:S(2)}, u32[]{:S(2)}) collective-permute-start(bf16[192,512]{1,0:T(8,128)(2,1)S(1)} %collective-permute-done.18.refs_2_), channel_id=1, source_target_pairs={{0,1},{1,0},{2,3},{3,2},{4,5},{5,4},{6,7},{7,6},{8,9},{9,8},{10,11... | collective-permute-start | bytes 589832 | tf_op jit(solution)/shard_map/ppermute | solution.py:363
  57.9 1.8 %collective-permute-start.20 = (bf16[2,384,256]{2,1,0:T(8,128)(2,1)S(1)}, bf16[2,384,256]{2,1,0:T(8,128)(2,1)S(1)}, u32[]{:S(2)}, u32[]{:S(2)}) collective-permute-start(bf16[2,384,256]{2,1,0:T(8,128)(2,1)S(1)} %get-tuple-element.83), channel_id=1, source_target_pairs={{0,1},{1,0},{2,3},{3,2},{4,5},{5,4},{6,7},{7,6},{8,9},{9,8},{10,11... | collective-permute-start | bytes 1179656 | tf_op jit(solution)/shard_map/ppermute | solution.py:363
  58.2 13.7 %collective-permute-start.15 = (bf16[192,256]{1,0:T(8,128)(2,1)S(1)}, bf16[192,256]{1,0:T(8,128)(2,1)S(1)}, u32[]{:S(2)}, u32[]{:S(2)}) collective-permute-start(bf16[192,256]{1,0:T(8,128)(2,1)S(1)} %get-tuple-element.75), channel_id=1, source_target_pairs={{0,2},{1,3},{2,0},{3,1},{4,6},{5,7},{6,4},{7,5},{8,10},{9,11},{10,... | collective-permute-start | bytes 294920 | tf_op jit(solution)/shard_map/ppermute | solution.py:363
  58.8 2.2 %collective-permute-start.21 = (bf16[192,256]{1,0:T(8,128)(2,1)S(1)}, bf16[192,256]{1,0:T(8,128)(2,1)S(1)}, u32[]{:S(2)}, u32[]{:S(2)}) collective-permute-start(bf16[192,256]{1,0:T(8,128)(2,1)S(1)} %collective-permute-done.12.refs_0_), channel_id=1, source_target_pairs={{0,1},{1,0},{2,3},{3,2},{4,5},{5,4},{6,7},{7,6},{8,9},{9,8},{10,11... | collective-permute-start | bytes 294920 | tf_op jit(solution)/shard_map/ppermute | solution.py:363
  58.8 2.2 %collective-permute-start.22 = (bf16[192,256]{1,0:T(8,128)(2,1)S(1)}, bf16[192,256]{1,0:T(8,128)(2,1)S(1)}, u32[]{:S(2)}, u32[]{:S(2)}) collective-permute-start(bf16[192,256]{1,0:T(8,128)(2,1)S(1)} %collective-permute-done.14.refs_1_), channel_id=1, source_target_pairs={{0,1},{1,0},{2,3},{3,2},{4,5},{5,4},{6,7},{7,6},{8,9},{9,8},{10,11... | collective-permute-start | bytes 294920 | tf_op jit(solution)/shard_map/ppermute | solution.py:363
  59.8 5.5 %collective-permute-start.25 = (bf16[192,256]{1,0:T(8,128)(2,1)S(1)}, bf16[192,256]{1,0:T(8,128)(2,1)S(1)}, u32[]{:S(2)}, u32[]{:S(2)}) collective-permute-start(bf16[192,256]{1,0:T(8,128)(2,1)S(1)} %fusion.4), channel_id=1, source_target_pairs={{0,2},{1,3},{2,0},{3,1},{4,6},{5,7},{6,4},{7,5},{8,10},{9,11},{10,... | collective-permute-start | bytes 294920 | tf_op jit(solution)/shard_map/ppermute | solution.py:363
  62.0 2.7 %collective-permute-start.26 = (bf16[2,192,256]{2,1,0:T(8,128)(2,1)S(1)}, bf16[2,192,256]{2,1,0:T(8,128)(2,1)S(1)}, u32[]{:S(2)}, u32[]{:S(2)}) collective-permute-start(bf16[2,192,256]{2,1,0:T(8,128)(2,1)S(1)} %get-tuple-element.87), channel_id=1, source_target_pairs={{0,1},{1,0},{2,3},{3,2},{4,5},{5,4},{6,7},{7,6},{8,9},{9,8},{10,11... | collective-permute-start | bytes 589832 | tf_op jit(solution)/shard_map/ppermute | solution.py:363
  62.1 10.0 %collective-permute-start.24 = (bf16[192,256]{1,0:T(8,128)(2,1)S(1)}, bf16[192,256]{1,0:T(8,128)(2,1)S(1)}, u32[]{:S(2)}, u32[]{:S(2)}) collective-permute-start(bf16[192,256]{1,0:T(8,128)(2,1)S(1)} %get-tuple-element.95), channel_id=1, source_target_pairs={{0,6},{1,7},{2,4},{3,5},{4,2},{5,3},{6,0},{7,1},{8,14},{9,15},{10,... | collective-permute-start | bytes 294920 | tf_op jit(solution)/shard_map/ppermute | solution.py:363
  63.2 9.0 %collective-permute-start.23 = (bf16[192,256]{1,0:T(8,128)(2,1)S(1)}, bf16[192,256]{1,0:T(8,128)(2,1)S(1)}, u32[]{:S(2)}, u32[]{:S(2)}) collective-permute-start(bf16[192,256]{1,0:T(8,128)(2,1)S(1)} %get-tuple-element.96), channel_id=1, source_target_pairs={{0,4},{1,5},{2,6},{3,7},{4,0},{5,1},{6,2},{7,3},{8,12},{9,13},{10,... | collective-permute-start | bytes 294920 | tf_op jit(solution)/shard_map/ppermute | solution.py:363
  65.3 5.1 %collective-permute-start.28 = (bf16[192,256]{1,0:T(8,128)(2,1)S(1)}, bf16[192,256]{1,0:T(8,128)(2,1)S(1)}, u32[]{:S(2)}, u32[]{:S(2)}) collective-permute-start(bf16[192,256]{1,0:T(8,128)(2,1)S(1)} %fusion.5), channel_id=1, source_target_pairs={{0,2},{1,3},{2,0},{3,1},{4,6},{5,7},{6,4},{7,5},{8,10},{9,11},{10,... | collective-permute-start | bytes 294920 | tf_op jit(solution)/shard_map/ppermute | solution.py:363
  65.9 7.7 %collective-permute-start.27 = (bf16[192,256]{1,0:T(8,128)(2,1)S(1)}, bf16[192,256]{1,0:T(8,128)(2,1)S(1)}, u32[]{:S(2)}, u32[]{:S(2)}) collective-permute-start(bf16[192,256]{1,0:T(8,128)(2,1)S(1)} %fusion.3), channel_id=1, source_target_pairs={{0,8},{1,9},{2,10},{3,11},{4,12},{5,13},{6,14},{7,15},{8,0},{9,1},... | collective-permute-start | bytes 294920 | tf_op jit(solution)/shard_map/ppermute | solution.py:363
  70.4 6.5 %collective-permute-start.29 = (bf16[192,256]{1,0:T(8,128)(2,1)S(1)}, bf16[192,256]{1,0:T(8,128)(2,1)S(1)}, u32[]{:S(2)}, u32[]{:S(2)}) collective-permute-start(bf16[192,256]{1,0:T(8,128)(2,1)S(1)} %fusion.1), channel_id=1, source_target_pairs={{0,12},{1,13},{2,14},{3,15},{4,8},{5,9},{6,10},{7,11},{8,4},{9,5},... | collective-permute-start | bytes 294920 | tf_op jit(solution)/shard_map/ppermute | solution.py:363

commit v16 on v15

--- a/solution.py
+++ b/solution.py
@@ -440,13 +440,13 @@
                 earlier.append(pieces[-1])
                 wait = pieces[-1]
         home[0] = send_home(0, own_sum, wait)
-        turns = [[k for k in sends if k < groups - 1], [groups - 1]] if groups > 2 else [sends]
+        turns = [[groups - 1], [k for k in sends if k < groups - 1]] if groups > 2 else [sends]
         for turn in turns:
             blocks, orders = [], []
             for k in turn:
                 pieces, places = relays[k]
-                if started is not None:
-                    pieces = [after(piece, started) for piece in pieces]
+                if started is None and len(turns) > 1:
+                    pieces = [after(piece, arrived[turns[1][0]]) for piece in pieces]
                 pieces = pieces + [hop(piece, 0, 1) for piece in pieces]
                 places = places + [index ^ 1 for index in places]
                 blocks.append(pieces)
@@ -460,18 +460,19 @@
                 for i, k in enumerate(turn):
                     rows = summed[:, i * slots : (i + 1) * slots]
                     if k in far:
-                        crossed = [hop(rows[j].astype(BF16), 0, 2 * j) for j in range(1, pairs)]
-                        crossing[k] = [rows[0]] + crossed
+                        leaves = [rows[j].astype(BF16) for j in range(1, pairs)]
+                        earlier = earlier + leaves
+                        crossing[k] = [rows[0]] + [hop(part, 0, 2 * j) for j, part in enumerate(leaves, 1)]
                     else:
                         near = k, rows
         for k, (total, *crossed) in crossing.items():
             for part in crossed:
-                total += (part if k == groups - 1 else after(part, summed)).astype(F32)
+                total += (after(part, summed) if k == groups - 1 else part).astype(F32)
             total = total.astype(BF16)
             home[k] = [hop(total, k, 0)]
         if sends:
             home[near[0]] = send_home(near[0], after(near[1], give))
-        order = [0] + sorted(sends)
+        order = sorted(sends, key=lambda k: (k == 1, -k)) + [0]
     else:
         mine = spread(leaving[0])
         home[0] = send_home(0, sum_cores(*expert([[0, 1]], [[mine, hop(mine, 0, 1)]])))

time: 78 us -> 81.8 us (1.049)
  starting transfers between devices: 31.2 us -> 35.8 us
  waiting for transfers between devices: 32.6 us -> 31.7 us
    ppermute x30, starting transfers between devices: 31.2 us -> 35.8 us  [hop(): return lax.ppermute(value, ('expert', 'mp'), moves)]
    ppermute x30, waiting for transfers between devices: 32.6 us -> 31.7 us  [hop(): return lax.ppermute(value, ('expert', 'mp'), moves)]
  transfers between devices with their start and end apart: 30 -> 30, of which waited for: 13 -> 17; matrix products, arithmetic and copies ran while one was open for 0% -> 0% of each run, Pallas kernels for 12% -> 11%
where the time goes in v16:
time: 81.8 us; the launch traced here: 81.6 us
  starting transfers between devices  35.8 us (44%)
  waiting for transfers between devices  31.7 us (39%)
  Pallas kernels  12.7 us (16%)
  between operations  0.97 us (1%)
    ppermute x30, starting transfers between devices, hop(): return lax.ppermute(value, ('expert', 'mp'), moves)  35.8 us
    ppermute x30, waiting for transfers between devices, hop(): return lax.ppermute(value, ('expert', 'mp'), moves)  31.7 us
    pallas_call x3, Pallas kernels, run_expert(): pl.pallas_call(functools.partial(expert_kernel, tuple(map(tuple, orders))...  3.85 us
    pallas_call x4, Pallas kernels, attend(): pl.pallas_call(attend_kernel, in_specs=[WHOLE] * 2, out_specs=WHOLE, out_...  2.8 us
    pallas_call x1, Pallas kernels, ask(): pl.pallas_call(query_kernel, in_specs=[pl.BlockSpec(memory_space=pltpu.HB...  1.81 us
  transfers between devices with their start and end apart: 30, of which 17 were waited for; matrix products, arithmetic and copies ran while one was open for 0% of the time, Pallas kernels for 11%

profile of v16, /device:TPU:0, one launch (start us, length us, event | category | flops | bytes accessed | tf_op | source)
XLA Modules:
  0.0 81.6 jit_solution(5850357116241205748)
XLA Ops:
  0.0 2.9 %collective-permute-start.9 = (bf16[256,1024]{1,0:T(8,128)(2,1)}, bf16[256,1024]{1,0:T(8,128)(2,1)S(1)}, u32[]{:S(2)}, u32[]{:S(2)}) collective-permute-start(bf16[256,1024]{1,0:T(8,128)(2,1)} %refs_5_), channel_id=1, source_target_pairs={{0,2},{1,3},{2,0},{3,1},{4,6},{5,7},{6,4},{7,5},{8,10},{9,11},{10,... | collective-permute-start | bytes 1572872 | tf_op jit(solution)/shard_map/ppermute | solution.py:363
  2.9 1.8 %query.1 = (bf16[256,256]{1,0:T(8,128)(2,1)S(1)}, bf16[2,512,256]{2,1,0:T(8,128)(2,1)S(1)}) custom-call(bf16[256,1024]{1,0:T(8,128)(2,1)} %refs_0_.1, bf16[1024,256]{1,0:T(8,128)(2,1)} %weight.1, bf16[2,512,256]{2,1,0:T(8,128)(2,1)} %bitcast.39), custom_call_target="tpu_custom_call" | custom-call | tf_op jit(solution)/shard_map/query/pallas_call | solution.py:65
  4.8 0.0 copy-start.3
  4.8 0.0 copy-start.5
  4.8 0.0 copy-start.2
  4.8 2.6 %collective-permute-start.1 = (bf16[256,256]{1,0:T(8,128)(2,1)S(1)}, bf16[256,256]{1,0:T(8,128)(2,1)S(1)}, u32[]{:S(2)}, u32[]{:S(2)}) collective-permute-start(bf16[256,256]{1,0:T(8,128)(2,1)S(1)} %get-tuple-element.51.queries), channel_id=1, source_target_pairs={{0,8},{1,9},{2,10},{3,11},{4,12},{5,13},{6,14},{7,15},{8,0},{9,1},... | collective-permute-start | bytes 393224 | tf_op jit(solution)/shard_map/ppermute | solution.py:363
  7.4 1.6 %collective-permute-start = (bf16[256,256]{1,0:T(8,128)(2,1)S(1)}, bf16[256,256]{1,0:T(8,128)(2,1)S(1)}, u32[]{:S(2)}, u32[]{:S(2)}) collective-permute-start(bf16[256,256]{1,0:T(8,128)(2,1)S(1)} %get-tuple-element.51.queries), channel_id=1, source_target_pairs={{0,4},{1,5},{2,6},{3,7},{4,0},{5,1},{6,2},{7,3},{8,12},{9,13},{10,... | collective-permute-start | bytes 393224 | tf_op jit(solution)/shard_map/ppermute | solution.py:363
  9.0 0.7 attend.4.refs_0_
  9.7 3.9 %collective-permute-done.1.queries = bf16[256,256]{1,0:T(8,128)(2,1)S(1)} collective-permute-done((bf16[256,256]{1,0:T(8,128)(2,1)S(1)}, bf16[256,256]{1,0:T(8,128)(2,1)S(1)}, u32[]{:S(2)}, u32[]{:S(2)}) %collective-permute-start.1) | collective-permute-done | bytes 131104 | tf_op jit(solution)/shard_map/ppermute | solution.py:363
  13.6 0.6 collective-permute-start.4
  14.2 0.7 attend.5
  14.9 3.4 %collective-permute-start.3 = (bf16[256,256]{1,0:T(8,128)(2,1)S(1)}, bf16[256,256]{1,0:T(8,128)(2,1)S(1)}, u32[]{:S(2)}, u32[]{:S(2)}) collective-permute-start(bf16[256,256]{1,0:T(8,128)(2,1)S(1)} %attend.5), channel_id=1, source_target_pairs={{0,8},{1,9},{2,10},{3,11},{4,12},{5,13},{6,14},{7,15},{8,0},{9,1},... | collective-permute-start | bytes 393224 | tf_op jit(solution)/shard_map/ppermute | solution.py:363
  18.4 0.7 attend.6
  19.1 0.1 collective-permute-start.2
  19.1 0.7 attend.7
  19.9 0.0 copy-start.4
  19.9 5.9 %collective-permute-start.5 = (bf16[256,256]{1,0:T(8,128)(2,1)S(1)}, bf16[256,256]{1,0:T(8,128)(2,1)S(1)}, u32[]{:S(2)}, u32[]{:S(2)}) collective-permute-start(bf16[256,256]{1,0:T(8,128)(2,1)S(1)} %attend.7), channel_id=1, source_target_pairs={{0,12},{1,13},{2,14},{3,15},{4,8},{5,9},{6,10},{7,11},{8,4},{9,5},... | collective-permute-start | bytes 393224 | tf_op jit(solution)/shard_map/ppermute | solution.py:363
  26.4 2.8 %collective-permute-done.5.refs_3_ = bf16[256,256]{1,0:T(8,128)(2,1)S(1)} collective-permute-done((bf16[256,256]{1,0:T(8,128)(2,1)S(1)}, bf16[256,256]{1,0:T(8,128)(2,1)S(1)}, u32[]{:S(2)}, u32[]{:S(2)}) %collective-permute-start.5) | collective-permute-done | bytes 131104 | tf_op jit(solution)/shard_map/ppermute | solution.py:363
  29.3 0.1 pick.1.refs_1_
  29.4 0.1 collective-permute-start.10
  29.5 0.5 collective-permute-start.11
  30.0 0.5 collective-permute-start.6
  30.6 1.0 %route.1 = (s32[256,2]{1,0:T(8,128)S(1)}, bf16[192,256]{1,0:T(8,128)(2,1)S(1)}, bf16[192,256]{1,0:T(8,128)(2,1)S(1)}, bf16[192,256]{1,0:T(8,128)(2,1)S(1)}, bf16...) custom-call(s32[2,256]{1,0:T(2,128)S(1)} %bitcast.38), custom_call_target="tpu_custom_call" | custom-call | tf_op jit(solution)/shard_map/route/pallas_call | solution.py:177
  31.5 0.1 collective-permute-start.7
  31.6 3.9 %collective-permute-done.6.refs_2_ = bf16[256,256]{1,0:T(8,128)(2,1)S(1)} collective-permute-done((bf16[256,256]{1,0:T(8,128)(2,1)S(1)}, bf16[256,256]{1,0:T(8,128)(2,1)S(1)}, u32[]{:S(2)}, u32[]{:S(2)}) %collective-permute-start.6) | collective-permute-done | bytes 131104 | tf_op jit(solution)/shard_map/ppermute | solution.py:363
  35.5 1.3 %collective-permute-done.8.refs_4_ = bf16[256,256]{1,0:T(8,128)(2,1)S(1)} collective-permute-done((bf16[256,256]{1,0:T(8,128)(2,1)S(1)}, bf16[256,256]{1,0:T(8,128)(2,1)S(1)}, u32[]{:S(2)}, u32[]{:S(2)}) %collective-permute-start.8) | collective-permute-done | bytes 131104 | tf_op jit(solution)/shard_map/ppermute | solution.py:363
  36.9 1.1 %state.1 = (bf16[256,1024]{1,0:T(8,128)(2,1)S(1)}, bf16[192,512]{1,0:T(8,128)(2,1)S(1)}, bf16[192,256]{1,0:T(8,128)(2,1)S(1)}, bf16[192,512]{1,0:T(8,128)(2,1)S(1)}) custom-call(bf16[256,1024]{1,0:T(8,128)(2,1)S(1)} %copy-done.2, bf16[256,256]{1,0:T(8,128)(2,1)S(1)} %pick.1.refs_1_, bf16[256,256]{1,0:T(8,128)(2,1)S(1)} %collective-permute-done.6.refs_2_, ...), custom_call_target="tpu_custom_call" | custom-call | tf_op jit(solution)/shard_map/state/pallas_call | solution.py:210
  38.0 3.4 %collective-permute-start.12 = (bf16[192,256]{1,0:T(8,128)(2,1)S(1)}, bf16[192,256]{1,0:T(8,128)(2,1)S(1)}, u32[]{:S(2)}, u32[]{:S(2)}) collective-permute-start(bf16[192,256]{1,0:T(8,128)(2,1)S(1)} %get-tuple-element.70), channel_id=1, source_target_pairs={{0,12},{1,13},{2,14},{3,15},{4,8},{5,9},{6,10},{7,11},{8,4},{9,5},... | collective-permute-start | bytes 294920 | tf_op jit(solution)/shard_map/ppermute | solution.py:363
  41.4 0.5 home.1
  41.9 1.0 %expert.3 = (f32[2,192,256]{2,1,0:T(8,128)S(1)}, bf16[2,192,256]{2,1,0:T(8,128)(2,1)S(1)}) custom-call(bf16[192,512]{1,0:T(8,128)(2,1)S(1)} %get-tuple-element.73.refs_0_, bf16[192,512]{1,0:T(8,128)(2,1)S(1)} %get-tuple-element.74.refs_1_, bf16[1024,1024]{1,0:T(8,128)(2,1)S(1)} %bitcast.31, bf16[1024,1024]{1,0:T(8,128)(2,1)S(1)} %bitcast.34), custom_call_target="tpu_custom_call" | custom-call | tf_op jit(solution)/shard_map/expert/pallas_call | solution.py:289
  42.9 2.7 %collective-permute-done.12.refs_0_ = bf16[192,256]{1,0:T(8,128)(2,1)S(1)} collective-permute-done((bf16[192,256]{1,0:T(8,128)(2,1)S(1)}, bf16[192,256]{1,0:T(8,128)(2,1)S(1)}, u32[]{:S(2)}, u32[]{:S(2)}) %collective-permute-start.12) | collective-permute-done | bytes 98336 | tf_op jit(solution)/shard_map/ppermute | solution.py:363
  45.6 0.5 collective-permute-start.15
  46.1 5.9 %collective-permute-start.21 = (bf16[192,512]{1,0:T(8,128)(2,1)S(1)}, bf16[192,512]{1,0:T(8,128)(2,1)S(1)}, u32[]{:S(2)}, u32[]{:S(2)}) collective-permute-start(bf16[192,512]{1,0:T(8,128)(2,1)S(1)} %get-tuple-element.85), channel_id=1, source_target_pairs={{0,4},{1,5},{2,6},{3,7},{4,0},{5,1},{6,2},{7,3},{8,12},{9,13},{10,... | collective-permute-start | bytes 589832 | tf_op jit(solution)/shard_map/ppermute | solution.py:363
  52.0 2.4 %collective-permute-done.13.refs_0_ = bf16[192,512]{1,0:T(8,128)(2,1)S(1)} collective-permute-done((bf16[192,512]{1,0:T(8,128)(2,1)S(1)}, bf16[192,512]{1,0:T(8,128)(2,1)S(1)}, u32[]{:S(2)}, u32[]{:S(2)}) %collective-permute-start.13) | collective-permute-done | bytes 196640 | tf_op jit(solution)/shard_map/ppermute | solution.py:363
  54.4 0.5 collective-permute-start.17
  55.0 0.7 collective-permute-done.16.refs_2_
  55.7 0.2 collective-permute-done.17.refs_3_
  55.9 1.0 %expert.4 = (f32[2,192,256]{2,1,0:T(8,128)S(1)}, bf16[2,192,256]{2,1,0:T(8,128)(2,1)S(1)}) custom-call(bf16[192,256]{1,0:T(8,128)(2,1)S(1)} %collective-permute-done.12.refs_0_, bf16[192,256]{1,0:T(8,128)(2,1)S(1)} %collective-permute-done.15.refs_1_, bf16[192,256]{1,0:T(8,128)(2,1)S(1)} %collective-permute-done.16.refs_2_, ...), custom_call_target="tpu_custom_call" | custom-call | tf_op jit(solution)/shard_map/expert/pallas_call | solution.py:289
  56.9 0.4 collective-permute-start.18
  57.3 0.2 collective-permute-start.20
  57.5 1.0 %collective-permute-done.21.refs_2_ = bf16[192,512]{1,0:T(8,128)(2,1)S(1)} collective-permute-done((bf16[192,512]{1,0:T(8,128)(2,1)S(1)}, bf16[192,512]{1,0:T(8,128)(2,1)S(1)}, u32[]{:S(2)}, u32[]{:S(2)}) %collective-permute-start.21) | collective-permute-done | bytes 196640 | tf_op jit(solution)/shard_map/ppermute | solution.py:363
  58.5 0.1 collective-permute-start.22
  58.7 0.1 collective-permute-done.20.refs_1_
  58.8 1.2 %collective-permute-done.22.refs_3_ = bf16[192,512]{1,0:T(8,128)(2,1)S(1)} collective-permute-done((bf16[192,512]{1,0:T(8,128)(2,1)S(1)}, bf16[192,512]{1,0:T(8,128)(2,1)S(1)}, u32[]{:S(2)}, u32[]{:S(2)}) %collective-permute-start.22) | collective-permute-done | bytes 196640 | tf_op jit(solution)/shard_map/ppermute | solution.py:363
  60.0 1.8 %expert.5 = (f32[2,384,256]{2,1,0:T(8,128)S(1)}, bf16[2,384,256]{2,1,0:T(8,128)(2,1)S(1)}) custom-call(bf16[192,512]{1,0:T(8,128)(2,1)S(1)} %collective-permute-done.13.refs_0_, bf16[192,512]{1,0:T(8,128)(2,1)S(1)} %collective-permute-done.20.refs_1_, bf16[192,512]{1,0:T(8,128)(2,1)S(1)} %collective-permute-done.21.refs_2_, ...), custom_call_target="tpu_custom_call" | custom-call | tf_op jit(solution)/shard_map/expert/pallas_call | solution.py:289
  61.8 0.2 collective-permute-start.23
  62.0 0.6 collective-permute-start.19
  62.6 0.9 %collective-permute-done.23 = bf16[2,384,256]{2,1,0:T(8,128)(2,1)S(1)} collective-permute-done((bf16[2,384,256]{2,1,0:T(8,128)(2,1)S(1)}, bf16[2,384,256]{2,1,0:T(8,128)(2,1)S(1)}, u32[]{:S(2)}, u32[]{:S(2)}) %collective-permute-start.23) | collective-permute-done | bytes 393248 | tf_op jit(solution)/shard_map/ppermute | solution.py:363
  63.6 0.1 convert_add_fusion
  63.7 3.4 %collective-permute-done.19 = bf16[192,256]{1,0:T(8,128)(2,1)S(1)} collective-permute-done((bf16[192,256]{1,0:T(8,128)(2,1)S(1)}, bf16[192,256]{1,0:T(8,128)(2,1)S(1)}, u32[]{:S(2)}, u32[]{:S(2)}) %collective-permute-start.19) | collective-permute-done | bytes 98336 | tf_op jit(solution)/shard_map/ppermute | solution.py:363
  67.2 0.6 collective-permute-start.25
  67.8 1.5 %collective-permute-start.24 = (bf16[192,256]{1,0:T(8,128)(2,1)S(1)}, bf16[192,256]{1,0:T(8,128)(2,1)S(1)}, u32[]{:S(2)}, u32[]{:S(2)}) collective-permute-start(bf16[192,256]{1,0:T(8,128)(2,1)S(1)} %fusion.3), channel_id=1, source_target_pairs={{0,12},{1,13},{2,14},{3,15},{4,8},{5,9},{6,10},{7,11},{8,4},{9,5},... | collective-permute-start | bytes 294920 | tf_op jit(solution)/shard_map/ppermute | solution.py:363
  69.3 2.6 %collective-permute-done.25 = bf16[192,256]{1,0:T(8,128)(2,1)S(1)} collective-permute-done((bf16[192,256]{1,0:T(8,128)(2,1)S(1)}, bf16[192,256]{1,0:T(8,128)(2,1)S(1)}, u32[]{:S(2)}, u32[]{:S(2)}) %collective-permute-start.25) | collective-permute-done | bytes 98336 | tf_op jit(solution)/shard_map/ppermute | solution.py:363
  71.9 0.1 collective-permute-start.26
  72.0 1.9 %collective-permute-start.28 = (bf16[192,256]{1,0:T(8,128)(2,1)S(1)}, bf16[192,256]{1,0:T(8,128)(2,1)S(1)}, u32[]{:S(2)}, u32[]{:S(2)}) collective-permute-start(bf16[192,256]{1,0:T(8,128)(2,1)S(1)} %get-tuple-element.99), channel_id=1, source_target_pairs={{0,6},{1,7},{2,4},{3,5},{4,2},{5,3},{6,0},{7,1},{8,14},{9,15},{10,... | collective-permute-start | bytes 294920 | tf_op jit(solution)/shard_map/ppermute | solution.py:363
  73.9 0.5 collective-permute-start.27
  74.4 1.1 %collective-permute-start.29 = (bf16[192,256]{1,0:T(8,128)(2,1)S(1)}, bf16[192,256]{1,0:T(8,128)(2,1)S(1)}, u32[]{:S(2)}, u32[]{:S(2)}) collective-permute-start(bf16[192,256]{1,0:T(8,128)(2,1)S(1)} %get-tuple-element.96), channel_id=1, source_target_pairs={{0,2},{1,3},{2,0},{3,1},{4,6},{5,7},{6,4},{7,5},{8,10},{9,11},{10,... | collective-permute-start | bytes 294920 | tf_op jit(solution)/shard_map/ppermute | solution.py:363
  75.5 0.2 combine.4.base
  75.8 3.4 %collective-permute-done.26.refs_0_ = bf16[192,256]{1,0:T(8,128)(2,1)S(1)} collective-permute-done((bf16[192,256]{1,0:T(8,128)(2,1)S(1)}, bf16[192,256]{1,0:T(8,128)(2,1)S(1)}, u32[]{:S(2)}, u32[]{:S(2)}) %collective-permute-start.26) | collective-permute-done | bytes 98336 | tf_op jit(solution)/shard_map/ppermute | solution.py:363
  79.2 0.2 combine.5.base
  79.4 0.8 collective-permute-done.28.refs_1_
  80.2 0.3 collective-permute-done.27.refs_0_
  80.5 0.2 combine.6.base
  80.7 0.9 %combine.7 = bf16[256,256]{1,0:T(8,128)(2,1)} custom-call(f32[256,2]{1,0:T(8,128)S(1)} %get-tuple-element.66.gates, f32[256,256]{1,0:T(8,128)S(1)} %combine.6.base, bf16[256,192]{1,0:T(8,128)(2,1)S(1)} %get-tuple-element.94.first, bf16[256,192]{1,0:T(8,128)(2,1)S(1)} %get-tuple-element.95.second, bf16[192,256]{1,0:T(8,128)(2,1)S(1)} %get-tuple-element.98.refs_0_, ...), custom_call_target="tpu_custom_call" | custom-call | tf_op jit(solution)/shard_map/combine/pallas_call | solution.py:315
  (34 shorter events, 0.3 us)
Async XLA Ops:
  0.0 29.5 %collective-permute-start.9 = (bf16[256,1024]{1,0:T(8,128)(2,1)}, bf16[256,1024]{1,0:T(8,128)(2,1)S(1)}, u32[]{:S(2)}, u32[]{:S(2)}) collective-permute-start(bf16[256,1024]{1,0:T(8,128)(2,1)} %refs_5_), channel_id=1, source_target_pairs={{0,2},{1,3},{2,0},{3,1},{4,6},{5,7},{6,4},{7,5},{8,10},{9,11},{10,... | collective-permute-start | bytes 1572872 | tf_op jit(solution)/shard_map/ppermute | solution.py:363
  4.8 24.7 %copy-start.3 = (bf16[256,1024]{1,0:T(8,128)(2,1)S(1)}, bf16[256,1024]{1,0:T(8,128)(2,1)}, u32[]{:S(2)}) copy-start(bf16[256,1024]{1,0:T(8,128)(2,1)} %refs_5_) | copy-start | bytes 1572868
  4.8 25.8 %copy-start.5 = (s32[256,2]{0,1:T(2,128)S(1)}, s32[256,2]{0,1:T(2,128)}, u32[]{:S(2)}) copy-start(s32[256,2]{0,1:T(2,128)} %param.15) | copy-start | bytes 6148
  4.8 32.1 %copy-start.2 = (bf16[256,1024]{1,0:T(8,128)(2,1)S(1)}, bf16[256,1024]{1,0:T(8,128)(2,1)}, u32[]{:S(2)}) copy-start(bf16[256,1024]{1,0:T(8,128)(2,1)} %refs_0_.1) | copy-start | bytes 1572868
  4.8 8.8 %collective-permute-start.1 = (bf16[256,256]{1,0:T(8,128)(2,1)S(1)}, bf16[256,256]{1,0:T(8,128)(2,1)S(1)}, u32[]{:S(2)}, u32[]{:S(2)}) collective-permute-start(bf16[256,256]{1,0:T(8,128)(2,1)S(1)} %get-tuple-element.51.queries), channel_id=1, source_target_pairs={{0,8},{1,9},{2,10},{3,11},{4,12},{5,13},{6,14},{7,15},{8,0},{9,1},... | collective-permute-start | bytes 393224 | tf_op jit(solution)/shard_map/ppermute | solution.py:363
  7.4 10.9 %collective-permute-start = (bf16[256,256]{1,0:T(8,128)(2,1)S(1)}, bf16[256,256]{1,0:T(8,128)(2,1)S(1)}, u32[]{:S(2)}, u32[]{:S(2)}) collective-permute-start(bf16[256,256]{1,0:T(8,128)(2,1)S(1)} %get-tuple-element.51.queries), channel_id=1, source_target_pairs={{0,4},{1,5},{2,6},{3,7},{4,0},{5,1},{6,2},{7,3},{8,12},{9,13},{10,... | collective-permute-start | bytes 393224 | tf_op jit(solution)/shard_map/ppermute | solution.py:363
  13.6 5.5 %collective-permute-start.4 = (bf16[256,256]{1,0:T(8,128)(2,1)S(1)}, bf16[256,256]{1,0:T(8,128)(2,1)S(1)}, u32[]{:S(2)}, u32[]{:S(2)}) collective-permute-start(bf16[256,256]{1,0:T(8,128)(2,1)S(1)} %collective-permute-done.1.queries), channel_id=1, source_target_pairs={{0,4},{1,5},{2,6},{3,7},{4,0},{5,1},{6,2},{7,3},{8,12},{9,13},{10,... | collective-permute-start | bytes 393224 | tf_op jit(solution)/shard_map/ppermute | solution.py:363
  14.9 11.5 %collective-permute-start.3 = (bf16[256,256]{1,0:T(8,128)(2,1)S(1)}, bf16[256,256]{1,0:T(8,128)(2,1)S(1)}, u32[]{:S(2)}, u32[]{:S(2)}) collective-permute-start(bf16[256,256]{1,0:T(8,128)(2,1)S(1)} %attend.5), channel_id=1, source_target_pairs={{0,8},{1,9},{2,10},{3,11},{4,12},{5,13},{6,14},{7,15},{8,0},{9,1},... | collective-permute-start | bytes 393224 | tf_op jit(solution)/shard_map/ppermute | solution.py:363
  19.1 7.4 %collective-permute-start.2 = (bf16[256,256]{1,0:T(8,128)(2,1)S(1)}, bf16[256,256]{1,0:T(8,128)(2,1)S(1)}, u32[]{:S(2)}, u32[]{:S(2)}) collective-permute-start(bf16[256,256]{1,0:T(8,128)(2,1)S(1)} %attend.6), channel_id=1, source_target_pairs={{0,4},{1,5},{2,6},{3,7},{4,0},{5,1},{6,2},{7,3},{8,12},{9,13},{10,... | collective-permute-start | bytes 393224 | tf_op jit(solution)/shard_map/ppermute | solution.py:363
  19.9 21.5 %copy-start.4 = (bf16[1024,4]{0,1:T(4,128)(2,1)S(1)}, bf16[1024,4]{0,1:T(4,128)(2,1)}, u32[]{:S(2)}) copy-start(bf16[1024,4]{0,1:T(4,128)(2,1)} %param.14) | copy-start | bytes 24580
  19.9 9.4 %collective-permute-start.5 = (bf16[256,256]{1,0:T(8,128)(2,1)S(1)}, bf16[256,256]{1,0:T(8,128)(2,1)S(1)}, u32[]{:S(2)}, u32[]{:S(2)}) collective-permute-start(bf16[256,256]{1,0:T(8,128)(2,1)S(1)} %attend.7), channel_id=1, source_target_pairs={{0,12},{1,13},{2,14},{3,15},{4,8},{5,9},{6,10},{7,11},{8,4},{9,5},... | collective-permute-start | bytes 393224 | tf_op jit(solution)/shard_map/ppermute | solution.py:363
  29.4 7.4 %collective-permute-start.10 = (bf16[256,1024]{1,0:T(8,128)(2,1)S(1)}, bf16[256,1024]{1,0:T(8,128)(2,1)S(1)}, u32[]{:S(2)}, u32[]{:S(2)}) collective-permute-start(bf16[256,1024]{1,0:T(8,128)(2,1)S(1)} %copy-done.3), channel_id=1, source_target_pairs={{0,1},{1,0},{2,3},{3,2},{4,5},{5,4},{6,7},{7,6},{8,9},{9,8},{10,11... | collective-permute-start | bytes 1572872 | tf_op jit(solution)/shard_map/ppermute | solution.py:363
  29.5 7.3 %collective-permute-start.11 = (bf16[256,1024]{1,0:T(8,128)(2,1)S(1)}, bf16[256,1024]{1,0:T(8,128)(2,1)S(1)}, u32[]{:S(2)}, u32[]{:S(2)}) collective-permute-start(bf16[256,1024]{1,0:T(8,128)(2,1)S(1)} %collective-permute-done.9.refs_6_), channel_id=1, source_target_pairs={{0,1},{1,0},{2,3},{3,2},{4,5},{5,4},{6,7},{7,6},{8,9},{9,8},{10,11... | collective-permute-start | bytes 1572872 | tf_op jit(solution)/shard_map/ppermute | solution.py:363
  30.0 5.5 %collective-permute-start.6 = (bf16[256,256]{1,0:T(8,128)(2,1)S(1)}, bf16[256,256]{1,0:T(8,128)(2,1)S(1)}, u32[]{:S(2)}, u32[]{:S(2)}) collective-permute-start(bf16[256,256]{1,0:T(8,128)(2,1)S(1)} %pick.1.refs_1_), channel_id=1, source_target_pairs={{0,2},{1,3},{2,0},{3,1},{4,6},{5,7},{6,4},{7,5},{8,10},{9,11},{10,... | collective-permute-start | bytes 393224 | tf_op jit(solution)/shard_map/ppermute | solution.py:363
  31.5 4.0 %collective-permute-start.7 = (bf16[256,256]{1,0:T(8,128)(2,1)S(1)}, bf16[256,256]{1,0:T(8,128)(2,1)S(1)}, u32[]{:S(2)}, u32[]{:S(2)}) collective-permute-start(bf16[256,256]{1,0:T(8,128)(2,1)S(1)} %pick.1.refs_1_), channel_id=1, source_target_pairs={{0,1},{1,0},{2,3},{3,2},{4,5},{5,4},{6,7},{7,6},{8,9},{9,8},{10,11... | collective-permute-start | bytes 393224 | tf_op jit(solution)/shard_map/ppermute | solution.py:363
  35.5 1.3 %collective-permute-start.8 = (bf16[256,256]{1,0:T(8,128)(2,1)S(1)}, bf16[256,256]{1,0:T(8,128)(2,1)S(1)}, u32[]{:S(2)}, u32[]{:S(2)}) collective-permute-start(bf16[256,256]{1,0:T(8,128)(2,1)S(1)} %collective-permute-done.6.refs_2_), channel_id=1, source_target_pairs={{0,1},{1,0},{2,3},{3,2},{4,5},{5,4},{6,7},{7,6},{8,9},{9,8},{10,11... | collective-permute-start | bytes 393224 | tf_op jit(solution)/shard_map/ppermute | solution.py:363
  36.9 5.0 %copy-start = (bf16[1,1024,1024]{2,1,0:T(8,128)(2,1)S(1)}, bf16[1,1024,1024]{2,1,0:T(8,128)(2,1)}, u32[]{:S(2)}) copy-start(bf16[1,1024,1024]{2,1,0:T(8,128)(2,1)} %param.16) | copy-start | bytes 6291460
  36.9 5.0 %copy-start.1 = (bf16[1,1024,1024]{2,1,0:T(8,128)(2,1)S(1)}, bf16[1,1024,1024]{2,1,0:T(8,128)(2,1)}, u32[]{:S(2)}) copy-start(bf16[1,1024,1024]{2,1,0:T(8,128)(2,1)} %param.17) | copy-start | bytes 6291460
  38.0 7.6 %collective-permute-start.12 = (bf16[192,256]{1,0:T(8,128)(2,1)S(1)}, bf16[192,256]{1,0:T(8,128)(2,1)S(1)}, u32[]{:S(2)}, u32[]{:S(2)}) collective-permute-start(bf16[192,256]{1,0:T(8,128)(2,1)S(1)} %get-tuple-element.70), channel_id=1, source_target_pairs={{0,12},{1,13},{2,14},{3,15},{4,8},{5,9},{6,10},{7,11},{8,4},{9,5},... | collective-permute-start | bytes 294920 | tf_op jit(solution)/shard_map/ppermute | solution.py:363
  41.3 13.1 %collective-permute-start.13 = (bf16[192,512]{1,0:T(8,128)(2,1)S(1)}, bf16[192,512]{1,0:T(8,128)(2,1)S(1)}, u32[]{:S(2)}, u32[]{:S(2)}) collective-permute-start(bf16[192,512]{1,0:T(8,128)(2,1)S(1)} %get-tuple-element.71), channel_id=1, source_target_pairs={{0,8},{1,9},{2,10},{3,11},{4,12},{5,13},{6,14},{7,15},{8,0},{9,1},... | collective-permute-start | bytes 589832 | tf_op jit(solution)/shard_map/ppermute | solution.py:363
  45.6 9.4 %collective-permute-start.14 = (bf16[2,192,256]{2,1,0:T(8,128)(2,1)S(1)}, bf16[2,192,256]{2,1,0:T(8,128)(2,1)S(1)}, u32[]{:S(2)}, u32[]{:S(2)}) collective-permute-start(bf16[2,192,256]{2,1,0:T(8,128)(2,1)S(1)} %get-tuple-element.77), channel_id=1, source_target_pairs={{0,1},{1,0},{2,3},{3,2},{4,5},{5,4},{6,7},{7,6},{8,9},{9,8},{10,11... | collective-permute-start | bytes 589832 | tf_op jit(solution)/shard_map/ppermute | solution.py:363
  45.6 8.9 %collective-permute-start.15 = (bf16[192,256]{1,0:T(8,128)(2,1)S(1)}, bf16[192,256]{1,0:T(8,128)(2,1)S(1)}, u32[]{:S(2)}, u32[]{:S(2)}) collective-permute-start(bf16[192,256]{1,0:T(8,128)(2,1)S(1)} %collective-permute-done.12.refs_0_), channel_id=1, source_target_pairs={{0,2},{1,3},{2,0},{3,1},{4,6},{5,7},{6,4},{7,5},{8,10},{9,11},{10,... | collective-permute-start | bytes 294920 | tf_op jit(solution)/shard_map/ppermute | solution.py:363
  46.1 12.4 %collective-permute-start.21 = (bf16[192,512]{1,0:T(8,128)(2,1)S(1)}, bf16[192,512]{1,0:T(8,128)(2,1)S(1)}, u32[]{:S(2)}, u32[]{:S(2)}) collective-permute-start(bf16[192,512]{1,0:T(8,128)(2,1)S(1)} %get-tuple-element.85), channel_id=1, source_target_pairs={{0,4},{1,5},{2,6},{3,7},{4,0},{5,1},{6,2},{7,3},{8,12},{9,13},{10,... | collective-permute-start | bytes 589832 | tf_op jit(solution)/shard_map/ppermute | solution.py:363
  54.4 1.3 %collective-permute-start.16 = (bf16[192,256]{1,0:T(8,128)(2,1)S(1)}, bf16[192,256]{1,0:T(8,128)(2,1)S(1)}, u32[]{:S(2)}, u32[]{:S(2)}) collective-permute-start(bf16[192,256]{1,0:T(8,128)(2,1)S(1)} %collective-permute-done.12.refs_0_), channel_id=1, source_target_pairs={{0,1},{1,0},{2,3},{3,2},{4,5},{5,4},{6,7},{7,6},{8,9},{9,8},{10,11... | collective-permute-start | bytes 294920 | tf_op jit(solution)/shard_map/ppermute | solution.py:363
  54.4 1.5 %collective-permute-start.17 = (bf16[192,256]{1,0:T(8,128)(2,1)S(1)}, bf16[192,256]{1,0:T(8,128)(2,1)S(1)}, u32[]{:S(2)}, u32[]{:S(2)}) collective-permute-start(bf16[192,256]{1,0:T(8,128)(2,1)S(1)} %collective-permute-done.15.refs_1_), channel_id=1, source_target_pairs={{0,1},{1,0},{2,3},{3,2},{4,5},{5,4},{6,7},{7,6},{8,9},{9,8},{10,11... | collective-permute-start | bytes 294920 | tf_op jit(solution)/shard_map/ppermute | solution.py:363
  56.9 1.7 %collective-permute-start.18 = (bf16[2,192,256]{2,1,0:T(8,128)(2,1)S(1)}, bf16[2,192,256]{2,1,0:T(8,128)(2,1)S(1)}, u32[]{:S(2)}, u32[]{:S(2)}) collective-permute-start(bf16[2,192,256]{2,1,0:T(8,128)(2,1)S(1)} %get-tuple-element.82), channel_id=1, source_target_pairs={{0,1},{1,0},{2,3},{3,2},{4,5},{5,4},{6,7},{7,6},{8,9},{9,8},{10,11... | collective-permute-start | bytes 589832 | tf_op jit(solution)/shard_map/ppermute | solution.py:363
  57.3 1.4 %collective-permute-start.20 = (bf16[192,512]{1,0:T(8,128)(2,1)S(1)}, bf16[192,512]{1,0:T(8,128)(2,1)S(1)}, u32[]{:S(2)}, u32[]{:S(2)}) collective-permute-start(bf16[192,512]{1,0:T(8,128)(2,1)S(1)} %collective-permute-done.13.refs_0_), channel_id=1, source_target_pairs={{0,1},{1,0},{2,3},{3,2},{4,5},{5,4},{6,7},{7,6},{8,9},{9,8},{10,11... | collective-permute-start | bytes 589832 | tf_op jit(solution)/shard_map/ppermute | solution.py:363
  58.5 1.4 %collective-permute-start.22 = (bf16[192,512]{1,0:T(8,128)(2,1)S(1)}, bf16[192,512]{1,0:T(8,128)(2,1)S(1)}, u32[]{:S(2)}, u32[]{:S(2)}) collective-permute-start(bf16[192,512]{1,0:T(8,128)(2,1)S(1)} %collective-permute-done.21.refs_2_), channel_id=1, source_target_pairs={{0,1},{1,0},{2,3},{3,2},{4,5},{5,4},{6,7},{7,6},{8,9},{9,8},{10,11... | collective-permute-start | bytes 589832 | tf_op jit(solution)/shard_map/ppermute | solution.py:363
  61.8 1.8 %collective-permute-start.23 = (bf16[2,384,256]{2,1,0:T(8,128)(2,1)S(1)}, bf16[2,384,256]{2,1,0:T(8,128)(2,1)S(1)}, u32[]{:S(2)}, u32[]{:S(2)}) collective-permute-start(bf16[2,384,256]{2,1,0:T(8,128)(2,1)S(1)} %get-tuple-element.87), channel_id=1, source_target_pairs={{0,1},{1,0},{2,3},{3,2},{4,5},{5,4},{6,7},{7,6},{8,9},{9,8},{10,11... | collective-permute-start | bytes 1179656 | tf_op jit(solution)/shard_map/ppermute | solution.py:363
  62.0 5.1 %collective-permute-start.19 = (bf16[192,256]{1,0:T(8,128)(2,1)S(1)}, bf16[192,256]{1,0:T(8,128)(2,1)S(1)}, u32[]{:S(2)}, u32[]{:S(2)}) collective-permute-start(bf16[192,256]{1,0:T(8,128)(2,1)S(1)} %fusion.4), channel_id=1, source_target_pairs={{0,2},{1,3},{2,0},{3,1},{4,6},{5,7},{6,4},{7,5},{8,10},{9,11},{10,... | collective-permute-start | bytes 294920 | tf_op jit(solution)/shard_map/ppermute | solution.py:363
  67.2 4.7 %collective-permute-start.25 = (bf16[192,256]{1,0:T(8,128)(2,1)S(1)}, bf16[192,256]{1,0:T(8,128)(2,1)S(1)}, u32[]{:S(2)}, u32[]{:S(2)}) collective-permute-start(bf16[192,256]{1,0:T(8,128)(2,1)S(1)} %fusion.5), channel_id=1, source_target_pairs={{0,2},{1,3},{2,0},{3,1},{4,6},{5,7},{6,4},{7,5},{8,10},{9,11},{10,... | collective-permute-start | bytes 294920 | tf_op jit(solution)/shard_map/ppermute | solution.py:363
  67.8 7.7 %collective-permute-start.24 = (bf16[192,256]{1,0:T(8,128)(2,1)S(1)}, bf16[192,256]{1,0:T(8,128)(2,1)S(1)}, u32[]{:S(2)}, u32[]{:S(2)}) collective-permute-start(bf16[192,256]{1,0:T(8,128)(2,1)S(1)} %fusion.3), channel_id=1, source_target_pairs={{0,12},{1,13},{2,14},{3,15},{4,8},{5,9},{6,10},{7,11},{8,4},{9,5},... | collective-permute-start | bytes 294920 | tf_op jit(solution)/shard_map/ppermute | solution.py:363
  71.9 7.3 %collective-permute-start.26 = (bf16[192,256]{1,0:T(8,128)(2,1)S(1)}, bf16[192,256]{1,0:T(8,128)(2,1)S(1)}, u32[]{:S(2)}, u32[]{:S(2)}) collective-permute-start(bf16[192,256]{1,0:T(8,128)(2,1)S(1)} %fusion.1), channel_id=1, source_target_pairs={{0,8},{1,9},{2,10},{3,11},{4,12},{5,13},{6,14},{7,15},{8,0},{9,1},... | collective-permute-start | bytes 294920 | tf_op jit(solution)/shard_map/ppermute | solution.py:363
  72.0 8.2 %collective-permute-start.28 = (bf16[192,256]{1,0:T(8,128)(2,1)S(1)}, bf16[192,256]{1,0:T(8,128)(2,1)S(1)}, u32[]{:S(2)}, u32[]{:S(2)}) collective-permute-start(bf16[192,256]{1,0:T(8,128)(2,1)S(1)} %get-tuple-element.99), channel_id=1, source_target_pairs={{0,6},{1,7},{2,4},{3,5},{4,2},{5,3},{6,0},{7,1},{8,14},{9,15},{10,... | collective-permute-start | bytes 294920 | tf_op jit(solution)/shard_map/ppermute | solution.py:363
  73.9 6.5 %collective-permute-start.27 = (bf16[192,256]{1,0:T(8,128)(2,1)S(1)}, bf16[192,256]{1,0:T(8,128)(2,1)S(1)}, u32[]{:S(2)}, u32[]{:S(2)}) collective-permute-start(bf16[192,256]{1,0:T(8,128)(2,1)S(1)} %get-tuple-element.100), channel_id=1, source_target_pairs={{0,4},{1,5},{2,6},{3,7},{4,0},{5,1},{6,2},{7,3},{8,12},{9,13},{10,... | collective-permute-start | bytes 294920 | tf_op jit(solution)/shard_map/ppermute | solution.py:363
  74.4 6.3 %collective-permute-start.29 = (bf16[192,256]{1,0:T(8,128)(2,1)S(1)}, bf16[192,256]{1,0:T(8,128)(2,1)S(1)}, u32[]{:S(2)}, u32[]{:S(2)}) collective-permute-start(bf16[192,256]{1,0:T(8,128)(2,1)S(1)} %get-tuple-element.96), channel_id=1, source_target_pairs={{0,2},{1,3},{2,0},{3,1},{4,6},{5,7},{6,4},{7,5},{8,10},{9,11},{10,... | collective-permute-start | bytes 294920 | tf_op jit(solution)/shard_map/ppermute | solution.py:363

commit v17 on v15

--- a/solution.py
+++ b/solution.py
@@ -11,7 +11,7 @@
 HEAD_DIM = 128
 SHARPNESS = HEAD_DIM**-0.5 * math.log2(math.e)
 DIRECT = 8
-CUTS = 4
+CUTS = 1
 TILE = 256
 F32, BF16 = jnp.float32, jnp.bfloat16
 PARAMS = pltpu.CompilerParams(vmem_limit_bytes=20 * 2**20)

time: 78 us -> 77.7 us (level)
  transfers between devices with their start and end apart: 30 -> 30, of which waited for: 13 -> 13; matrix products, arithmetic and copies ran while one was open for 0% -> 0% of each run, Pallas kernels for 12% -> 11%
where the time goes in v17:
time: 77.7 us; the launch traced here: 77.6 us
  waiting for transfers between devices  32.6 us (42%)
  starting transfers between devices  31.2 us (40%)
  Pallas kernels  12.5 us (16%)
  between operations  1 us (1%)
    ppermute x30, waiting for transfers between devices, hop(): return lax.ppermute(value, ('expert', 'mp'), moves)  32.6 us
    ppermute x30, starting transfers between devices, hop(): return lax.ppermute(value, ('expert', 'mp'), moves)  31.2 us
    pallas_call x3, Pallas kernels, run_expert(): pl.pallas_call(functools.partial(expert_kernel, tuple(map(tuple, orders))...  3.86 us
    pallas_call x4, Pallas kernels, attend(): pl.pallas_call(attend_kernel, in_specs=[WHOLE] * 2, out_specs=WHOLE, out_...  2.8 us
    pallas_call x4, Pallas kernels, combine(): pl.pallas_call(functools.partial(combine_kernel, len(parts)), in_specs=[W...  1.59 us
  transfers between devices with their start and end apart: 30, of which 13 were waited for; matrix products, arithmetic and copies ran while one was open for 0% of the time, Pallas kernels for 11%

profile of v17, /device:TPU:0, one launch (start us, length us, event | category | flops | bytes accessed | tf_op | source)
XLA Modules:
  0.0 77.6 jit_solution(3474901155837479918)
XLA Ops:
  0.0 2.9 %collective-permute-start.9 = (bf16[256,1024]{1,0:T(8,128)(2,1)}, bf16[256,1024]{1,0:T(8,128)(2,1)S(1)}, u32[]{:S(2)}, u32[]{:S(2)}) collective-permute-start(bf16[256,1024]{1,0:T(8,128)(2,1)} %refs_5_), channel_id=1, source_target_pairs={{0,2},{1,3},{2,0},{3,1},{4,6},{5,7},{6,4},{7,5},{8,10},{9,11},{10,... | collective-permute-start | bytes 1572872 | tf_op jit(solution)/shard_map/ppermute | solution.py:363
  2.9 1.5 %query.1 = (bf16[256,256]{1,0:T(8,128)(2,1)S(1)}, bf16[2,512,256]{2,1,0:T(8,128)(2,1)S(1)}) custom-call(bf16[256,1024]{1,0:T(8,128)(2,1)} %refs_0_.1, bf16[1024,256]{1,0:T(8,128)(2,1)} %weight.1, bf16[2,512,256]{2,1,0:T(8,128)(2,1)} %bitcast.39), custom_call_target="tpu_custom_call" | custom-call | tf_op jit(solution)/shard_map/query/pallas_call | solution.py:65
  4.5 0.0 copy-start.3
  4.5 0.0 copy-start.5
  4.5 0.0 copy-start.2
  4.5 2.7 %collective-permute-start.1 = (bf16[256,256]{1,0:T(8,128)(2,1)S(1)}, bf16[256,256]{1,0:T(8,128)(2,1)S(1)}, u32[]{:S(2)}, u32[]{:S(2)}) collective-permute-start(bf16[256,256]{1,0:T(8,128)(2,1)S(1)} %get-tuple-element.50.queries), channel_id=1, source_target_pairs={{0,8},{1,9},{2,10},{3,11},{4,12},{5,13},{6,14},{7,15},{8,0},{9,1},... | collective-permute-start | bytes 393224 | tf_op jit(solution)/shard_map/ppermute | solution.py:363
  7.2 1.6 %collective-permute-start = (bf16[256,256]{1,0:T(8,128)(2,1)S(1)}, bf16[256,256]{1,0:T(8,128)(2,1)S(1)}, u32[]{:S(2)}, u32[]{:S(2)}) collective-permute-start(bf16[256,256]{1,0:T(8,128)(2,1)S(1)} %get-tuple-element.50.queries), channel_id=1, source_target_pairs={{0,4},{1,5},{2,6},{3,7},{4,0},{5,1},{6,2},{7,3},{8,12},{9,13},{10,... | collective-permute-start | bytes 393224 | tf_op jit(solution)/shard_map/ppermute | solution.py:363
  8.7 0.7 attend.4.refs_0_
  9.4 3.9 %collective-permute-done.1.queries = bf16[256,256]{1,0:T(8,128)(2,1)S(1)} collective-permute-done((bf16[256,256]{1,0:T(8,128)(2,1)S(1)}, bf16[256,256]{1,0:T(8,128)(2,1)S(1)}, u32[]{:S(2)}, u32[]{:S(2)}) %collective-permute-start.1) | collective-permute-done | bytes 131104 | tf_op jit(solution)/shard_map/ppermute | solution.py:363
  13.3 0.6 collective-permute-start.4
  13.9 0.7 attend.5
  14.6 3.4 %collective-permute-start.3 = (bf16[256,256]{1,0:T(8,128)(2,1)S(1)}, bf16[256,256]{1,0:T(8,128)(2,1)S(1)}, u32[]{:S(2)}, u32[]{:S(2)}) collective-permute-start(bf16[256,256]{1,0:T(8,128)(2,1)S(1)} %attend.5), channel_id=1, source_target_pairs={{0,8},{1,9},{2,10},{3,11},{4,12},{5,13},{6,14},{7,15},{8,0},{9,1},... | collective-permute-start | bytes 393224 | tf_op jit(solution)/shard_map/ppermute | solution.py:363
  18.1 0.7 attend.6
  18.8 0.1 collective-permute-start.2
  18.9 0.7 attend.7
  19.6 0.0 copy-start.4
  19.6 5.9 %collective-permute-start.5 = (bf16[256,256]{1,0:T(8,128)(2,1)S(1)}, bf16[256,256]{1,0:T(8,128)(2,1)S(1)}, u32[]{:S(2)}, u32[]{:S(2)}) collective-permute-start(bf16[256,256]{1,0:T(8,128)(2,1)S(1)} %attend.7), channel_id=1, source_target_pairs={{0,12},{1,13},{2,14},{3,15},{4,8},{5,9},{6,10},{7,11},{8,4},{9,5},... | collective-permute-start | bytes 393224 | tf_op jit(solution)/shard_map/ppermute | solution.py:363
  26.1 0.0 collective-permute-done.2.refs_1_
  26.2 2.8 %collective-permute-done.5.refs_3_ = bf16[256,256]{1,0:T(8,128)(2,1)S(1)} collective-permute-done((bf16[256,256]{1,0:T(8,128)(2,1)S(1)}, bf16[256,256]{1,0:T(8,128)(2,1)S(1)}, u32[]{:S(2)}, u32[]{:S(2)}) %collective-permute-start.5) | collective-permute-done | bytes 131104 | tf_op jit(solution)/shard_map/ppermute | solution.py:363
  29.0 0.1 pick.1.refs_1_
  29.1 0.1 collective-permute-start.10
  29.2 0.5 collective-permute-start.11
  29.7 0.5 collective-permute-start.6
  30.3 1.0 %route.1 = (s32[256,2]{1,0:T(8,128)S(1)}, bf16[192,256]{1,0:T(8,128)(2,1)S(1)}, bf16[192,256]{1,0:T(8,128)(2,1)S(1)}, bf16[192,256]{1,0:T(8,128)(2,1)S(1)}, bf16...) custom-call(s32[2,256]{1,0:T(2,128)S(1)} %bitcast.38), custom_call_target="tpu_custom_call" | custom-call | tf_op jit(solution)/shard_map/route/pallas_call | solution.py:177
  31.2 0.1 collective-permute-start.7
  31.3 3.9 %collective-permute-done.6.refs_2_ = bf16[256,256]{1,0:T(8,128)(2,1)S(1)} collective-permute-done((bf16[256,256]{1,0:T(8,128)(2,1)S(1)}, bf16[256,256]{1,0:T(8,128)(2,1)S(1)}, u32[]{:S(2)}, u32[]{:S(2)}) %collective-permute-start.6) | collective-permute-done | bytes 131104 | tf_op jit(solution)/shard_map/ppermute | solution.py:363
  35.2 1.3 %collective-permute-done.8.refs_4_ = bf16[256,256]{1,0:T(8,128)(2,1)S(1)} collective-permute-done((bf16[256,256]{1,0:T(8,128)(2,1)S(1)}, bf16[256,256]{1,0:T(8,128)(2,1)S(1)}, u32[]{:S(2)}, u32[]{:S(2)}) %collective-permute-start.8) | collective-permute-done | bytes 131104 | tf_op jit(solution)/shard_map/ppermute | solution.py:363
  36.6 0.0 collective-permute-done.10.refs_7_
  36.6 0.0 collective-permute-done.11.refs_8_
  36.6 0.0 copy-start
  36.6 0.0 copy-start.1
  36.6 1.1 %state.1 = (bf16[256,1024]{1,0:T(8,128)(2,1)S(1)}, bf16[192,512]{1,0:T(8,128)(2,1)S(1)}, bf16[192,256]{1,0:T(8,128)(2,1)S(1)}, bf16[192,512]{1,0:T(8,128)(2,1)S(1)}) custom-call(bf16[256,1024]{1,0:T(8,128)(2,1)S(1)} %copy-done.2, bf16[256,256]{1,0:T(8,128)(2,1)S(1)} %pick.1.refs_1_, bf16[256,256]{1,0:T(8,128)(2,1)S(1)} %collective-permute-done.6.refs_2_, ...), custom_call_target="tpu_custom_call" | custom-call | tf_op jit(solution)/shard_map/state/pallas_call | solution.py:210
  37.7 3.4 %collective-permute-start.12 = (bf16[192,256]{1,0:T(8,128)(2,1)S(1)}, bf16[192,256]{1,0:T(8,128)(2,1)S(1)}, u32[]{:S(2)}, u32[]{:S(2)}) collective-permute-start(bf16[192,256]{1,0:T(8,128)(2,1)S(1)} %get-tuple-element.73), channel_id=1, source_target_pairs={{0,12},{1,13},{2,14},{3,15},{4,8},{5,9},{6,10},{7,11},{8,4},{9,5},... | collective-permute-start | bytes 294920 | tf_op jit(solution)/shard_map/ppermute | solution.py:363
  41.1 1.1 %collective-permute-start.18 = (bf16[192,512]{1,0:T(8,128)(2,1)S(1)}, bf16[192,512]{1,0:T(8,128)(2,1)S(1)}, u32[]{:S(2)}, u32[]{:S(2)}) collective-permute-start(bf16[192,512]{1,0:T(8,128)(2,1)S(1)} %get-tuple-element.81), channel_id=1, source_target_pairs={{0,4},{1,5},{2,6},{3,7},{4,0},{5,1},{6,2},{7,3},{8,12},{9,13},{10,... | collective-permute-start | bytes 589832 | tf_op jit(solution)/shard_map/ppermute | solution.py:363
  42.1 0.5 home.1
  42.7 1.0 %expert.3 = (f32[2,192,256]{2,1,0:T(8,128)S(1)}, bf16[2,192,256]{2,1,0:T(8,128)(2,1)S(1)}) custom-call(bf16[192,512]{1,0:T(8,128)(2,1)S(1)} %get-tuple-element.69.refs_0_, bf16[192,512]{1,0:T(8,128)(2,1)S(1)} %get-tuple-element.70.refs_1_, bf16[1024,1024]{1,0:T(8,128)(2,1)S(1)} %bitcast.31, bf16[1024,1024]{1,0:T(8,128)(2,1)S(1)} %bitcast.34), custom_call_target="tpu_custom_call" | custom-call | tf_op jit(solution)/shard_map/expert/pallas_call | solution.py:289
  43.7 1.6 %collective-permute-done.12.refs_0_ = bf16[192,256]{1,0:T(8,128)(2,1)S(1)} collective-permute-done((bf16[192,256]{1,0:T(8,128)(2,1)S(1)}, bf16[192,256]{1,0:T(8,128)(2,1)S(1)}, u32[]{:S(2)}, u32[]{:S(2)}) %collective-permute-start.12) | collective-permute-done | bytes 98336 | tf_op jit(solution)/shard_map/ppermute | solution.py:363
  45.3 0.5 collective-permute-start.14
  45.8 8.2 %collective-permute-done.16.refs_0_ = bf16[192,512]{1,0:T(8,128)(2,1)S(1)} collective-permute-done((bf16[192,512]{1,0:T(8,128)(2,1)S(1)}, bf16[192,512]{1,0:T(8,128)(2,1)S(1)}, u32[]{:S(2)}, u32[]{:S(2)}) %collective-permute-start.16) | collective-permute-done | bytes 196640 | tf_op jit(solution)/shard_map/ppermute | solution.py:363
  54.0 0.5 collective-permute-start.19
  54.6 0.9 %collective-permute-done.17.refs_1_ = bf16[192,512]{1,0:T(8,128)(2,1)S(1)} collective-permute-done((bf16[192,512]{1,0:T(8,128)(2,1)S(1)}, bf16[192,512]{1,0:T(8,128)(2,1)S(1)}, u32[]{:S(2)}, u32[]{:S(2)}) %collective-permute-start.17) | collective-permute-done | bytes 196640 | tf_op jit(solution)/shard_map/ppermute | solution.py:363
  55.5 0.3 collective-permute-done.19.refs_3_
  55.8 1.8 %expert.4 = (f32[2,384,256]{2,1,0:T(8,128)S(1)}, bf16[2,384,256]{2,1,0:T(8,128)(2,1)S(1)}) custom-call(bf16[192,512]{1,0:T(8,128)(2,1)S(1)} %collective-permute-done.16.refs_0_, bf16[192,512]{1,0:T(8,128)(2,1)S(1)} %collective-permute-done.17.refs_1_, bf16[192,512]{1,0:T(8,128)(2,1)S(1)} %collective-permute-done.18.refs_2_, ...), custom_call_target="tpu_custom_call" | custom-call | tf_op jit(solution)/shard_map/expert/pallas_call | solution.py:289
  57.6 0.3 collective-permute-start.20
  57.9 0.6 collective-permute-start.15
  58.5 0.5 collective-permute-start.22
  59.0 0.4 collective-permute-done.20
  59.4 0.1 convert_add_fusion
  59.5 1.2 %collective-permute-start.25 = (bf16[192,256]{1,0:T(8,128)(2,1)S(1)}, bf16[192,256]{1,0:T(8,128)(2,1)S(1)}, u32[]{:S(2)}, u32[]{:S(2)}) collective-permute-start(bf16[192,256]{1,0:T(8,128)(2,1)S(1)} %fusion.4), channel_id=1, source_target_pairs={{0,2},{1,3},{2,0},{3,1},{4,6},{5,7},{6,4},{7,5},{8,10},{9,11},{10,... | collective-permute-start | bytes 294920 | tf_op jit(solution)/shard_map/ppermute | solution.py:363
  60.7 1.0 %expert.5 = (f32[2,192,256]{2,1,0:T(8,128)S(1)}, bf16[2,192,256]{2,1,0:T(8,128)(2,1)S(1)}) custom-call(bf16[192,256]{1,0:T(8,128)(2,1)S(1)} %collective-permute-done.12.refs_0_, bf16[192,256]{1,0:T(8,128)(2,1)S(1)} %collective-permute-done.14.refs_1_, bf16[192,256]{1,0:T(8,128)(2,1)S(1)} %collective-permute-done.21.refs_2_, ...), custom_call_target="tpu_custom_call" | custom-call | tf_op jit(solution)/shard_map/expert/pallas_call | solution.py:289
  61.8 0.1 collective-permute-start.26
  61.9 1.0 %collective-permute-start.24 = (bf16[192,256]{1,0:T(8,128)(2,1)S(1)}, bf16[192,256]{1,0:T(8,128)(2,1)S(1)}, u32[]{:S(2)}, u32[]{:S(2)}) collective-permute-start(bf16[192,256]{1,0:T(8,128)(2,1)S(1)} %get-tuple-element.95), channel_id=1, source_target_pairs={{0,6},{1,7},{2,4},{3,5},{4,2},{5,3},{6,0},{7,1},{8,14},{9,15},{10,... | collective-permute-start | bytes 294920 | tf_op jit(solution)/shard_map/ppermute | solution.py:363
  62.9 1.6 %collective-permute-start.23 = (bf16[192,256]{1,0:T(8,128)(2,1)S(1)}, bf16[192,256]{1,0:T(8,128)(2,1)S(1)}, u32[]{:S(2)}, u32[]{:S(2)}) collective-permute-start(bf16[192,256]{1,0:T(8,128)(2,1)S(1)} %get-tuple-element.96), channel_id=1, source_target_pairs={{0,4},{1,5},{2,6},{3,7},{4,0},{5,1},{6,2},{7,3},{8,12},{9,13},{10,... | collective-permute-start | bytes 294920 | tf_op jit(solution)/shard_map/ppermute | solution.py:363
  64.5 0.5 collective-permute-done.25
  65.1 0.5 collective-permute-start.28
  65.6 0.1 collective-permute-start.27
  65.7 4.4 %collective-permute-done.28 = bf16[192,256]{1,0:T(8,128)(2,1)S(1)} collective-permute-done((bf16[192,256]{1,0:T(8,128)(2,1)S(1)}, bf16[192,256]{1,0:T(8,128)(2,1)S(1)}, u32[]{:S(2)}, u32[]{:S(2)}) %collective-permute-start.28) | collective-permute-done | bytes 98336 | tf_op jit(solution)/shard_map/ppermute | solution.py:363
  70.1 1.5 %collective-permute-start.29 = (bf16[192,256]{1,0:T(8,128)(2,1)S(1)}, bf16[192,256]{1,0:T(8,128)(2,1)S(1)}, u32[]{:S(2)}, u32[]{:S(2)}) collective-permute-start(bf16[192,256]{1,0:T(8,128)(2,1)S(1)} %fusion.1), channel_id=1, source_target_pairs={{0,12},{1,13},{2,14},{3,15},{4,8},{5,9},{6,10},{7,11},{8,4},{9,5},... | collective-permute-start | bytes 294920 | tf_op jit(solution)/shard_map/ppermute | solution.py:363
  71.6 0.2 combine.4.base
  71.9 0.2 combine.5.base
  72.1 1.2 %collective-permute-done.27.refs_0_ = bf16[192,256]{1,0:T(8,128)(2,1)S(1)} collective-permute-done((bf16[192,256]{1,0:T(8,128)(2,1)S(1)}, bf16[192,256]{1,0:T(8,128)(2,1)S(1)}, u32[]{:S(2)}, u32[]{:S(2)}) %collective-permute-start.27) | collective-permute-done | bytes 98336 | tf_op jit(solution)/shard_map/ppermute | solution.py:363
  73.3 0.2 combine.6.base
  73.6 3.1 %collective-permute-done.29.refs_0_ = bf16[192,256]{1,0:T(8,128)(2,1)S(1)} collective-permute-done((bf16[192,256]{1,0:T(8,128)(2,1)S(1)}, bf16[192,256]{1,0:T(8,128)(2,1)S(1)}, u32[]{:S(2)}, u32[]{:S(2)}) %collective-permute-start.29) | collective-permute-done | bytes 98336 | tf_op jit(solution)/shard_map/ppermute | solution.py:363
  76.7 0.9 %combine.7 = bf16[256,256]{1,0:T(8,128)(2,1)} custom-call(f32[256,2]{1,0:T(8,128)S(1)} %get-tuple-element.65.gates, f32[256,256]{1,0:T(8,128)S(1)} %combine.6.base, bf16[256,192]{1,0:T(8,128)(2,1)S(1)} %get-tuple-element.93.first, bf16[256,192]{1,0:T(8,128)(2,1)S(1)} %get-tuple-element.94.second, bf16[192,256]{1,0:T(8,128)(2,1)S(1)} %collective-permute-done.29.refs_0_), custom_call_target="tpu_custom_call" | custom-call | tf_op jit(solution)/shard_map/combine/pallas_call | solution.py:315
  (34 shorter events, 0.3 us)
Async XLA Ops:
  0.0 29.2 %collective-permute-start.9 = (bf16[256,1024]{1,0:T(8,128)(2,1)}, bf16[256,1024]{1,0:T(8,128)(2,1)S(1)}, u32[]{:S(2)}, u32[]{:S(2)}) collective-permute-start(bf16[256,1024]{1,0:T(8,128)(2,1)} %refs_5_), channel_id=1, source_target_pairs={{0,2},{1,3},{2,0},{3,1},{4,6},{5,7},{6,4},{7,5},{8,10},{9,11},{10,... | collective-permute-start | bytes 1572872 | tf_op jit(solution)/shard_map/ppermute | solution.py:363
  4.5 24.7 %copy-start.3 = (bf16[256,1024]{1,0:T(8,128)(2,1)S(1)}, bf16[256,1024]{1,0:T(8,128)(2,1)}, u32[]{:S(2)}) copy-start(bf16[256,1024]{1,0:T(8,128)(2,1)} %refs_5_) | copy-start | bytes 1572868
  4.5 25.8 %copy-start.5 = (s32[256,2]{0,1:T(2,128)S(1)}, s32[256,2]{0,1:T(2,128)}, u32[]{:S(2)}) copy-start(s32[256,2]{0,1:T(2,128)} %param.15) | copy-start | bytes 6148
  4.5 32.1 %copy-start.2 = (bf16[256,1024]{1,0:T(8,128)(2,1)S(1)}, bf16[256,1024]{1,0:T(8,128)(2,1)}, u32[]{:S(2)}) copy-start(bf16[256,1024]{1,0:T(8,128)(2,1)} %refs_0_.1) | copy-start | bytes 1572868
  4.5 8.8 %collective-permute-start.1 = (bf16[256,256]{1,0:T(8,128)(2,1)S(1)}, bf16[256,256]{1,0:T(8,128)(2,1)S(1)}, u32[]{:S(2)}, u32[]{:S(2)}) collective-permute-start(bf16[256,256]{1,0:T(8,128)(2,1)S(1)} %get-tuple-element.50.queries), channel_id=1, source_target_pairs={{0,8},{1,9},{2,10},{3,11},{4,12},{5,13},{6,14},{7,15},{8,0},{9,1},... | collective-permute-start | bytes 393224 | tf_op jit(solution)/shard_map/ppermute | solution.py:363
  7.2 10.9 %collective-permute-start = (bf16[256,256]{1,0:T(8,128)(2,1)S(1)}, bf16[256,256]{1,0:T(8,128)(2,1)S(1)}, u32[]{:S(2)}, u32[]{:S(2)}) collective-permute-start(bf16[256,256]{1,0:T(8,128)(2,1)S(1)} %get-tuple-element.50.queries), channel_id=1, source_target_pairs={{0,4},{1,5},{2,6},{3,7},{4,0},{5,1},{6,2},{7,3},{8,12},{9,13},{10,... | collective-permute-start | bytes 393224 | tf_op jit(solution)/shard_map/ppermute | solution.py:363
  13.3 5.5 %collective-permute-start.4 = (bf16[256,256]{1,0:T(8,128)(2,1)S(1)}, bf16[256,256]{1,0:T(8,128)(2,1)S(1)}, u32[]{:S(2)}, u32[]{:S(2)}) collective-permute-start(bf16[256,256]{1,0:T(8,128)(2,1)S(1)} %collective-permute-done.1.queries), channel_id=1, source_target_pairs={{0,4},{1,5},{2,6},{3,7},{4,0},{5,1},{6,2},{7,3},{8,12},{9,13},{10,... | collective-permute-start | bytes 393224 | tf_op jit(solution)/shard_map/ppermute | solution.py:363
  14.6 11.5 %collective-permute-start.3 = (bf16[256,256]{1,0:T(8,128)(2,1)S(1)}, bf16[256,256]{1,0:T(8,128)(2,1)S(1)}, u32[]{:S(2)}, u32[]{:S(2)}) collective-permute-start(bf16[256,256]{1,0:T(8,128)(2,1)S(1)} %attend.5), channel_id=1, source_target_pairs={{0,8},{1,9},{2,10},{3,11},{4,12},{5,13},{6,14},{7,15},{8,0},{9,1},... | collective-permute-start | bytes 393224 | tf_op jit(solution)/shard_map/ppermute | solution.py:363
  18.8 7.4 %collective-permute-start.2 = (bf16[256,256]{1,0:T(8,128)(2,1)S(1)}, bf16[256,256]{1,0:T(8,128)(2,1)S(1)}, u32[]{:S(2)}, u32[]{:S(2)}) collective-permute-start(bf16[256,256]{1,0:T(8,128)(2,1)S(1)} %attend.6), channel_id=1, source_target_pairs={{0,4},{1,5},{2,6},{3,7},{4,0},{5,1},{6,2},{7,3},{8,12},{9,13},{10,... | collective-permute-start | bytes 393224 | tf_op jit(solution)/shard_map/ppermute | solution.py:363
  19.6 22.6 %copy-start.4 = (bf16[1024,4]{0,1:T(4,128)(2,1)S(1)}, bf16[1024,4]{0,1:T(4,128)(2,1)}, u32[]{:S(2)}) copy-start(bf16[1024,4]{0,1:T(4,128)(2,1)} %param.14) | copy-start | bytes 24580
  19.6 9.4 %collective-permute-start.5 = (bf16[256,256]{1,0:T(8,128)(2,1)S(1)}, bf16[256,256]{1,0:T(8,128)(2,1)S(1)}, u32[]{:S(2)}, u32[]{:S(2)}) collective-permute-start(bf16[256,256]{1,0:T(8,128)(2,1)S(1)} %attend.7), channel_id=1, source_target_pairs={{0,12},{1,13},{2,14},{3,15},{4,8},{5,9},{6,10},{7,11},{8,4},{9,5},... | collective-permute-start | bytes 393224 | tf_op jit(solution)/shard_map/ppermute | solution.py:363
  29.1 7.4 %collective-permute-start.10 = (bf16[256,1024]{1,0:T(8,128)(2,1)S(1)}, bf16[256,1024]{1,0:T(8,128)(2,1)S(1)}, u32[]{:S(2)}, u32[]{:S(2)}) collective-permute-start(bf16[256,1024]{1,0:T(8,128)(2,1)S(1)} %copy-done.3), channel_id=1, source_target_pairs={{0,1},{1,0},{2,3},{3,2},{4,5},{5,4},{6,7},{7,6},{8,9},{9,8},{10,11... | collective-permute-start | bytes 1572872 | tf_op jit(solution)/shard_map/ppermute | solution.py:363
  29.2 7.3 %collective-permute-start.11 = (bf16[256,1024]{1,0:T(8,128)(2,1)S(1)}, bf16[256,1024]{1,0:T(8,128)(2,1)S(1)}, u32[]{:S(2)}, u32[]{:S(2)}) collective-permute-start(bf16[256,1024]{1,0:T(8,128)(2,1)S(1)} %collective-permute-done.9.refs_6_), channel_id=1, source_target_pairs={{0,1},{1,0},{2,3},{3,2},{4,5},{5,4},{6,7},{7,6},{8,9},{9,8},{10,11... | collective-permute-start | bytes 1572872 | tf_op jit(solution)/shard_map/ppermute | solution.py:363
  29.7 5.5 %collective-permute-start.6 = (bf16[256,256]{1,0:T(8,128)(2,1)S(1)}, bf16[256,256]{1,0:T(8,128)(2,1)S(1)}, u32[]{:S(2)}, u32[]{:S(2)}) collective-permute-start(bf16[256,256]{1,0:T(8,128)(2,1)S(1)} %pick.1.refs_1_), channel_id=1, source_target_pairs={{0,2},{1,3},{2,0},{3,1},{4,6},{5,7},{6,4},{7,5},{8,10},{9,11},{10,... | collective-permute-start | bytes 393224 | tf_op jit(solution)/shard_map/ppermute | solution.py:363
  31.2 4.0 %collective-permute-start.7 = (bf16[256,256]{1,0:T(8,128)(2,1)S(1)}, bf16[256,256]{1,0:T(8,128)(2,1)S(1)}, u32[]{:S(2)}, u32[]{:S(2)}) collective-permute-start(bf16[256,256]{1,0:T(8,128)(2,1)S(1)} %pick.1.refs_1_), channel_id=1, source_target_pairs={{0,1},{1,0},{2,3},{3,2},{4,5},{5,4},{6,7},{7,6},{8,9},{9,8},{10,11... | collective-permute-start | bytes 393224 | tf_op jit(solution)/shard_map/ppermute | solution.py:363
  35.2 1.3 %collective-permute-start.8 = (bf16[256,256]{1,0:T(8,128)(2,1)S(1)}, bf16[256,256]{1,0:T(8,128)(2,1)S(1)}, u32[]{:S(2)}, u32[]{:S(2)}) collective-permute-start(bf16[256,256]{1,0:T(8,128)(2,1)S(1)} %collective-permute-done.6.refs_2_), channel_id=1, source_target_pairs={{0,1},{1,0},{2,3},{3,2},{4,5},{5,4},{6,7},{7,6},{8,9},{9,8},{10,11... | collective-permute-start | bytes 393224 | tf_op jit(solution)/shard_map/ppermute | solution.py:363
  36.6 6.1 %copy-start = (bf16[1,1024,1024]{2,1,0:T(8,128)(2,1)S(1)}, bf16[1,1024,1024]{2,1,0:T(8,128)(2,1)}, u32[]{:S(2)}) copy-start(bf16[1,1024,1024]{2,1,0:T(8,128)(2,1)} %param.16) | copy-start | bytes 6291460
  36.6 6.1 %copy-start.1 = (bf16[1,1024,1024]{2,1,0:T(8,128)(2,1)S(1)}, bf16[1,1024,1024]{2,1,0:T(8,128)(2,1)}, u32[]{:S(2)}) copy-start(bf16[1,1024,1024]{2,1,0:T(8,128)(2,1)} %param.17) | copy-start | bytes 6291460
  37.7 7.6 %collective-permute-start.12 = (bf16[192,256]{1,0:T(8,128)(2,1)S(1)}, bf16[192,256]{1,0:T(8,128)(2,1)S(1)}, u32[]{:S(2)}, u32[]{:S(2)}) collective-permute-start(bf16[192,256]{1,0:T(8,128)(2,1)S(1)} %get-tuple-element.73), channel_id=1, source_target_pairs={{0,12},{1,13},{2,14},{3,15},{4,8},{5,9},{6,10},{7,11},{8,4},{9,5},... | collective-permute-start | bytes 294920 | tf_op jit(solution)/shard_map/ppermute | solution.py:363
  41.1 13.0 %collective-permute-start.16 = (bf16[192,512]{1,0:T(8,128)(2,1)S(1)}, bf16[192,512]{1,0:T(8,128)(2,1)S(1)}, u32[]{:S(2)}, u32[]{:S(2)}) collective-permute-start(bf16[192,512]{1,0:T(8,128)(2,1)S(1)} %get-tuple-element.78), channel_id=1, source_target_pairs={{0,8},{1,9},{2,10},{3,11},{4,12},{5,13},{6,14},{7,15},{8,0},{9,1},... | collective-permute-start | bytes 589832 | tf_op jit(solution)/shard_map/ppermute | solution.py:363
  41.1 13.0 %collective-permute-start.18 = (bf16[192,512]{1,0:T(8,128)(2,1)S(1)}, bf16[192,512]{1,0:T(8,128)(2,1)S(1)}, u32[]{:S(2)}, u32[]{:S(2)}) collective-permute-start(bf16[192,512]{1,0:T(8,128)(2,1)S(1)} %get-tuple-element.81), channel_id=1, source_target_pairs={{0,4},{1,5},{2,6},{3,7},{4,0},{5,1},{6,2},{7,3},{8,12},{9,13},{10,... | collective-permute-start | bytes 589832 | tf_op jit(solution)/shard_map/ppermute | solution.py:363
  45.3 9.3 %collective-permute-start.13 = (bf16[2,192,256]{2,1,0:T(8,128)(2,1)S(1)}, bf16[2,192,256]{2,1,0:T(8,128)(2,1)S(1)}, u32[]{:S(2)}, u32[]{:S(2)}) collective-permute-start(bf16[2,192,256]{2,1,0:T(8,128)(2,1)S(1)} %get-tuple-element.74), channel_id=1, source_target_pairs={{0,1},{1,0},{2,3},{3,2},{4,5},{5,4},{6,7},{7,6},{8,9},{9,8},{10,11... | collective-permute-start | bytes 589832 | tf_op jit(solution)/shard_map/ppermute | solution.py:363
  45.3 9.3 %collective-permute-start.14 = (bf16[192,256]{1,0:T(8,128)(2,1)S(1)}, bf16[192,256]{1,0:T(8,128)(2,1)S(1)}, u32[]{:S(2)}, u32[]{:S(2)}) collective-permute-start(bf16[192,256]{1,0:T(8,128)(2,1)S(1)} %collective-permute-done.12.refs_0_), channel_id=1, source_target_pairs={{0,2},{1,3},{2,0},{3,1},{4,6},{5,7},{6,4},{7,5},{8,10},{9,11},{10,... | collective-permute-start | bytes 294920 | tf_op jit(solution)/shard_map/ppermute | solution.py:363
  54.0 1.4 %collective-permute-start.17 = (bf16[192,512]{1,0:T(8,128)(2,1)S(1)}, bf16[192,512]{1,0:T(8,128)(2,1)S(1)}, u32[]{:S(2)}, u32[]{:S(2)}) collective-permute-start(bf16[192,512]{1,0:T(8,128)(2,1)S(1)} %collective-permute-done.16.refs_0_), channel_id=1, source_target_pairs={{0,1},{1,0},{2,3},{3,2},{4,5},{5,4},{6,7},{7,6},{8,9},{9,8},{10,11... | collective-permute-start | bytes 589832 | tf_op jit(solution)/shard_map/ppermute | solution.py:363
  54.0 1.7 %collective-permute-start.19 = (bf16[192,512]{1,0:T(8,128)(2,1)S(1)}, bf16[192,512]{1,0:T(8,128)(2,1)S(1)}, u32[]{:S(2)}, u32[]{:S(2)}) collective-permute-start(bf16[192,512]{1,0:T(8,128)(2,1)S(1)} %collective-permute-done.18.refs_2_), channel_id=1, source_target_pairs={{0,1},{1,0},{2,3},{3,2},{4,5},{5,4},{6,7},{7,6},{8,9},{9,8},{10,11... | collective-permute-start | bytes 589832 | tf_op jit(solution)/shard_map/ppermute | solution.py:363
  57.6 1.8 %collective-permute-start.20 = (bf16[2,384,256]{2,1,0:T(8,128)(2,1)S(1)}, bf16[2,384,256]{2,1,0:T(8,128)(2,1)S(1)}, u32[]{:S(2)}, u32[]{:S(2)}) collective-permute-start(bf16[2,384,256]{2,1,0:T(8,128)(2,1)S(1)} %get-tuple-element.83), channel_id=1, source_target_pairs={{0,1},{1,0},{2,3},{3,2},{4,5},{5,4},{6,7},{7,6},{8,9},{9,8},{10,11... | collective-permute-start | bytes 1179656 | tf_op jit(solution)/shard_map/ppermute | solution.py:363
  57.9 13.7 %collective-permute-start.15 = (bf16[192,256]{1,0:T(8,128)(2,1)S(1)}, bf16[192,256]{1,0:T(8,128)(2,1)S(1)}, u32[]{:S(2)}, u32[]{:S(2)}) collective-permute-start(bf16[192,256]{1,0:T(8,128)(2,1)S(1)} %get-tuple-element.75), channel_id=1, source_target_pairs={{0,2},{1,3},{2,0},{3,1},{4,6},{5,7},{6,4},{7,5},{8,10},{9,11},{10,... | collective-permute-start | bytes 294920 | tf_op jit(solution)/shard_map/ppermute | solution.py:363
  58.5 2.2 %collective-permute-start.21 = (bf16[192,256]{1,0:T(8,128)(2,1)S(1)}, bf16[192,256]{1,0:T(8,128)(2,1)S(1)}, u32[]{:S(2)}, u32[]{:S(2)}) collective-permute-start(bf16[192,256]{1,0:T(8,128)(2,1)S(1)} %collective-permute-done.12.refs_0_), channel_id=1, source_target_pairs={{0,1},{1,0},{2,3},{3,2},{4,5},{5,4},{6,7},{7,6},{8,9},{9,8},{10,11... | collective-permute-start | bytes 294920 | tf_op jit(solution)/shard_map/ppermute | solution.py:363
  58.5 2.2 %collective-permute-start.22 = (bf16[192,256]{1,0:T(8,128)(2,1)S(1)}, bf16[192,256]{1,0:T(8,128)(2,1)S(1)}, u32[]{:S(2)}, u32[]{:S(2)}) collective-permute-start(bf16[192,256]{1,0:T(8,128)(2,1)S(1)} %collective-permute-done.14.refs_1_), channel_id=1, source_target_pairs={{0,1},{1,0},{2,3},{3,2},{4,5},{5,4},{6,7},{7,6},{8,9},{9,8},{10,11... | collective-permute-start | bytes 294920 | tf_op jit(solution)/shard_map/ppermute | solution.py:363
  59.5 5.5 %collective-permute-start.25 = (bf16[192,256]{1,0:T(8,128)(2,1)S(1)}, bf16[192,256]{1,0:T(8,128)(2,1)S(1)}, u32[]{:S(2)}, u32[]{:S(2)}) collective-permute-start(bf16[192,256]{1,0:T(8,128)(2,1)S(1)} %fusion.4), channel_id=1, source_target_pairs={{0,2},{1,3},{2,0},{3,1},{4,6},{5,7},{6,4},{7,5},{8,10},{9,11},{10,... | collective-permute-start | bytes 294920 | tf_op jit(solution)/shard_map/ppermute | solution.py:363
  61.8 2.7 %collective-permute-start.26 = (bf16[2,192,256]{2,1,0:T(8,128)(2,1)S(1)}, bf16[2,192,256]{2,1,0:T(8,128)(2,1)S(1)}, u32[]{:S(2)}, u32[]{:S(2)}) collective-permute-start(bf16[2,192,256]{2,1,0:T(8,128)(2,1)S(1)} %get-tuple-element.87), channel_id=1, source_target_pairs={{0,1},{1,0},{2,3},{3,2},{4,5},{5,4},{6,7},{7,6},{8,9},{9,8},{10,11... | collective-permute-start | bytes 589832 | tf_op jit(solution)/shard_map/ppermute | solution.py:363
  61.9 10.0 %collective-permute-start.24 = (bf16[192,256]{1,0:T(8,128)(2,1)S(1)}, bf16[192,256]{1,0:T(8,128)(2,1)S(1)}, u32[]{:S(2)}, u32[]{:S(2)}) collective-permute-start(bf16[192,256]{1,0:T(8,128)(2,1)S(1)} %get-tuple-element.95), channel_id=1, source_target_pairs={{0,6},{1,7},{2,4},{3,5},{4,2},{5,3},{6,0},{7,1},{8,14},{9,15},{10,... | collective-permute-start | bytes 294920 | tf_op jit(solution)/shard_map/ppermute | solution.py:363
  62.9 9.0 %collective-permute-start.23 = (bf16[192,256]{1,0:T(8,128)(2,1)S(1)}, bf16[192,256]{1,0:T(8,128)(2,1)S(1)}, u32[]{:S(2)}, u32[]{:S(2)}) collective-permute-start(bf16[192,256]{1,0:T(8,128)(2,1)S(1)} %get-tuple-element.96), channel_id=1, source_target_pairs={{0,4},{1,5},{2,6},{3,7},{4,0},{5,1},{6,2},{7,3},{8,12},{9,13},{10,... | collective-permute-start | bytes 294920 | tf_op jit(solution)/shard_map/ppermute | solution.py:363
  65.1 5.1 %collective-permute-start.28 = (bf16[192,256]{1,0:T(8,128)(2,1)S(1)}, bf16[192,256]{1,0:T(8,128)(2,1)S(1)}, u32[]{:S(2)}, u32[]{:S(2)}) collective-permute-start(bf16[192,256]{1,0:T(8,128)(2,1)S(1)} %fusion.5), channel_id=1, source_target_pairs={{0,2},{1,3},{2,0},{3,1},{4,6},{5,7},{6,4},{7,5},{8,10},{9,11},{10,... | collective-permute-start | bytes 294920 | tf_op jit(solution)/shard_map/ppermute | solution.py:363
  65.6 7.7 %collective-permute-start.27 = (bf16[192,256]{1,0:T(8,128)(2,1)S(1)}, bf16[192,256]{1,0:T(8,128)(2,1)S(1)}, u32[]{:S(2)}, u32[]{:S(2)}) collective-permute-start(bf16[192,256]{1,0:T(8,128)(2,1)S(1)} %fusion.3), channel_id=1, source_target_pairs={{0,8},{1,9},{2,10},{3,11},{4,12},{5,13},{6,14},{7,15},{8,0},{9,1},... | collective-permute-start | bytes 294920 | tf_op jit(solution)/shard_map/ppermute | solution.py:363
  70.1 6.5 %collective-permute-start.29 = (bf16[192,256]{1,0:T(8,128)(2,1)S(1)}, bf16[192,256]{1,0:T(8,128)(2,1)S(1)}, u32[]{:S(2)}, u32[]{:S(2)}) collective-permute-start(bf16[192,256]{1,0:T(8,128)(2,1)S(1)} %fusion.1), channel_id=1, source_target_pairs={{0,12},{1,13},{2,14},{3,15},{4,8},{5,9},{6,10},{7,11},{8,4},{9,5},... | collective-permute-start | bytes 294920 | tf_op jit(solution)/shard_map/ppermute | solution.py:363

commit v18 on v17

--- a/solution.py
+++ b/solution.py
@@ -11,7 +11,6 @@
 HEAD_DIM = 128
 SHARPNESS = HEAD_DIM**-0.5 * math.log2(math.e)
 DIRECT = 8
-CUTS = 1
 TILE = 256
 F32, BF16 = jnp.float32, jnp.bfloat16
 PARAMS = pltpu.CompilerParams(vmem_limit_bytes=20 * 2**20)
@@ -31,54 +30,52 @@
     return lax.axis_index("expert"), lax.axis_index("mp")
 
 
-def query_kernel(tokens, weight, source, out, staged, tokens_here, weight_here, sems):
-    features = tokens.shape[1]
-    depth = features // CUTS
-    copies, later = [], []
-    for i in range(CUTS):
-        part = pl.ds(i * depth, depth)
-        copies.append(
-            (
-                pltpu.make_async_copy(tokens.at[:, part], tokens_here.at[:, part], sems.at[0, i]),
-                pltpu.make_async_copy(weight.at[part, :], weight_here.at[part, :], sems.at[1, i]),
-            )
-        )
-        rows = pl.ds(i * (source.shape[1] // CUTS), source.shape[1] // CUTS)
-        later.append(pltpu.make_async_copy(source.at[:, rows], staged.at[:, rows], sems.at[2, i]))
-    for pair in copies:
-        for copy in pair:
-            copy.start()
-    for copy in later:
+def query_kernel(tokens, weight, out, tokens_here, weight_here, sems):
+    copies = [
+        pltpu.make_async_copy(tokens, tokens_here, sems.at[0]),
+        pltpu.make_async_copy(weight, weight_here, sems.at[1]),
+    ]
+    for copy in copies:
         copy.start()
-    total = jnp.zeros(out.shape, F32)
-    for i, pair in enumerate(copies):
-        for copy in pair:
-            copy.wait()
-        part = slice(i * depth, (i + 1) * depth)
-        total += dot(tokens_here[:, part], weight_here[part, :])
-    out[...] = total.astype(BF16)
-    for copy in later:
+    for copy in copies:
         copy.wait()
-
-
-def ask(tokens, weight, source):
+    out[...] = dot(tokens_here[...], weight_here[...]).astype(BF16)
+
+
+def ask(tokens, weight):
     return pl.pallas_call(
         query_kernel,
-        in_specs=[pl.BlockSpec(memory_space=pltpu.HBM)] * 3,
-        out_specs=[WHOLE] * 2,
-        out_shape=[
-            jax.ShapeDtypeStruct((tokens.shape[0], weight.shape[1]), BF16),
-            jax.ShapeDtypeStruct(source.shape, BF16),
-        ],
+        in_specs=[pl.BlockSpec(memory_space=pltpu.HBM)] * 2,
+        out_specs=WHOLE,
+        out_shape=jax.ShapeDtypeStruct((tokens.shape[0], weight.shape[1]), BF16),
         scratch_shapes=[
             pltpu.VMEM(tokens.shape, BF16),
             pltpu.VMEM(weight.shape, BF16),
-            pltpu.SemaphoreType.DMA((3, CUTS)),
+            pltpu.SemaphoreType.DMA((2,)),
         ],
         compiler_params=PARAMS,
         cost_estimate=CHEAP,
         name="query",
-    )(in_hbm(tokens), in_hbm(weight), in_hbm(source))
+    )(in_hbm(tokens), in_hbm(weight))
+
+
+def stage_kernel(source, out, sem):
+    copy = pltpu.make_async_copy(source, out, sem)
+    copy.start()
+    copy.wait()
+
+
+def stage(source):
+    return pl.pallas_call(
+        stage_kernel,
+        in_specs=[pl.BlockSpec(memory_space=pltpu.HBM)],
+        out_specs=WHOLE,
+        out_shape=jax.ShapeDtypeStruct(source.shape, BF16),
+        scratch_shapes=[pltpu.SemaphoreType.DMA],
+        compiler_params=PARAMS,
+        cost_estimate=CHEAP,
+        name="stage",
+    )(in_hbm(source))
 
 
 def attend_kernel(queries, source, out):
@@ -371,7 +368,8 @@
 
     steps = range(groups) if direct else [0]
 
-    queries, source = ask(tokens, query_weight, encoder_states[0])
+    queries = ask(tokens, query_weight)
+    source = stage(after(encoder_states[0], queries))
     expert_bits = bits_of(groups)
     bits = bits_of(slices)
     if direct:

time: 77.7 us -> 77.7 us (level)
  waiting for transfers between devices: 32.6 us -> 31.5 us
  Pallas kernels: 12.5 us -> 13.5 us
    ppermute x30, waiting for transfers between devices: 32.6 us -> 31.5 us  [hop(): return lax.ppermute(value, ('expert', 'mp'), moves)]
    pallas_call x0 -> x1, Pallas kernels: none -> 1.05 us  [stage(): pl.pallas_call(stage_kernel, in_specs=[pl.BlockSpec(memory_space=pltpu.HB...]
  transfers between devices with their start and end apart: 30 -> 30, of which waited for: 13 -> 13; matrix products, arithmetic and copies ran while one was open for 0% -> 0% of each run, Pallas kernels for 11% -> 13%
where the time goes in v18:
time: 77.7 us; the launch traced here: 77.5 us
  waiting for transfers between devices  31.5 us (41%)
  starting transfers between devices  31.2 us (40%)
  Pallas kernels  13.5 us (17%)
  between operations  1.01 us (1%)
    ppermute x30, waiting for transfers between devices, hop(): return lax.ppermute(value, ('expert', 'mp'), moves)  31.5 us
    ppermute x30, starting transfers between devices, hop(): return lax.ppermute(value, ('expert', 'mp'), moves)  31.2 us
    pallas_call x3, Pallas kernels, run_expert(): pl.pallas_call(functools.partial(expert_kernel, tuple(map(tuple, orders))...  3.86 us
    pallas_call x4, Pallas kernels, attend(): pl.pallas_call(attend_kernel, in_specs=[WHOLE] * 2, out_specs=WHOLE, out_...  2.8 us
    pallas_call x4, Pallas kernels, combine(): pl.pallas_call(functools.partial(combine_kernel, len(parts)), in_specs=[W...  1.59 us
  transfers between devices with their start and end apart: 30, of which 13 were waited for; matrix products, arithmetic and copies ran while one was open for 0% of the time, Pallas kernels for 13%

profile of v18, /device:TPU:0, one launch (start us, length us, event | category | flops | bytes accessed | tf_op | source)
XLA Modules:
  0.0 77.5 jit_solution(9170866856997229912)
XLA Ops:
  0.0 2.9 %collective-permute-start.9 = (bf16[256,1024]{1,0:T(8,128)(2,1)}, bf16[256,1024]{1,0:T(8,128)(2,1)S(1)}, u32[]{:S(2)}, u32[]{:S(2)}) collective-permute-start(bf16[256,1024]{1,0:T(8,128)(2,1)} %refs_5_), channel_id=1, source_target_pairs={{0,2},{1,3},{2,0},{3,1},{4,6},{5,7},{6,4},{7,5},{8,10},{9,11},{10,... | collective-permute-start | bytes 1572872 | tf_op jit(solution)/shard_map/ppermute | solution.py:360
  2.9 1.5 %query.1.queries = bf16[256,256]{1,0:T(8,128)(2,1)S(1)} custom-call(bf16[256,1024]{1,0:T(8,128)(2,1)} %refs_0_.1, bf16[1024,256]{1,0:T(8,128)(2,1)} %weight.1), custom_call_target="tpu_custom_call" | custom-call | tf_op jit(solution)/shard_map/query/pallas_call | solution.py:46
  4.5 2.7 %collective-permute-start.1 = (bf16[256,256]{1,0:T(8,128)(2,1)S(1)}, bf16[256,256]{1,0:T(8,128)(2,1)S(1)}, u32[]{:S(2)}, u32[]{:S(2)}) collective-permute-start(bf16[256,256]{1,0:T(8,128)(2,1)S(1)} %query.1.queries), channel_id=1, source_target_pairs={{0,8},{1,9},{2,10},{3,11},{4,12},{5,13},{6,14},{7,15},{8,0},{9,1},... | collective-permute-start | bytes 393224 | tf_op jit(solution)/shard_map/ppermute | solution.py:360
  7.1 1.6 %collective-permute-start = (bf16[256,256]{1,0:T(8,128)(2,1)S(1)}, bf16[256,256]{1,0:T(8,128)(2,1)S(1)}, u32[]{:S(2)}, u32[]{:S(2)}) collective-permute-start(bf16[256,256]{1,0:T(8,128)(2,1)S(1)} %query.1.queries), channel_id=1, source_target_pairs={{0,4},{1,5},{2,6},{3,7},{4,0},{5,1},{6,2},{7,3},{8,12},{9,13},{10,... | collective-permute-start | bytes 393224 | tf_op jit(solution)/shard_map/ppermute | solution.py:360
  8.7 1.0 %stage.1.source = bf16[2,512,256]{2,1,0:T(8,128)(2,1)S(1)} custom-call(bf16[2,512,256]{2,1,0:T(8,128)(2,1)} %bitcast.39), custom_call_target="tpu_custom_call" | custom-call | tf_op jit(solution)/shard_map/stage/pallas_call | solution.py:69
  9.8 0.0 copy-start.3
  9.8 0.0 copy-start.5
  9.8 0.0 copy-start.2
  9.8 0.7 attend.4.refs_0_
  10.5 2.8 %collective-permute-done.1.queries = bf16[256,256]{1,0:T(8,128)(2,1)S(1)} collective-permute-done((bf16[256,256]{1,0:T(8,128)(2,1)S(1)}, bf16[256,256]{1,0:T(8,128)(2,1)S(1)}, u32[]{:S(2)}, u32[]{:S(2)}) %collective-permute-start.1) | collective-permute-done | bytes 131104 | tf_op jit(solution)/shard_map/ppermute | solution.py:360
  13.3 0.6 collective-permute-start.4
  13.9 0.7 attend.5
  14.6 3.4 %collective-permute-start.3 = (bf16[256,256]{1,0:T(8,128)(2,1)S(1)}, bf16[256,256]{1,0:T(8,128)(2,1)S(1)}, u32[]{:S(2)}, u32[]{:S(2)}) collective-permute-start(bf16[256,256]{1,0:T(8,128)(2,1)S(1)} %attend.5), channel_id=1, source_target_pairs={{0,8},{1,9},{2,10},{3,11},{4,12},{5,13},{6,14},{7,15},{8,0},{9,1},... | collective-permute-start | bytes 393224 | tf_op jit(solution)/shard_map/ppermute | solution.py:360
  18.0 0.7 attend.6
  18.7 0.1 collective-permute-start.2
  18.8 0.0 collective-permute-done.4.queries
  18.8 0.7 attend.7
  19.5 0.0 copy-start.4
  19.5 5.9 %collective-permute-start.5 = (bf16[256,256]{1,0:T(8,128)(2,1)S(1)}, bf16[256,256]{1,0:T(8,128)(2,1)S(1)}, u32[]{:S(2)}, u32[]{:S(2)}) collective-permute-start(bf16[256,256]{1,0:T(8,128)(2,1)S(1)} %attend.7), channel_id=1, source_target_pairs={{0,12},{1,13},{2,14},{3,15},{4,8},{5,9},{6,10},{7,11},{8,4},{9,5},... | collective-permute-start | bytes 393224 | tf_op jit(solution)/shard_map/ppermute | solution.py:360
  26.1 0.0 collective-permute-done.2.refs_1_
  26.1 2.8 %collective-permute-done.5.refs_3_ = bf16[256,256]{1,0:T(8,128)(2,1)S(1)} collective-permute-done((bf16[256,256]{1,0:T(8,128)(2,1)S(1)}, bf16[256,256]{1,0:T(8,128)(2,1)S(1)}, u32[]{:S(2)}, u32[]{:S(2)}) %collective-permute-start.5) | collective-permute-done | bytes 131104 | tf_op jit(solution)/shard_map/ppermute | solution.py:360
  28.9 0.1 pick.1.refs_1_
  29.1 0.1 collective-permute-start.10
  29.2 0.5 collective-permute-start.11
  29.7 0.5 collective-permute-start.6
  30.2 1.0 %route.1 = (s32[256,2]{1,0:T(8,128)S(1)}, bf16[192,256]{1,0:T(8,128)(2,1)S(1)}, bf16[192,256]{1,0:T(8,128)(2,1)S(1)}, bf16[192,256]{1,0:T(8,128)(2,1)S(1)}, bf16...) custom-call(s32[2,256]{1,0:T(2,128)S(1)} %bitcast.38), custom_call_target="tpu_custom_call" | custom-call | tf_op jit(solution)/shard_map/route/pallas_call | solution.py:174
  31.2 0.1 collective-permute-start.7
  31.3 3.9 %collective-permute-done.6.refs_2_ = bf16[256,256]{1,0:T(8,128)(2,1)S(1)} collective-permute-done((bf16[256,256]{1,0:T(8,128)(2,1)S(1)}, bf16[256,256]{1,0:T(8,128)(2,1)S(1)}, u32[]{:S(2)}, u32[]{:S(2)}) %collective-permute-start.6) | collective-permute-done | bytes 131104 | tf_op jit(solution)/shard_map/ppermute | solution.py:360
  35.2 1.3 %collective-permute-done.8.refs_4_ = bf16[256,256]{1,0:T(8,128)(2,1)S(1)} collective-permute-done((bf16[256,256]{1,0:T(8,128)(2,1)S(1)}, bf16[256,256]{1,0:T(8,128)(2,1)S(1)}, u32[]{:S(2)}, u32[]{:S(2)}) %collective-permute-start.8) | collective-permute-done | bytes 131104 | tf_op jit(solution)/shard_map/ppermute | solution.py:360
  36.5 0.0 copy-start
  36.5 0.0 copy-start.1
  36.6 1.1 %state.1 = (bf16[256,1024]{1,0:T(8,128)(2,1)S(1)}, bf16[192,512]{1,0:T(8,128)(2,1)S(1)}, bf16[192,256]{1,0:T(8,128)(2,1)S(1)}, bf16[192,512]{1,0:T(8,128)(2,1)S(1)}) custom-call(bf16[256,1024]{1,0:T(8,128)(2,1)S(1)} %copy-done.2, bf16[256,256]{1,0:T(8,128)(2,1)S(1)} %pick.1.refs_1_, bf16[256,256]{1,0:T(8,128)(2,1)S(1)} %collective-permute-done.6.refs_2_, ...), custom_call_target="tpu_custom_call" | custom-call | tf_op jit(solution)/shard_map/state/pallas_call | solution.py:207
  37.6 3.4 %collective-permute-start.12 = (bf16[192,256]{1,0:T(8,128)(2,1)S(1)}, bf16[192,256]{1,0:T(8,128)(2,1)S(1)}, u32[]{:S(2)}, u32[]{:S(2)}) collective-permute-start(bf16[192,256]{1,0:T(8,128)(2,1)S(1)} %get-tuple-element.71), channel_id=1, source_target_pairs={{0,12},{1,13},{2,14},{3,15},{4,8},{5,9},{6,10},{7,11},{8,4},{9,5},... | collective-permute-start | bytes 294920 | tf_op jit(solution)/shard_map/ppermute | solution.py:360
  41.0 1.1 %collective-permute-start.18 = (bf16[192,512]{1,0:T(8,128)(2,1)S(1)}, bf16[192,512]{1,0:T(8,128)(2,1)S(1)}, u32[]{:S(2)}, u32[]{:S(2)}) collective-permute-start(bf16[192,512]{1,0:T(8,128)(2,1)S(1)} %get-tuple-element.79), channel_id=1, source_target_pairs={{0,4},{1,5},{2,6},{3,7},{4,0},{5,1},{6,2},{7,3},{8,12},{9,13},{10,... | collective-permute-start | bytes 589832 | tf_op jit(solution)/shard_map/ppermute | solution.py:360
  42.1 0.5 home.1
  42.6 1.0 %expert.3 = (f32[2,192,256]{2,1,0:T(8,128)S(1)}, bf16[2,192,256]{2,1,0:T(8,128)(2,1)S(1)}) custom-call(bf16[192,512]{1,0:T(8,128)(2,1)S(1)} %get-tuple-element.67.refs_0_, bf16[192,512]{1,0:T(8,128)(2,1)S(1)} %get-tuple-element.68.refs_1_, bf16[1024,1024]{1,0:T(8,128)(2,1)S(1)} %bitcast.31, bf16[1024,1024]{1,0:T(8,128)(2,1)S(1)} %bitcast.34), custom_call_target="tpu_custom_call" | custom-call | tf_op jit(solution)/shard_map/expert/pallas_call | solution.py:286
  43.6 1.6 %collective-permute-done.12.refs_0_ = bf16[192,256]{1,0:T(8,128)(2,1)S(1)} collective-permute-done((bf16[192,256]{1,0:T(8,128)(2,1)S(1)}, bf16[192,256]{1,0:T(8,128)(2,1)S(1)}, u32[]{:S(2)}, u32[]{:S(2)}) %collective-permute-start.12) | collective-permute-done | bytes 98336 | tf_op jit(solution)/shard_map/ppermute | solution.py:360
  45.2 0.5 collective-permute-start.14
  45.8 8.2 %collective-permute-done.16.refs_0_ = bf16[192,512]{1,0:T(8,128)(2,1)S(1)} collective-permute-done((bf16[192,512]{1,0:T(8,128)(2,1)S(1)}, bf16[192,512]{1,0:T(8,128)(2,1)S(1)}, u32[]{:S(2)}, u32[]{:S(2)}) %collective-permute-start.16) | collective-permute-done | bytes 196640 | tf_op jit(solution)/shard_map/ppermute | solution.py:360
  54.0 0.5 collective-permute-start.19
  54.6 0.9 %collective-permute-done.17.refs_1_ = bf16[192,512]{1,0:T(8,128)(2,1)S(1)} collective-permute-done((bf16[192,512]{1,0:T(8,128)(2,1)S(1)}, bf16[192,512]{1,0:T(8,128)(2,1)S(1)}, u32[]{:S(2)}, u32[]{:S(2)}) %collective-permute-start.17) | collective-permute-done | bytes 196640 | tf_op jit(solution)/shard_map/ppermute | solution.py:360
  55.4 0.3 collective-permute-done.19.refs_3_
  55.7 1.8 %expert.4 = (f32[2,384,256]{2,1,0:T(8,128)S(1)}, bf16[2,384,256]{2,1,0:T(8,128)(2,1)S(1)}) custom-call(bf16[192,512]{1,0:T(8,128)(2,1)S(1)} %collective-permute-done.16.refs_0_, bf16[192,512]{1,0:T(8,128)(2,1)S(1)} %collective-permute-done.17.refs_1_, bf16[192,512]{1,0:T(8,128)(2,1)S(1)} %collective-permute-done.18.refs_2_, ...), custom_call_target="tpu_custom_call" | custom-call | tf_op jit(solution)/shard_map/expert/pallas_call | solution.py:286
  57.5 0.3 collective-permute-start.20
  57.9 0.6 collective-permute-start.15
  58.5 0.5 collective-permute-start.22
  59.0 0.4 collective-permute-done.20
  59.3 0.1 convert_add_fusion
  59.5 1.2 %collective-permute-start.25 = (bf16[192,256]{1,0:T(8,128)(2,1)S(1)}, bf16[192,256]{1,0:T(8,128)(2,1)S(1)}, u32[]{:S(2)}, u32[]{:S(2)}) collective-permute-start(bf16[192,256]{1,0:T(8,128)(2,1)S(1)} %fusion.4), channel_id=1, source_target_pairs={{0,2},{1,3},{2,0},{3,1},{4,6},{5,7},{6,4},{7,5},{8,10},{9,11},{10,... | collective-permute-start | bytes 294920 | tf_op jit(solution)/shard_map/ppermute | solution.py:360
  60.7 1.0 %expert.5 = (f32[2,192,256]{2,1,0:T(8,128)S(1)}, bf16[2,192,256]{2,1,0:T(8,128)(2,1)S(1)}) custom-call(bf16[192,256]{1,0:T(8,128)(2,1)S(1)} %collective-permute-done.12.refs_0_, bf16[192,256]{1,0:T(8,128)(2,1)S(1)} %collective-permute-done.14.refs_1_, bf16[192,256]{1,0:T(8,128)(2,1)S(1)} %collective-permute-done.21.refs_2_, ...), custom_call_target="tpu_custom_call" | custom-call | tf_op jit(solution)/shard_map/expert/pallas_call | solution.py:286
  61.7 0.1 collective-permute-start.26
  61.8 1.0 %collective-permute-start.24 = (bf16[192,256]{1,0:T(8,128)(2,1)S(1)}, bf16[192,256]{1,0:T(8,128)(2,1)S(1)}, u32[]{:S(2)}, u32[]{:S(2)}) collective-permute-start(bf16[192,256]{1,0:T(8,128)(2,1)S(1)} %get-tuple-element.93), channel_id=1, source_target_pairs={{0,6},{1,7},{2,4},{3,5},{4,2},{5,3},{6,0},{7,1},{8,14},{9,15},{10,... | collective-permute-start | bytes 294920 | tf_op jit(solution)/shard_map/ppermute | solution.py:360
  62.8 1.6 %collective-permute-start.23 = (bf16[192,256]{1,0:T(8,128)(2,1)S(1)}, bf16[192,256]{1,0:T(8,128)(2,1)S(1)}, u32[]{:S(2)}, u32[]{:S(2)}) collective-permute-start(bf16[192,256]{1,0:T(8,128)(2,1)S(1)} %get-tuple-element.94), channel_id=1, source_target_pairs={{0,4},{1,5},{2,6},{3,7},{4,0},{5,1},{6,2},{7,3},{8,12},{9,13},{10,... | collective-permute-start | bytes 294920 | tf_op jit(solution)/shard_map/ppermute | solution.py:360
  64.5 0.5 collective-permute-done.25
  65.0 0.5 collective-permute-start.28
  65.6 0.1 collective-permute-start.27
  65.6 4.4 %collective-permute-done.28 = bf16[192,256]{1,0:T(8,128)(2,1)S(1)} collective-permute-done((bf16[192,256]{1,0:T(8,128)(2,1)S(1)}, bf16[192,256]{1,0:T(8,128)(2,1)S(1)}, u32[]{:S(2)}, u32[]{:S(2)}) %collective-permute-start.28) | collective-permute-done | bytes 98336 | tf_op jit(solution)/shard_map/ppermute | solution.py:360
  70.1 1.5 %collective-permute-start.29 = (bf16[192,256]{1,0:T(8,128)(2,1)S(1)}, bf16[192,256]{1,0:T(8,128)(2,1)S(1)}, u32[]{:S(2)}, u32[]{:S(2)}) collective-permute-start(bf16[192,256]{1,0:T(8,128)(2,1)S(1)} %fusion.1), channel_id=1, source_target_pairs={{0,12},{1,13},{2,14},{3,15},{4,8},{5,9},{6,10},{7,11},{8,4},{9,5},... | collective-permute-start | bytes 294920 | tf_op jit(solution)/shard_map/ppermute | solution.py:360
  71.6 0.2 combine.4.base
  71.9 0.2 combine.5.base
  72.1 1.2 %collective-permute-done.27.refs_0_ = bf16[192,256]{1,0:T(8,128)(2,1)S(1)} collective-permute-done((bf16[192,256]{1,0:T(8,128)(2,1)S(1)}, bf16[192,256]{1,0:T(8,128)(2,1)S(1)}, u32[]{:S(2)}, u32[]{:S(2)}) %collective-permute-start.27) | collective-permute-done | bytes 98336 | tf_op jit(solution)/shard_map/ppermute | solution.py:360
  73.3 0.2 combine.6.base
  73.5 3.1 %collective-permute-done.29.refs_0_ = bf16[192,256]{1,0:T(8,128)(2,1)S(1)} collective-permute-done((bf16[192,256]{1,0:T(8,128)(2,1)S(1)}, bf16[192,256]{1,0:T(8,128)(2,1)S(1)}, u32[]{:S(2)}, u32[]{:S(2)}) %collective-permute-start.29) | collective-permute-done | bytes 98336 | tf_op jit(solution)/shard_map/ppermute | solution.py:360
  76.6 0.9 %combine.7 = bf16[256,256]{1,0:T(8,128)(2,1)} custom-call(f32[256,2]{1,0:T(8,128)S(1)} %get-tuple-element.63.gates, f32[256,256]{1,0:T(8,128)S(1)} %combine.6.base, bf16[256,192]{1,0:T(8,128)(2,1)S(1)} %get-tuple-element.91.first, bf16[256,192]{1,0:T(8,128)(2,1)S(1)} %get-tuple-element.92.second, bf16[192,256]{1,0:T(8,128)(2,1)S(1)} %collective-permute-done.29.refs_0_), custom_call_target="tpu_custom_call" | custom-call | tf_op jit(solution)/shard_map/combine/pallas_call | solution.py:312
  (35 shorter events, 0.3 us)
Async XLA Ops:
  0.0 29.2 %collective-permute-start.9 = (bf16[256,1024]{1,0:T(8,128)(2,1)}, bf16[256,1024]{1,0:T(8,128)(2,1)S(1)}, u32[]{:S(2)}, u32[]{:S(2)}) collective-permute-start(bf16[256,1024]{1,0:T(8,128)(2,1)} %refs_5_), channel_id=1, source_target_pairs={{0,2},{1,3},{2,0},{3,1},{4,6},{5,7},{6,4},{7,5},{8,10},{9,11},{10,... | collective-permute-start | bytes 1572872 | tf_op jit(solution)/shard_map/ppermute | solution.py:360
  4.5 8.8 %collective-permute-start.1 = (bf16[256,256]{1,0:T(8,128)(2,1)S(1)}, bf16[256,256]{1,0:T(8,128)(2,1)S(1)}, u32[]{:S(2)}, u32[]{:S(2)}) collective-permute-start(bf16[256,256]{1,0:T(8,128)(2,1)S(1)} %query.1.queries), channel_id=1, source_target_pairs={{0,8},{1,9},{2,10},{3,11},{4,12},{5,13},{6,14},{7,15},{8,0},{9,1},... | collective-permute-start | bytes 393224 | tf_op jit(solution)/shard_map/ppermute | solution.py:360
  7.1 10.9 %collective-permute-start = (bf16[256,256]{1,0:T(8,128)(2,1)S(1)}, bf16[256,256]{1,0:T(8,128)(2,1)S(1)}, u32[]{:S(2)}, u32[]{:S(2)}) collective-permute-start(bf16[256,256]{1,0:T(8,128)(2,1)S(1)} %query.1.queries), channel_id=1, source_target_pairs={{0,4},{1,5},{2,6},{3,7},{4,0},{5,1},{6,2},{7,3},{8,12},{9,13},{10,... | collective-permute-start | bytes 393224 | tf_op jit(solution)/shard_map/ppermute | solution.py:360
  9.8 19.3 %copy-start.3 = (bf16[256,1024]{1,0:T(8,128)(2,1)S(1)}, bf16[256,1024]{1,0:T(8,128)(2,1)}, u32[]{:S(2)}) copy-start(bf16[256,1024]{1,0:T(8,128)(2,1)} %refs_5_) | copy-start | bytes 1572868
  9.8 20.5 %copy-start.5 = (s32[256,2]{0,1:T(2,128)S(1)}, s32[256,2]{0,1:T(2,128)}, u32[]{:S(2)}) copy-start(s32[256,2]{0,1:T(2,128)} %param.15) | copy-start | bytes 6148
  9.8 26.7 %copy-start.2 = (bf16[256,1024]{1,0:T(8,128)(2,1)S(1)}, bf16[256,1024]{1,0:T(8,128)(2,1)}, u32[]{:S(2)}) copy-start(bf16[256,1024]{1,0:T(8,128)(2,1)} %refs_0_.1) | copy-start | bytes 1572868
  13.3 5.5 %collective-permute-start.4 = (bf16[256,256]{1,0:T(8,128)(2,1)S(1)}, bf16[256,256]{1,0:T(8,128)(2,1)S(1)}, u32[]{:S(2)}, u32[]{:S(2)}) collective-permute-start(bf16[256,256]{1,0:T(8,128)(2,1)S(1)} %collective-permute-done.1.queries), channel_id=1, source_target_pairs={{0,4},{1,5},{2,6},{3,7},{4,0},{5,1},{6,2},{7,3},{8,12},{9,13},{10,... | collective-permute-start | bytes 393224 | tf_op jit(solution)/shard_map/ppermute | solution.py:360
  14.6 11.5 %collective-permute-start.3 = (bf16[256,256]{1,0:T(8,128)(2,1)S(1)}, bf16[256,256]{1,0:T(8,128)(2,1)S(1)}, u32[]{:S(2)}, u32[]{:S(2)}) collective-permute-start(bf16[256,256]{1,0:T(8,128)(2,1)S(1)} %attend.5), channel_id=1, source_target_pairs={{0,8},{1,9},{2,10},{3,11},{4,12},{5,13},{6,14},{7,15},{8,0},{9,1},... | collective-permute-start | bytes 393224 | tf_op jit(solution)/shard_map/ppermute | solution.py:360
  18.7 7.4 %collective-permute-start.2 = (bf16[256,256]{1,0:T(8,128)(2,1)S(1)}, bf16[256,256]{1,0:T(8,128)(2,1)S(1)}, u32[]{:S(2)}, u32[]{:S(2)}) collective-permute-start(bf16[256,256]{1,0:T(8,128)(2,1)S(1)} %attend.6), channel_id=1, source_target_pairs={{0,4},{1,5},{2,6},{3,7},{4,0},{5,1},{6,2},{7,3},{8,12},{9,13},{10,... | collective-permute-start | bytes 393224 | tf_op jit(solution)/shard_map/ppermute | solution.py:360
  19.5 22.6 %copy-start.4 = (bf16[1024,4]{0,1:T(4,128)(2,1)S(1)}, bf16[1024,4]{0,1:T(4,128)(2,1)}, u32[]{:S(2)}) copy-start(bf16[1024,4]{0,1:T(4,128)(2,1)} %param.14) | copy-start | bytes 24580
  19.5 9.4 %collective-permute-start.5 = (bf16[256,256]{1,0:T(8,128)(2,1)S(1)}, bf16[256,256]{1,0:T(8,128)(2,1)S(1)}, u32[]{:S(2)}, u32[]{:S(2)}) collective-permute-start(bf16[256,256]{1,0:T(8,128)(2,1)S(1)} %attend.7), channel_id=1, source_target_pairs={{0,12},{1,13},{2,14},{3,15},{4,8},{5,9},{6,10},{7,11},{8,4},{9,5},... | collective-permute-start | bytes 393224 | tf_op jit(solution)/shard_map/ppermute | solution.py:360
  29.1 7.4 %collective-permute-start.10 = (bf16[256,1024]{1,0:T(8,128)(2,1)S(1)}, bf16[256,1024]{1,0:T(8,128)(2,1)S(1)}, u32[]{:S(2)}, u32[]{:S(2)}) collective-permute-start(bf16[256,1024]{1,0:T(8,128)(2,1)S(1)} %copy-done.3), channel_id=1, source_target_pairs={{0,1},{1,0},{2,3},{3,2},{4,5},{5,4},{6,7},{7,6},{8,9},{9,8},{10,11... | collective-permute-start | bytes 1572872 | tf_op jit(solution)/shard_map/ppermute | solution.py:360
  29.2 7.3 %collective-permute-start.11 = (bf16[256,1024]{1,0:T(8,128)(2,1)S(1)}, bf16[256,1024]{1,0:T(8,128)(2,1)S(1)}, u32[]{:S(2)}, u32[]{:S(2)}) collective-permute-start(bf16[256,1024]{1,0:T(8,128)(2,1)S(1)} %collective-permute-done.9.refs_6_), channel_id=1, source_target_pairs={{0,1},{1,0},{2,3},{3,2},{4,5},{5,4},{6,7},{7,6},{8,9},{9,8},{10,11... | collective-permute-start | bytes 1572872 | tf_op jit(solution)/shard_map/ppermute | solution.py:360
  29.7 5.5 %collective-permute-start.6 = (bf16[256,256]{1,0:T(8,128)(2,1)S(1)}, bf16[256,256]{1,0:T(8,128)(2,1)S(1)}, u32[]{:S(2)}, u32[]{:S(2)}) collective-permute-start(bf16[256,256]{1,0:T(8,128)(2,1)S(1)} %pick.1.refs_1_), channel_id=1, source_target_pairs={{0,2},{1,3},{2,0},{3,1},{4,6},{5,7},{6,4},{7,5},{8,10},{9,11},{10,... | collective-permute-start | bytes 393224 | tf_op jit(solution)/shard_map/ppermute | solution.py:360
  31.2 4.0 %collective-permute-start.7 = (bf16[256,256]{1,0:T(8,128)(2,1)S(1)}, bf16[256,256]{1,0:T(8,128)(2,1)S(1)}, u32[]{:S(2)}, u32[]{:S(2)}) collective-permute-start(bf16[256,256]{1,0:T(8,128)(2,1)S(1)} %pick.1.refs_1_), channel_id=1, source_target_pairs={{0,1},{1,0},{2,3},{3,2},{4,5},{5,4},{6,7},{7,6},{8,9},{9,8},{10,11... | collective-permute-start | bytes 393224 | tf_op jit(solution)/shard_map/ppermute | solution.py:360
  35.2 1.3 %collective-permute-start.8 = (bf16[256,256]{1,0:T(8,128)(2,1)S(1)}, bf16[256,256]{1,0:T(8,128)(2,1)S(1)}, u32[]{:S(2)}, u32[]{:S(2)}) collective-permute-start(bf16[256,256]{1,0:T(8,128)(2,1)S(1)} %collective-permute-done.6.refs_2_), channel_id=1, source_target_pairs={{0,1},{1,0},{2,3},{3,2},{4,5},{5,4},{6,7},{7,6},{8,9},{9,8},{10,11... | collective-permute-start | bytes 393224 | tf_op jit(solution)/shard_map/ppermute | solution.py:360
  36.5 6.1 %copy-start = (bf16[1,1024,1024]{2,1,0:T(8,128)(2,1)S(1)}, bf16[1,1024,1024]{2,1,0:T(8,128)(2,1)}, u32[]{:S(2)}) copy-start(bf16[1,1024,1024]{2,1,0:T(8,128)(2,1)} %param.16) | copy-start | bytes 6291460
  36.5 6.1 %copy-start.1 = (bf16[1,1024,1024]{2,1,0:T(8,128)(2,1)S(1)}, bf16[1,1024,1024]{2,1,0:T(8,128)(2,1)}, u32[]{:S(2)}) copy-start(bf16[1,1024,1024]{2,1,0:T(8,128)(2,1)} %param.17) | copy-start | bytes 6291460
  37.6 7.6 %collective-permute-start.12 = (bf16[192,256]{1,0:T(8,128)(2,1)S(1)}, bf16[192,256]{1,0:T(8,128)(2,1)S(1)}, u32[]{:S(2)}, u32[]{:S(2)}) collective-permute-start(bf16[192,256]{1,0:T(8,128)(2,1)S(1)} %get-tuple-element.71), channel_id=1, source_target_pairs={{0,12},{1,13},{2,14},{3,15},{4,8},{5,9},{6,10},{7,11},{8,4},{9,5},... | collective-permute-start | bytes 294920 | tf_op jit(solution)/shard_map/ppermute | solution.py:360
  41.0 13.0 %collective-permute-start.16 = (bf16[192,512]{1,0:T(8,128)(2,1)S(1)}, bf16[192,512]{1,0:T(8,128)(2,1)S(1)}, u32[]{:S(2)}, u32[]{:S(2)}) collective-permute-start(bf16[192,512]{1,0:T(8,128)(2,1)S(1)} %get-tuple-element.76), channel_id=1, source_target_pairs={{0,8},{1,9},{2,10},{3,11},{4,12},{5,13},{6,14},{7,15},{8,0},{9,1},... | collective-permute-start | bytes 589832 | tf_op jit(solution)/shard_map/ppermute | solution.py:360
  41.0 13.0 %collective-permute-start.18 = (bf16[192,512]{1,0:T(8,128)(2,1)S(1)}, bf16[192,512]{1,0:T(8,128)(2,1)S(1)}, u32[]{:S(2)}, u32[]{:S(2)}) collective-permute-start(bf16[192,512]{1,0:T(8,128)(2,1)S(1)} %get-tuple-element.79), channel_id=1, source_target_pairs={{0,4},{1,5},{2,6},{3,7},{4,0},{5,1},{6,2},{7,3},{8,12},{9,13},{10,... | collective-permute-start | bytes 589832 | tf_op jit(solution)/shard_map/ppermute | solution.py:360
  45.2 9.3 %collective-permute-start.13 = (bf16[2,192,256]{2,1,0:T(8,128)(2,1)S(1)}, bf16[2,192,256]{2,1,0:T(8,128)(2,1)S(1)}, u32[]{:S(2)}, u32[]{:S(2)}) collective-permute-start(bf16[2,192,256]{2,1,0:T(8,128)(2,1)S(1)} %get-tuple-element.72), channel_id=1, source_target_pairs={{0,1},{1,0},{2,3},{3,2},{4,5},{5,4},{6,7},{7,6},{8,9},{9,8},{10,11... | collective-permute-start | bytes 589832 | tf_op jit(solution)/shard_map/ppermute | solution.py:360
  45.2 9.3 %collective-permute-start.14 = (bf16[192,256]{1,0:T(8,128)(2,1)S(1)}, bf16[192,256]{1,0:T(8,128)(2,1)S(1)}, u32[]{:S(2)}, u32[]{:S(2)}) collective-permute-start(bf16[192,256]{1,0:T(8,128)(2,1)S(1)} %collective-permute-done.12.refs_0_), channel_id=1, source_target_pairs={{0,2},{1,3},{2,0},{3,1},{4,6},{5,7},{6,4},{7,5},{8,10},{9,11},{10,... | collective-permute-start | bytes 294920 | tf_op jit(solution)/shard_map/ppermute | solution.py:360
  54.0 1.4 %collective-permute-start.17 = (bf16[192,512]{1,0:T(8,128)(2,1)S(1)}, bf16[192,512]{1,0:T(8,128)(2,1)S(1)}, u32[]{:S(2)}, u32[]{:S(2)}) collective-permute-start(bf16[192,512]{1,0:T(8,128)(2,1)S(1)} %collective-permute-done.16.refs_0_), channel_id=1, source_target_pairs={{0,1},{1,0},{2,3},{3,2},{4,5},{5,4},{6,7},{7,6},{8,9},{9,8},{10,11... | collective-permute-start | bytes 589832 | tf_op jit(solution)/shard_map/ppermute | solution.py:360
  54.0 1.7 %collective-permute-start.19 = (bf16[192,512]{1,0:T(8,128)(2,1)S(1)}, bf16[192,512]{1,0:T(8,128)(2,1)S(1)}, u32[]{:S(2)}, u32[]{:S(2)}) collective-permute-start(bf16[192,512]{1,0:T(8,128)(2,1)S(1)} %collective-permute-done.18.refs_2_), channel_id=1, source_target_pairs={{0,1},{1,0},{2,3},{3,2},{4,5},{5,4},{6,7},{7,6},{8,9},{9,8},{10,11... | collective-permute-start | bytes 589832 | tf_op jit(solution)/shard_map/ppermute | solution.py:360
  57.5 1.8 %collective-permute-start.20 = (bf16[2,384,256]{2,1,0:T(8,128)(2,1)S(1)}, bf16[2,384,256]{2,1,0:T(8,128)(2,1)S(1)}, u32[]{:S(2)}, u32[]{:S(2)}) collective-permute-start(bf16[2,384,256]{2,1,0:T(8,128)(2,1)S(1)} %get-tuple-element.81), channel_id=1, source_target_pairs={{0,1},{1,0},{2,3},{3,2},{4,5},{5,4},{6,7},{7,6},{8,9},{9,8},{10,11... | collective-permute-start | bytes 1179656 | tf_op jit(solution)/shard_map/ppermute | solution.py:360
  57.9 13.7 %collective-permute-start.15 = (bf16[192,256]{1,0:T(8,128)(2,1)S(1)}, bf16[192,256]{1,0:T(8,128)(2,1)S(1)}, u32[]{:S(2)}, u32[]{:S(2)}) collective-permute-start(bf16[192,256]{1,0:T(8,128)(2,1)S(1)} %get-tuple-element.73), channel_id=1, source_target_pairs={{0,2},{1,3},{2,0},{3,1},{4,6},{5,7},{6,4},{7,5},{8,10},{9,11},{10,... | collective-permute-start | bytes 294920 | tf_op jit(solution)/shard_map/ppermute | solution.py:360
  58.5 2.2 %collective-permute-start.21 = (bf16[192,256]{1,0:T(8,128)(2,1)S(1)}, bf16[192,256]{1,0:T(8,128)(2,1)S(1)}, u32[]{:S(2)}, u32[]{:S(2)}) collective-permute-start(bf16[192,256]{1,0:T(8,128)(2,1)S(1)} %collective-permute-done.12.refs_0_), channel_id=1, source_target_pairs={{0,1},{1,0},{2,3},{3,2},{4,5},{5,4},{6,7},{7,6},{8,9},{9,8},{10,11... | collective-permute-start | bytes 294920 | tf_op jit(solution)/shard_map/ppermute | solution.py:360
  58.5 2.2 %collective-permute-start.22 = (bf16[192,256]{1,0:T(8,128)(2,1)S(1)}, bf16[192,256]{1,0:T(8,128)(2,1)S(1)}, u32[]{:S(2)}, u32[]{:S(2)}) collective-permute-start(bf16[192,256]{1,0:T(8,128)(2,1)S(1)} %collective-permute-done.14.refs_1_), channel_id=1, source_target_pairs={{0,1},{1,0},{2,3},{3,2},{4,5},{5,4},{6,7},{7,6},{8,9},{9,8},{10,11... | collective-permute-start | bytes 294920 | tf_op jit(solution)/shard_map/ppermute | solution.py:360
  59.5 5.5 %collective-permute-start.25 = (bf16[192,256]{1,0:T(8,128)(2,1)S(1)}, bf16[192,256]{1,0:T(8,128)(2,1)S(1)}, u32[]{:S(2)}, u32[]{:S(2)}) collective-permute-start(bf16[192,256]{1,0:T(8,128)(2,1)S(1)} %fusion.4), channel_id=1, source_target_pairs={{0,2},{1,3},{2,0},{3,1},{4,6},{5,7},{6,4},{7,5},{8,10},{9,11},{10,... | collective-permute-start | bytes 294920 | tf_op jit(solution)/shard_map/ppermute | solution.py:360
  61.7 2.7 %collective-permute-start.26 = (bf16[2,192,256]{2,1,0:T(8,128)(2,1)S(1)}, bf16[2,192,256]{2,1,0:T(8,128)(2,1)S(1)}, u32[]{:S(2)}, u32[]{:S(2)}) collective-permute-start(bf16[2,192,256]{2,1,0:T(8,128)(2,1)S(1)} %get-tuple-element.85), channel_id=1, source_target_pairs={{0,1},{1,0},{2,3},{3,2},{4,5},{5,4},{6,7},{7,6},{8,9},{9,8},{10,11... | collective-permute-start | bytes 589832 | tf_op jit(solution)/shard_map/ppermute | solution.py:360
  61.8 10.0 %collective-permute-start.24 = (bf16[192,256]{1,0:T(8,128)(2,1)S(1)}, bf16[192,256]{1,0:T(8,128)(2,1)S(1)}, u32[]{:S(2)}, u32[]{:S(2)}) collective-permute-start(bf16[192,256]{1,0:T(8,128)(2,1)S(1)} %get-tuple-element.93), channel_id=1, source_target_pairs={{0,6},{1,7},{2,4},{3,5},{4,2},{5,3},{6,0},{7,1},{8,14},{9,15},{10,... | collective-permute-start | bytes 294920 | tf_op jit(solution)/shard_map/ppermute | solution.py:360
  62.8 9.0 %collective-permute-start.23 = (bf16[192,256]{1,0:T(8,128)(2,1)S(1)}, bf16[192,256]{1,0:T(8,128)(2,1)S(1)}, u32[]{:S(2)}, u32[]{:S(2)}) collective-permute-start(bf16[192,256]{1,0:T(8,128)(2,1)S(1)} %get-tuple-element.94), channel_id=1, source_target_pairs={{0,4},{1,5},{2,6},{3,7},{4,0},{5,1},{6,2},{7,3},{8,12},{9,13},{10,... | collective-permute-start | bytes 294920 | tf_op jit(solution)/shard_map/ppermute | solution.py:360
  65.0 5.1 %collective-permute-start.28 = (bf16[192,256]{1,0:T(8,128)(2,1)S(1)}, bf16[192,256]{1,0:T(8,128)(2,1)S(1)}, u32[]{:S(2)}, u32[]{:S(2)}) collective-permute-start(bf16[192,256]{1,0:T(8,128)(2,1)S(1)} %fusion.5), channel_id=1, source_target_pairs={{0,2},{1,3},{2,0},{3,1},{4,6},{5,7},{6,4},{7,5},{8,10},{9,11},{10,... | collective-permute-start | bytes 294920 | tf_op jit(solution)/shard_map/ppermute | solution.py:360
  65.6 7.7 %collective-permute-start.27 = (bf16[192,256]{1,0:T(8,128)(2,1)S(1)}, bf16[192,256]{1,0:T(8,128)(2,1)S(1)}, u32[]{:S(2)}, u32[]{:S(2)}) collective-permute-start(bf16[192,256]{1,0:T(8,128)(2,1)S(1)} %fusion.3), channel_id=1, source_target_pairs={{0,8},{1,9},{2,10},{3,11},{4,12},{5,13},{6,14},{7,15},{8,0},{9,1},... | collective-permute-start | bytes 294920 | tf_op jit(solution)/shard_map/ppermute | solution.py:360
  70.1 6.5 %collective-permute-start.29 = (bf16[192,256]{1,0:T(8,128)(2,1)S(1)}, bf16[192,256]{1,0:T(8,128)(2,1)S(1)}, u32[]{:S(2)}, u32[]{:S(2)}) collective-permute-start(bf16[192,256]{1,0:T(8,128)(2,1)S(1)} %fusion.1), channel_id=1, source_target_pairs={{0,12},{1,13},{2,14},{3,15},{4,8},{5,9},{6,10},{7,11},{8,4},{9,5},... | collective-permute-start | bytes 294920 | tf_op jit(solution)/shard_map/ppermute | solution.py:360

commit v19 on v17

--- a/solution.py
+++ b/solution.py
@@ -12,7 +12,7 @@
 SHARPNESS = HEAD_DIM**-0.5 * math.log2(math.e)
 DIRECT = 8
 CUTS = 1
-TILE = 256
+TILE = 512
 F32, BF16 = jnp.float32, jnp.bfloat16
 PARAMS = pltpu.CompilerParams(vmem_limit_bytes=20 * 2**20)
 CHEAP = pl.CostEstimate(flops=0, bytes_accessed=0, transcendentals=0)

time: 77.7 us -> 77.7 us (level)
  no operation moved by 1% of the time
where the time goes in v19:
time: 77.7 us; the launch traced here: 77.6 us
  waiting for transfers between devices  32.6 us (42%)
  starting transfers between devices  31.2 us (40%)
  Pallas kernels  12.5 us (16%)
  between operations  1 us (1%)
    ppermute x30, waiting for transfers between devices, hop(): return lax.ppermute(value, ('expert', 'mp'), moves)  32.6 us
    ppermute x30, starting transfers between devices, hop(): return lax.ppermute(value, ('expert', 'mp'), moves)  31.2 us
    pallas_call x3, Pallas kernels, run_expert(): pl.pallas_call(functools.partial(expert_kernel, tuple(map(tuple, orders))...  3.86 us
    pallas_call x4, Pallas kernels, attend(): pl.pallas_call(attend_kernel, in_specs=[WHOLE] * 2, out_specs=WHOLE, out_...  2.8 us
    pallas_call x4, Pallas kernels, combine(): pl.pallas_call(functools.partial(combine_kernel, len(parts)), in_specs=[W...  1.59 us
  transfers between devices with their start and end apart: 30, of which 13 were waited for; matrix products, arithmetic and copies ran while one was open for 0% of the time, Pallas kernels for 11%

profile of v19, /device:TPU:0, one launch (start us, length us, event | category | flops | bytes accessed | tf_op | source)
XLA Modules:
  0.0 77.6 jit_solution(3474901155837479918)
XLA Ops:
  0.0 2.9 %collective-permute-start.9 = (bf16[256,1024]{1,0:T(8,128)(2,1)}, bf16[256,1024]{1,0:T(8,128)(2,1)S(1)}, u32[]{:S(2)}, u32[]{:S(2)}) collective-permute-start(bf16[256,1024]{1,0:T(8,128)(2,1)} %refs_5_), channel_id=1, source_target_pairs={{0,2},{1,3},{2,0},{3,1},{4,6},{5,7},{6,4},{7,5},{8,10},{9,11},{10,... | collective-permute-start | bytes 1572872 | tf_op jit(solution)/shard_map/ppermute | solution.py:363
  2.9 1.5 %query.1 = (bf16[256,256]{1,0:T(8,128)(2,1)S(1)}, bf16[2,512,256]{2,1,0:T(8,128)(2,1)S(1)}) custom-call(bf16[256,1024]{1,0:T(8,128)(2,1)} %refs_0_.1, bf16[1024,256]{1,0:T(8,128)(2,1)} %weight.1, bf16[2,512,256]{2,1,0:T(8,128)(2,1)} %bitcast.39), custom_call_target="tpu_custom_call" | custom-call | tf_op jit(solution)/shard_map/query/pallas_call | solution.py:65
  4.5 0.0 copy-start.3
  4.5 0.0 copy-start.5
  4.5 0.0 copy-start.2
  4.5 2.7 %collective-permute-start.1 = (bf16[256,256]{1,0:T(8,128)(2,1)S(1)}, bf16[256,256]{1,0:T(8,128)(2,1)S(1)}, u32[]{:S(2)}, u32[]{:S(2)}) collective-permute-start(bf16[256,256]{1,0:T(8,128)(2,1)S(1)} %get-tuple-element.50.queries), channel_id=1, source_target_pairs={{0,8},{1,9},{2,10},{3,11},{4,12},{5,13},{6,14},{7,15},{8,0},{9,1},... | collective-permute-start | bytes 393224 | tf_op jit(solution)/shard_map/ppermute | solution.py:363
  7.2 1.6 %collective-permute-start = (bf16[256,256]{1,0:T(8,128)(2,1)S(1)}, bf16[256,256]{1,0:T(8,128)(2,1)S(1)}, u32[]{:S(2)}, u32[]{:S(2)}) collective-permute-start(bf16[256,256]{1,0:T(8,128)(2,1)S(1)} %get-tuple-element.50.queries), channel_id=1, source_target_pairs={{0,4},{1,5},{2,6},{3,7},{4,0},{5,1},{6,2},{7,3},{8,12},{9,13},{10,... | collective-permute-start | bytes 393224 | tf_op jit(solution)/shard_map/ppermute | solution.py:363
  8.7 0.7 attend.4.refs_0_
  9.4 3.9 %collective-permute-done.1.queries = bf16[256,256]{1,0:T(8,128)(2,1)S(1)} collective-permute-done((bf16[256,256]{1,0:T(8,128)(2,1)S(1)}, bf16[256,256]{1,0:T(8,128)(2,1)S(1)}, u32[]{:S(2)}, u32[]{:S(2)}) %collective-permute-start.1) | collective-permute-done | bytes 131104 | tf_op jit(solution)/shard_map/ppermute | solution.py:363
  13.3 0.6 collective-permute-start.4
  13.9 0.7 attend.5
  14.6 3.4 %collective-permute-start.3 = (bf16[256,256]{1,0:T(8,128)(2,1)S(1)}, bf16[256,256]{1,0:T(8,128)(2,1)S(1)}, u32[]{:S(2)}, u32[]{:S(2)}) collective-permute-start(bf16[256,256]{1,0:T(8,128)(2,1)S(1)} %attend.5), channel_id=1, source_target_pairs={{0,8},{1,9},{2,10},{3,11},{4,12},{5,13},{6,14},{7,15},{8,0},{9,1},... | collective-permute-start | bytes 393224 | tf_op jit(solution)/shard_map/ppermute | solution.py:363
  18.1 0.7 attend.6
  18.8 0.1 collective-permute-start.2
  18.9 0.7 attend.7
  19.6 0.0 copy-start.4
  19.6 5.9 %collective-permute-start.5 = (bf16[256,256]{1,0:T(8,128)(2,1)S(1)}, bf16[256,256]{1,0:T(8,128)(2,1)S(1)}, u32[]{:S(2)}, u32[]{:S(2)}) collective-permute-start(bf16[256,256]{1,0:T(8,128)(2,1)S(1)} %attend.7), channel_id=1, source_target_pairs={{0,12},{1,13},{2,14},{3,15},{4,8},{5,9},{6,10},{7,11},{8,4},{9,5},... | collective-permute-start | bytes 393224 | tf_op jit(solution)/shard_map/ppermute | solution.py:363
  26.1 0.0 collective-permute-done.2.refs_1_
  26.2 2.8 %collective-permute-done.5.refs_3_ = bf16[256,256]{1,0:T(8,128)(2,1)S(1)} collective-permute-done((bf16[256,256]{1,0:T(8,128)(2,1)S(1)}, bf16[256,256]{1,0:T(8,128)(2,1)S(1)}, u32[]{:S(2)}, u32[]{:S(2)}) %collective-permute-start.5) | collective-permute-done | bytes 131104 | tf_op jit(solution)/shard_map/ppermute | solution.py:363
  29.0 0.1 pick.1.refs_1_
  29.1 0.1 collective-permute-start.10
  29.2 0.5 collective-permute-start.11
  29.7 0.5 collective-permute-start.6
  30.3 1.0 %route.1 = (s32[256,2]{1,0:T(8,128)S(1)}, bf16[192,256]{1,0:T(8,128)(2,1)S(1)}, bf16[192,256]{1,0:T(8,128)(2,1)S(1)}, bf16[192,256]{1,0:T(8,128)(2,1)S(1)}, bf16...) custom-call(s32[2,256]{1,0:T(2,128)S(1)} %bitcast.38), custom_call_target="tpu_custom_call" | custom-call | tf_op jit(solution)/shard_map/route/pallas_call | solution.py:177
  31.2 0.1 collective-permute-start.7
  31.3 3.9 %collective-permute-done.6.refs_2_ = bf16[256,256]{1,0:T(8,128)(2,1)S(1)} collective-permute-done((bf16[256,256]{1,0:T(8,128)(2,1)S(1)}, bf16[256,256]{1,0:T(8,128)(2,1)S(1)}, u32[]{:S(2)}, u32[]{:S(2)}) %collective-permute-start.6) | collective-permute-done | bytes 131104 | tf_op jit(solution)/shard_map/ppermute | solution.py:363
  35.2 1.3 %collective-permute-done.8.refs_4_ = bf16[256,256]{1,0:T(8,128)(2,1)S(1)} collective-permute-done((bf16[256,256]{1,0:T(8,128)(2,1)S(1)}, bf16[256,256]{1,0:T(8,128)(2,1)S(1)}, u32[]{:S(2)}, u32[]{:S(2)}) %collective-permute-start.8) | collective-permute-done | bytes 131104 | tf_op jit(solution)/shard_map/ppermute | solution.py:363
  36.6 0.0 collective-permute-done.10.refs_7_
  36.6 0.0 collective-permute-done.11.refs_8_
  36.6 0.0 copy-start
  36.6 0.0 copy-start.1
  36.6 1.1 %state.1 = (bf16[256,1024]{1,0:T(8,128)(2,1)S(1)}, bf16[192,512]{1,0:T(8,128)(2,1)S(1)}, bf16[192,256]{1,0:T(8,128)(2,1)S(1)}, bf16[192,512]{1,0:T(8,128)(2,1)S(1)}) custom-call(bf16[256,1024]{1,0:T(8,128)(2,1)S(1)} %copy-done.2, bf16[256,256]{1,0:T(8,128)(2,1)S(1)} %pick.1.refs_1_, bf16[256,256]{1,0:T(8,128)(2,1)S(1)} %collective-permute-done.6.refs_2_, ...), custom_call_target="tpu_custom_call" | custom-call | tf_op jit(solution)/shard_map/state/pallas_call | solution.py:210
  37.7 3.4 %collective-permute-start.12 = (bf16[192,256]{1,0:T(8,128)(2,1)S(1)}, bf16[192,256]{1,0:T(8,128)(2,1)S(1)}, u32[]{:S(2)}, u32[]{:S(2)}) collective-permute-start(bf16[192,256]{1,0:T(8,128)(2,1)S(1)} %get-tuple-element.73), channel_id=1, source_target_pairs={{0,12},{1,13},{2,14},{3,15},{4,8},{5,9},{6,10},{7,11},{8,4},{9,5},... | collective-permute-start | bytes 294920 | tf_op jit(solution)/shard_map/ppermute | solution.py:363
  41.1 1.1 %collective-permute-start.18 = (bf16[192,512]{1,0:T(8,128)(2,1)S(1)}, bf16[192,512]{1,0:T(8,128)(2,1)S(1)}, u32[]{:S(2)}, u32[]{:S(2)}) collective-permute-start(bf16[192,512]{1,0:T(8,128)(2,1)S(1)} %get-tuple-element.81), channel_id=1, source_target_pairs={{0,4},{1,5},{2,6},{3,7},{4,0},{5,1},{6,2},{7,3},{8,12},{9,13},{10,... | collective-permute-start | bytes 589832 | tf_op jit(solution)/shard_map/ppermute | solution.py:363
  42.1 0.5 home.1
  42.7 1.0 %expert.3 = (f32[2,192,256]{2,1,0:T(8,128)S(1)}, bf16[2,192,256]{2,1,0:T(8,128)(2,1)S(1)}) custom-call(bf16[192,512]{1,0:T(8,128)(2,1)S(1)} %get-tuple-element.69.refs_0_, bf16[192,512]{1,0:T(8,128)(2,1)S(1)} %get-tuple-element.70.refs_1_, bf16[1024,1024]{1,0:T(8,128)(2,1)S(1)} %bitcast.31, bf16[1024,1024]{1,0:T(8,128)(2,1)S(1)} %bitcast.34), custom_call_target="tpu_custom_call" | custom-call | tf_op jit(solution)/shard_map/expert/pallas_call | solution.py:289
  43.7 1.6 %collective-permute-done.12.refs_0_ = bf16[192,256]{1,0:T(8,128)(2,1)S(1)} collective-permute-done((bf16[192,256]{1,0:T(8,128)(2,1)S(1)}, bf16[192,256]{1,0:T(8,128)(2,1)S(1)}, u32[]{:S(2)}, u32[]{:S(2)}) %collective-permute-start.12) | collective-permute-done | bytes 98336 | tf_op jit(solution)/shard_map/ppermute | solution.py:363
  45.3 0.5 collective-permute-start.14
  45.8 8.2 %collective-permute-done.16.refs_0_ = bf16[192,512]{1,0:T(8,128)(2,1)S(1)} collective-permute-done((bf16[192,512]{1,0:T(8,128)(2,1)S(1)}, bf16[192,512]{1,0:T(8,128)(2,1)S(1)}, u32[]{:S(2)}, u32[]{:S(2)}) %collective-permute-start.16) | collective-permute-done | bytes 196640 | tf_op jit(solution)/shard_map/ppermute | solution.py:363
  54.0 0.5 collective-permute-start.19
  54.6 0.9 %collective-permute-done.17.refs_1_ = bf16[192,512]{1,0:T(8,128)(2,1)S(1)} collective-permute-done((bf16[192,512]{1,0:T(8,128)(2,1)S(1)}, bf16[192,512]{1,0:T(8,128)(2,1)S(1)}, u32[]{:S(2)}, u32[]{:S(2)}) %collective-permute-start.17) | collective-permute-done | bytes 196640 | tf_op jit(solution)/shard_map/ppermute | solution.py:363
  55.5 0.3 collective-permute-done.19.refs_3_
  55.8 1.8 %expert.4 = (f32[2,384,256]{2,1,0:T(8,128)S(1)}, bf16[2,384,256]{2,1,0:T(8,128)(2,1)S(1)}) custom-call(bf16[192,512]{1,0:T(8,128)(2,1)S(1)} %collective-permute-done.16.refs_0_, bf16[192,512]{1,0:T(8,128)(2,1)S(1)} %collective-permute-done.17.refs_1_, bf16[192,512]{1,0:T(8,128)(2,1)S(1)} %collective-permute-done.18.refs_2_, ...), custom_call_target="tpu_custom_call" | custom-call | tf_op jit(solution)/shard_map/expert/pallas_call | solution.py:289
  57.6 0.3 collective-permute-start.20
  57.9 0.6 collective-permute-start.15
  58.5 0.5 collective-permute-start.22
  59.0 0.4 collective-permute-done.20
  59.4 0.1 convert_add_fusion
  59.5 1.2 %collective-permute-start.25 = (bf16[192,256]{1,0:T(8,128)(2,1)S(1)}, bf16[192,256]{1,0:T(8,128)(2,1)S(1)}, u32[]{:S(2)}, u32[]{:S(2)}) collective-permute-start(bf16[192,256]{1,0:T(8,128)(2,1)S(1)} %fusion.4), channel_id=1, source_target_pairs={{0,2},{1,3},{2,0},{3,1},{4,6},{5,7},{6,4},{7,5},{8,10},{9,11},{10,... | collective-permute-start | bytes 294920 | tf_op jit(solution)/shard_map/ppermute | solution.py:363
  60.7 1.0 %expert.5 = (f32[2,192,256]{2,1,0:T(8,128)S(1)}, bf16[2,192,256]{2,1,0:T(8,128)(2,1)S(1)}) custom-call(bf16[192,256]{1,0:T(8,128)(2,1)S(1)} %collective-permute-done.12.refs_0_, bf16[192,256]{1,0:T(8,128)(2,1)S(1)} %collective-permute-done.14.refs_1_, bf16[192,256]{1,0:T(8,128)(2,1)S(1)} %collective-permute-done.21.refs_2_, ...), custom_call_target="tpu_custom_call" | custom-call | tf_op jit(solution)/shard_map/expert/pallas_call | solution.py:289
  61.8 0.1 collective-permute-start.26
  61.9 1.0 %collective-permute-start.24 = (bf16[192,256]{1,0:T(8,128)(2,1)S(1)}, bf16[192,256]{1,0:T(8,128)(2,1)S(1)}, u32[]{:S(2)}, u32[]{:S(2)}) collective-permute-start(bf16[192,256]{1,0:T(8,128)(2,1)S(1)} %get-tuple-element.95), channel_id=1, source_target_pairs={{0,6},{1,7},{2,4},{3,5},{4,2},{5,3},{6,0},{7,1},{8,14},{9,15},{10,... | collective-permute-start | bytes 294920 | tf_op jit(solution)/shard_map/ppermute | solution.py:363
  62.9 1.6 %collective-permute-start.23 = (bf16[192,256]{1,0:T(8,128)(2,1)S(1)}, bf16[192,256]{1,0:T(8,128)(2,1)S(1)}, u32[]{:S(2)}, u32[]{:S(2)}) collective-permute-start(bf16[192,256]{1,0:T(8,128)(2,1)S(1)} %get-tuple-element.96), channel_id=1, source_target_pairs={{0,4},{1,5},{2,6},{3,7},{4,0},{5,1},{6,2},{7,3},{8,12},{9,13},{10,... | collective-permute-start | bytes 294920 | tf_op jit(solution)/shard_map/ppermute | solution.py:363
  64.5 0.5 collective-permute-done.25
  65.1 0.5 collective-permute-start.28
  65.6 0.1 collective-permute-start.27
  65.7 4.4 %collective-permute-done.28 = bf16[192,256]{1,0:T(8,128)(2,1)S(1)} collective-permute-done((bf16[192,256]{1,0:T(8,128)(2,1)S(1)}, bf16[192,256]{1,0:T(8,128)(2,1)S(1)}, u32[]{:S(2)}, u32[]{:S(2)}) %collective-permute-start.28) | collective-permute-done | bytes 98336 | tf_op jit(solution)/shard_map/ppermute | solution.py:363
  70.1 1.5 %collective-permute-start.29 = (bf16[192,256]{1,0:T(8,128)(2,1)S(1)}, bf16[192,256]{1,0:T(8,128)(2,1)S(1)}, u32[]{:S(2)}, u32[]{:S(2)}) collective-permute-start(bf16[192,256]{1,0:T(8,128)(2,1)S(1)} %fusion.1), channel_id=1, source_target_pairs={{0,12},{1,13},{2,14},{3,15},{4,8},{5,9},{6,10},{7,11},{8,4},{9,5},... | collective-permute-start | bytes 294920 | tf_op jit(solution)/shard_map/ppermute | solution.py:363
  71.6 0.2 combine.4.base
  71.9 0.2 combine.5.base
  72.1 1.2 %collective-permute-done.27.refs_0_ = bf16[192,256]{1,0:T(8,128)(2,1)S(1)} collective-permute-done((bf16[192,256]{1,0:T(8,128)(2,1)S(1)}, bf16[192,256]{1,0:T(8,128)(2,1)S(1)}, u32[]{:S(2)}, u32[]{:S(2)}) %collective-permute-start.27) | collective-permute-done | bytes 98336 | tf_op jit(solution)/shard_map/ppermute | solution.py:363
  73.3 0.2 combine.6.base
  73.6 3.1 %collective-permute-done.29.refs_0_ = bf16[192,256]{1,0:T(8,128)(2,1)S(1)} collective-permute-done((bf16[192,256]{1,0:T(8,128)(2,1)S(1)}, bf16[192,256]{1,0:T(8,128)(2,1)S(1)}, u32[]{:S(2)}, u32[]{:S(2)}) %collective-permute-start.29) | collective-permute-done | bytes 98336 | tf_op jit(solution)/shard_map/ppermute | solution.py:363
  76.7 0.9 %combine.7 = bf16[256,256]{1,0:T(8,128)(2,1)} custom-call(f32[256,2]{1,0:T(8,128)S(1)} %get-tuple-element.65.gates, f32[256,256]{1,0:T(8,128)S(1)} %combine.6.base, bf16[256,192]{1,0:T(8,128)(2,1)S(1)} %get-tuple-element.93.first, bf16[256,192]{1,0:T(8,128)(2,1)S(1)} %get-tuple-element.94.second, bf16[192,256]{1,0:T(8,128)(2,1)S(1)} %collective-permute-done.29.refs_0_), custom_call_target="tpu_custom_call" | custom-call | tf_op jit(solution)/shard_map/combine/pallas_call | solution.py:315
  (34 shorter events, 0.3 us)
Async XLA Ops:
  0.0 29.2 %collective-permute-start.9 = (bf16[256,1024]{1,0:T(8,128)(2,1)}, bf16[256,1024]{1,0:T(8,128)(2,1)S(1)}, u32[]{:S(2)}, u32[]{:S(2)}) collective-permute-start(bf16[256,1024]{1,0:T(8,128)(2,1)} %refs_5_), channel_id=1, source_target_pairs={{0,2},{1,3},{2,0},{3,1},{4,6},{5,7},{6,4},{7,5},{8,10},{9,11},{10,... | collective-permute-start | bytes 1572872 | tf_op jit(solution)/shard_map/ppermute | solution.py:363
  4.5 24.7 %copy-start.3 = (bf16[256,1024]{1,0:T(8,128)(2,1)S(1)}, bf16[256,1024]{1,0:T(8,128)(2,1)}, u32[]{:S(2)}) copy-start(bf16[256,1024]{1,0:T(8,128)(2,1)} %refs_5_) | copy-start | bytes 1572868
  4.5 25.8 %copy-start.5 = (s32[256,2]{0,1:T(2,128)S(1)}, s32[256,2]{0,1:T(2,128)}, u32[]{:S(2)}) copy-start(s32[256,2]{0,1:T(2,128)} %param.15) | copy-start | bytes 6148
  4.5 32.1 %copy-start.2 = (bf16[256,1024]{1,0:T(8,128)(2,1)S(1)}, bf16[256,1024]{1,0:T(8,128)(2,1)}, u32[]{:S(2)}) copy-start(bf16[256,1024]{1,0:T(8,128)(2,1)} %refs_0_.1) | copy-start | bytes 1572868
  4.5 8.8 %collective-permute-start.1 = (bf16[256,256]{1,0:T(8,128)(2,1)S(1)}, bf16[256,256]{1,0:T(8,128)(2,1)S(1)}, u32[]{:S(2)}, u32[]{:S(2)}) collective-permute-start(bf16[256,256]{1,0:T(8,128)(2,1)S(1)} %get-tuple-element.50.queries), channel_id=1, source_target_pairs={{0,8},{1,9},{2,10},{3,11},{4,12},{5,13},{6,14},{7,15},{8,0},{9,1},... | collective-permute-start | bytes 393224 | tf_op jit(solution)/shard_map/ppermute | solution.py:363
  7.2 10.9 %collective-permute-start = (bf16[256,256]{1,0:T(8,128)(2,1)S(1)}, bf16[256,256]{1,0:T(8,128)(2,1)S(1)}, u32[]{:S(2)}, u32[]{:S(2)}) collective-permute-start(bf16[256,256]{1,0:T(8,128)(2,1)S(1)} %get-tuple-element.50.queries), channel_id=1, source_target_pairs={{0,4},{1,5},{2,6},{3,7},{4,0},{5,1},{6,2},{7,3},{8,12},{9,13},{10,... | collective-permute-start | bytes 393224 | tf_op jit(solution)/shard_map/ppermute | solution.py:363
  13.3 5.5 %collective-permute-start.4 = (bf16[256,256]{1,0:T(8,128)(2,1)S(1)}, bf16[256,256]{1,0:T(8,128)(2,1)S(1)}, u32[]{:S(2)}, u32[]{:S(2)}) collective-permute-start(bf16[256,256]{1,0:T(8,128)(2,1)S(1)} %collective-permute-done.1.queries), channel_id=1, source_target_pairs={{0,4},{1,5},{2,6},{3,7},{4,0},{5,1},{6,2},{7,3},{8,12},{9,13},{10,... | collective-permute-start | bytes 393224 | tf_op jit(solution)/shard_map/ppermute | solution.py:363
  14.6 11.5 %collective-permute-start.3 = (bf16[256,256]{1,0:T(8,128)(2,1)S(1)}, bf16[256,256]{1,0:T(8,128)(2,1)S(1)}, u32[]{:S(2)}, u32[]{:S(2)}) collective-permute-start(bf16[256,256]{1,0:T(8,128)(2,1)S(1)} %attend.5), channel_id=1, source_target_pairs={{0,8},{1,9},{2,10},{3,11},{4,12},{5,13},{6,14},{7,15},{8,0},{9,1},... | collective-permute-start | bytes 393224 | tf_op jit(solution)/shard_map/ppermute | solution.py:363
  18.8 7.4 %collective-permute-start.2 = (bf16[256,256]{1,0:T(8,128)(2,1)S(1)}, bf16[256,256]{1,0:T(8,128)(2,1)S(1)}, u32[]{:S(2)}, u32[]{:S(2)}) collective-permute-start(bf16[256,256]{1,0:T(8,128)(2,1)S(1)} %attend.6), channel_id=1, source_target_pairs={{0,4},{1,5},{2,6},{3,7},{4,0},{5,1},{6,2},{7,3},{8,12},{9,13},{10,... | collective-permute-start | bytes 393224 | tf_op jit(solution)/shard_map/ppermute | solution.py:363
  19.6 22.6 %copy-start.4 = (bf16[1024,4]{0,1:T(4,128)(2,1)S(1)}, bf16[1024,4]{0,1:T(4,128)(2,1)}, u32[]{:S(2)}) copy-start(bf16[1024,4]{0,1:T(4,128)(2,1)} %param.14) | copy-start | bytes 24580
  19.6 9.4 %collective-permute-start.5 = (bf16[256,256]{1,0:T(8,128)(2,1)S(1)}, bf16[256,256]{1,0:T(8,128)(2,1)S(1)}, u32[]{:S(2)}, u32[]{:S(2)}) collective-permute-start(bf16[256,256]{1,0:T(8,128)(2,1)S(1)} %attend.7), channel_id=1, source_target_pairs={{0,12},{1,13},{2,14},{3,15},{4,8},{5,9},{6,10},{7,11},{8,4},{9,5},... | collective-permute-start | bytes 393224 | tf_op jit(solution)/shard_map/ppermute | solution.py:363
  29.1 7.4 %collective-permute-start.10 = (bf16[256,1024]{1,0:T(8,128)(2,1)S(1)}, bf16[256,1024]{1,0:T(8,128)(2,1)S(1)}, u32[]{:S(2)}, u32[]{:S(2)}) collective-permute-start(bf16[256,1024]{1,0:T(8,128)(2,1)S(1)} %copy-done.3), channel_id=1, source_target_pairs={{0,1},{1,0},{2,3},{3,2},{4,5},{5,4},{6,7},{7,6},{8,9},{9,8},{10,11... | collective-permute-start | bytes 1572872 | tf_op jit(solution)/shard_map/ppermute | solution.py:363
  29.2 7.3 %collective-permute-start.11 = (bf16[256,1024]{1,0:T(8,128)(2,1)S(1)}, bf16[256,1024]{1,0:T(8,128)(2,1)S(1)}, u32[]{:S(2)}, u32[]{:S(2)}) collective-permute-start(bf16[256,1024]{1,0:T(8,128)(2,1)S(1)} %collective-permute-done.9.refs_6_), channel_id=1, source_target_pairs={{0,1},{1,0},{2,3},{3,2},{4,5},{5,4},{6,7},{7,6},{8,9},{9,8},{10,11... | collective-permute-start | bytes 1572872 | tf_op jit(solution)/shard_map/ppermute | solution.py:363
  29.7 5.5 %collective-permute-start.6 = (bf16[256,256]{1,0:T(8,128)(2,1)S(1)}, bf16[256,256]{1,0:T(8,128)(2,1)S(1)}, u32[]{:S(2)}, u32[]{:S(2)}) collective-permute-start(bf16[256,256]{1,0:T(8,128)(2,1)S(1)} %pick.1.refs_1_), channel_id=1, source_target_pairs={{0,2},{1,3},{2,0},{3,1},{4,6},{5,7},{6,4},{7,5},{8,10},{9,11},{10,... | collective-permute-start | bytes 393224 | tf_op jit(solution)/shard_map/ppermute | solution.py:363
  31.2 4.0 %collective-permute-start.7 = (bf16[256,256]{1,0:T(8,128)(2,1)S(1)}, bf16[256,256]{1,0:T(8,128)(2,1)S(1)}, u32[]{:S(2)}, u32[]{:S(2)}) collective-permute-start(bf16[256,256]{1,0:T(8,128)(2,1)S(1)} %pick.1.refs_1_), channel_id=1, source_target_pairs={{0,1},{1,0},{2,3},{3,2},{4,5},{5,4},{6,7},{7,6},{8,9},{9,8},{10,11... | collective-permute-start | bytes 393224 | tf_op jit(solution)/shard_map/ppermute | solution.py:363
  35.2 1.3 %collective-permute-start.8 = (bf16[256,256]{1,0:T(8,128)(2,1)S(1)}, bf16[256,256]{1,0:T(8,128)(2,1)S(1)}, u32[]{:S(2)}, u32[]{:S(2)}) collective-permute-start(bf16[256,256]{1,0:T(8,128)(2,1)S(1)} %collective-permute-done.6.refs_2_), channel_id=1, source_target_pairs={{0,1},{1,0},{2,3},{3,2},{4,5},{5,4},{6,7},{7,6},{8,9},{9,8},{10,11... | collective-permute-start | bytes 393224 | tf_op jit(solution)/shard_map/ppermute | solution.py:363
  36.6 6.1 %copy-start = (bf16[1,1024,1024]{2,1,0:T(8,128)(2,1)S(1)}, bf16[1,1024,1024]{2,1,0:T(8,128)(2,1)}, u32[]{:S(2)}) copy-start(bf16[1,1024,1024]{2,1,0:T(8,128)(2,1)} %param.16) | copy-start | bytes 6291460
  36.6 6.1 %copy-start.1 = (bf16[1,1024,1024]{2,1,0:T(8,128)(2,1)S(1)}, bf16[1,1024,1024]{2,1,0:T(8,128)(2,1)}, u32[]{:S(2)}) copy-start(bf16[1,1024,1024]{2,1,0:T(8,128)(2,1)} %param.17) | copy-start | bytes 6291460
  37.7 7.6 %collective-permute-start.12 = (bf16[192,256]{1,0:T(8,128)(2,1)S(1)}, bf16[192,256]{1,0:T(8,128)(2,1)S(1)}, u32[]{:S(2)}, u32[]{:S(2)}) collective-permute-start(bf16[192,256]{1,0:T(8,128)(2,1)S(1)} %get-tuple-element.73), channel_id=1, source_target_pairs={{0,12},{1,13},{2,14},{3,15},{4,8},{5,9},{6,10},{7,11},{8,4},{9,5},... | collective-permute-start | bytes 294920 | tf_op jit(solution)/shard_map/ppermute | solution.py:363
  41.1 13.0 %collective-permute-start.16 = (bf16[192,512]{1,0:T(8,128)(2,1)S(1)}, bf16[192,512]{1,0:T(8,128)(2,1)S(1)}, u32[]{:S(2)}, u32[]{:S(2)}) collective-permute-start(bf16[192,512]{1,0:T(8,128)(2,1)S(1)} %get-tuple-element.78), channel_id=1, source_target_pairs={{0,8},{1,9},{2,10},{3,11},{4,12},{5,13},{6,14},{7,15},{8,0},{9,1},... | collective-permute-start | bytes 589832 | tf_op jit(solution)/shard_map/ppermute | solution.py:363
  41.1 13.0 %collective-permute-start.18 = (bf16[192,512]{1,0:T(8,128)(2,1)S(1)}, bf16[192,512]{1,0:T(8,128)(2,1)S(1)}, u32[]{:S(2)}, u32[]{:S(2)}) collective-permute-start(bf16[192,512]{1,0:T(8,128)(2,1)S(1)} %get-tuple-element.81), channel_id=1, source_target_pairs={{0,4},{1,5},{2,6},{3,7},{4,0},{5,1},{6,2},{7,3},{8,12},{9,13},{10,... | collective-permute-start | bytes 589832 | tf_op jit(solution)/shard_map/ppermute | solution.py:363
  45.3 9.3 %collective-permute-start.13 = (bf16[2,192,256]{2,1,0:T(8,128)(2,1)S(1)}, bf16[2,192,256]{2,1,0:T(8,128)(2,1)S(1)}, u32[]{:S(2)}, u32[]{:S(2)}) collective-permute-start(bf16[2,192,256]{2,1,0:T(8,128)(2,1)S(1)} %get-tuple-element.74), channel_id=1, source_target_pairs={{0,1},{1,0},{2,3},{3,2},{4,5},{5,4},{6,7},{7,6},{8,9},{9,8},{10,11... | collective-permute-start | bytes 589832 | tf_op jit(solution)/shard_map/ppermute | solution.py:363
  45.3 9.3 %collective-permute-start.14 = (bf16[192,256]{1,0:T(8,128)(2,1)S(1)}, bf16[192,256]{1,0:T(8,128)(2,1)S(1)}, u32[]{:S(2)}, u32[]{:S(2)}) collective-permute-start(bf16[192,256]{1,0:T(8,128)(2,1)S(1)} %collective-permute-done.12.refs_0_), channel_id=1, source_target_pairs={{0,2},{1,3},{2,0},{3,1},{4,6},{5,7},{6,4},{7,5},{8,10},{9,11},{10,... | collective-permute-start | bytes 294920 | tf_op jit(solution)/shard_map/ppermute | solution.py:363
  54.0 1.4 %collective-permute-start.17 = (bf16[192,512]{1,0:T(8,128)(2,1)S(1)}, bf16[192,512]{1,0:T(8,128)(2,1)S(1)}, u32[]{:S(2)}, u32[]{:S(2)}) collective-permute-start(bf16[192,512]{1,0:T(8,128)(2,1)S(1)} %collective-permute-done.16.refs_0_), channel_id=1, source_target_pairs={{0,1},{1,0},{2,3},{3,2},{4,5},{5,4},{6,7},{7,6},{8,9},{9,8},{10,11... | collective-permute-start | bytes 589832 | tf_op jit(solution)/shard_map/ppermute | solution.py:363
  54.0 1.7 %collective-permute-start.19 = (bf16[192,512]{1,0:T(8,128)(2,1)S(1)}, bf16[192,512]{1,0:T(8,128)(2,1)S(1)}, u32[]{:S(2)}, u32[]{:S(2)}) collective-permute-start(bf16[192,512]{1,0:T(8,128)(2,1)S(1)} %collective-permute-done.18.refs_2_), channel_id=1, source_target_pairs={{0,1},{1,0},{2,3},{3,2},{4,5},{5,4},{6,7},{7,6},{8,9},{9,8},{10,11... | collective-permute-start | bytes 589832 | tf_op jit(solution)/shard_map/ppermute | solution.py:363
  57.6 1.8 %collective-permute-start.20 = (bf16[2,384,256]{2,1,0:T(8,128)(2,1)S(1)}, bf16[2,384,256]{2,1,0:T(8,128)(2,1)S(1)}, u32[]{:S(2)}, u32[]{:S(2)}) collective-permute-start(bf16[2,384,256]{2,1,0:T(8,128)(2,1)S(1)} %get-tuple-element.83), channel_id=1, source_target_pairs={{0,1},{1,0},{2,3},{3,2},{4,5},{5,4},{6,7},{7,6},{8,9},{9,8},{10,11... | collective-permute-start | bytes 1179656 | tf_op jit(solution)/shard_map/ppermute | solution.py:363
  57.9 13.7 %collective-permute-start.15 = (bf16[192,256]{1,0:T(8,128)(2,1)S(1)}, bf16[192,256]{1,0:T(8,128)(2,1)S(1)}, u32[]{:S(2)}, u32[]{:S(2)}) collective-permute-start(bf16[192,256]{1,0:T(8,128)(2,1)S(1)} %get-tuple-element.75), channel_id=1, source_target_pairs={{0,2},{1,3},{2,0},{3,1},{4,6},{5,7},{6,4},{7,5},{8,10},{9,11},{10,... | collective-permute-start | bytes 294920 | tf_op jit(solution)/shard_map/ppermute | solution.py:363
  58.5 2.2 %collective-permute-start.21 = (bf16[192,256]{1,0:T(8,128)(2,1)S(1)}, bf16[192,256]{1,0:T(8,128)(2,1)S(1)}, u32[]{:S(2)}, u32[]{:S(2)}) collective-permute-start(bf16[192,256]{1,0:T(8,128)(2,1)S(1)} %collective-permute-done.12.refs_0_), channel_id=1, source_target_pairs={{0,1},{1,0},{2,3},{3,2},{4,5},{5,4},{6,7},{7,6},{8,9},{9,8},{10,11... | collective-permute-start | bytes 294920 | tf_op jit(solution)/shard_map/ppermute | solution.py:363
  58.5 2.2 %collective-permute-start.22 = (bf16[192,256]{1,0:T(8,128)(2,1)S(1)}, bf16[192,256]{1,0:T(8,128)(2,1)S(1)}, u32[]{:S(2)}, u32[]{:S(2)}) collective-permute-start(bf16[192,256]{1,0:T(8,128)(2,1)S(1)} %collective-permute-done.14.refs_1_), channel_id=1, source_target_pairs={{0,1},{1,0},{2,3},{3,2},{4,5},{5,4},{6,7},{7,6},{8,9},{9,8},{10,11... | collective-permute-start | bytes 294920 | tf_op jit(solution)/shard_map/ppermute | solution.py:363
  59.5 5.5 %collective-permute-start.25 = (bf16[192,256]{1,0:T(8,128)(2,1)S(1)}, bf16[192,256]{1,0:T(8,128)(2,1)S(1)}, u32[]{:S(2)}, u32[]{:S(2)}) collective-permute-start(bf16[192,256]{1,0:T(8,128)(2,1)S(1)} %fusion.4), channel_id=1, source_target_pairs={{0,2},{1,3},{2,0},{3,1},{4,6},{5,7},{6,4},{7,5},{8,10},{9,11},{10,... | collective-permute-start | bytes 294920 | tf_op jit(solution)/shard_map/ppermute | solution.py:363
  61.8 2.7 %collective-permute-start.26 = (bf16[2,192,256]{2,1,0:T(8,128)(2,1)S(1)}, bf16[2,192,256]{2,1,0:T(8,128)(2,1)S(1)}, u32[]{:S(2)}, u32[]{:S(2)}) collective-permute-start(bf16[2,192,256]{2,1,0:T(8,128)(2,1)S(1)} %get-tuple-element.87), channel_id=1, source_target_pairs={{0,1},{1,0},{2,3},{3,2},{4,5},{5,4},{6,7},{7,6},{8,9},{9,8},{10,11... | collective-permute-start | bytes 589832 | tf_op jit(solution)/shard_map/ppermute | solution.py:363
  61.9 10.0 %collective-permute-start.24 = (bf16[192,256]{1,0:T(8,128)(2,1)S(1)}, bf16[192,256]{1,0:T(8,128)(2,1)S(1)}, u32[]{:S(2)}, u32[]{:S(2)}) collective-permute-start(bf16[192,256]{1,0:T(8,128)(2,1)S(1)} %get-tuple-element.95), channel_id=1, source_target_pairs={{0,6},{1,7},{2,4},{3,5},{4,2},{5,3},{6,0},{7,1},{8,14},{9,15},{10,... | collective-permute-start | bytes 294920 | tf_op jit(solution)/shard_map/ppermute | solution.py:363
  62.9 9.0 %collective-permute-start.23 = (bf16[192,256]{1,0:T(8,128)(2,1)S(1)}, bf16[192,256]{1,0:T(8,128)(2,1)S(1)}, u32[]{:S(2)}, u32[]{:S(2)}) collective-permute-start(bf16[192,256]{1,0:T(8,128)(2,1)S(1)} %get-tuple-element.96), channel_id=1, source_target_pairs={{0,4},{1,5},{2,6},{3,7},{4,0},{5,1},{6,2},{7,3},{8,12},{9,13},{10,... | collective-permute-start | bytes 294920 | tf_op jit(solution)/shard_map/ppermute | solution.py:363
  65.1 5.1 %collective-permute-start.28 = (bf16[192,256]{1,0:T(8,128)(2,1)S(1)}, bf16[192,256]{1,0:T(8,128)(2,1)S(1)}, u32[]{:S(2)}, u32[]{:S(2)}) collective-permute-start(bf16[192,256]{1,0:T(8,128)(2,1)S(1)} %fusion.5), channel_id=1, source_target_pairs={{0,2},{1,3},{2,0},{3,1},{4,6},{5,7},{6,4},{7,5},{8,10},{9,11},{10,... | collective-permute-start | bytes 294920 | tf_op jit(solution)/shard_map/ppermute | solution.py:363
  65.6 7.7 %collective-permute-start.27 = (bf16[192,256]{1,0:T(8,128)(2,1)S(1)}, bf16[192,256]{1,0:T(8,128)(2,1)S(1)}, u32[]{:S(2)}, u32[]{:S(2)}) collective-permute-start(bf16[192,256]{1,0:T(8,128)(2,1)S(1)} %fusion.3), channel_id=1, source_target_pairs={{0,8},{1,9},{2,10},{3,11},{4,12},{5,13},{6,14},{7,15},{8,0},{9,1},... | collective-permute-start | bytes 294920 | tf_op jit(solution)/shard_map/ppermute | solution.py:363
  70.1 6.5 %collective-permute-start.29 = (bf16[192,256]{1,0:T(8,128)(2,1)S(1)}, bf16[192,256]{1,0:T(8,128)(2,1)S(1)}, u32[]{:S(2)}, u32[]{:S(2)}) collective-permute-start(bf16[192,256]{1,0:T(8,128)(2,1)S(1)} %fusion.1), channel_id=1, source_target_pairs={{0,12},{1,13},{2,14},{3,15},{4,8},{5,9},{6,10},{7,11},{8,4},{9,5},... | collective-permute-start | bytes 294920 | tf_op jit(solution)/shard_map/ppermute | solution.py:363

commit v20 on v17

--- a/solution.py
+++ b/solution.py
@@ -439,7 +439,7 @@
             if k in relayed:
                 earlier.append(pieces[-1])
                 wait = pieces[-1]
-        home[0] = send_home(0, own_sum, wait)
+        home[0] = send_home(0, own_sum)
         turns = [[k for k in sends if k < groups - 1], [groups - 1]] if groups > 2 else [sends]
         for turn in turns:
             blocks, orders = [], []

time: 77.7 us -> 77.7 us (level)
  no operation moved by 1% of the time
where the time goes in v20:
time: 77.7 us; the launch traced here: 77.6 us
  waiting for transfers between devices  32.6 us (42%)
  starting transfers between devices  31.2 us (40%)
  Pallas kernels  12.5 us (16%)
  between operations  1 us (1%)
    ppermute x30, waiting for transfers between devices, hop(): return lax.ppermute(value, ('expert', 'mp'), moves)  32.6 us
    ppermute x30, starting transfers between devices, hop(): return lax.ppermute(value, ('expert', 'mp'), moves)  31.2 us
    pallas_call x3, Pallas kernels, run_expert(): pl.pallas_call(functools.partial(expert_kernel, tuple(map(tuple, orders))...  3.86 us
    pallas_call x4, Pallas kernels, attend(): pl.pallas_call(attend_kernel, in_specs=[WHOLE] * 2, out_specs=WHOLE, out_...  2.8 us
    pallas_call x4, Pallas kernels, combine(): pl.pallas_call(functools.partial(combine_kernel, len(parts)), in_specs=[W...  1.59 us
  transfers between devices with their start and end apart: 30, of which 13 were waited for; matrix products, arithmetic and copies ran while one was open for 0% of the time, Pallas kernels for 11%

profile of v20, /device:TPU:0, one launch (start us, length us, event | category | flops | bytes accessed | tf_op | source)
XLA Modules:
  0.0 77.6 jit_solution(3474901155837479918)
XLA Ops:
  0.0 2.9 %collective-permute-start.9 = (bf16[256,1024]{1,0:T(8,128)(2,1)}, bf16[256,1024]{1,0:T(8,128)(2,1)S(1)}, u32[]{:S(2)}, u32[]{:S(2)}) collective-permute-start(bf16[256,1024]{1,0:T(8,128)(2,1)} %refs_5_), channel_id=1, source_target_pairs={{0,2},{1,3},{2,0},{3,1},{4,6},{5,7},{6,4},{7,5},{8,10},{9,11},{10,... | collective-permute-start | bytes 1572872 | tf_op jit(solution)/shard_map/ppermute | solution.py:363
  2.9 1.5 %query.1 = (bf16[256,256]{1,0:T(8,128)(2,1)S(1)}, bf16[2,512,256]{2,1,0:T(8,128)(2,1)S(1)}) custom-call(bf16[256,1024]{1,0:T(8,128)(2,1)} %refs_0_.1, bf16[1024,256]{1,0:T(8,128)(2,1)} %weight.1, bf16[2,512,256]{2,1,0:T(8,128)(2,1)} %bitcast.39), custom_call_target="tpu_custom_call" | custom-call | tf_op jit(solution)/shard_map/query/pallas_call | solution.py:65
  4.5 0.0 copy-start.3
  4.5 0.0 copy-start.5
  4.5 0.0 copy-start.2
  4.5 2.7 %collective-permute-start.1 = (bf16[256,256]{1,0:T(8,128)(2,1)S(1)}, bf16[256,256]{1,0:T(8,128)(2,1)S(1)}, u32[]{:S(2)}, u32[]{:S(2)}) collective-permute-start(bf16[256,256]{1,0:T(8,128)(2,1)S(1)} %get-tuple-element.49.queries), channel_id=1, source_target_pairs={{0,8},{1,9},{2,10},{3,11},{4,12},{5,13},{6,14},{7,15},{8,0},{9,1},... | collective-permute-start | bytes 393224 | tf_op jit(solution)/shard_map/ppermute | solution.py:363
  7.2 1.6 %collective-permute-start = (bf16[256,256]{1,0:T(8,128)(2,1)S(1)}, bf16[256,256]{1,0:T(8,128)(2,1)S(1)}, u32[]{:S(2)}, u32[]{:S(2)}) collective-permute-start(bf16[256,256]{1,0:T(8,128)(2,1)S(1)} %get-tuple-element.49.queries), channel_id=1, source_target_pairs={{0,4},{1,5},{2,6},{3,7},{4,0},{5,1},{6,2},{7,3},{8,12},{9,13},{10,... | collective-permute-start | bytes 393224 | tf_op jit(solution)/shard_map/ppermute | solution.py:363
  8.7 0.7 attend.4.refs_0_
  9.4 3.9 %collective-permute-done.1.queries = bf16[256,256]{1,0:T(8,128)(2,1)S(1)} collective-permute-done((bf16[256,256]{1,0:T(8,128)(2,1)S(1)}, bf16[256,256]{1,0:T(8,128)(2,1)S(1)}, u32[]{:S(2)}, u32[]{:S(2)}) %collective-permute-start.1) | collective-permute-done | bytes 131104 | tf_op jit(solution)/shard_map/ppermute | solution.py:363
  13.3 0.6 collective-permute-start.4
  13.9 0.7 attend.5
  14.6 3.4 %collective-permute-start.3 = (bf16[256,256]{1,0:T(8,128)(2,1)S(1)}, bf16[256,256]{1,0:T(8,128)(2,1)S(1)}, u32[]{:S(2)}, u32[]{:S(2)}) collective-permute-start(bf16[256,256]{1,0:T(8,128)(2,1)S(1)} %attend.5), channel_id=1, source_target_pairs={{0,8},{1,9},{2,10},{3,11},{4,12},{5,13},{6,14},{7,15},{8,0},{9,1},... | collective-permute-start | bytes 393224 | tf_op jit(solution)/shard_map/ppermute | solution.py:363
  18.1 0.7 attend.6
  18.8 0.1 collective-permute-start.2
  18.9 0.7 attend.7
  19.6 0.0 copy-start.4
  19.6 5.9 %collective-permute-start.5 = (bf16[256,256]{1,0:T(8,128)(2,1)S(1)}, bf16[256,256]{1,0:T(8,128)(2,1)S(1)}, u32[]{:S(2)}, u32[]{:S(2)}) collective-permute-start(bf16[256,256]{1,0:T(8,128)(2,1)S(1)} %attend.7), channel_id=1, source_target_pairs={{0,12},{1,13},{2,14},{3,15},{4,8},{5,9},{6,10},{7,11},{8,4},{9,5},... | collective-permute-start | bytes 393224 | tf_op jit(solution)/shard_map/ppermute | solution.py:363
  26.1 0.0 collective-permute-done.2.refs_1_
  26.2 2.8 %collective-permute-done.5.refs_3_ = bf16[256,256]{1,0:T(8,128)(2,1)S(1)} collective-permute-done((bf16[256,256]{1,0:T(8,128)(2,1)S(1)}, bf16[256,256]{1,0:T(8,128)(2,1)S(1)}, u32[]{:S(2)}, u32[]{:S(2)}) %collective-permute-start.5) | collective-permute-done | bytes 131104 | tf_op jit(solution)/shard_map/ppermute | solution.py:363
  29.0 0.1 pick.1.refs_1_
  29.1 0.1 collective-permute-start.10
  29.2 0.5 collective-permute-start.11
  29.7 0.5 collective-permute-start.6
  30.3 1.0 %route.1 = (s32[256,2]{1,0:T(8,128)S(1)}, bf16[192,256]{1,0:T(8,128)(2,1)S(1)}, bf16[192,256]{1,0:T(8,128)(2,1)S(1)}, bf16[192,256]{1,0:T(8,128)(2,1)S(1)}, bf16...) custom-call(s32[2,256]{1,0:T(2,128)S(1)} %bitcast.38), custom_call_target="tpu_custom_call" | custom-call | tf_op jit(solution)/shard_map/route/pallas_call | solution.py:177
  31.2 0.1 collective-permute-start.7
  31.3 3.9 %collective-permute-done.6.refs_2_ = bf16[256,256]{1,0:T(8,128)(2,1)S(1)} collective-permute-done((bf16[256,256]{1,0:T(8,128)(2,1)S(1)}, bf16[256,256]{1,0:T(8,128)(2,1)S(1)}, u32[]{:S(2)}, u32[]{:S(2)}) %collective-permute-start.6) | collective-permute-done | bytes 131104 | tf_op jit(solution)/shard_map/ppermute | solution.py:363
  35.2 1.3 %collective-permute-done.8.refs_4_ = bf16[256,256]{1,0:T(8,128)(2,1)S(1)} collective-permute-done((bf16[256,256]{1,0:T(8,128)(2,1)S(1)}, bf16[256,256]{1,0:T(8,128)(2,1)S(1)}, u32[]{:S(2)}, u32[]{:S(2)}) %collective-permute-start.8) | collective-permute-done | bytes 131104 | tf_op jit(solution)/shard_map/ppermute | solution.py:363
  36.6 0.0 collective-permute-done.10.refs_7_
  36.6 0.0 collective-permute-done.11.refs_8_
  36.6 0.0 copy-start
  36.6 0.0 copy-start.1
  36.6 1.1 %state.1 = (bf16[256,1024]{1,0:T(8,128)(2,1)S(1)}, bf16[192,512]{1,0:T(8,128)(2,1)S(1)}, bf16[192,256]{1,0:T(8,128)(2,1)S(1)}, bf16[192,512]{1,0:T(8,128)(2,1)S(1)}) custom-call(bf16[256,1024]{1,0:T(8,128)(2,1)S(1)} %copy-done.2, bf16[256,256]{1,0:T(8,128)(2,1)S(1)} %pick.1.refs_1_, bf16[256,256]{1,0:T(8,128)(2,1)S(1)} %collective-permute-done.6.refs_2_, ...), custom_call_target="tpu_custom_call" | custom-call | tf_op jit(solution)/shard_map/state/pallas_call | solution.py:210
  37.7 3.4 %collective-permute-start.12 = (bf16[192,256]{1,0:T(8,128)(2,1)S(1)}, bf16[192,256]{1,0:T(8,128)(2,1)S(1)}, u32[]{:S(2)}, u32[]{:S(2)}) collective-permute-start(bf16[192,256]{1,0:T(8,128)(2,1)S(1)} %get-tuple-element.72), channel_id=1, source_target_pairs={{0,12},{1,13},{2,14},{3,15},{4,8},{5,9},{6,10},{7,11},{8,4},{9,5},... | collective-permute-start | bytes 294920 | tf_op jit(solution)/shard_map/ppermute | solution.py:363
  41.1 1.1 %collective-permute-start.18 = (bf16[192,512]{1,0:T(8,128)(2,1)S(1)}, bf16[192,512]{1,0:T(8,128)(2,1)S(1)}, u32[]{:S(2)}, u32[]{:S(2)}) collective-permute-start(bf16[192,512]{1,0:T(8,128)(2,1)S(1)} %get-tuple-element.79), channel_id=1, source_target_pairs={{0,4},{1,5},{2,6},{3,7},{4,0},{5,1},{6,2},{7,3},{8,12},{9,13},{10,... | collective-permute-start | bytes 589832 | tf_op jit(solution)/shard_map/ppermute | solution.py:363
  42.1 0.5 home.1
  42.7 1.0 %expert.3 = (f32[2,192,256]{2,1,0:T(8,128)S(1)}, bf16[2,192,256]{2,1,0:T(8,128)(2,1)S(1)}) custom-call(bf16[192,512]{1,0:T(8,128)(2,1)S(1)} %get-tuple-element.68.refs_0_, bf16[192,512]{1,0:T(8,128)(2,1)S(1)} %get-tuple-element.69.refs_1_, bf16[1024,1024]{1,0:T(8,128)(2,1)S(1)} %bitcast.31, bf16[1024,1024]{1,0:T(8,128)(2,1)S(1)} %bitcast.34), custom_call_target="tpu_custom_call" | custom-call | tf_op jit(solution)/shard_map/expert/pallas_call | solution.py:289
  43.7 1.6 %collective-permute-done.12.refs_0_ = bf16[192,256]{1,0:T(8,128)(2,1)S(1)} collective-permute-done((bf16[192,256]{1,0:T(8,128)(2,1)S(1)}, bf16[192,256]{1,0:T(8,128)(2,1)S(1)}, u32[]{:S(2)}, u32[]{:S(2)}) %collective-permute-start.12) | collective-permute-done | bytes 98336 | tf_op jit(solution)/shard_map/ppermute | solution.py:363
  45.3 0.5 collective-permute-start.16
  45.8 8.2 %collective-permute-done.15.refs_0_ = bf16[192,512]{1,0:T(8,128)(2,1)S(1)} collective-permute-done((bf16[192,512]{1,0:T(8,128)(2,1)S(1)}, bf16[192,512]{1,0:T(8,128)(2,1)S(1)}, u32[]{:S(2)}, u32[]{:S(2)}) %collective-permute-start.15) | collective-permute-done | bytes 196640 | tf_op jit(solution)/shard_map/ppermute | solution.py:363
  54.0 0.5 collective-permute-start.19
  54.6 0.9 %collective-permute-done.17.refs_1_ = bf16[192,512]{1,0:T(8,128)(2,1)S(1)} collective-permute-done((bf16[192,512]{1,0:T(8,128)(2,1)S(1)}, bf16[192,512]{1,0:T(8,128)(2,1)S(1)}, u32[]{:S(2)}, u32[]{:S(2)}) %collective-permute-start.17) | collective-permute-done | bytes 196640 | tf_op jit(solution)/shard_map/ppermute | solution.py:363
  55.5 0.3 collective-permute-done.19.refs_3_
  55.8 1.8 %expert.4 = (f32[2,384,256]{2,1,0:T(8,128)S(1)}, bf16[2,384,256]{2,1,0:T(8,128)(2,1)S(1)}) custom-call(bf16[192,512]{1,0:T(8,128)(2,1)S(1)} %collective-permute-done.15.refs_0_, bf16[192,512]{1,0:T(8,128)(2,1)S(1)} %collective-permute-done.17.refs_1_, bf16[192,512]{1,0:T(8,128)(2,1)S(1)} %collective-permute-done.18.refs_2_, ...), custom_call_target="tpu_custom_call" | custom-call | tf_op jit(solution)/shard_map/expert/pallas_call | solution.py:289
  57.6 0.3 collective-permute-start.20
  57.9 0.6 collective-permute-start.14
  58.5 0.5 collective-permute-start.22
  59.0 0.4 collective-permute-done.20
  59.4 0.1 convert_add_fusion
  59.5 1.2 %collective-permute-start.25 = (bf16[192,256]{1,0:T(8,128)(2,1)S(1)}, bf16[192,256]{1,0:T(8,128)(2,1)S(1)}, u32[]{:S(2)}, u32[]{:S(2)}) collective-permute-start(bf16[192,256]{1,0:T(8,128)(2,1)S(1)} %fusion.4), channel_id=1, source_target_pairs={{0,2},{1,3},{2,0},{3,1},{4,6},{5,7},{6,4},{7,5},{8,10},{9,11},{10,... | collective-permute-start | bytes 294920 | tf_op jit(solution)/shard_map/ppermute | solution.py:363
  60.7 1.0 %expert.5 = (f32[2,192,256]{2,1,0:T(8,128)S(1)}, bf16[2,192,256]{2,1,0:T(8,128)(2,1)S(1)}) custom-call(bf16[192,256]{1,0:T(8,128)(2,1)S(1)} %collective-permute-done.12.refs_0_, bf16[192,256]{1,0:T(8,128)(2,1)S(1)} %collective-permute-done.16.refs_1_, bf16[192,256]{1,0:T(8,128)(2,1)S(1)} %collective-permute-done.21.refs_2_, ...), custom_call_target="tpu_custom_call" | custom-call | tf_op jit(solution)/shard_map/expert/pallas_call | solution.py:289
  61.8 0.1 collective-permute-start.26
  61.9 1.0 %collective-permute-start.24 = (bf16[192,256]{1,0:T(8,128)(2,1)S(1)}, bf16[192,256]{1,0:T(8,128)(2,1)S(1)}, u32[]{:S(2)}, u32[]{:S(2)}) collective-permute-start(bf16[192,256]{1,0:T(8,128)(2,1)S(1)} %get-tuple-element.93), channel_id=1, source_target_pairs={{0,6},{1,7},{2,4},{3,5},{4,2},{5,3},{6,0},{7,1},{8,14},{9,15},{10,... | collective-permute-start | bytes 294920 | tf_op jit(solution)/shard_map/ppermute | solution.py:363
  62.9 1.6 %collective-permute-start.23 = (bf16[192,256]{1,0:T(8,128)(2,1)S(1)}, bf16[192,256]{1,0:T(8,128)(2,1)S(1)}, u32[]{:S(2)}, u32[]{:S(2)}) collective-permute-start(bf16[192,256]{1,0:T(8,128)(2,1)S(1)} %get-tuple-element.94), channel_id=1, source_target_pairs={{0,4},{1,5},{2,6},{3,7},{4,0},{5,1},{6,2},{7,3},{8,12},{9,13},{10,... | collective-permute-start | bytes 294920 | tf_op jit(solution)/shard_map/ppermute | solution.py:363
  64.5 0.5 collective-permute-done.25
  65.1 0.5 collective-permute-start.28
  65.6 0.1 collective-permute-start.27
  65.7 4.4 %collective-permute-done.28 = bf16[192,256]{1,0:T(8,128)(2,1)S(1)} collective-permute-done((bf16[192,256]{1,0:T(8,128)(2,1)S(1)}, bf16[192,256]{1,0:T(8,128)(2,1)S(1)}, u32[]{:S(2)}, u32[]{:S(2)}) %collective-permute-start.28) | collective-permute-done | bytes 98336 | tf_op jit(solution)/shard_map/ppermute | solution.py:363
  70.1 1.5 %collective-permute-start.29 = (bf16[192,256]{1,0:T(8,128)(2,1)S(1)}, bf16[192,256]{1,0:T(8,128)(2,1)S(1)}, u32[]{:S(2)}, u32[]{:S(2)}) collective-permute-start(bf16[192,256]{1,0:T(8,128)(2,1)S(1)} %fusion.1), channel_id=1, source_target_pairs={{0,12},{1,13},{2,14},{3,15},{4,8},{5,9},{6,10},{7,11},{8,4},{9,5},... | collective-permute-start | bytes 294920 | tf_op jit(solution)/shard_map/ppermute | solution.py:363
  71.6 0.2 combine.4.base
  71.9 0.2 combine.5.base
  72.1 1.2 %collective-permute-done.27.refs_0_ = bf16[192,256]{1,0:T(8,128)(2,1)S(1)} collective-permute-done((bf16[192,256]{1,0:T(8,128)(2,1)S(1)}, bf16[192,256]{1,0:T(8,128)(2,1)S(1)}, u32[]{:S(2)}, u32[]{:S(2)}) %collective-permute-start.27) | collective-permute-done | bytes 98336 | tf_op jit(solution)/shard_map/ppermute | solution.py:363
  73.3 0.2 combine.6.base
  73.6 3.1 %collective-permute-done.29.refs_0_ = bf16[192,256]{1,0:T(8,128)(2,1)S(1)} collective-permute-done((bf16[192,256]{1,0:T(8,128)(2,1)S(1)}, bf16[192,256]{1,0:T(8,128)(2,1)S(1)}, u32[]{:S(2)}, u32[]{:S(2)}) %collective-permute-start.29) | collective-permute-done | bytes 98336 | tf_op jit(solution)/shard_map/ppermute | solution.py:363
  76.7 0.9 %combine.7 = bf16[256,256]{1,0:T(8,128)(2,1)} custom-call(f32[256,2]{1,0:T(8,128)S(1)} %get-tuple-element.64.gates, f32[256,256]{1,0:T(8,128)S(1)} %combine.6.base, bf16[256,192]{1,0:T(8,128)(2,1)S(1)} %get-tuple-element.91.first, bf16[256,192]{1,0:T(8,128)(2,1)S(1)} %get-tuple-element.92.second, bf16[192,256]{1,0:T(8,128)(2,1)S(1)} %collective-permute-done.29.refs_0_), custom_call_target="tpu_custom_call" | custom-call | tf_op jit(solution)/shard_map/combine/pallas_call | solution.py:315
  (34 shorter events, 0.3 us)
Async XLA Ops:
  0.0 29.2 %collective-permute-start.9 = (bf16[256,1024]{1,0:T(8,128)(2,1)}, bf16[256,1024]{1,0:T(8,128)(2,1)S(1)}, u32[]{:S(2)}, u32[]{:S(2)}) collective-permute-start(bf16[256,1024]{1,0:T(8,128)(2,1)} %refs_5_), channel_id=1, source_target_pairs={{0,2},{1,3},{2,0},{3,1},{4,6},{5,7},{6,4},{7,5},{8,10},{9,11},{10,... | collective-permute-start | bytes 1572872 | tf_op jit(solution)/shard_map/ppermute | solution.py:363
  4.5 24.7 %copy-start.3 = (bf16[256,1024]{1,0:T(8,128)(2,1)S(1)}, bf16[256,1024]{1,0:T(8,128)(2,1)}, u32[]{:S(2)}) copy-start(bf16[256,1024]{1,0:T(8,128)(2,1)} %refs_5_) | copy-start | bytes 1572868
  4.5 25.8 %copy-start.5 = (s32[256,2]{0,1:T(2,128)S(1)}, s32[256,2]{0,1:T(2,128)}, u32[]{:S(2)}) copy-start(s32[256,2]{0,1:T(2,128)} %param.15) | copy-start | bytes 6148
  4.5 32.1 %copy-start.2 = (bf16[256,1024]{1,0:T(8,128)(2,1)S(1)}, bf16[256,1024]{1,0:T(8,128)(2,1)}, u32[]{:S(2)}) copy-start(bf16[256,1024]{1,0:T(8,128)(2,1)} %refs_0_.1) | copy-start | bytes 1572868
  4.5 8.8 %collective-permute-start.1 = (bf16[256,256]{1,0:T(8,128)(2,1)S(1)}, bf16[256,256]{1,0:T(8,128)(2,1)S(1)}, u32[]{:S(2)}, u32[]{:S(2)}) collective-permute-start(bf16[256,256]{1,0:T(8,128)(2,1)S(1)} %get-tuple-element.49.queries), channel_id=1, source_target_pairs={{0,8},{1,9},{2,10},{3,11},{4,12},{5,13},{6,14},{7,15},{8,0},{9,1},... | collective-permute-start | bytes 393224 | tf_op jit(solution)/shard_map/ppermute | solution.py:363
  7.2 10.9 %collective-permute-start = (bf16[256,256]{1,0:T(8,128)(2,1)S(1)}, bf16[256,256]{1,0:T(8,128)(2,1)S(1)}, u32[]{:S(2)}, u32[]{:S(2)}) collective-permute-start(bf16[256,256]{1,0:T(8,128)(2,1)S(1)} %get-tuple-element.49.queries), channel_id=1, source_target_pairs={{0,4},{1,5},{2,6},{3,7},{4,0},{5,1},{6,2},{7,3},{8,12},{9,13},{10,... | collective-permute-start | bytes 393224 | tf_op jit(solution)/shard_map/ppermute | solution.py:363
  13.3 5.5 %collective-permute-start.4 = (bf16[256,256]{1,0:T(8,128)(2,1)S(1)}, bf16[256,256]{1,0:T(8,128)(2,1)S(1)}, u32[]{:S(2)}, u32[]{:S(2)}) collective-permute-start(bf16[256,256]{1,0:T(8,128)(2,1)S(1)} %collective-permute-done.1.queries), channel_id=1, source_target_pairs={{0,4},{1,5},{2,6},{3,7},{4,0},{5,1},{6,2},{7,3},{8,12},{9,13},{10,... | collective-permute-start | bytes 393224 | tf_op jit(solution)/shard_map/ppermute | solution.py:363
  14.6 11.5 %collective-permute-start.3 = (bf16[256,256]{1,0:T(8,128)(2,1)S(1)}, bf16[256,256]{1,0:T(8,128)(2,1)S(1)}, u32[]{:S(2)}, u32[]{:S(2)}) collective-permute-start(bf16[256,256]{1,0:T(8,128)(2,1)S(1)} %attend.5), channel_id=1, source_target_pairs={{0,8},{1,9},{2,10},{3,11},{4,12},{5,13},{6,14},{7,15},{8,0},{9,1},... | collective-permute-start | bytes 393224 | tf_op jit(solution)/shard_map/ppermute | solution.py:363
  18.8 7.4 %collective-permute-start.2 = (bf16[256,256]{1,0:T(8,128)(2,1)S(1)}, bf16[256,256]{1,0:T(8,128)(2,1)S(1)}, u32[]{:S(2)}, u32[]{:S(2)}) collective-permute-start(bf16[256,256]{1,0:T(8,128)(2,1)S(1)} %attend.6), channel_id=1, source_target_pairs={{0,4},{1,5},{2,6},{3,7},{4,0},{5,1},{6,2},{7,3},{8,12},{9,13},{10,... | collective-permute-start | bytes 393224 | tf_op jit(solution)/shard_map/ppermute | solution.py:363
  19.6 22.6 %copy-start.4 = (bf16[1024,4]{0,1:T(4,128)(2,1)S(1)}, bf16[1024,4]{0,1:T(4,128)(2,1)}, u32[]{:S(2)}) copy-start(bf16[1024,4]{0,1:T(4,128)(2,1)} %param.14) | copy-start | bytes 24580
  19.6 9.4 %collective-permute-start.5 = (bf16[256,256]{1,0:T(8,128)(2,1)S(1)}, bf16[256,256]{1,0:T(8,128)(2,1)S(1)}, u32[]{:S(2)}, u32[]{:S(2)}) collective-permute-start(bf16[256,256]{1,0:T(8,128)(2,1)S(1)} %attend.7), channel_id=1, source_target_pairs={{0,12},{1,13},{2,14},{3,15},{4,8},{5,9},{6,10},{7,11},{8,4},{9,5},... | collective-permute-start | bytes 393224 | tf_op jit(solution)/shard_map/ppermute | solution.py:363
  29.1 7.4 %collective-permute-start.10 = (bf16[256,1024]{1,0:T(8,128)(2,1)S(1)}, bf16[256,1024]{1,0:T(8,128)(2,1)S(1)}, u32[]{:S(2)}, u32[]{:S(2)}) collective-permute-start(bf16[256,1024]{1,0:T(8,128)(2,1)S(1)} %copy-done.3), channel_id=1, source_target_pairs={{0,1},{1,0},{2,3},{3,2},{4,5},{5,4},{6,7},{7,6},{8,9},{9,8},{10,11... | collective-permute-start | bytes 1572872 | tf_op jit(solution)/shard_map/ppermute | solution.py:363
  29.2 7.3 %collective-permute-start.11 = (bf16[256,1024]{1,0:T(8,128)(2,1)S(1)}, bf16[256,1024]{1,0:T(8,128)(2,1)S(1)}, u32[]{:S(2)}, u32[]{:S(2)}) collective-permute-start(bf16[256,1024]{1,0:T(8,128)(2,1)S(1)} %collective-permute-done.9.refs_6_), channel_id=1, source_target_pairs={{0,1},{1,0},{2,3},{3,2},{4,5},{5,4},{6,7},{7,6},{8,9},{9,8},{10,11... | collective-permute-start | bytes 1572872 | tf_op jit(solution)/shard_map/ppermute | solution.py:363
  29.7 5.5 %collective-permute-start.6 = (bf16[256,256]{1,0:T(8,128)(2,1)S(1)}, bf16[256,256]{1,0:T(8,128)(2,1)S(1)}, u32[]{:S(2)}, u32[]{:S(2)}) collective-permute-start(bf16[256,256]{1,0:T(8,128)(2,1)S(1)} %pick.1.refs_1_), channel_id=1, source_target_pairs={{0,2},{1,3},{2,0},{3,1},{4,6},{5,7},{6,4},{7,5},{8,10},{9,11},{10,... | collective-permute-start | bytes 393224 | tf_op jit(solution)/shard_map/ppermute | solution.py:363
  31.2 4.0 %collective-permute-start.7 = (bf16[256,256]{1,0:T(8,128)(2,1)S(1)}, bf16[256,256]{1,0:T(8,128)(2,1)S(1)}, u32[]{:S(2)}, u32[]{:S(2)}) collective-permute-start(bf16[256,256]{1,0:T(8,128)(2,1)S(1)} %pick.1.refs_1_), channel_id=1, source_target_pairs={{0,1},{1,0},{2,3},{3,2},{4,5},{5,4},{6,7},{7,6},{8,9},{9,8},{10,11... | collective-permute-start | bytes 393224 | tf_op jit(solution)/shard_map/ppermute | solution.py:363
  35.2 1.3 %collective-permute-start.8 = (bf16[256,256]{1,0:T(8,128)(2,1)S(1)}, bf16[256,256]{1,0:T(8,128)(2,1)S(1)}, u32[]{:S(2)}, u32[]{:S(2)}) collective-permute-start(bf16[256,256]{1,0:T(8,128)(2,1)S(1)} %collective-permute-done.6.refs_2_), channel_id=1, source_target_pairs={{0,1},{1,0},{2,3},{3,2},{4,5},{5,4},{6,7},{7,6},{8,9},{9,8},{10,11... | collective-permute-start | bytes 393224 | tf_op jit(solution)/shard_map/ppermute | solution.py:363
  36.6 6.1 %copy-start = (bf16[1,1024,1024]{2,1,0:T(8,128)(2,1)S(1)}, bf16[1,1024,1024]{2,1,0:T(8,128)(2,1)}, u32[]{:S(2)}) copy-start(bf16[1,1024,1024]{2,1,0:T(8,128)(2,1)} %param.16) | copy-start | bytes 6291460
  36.6 6.1 %copy-start.1 = (bf16[1,1024,1024]{2,1,0:T(8,128)(2,1)S(1)}, bf16[1,1024,1024]{2,1,0:T(8,128)(2,1)}, u32[]{:S(2)}) copy-start(bf16[1,1024,1024]{2,1,0:T(8,128)(2,1)} %param.17) | copy-start | bytes 6291460
  37.7 7.6 %collective-permute-start.12 = (bf16[192,256]{1,0:T(8,128)(2,1)S(1)}, bf16[192,256]{1,0:T(8,128)(2,1)S(1)}, u32[]{:S(2)}, u32[]{:S(2)}) collective-permute-start(bf16[192,256]{1,0:T(8,128)(2,1)S(1)} %get-tuple-element.72), channel_id=1, source_target_pairs={{0,12},{1,13},{2,14},{3,15},{4,8},{5,9},{6,10},{7,11},{8,4},{9,5},... | collective-permute-start | bytes 294920 | tf_op jit(solution)/shard_map/ppermute | solution.py:363
  41.1 13.0 %collective-permute-start.15 = (bf16[192,512]{1,0:T(8,128)(2,1)S(1)}, bf16[192,512]{1,0:T(8,128)(2,1)S(1)}, u32[]{:S(2)}, u32[]{:S(2)}) collective-permute-start(bf16[192,512]{1,0:T(8,128)(2,1)S(1)} %get-tuple-element.76), channel_id=1, source_target_pairs={{0,8},{1,9},{2,10},{3,11},{4,12},{5,13},{6,14},{7,15},{8,0},{9,1},... | collective-permute-start | bytes 589832 | tf_op jit(solution)/shard_map/ppermute | solution.py:363
  41.1 13.0 %collective-permute-start.18 = (bf16[192,512]{1,0:T(8,128)(2,1)S(1)}, bf16[192,512]{1,0:T(8,128)(2,1)S(1)}, u32[]{:S(2)}, u32[]{:S(2)}) collective-permute-start(bf16[192,512]{1,0:T(8,128)(2,1)S(1)} %get-tuple-element.79), channel_id=1, source_target_pairs={{0,4},{1,5},{2,6},{3,7},{4,0},{5,1},{6,2},{7,3},{8,12},{9,13},{10,... | collective-permute-start | bytes 589832 | tf_op jit(solution)/shard_map/ppermute | solution.py:363
  45.3 9.3 %collective-permute-start.13 = (bf16[2,192,256]{2,1,0:T(8,128)(2,1)S(1)}, bf16[2,192,256]{2,1,0:T(8,128)(2,1)S(1)}, u32[]{:S(2)}, u32[]{:S(2)}) collective-permute-start(bf16[2,192,256]{2,1,0:T(8,128)(2,1)S(1)} %get-tuple-element.73), channel_id=1, source_target_pairs={{0,1},{1,0},{2,3},{3,2},{4,5},{5,4},{6,7},{7,6},{8,9},{9,8},{10,11... | collective-permute-start | bytes 589832 | tf_op jit(solution)/shard_map/ppermute | solution.py:363
  45.3 9.3 %collective-permute-start.16 = (bf16[192,256]{1,0:T(8,128)(2,1)S(1)}, bf16[192,256]{1,0:T(8,128)(2,1)S(1)}, u32[]{:S(2)}, u32[]{:S(2)}) collective-permute-start(bf16[192,256]{1,0:T(8,128)(2,1)S(1)} %collective-permute-done.12.refs_0_), channel_id=1, source_target_pairs={{0,2},{1,3},{2,0},{3,1},{4,6},{5,7},{6,4},{7,5},{8,10},{9,11},{10,... | collective-permute-start | bytes 294920 | tf_op jit(solution)/shard_map/ppermute | solution.py:363
  54.0 1.4 %collective-permute-start.17 = (bf16[192,512]{1,0:T(8,128)(2,1)S(1)}, bf16[192,512]{1,0:T(8,128)(2,1)S(1)}, u32[]{:S(2)}, u32[]{:S(2)}) collective-permute-start(bf16[192,512]{1,0:T(8,128)(2,1)S(1)} %collective-permute-done.15.refs_0_), channel_id=1, source_target_pairs={{0,1},{1,0},{2,3},{3,2},{4,5},{5,4},{6,7},{7,6},{8,9},{9,8},{10,11... | collective-permute-start | bytes 589832 | tf_op jit(solution)/shard_map/ppermute | solution.py:363
  54.0 1.7 %collective-permute-start.19 = (bf16[192,512]{1,0:T(8,128)(2,1)S(1)}, bf16[192,512]{1,0:T(8,128)(2,1)S(1)}, u32[]{:S(2)}, u32[]{:S(2)}) collective-permute-start(bf16[192,512]{1,0:T(8,128)(2,1)S(1)} %collective-permute-done.18.refs_2_), channel_id=1, source_target_pairs={{0,1},{1,0},{2,3},{3,2},{4,5},{5,4},{6,7},{7,6},{8,9},{9,8},{10,11... | collective-permute-start | bytes 589832 | tf_op jit(solution)/shard_map/ppermute | solution.py:363
  57.6 1.8 %collective-permute-start.20 = (bf16[2,384,256]{2,1,0:T(8,128)(2,1)S(1)}, bf16[2,384,256]{2,1,0:T(8,128)(2,1)S(1)}, u32[]{:S(2)}, u32[]{:S(2)}) collective-permute-start(bf16[2,384,256]{2,1,0:T(8,128)(2,1)S(1)} %get-tuple-element.81), channel_id=1, source_target_pairs={{0,1},{1,0},{2,3},{3,2},{4,5},{5,4},{6,7},{7,6},{8,9},{9,8},{10,11... | collective-permute-start | bytes 1179656 | tf_op jit(solution)/shard_map/ppermute | solution.py:363
  57.9 13.7 %collective-permute-start.14 = (bf16[192,256]{1,0:T(8,128)(2,1)S(1)}, bf16[192,256]{1,0:T(8,128)(2,1)S(1)}, u32[]{:S(2)}, u32[]{:S(2)}) collective-permute-start(bf16[192,256]{1,0:T(8,128)(2,1)S(1)} %get-tuple-element.95), channel_id=1, source_target_pairs={{0,2},{1,3},{2,0},{3,1},{4,6},{5,7},{6,4},{7,5},{8,10},{9,11},{10,... | collective-permute-start | bytes 294920 | tf_op jit(solution)/shard_map/ppermute | solution.py:363
  58.5 2.2 %collective-permute-start.21 = (bf16[192,256]{1,0:T(8,128)(2,1)S(1)}, bf16[192,256]{1,0:T(8,128)(2,1)S(1)}, u32[]{:S(2)}, u32[]{:S(2)}) collective-permute-start(bf16[192,256]{1,0:T(8,128)(2,1)S(1)} %collective-permute-done.12.refs_0_), channel_id=1, source_target_pairs={{0,1},{1,0},{2,3},{3,2},{4,5},{5,4},{6,7},{7,6},{8,9},{9,8},{10,11... | collective-permute-start | bytes 294920 | tf_op jit(solution)/shard_map/ppermute | solution.py:363
  58.5 2.2 %collective-permute-start.22 = (bf16[192,256]{1,0:T(8,128)(2,1)S(1)}, bf16[192,256]{1,0:T(8,128)(2,1)S(1)}, u32[]{:S(2)}, u32[]{:S(2)}) collective-permute-start(bf16[192,256]{1,0:T(8,128)(2,1)S(1)} %collective-permute-done.16.refs_1_), channel_id=1, source_target_pairs={{0,1},{1,0},{2,3},{3,2},{4,5},{5,4},{6,7},{7,6},{8,9},{9,8},{10,11... | collective-permute-start | bytes 294920 | tf_op jit(solution)/shard_map/ppermute | solution.py:363
  59.5 5.5 %collective-permute-start.25 = (bf16[192,256]{1,0:T(8,128)(2,1)S(1)}, bf16[192,256]{1,0:T(8,128)(2,1)S(1)}, u32[]{:S(2)}, u32[]{:S(2)}) collective-permute-start(bf16[192,256]{1,0:T(8,128)(2,1)S(1)} %fusion.4), channel_id=1, source_target_pairs={{0,2},{1,3},{2,0},{3,1},{4,6},{5,7},{6,4},{7,5},{8,10},{9,11},{10,... | collective-permute-start | bytes 294920 | tf_op jit(solution)/shard_map/ppermute | solution.py:363
  61.8 2.7 %collective-permute-start.26 = (bf16[2,192,256]{2,1,0:T(8,128)(2,1)S(1)}, bf16[2,192,256]{2,1,0:T(8,128)(2,1)S(1)}, u32[]{:S(2)}, u32[]{:S(2)}) collective-permute-start(bf16[2,192,256]{2,1,0:T(8,128)(2,1)S(1)} %get-tuple-element.85), channel_id=1, source_target_pairs={{0,1},{1,0},{2,3},{3,2},{4,5},{5,4},{6,7},{7,6},{8,9},{9,8},{10,11... | collective-permute-start | bytes 589832 | tf_op jit(solution)/shard_map/ppermute | solution.py:363
  61.9 10.0 %collective-permute-start.24 = (bf16[192,256]{1,0:T(8,128)(2,1)S(1)}, bf16[192,256]{1,0:T(8,128)(2,1)S(1)}, u32[]{:S(2)}, u32[]{:S(2)}) collective-permute-start(bf16[192,256]{1,0:T(8,128)(2,1)S(1)} %get-tuple-element.93), channel_id=1, source_target_pairs={{0,6},{1,7},{2,4},{3,5},{4,2},{5,3},{6,0},{7,1},{8,14},{9,15},{10,... | collective-permute-start | bytes 294920 | tf_op jit(solution)/shard_map/ppermute | solution.py:363
  62.9 9.0 %collective-permute-start.23 = (bf16[192,256]{1,0:T(8,128)(2,1)S(1)}, bf16[192,256]{1,0:T(8,128)(2,1)S(1)}, u32[]{:S(2)}, u32[]{:S(2)}) collective-permute-start(bf16[192,256]{1,0:T(8,128)(2,1)S(1)} %get-tuple-element.94), channel_id=1, source_target_pairs={{0,4},{1,5},{2,6},{3,7},{4,0},{5,1},{6,2},{7,3},{8,12},{9,13},{10,... | collective-permute-start | bytes 294920 | tf_op jit(solution)/shard_map/ppermute | solution.py:363
  65.1 5.1 %collective-permute-start.28 = (bf16[192,256]{1,0:T(8,128)(2,1)S(1)}, bf16[192,256]{1,0:T(8,128)(2,1)S(1)}, u32[]{:S(2)}, u32[]{:S(2)}) collective-permute-start(bf16[192,256]{1,0:T(8,128)(2,1)S(1)} %fusion.5), channel_id=1, source_target_pairs={{0,2},{1,3},{2,0},{3,1},{4,6},{5,7},{6,4},{7,5},{8,10},{9,11},{10,... | collective-permute-start | bytes 294920 | tf_op jit(solution)/shard_map/ppermute | solution.py:363
  65.6 7.7 %collective-permute-start.27 = (bf16[192,256]{1,0:T(8,128)(2,1)S(1)}, bf16[192,256]{1,0:T(8,128)(2,1)S(1)}, u32[]{:S(2)}, u32[]{:S(2)}) collective-permute-start(bf16[192,256]{1,0:T(8,128)(2,1)S(1)} %fusion.3), channel_id=1, source_target_pairs={{0,8},{1,9},{2,10},{3,11},{4,12},{5,13},{6,14},{7,15},{8,0},{9,1},... | collective-permute-start | bytes 294920 | tf_op jit(solution)/shard_map/ppermute | solution.py:363
  70.1 6.5 %collective-permute-start.29 = (bf16[192,256]{1,0:T(8,128)(2,1)S(1)}, bf16[192,256]{1,0:T(8,128)(2,1)S(1)}, u32[]{:S(2)}, u32[]{:S(2)}) collective-permute-start(bf16[192,256]{1,0:T(8,128)(2,1)S(1)} %fusion.1), channel_id=1, source_target_pairs={{0,12},{1,13},{2,14},{3,15},{4,8},{5,9},{6,10},{7,11},{8,4},{9,5},... | collective-permute-start | bytes 294920 | tf_op jit(solution)/shard_map/ppermute | solution.py:363
